TPU v7x, 32 devices: a whole 2x2x4 slice. The times are simulated.
32 devices in a mesh: seq: 16 (over z, y, x), dp: 2 (over core).
Axes of the slice: x: 2, y: 2, z: 4, core: 2. Of those that a mesh axis runs over, the one named last changes fastest.
Arguments:
- queries: bfloat16 [2, 4096, 1024], P('dp', 'seq'), may hold values from -6 to 6
- keys: bfloat16 [2, 4096, 1024], P('dp', 'seq'), may hold values from -6 to 6
- values: bfloat16 [2, 4096, 1024], P('dp', 'seq'), may hold values from -36 to 36, as said below
- out_gain: float32 [1024], replicated, may hold values from 0.5 to 1.5
- grad_out: bfloat16 [2, 4096, 1024], P('dp', 'seq'), may hold values from -16 to 16, as said below
Outputs:
- grad_q: bfloat16 [2, 4096, 1024], P('dp', 'seq')
- grad_k: bfloat16 [2, 4096, 1024], P('dp', 'seq')
- grad_v: bfloat16 [2, 4096, 1024], P('dp', 'seq')
- grad_gain: float32 [1024], replicated
Inputs may be any that keep to these rules, and one draw needn't show every extreme that they name: `values`: Real-valued entries. `grad_out`: Real-valued entries.
All inputs are finite; a program needn't handle non-finite values.
Results may differ from a plain program's by a relative error of at most 0.0075.
Values sent between devices are 32-bit elements; how exact they have to be, the bound alone decides.
No kernel may reach another device: no remote copies, remote signals or barrier semaphores. Data moves between devices by JAX's collectives and lax.ppermute only.
A program may use at most 128 MiB of HBM per device.

v0:
```python
import math

import jax
import jax.numpy as jnp
from jax import lax
from jax.sharding import PartitionSpec as P

HEADS = 8
DH = 128
BLOCK = 256


EPSILON = 1e-06


def carried_in(part, axis, combine, identity, reverse):
    count = lax.axis_size(axis)
    place = lax.axis_index(axis)
    ahead = count - 1 - place if reverse else place
    gathered = lax.all_gather(part, axis)
    state = jnp.zeros_like(part) + jnp.asarray(identity, part.dtype)

    def one(hop, state):
        source = count - 1 - hop if reverse else hop
        return combine(state, lax.dynamic_index_in_dim(gathered, source, 0, False))

    return lax.fori_loop(0, ahead, one, state)


def add_states(earlier, later):
    return earlier + later


def head_major(array, blocks_dev):
    seq_rows = array.shape[1]
    return (
        array.reshape(seq_rows, HEADS, DH).transpose(1, 0, 2).reshape(HEADS, blocks_dev, BLOCK, DH)
    )


def row_major(array, full_shape):
    seq_rows = full_shape[1]
    return array.reshape(HEADS, seq_rows, DH).transpose(1, 0, 2).reshape(full_shape)


def local(queries, keys, values, out_gain, grad_out):
    seq_rows = queries.shape[1]
    blocks_dev = seq_rows // BLOCK
    query_blocks = head_major(queries, blocks_dev)
    key_blocks = head_major(keys, blocks_dev)
    value_blocks = head_major(values, blocks_dev)
    causal = lax.broadcasted_iota(jnp.int32, (BLOCK, BLOCK), 0) >= lax.broadcasted_iota(
        jnp.int32, (BLOCK, BLOCK), 1
    )
    raw_scores = jnp.einsum(
        "hctd,hcsd->hcts", query_blocks, key_blocks, preferred_element_type=jnp.float32
    )
    scores_low = jnp.where(causal, raw_scores, 0.0).astype(jnp.bfloat16)
    deltas = jnp.einsum(
        "hcsd,hcse->hcde", key_blocks, value_blocks, preferred_element_type=jnp.float32
    )
    local_total = jnp.sum(deltas, axis=1)
    carried = carried_in(local_total, "seq", add_states, jnp.zeros_like(local_total), False)
    prefix_state = (carried[:, None] + jnp.cumsum(deltas, axis=1) - deltas).astype(jnp.bfloat16)
    attention = jnp.einsum(
        "hcts,hcse->hcte", scores_low, value_blocks, preferred_element_type=jnp.float32
    )
    attention = attention + jnp.einsum(
        "hctd,hcde->hcte", query_blocks, prefix_state, preferred_element_type=jnp.float32
    )
    root_mean = jnp.sqrt(jnp.mean(attention * attention, axis=-1, keepdims=True) + EPSILON)
    normed = attention / root_mean
    cotangent = head_major(grad_out, blocks_dev).astype(jnp.float32)
    gain_terms = jnp.sum(normed * cotangent, axis=(1, 2)).reshape(-1)
    scaled = out_gain.reshape(HEADS, 1, 1, DH) * cotangent
    grad_attn = (
        (scaled - normed * jnp.mean(normed * scaled, axis=-1, keepdims=True)) / root_mean
    ).astype(jnp.bfloat16)
    grad_deltas = jnp.einsum(
        "hctd,hcte->hcde", query_blocks, grad_attn, preferred_element_type=jnp.float32
    )
    grad_total = jnp.sum(grad_deltas, axis=1)
    after_local = grad_total[:, None] - jnp.cumsum(grad_deltas, axis=1)
    later_sum = carried_in(grad_total, "seq", add_states, jnp.zeros_like(grad_total), True)
    grad_state = (later_sum[:, None] + after_local).astype(jnp.bfloat16)
    raw_grad = jnp.einsum(
        "hcte,hcse->hcts", grad_attn, value_blocks, preferred_element_type=jnp.float32
    )
    grad_scores = jnp.where(causal, raw_grad, 0.0).astype(jnp.bfloat16)
    grad_query = jnp.einsum(
        "hcts,hcsd->hctd", grad_scores, key_blocks, preferred_element_type=jnp.float32
    )
    grad_query = grad_query + jnp.einsum(
        "hcte,hcde->hctd", grad_attn, prefix_state, preferred_element_type=jnp.float32
    )
    grad_key = jnp.einsum(
        "hcts,hctd->hcsd", grad_scores, query_blocks, preferred_element_type=jnp.float32
    )
    grad_key = grad_key + jnp.einsum(
        "hcse,hcde->hcsd", value_blocks, grad_state, preferred_element_type=jnp.float32
    )
    grad_value = jnp.einsum(
        "hcts,hcte->hcse", scores_low, grad_attn, preferred_element_type=jnp.float32
    )
    grad_value = grad_value + jnp.einsum(
        "hcsd,hcde->hcse", key_blocks, grad_state, preferred_element_type=jnp.float32
    )
    gain_total = lax.psum(gain_terms, ("seq", "dp"))
    position_count = lax.axis_size("seq") * lax.axis_size("dp") * seq_rows
    grad_gain = gain_total / math.sqrt(position_count)
    return (
        row_major(grad_query.astype(jnp.bfloat16), queries.shape),
        row_major(grad_key.astype(jnp.bfloat16), queries.shape),
        row_major(grad_value.astype(jnp.bfloat16), queries.shape),
        grad_gain,
    )


def solution(mesh):
    return jax.shard_map(
        local,
        mesh=mesh,
        in_specs=(
            P("dp", "seq", None),
            P("dp", "seq", None),
            P("dp", "seq", None),
            P(),
            P("dp", "seq", None),
        ),
        out_specs=(P("dp", "seq", None), P("dp", "seq", None), P("dp", "seq", None), P()),
        check_vma=False,
    )
```

profile of v0, /device:TPU:0, one launch (start us, length us, event | category | flops | bytes accessed | tf_op | source)
XLA Modules:
  0.0 292.8 jit_solution(3879571089437020348)
XLA Ops:
  7.2 1.2 copy.60
  8.4 1.2 copy.61
  9.6 1.1 fusion.11
  12.6 1.5 fusion.8
  14.2 112.7 %all-gather.5.cloned.1.call-done = f32[128,128,128]{2,1,0:T(8,128)} async-done(((f32[8,128,128]{2,1,0:T(8,128)}), f32[128,128,128]{2,1,0:T(8,128)}) %all-gather.5.cloned.1.call-update) | async-done | bytes 8388624 | tf_op jit(solution)/shard_map/all_gather | solution.py:20
  127.0 1.1 fusion.6
  128.1 1.6 multiply_reduce_fusion.2
  130.7 1.0 copy.37
  133.3 1.0 copy.40
  134.3 55.3 %psum.7 = f32[1024]{0:T(1024)S(1)} all-reduce(f32[1024]{0:T(1024)S(1)} %bitcast.115), channel_id=1, replica_groups=mesh['seq'=16,'dp'=2] {'seq','dp'}, use_global_device_ids=true, to_apply=%region_7.8 | all-reduce | flops 1024 | bytes 8192 | tf_op jit(solution)/shard_map/psum | solution.py:108
  190.1 2.6 convolution_bitcast_fusion.3
  193.1 69.0 %all-gather.7.cloned.1.call-done = f32[128,128,128]{2,1,0:T(8,128)} async-done(((f32[8,128,128]{2,1,0:T(8,128)}), f32[128,128,128]{2,1,0:T(8,128)}) %all-gather.7.cloned.1.call-update) | async-done | bytes 8388624 | tf_op jit(solution)/shard_map/all_gather | solution.py:20
  262.0 17.9 %while.23 = (s32[]{:T(128)}, f32[8,128,128]{2,1,0:T(8,128)S(1)}, s32[]{:T(128)}, f32[16,8,128,128]{3,2,1,0:T(8,128)}, s32[]{:T(128)}, /*index=5*/s32[]{:T(128)}, s32[]{:T(128)}, s32[]{:T(128)}) while((s32[]{:T(128)}, f32[8,128,128]{2,1,0:T(8,128)S(1)}, s32[]{:T(128)}, f32[16,8,128,128]{3,2,1,0:T(8,128)}, s32[]{:T(128)}, /*index=5*/s32[]{:T(128)}, ...), condition=%wide.region_5.6_spmd, body=%wide.region_4.5_spmd.sunk | while | flops 131078 | bytes 1573007 | solution.py:27
  262.1 1.2 bitcast_add_fusion.5
  263.3 1.2 bitcast_add_fusion.5
  264.5 1.2 bitcast_add_fusion.5
  265.6 1.2 bitcast_add_fusion.5
  266.8 1.2 bitcast_add_fusion.5
  268.0 1.2 bitcast_add_fusion.5
  269.2 1.2 bitcast_add_fusion.5
  270.4 1.2 bitcast_add_fusion.5
  271.6 1.2 bitcast_add_fusion.5
  272.8 1.2 bitcast_add_fusion.5
  274.0 1.2 bitcast_add_fusion.5
  275.2 1.2 bitcast_add_fusion.5
  276.4 1.2 bitcast_add_fusion.5
  277.6 1.2 bitcast_add_fusion.5
  278.8 1.2 bitcast_add_fusion.5
  280.9 1.1 add_convert_fusion
  282.0 1.5 fusion.4
  283.6 1.0 copy.42
  284.9 1.0 copy.41
  (35 shorter events, 6.7 us)
Async XLA Ops:
  7.2 119.7 %all-gather.5.cloned.1.call-start = ((), (), s32[]{:S(2)}) async-start(), calls=%async_computation | async-start | bytes 8912896 | tf_op jit(solution)/shard_map/all_gather | solution.py:20
  7.2 3.7 %copy-start.4 = (bf16[1,256,1024]{2,1,0:T(8,128)(2,1)S(1)}, bf16[1,256,1024]{2,1,0:T(8,128)(2,1)}, u32[]{:S(2)}) copy-start(bf16[1,256,1024]{2,1,0:T(8,128)(2,1)} %param.9) | copy-start | bytes 1572868
  8.4 2.6 copy-start.3
  10.8 251.2 %all-gather.7.cloned.1.call-start = ((), (), s32[]{:S(2)}) async-start(), calls=%async_computation.1 | async-start | bytes 8912896 | tf_op jit(solution)/shard_map/all_gather | solution.py:20
  11.7 1.0 copy-start
  127.0 2.7 copy-start.5
  132.3 1.0 copy-start.1
  189.5 3.2 %copy-start.2 = (bf16[8,256,256]{2,1,0:T(8,128)(2,1)S(1)}, bf16[8,256,256]{2,1,0:T(8,128)(2,1)}, u32[]{:S(2)}) copy-start(bf16[8,256,256]{2,1,0:T(8,128)(2,1)} %copy-done.1) | copy-start | bytes 3145732
Sparse Core Ops, SparseCore 0:
  11.3 115.5 all-gather.4
  131.9 130.0 all-gather.6
where the time goes:
time: 294 us; the launch traced here: 293 us
  waiting for transfers between devices  182 us (62%)
  blocking collectives  55.3 us (19%)
  other arithmetic  21.1 us (7%)
  between operations  14.3 us (5%)
  matrix products  11.1 us (4%)
  local copies, waits for them, and re-layouts  8.91 us (3%)
    all_gather x2, waiting for transfers between devices, carried_in(): gathered = lax.all_gather(part, axis)  182 us
    psum x1, blocking collectives, local(): gain_total = lax.psum(gain_terms, ('seq', 'dp'))  55.3 us
    add x15, other arithmetic, add_states(): return earlier + later  17.5 us
    unnamed x18, local copies, waits for them, and re-layouts  6.64 us
  transfers between devices with their start and end apart: 2, of which 2 were waited for; matrix products, arithmetic and copies ran while one was open for 3% of the time, Pallas kernels for 0%

commit v1 on v0

--- a/solution.py
+++ b/solution.py
@@ -13,22 +13,44 @@
 EPSILON = 1e-06
 
 
-def carried_in(part, axis, combine, identity, reverse):
+def carried_in(part, axis, reverse):
     count = lax.axis_size(axis)
     place = lax.axis_index(axis)
-    ahead = count - 1 - place if reverse else place
-    gathered = lax.all_gather(part, axis)
-    state = jnp.zeros_like(part) + jnp.asarray(identity, part.dtype)
+    group = math.gcd(count, 4)
+    member = lax.rem(place, group)
+    quarters = part.reshape((group, HEADS // group) + part.shape[1:])
 
-    def one(hop, state):
-        source = count - 1 - hop if reverse else hop
-        return combine(state, lax.dynamic_index_in_dim(gathered, source, 0, False))
+    def swap(array, mask):
+        if mask == 0:
+            return array
+        return lax.ppermute(array, axis, [(s, s ^ mask) for s in range(count)])
 
-    return lax.fori_loop(0, ahead, one, state)
+    def before(first, second):
+        return first > second if reverse else first < second
 
+    def pick(array, at):
+        return lax.dynamic_index_in_dim(array, at, 0, False)
 
-def add_states(earlier, later):
-    return earlier + later
+    held = [swap(pick(quarters, member ^ mask), mask) for mask in range(group)]
+    total = sum(held[1:], held[0])
+    carried = jnp.zeros_like(total)
+    reach = 1
+    while reach * group < count:
+        step = -reach * group if reverse else reach * group
+        pairs = [(s, s + step) for s in range(count) if 0 <= s + step < count]
+        arrived = lax.ppermute(total, axis, pairs)
+        carried = carried + arrived
+        total = total + arrived
+        reach *= 2
+    back = []
+    for mask in range(group):
+        target = member ^ mask
+        own = carried
+        for other in range(group):
+            own = own + jnp.where(before(member ^ other, target), held[other], 0.0)
+        back.append(swap(own, mask))
+    back = jnp.stack(back)
+    return jnp.concatenate([pick(back, member ^ quarter) for quarter in range(group)])
 
 
 def head_major(array, blocks_dev):
@@ -60,7 +82,7 @@
         "hcsd,hcse->hcde", key_blocks, value_blocks, preferred_element_type=jnp.float32
     )
     local_total = jnp.sum(deltas, axis=1)
-    carried = carried_in(local_total, "seq", add_states, jnp.zeros_like(local_total), False)
+    carried = carried_in(local_total, "seq", False)
     prefix_state = (carried[:, None] + jnp.cumsum(deltas, axis=1) - deltas).astype(jnp.bfloat16)
     attention = jnp.einsum(
         "hcts,hcse->hcte", scores_low, value_blocks, preferred_element_type=jnp.float32
@@ -81,7 +103,7 @@
     )
     grad_total = jnp.sum(grad_deltas, axis=1)
     after_local = grad_total[:, None] - jnp.cumsum(grad_deltas, axis=1)
-    later_sum = carried_in(grad_total, "seq", add_states, jnp.zeros_like(grad_total), True)
+    later_sum = carried_in(grad_total, "seq", True)
     grad_state = (later_sum[:, None] + after_local).astype(jnp.bfloat16)
     raw_grad = jnp.einsum(
         "hcte,hcse->hcts", grad_attn, value_blocks, preferred_element_type=jnp.float32

time: 294 us -> 123 us (0.42)
  waiting for transfers between devices: 182 us -> 23.3 us
  starting transfers between devices: 0.08 us -> 27.5 us
  other arithmetic: 21.1 us -> 5.81 us
  blocking collectives: 55.3 us -> 40.4 us
  between operations: 14.3 us -> 1.18 us
  local copies, waits for them, and re-layouts: 8.91 us -> 12.2 us
    all_gather x2 -> x0, waiting for transfers between devices: 182 us -> none  [carried_in(): gathered = lax.all_gather(part, axis)]
    ppermute x0 -> x16, starting transfers between devices: none -> 27.5 us  [the longest x12 15.4 us: swap(): return lax.ppermute(array, axis, [(s, s ^ mask) for s in range(count)])]
    ppermute x0 -> x16, waiting for transfers between devices: none -> 23.3 us  [the longest x12 14.7 us: swap(): return lax.ppermute(array, axis, [(s, s ^ mask) for s in range(count)])]
    add x15 -> x6, other arithmetic: 17.5 us -> 1.65 us  [the longest x2 0.88 us: carried_in(): own = own + jnp.where(before(member ^ other, target), held[other], 0.0)]
    psum x1, blocking collectives: 55.3 us -> 40.4 us  [local(): gain_total = lax.psum(gain_terms, ('seq', 'dp'))]
    unnamed x18 -> x48, local copies, waits for them, and re-layouts: 6.64 us -> 8.02 us
  transfers between devices with their start and end apart: 2 -> 16, of which waited for: 2 -> 10; matrix products, arithmetic and copies ran while one was open for 3% -> 10% of each run, Pallas kernels for 0% -> 0%
where the time goes in v1:
time: 123 us; the launch traced here: 122 us
  blocking collectives  40.4 us (33%)
  starting transfers between devices  27.5 us (22%)
  waiting for transfers between devices  23.3 us (19%)
  local copies, waits for them, and re-layouts  12.2 us (10%)
  matrix products  11.9 us (10%)
  other arithmetic  5.81 us (5%)
    psum x1, blocking collectives, local(): gain_total = lax.psum(gain_terms, ('seq', 'dp'))  40.4 us
    ppermute x12, starting transfers between devices, swap(): return lax.ppermute(array, axis, [(s, s ^ mask) for s in range(count)])  15.4 us
    ppermute x12, waiting for transfers between devices, swap(): return lax.ppermute(array, axis, [(s, s ^ mask) for s in range(count)])  14.7 us
    ppermute x4, starting transfers between devices, carried_in(): arrived = lax.ppermute(total, axis, pairs)  12.1 us
    ppermute x4, waiting for transfers between devices, carried_in(): arrived = lax.ppermute(total, axis, pairs)  8.63 us
    unnamed x48, local copies, waits for them, and re-layouts  8.02 us
    dynamic_slice x10, local copies, waits for them, and re-layouts, pick(): return lax.dynamic_index_in_dim(array, at, 0, False)  2.82 us
    dot_general x1, matrix products, local(): jnp.einsum('hcts,hcsd->hctd', grad_scores, key_blocks, preferred_element_...  2.7 us
  transfers between devices with their start and end apart: 16, of which 10 were waited for; matrix products, arithmetic and copies ran while one was open for 10% of the time, Pallas kernels for 0%

profile of v1, /device:TPU:0, one launch (start us, length us, event | category | flops | bytes accessed | tf_op | source)
XLA Modules:
  0.0 122.3 jit_solution(8326796813783681011)
XLA Ops:
  0.7 1.2 copy.50
  2.4 3.0 %collective-permute-start = (f32[2,128,128]{2,1,0:T(8,128)S(1)}, f32[2,128,128]{2,1,0:T(8,128)S(1)}, u32[]{:S(2)}, u32[]{:S(2)}) collective-permute-start(f32[2,128,128]{2,1,0:T(8,128)S(1)} %get-tuple-element.29), channel_id=1, source_target_pairs={{0,2},{2,0},{4,6},{6,4},{8,10},{10,8},{12,14},{14,12},{16,18},{18,... | collective-permute-start | bytes 393224 | tf_op jit(solution)/shard_map/ppermute | solution.py:26
  5.4 1.5 %collective-permute-start.1 = (f32[2,128,128]{2,1,0:T(8,128)S(1)}, f32[2,128,128]{2,1,0:T(8,128)S(1)}, u32[]{:S(2)}, u32[]{:S(2)}) collective-permute-start(f32[2,128,128]{2,1,0:T(8,128)S(1)} %get-tuple-element.31), channel_id=1, source_target_pairs={{0,4},{2,6},{4,0},{6,2},{8,12},{10,14},{12,8},{14,10},{16,20},{18,... | collective-permute-start | bytes 393224 | tf_op jit(solution)/shard_map/ppermute | solution.py:26
  6.9 2.4 %collective-permute-done = f32[2,128,128]{2,1,0:T(8,128)S(1)} collective-permute-done((f32[2,128,128]{2,1,0:T(8,128)S(1)}, f32[2,128,128]{2,1,0:T(8,128)S(1)}, u32[]{:S(2)}, u32[]{:S(2)}) %collective-permute-start) | collective-permute-done | bytes 131104 | tf_op jit(solution)/shard_map/ppermute | solution.py:26
  9.3 3.9 %collective-permute-done.1 = f32[2,128,128]{2,1,0:T(8,128)S(1)} collective-permute-done((f32[2,128,128]{2,1,0:T(8,128)S(1)}, f32[2,128,128]{2,1,0:T(8,128)S(1)}, u32[]{:S(2)}, u32[]{:S(2)}) %collective-permute-start.1) | collective-permute-done | bytes 131104 | tf_op jit(solution)/shard_map/ppermute | solution.py:26
  13.2 3.5 %collective-permute-start.3 = (f32[2,128,128]{2,1,0:T(8,128)S(1)}, f32[2,128,128]{2,1,0:T(8,128)S(1)}, u32[]{:S(2)}, u32[]{:S(2)}) collective-permute-start(f32[2,128,128]{2,1,0:T(8,128)S(1)} %fusion.44), channel_id=1, source_target_pairs={{0,8},{2,10},{4,12},{6,14},{8,16},{10,18},{12,20},{14,22},{16,24},... | collective-permute-start | bytes 393224 | tf_op jit(solution)/shard_map/ppermute | solution.py:41
  16.9 2.3 %collective-permute-done.3 = f32[2,128,128]{2,1,0:T(8,128)S(1)} collective-permute-done((f32[2,128,128]{2,1,0:T(8,128)S(1)}, f32[2,128,128]{2,1,0:T(8,128)S(1)}, u32[]{:S(2)}, u32[]{:S(2)}) %collective-permute-start.3) | collective-permute-done | bytes 131104 | tf_op jit(solution)/shard_map/ppermute | solution.py:41
  19.9 6.0 %collective-permute-start.4 = (f32[2,128,128]{2,1,0:T(8,128)}, f32[2,128,128]{2,1,0:T(8,128)}, u32[]{:S(2)}, u32[]{:S(2)}) collective-permute-start(f32[2,128,128]{2,1,0:T(8,128)} %add.187), channel_id=1, source_target_pairs={{0,16},{2,18},{4,20},{6,22},{8,24},{10,26},{12,28},{14,30},{1,17},... | collective-permute-start | bytes 393224 | tf_op jit(solution)/shard_map/ppermute | solution.py:41
  26.4 1.7 %collective-permute-done.4 = f32[2,128,128]{2,1,0:T(8,128)} collective-permute-done((f32[2,128,128]{2,1,0:T(8,128)}, f32[2,128,128]{2,1,0:T(8,128)}, u32[]{:S(2)}, u32[]{:S(2)}) %collective-permute-start.4) | collective-permute-done | bytes 131104 | tf_op jit(solution)/shard_map/ppermute | solution.py:41
  28.1 1.7 %add_bitcast_fusion.1 = (f32[1,2,128,128]{3,2,1,0:T(8,128)}, f32[2,128,128]{2,1,0:T(8,128)S(1)}) fusion(f32[2,128,128]{2,1,0:T(8,128)S(1)} %collective-permute-done.2, f32[2,128,128]{2,1,0:T(8,128)S(1)} %collective-permute-done.1, f32[2,128,128]{2,1,0:T(8,128)S(1)} %collective-permute-done, pred[]{:T(512)S(6)} %lt.70, pred[]{:T(512)S(6)} %lt.69, ...), kind=kLoop, calls=%fused_computation.86 | loop fusion | flops 229376 | bytes 917507 | tf_op jit(solution)/shard_map/stack | solution.py:52
  30.5 1.2 collective-permute-start.5
  32.6 1.4 %collective-permute-start.7 = (f32[2,128,128]{2,1,0:T(8,128)}, f32[2,128,128]{2,1,0:T(8,128)}, u32[]{:S(2)}, u32[]{:S(2)}) collective-permute-start(f32[2,128,128]{2,1,0:T(8,128)} %get-tuple-element.16), channel_id=1, source_target_pairs={{0,6},{2,4},{4,2},{6,0},{8,14},{10,12},{12,10},{14,8},{16,22},{18,... | collective-permute-start | bytes 393224 | tf_op jit(solution)/shard_map/ppermute | solution.py:26
  34.0 1.4 %fusion.9 = f32[8,256,128]{1,2,0:T(8,128)} fusion(bf16[8,256,256]{2,1,0:T(8,128)(2,1)S(1)} %select_convert_fusion.1, bf16[8,256,128]{2,0,1:T(8,128)(2,1)S(1)} %bitcast.174), kind=kOutput, calls=%fused_computation.26 | convolution fusion | flops 134217728 | bytes 2621440 | tf_op jit(solution)/shard_map/hcts,hcse->hcte/dot_general | solution.py:87
  35.5 1.3 %copy.9 = f32[1,256,1024]{1,2,0:T(8,128)S(1)} copy(bf16[1,256,1024]{2,1,0:T(8,128)(2,1)} %param.9) | data formatting | bytes 1572864 | tf_op jit(solution)/shard_map/convert_element_type | solution.py:95
  36.9 1.8 %collective-permute-done.7 = f32[2,128,128]{2,1,0:T(8,128)} collective-permute-done((f32[2,128,128]{2,1,0:T(8,128)}, f32[2,128,128]{2,1,0:T(8,128)}, u32[]{:S(2)}, u32[]{:S(2)}) %collective-permute-start.7) | collective-permute-done | bytes 131104 | tf_op jit(solution)/shard_map/ppermute | solution.py:26
  39.8 1.1 copy-done.5
  43.6 1.3 %convolution_bitcast_fusion.3 = f32[256,8,128]{0,2,1:T(8,128)} fusion(bf16[8,256,128]{1,2,0:T(8,128)(2,1)S(1)} %divide_convert_fusion, bf16[8,256,256]{2,1,0:T(8,128)(2,1)S(1)} %copy-done.2), kind=kOutput, calls=%fused_computation.9 | convolution fusion | flops 134217728 | bytes 2621440 | tf_op jit(solution)/shard_map/hcts,hcte->hcse/dot_general | solution.py:124
  44.9 1.5 %select_convert_fusion = bf16[8,256,256]{2,1,0:T(8,128)(2,1)} fusion(bf16[8,256,128]{1,2,0:T(8,128)(2,1)S(1)} %divide_convert_fusion, pred[256,256]{1,0:T(8,128)(4,1)S(1)} %copy-done.19, bf16[256,8,128]{2,1,0:T(8,128)(2,1)S(1)} %bitcast.175), kind=kOutput, calls=%fused_computation | convolution fusion | flops 135266304 | bytes 2162688 | tf_op jit(solution)/shard_map/hcte,hcse->hcts/dot_general | solution.py:108
  47.2 1.4 %collective-permute-start.10 = (f32[2,128,128]{2,1,0:T(8,128)}, f32[2,128,128]{2,1,0:T(8,128)S(1)}, u32[]{:S(2)}, u32[]{:S(2)}) collective-permute-start(f32[2,128,128]{2,1,0:T(8,128)} %bitcast.33), channel_id=1, source_target_pairs={{0,6},{2,4},{4,2},{6,0},{8,14},{10,12},{12,10},{14,8},{16,22},{18,... | collective-permute-start | bytes 393224 | tf_op jit(solution)/shard_map/ppermute | solution.py:26
  49.4 1.2 collective-permute-start.8
  52.2 2.7 %fusion.21 = f32[8,256,128]{1,2,0:T(8,128)} fusion(bf16[8,256,256]{2,1,0:T(8,128)(2,1)} %select_convert_fusion, bf16[8,256,128]{2,0,1:T(8,128)(2,1)S(1)} %bitcast.179), kind=kOutput, calls=%fused_computation.39 | convolution fusion | flops 134217728 | bytes 2621440 | tf_op jit(solution)/shard_map/hcts,hcsd->hctd/dot_general | solution.py:112
  55.0 1.5 %collective-permute-done.9 = f32[2,128,128]{2,1,0:T(8,128)S(1)} collective-permute-done((f32[2,128,128]{2,1,0:T(8,128)}, f32[2,128,128]{2,1,0:T(8,128)S(1)}, u32[]{:S(2)}, u32[]{:S(2)}) %collective-permute-start.9) | collective-permute-done | bytes 131104 | tf_op jit(solution)/shard_map/ppermute | solution.py:26
  56.6 1.3 %collective-permute-start.11 = (f32[2,128,128]{2,1,0:T(8,128)S(1)}, f32[2,128,128]{2,1,0:T(8,128)S(1)}, u32[]{:S(2)}, u32[]{:S(2)}) collective-permute-start(f32[2,128,128]{2,1,0:T(8,128)S(1)} %fusion.33), channel_id=1, source_target_pairs={{8,0},{10,2},{12,4},{14,6},{16,8},{18,10},{20,12},{22,14},{24,16},... | collective-permute-start | bytes 393224 | tf_op jit(solution)/shard_map/ppermute | solution.py:41
  57.9 2.6 %convolution_bitcast_fusion.4 = f32[256,8,128]{0,2,1:T(8,128)} fusion(bf16[8,256,256]{2,1,0:T(8,128)(2,1)} %select_convert_fusion, bf16[8,256,128]{2,0,1:T(8,128)(2,1)S(1)} %bitcast.184), kind=kOutput, calls=%fused_computation.10 | convolution fusion | flops 134217728 | bytes 2621440 | tf_op jit(solution)/shard_map/hcts,hctd->hcsd/dot_general | solution.py:118
  60.5 4.6 %collective-permute-done.11 = f32[2,128,128]{2,1,0:T(8,128)S(1)} collective-permute-done((f32[2,128,128]{2,1,0:T(8,128)S(1)}, f32[2,128,128]{2,1,0:T(8,128)S(1)}, u32[]{:S(2)}, u32[]{:S(2)}) %collective-permute-start.11) | collective-permute-done | bytes 131104 | tf_op jit(solution)/shard_map/ppermute | solution.py:41
  65.2 1.3 %collective-permute-start.12 = (f32[2,128,128]{2,1,0:T(8,128)S(1)}, f32[2,128,128]{2,1,0:T(8,128)S(1)}, u32[]{:S(2)}, u32[]{:S(2)}) collective-permute-start(f32[2,128,128]{2,1,0:T(8,128)S(1)} %add.209), channel_id=1, source_target_pairs={{16,0},{18,2},{20,4},{22,6},{24,8},{26,10},{28,12},{30,14},{17,1},... | collective-permute-start | bytes 393224 | tf_op jit(solution)/shard_map/ppermute | solution.py:41
  66.8 1.0 copy.29
  67.8 40.4 %psum.7 = f32[1024]{0:T(1024)S(1)} all-reduce(f32[1024]{0:T(1024)S(1)} %bitcast.206), channel_id=1, replica_groups=mesh['seq'=16,'dp'=2] {'seq','dp'}, use_global_device_ids=true, to_apply=%region_3.4 | all-reduce | flops 1024 | bytes 8192 | tf_op jit(solution)/shard_map/psum | solution.py:130
  108.4 2.3 %collective-permute-start.13 = (f32[2,128,128]{2,1,0:T(8,128)S(1)}, f32[2,128,128]{2,1,0:T(8,128)S(1)}, u32[]{:S(2)}, u32[]{:S(2)}) collective-permute-start(f32[2,128,128]{2,1,0:T(8,128)S(1)} %get-tuple-element.32), channel_id=1, source_target_pairs={{0,2},{2,0},{4,6},{6,4},{8,10},{10,8},{12,14},{14,12},{16,18},{18,... | collective-permute-start | bytes 393224 | tf_op jit(solution)/shard_map/ppermute | solution.py:26
  112.9 2.0 %collective-permute-done.13 = f32[2,128,128]{2,1,0:T(8,128)S(1)} collective-permute-done((f32[2,128,128]{2,1,0:T(8,128)S(1)}, f32[2,128,128]{2,1,0:T(8,128)S(1)}, u32[]{:S(2)}, u32[]{:S(2)}) %collective-permute-start.13) | collective-permute-done | bytes 131104 | tf_op jit(solution)/shard_map/ppermute | solution.py:26
  114.9 2.9 %collective-permute-done.14 = f32[2,128,128]{2,1,0:T(8,128)S(1)} collective-permute-done((f32[2,128,128]{2,1,0:T(8,128)S(1)}, f32[2,128,128]{2,1,0:T(8,128)S(1)}, u32[]{:S(2)}, u32[]{:S(2)}) %collective-permute-start.14) | collective-permute-done | bytes 131104 | tf_op jit(solution)/shard_map/ppermute | solution.py:26
  119.6 1.0 copy.31
  (92 shorter events, 16.6 us)
Async XLA Ops:
  2.3 14.4 %copy-start.13 = (bf16[1,256,1024]{2,1,0:T(8,128)(2,1)S(1)}, bf16[1,256,1024]{2,1,0:T(8,128)(2,1)}, u32[]{:S(2)}) copy-start(bf16[1,256,1024]{2,1,0:T(8,128)(2,1)} %param.5) | copy-start | bytes 1572868
  2.4 6.9 %collective-permute-start = (f32[2,128,128]{2,1,0:T(8,128)S(1)}, f32[2,128,128]{2,1,0:T(8,128)S(1)}, u32[]{:S(2)}, u32[]{:S(2)}) collective-permute-start(f32[2,128,128]{2,1,0:T(8,128)S(1)} %get-tuple-element.29), channel_id=1, source_target_pairs={{0,2},{2,0},{4,6},{6,4},{8,10},{10,8},{12,14},{14,12},{16,18},{18,... | collective-permute-start | bytes 393224 | tf_op jit(solution)/shard_map/ppermute | solution.py:26
  5.4 7.8 %collective-permute-start.1 = (f32[2,128,128]{2,1,0:T(8,128)S(1)}, f32[2,128,128]{2,1,0:T(8,128)S(1)}, u32[]{:S(2)}, u32[]{:S(2)}) collective-permute-start(f32[2,128,128]{2,1,0:T(8,128)S(1)} %get-tuple-element.31), channel_id=1, source_target_pairs={{0,4},{2,6},{4,0},{6,2},{8,12},{10,14},{12,8},{14,10},{16,20},{18,... | collective-permute-start | bytes 393224 | tf_op jit(solution)/shard_map/ppermute | solution.py:26
  6.9 6.3 %collective-permute-start.2 = (f32[2,128,128]{2,1,0:T(8,128)S(1)}, f32[2,128,128]{2,1,0:T(8,128)S(1)}, u32[]{:S(2)}, u32[]{:S(2)}) collective-permute-start(f32[2,128,128]{2,1,0:T(8,128)S(1)} %get-tuple-element.30), channel_id=1, source_target_pairs={{0,6},{2,4},{4,2},{6,0},{8,14},{10,12},{12,10},{14,8},{16,22},{18,... | collective-permute-start | bytes 393224 | tf_op jit(solution)/shard_map/ppermute | solution.py:26
  13.2 6.0 %collective-permute-start.3 = (f32[2,128,128]{2,1,0:T(8,128)S(1)}, f32[2,128,128]{2,1,0:T(8,128)S(1)}, u32[]{:S(2)}, u32[]{:S(2)}) collective-permute-start(f32[2,128,128]{2,1,0:T(8,128)S(1)} %fusion.44), channel_id=1, source_target_pairs={{0,8},{2,10},{4,12},{6,14},{8,16},{10,18},{12,20},{14,22},{16,24},... | collective-permute-start | bytes 393224 | tf_op jit(solution)/shard_map/ppermute | solution.py:41
  16.8 9.1 %copy-start.18 = (pred[256,256]{1,0:T(8,128)(4,1)}, pred[256,256]{1,0:T(8,128)(4,1)S(1)}, u32[]{:S(2)}) copy-start(pred[256,256]{1,0:T(8,128)(4,1)S(1)} %iota_compare_fusion) | copy-start | bytes 196612
  19.2 6.7 %copy-start.14 = (f32[2,128,128]{2,1,0:T(8,128)}, f32[2,128,128]{2,1,0:T(8,128)S(1)}, u32[]{:S(2)}) copy-start(f32[2,128,128]{2,1,0:T(8,128)S(1)} %collective-permute-done.3) | copy-start | bytes 393220
  19.9 8.2 %collective-permute-start.4 = (f32[2,128,128]{2,1,0:T(8,128)}, f32[2,128,128]{2,1,0:T(8,128)}, u32[]{:S(2)}, u32[]{:S(2)}) collective-permute-start(f32[2,128,128]{2,1,0:T(8,128)} %add.187), channel_id=1, source_target_pairs={{0,16},{2,18},{4,20},{6,22},{8,24},{10,26},{12,28},{14,30},{1,17},... | collective-permute-start | bytes 393224 | tf_op jit(solution)/shard_map/ppermute | solution.py:41
  26.4 9.1 %copy-start.1 = (bf16[8,256,256]{2,1,0:T(8,128)(2,1)}, bf16[8,256,256]{2,1,0:T(8,128)(2,1)S(1)}, u32[]{:S(2)}) copy-start(bf16[8,256,256]{2,1,0:T(8,128)(2,1)S(1)} %select_convert_fusion.1) | copy-start | bytes 3145732
  30.5 6.2 %collective-permute-start.5 = (f32[2,128,128]{2,1,0:T(8,128)}, f32[2,128,128]{2,1,0:T(8,128)S(1)}, u32[]{:S(2)}, u32[]{:S(2)}) collective-permute-start(f32[2,128,128]{2,1,0:T(8,128)} %get-tuple-element.14), channel_id=1, source_target_pairs={{0,2},{2,0},{4,6},{6,4},{8,10},{10,8},{12,14},{14,12},{16,18},{18,... | collective-permute-start | bytes 393224 | tf_op jit(solution)/shard_map/ppermute | solution.py:26
  31.8 5.2 %collective-permute-start.6 = (f32[2,128,128]{2,1,0:T(8,128)}, f32[2,128,128]{2,1,0:T(8,128)S(1)}, u32[]{:S(2)}, u32[]{:S(2)}) collective-permute-start(f32[2,128,128]{2,1,0:T(8,128)} %get-tuple-element.15), channel_id=1, source_target_pairs={{0,4},{2,6},{4,0},{6,2},{8,12},{10,14},{12,8},{14,10},{16,20},{18,... | collective-permute-start | bytes 393224 | tf_op jit(solution)/shard_map/ppermute | solution.py:26
  32.6 6.2 %collective-permute-start.7 = (f32[2,128,128]{2,1,0:T(8,128)}, f32[2,128,128]{2,1,0:T(8,128)}, u32[]{:S(2)}, u32[]{:S(2)}) collective-permute-start(f32[2,128,128]{2,1,0:T(8,128)} %get-tuple-element.16), channel_id=1, source_target_pairs={{0,6},{2,4},{4,2},{6,0},{8,14},{10,12},{12,10},{14,8},{16,22},{18,... | collective-permute-start | bytes 393224 | tf_op jit(solution)/shard_map/ppermute | solution.py:26
  35.5 3.3 %copy-start.17 = (f32[1,2,128,128]{3,2,1,0:T(8,128)S(1)}, f32[1,2,128,128]{3,2,1,0:T(8,128)}, u32[]{:S(2)}) copy-start(f32[1,2,128,128]{3,2,1,0:T(8,128)} %get-tuple-element.12) | copy-start | bytes 393220
  43.6 1.3 %copy-start.19 = (pred[256,256]{1,0:T(8,128)(4,1)S(1)}, pred[256,256]{1,0:T(8,128)(4,1)}, u32[]{:S(2)}) copy-start(pred[256,256]{1,0:T(8,128)(4,1)} %copy-done.18) | copy-start | bytes 196612
  47.2 7.8 %collective-permute-start.10 = (f32[2,128,128]{2,1,0:T(8,128)}, f32[2,128,128]{2,1,0:T(8,128)S(1)}, u32[]{:S(2)}, u32[]{:S(2)}) collective-permute-start(f32[2,128,128]{2,1,0:T(8,128)} %bitcast.33), channel_id=1, source_target_pairs={{0,6},{2,4},{4,2},{6,0},{8,14},{10,12},{12,10},{14,8},{16,22},{18,... | collective-permute-start | bytes 393224 | tf_op jit(solution)/shard_map/ppermute | solution.py:26
  49.4 5.6 %collective-permute-start.8 = (f32[2,128,128]{2,1,0:T(8,128)}, f32[2,128,128]{2,1,0:T(8,128)S(1)}, u32[]{:S(2)}, u32[]{:S(2)}) collective-permute-start(f32[2,128,128]{2,1,0:T(8,128)} %bitcast.31), channel_id=1, source_target_pairs={{0,2},{2,0},{4,6},{6,4},{8,10},{10,8},{12,14},{14,12},{16,18},{18,... | collective-permute-start | bytes 393224 | tf_op jit(solution)/shard_map/ppermute | solution.py:26
  51.4 5.2 %collective-permute-start.9 = (f32[2,128,128]{2,1,0:T(8,128)}, f32[2,128,128]{2,1,0:T(8,128)S(1)}, u32[]{:S(2)}, u32[]{:S(2)}) collective-permute-start(f32[2,128,128]{2,1,0:T(8,128)} %bitcast.32), channel_id=1, source_target_pairs={{0,4},{2,6},{4,0},{6,2},{8,12},{10,14},{12,8},{14,10},{16,20},{18,... | collective-permute-start | bytes 393224 | tf_op jit(solution)/shard_map/ppermute | solution.py:26
  55.0 5.5 %copy-start.6 = (f32[2,128,128]{2,1,0:T(8,128)}, f32[2,128,128]{2,1,0:T(8,128)S(1)}, u32[]{:S(2)}) copy-start(f32[2,128,128]{2,1,0:T(8,128)S(1)} %collective-permute-done.10) | copy-start | bytes 393220
  55.0 5.5 %copy-start.8 = (f32[2,128,128]{2,1,0:T(8,128)}, f32[2,128,128]{2,1,0:T(8,128)S(1)}, u32[]{:S(2)}) copy-start(f32[2,128,128]{2,1,0:T(8,128)S(1)} %collective-permute-done.8) | copy-start | bytes 393220
  56.5 4.0 %copy-start.10 = (f32[2,128,128]{2,1,0:T(8,128)}, f32[2,128,128]{2,1,0:T(8,128)S(1)}, u32[]{:S(2)}) copy-start(f32[2,128,128]{2,1,0:T(8,128)S(1)} %collective-permute-done.9) | copy-start | bytes 393220
  56.6 8.6 %collective-permute-start.11 = (f32[2,128,128]{2,1,0:T(8,128)S(1)}, f32[2,128,128]{2,1,0:T(8,128)S(1)}, u32[]{:S(2)}, u32[]{:S(2)}) collective-permute-start(f32[2,128,128]{2,1,0:T(8,128)S(1)} %fusion.33), channel_id=1, source_target_pairs={{8,0},{10,2},{12,4},{14,6},{16,8},{18,10},{20,12},{22,14},{24,16},... | collective-permute-start | bytes 393224 | tf_op jit(solution)/shard_map/ppermute | solution.py:41
  57.9 8.6 %copy-start.4 = (f32[8,256,128]{1,2,0:T(8,128)S(1)}, f32[8,256,128]{1,2,0:T(8,128)}, u32[]{:S(2)}) copy-start(f32[8,256,128]{1,2,0:T(8,128)} %fusion.21) | copy-start | bytes 3145732
  65.1 1.6 %copy-start.15 = (f32[2,128,128]{2,1,0:T(8,128)}, f32[2,128,128]{2,1,0:T(8,128)S(1)}, u32[]{:S(2)}) copy-start(f32[2,128,128]{2,1,0:T(8,128)S(1)} %collective-permute-done.11) | copy-start | bytes 393220
  65.2 43.1 %collective-permute-start.12 = (f32[2,128,128]{2,1,0:T(8,128)S(1)}, f32[2,128,128]{2,1,0:T(8,128)S(1)}, u32[]{:S(2)}, u32[]{:S(2)}) collective-permute-start(f32[2,128,128]{2,1,0:T(8,128)S(1)} %add.209), channel_id=1, source_target_pairs={{16,0},{18,2},{20,4},{22,6},{24,8},{26,10},{28,12},{30,14},{17,1},... | collective-permute-start | bytes 393224 | tf_op jit(solution)/shard_map/ppermute | solution.py:41
  66.8 41.5 %copy-start.7 = (f32[2,128,128]{2,1,0:T(8,128)S(1)}, f32[2,128,128]{2,1,0:T(8,128)}, u32[]{:S(2)}) copy-start(f32[2,128,128]{2,1,0:T(8,128)} %copy-done.6) | copy-start | bytes 393220
  66.8 41.5 %copy-start.9 = (f32[2,128,128]{2,1,0:T(8,128)S(1)}, f32[2,128,128]{2,1,0:T(8,128)}, u32[]{:S(2)}) copy-start(f32[2,128,128]{2,1,0:T(8,128)} %copy-done.8) | copy-start | bytes 393220
  66.8 41.5 %copy-start.11 = (f32[2,128,128]{2,1,0:T(8,128)S(1)}, f32[2,128,128]{2,1,0:T(8,128)}, u32[]{:S(2)}) copy-start(f32[2,128,128]{2,1,0:T(8,128)} %copy-done.10) | copy-start | bytes 393220
  66.8 41.5 %copy-start.16 = (f32[2,128,128]{2,1,0:T(8,128)S(1)}, f32[2,128,128]{2,1,0:T(8,128)}, u32[]{:S(2)}) copy-start(f32[2,128,128]{2,1,0:T(8,128)} %copy-done.15) | copy-start | bytes 393220
  108.4 6.5 %collective-permute-start.13 = (f32[2,128,128]{2,1,0:T(8,128)S(1)}, f32[2,128,128]{2,1,0:T(8,128)S(1)}, u32[]{:S(2)}, u32[]{:S(2)}) collective-permute-start(f32[2,128,128]{2,1,0:T(8,128)S(1)} %get-tuple-element.32), channel_id=1, source_target_pairs={{0,2},{2,0},{4,6},{6,4},{8,10},{10,8},{12,14},{14,12},{16,18},{18,... | collective-permute-start | bytes 393224 | tf_op jit(solution)/shard_map/ppermute | solution.py:26
  110.7 7.1 %collective-permute-start.14 = (f32[2,128,128]{2,1,0:T(8,128)S(1)}, f32[2,128,128]{2,1,0:T(8,128)S(1)}, u32[]{:S(2)}, u32[]{:S(2)}) collective-permute-start(f32[2,128,128]{2,1,0:T(8,128)S(1)} %get-tuple-element.33), channel_id=1, source_target_pairs={{0,4},{2,6},{4,0},{6,2},{8,12},{10,14},{12,8},{14,10},{16,20},{18,... | collective-permute-start | bytes 393224 | tf_op jit(solution)/shard_map/ppermute | solution.py:26
  111.4 6.4 %collective-permute-start.15 = (f32[2,128,128]{2,1,0:T(8,128)S(1)}, f32[2,128,128]{2,1,0:T(8,128)S(1)}, u32[]{:S(2)}, u32[]{:S(2)}) collective-permute-start(f32[2,128,128]{2,1,0:T(8,128)S(1)} %get-tuple-element.34), channel_id=1, source_target_pairs={{0,6},{2,4},{4,2},{6,0},{8,14},{10,12},{12,10},{14,8},{16,22},{18,... | collective-permute-start | bytes 393224 | tf_op jit(solution)/shard_map/ppermute | solution.py:26
  119.6 1.4 %copy-start.3 = (f32[256,8,128]{0,2,1:T(8,128)S(1)}, f32[256,8,128]{0,2,1:T(8,128)}, u32[]{:S(2)}) copy-start(f32[256,8,128]{0,2,1:T(8,128)} %convolution_bitcast_fusion.4) | copy-start | bytes 3145732
  (5 other events, 5.6 us)

commit v2 on v0

--- a/solution.py
+++ b/solution.py
@@ -13,22 +13,38 @@
 EPSILON = 1e-06
 
 
-def carried_in(part, axis, combine, identity, reverse):
+def carried_in(part, axis, reverse):
     count = lax.axis_size(axis)
     place = lax.axis_index(axis)
-    ahead = count - 1 - place if reverse else place
-    gathered = lax.all_gather(part, axis)
-    state = jnp.zeros_like(part) + jnp.asarray(identity, part.dtype)
+    group = math.gcd(count, HEADS)
+    owned = HEADS // group
+    rows = part.shape[1]
+    teams = [list(range(first, first + group)) for first in range(0, count, group)]
 
-    def one(hop, state):
-        source = count - 1 - hop if reverse else hop
-        return combine(state, lax.dynamic_index_in_dim(gathered, source, 0, False))
+    def spread(array):
+        return lax.all_to_all(array, axis, 0, 0, axis_index_groups=teams)
 
-    return lax.fori_loop(0, ahead, one, state)
-
-
-def add_states(earlier, later):
-    return earlier + later
+    held = spread(part.reshape(group, owned, rows, DH))
+    order = range(group - 1, -1, -1) if reverse else range(group)
+    total = jnp.zeros_like(held[0])
+    ahead = [None] * group
+    for member in order:
+        ahead[member] = total
+        total = total + held[member]
+    carried = jnp.zeros_like(total)
+    mask = group
+    while mask < count:
+        arrived = lax.ppermute(total, axis, [(s, s ^ mask) for s in range(count)])
+        later = (place & mask) != 0
+        carried = carried + jnp.where(later != reverse, arrived, 0.0)
+        total = total + arrived
+        mask *= 2
+    summed = jnp.stack([ahead[member] + carried for member in range(group)])
+    if rows > DH:
+        summed = jnp.concatenate(
+            [summed[:, :, :DH], jnp.broadcast_to(total[:, DH:], (group, owned, rows - DH, DH))], axis=2
+        )
+    return spread(summed).reshape(part.shape)
 
 
 def head_major(array, blocks_dev):
@@ -60,7 +76,7 @@
         "hcsd,hcse->hcde", key_blocks, value_blocks, preferred_element_type=jnp.float32
     )
     local_total = jnp.sum(deltas, axis=1)
-    carried = carried_in(local_total, "seq", add_states, jnp.zeros_like(local_total), False)
+    carried = carried_in(local_total, "seq", False)
     prefix_state = (carried[:, None] + jnp.cumsum(deltas, axis=1) - deltas).astype(jnp.bfloat16)
     attention = jnp.einsum(
         "hcts,hcse->hcte", scores_low, value_blocks, preferred_element_type=jnp.float32
@@ -81,7 +97,15 @@
     )
     grad_total = jnp.sum(grad_deltas, axis=1)
     after_local = grad_total[:, None] - jnp.cumsum(grad_deltas, axis=1)
-    later_sum = carried_in(grad_total, "seq", add_states, jnp.zeros_like(grad_total), True)
+    extra = jnp.broadcast_to(gain_terms.reshape(HEADS, 1, DH), (HEADS, 8, DH))
+    later_all = carried_in(jnp.concatenate([grad_total, extra], axis=1), "seq", True)
+    later_sum = later_all[:, :DH]
+    gain_total = later_all[:, DH].reshape(-1)
+    mask = 1
+    while mask < lax.axis_size("dp"):
+        pairs = [(d, d ^ mask) for d in range(lax.axis_size("dp"))]
+        gain_total = gain_total + lax.ppermute(gain_total, "dp", pairs)
+        mask *= 2
     grad_state = (later_sum[:, None] + after_local).astype(jnp.bfloat16)
     raw_grad = jnp.einsum(
         "hcte,hcse->hcts", grad_attn, value_blocks, preferred_element_type=jnp.float32
@@ -105,7 +129,6 @@
     grad_value = grad_value + jnp.einsum(
         "hcsd,hcde->hcse", key_blocks, grad_state, preferred_element_type=jnp.float32
     )
-    gain_total = lax.psum(gain_terms, ("seq", "dp"))
     position_count = lax.axis_size("seq") * lax.axis_size("dp") * seq_rows
     grad_gain = gain_total / math.sqrt(position_count)
     return (

time: 294 us -> 83.3 us (0.28)
  waiting for transfers between devices: 182 us -> 19.4 us
  blocking collectives: 55.3 us -> 15.4 us
  starting transfers between devices: 0.08 us -> 16.1 us
  between operations: 14.3 us -> 0.92 us
  other arithmetic: 21.1 us -> 10.7 us
    all_gather x2 -> x0, waiting for transfers between devices: 182 us -> none  [carried_in(): gathered = lax.all_gather(part, axis)]
    psum x1 -> x0, blocking collectives: 55.3 us -> none  [local(): gain_total = lax.psum(gain_terms, ('seq', 'dp'))]
    add x15 -> x2, other arithmetic: 17.5 us -> 0.06 us  [carried_in(): total = total + held[member]]
    all_to_all x0 -> x1, blocking collectives: none -> 15.4 us  [spread(): return lax.all_to_all(array, axis, 0, 0, axis_index_groups=teams)]
    all_to_all x0 -> x3, waiting for transfers between devices: none -> 13.2 us  [spread(): return lax.all_to_all(array, axis, 0, 0, axis_index_groups=teams)]
    all_to_all x0 -> x3, starting transfers between devices: none -> 11.9 us  [spread(): return lax.all_to_all(array, axis, 0, 0, axis_index_groups=teams)]
    ppermute x0 -> x3, waiting for transfers between devices: none -> 6.15 us  [the longest x2 6.15 us: carried_in(): arrived = lax.ppermute(total, axis, [(s, s ^ mask) for s in range(count)])]
    unnamed x0 -> x14, other arithmetic: none -> 4.6 us
  transfers between devices with their start and end apart: 2 -> 6, of which waited for: 2 -> 5; matrix products, arithmetic and copies ran while one was open for 3% -> 17% of each run, Pallas kernels for 0% -> 0%
where the time goes in v2:
time: 83.3 us; the launch traced here: 82.6 us
  waiting for transfers between devices  19.4 us (23%)
  starting transfers between devices  16.1 us (19%)
  blocking collectives  15.4 us (18%)
  local copies, waits for them, and re-layouts  10.8 us (13%)
  other arithmetic  10.7 us (13%)
  matrix products  9.28 us (11%)
  between operations  0.92 us (1%)
    all_to_all x1, blocking collectives, spread(): return lax.all_to_all(array, axis, 0, 0, axis_index_groups=teams)  15.4 us
    all_to_all x3, waiting for transfers between devices, spread(): return lax.all_to_all(array, axis, 0, 0, axis_index_groups=teams)  13.2 us
    all_to_all x3, starting transfers between devices, spread(): return lax.all_to_all(array, axis, 0, 0, axis_index_groups=teams)  11.9 us
    unnamed x29, local copies, waits for them, and re-layouts  8.55 us
    ppermute x2, waiting for transfers between devices, carried_in(): arrived = lax.ppermute(total, axis, [(s, s ^ mask) for s in range(count)])  6.15 us
    unnamed x14, other arithmetic  4.6 us
    ppermute x2, starting transfers between devices, carried_in(): arrived = lax.ppermute(total, axis, [(s, s ^ mask) for s in range(count)])  4.28 us
  transfers between devices with their start and end apart: 6, of which 5 were waited for; matrix products, arithmetic and copies ran while one was open for 17% of the time, Pallas kernels for 0%

profile of v2, /device:TPU:0, one launch (start us, length us, event | category | flops | bytes accessed | tf_op | source)
XLA Modules:
  0.0 82.6 jit_solution(5891309777056080428)
XLA Ops:
  0.6 1.2 %copy.110 = bf16[32,8,8,128]{3,2,1,0:T(8,128)(2,1)S(1)} copy(bf16[32,8,8,128]{3,1,2,0:T(8,128)(2,1)} %bitcast.271) | data formatting | bytes 1048576
  2.3 15.4 %all_to_all.20 = f32[8,1,128,128]{3,2,1,0:T(8,128)S(1)} all-to-all(f32[8,1,128,128]{3,2,1,0:T(8,128)S(1)} %bitcast.267), channel_id=1, replica_groups={{0,2,4,6,8,10,12,14},{16,18,20,22,24,26,28,30},{1,3,5,7,9,11,13,15},{17..., dimensions={0} | all-to-all | bytes 1048576 | tf_op jit(solution)/shard_map/all_to_all | solution.py:25
  17.7 2.7 %collective-permute-start = (f32[1,128,128]{2,1,0:T(8,128)S(1)}, f32[1,128,128]{2,1,0:T(8,128)S(1)}, u32[]{:S(2)}, u32[]{:S(2)}) collective-permute-start(f32[1,128,128]{2,1,0:T(8,128)S(1)} %get-tuple-element.21), channel_id=1, source_target_pairs={{0,16},{2,18},{4,20},{6,22},{8,24},{10,26},{12,28},{14,30},{16,0},... | collective-permute-start | bytes 196616 | tf_op jit(solution)/shard_map/ppermute | solution.py:37
  20.4 3.3 %collective-permute-done = f32[1,128,128]{2,1,0:T(8,128)S(1)} collective-permute-done((f32[1,128,128]{2,1,0:T(8,128)S(1)}, f32[1,128,128]{2,1,0:T(8,128)S(1)}, u32[]{:S(2)}, u32[]{:S(2)}) %collective-permute-start) | collective-permute-done | bytes 65568 | tf_op jit(solution)/shard_map/ppermute | solution.py:37
  24.9 0.6 bitcast_dynamic-update-slice_fusion.13
  25.6 0.6 bitcast_dynamic-update-slice_fusion.12
  26.9 0.6 bitcast_dynamic-update-slice_fusion.10
  28.8 4.1 %all-to-all-start.1 = ((f32[8,1,128,128]{3,2,1,0:T(8,128)}), f32[8,1,128,128]{3,2,1,0:T(8,128)}, u32[]{:S(2)}, u32[]{:S(2)}) async-start(f32[8,1,128,128]{3,2,1,0:T(8,128)} %bitcast_dynamic-update-slice_fusion.8), calls=%async_computation.1 | async-start | bytes 1048576 | tf_op jit(solution)/shard_map/all_to_all | solution.py:25
  33.2 1.2 %copy.73 = f32[1,256,1024]{1,2,0:T(8,128)S(1)} copy(bf16[1,256,1024]{2,1,0:T(8,128)(2,1)} %param.9) | data formatting | bytes 1572864 | tf_op jit(solution)/shard_map/convert_element_type | solution.py:89
  35.0 1.0 %copy-done.2 = bf16[8,256,256]{2,1,0:T(8,128)(2,1)} copy-done((bf16[8,256,256]{2,1,0:T(8,128)(2,1)}, bf16[8,256,256]{2,1,0:T(8,128)(2,1)S(1)}, u32[]{:S(2)}) %copy-start.2) | copy-done | bytes 1048600
  35.9 1.5 %fusion.8 = f32[8,256,128]{1,2,0:T(8,128)} fusion(bf16[8,256,256]{2,1,0:T(8,128)(2,1)S(1)} %select_convert_fusion.1, bf16[8,256,128]{2,0,1:T(8,128)(2,1)S(1)} %bitcast.256), kind=kOutput, calls=%fused_computation.25 | convolution fusion | flops 134217728 | bytes 2621440 | tf_op jit(solution)/shard_map/hcts,hcse->hcte/dot_general | solution.py:81
  37.4 3.2 %all-to-all-done.1 = f32[8,1,128,128]{3,2,1,0:T(8,128)} async-done(((f32[8,1,128,128]{3,2,1,0:T(8,128)}), f32[8,1,128,128]{3,2,1,0:T(8,128)}, u32[]{:S(2)}, u32[]{:S(2)}) %all-to-all-start.1) | async-done | bytes 524320 | tf_op jit(solution)/shard_map/all_to_all | solution.py:25
  40.6 1.2 %fusion.24 = bf16[8,128,128]{2,1,0:T(8,128)(2,1)S(1)} fusion(f32[8,128,128]{2,1,0:T(8,128)S(1)} %fusion.11, f32[8,1,128,128]{3,2,1,0:T(8,128)} %all-to-all-done.1), kind=kLoop, calls=%fused_computation.42 | loop fusion | flops 393216 | bytes 1310720 | tf_op jit(solution)/shard_map/reshape.15
  43.8 0.8 copy-done
  44.5 0.9 %maximum_bitcast_fusion = f32[8,1,136,128]{3,2,1,0:T(8,128)} fusion(f32[8,8,128]{2,1,0:T(8,128)S(1)} %broadcast_in_dim.35, f32[8,128,128]{2,1,0:T(8,128)S(1)} %convolution_bitcast_fusion.5), kind=kLoop, calls=%fused_computation.20 | loop fusion | flops 139264 | bytes 1114112 | tf_op jit(solution)/shard_map/reshape | solution.py:27
  45.4 3.5 %all-to-all-start.2 = ((f32[8,1,136,128]{3,2,1,0:T(8,128)}), f32[8,1,136,128]{3,2,1,0:T(8,128)S(1)}, u32[]{:S(2)}, u32[]{:S(2)}) async-start(f32[8,1,136,128]{3,2,1,0:T(8,128)} %maximum_bitcast_fusion), calls=%async_computation.2 | async-start | bytes 1114112 | tf_op jit(solution)/shard_map/all_to_all | solution.py:25
  49.0 8.5 %all-to-all-done.2 = f32[8,1,136,128]{3,2,1,0:T(8,128)S(1)} async-done(((f32[8,1,136,128]{3,2,1,0:T(8,128)}), f32[8,1,136,128]{3,2,1,0:T(8,128)S(1)}, u32[]{:S(2)}, u32[]{:S(2)}) %all-to-all-start.2) | async-done | bytes 557088 | tf_op jit(solution)/shard_map/all_to_all | solution.py:25
  57.5 1.6 %collective-permute-start.1 = (f32[1,136,128]{2,1,0:T(8,128)S(1)}, f32[1,136,128]{2,1,0:T(8,128)S(1)}, u32[]{:S(2)}, u32[]{:S(2)}) collective-permute-start(f32[1,136,128]{2,1,0:T(8,128)S(1)} %get-tuple-element.18), channel_id=1, source_target_pairs={{0,16},{2,18},{4,20},{6,22},{8,24},{10,26},{12,28},{14,30},{16,0},... | collective-permute-start | bytes 208904 | tf_op jit(solution)/shard_map/ppermute | solution.py:37
  59.1 1.5 %select_convert_fusion = bf16[8,256,256]{2,1,0:T(8,128)(2,1)} fusion(bf16[8,256,128]{1,2,0:T(8,128)(2,1)S(1)} %divide_convert_fusion, pred[256,256]{1,0:T(8,128)(4,1)S(1)} %iota_compare_fusion, bf16[256,8,128]{2,1,0:T(8,128)(2,1)S(1)} %bitcast.257), kind=kOutput, calls=%fused_computation | convolution fusion | flops 135266304 | bytes 2162688 | tf_op jit(solution)/shard_map/hcte,hcse->hcts/dot_general | solution.py:110
  60.6 2.9 %collective-permute-done.1 = f32[1,136,128]{2,1,0:T(8,128)S(1)} collective-permute-done((f32[1,136,128]{2,1,0:T(8,128)S(1)}, f32[1,136,128]{2,1,0:T(8,128)S(1)}, u32[]{:S(2)}, u32[]{:S(2)}) %collective-permute-start.1) | collective-permute-done | bytes 69664 | tf_op jit(solution)/shard_map/ppermute | solution.py:37
  63.7 0.9 %pad_maximum_fusion = f32[8,1,136,128]{3,2,1,0:T(8,128)} fusion(f32[8,1,8,128]{3,2,1,0:T(8,128)S(1)} %broadcast_in_dim.37, f32[8,1,128,128]{3,2,1,0:T(8,128)S(1)} %slice.99), kind=kLoop, calls=%fused_computation.21 | loop fusion | flops 139264 | bytes 1114112 | tf_op jit(solution)/shard_map/concatenate | solution.py:44
  64.6 4.2 %all-to-all-start.3 = ((f32[8,1,136,128]{3,2,1,0:T(8,128)}), f32[8,1,136,128]{3,2,1,0:T(8,128)}, u32[]{:S(2)}, u32[]{:S(2)}) async-start(f32[8,1,136,128]{3,2,1,0:T(8,128)} %pad_maximum_fusion), calls=%async_computation.3 | async-start | bytes 1114112 | tf_op jit(solution)/shard_map/all_to_all | solution.py:25
  69.3 1.1 %fusion.5 = bf16[8,256,128]{1,2,0:T(8,128)(2,1)} fusion(f32[8,256,128]{1,2,0:T(8,128)S(1)} %fusion.16, bf16[8,128,128]{2,1,0:T(8,128)(2,1)S(1)} %fusion.24, bf16[8,256,128]{1,2,0:T(8,128)(2,1)S(1)} %divide_convert_fusion), kind=kOutput, calls=%fused_computation.13 | convolution fusion | flops 67633152 | bytes 2359296 | tf_op jit(solution)/shard_map/hcte,hcde->hctd/dot_general | solution.py:117
  70.3 2.1 %copy.90 = bf16[1,256,1024]{2,1,0:T(8,128)(2,1)} copy(bf16[1,256,1024]{1,2,0:T(8,128)(2,1)} %bitcast.270) | data formatting | bytes 1048576
  72.5 1.3 %convolution_bitcast_fusion.3 = f32[256,8,128]{0,2,1:T(8,128)} fusion(bf16[8,256,128]{1,2,0:T(8,128)(2,1)S(1)} %divide_convert_fusion, bf16[8,256,256]{2,1,0:T(8,128)(2,1)S(1)} %copy-done.3), kind=kOutput, calls=%fused_computation.9 | convolution fusion | flops 134217728 | bytes 2621440 | tf_op jit(solution)/shard_map/hcts,hcte->hcse/dot_general | solution.py:126
  73.8 1.3 %convolution_bitcast_fusion.4 = f32[256,8,128]{0,2,1:T(8,128)} fusion(bf16[8,256,128]{1,2,0:T(8,128)(2,1)S(1)} %bitcast.266, bf16[8,256,256]{2,1,0:T(8,128)(2,1)S(1)} %copy-done.5), kind=kOutput, calls=%fused_computation.10 | convolution fusion | flops 134217728 | bytes 2621440 | tf_op jit(solution)/shard_map/hcts,hctd->hcsd/dot_general | solution.py:120
  75.1 1.5 %all-to-all-done.3 = f32[8,1,136,128]{3,2,1,0:T(8,128)} async-done(((f32[8,1,136,128]{3,2,1,0:T(8,128)}), f32[8,1,136,128]{3,2,1,0:T(8,128)}, u32[]{:S(2)}, u32[]{:S(2)}) %all-to-all-start.3) | async-done | bytes 557088 | tf_op jit(solution)/shard_map/all_to_all | solution.py:25
  76.6 1.1 %fusion.7 = bf16[8,128,128]{2,1,0:T(8,128)(2,1)S(1)} fusion(f32[8,136,128]{2,1,0:T(8,128)} %bitcast.56, f32[8,128,128]{2,1,0:T(8,128)S(1)} %copy-done.1), kind=kLoop, calls=%fused_computation.24 | loop fusion | flops 393216 | bytes 1310720 | tf_op jit(solution)/shard_map/convert_element_type | solution.py:109
  77.7 0.8 slice.103
  78.8 0.9 %copy-done.7 = f32[256,8,128]{0,2,1:T(8,128)S(1)} copy-done((f32[256,8,128]{0,2,1:T(8,128)S(1)}, f32[256,8,128]{0,2,1:T(8,128)}, u32[]{:S(2)}) %copy-start.7) | copy-done | bytes 1048600
  80.0 1.0 %copy.92 = bf16[1,256,1024]{2,1,0:T(8,128)(2,1)} copy(bf16[1,256,1024]{1,2,0:T(8,128)(2,1)S(1)} %bitcast.268) | data formatting | bytes 1048576
  81.0 1.0 %copy.91 = bf16[1,256,1024]{2,1,0:T(8,128)(2,1)} copy(bf16[1,256,1024]{1,2,0:T(8,128)(2,1)S(1)} %bitcast.269) | data formatting | bytes 1048576
  (57 shorter events, 8.3 us)
Async XLA Ops:
  0.6 1.2 %copy-start.9 = (bf16[1,256,1024]{2,1,0:T(8,128)(2,1)S(1)}, bf16[1,256,1024]{2,1,0:T(8,128)(2,1)}, u32[]{:S(2)}) copy-start(bf16[1,256,1024]{2,1,0:T(8,128)(2,1)} %param.7) | copy-start | bytes 1572868
  17.7 5.9 %collective-permute-start = (f32[1,128,128]{2,1,0:T(8,128)S(1)}, f32[1,128,128]{2,1,0:T(8,128)S(1)}, u32[]{:S(2)}, u32[]{:S(2)}) collective-permute-start(f32[1,128,128]{2,1,0:T(8,128)S(1)} %get-tuple-element.21), channel_id=1, source_target_pairs={{0,16},{2,18},{4,20},{6,22},{8,24},{10,26},{12,28},{14,30},{16,0},... | collective-permute-start | bytes 196616 | tf_op jit(solution)/shard_map/ppermute | solution.py:37
  26.2 6.7 %copy-start.10 = (bf16[1,256,1024]{2,1,0:T(8,128)(2,1)S(1)}, bf16[1,256,1024]{2,1,0:T(8,128)(2,1)}, u32[]{:S(2)}) copy-start(bf16[1,256,1024]{2,1,0:T(8,128)(2,1)} %param.5) | copy-start | bytes 1572868
  28.8 11.8 %all-to-all-start.1 = ((f32[8,1,128,128]{3,2,1,0:T(8,128)}), f32[8,1,128,128]{3,2,1,0:T(8,128)}, u32[]{:S(2)}, u32[]{:S(2)}) async-start(f32[8,1,128,128]{3,2,1,0:T(8,128)} %bitcast_dynamic-update-slice_fusion.8), calls=%async_computation.1 | async-start | bytes 1048576 | tf_op jit(solution)/shard_map/all_to_all | solution.py:25
  35.0 1.0 %copy-start.2 = (bf16[8,256,256]{2,1,0:T(8,128)(2,1)}, bf16[8,256,256]{2,1,0:T(8,128)(2,1)S(1)}, u32[]{:S(2)}) copy-start(bf16[8,256,256]{2,1,0:T(8,128)(2,1)S(1)} %select_convert_fusion.1) | copy-start | bytes 3145732
  40.6 1.4 %copy-start.8 = (f32[8,256,128]{1,2,0:T(8,128)S(1)}, f32[8,256,128]{1,2,0:T(8,128)}, u32[]{:S(2)}) copy-start(f32[8,256,128]{1,2,0:T(8,128)} %fusion.8) | copy-start | bytes 3145732
  42.0 0.7 copy-start.11
  43.7 0.8 copy-start
  45.4 12.0 %all-to-all-start.2 = ((f32[8,1,136,128]{3,2,1,0:T(8,128)}), f32[8,1,136,128]{3,2,1,0:T(8,128)S(1)}, u32[]{:S(2)}, u32[]{:S(2)}) async-start(f32[8,1,136,128]{3,2,1,0:T(8,128)} %maximum_bitcast_fusion), calls=%async_computation.2 | async-start | bytes 1114112 | tf_op jit(solution)/shard_map/all_to_all | solution.py:25
  57.5 6.0 %collective-permute-start.1 = (f32[1,136,128]{2,1,0:T(8,128)S(1)}, f32[1,136,128]{2,1,0:T(8,128)S(1)}, u32[]{:S(2)}, u32[]{:S(2)}) collective-permute-start(f32[1,136,128]{2,1,0:T(8,128)S(1)} %get-tuple-element.18), channel_id=1, source_target_pairs={{0,16},{2,18},{4,20},{6,22},{8,24},{10,26},{12,28},{14,30},{16,0},... | collective-permute-start | bytes 208904 | tf_op jit(solution)/shard_map/ppermute | solution.py:37
  63.7 5.1 %copy-start.4 = (bf16[8,256,256]{2,1,0:T(8,128)(2,1)S(1)}, bf16[8,256,256]{2,1,0:T(8,128)(2,1)}, u32[]{:S(2)}) copy-start(bf16[8,256,256]{2,1,0:T(8,128)(2,1)} %select_convert_fusion) | copy-start | bytes 3145732
  64.6 12.0 %all-to-all-start.3 = ((f32[8,1,136,128]{3,2,1,0:T(8,128)}), f32[8,1,136,128]{3,2,1,0:T(8,128)}, u32[]{:S(2)}, u32[]{:S(2)}) async-start(f32[8,1,136,128]{3,2,1,0:T(8,128)} %pad_maximum_fusion), calls=%async_computation.3 | async-start | bytes 1114112 | tf_op jit(solution)/shard_map/all_to_all | solution.py:25
  70.3 2.1 %copy-start.3 = (bf16[8,256,256]{2,1,0:T(8,128)(2,1)S(1)}, bf16[8,256,256]{2,1,0:T(8,128)(2,1)}, u32[]{:S(2)}) copy-start(bf16[8,256,256]{2,1,0:T(8,128)(2,1)} %copy-done.2) | copy-start | bytes 3145732
  72.5 1.3 %copy-start.5 = (bf16[8,256,256]{2,1,0:T(8,128)(2,1)S(1)}, bf16[8,256,256]{2,1,0:T(8,128)(2,1)}, u32[]{:S(2)}) copy-start(bf16[8,256,256]{2,1,0:T(8,128)(2,1)} %select_convert_fusion) | copy-start | bytes 3145732
  73.8 2.8 %copy-start.1 = (f32[8,128,128]{2,1,0:T(8,128)S(1)}, f32[8,128,128]{2,1,0:T(8,128)}, u32[]{:S(2)}) copy-start(f32[8,128,128]{2,1,0:T(8,128)} %copy-done) | copy-start | bytes 1572868
  75.1 3.4 %copy-start.6 = (f32[256,8,128]{0,2,1:T(8,128)S(1)}, f32[256,8,128]{0,2,1:T(8,128)}, u32[]{:S(2)}) copy-start(f32[256,8,128]{0,2,1:T(8,128)} %convolution_bitcast_fusion.3) | copy-start | bytes 3145732
  78.5 1.2 %copy-start.7 = (f32[256,8,128]{0,2,1:T(8,128)S(1)}, f32[256,8,128]{0,2,1:T(8,128)}, u32[]{:S(2)}) copy-start(f32[256,8,128]{0,2,1:T(8,128)} %convolution_bitcast_fusion.4) | copy-start | bytes 3145732
  78.5 3.5 %collective-permute-start.2 = (f32[1024]{0:T(1024)S(1)}, f32[1024]{0:T(1024)S(1)}, u32[]{:S(2)}, u32[]{:S(2)}) collective-permute-start(f32[1024]{0:T(1024)S(1)} %bitcast.275), channel_id=1, source_target_pairs={{0,1},{1,0},{2,3},{3,2},{4,5},{5,4},{6,7},{7,6},{8,9},{9,8},{10,11... | collective-permute-start | bytes 12296 | tf_op jit(solution)/shard_map/ppermute | solution.py:107

commit v3 on v0

v3 whole, which is shorter than its diff:
```python
import functools
import math

import jax
import jax.numpy as jnp
from jax import lax
from jax.experimental import pallas as pl
from jax.experimental.pallas import tpu as pltpu
from jax.sharding import PartitionSpec as P

HEADS = 8
DH = 128
BLOCK = 256
CHAINS = 2
CHAIN_HEADS = HEADS // CHAINS
WIDE = CHAIN_HEADS * DH
GAIN_ROWS = 8
EPSILON = 1e-06

NT = (((1,), (1,)), ((), ()))
TN = (((0,), (0,)), ((), ()))
NN = (((1,), (0,)), ((), ()))


def dot(left, right, dims):
    return lax.dot_general(left, right, dims, preferred_element_type=jnp.float32)


def columns(member, mask):
    return pl.ds(pl.multiple_of((member ^ mask) * DH, DH), DH)


def causal():
    shape = (BLOCK, BLOCK)
    return lax.broadcasted_iota(jnp.int32, shape, 0) >= lax.broadcasted_iota(jnp.int32, shape, 1)


def delta_body(member_ref, key_ref, value_ref, *delta_refs):
    for mask, delta_ref in enumerate(delta_refs):
        at = columns(member_ref[0], mask)
        delta_ref[...] = dot(key_ref[:, at], value_ref[:, at], TN)


def inner_body(query_ref, key_ref, value_ref, inner_ref):
    keep = causal()
    for head in range(CHAIN_HEADS):
        at = pl.ds(head * DH, DH)
        raw = dot(query_ref[:, at], key_ref[:, at], NT)
        scores = jnp.where(keep, raw, 0.0).astype(jnp.bfloat16)
        inner_ref[:, at] = dot(scores, value_ref[:, at], NN)


def norm_body(member_ref, query_ref, grad_ref, inner_ref, gain_ref, *refs):
    state_refs, (attn_ref, *delta_refs) = refs[:CHAIN_HEADS], refs[CHAIN_HEADS:]
    for mask, state_ref in enumerate(state_refs):
        at = columns(member_ref[0], mask)
        query = query_ref[:, at]
        attn = inner_ref[:, at] + dot(query, state_ref[...].astype(jnp.bfloat16), NN)
        root = jnp.sqrt(jnp.mean(attn * attn, axis=-1, keepdims=True) + EPSILON)
        normed = attn / root
        cotangent = grad_ref[:, at].astype(jnp.float32)
        product = normed * cotangent
        gain = gain_ref[:, at]
        scaled = gain * cotangent
        shared = jnp.mean(normed * scaled, axis=-1, keepdims=True)
        grad_attn = ((scaled - normed * shared) / root).astype(jnp.bfloat16)
        attn_ref[:, at] = grad_attn
        delta_refs[mask][:DH] = dot(query, grad_attn, TN)
        delta_refs[mask][DH:] = jnp.broadcast_to(jnp.sum(product, axis=0, keepdims=True), (GAIN_ROWS, DH))


def partial_body(member_ref, query_ref, key_ref, value_ref, attn_ref, *refs):
    state_refs, (grad_query_ref, key_part_ref, value_part_ref) = refs[:CHAIN_HEADS], refs[-3:]
    keep = causal()
    for mask, state_ref in enumerate(state_refs):
        at = columns(member_ref[0], mask)
        query, key, value, grad_attn = query_ref[:, at], key_ref[:, at], value_ref[:, at], attn_ref[:, at]
        scores = jnp.where(keep, dot(query, key, NT), 0.0).astype(jnp.bfloat16)
        grad_scores = jnp.where(keep, dot(grad_attn, value, NT), 0.0).astype(jnp.bfloat16)
        carried = dot(grad_attn, state_ref[...].astype(jnp.bfloat16), NT)
        grad_query_ref[:, at] = (dot(grad_scores, key, NN) + carried).astype(jnp.bfloat16)
        key_part_ref[:, at] = dot(grad_scores, query, TN)
        value_part_ref[:, at] = dot(scores, grad_attn, TN)


def final_body(member_ref, key_ref, value_ref, *refs):
    parts, states = refs[: 2 * CHAINS], refs[2 * CHAINS : -2]
    grad_key_ref, grad_value_ref = refs[-2:]
    for chain in range(CHAINS):
        for mask in range(CHAIN_HEADS):
            at = columns(member_ref[0], mask)
            wide = pl.ds(pl.multiple_of(chain * WIDE + (member_ref[0] ^ mask) * DH, DH), DH)
            state = states[chain * CHAIN_HEADS + mask][:DH].astype(jnp.bfloat16)
            key_part, value_part = parts[2 * chain][:, at], parts[2 * chain + 1][:, at]
            grad_key_ref[:, wide] = (key_part + dot(value_ref[:, wide], state, NT)).astype(jnp.bfloat16)
            grad_value_ref[:, wide] = (value_part + dot(key_ref[:, wide], state, NN)).astype(jnp.bfloat16)


def whole(*shape):
    return pl.BlockSpec(shape, lambda step: (0,) * len(shape))


def part_of(chain):
    return pl.BlockSpec((BLOCK, WIDE), lambda step: (0, chain))


MEMBER = pl.BlockSpec(memory_space=pltpu.SMEM)


def call(body, in_specs, out_specs, outs, flops, name, aliases=None):
    return pl.pallas_call(
        body,
        grid=(1,),
        in_specs=in_specs,
        out_specs=out_specs,
        out_shape=outs,
        input_output_aliases=aliases or {},
        compiler_params=pltpu.CompilerParams(vmem_limit_bytes=32 * 1024 * 1024),
        cost_estimate=pl.CostEstimate(flops=flops, bytes_accessed=2 << 20, transcendentals=0),
        name=name,
    )


def swap(array, axis, mask):
    if mask == 0:
        return array
    return lax.ppermute(array, axis, [(s, s ^ mask) for s in range(lax.axis_size(axis))])


def carried_in(held, axis, reverse):
    count, place = lax.axis_size(axis), lax.axis_index(axis)
    group = len(held)
    member = lax.rem(place, group)

    def later(first, second):
        return first < second if reverse else first > second

    held = [swap(piece, axis, mask) for mask, piece in enumerate(held)]
    total = functools.reduce(jnp.add, held)
    carried = jnp.zeros_like(total)
    mask = group
    while mask < count:
        arrived = swap(total, axis, mask)
        carried = carried + jnp.where(later(place, place ^ mask), arrived, 0.0)
        total = total + arrived
        mask *= 2
    back = []
    for mask in range(group):
        own = carried
        for other in range(group):
            own = own + jnp.where(later(member ^ mask, member ^ other), held[other], 0.0)
        if own.shape[0] > DH:
            own = jnp.concatenate([own[:DH], total[DH:]])
        back.append(swap(own, axis, mask))
    return back


def local(queries, keys, values, out_gain, grad_out):
    full = queries.shape
    flat = (full[0] * full[1], full[2])
    assert flat == (BLOCK, HEADS * DH)
    query, key, value, grad = (a.reshape(flat) for a in (queries, keys, values, grad_out))
    gain = out_gain.reshape(1, HEADS * DH)
    member = lax.rem(lax.axis_index("seq"), CHAIN_HEADS)
    member_in = member.astype(jnp.int32).reshape(1)
    square = jax.ShapeDtypeStruct((DH, DH), jnp.float32)
    taller = jax.ShapeDtypeStruct((DH + GAIN_ROWS, DH), jnp.float32)
    wide_float = jax.ShapeDtypeStruct((BLOCK, WIDE), jnp.float32)
    wide_low = jax.ShapeDtypeStruct((BLOCK, WIDE), jnp.bfloat16)
    full_low = jax.ShapeDtypeStruct(flat, jnp.bfloat16)
    squares = [whole(DH, DH)] * CHAIN_HEADS
    tallers = [whole(DH + GAIN_ROWS, DH)] * CHAIN_HEADS
    unit = 2 * BLOCK * DH * DH * CHAIN_HEADS

    states, inner = [], []
    for chain in range(CHAINS):
        cols = part_of(chain)
        deltas = call(
            delta_body, [MEMBER, cols, cols], squares, [square] * CHAIN_HEADS, unit, "delta"
        )(member_in, key, value)
        states.append(carried_in(deltas, "seq", False))
        inner.append(
            call(inner_body, [cols] * 3, whole(BLOCK, WIDE), wide_float, 4 * unit, "inner")(query, key, value)
        )

    later, parts, grad_query = [], [], None
    for chain in range(CHAINS):
        cols = part_of(chain)
        attn, *deltas = call(
            norm_body,
            [MEMBER, cols, cols, whole(BLOCK, WIDE), pl.BlockSpec((1, WIDE), lambda step, c=chain: (0, c))] + squares,
            [whole(BLOCK, WIDE)] + tallers,
            [wide_low] + [taller] * CHAIN_HEADS,
            2 * unit,
            "norm",
        )(member_in, query, grad, inner[chain], gain, *states[chain])
        later.append(carried_in(deltas, "seq", True))
        held = [] if grad_query is None else [grad_query]
        grad_query, key_part, value_part = call(
            partial_body,
            [MEMBER, cols, cols, cols, whole(BLOCK, WIDE)] + squares + [pl.BlockSpec(memory_space=pl.ANY)] * len(held),
            [cols, whole(BLOCK, WIDE), whole(BLOCK, WIDE)],
            [full_low, wide_float, wide_float],
            11 * unit,
            "partial",
            {5 + CHAIN_HEADS: 0} if held else None,
        )(member_in, query, key, value, attn, *states[chain], *held)
        parts += [key_part, value_part]

    gain_terms = jnp.stack([piece[DH] for chain in later for piece in chain])
    mask = 1
    while mask < lax.axis_size("dp"):
        gain_terms = gain_terms + swap(gain_terms, "dp", mask)
        mask *= 2
    grad_key, grad_value = call(
        final_body,
        [MEMBER] + [whole(*flat)] * 2 + [whole(BLOCK, WIDE)] * (2 * CHAINS) + tallers * CHAINS,
        [whole(*flat)] * 2,
        [full_low] * 2,
        4 * unit,
        "final",
    )(member_in, key, value, *parts, *[piece for chain in later for piece in chain])
    gain_terms = gain_terms.reshape(CHAINS, CHAIN_HEADS, DH)
    ordered = []
    for head in range(CHAIN_HEADS):
        picked = jnp.zeros((CHAINS, DH), jnp.float32)
        for mask in range(CHAIN_HEADS):
            picked = picked + jnp.where((member ^ mask) == head, gain_terms[:, mask], 0.0)
        ordered.append(picked)
    positions = lax.axis_size("seq") * lax.axis_size("dp") * BLOCK
    grad_gain = jnp.stack(ordered, axis=1).reshape(HEADS * DH) / math.sqrt(positions)
    return (grad_query.reshape(full), grad_key.reshape(full), grad_value.reshape(full), grad_gain)


def solution(mesh):
    sharded = P("dp", "seq", None)
    return jax.shard_map(
        local,
        mesh=mesh,
        in_specs=(sharded, sharded, sharded, P(), sharded),
        out_specs=(sharded, sharded, sharded, P()),
        check_vma=False,
    )
```

time: 294 us -> 77.5 us (0.26)
  waiting for transfers between devices: 182 us -> 8 us
  blocking collectives: 55.3 us -> 0 us
  starting transfers between devices: 0.08 us -> 45.1 us
  other arithmetic: 21.1 us -> 1.15 us
  between operations: 14.3 us -> 0.96 us
  matrix products: 11.1 us -> 0 us
  Pallas kernels: 0 us -> 9.28 us
  local copies, waits for them, and re-layouts: 8.91 us -> 12.4 us
    all_gather x2 -> x0, waiting for transfers between devices: 182 us -> none  [carried_in(): gathered = lax.all_gather(part, axis)]
    psum x1 -> x0, blocking collectives: 55.3 us -> none  [local(): gain_total = lax.psum(gain_terms, ('seq', 'dp'))]
    ppermute x0 -> x33, starting transfers between devices: none -> 45.1 us  [swap(): lax.ppermute(array, axis, [(s, s ^ mask) for s in range(lax.axis_size(axi...]
    add x15 -> x21, other arithmetic: 17.5 us -> 0.49 us  [the longest x8 0.31 us: carried_in(): own + jnp.where(later(member ^ mask, member ^ other), held[other], 0.0)]
    dot_general x12 -> x0, matrix products: 11.1 us -> none  [the longest x1 2.57 us: local(): jnp.einsum('hcts,hcte->hcse', scores_low, grad_attn, preferred_element_ty...]
    pallas_call x0 -> x9, Pallas kernels: none -> 9.28 us  [the longest x2 4.07 us: local(): call(partial_body, [MEMBER, cols, cols, cols, whole(BLOCK, WIDE)] + squar...]
    ppermute x0 -> x33, waiting for transfers between devices: none -> 8 us  [swap(): lax.ppermute(array, axis, [(s, s ^ mask) for s in range(lax.axis_size(axi...]
    unnamed x18 -> x50, local copies, waits for them, and re-layouts: 6.64 us -> 12.4 us
  transfers between devices with their start and end apart: 2 -> 33, of which waited for: 2 -> 10; matrix products, arithmetic and copies ran while one was open for 3% -> 1% of each run, Pallas kernels for 0% -> 12%
where the time goes in v3:
time: 77.5 us; the launch traced here: 76.9 us
  starting transfers between devices  45.1 us (58%)
  local copies, waits for them, and re-layouts  12.4 us (16%)
  Pallas kernels  9.28 us (12%)
  waiting for transfers between devices  8 us (10%)
  other arithmetic  1.15 us (1%)
  between operations  0.96 us (1%)
    ppermute x33, starting transfers between devices, swap(): lax.ppermute(array, axis, [(s, s ^ mask) for s in range(lax.axis_size(axi...  45.1 us
    unnamed x50, local copies, waits for them, and re-layouts  12.4 us
    ppermute x33, waiting for transfers between devices, swap(): lax.ppermute(array, axis, [(s, s ^ mask) for s in range(lax.axis_size(axi...  8 us
    pallas_call x2, Pallas kernels, local(): call(partial_body, [MEMBER, cols, cols, cols, whole(BLOCK, WIDE)] + squar...  4.07 us
    pallas_call x2, Pallas kernels, local(): call(norm_body, [MEMBER, cols, cols, whole(BLOCK, WIDE), pl.BlockSpec((1,...  1.71 us
    pallas_call x1, Pallas kernels, local(): call(final_body, [MEMBER] + [whole(*flat)] * 2 + [whole(BLOCK, WIDE)] * (...  1.55 us
  transfers between devices with their start and end apart: 33, of which 10 were waited for; matrix products, arithmetic and copies ran while one was open for 1% of the time, Pallas kernels for 12%

profile of v3, /device:TPU:0, one launch (start us, length us, event | category | flops | bytes accessed | tf_op | source)
XLA Modules:
  0.0 76.9 jit_solution(16341330821227825122)
XLA Ops:
  0.6 1.0 %copy-done = bf16[1,256,1024]{2,1,0:T(8,128)(2,1)S(1)} copy-done((bf16[1,256,1024]{2,1,0:T(8,128)(2,1)S(1)}, bf16[1,256,1024]{2,1,0:T(8,128)(2,1)}, u32[]{:S(2)}) %copy-start) | copy-done | bytes 524312
  1.7 1.0 %copy-done.2 = bf16[1,256,1024]{2,1,0:T(8,128)(2,1)S(1)} copy-done((bf16[1,256,1024]{2,1,0:T(8,128)(2,1)S(1)}, bf16[1,256,1024]{2,1,0:T(8,128)(2,1)}, u32[]{:S(2)}) %copy-start.2) | copy-done | bytes 524312
  3.0 3.0 %collective-permute-start.8 = (f32[128,128]{1,0:T(8,128)S(1)}, f32[128,128]{1,0:T(8,128)S(1)}, u32[]{:S(2)}, u32[]{:S(2)}) collective-permute-start(f32[128,128]{1,0:T(8,128)S(1)} %get-tuple-element.36), channel_id=1, source_target_pairs={{0,2},{2,0},{4,6},{6,4},{8,10},{10,8},{12,14},{14,12},{16,18},{18,... | collective-permute-start | bytes 196616 | tf_op jit(solution)/shard_map/ppermute | solution.py:127
  6.0 1.5 %collective-permute-start.9 = (f32[128,128]{1,0:T(8,128)S(1)}, f32[128,128]{1,0:T(8,128)S(1)}, u32[]{:S(2)}, u32[]{:S(2)}) collective-permute-start(f32[128,128]{1,0:T(8,128)S(1)} %get-tuple-element.37), channel_id=1, source_target_pairs={{0,4},{2,6},{4,0},{6,2},{8,12},{10,14},{12,8},{14,10},{16,20},{18,... | collective-permute-start | bytes 196616 | tf_op jit(solution)/shard_map/ppermute | solution.py:127
  7.9 2.0 %collective-permute-start = (f32[128,128]{1,0:T(8,128)S(1)}, f32[128,128]{1,0:T(8,128)S(1)}, u32[]{:S(2)}, u32[]{:S(2)}) collective-permute-start(f32[128,128]{1,0:T(8,128)S(1)} %get-tuple-element.31), channel_id=1, source_target_pairs={{0,2},{2,0},{4,6},{6,4},{8,10},{10,8},{12,14},{14,12},{16,18},{18,... | collective-permute-start | bytes 196616 | tf_op jit(solution)/shard_map/ppermute | solution.py:127
  9.9 1.5 %collective-permute-start.1 = (f32[128,128]{1,0:T(8,128)S(1)}, f32[128,128]{1,0:T(8,128)S(1)}, u32[]{:S(2)}, u32[]{:S(2)}) collective-permute-start(f32[128,128]{1,0:T(8,128)S(1)} %get-tuple-element.32), channel_id=1, source_target_pairs={{0,4},{2,6},{4,0},{6,2},{8,12},{10,14},{12,8},{14,10},{16,20},{18,... | collective-permute-start | bytes 196616 | tf_op jit(solution)/shard_map/ppermute | solution.py:127
  11.7 1.1 %collective-permute-done.10 = f32[128,128]{1,0:T(8,128)S(1)} collective-permute-done((f32[128,128]{1,0:T(8,128)S(1)}, f32[128,128]{1,0:T(8,128)S(1)}, u32[]{:S(2)}, u32[]{:S(2)}) %collective-permute-start.10) | collective-permute-done | bytes 65568 | tf_op jit(solution)/shard_map/ppermute | solution.py:127
  12.7 1.6 %collective-permute-start.11 = (f32[128,128]{1,0:T(8,128)S(1)}, f32[128,128]{1,0:T(8,128)S(1)}, u32[]{:S(2)}, u32[]{:S(2)}) collective-permute-start(f32[128,128]{1,0:T(8,128)S(1)} %add_add_fusion.2), channel_id=1, source_target_pairs={{0,8},{2,10},{4,12},{6,14},{8,0},{10,2},{12,4},{14,6},{16,24},{18,... | collective-permute-start | bytes 196616 | tf_op jit(solution)/shard_map/ppermute | solution.py:127
  14.8 1.8 %collective-permute-done.2 = f32[128,128]{1,0:T(8,128)S(1)} collective-permute-done((f32[128,128]{1,0:T(8,128)S(1)}, f32[128,128]{1,0:T(8,128)S(1)}, u32[]{:S(2)}, u32[]{:S(2)}) %collective-permute-start.2) | collective-permute-done | bytes 65568 | tf_op jit(solution)/shard_map/ppermute | solution.py:127
  16.6 1.6 %collective-permute-start.3 = (f32[128,128]{1,0:T(8,128)S(1)}, f32[128,128]{1,0:T(8,128)S(1)}, u32[]{:S(2)}, u32[]{:S(2)}) collective-permute-start(f32[128,128]{1,0:T(8,128)S(1)} %add_add_fusion.3), channel_id=1, source_target_pairs={{0,8},{2,10},{4,12},{6,14},{8,0},{10,2},{12,4},{14,6},{16,24},{18,... | collective-permute-start | bytes 196616 | tf_op jit(solution)/shard_map/ppermute | solution.py:127
  18.3 2.7 %collective-permute-start.12 = (f32[128,128]{1,0:T(8,128)S(1)}, f32[128,128]{1,0:T(8,128)S(1)}, u32[]{:S(2)}, u32[]{:S(2)}) collective-permute-start(f32[128,128]{1,0:T(8,128)S(1)} %add.297), channel_id=1, source_target_pairs={{0,16},{2,18},{4,20},{6,22},{8,24},{10,26},{12,28},{14,30},{16,0},... | collective-permute-start | bytes 196616 | tf_op jit(solution)/shard_map/ppermute | solution.py:127
  21.0 3.3 %collective-permute-start.4 = (f32[128,128]{1,0:T(8,128)S(1)}, f32[128,128]{1,0:T(8,128)S(1)}, u32[]{:S(2)}, u32[]{:S(2)}) collective-permute-start(f32[128,128]{1,0:T(8,128)S(1)} %add.280), channel_id=1, source_target_pairs={{0,16},{2,18},{4,20},{6,22},{8,24},{10,26},{12,28},{14,30},{16,0},... | collective-permute-start | bytes 196616 | tf_op jit(solution)/shard_map/ppermute | solution.py:127
  26.1 2.1 %collective-permute-start.15 = (f32[128,128]{1,0:T(8,128)S(1)}, f32[128,128]{1,0:T(8,128)S(1)}, u32[]{:S(2)}, u32[]{:S(2)}) collective-permute-start(f32[128,128]{1,0:T(8,128)S(1)} %get-tuple-element.56), channel_id=1, source_target_pairs={{0,6},{2,4},{4,2},{6,0},{8,14},{10,12},{12,10},{14,8},{16,22},{18,... | collective-permute-start | bytes 196616 | tf_op jit(solution)/shard_map/ppermute | solution.py:127
  30.6 2.1 %collective-permute-start.7 = (f32[128,128]{1,0:T(8,128)S(1)}, f32[128,128]{1,0:T(8,128)S(1)}, u32[]{:S(2)}, u32[]{:S(2)}) collective-permute-start(f32[128,128]{1,0:T(8,128)S(1)} %get-tuple-element.58), channel_id=1, source_target_pairs={{0,6},{2,4},{4,2},{6,0},{8,14},{10,12},{12,10},{14,8},{16,22},{18,... | collective-permute-start | bytes 196616 | tf_op jit(solution)/shard_map/ppermute | solution.py:127
  35.0 2.0 %collective-permute-start.18 = (f32[136,128]{1,0:T(8,128)S(1)}, f32[136,128]{1,0:T(8,128)S(1)}, u32[]{:S(2)}, u32[]{:S(2)}) collective-permute-start(f32[136,128]{1,0:T(8,128)S(1)} %get-tuple-element.49), channel_id=1, source_target_pairs={{0,6},{2,4},{4,2},{6,0},{8,14},{10,12},{12,10},{14,8},{16,22},{18,... | collective-permute-start | bytes 208904 | tf_op jit(solution)/shard_map/ppermute | solution.py:127
  40.2 2.1 %collective-permute-start.26 = (f32[136,128]{1,0:T(8,128)S(1)}, f32[136,128]{1,0:T(8,128)S(1)}, u32[]{:S(2)}, u32[]{:S(2)}) collective-permute-start(f32[136,128]{1,0:T(8,128)S(1)} %get-tuple-element.53), channel_id=1, source_target_pairs={{0,6},{2,4},{4,2},{6,0},{8,14},{10,12},{12,10},{14,8},{16,22},{18,... | collective-permute-start | bytes 208904 | tf_op jit(solution)/shard_map/ppermute | solution.py:127
  43.9 1.5 %collective-permute-done.26 = f32[136,128]{1,0:T(8,128)S(1)} collective-permute-done((f32[136,128]{1,0:T(8,128)S(1)}, f32[136,128]{1,0:T(8,128)S(1)}, u32[]{:S(2)}, u32[]{:S(2)}) %collective-permute-start.26) | collective-permute-done | bytes 69664 | tf_op jit(solution)/shard_map/ppermute | solution.py:127
  45.4 1.1 %collective-permute-start.27 = (f32[136,128]{1,0:T(8,128)S(1)}, f32[136,128]{1,0:T(8,128)S(1)}, u32[]{:S(2)}, u32[]{:S(2)}) collective-permute-start(f32[136,128]{1,0:T(8,128)S(1)} %add_add_fusion), channel_id=1, source_target_pairs={{0,8},{2,10},{4,12},{6,14},{8,0},{10,2},{12,4},{14,6},{16,24},{18,... | collective-permute-start | bytes 208904 | tf_op jit(solution)/shard_map/ppermute | solution.py:127
  46.8 2.4 %collective-permute-start.20 = (f32[136,128]{1,0:T(8,128)S(1)}, f32[136,128]{1,0:T(8,128)S(1)}, u32[]{:S(2)}, u32[]{:S(2)}) collective-permute-start(f32[136,128]{1,0:T(8,128)S(1)} %add.314), channel_id=1, source_target_pairs={{0,16},{2,18},{4,20},{6,22},{8,24},{10,26},{12,28},{14,30},{16,0},... | collective-permute-start | bytes 208904 | tf_op jit(solution)/shard_map/ppermute | solution.py:127
  49.8 2.0 %collective-permute-start.28 = (f32[136,128]{1,0:T(8,128)S(1)}, f32[136,128]{1,0:T(8,128)S(1)}, u32[]{:S(2)}, u32[]{:S(2)}) collective-permute-start(f32[136,128]{1,0:T(8,128)S(1)} %add.332), channel_id=1, source_target_pairs={{0,16},{2,18},{4,20},{6,22},{8,24},{10,26},{12,28},{14,30},{16,0},... | collective-permute-start | bytes 208904 | tf_op jit(solution)/shard_map/ppermute | solution.py:127
  51.8 1.0 %collective-permute-done.20 = f32[136,128]{1,0:T(8,128)S(1)} collective-permute-done((f32[136,128]{1,0:T(8,128)S(1)}, f32[136,128]{1,0:T(8,128)S(1)}, u32[]{:S(2)}, u32[]{:S(2)}) %collective-permute-start.20) | collective-permute-done | bytes 69664 | tf_op jit(solution)/shard_map/ppermute | solution.py:127
  52.9 0.9 %collective-permute-start.23 = (f32[136,128]{1,0:T(8,128)S(1)}, f32[136,128]{1,0:T(8,128)S(1)}, u32[]{:S(2)}, u32[]{:S(2)}) collective-permute-start(f32[136,128]{1,0:T(8,128)S(1)} %get-tuple-element.86), channel_id=1, source_target_pairs={{0,6},{2,4},{4,2},{6,0},{8,14},{10,12},{12,10},{14,8},{16,22},{18,... | collective-permute-start | bytes 208904 | tf_op jit(solution)/shard_map/ppermute | solution.py:127
  53.8 2.0 %collective-permute-start.21 = (f32[136,128]{1,0:T(8,128)S(1)}, f32[136,128]{1,0:T(8,128)S(1)}, u32[]{:S(2)}, u32[]{:S(2)}) collective-permute-start(f32[136,128]{1,0:T(8,128)S(1)} %get-tuple-element.87), channel_id=1, source_target_pairs={{0,2},{2,0},{4,6},{6,4},{8,10},{10,8},{12,14},{14,12},{16,18},{18,... | collective-permute-start | bytes 208904 | tf_op jit(solution)/shard_map/ppermute | solution.py:127
  56.6 1.5 %collective-permute-start.31 = (f32[136,128]{1,0:T(8,128)S(1)}, f32[136,128]{1,0:T(8,128)S(1)}, u32[]{:S(2)}, u32[]{:S(2)}) collective-permute-start(f32[136,128]{1,0:T(8,128)S(1)} %get-tuple-element.82), channel_id=1, source_target_pairs={{0,6},{2,4},{4,2},{6,0},{8,14},{10,12},{12,10},{14,8},{16,22},{18,... | collective-permute-start | bytes 208904 | tf_op jit(solution)/shard_map/ppermute | solution.py:127
  58.1 1.4 %collective-permute-start.29 = (f32[136,128]{1,0:T(8,128)S(1)}, f32[136,128]{1,0:T(8,128)S(1)}, u32[]{:S(2)}, u32[]{:S(2)}) collective-permute-start(f32[136,128]{1,0:T(8,128)S(1)} %get-tuple-element.83), channel_id=1, source_target_pairs={{0,2},{2,0},{4,6},{6,4},{8,10},{10,8},{12,14},{14,12},{16,18},{18,... | collective-permute-start | bytes 208904 | tf_op jit(solution)/shard_map/ppermute | solution.py:127
  60.2 2.0 %partial.2 = (bf16[256,1024]{1,0:T(8,128)(2,1)}, f32[256,512]{1,0:T(8,128)S(1)}, f32[256,512]{1,0:T(8,128)S(1)}) custom-call(s32[1]{0:T(128)} %bitcast.member_ref, bf16[256,1024]{1,0:T(8,128)(2,1)S(1)} %bitcast.29, bf16[256,1024]{1,0:T(8,128)(2,1)S(1)} %bitcast.15, bf16[256,1024]{1,0:T(8,128)(2,1)S(1)} %bitcast.22, ...), custom_call_target="tpu_custom_call" | custom-call | flops 369098752 | bytes 2097152 | tf_op jit(solution)/shard_map/partial/pallas_call | solution.py:199
  62.2 2.0 %partial.3 = (bf16[256,1024]{1,0:T(8,128)(2,1)}, f32[256,512]{1,0:T(8,128)S(1)}, f32[256,512]{1,0:T(8,128)S(1)}) custom-call(s32[1]{0:T(128)} %bitcast.member_ref, bf16[256,1024]{1,0:T(8,128)(2,1)S(1)} %bitcast.30, bf16[256,1024]{1,0:T(8,128)(2,1)S(1)} %bitcast.16, bf16[256,1024]{1,0:T(8,128)(2,1)S(1)} %bitcast.23, ...), custom_call_target="tpu_custom_call", output_to_operand_aliasing={{0}: (9, {})} | custom-call | flops 369098752 | bytes 2097152 | tf_op jit(solution)/shard_map/partial/pallas_call | solution.py:199
  68.4 1.0 %copy-done.7 = f32[256,512]{1,0:T(8,128)S(1)} copy-done((f32[256,512]{1,0:T(8,128)S(1)}, f32[256,512]{1,0:T(8,128)}, u32[]{:S(2)}) %copy-start.7) | copy-done | bytes 524312
  69.4 0.9 %copy-done.13 = f32[136,128]{1,0:T(8,128)S(1)} copy-done((f32[136,128]{1,0:T(8,128)S(1)}, f32[136,128]{1,0:T(8,128)}, u32[]{:S(2)}) %copy-start.13) | copy-done | bytes 69656
  70.3 0.9 %copy-done.15 = f32[136,128]{1,0:T(8,128)S(1)} copy-done((f32[136,128]{1,0:T(8,128)S(1)}, f32[136,128]{1,0:T(8,128)}, u32[]{:S(2)}) %copy-start.15) | copy-done | bytes 69656
  73.8 0.9 %copy-done.23 = f32[136,128]{1,0:T(8,128)S(1)} copy-done((f32[136,128]{1,0:T(8,128)S(1)}, f32[136,128]{1,0:T(8,128)}, u32[]{:S(2)}) %copy-start.23) | copy-done | bytes 69656
  74.7 1.6 %final.1 = (bf16[256,1024]{1,0:T(8,128)(2,1)}, bf16[256,1024]{1,0:T(8,128)(2,1)}) custom-call(s32[1]{0:T(128)} %bitcast.member_ref, bf16[256,1024]{1,0:T(8,128)(2,1)S(1)} %bitcast.17, bf16[256,1024]{1,0:T(8,128)(2,1)S(1)} %bitcast.24, f32[256,512]{1,0:T(8,128)S(1)} %get-tuple-element.42.refs_0_, f32[256,512]{1,0:T(8,128)S(1)} %get-tuple-element.43.refs_1_, ...), custom_call_target="tpu_custom_call" | custom-call | flops 134217728 | bytes 2097152 | tf_op jit(solution)/shard_map/final/pallas_call | solution.py:215
  (129 shorter events, 22.3 us)
Async XLA Ops:
  3.0 8.4 %collective-permute-start.8 = (f32[128,128]{1,0:T(8,128)S(1)}, f32[128,128]{1,0:T(8,128)S(1)}, u32[]{:S(2)}, u32[]{:S(2)}) collective-permute-start(f32[128,128]{1,0:T(8,128)S(1)} %get-tuple-element.36), channel_id=1, source_target_pairs={{0,2},{2,0},{4,6},{6,4},{8,10},{10,8},{12,14},{14,12},{16,18},{18,... | collective-permute-start | bytes 196616 | tf_op jit(solution)/shard_map/ppermute | solution.py:127
  6.0 5.6 %collective-permute-start.9 = (f32[128,128]{1,0:T(8,128)S(1)}, f32[128,128]{1,0:T(8,128)S(1)}, u32[]{:S(2)}, u32[]{:S(2)}) collective-permute-start(f32[128,128]{1,0:T(8,128)S(1)} %get-tuple-element.37), channel_id=1, source_target_pairs={{0,4},{2,6},{4,0},{6,2},{8,12},{10,14},{12,8},{14,10},{16,20},{18,... | collective-permute-start | bytes 196616 | tf_op jit(solution)/shard_map/ppermute | solution.py:127
  7.6 5.2 %collective-permute-start.10 = (f32[128,128]{1,0:T(8,128)S(1)}, f32[128,128]{1,0:T(8,128)S(1)}, u32[]{:S(2)}, u32[]{:S(2)}) collective-permute-start(f32[128,128]{1,0:T(8,128)S(1)} %get-tuple-element.38), channel_id=1, source_target_pairs={{0,6},{2,4},{4,2},{6,0},{8,14},{10,12},{12,10},{14,8},{16,22},{18,... | collective-permute-start | bytes 196616 | tf_op jit(solution)/shard_map/ppermute | solution.py:127
  7.9 6.5 %collective-permute-start = (f32[128,128]{1,0:T(8,128)S(1)}, f32[128,128]{1,0:T(8,128)S(1)}, u32[]{:S(2)}, u32[]{:S(2)}) collective-permute-start(f32[128,128]{1,0:T(8,128)S(1)} %get-tuple-element.31), channel_id=1, source_target_pairs={{0,2},{2,0},{4,6},{6,4},{8,10},{10,8},{12,14},{14,12},{16,18},{18,... | collective-permute-start | bytes 196616 | tf_op jit(solution)/shard_map/ppermute | solution.py:127
  9.9 4.9 %collective-permute-start.1 = (f32[128,128]{1,0:T(8,128)S(1)}, f32[128,128]{1,0:T(8,128)S(1)}, u32[]{:S(2)}, u32[]{:S(2)}) collective-permute-start(f32[128,128]{1,0:T(8,128)S(1)} %get-tuple-element.32), channel_id=1, source_target_pairs={{0,4},{2,6},{4,0},{6,2},{8,12},{10,14},{12,8},{14,10},{16,20},{18,... | collective-permute-start | bytes 196616 | tf_op jit(solution)/shard_map/ppermute | solution.py:127
  11.4 5.2 %collective-permute-start.2 = (f32[128,128]{1,0:T(8,128)S(1)}, f32[128,128]{1,0:T(8,128)S(1)}, u32[]{:S(2)}, u32[]{:S(2)}) collective-permute-start(f32[128,128]{1,0:T(8,128)S(1)} %get-tuple-element.33), channel_id=1, source_target_pairs={{0,6},{2,4},{4,2},{6,0},{8,14},{10,12},{12,10},{14,8},{16,22},{18,... | collective-permute-start | bytes 196616 | tf_op jit(solution)/shard_map/ppermute | solution.py:127
  12.7 5.5 %collective-permute-start.11 = (f32[128,128]{1,0:T(8,128)S(1)}, f32[128,128]{1,0:T(8,128)S(1)}, u32[]{:S(2)}, u32[]{:S(2)}) collective-permute-start(f32[128,128]{1,0:T(8,128)S(1)} %add_add_fusion.2), channel_id=1, source_target_pairs={{0,8},{2,10},{4,12},{6,14},{8,0},{10,2},{12,4},{14,6},{16,24},{18,... | collective-permute-start | bytes 196616 | tf_op jit(solution)/shard_map/ppermute | solution.py:127
  16.6 4.3 %collective-permute-start.3 = (f32[128,128]{1,0:T(8,128)S(1)}, f32[128,128]{1,0:T(8,128)S(1)}, u32[]{:S(2)}, u32[]{:S(2)}) collective-permute-start(f32[128,128]{1,0:T(8,128)S(1)} %add_add_fusion.3), channel_id=1, source_target_pairs={{0,8},{2,10},{4,12},{6,14},{8,0},{10,2},{12,4},{14,6},{16,24},{18,... | collective-permute-start | bytes 196616 | tf_op jit(solution)/shard_map/ppermute | solution.py:127
  18.3 6.3 %collective-permute-start.12 = (f32[128,128]{1,0:T(8,128)S(1)}, f32[128,128]{1,0:T(8,128)S(1)}, u32[]{:S(2)}, u32[]{:S(2)}) collective-permute-start(f32[128,128]{1,0:T(8,128)S(1)} %add.297), channel_id=1, source_target_pairs={{0,16},{2,18},{4,20},{6,22},{8,24},{10,26},{12,28},{14,30},{16,0},... | collective-permute-start | bytes 196616 | tf_op jit(solution)/shard_map/ppermute | solution.py:127
  21.0 7.3 %collective-permute-start.4 = (f32[128,128]{1,0:T(8,128)S(1)}, f32[128,128]{1,0:T(8,128)S(1)}, u32[]{:S(2)}, u32[]{:S(2)}) collective-permute-start(f32[128,128]{1,0:T(8,128)S(1)} %add.280), channel_id=1, source_target_pairs={{0,16},{2,18},{4,20},{6,22},{8,24},{10,26},{12,28},{14,30},{16,0},... | collective-permute-start | bytes 196616 | tf_op jit(solution)/shard_map/ppermute | solution.py:127
  24.7 5.9 %collective-permute-start.14 = (f32[128,128]{1,0:T(8,128)S(1)}, f32[128,128]{1,0:T(8,128)S(1)}, u32[]{:S(2)}, u32[]{:S(2)}) collective-permute-start(f32[128,128]{1,0:T(8,128)S(1)} %get-tuple-element.68), channel_id=1, source_target_pairs={{0,4},{2,6},{4,0},{6,2},{8,12},{10,14},{12,8},{14,10},{16,20},{18,... | collective-permute-start | bytes 196616 | tf_op jit(solution)/shard_map/ppermute | solution.py:127
  25.4 7.3 %collective-permute-start.13 = (f32[128,128]{1,0:T(8,128)S(1)}, f32[128,128]{1,0:T(8,128)S(1)}, u32[]{:S(2)}, u32[]{:S(2)}) collective-permute-start(f32[128,128]{1,0:T(8,128)S(1)} %get-tuple-element.69), channel_id=1, source_target_pairs={{0,2},{2,0},{4,6},{6,4},{8,10},{10,8},{12,14},{14,12},{16,18},{18,... | collective-permute-start | bytes 196616 | tf_op jit(solution)/shard_map/ppermute | solution.py:127
  26.1 6.5 %collective-permute-start.15 = (f32[128,128]{1,0:T(8,128)S(1)}, f32[128,128]{1,0:T(8,128)S(1)}, u32[]{:S(2)}, u32[]{:S(2)}) collective-permute-start(f32[128,128]{1,0:T(8,128)S(1)} %get-tuple-element.56), channel_id=1, source_target_pairs={{0,6},{2,4},{4,2},{6,0},{8,14},{10,12},{12,10},{14,8},{16,22},{18,... | collective-permute-start | bytes 196616 | tf_op jit(solution)/shard_map/ppermute | solution.py:127
  28.3 6.7 %collective-permute-start.6 = (f32[128,128]{1,0:T(8,128)S(1)}, f32[128,128]{1,0:T(8,128)S(1)}, u32[]{:S(2)}, u32[]{:S(2)}) collective-permute-start(f32[128,128]{1,0:T(8,128)S(1)} %get-tuple-element.71), channel_id=1, source_target_pairs={{0,4},{2,6},{4,0},{6,2},{8,12},{10,14},{12,8},{14,10},{16,20},{18,... | collective-permute-start | bytes 196616 | tf_op jit(solution)/shard_map/ppermute | solution.py:127
  29.8 8.0 %collective-permute-start.5 = (f32[128,128]{1,0:T(8,128)S(1)}, f32[128,128]{1,0:T(8,128)S(1)}, u32[]{:S(2)}, u32[]{:S(2)}) collective-permute-start(f32[128,128]{1,0:T(8,128)S(1)} %get-tuple-element.72), channel_id=1, source_target_pairs={{0,2},{2,0},{4,6},{6,4},{8,10},{10,8},{12,14},{14,12},{16,18},{18,... | collective-permute-start | bytes 196616 | tf_op jit(solution)/shard_map/ppermute | solution.py:127
  30.6 7.2 %collective-permute-start.7 = (f32[128,128]{1,0:T(8,128)S(1)}, f32[128,128]{1,0:T(8,128)S(1)}, u32[]{:S(2)}, u32[]{:S(2)}) collective-permute-start(f32[128,128]{1,0:T(8,128)S(1)} %get-tuple-element.58), channel_id=1, source_target_pairs={{0,6},{2,4},{4,2},{6,0},{8,14},{10,12},{12,10},{14,8},{16,22},{18,... | collective-permute-start | bytes 196616 | tf_op jit(solution)/shard_map/ppermute | solution.py:127
  33.5 6.7 %collective-permute-start.16 = (f32[136,128]{1,0:T(8,128)S(1)}, f32[136,128]{1,0:T(8,128)S(1)}, u32[]{:S(2)}, u32[]{:S(2)}) collective-permute-start(f32[136,128]{1,0:T(8,128)S(1)} %get-tuple-element.47), channel_id=1, source_target_pairs={{0,2},{2,0},{4,6},{6,4},{8,10},{10,8},{12,14},{14,12},{16,18},{18,... | collective-permute-start | bytes 208904 | tf_op jit(solution)/shard_map/ppermute | solution.py:127
  34.4 7.9 %collective-permute-start.17 = (f32[136,128]{1,0:T(8,128)S(1)}, f32[136,128]{1,0:T(8,128)S(1)}, u32[]{:S(2)}, u32[]{:S(2)}) collective-permute-start(f32[136,128]{1,0:T(8,128)S(1)} %get-tuple-element.48), channel_id=1, source_target_pairs={{0,4},{2,6},{4,0},{6,2},{8,12},{10,14},{12,8},{14,10},{16,20},{18,... | collective-permute-start | bytes 208904 | tf_op jit(solution)/shard_map/ppermute | solution.py:127
  35.0 7.2 %collective-permute-start.18 = (f32[136,128]{1,0:T(8,128)S(1)}, f32[136,128]{1,0:T(8,128)S(1)}, u32[]{:S(2)}, u32[]{:S(2)}) collective-permute-start(f32[136,128]{1,0:T(8,128)S(1)} %get-tuple-element.49), channel_id=1, source_target_pairs={{0,6},{2,4},{4,2},{6,0},{8,14},{10,12},{12,10},{14,8},{16,22},{18,... | collective-permute-start | bytes 208904 | tf_op jit(solution)/shard_map/ppermute | solution.py:127
  38.7 4.4 %collective-permute-start.24 = (f32[136,128]{1,0:T(8,128)S(1)}, f32[136,128]{1,0:T(8,128)S(1)}, u32[]{:S(2)}, u32[]{:S(2)}) collective-permute-start(f32[136,128]{1,0:T(8,128)S(1)} %get-tuple-element.51), channel_id=1, source_target_pairs={{0,2},{2,0},{4,6},{6,4},{8,10},{10,8},{12,14},{14,12},{16,18},{18,... | collective-permute-start | bytes 208904 | tf_op jit(solution)/shard_map/ppermute | solution.py:127
  40.2 5.2 %collective-permute-start.26 = (f32[136,128]{1,0:T(8,128)S(1)}, f32[136,128]{1,0:T(8,128)S(1)}, u32[]{:S(2)}, u32[]{:S(2)}) collective-permute-start(f32[136,128]{1,0:T(8,128)S(1)} %get-tuple-element.53), channel_id=1, source_target_pairs={{0,6},{2,4},{4,2},{6,0},{8,14},{10,12},{12,10},{14,8},{16,22},{18,... | collective-permute-start | bytes 208904 | tf_op jit(solution)/shard_map/ppermute | solution.py:127
  42.3 4.5 %collective-permute-start.19 = (f32[136,128]{1,0:T(8,128)S(1)}, f32[136,128]{1,0:T(8,128)S(1)}, u32[]{:S(2)}, u32[]{:S(2)}) collective-permute-start(f32[136,128]{1,0:T(8,128)S(1)} %add_add_fusion.1), channel_id=1, source_target_pairs={{0,8},{2,10},{4,12},{6,14},{8,0},{10,2},{12,4},{14,6},{16,24},{18,... | collective-permute-start | bytes 208904 | tf_op jit(solution)/shard_map/ppermute | solution.py:127
  45.4 4.4 %collective-permute-start.27 = (f32[136,128]{1,0:T(8,128)S(1)}, f32[136,128]{1,0:T(8,128)S(1)}, u32[]{:S(2)}, u32[]{:S(2)}) collective-permute-start(f32[136,128]{1,0:T(8,128)S(1)} %add_add_fusion), channel_id=1, source_target_pairs={{0,8},{2,10},{4,12},{6,14},{8,0},{10,2},{12,4},{14,6},{16,24},{18,... | collective-permute-start | bytes 208904 | tf_op jit(solution)/shard_map/ppermute | solution.py:127
  46.8 6.0 %collective-permute-start.20 = (f32[136,128]{1,0:T(8,128)S(1)}, f32[136,128]{1,0:T(8,128)S(1)}, u32[]{:S(2)}, u32[]{:S(2)}) collective-permute-start(f32[136,128]{1,0:T(8,128)S(1)} %add.314), channel_id=1, source_target_pairs={{0,16},{2,18},{4,20},{6,22},{8,24},{10,26},{12,28},{14,30},{16,0},... | collective-permute-start | bytes 208904 | tf_op jit(solution)/shard_map/ppermute | solution.py:127
  49.8 6.6 %collective-permute-start.28 = (f32[136,128]{1,0:T(8,128)S(1)}, f32[136,128]{1,0:T(8,128)S(1)}, u32[]{:S(2)}, u32[]{:S(2)}) collective-permute-start(f32[136,128]{1,0:T(8,128)S(1)} %add.332), channel_id=1, source_target_pairs={{0,16},{2,18},{4,20},{6,22},{8,24},{10,26},{12,28},{14,30},{16,0},... | collective-permute-start | bytes 208904 | tf_op jit(solution)/shard_map/ppermute | solution.py:127
  52.9 6.6 %collective-permute-start.23 = (f32[136,128]{1,0:T(8,128)S(1)}, f32[136,128]{1,0:T(8,128)S(1)}, u32[]{:S(2)}, u32[]{:S(2)}) collective-permute-start(f32[136,128]{1,0:T(8,128)S(1)} %get-tuple-element.86), channel_id=1, source_target_pairs={{0,6},{2,4},{4,2},{6,0},{8,14},{10,12},{12,10},{14,8},{16,22},{18,... | collective-permute-start | bytes 208904 | tf_op jit(solution)/shard_map/ppermute | solution.py:127
  53.8 11.3 %collective-permute-start.21 = (f32[136,128]{1,0:T(8,128)S(1)}, f32[136,128]{1,0:T(8,128)S(1)}, u32[]{:S(2)}, u32[]{:S(2)}) collective-permute-start(f32[136,128]{1,0:T(8,128)S(1)} %get-tuple-element.87), channel_id=1, source_target_pairs={{0,2},{2,0},{4,6},{6,4},{8,10},{10,8},{12,14},{14,12},{16,18},{18,... | collective-permute-start | bytes 208904 | tf_op jit(solution)/shard_map/ppermute | solution.py:127
  55.8 9.9 %collective-permute-start.22 = (f32[136,128]{1,0:T(8,128)S(1)}, f32[136,128]{1,0:T(8,128)S(1)}, u32[]{:S(2)}, u32[]{:S(2)}) collective-permute-start(f32[136,128]{1,0:T(8,128)S(1)} %get-tuple-element.88), channel_id=1, source_target_pairs={{0,4},{2,6},{4,0},{6,2},{8,12},{10,14},{12,8},{14,10},{16,20},{18,... | collective-permute-start | bytes 208904 | tf_op jit(solution)/shard_map/ppermute | solution.py:127
  56.6 9.7 %collective-permute-start.31 = (f32[136,128]{1,0:T(8,128)S(1)}, f32[136,128]{1,0:T(8,128)S(1)}, u32[]{:S(2)}, u32[]{:S(2)}) collective-permute-start(f32[136,128]{1,0:T(8,128)S(1)} %get-tuple-element.82), channel_id=1, source_target_pairs={{0,6},{2,4},{4,2},{6,0},{8,14},{10,12},{12,10},{14,8},{16,22},{18,... | collective-permute-start | bytes 208904 | tf_op jit(solution)/shard_map/ppermute | solution.py:127
  58.1 8.9 %collective-permute-start.29 = (f32[136,128]{1,0:T(8,128)S(1)}, f32[136,128]{1,0:T(8,128)S(1)}, u32[]{:S(2)}, u32[]{:S(2)}) collective-permute-start(f32[136,128]{1,0:T(8,128)S(1)} %get-tuple-element.83), channel_id=1, source_target_pairs={{0,2},{2,0},{4,6},{6,4},{8,10},{10,8},{12,14},{14,12},{16,18},{18,... | collective-permute-start | bytes 208904 | tf_op jit(solution)/shard_map/ppermute | solution.py:127
  59.6 8.1 %collective-permute-start.30 = (f32[136,128]{1,0:T(8,128)S(1)}, f32[136,128]{1,0:T(8,128)S(1)}, u32[]{:S(2)}, u32[]{:S(2)}) collective-permute-start(f32[136,128]{1,0:T(8,128)S(1)} %get-tuple-element.84), channel_id=1, source_target_pairs={{0,4},{2,6},{4,0},{6,2},{8,12},{10,14},{12,8},{14,10},{16,20},{18,... | collective-permute-start | bytes 208904 | tf_op jit(solution)/shard_map/ppermute | solution.py:127
  68.3 8.0 %collective-permute-start.32 = (f32[8,128]{1,0:T(8,128)S(1)}, f32[8,128]{1,0:T(8,128)S(1)}, u32[]{:S(2)}, u32[]{:S(2)}) collective-permute-start(f32[8,128]{1,0:T(8,128)S(1)} %stack.4), channel_id=1, source_target_pairs={{0,1},{1,0},{2,3},{3,2},{4,5},{5,4},{6,7},{7,6},{8,9},{9,8},{10,11... | collective-permute-start | bytes 12296 | tf_op jit(solution)/shard_map/ppermute | solution.py:127
  (27 other events, 54.4 us)

commit v4 on v3

v4 whole, which is shorter than its diff:
```python
import math

import jax
import jax.numpy as jnp
from jax import lax
from jax.experimental import pallas as pl
from jax.experimental.pallas import tpu as pltpu
from jax.sharding import PartitionSpec as P

HEADS = 8
DH = 128
BLOCK = 256
CHAINS = 2
CHAIN_HEADS = HEADS // CHAINS
WIDE = CHAIN_HEADS * DH
GAIN_ROWS = 8
HALF = CHAIN_HEADS // 2
EPSILON = 1e-06

NT = (((1,), (1,)), ((), ()))
TN = (((0,), (0,)), ((), ()))
NN = (((1,), (0,)), ((), ()))


def dot(left, right, dims):
    return lax.dot_general(left, right, dims, preferred_element_type=jnp.float32)


def columns(member, mask):
    return pl.ds(pl.multiple_of((member ^ mask) * DH, DH), DH)


def causal():
    shape = (BLOCK, BLOCK)
    return lax.broadcasted_iota(jnp.int32, shape, 0) >= lax.broadcasted_iota(jnp.int32, shape, 1)


def delta_body(member_ref, key_ref, value_ref, *delta_refs):
    for mask in range(CHAIN_HEADS):
        at = columns(member_ref[0], mask)
        delta_refs[mask // HALF][mask % HALF] = dot(key_ref[:, at], value_ref[:, at], TN)


def inner_body(query_ref, key_ref, value_ref, inner_ref):
    keep = causal()
    for head in range(CHAIN_HEADS):
        at = pl.ds(head * DH, DH)
        raw = dot(query_ref[:, at], key_ref[:, at], NT)
        scores = jnp.where(keep, raw, 0.0).astype(jnp.bfloat16)
        inner_ref[:, at] = dot(scores, value_ref[:, at], NN)


def norm_body(member_ref, query_ref, grad_ref, inner_ref, gain_ref, *refs):
    state_refs, (attn_ref, *delta_refs) = refs[:2], refs[2:]
    for mask in range(CHAIN_HEADS):
        at = columns(member_ref[0], mask)
        state_ref, delta_ref = state_refs[mask // HALF].at[mask % HALF], delta_refs[mask // HALF].at[mask % HALF]
        query = query_ref[:, at]
        attn = inner_ref[:, at] + dot(query, state_ref[...].astype(jnp.bfloat16), NN)
        root = jnp.sqrt(jnp.mean(attn * attn, axis=-1, keepdims=True) + EPSILON)
        normed = attn / root
        cotangent = grad_ref[:, at].astype(jnp.float32)
        scaled = gain_ref[:, at] * cotangent
        shared = jnp.mean(normed * scaled, axis=-1, keepdims=True)
        grad_attn = ((scaled - normed * shared) / root).astype(jnp.bfloat16)
        attn_ref[:, at] = grad_attn
        terms = jnp.sum(normed * cotangent, axis=0, keepdims=True)
        delta_ref[:DH] = dot(query, grad_attn, TN)
        delta_ref[DH:] = jnp.broadcast_to(terms, (GAIN_ROWS, DH))


def partial_body(member_ref, query_ref, key_ref, value_ref, attn_ref, *refs):
    state_refs, (grad_query_ref, key_part_ref, value_part_ref) = refs[:2], refs[-3:]
    keep = causal()
    for mask in range(CHAIN_HEADS):
        at = columns(member_ref[0], mask)
        query, key, value, grad_attn = query_ref[:, at], key_ref[:, at], value_ref[:, at], attn_ref[:, at]
        state = state_refs[mask // HALF][mask % HALF].astype(jnp.bfloat16)
        scores = jnp.where(keep, dot(query, key, NT), 0.0).astype(jnp.bfloat16)
        grad_scores = jnp.where(keep, dot(grad_attn, value, NT), 0.0).astype(jnp.bfloat16)
        grad_query_ref[:, at] = (dot(grad_scores, key, NN) + dot(grad_attn, state, NT)).astype(jnp.bfloat16)
        key_part_ref[:, at] = dot(grad_scores, query, TN)
        value_part_ref[:, at] = dot(scores, grad_attn, TN)


def final_body(member_ref, key_ref, value_ref, key_part_ref, value_part_ref, *refs):
    state_refs, (grad_key_ref, grad_value_ref) = refs[:2], refs[-2:]
    for mask in range(CHAIN_HEADS):
        at = columns(member_ref[0], mask)
        state = state_refs[mask // HALF][mask % HALF, :DH].astype(jnp.bfloat16)
        grad_key_ref[:, at] = (key_part_ref[:, at] + dot(value_ref[:, at], state, NT)).astype(jnp.bfloat16)
        grad_value_ref[:, at] = (value_part_ref[:, at] + dot(key_ref[:, at], state, NN)).astype(jnp.bfloat16)


def gain_body(member_ref, *refs):
    piece_refs, gain_ref = refs[:-1], refs[-1]
    for chain in range(CHAINS):
        for mask in range(CHAIN_HEADS):
            row = chain * CHAIN_HEADS + (member_ref[0] ^ mask)
            piece_ref = piece_refs[2 * chain + mask // HALF]
            gain_ref[pl.ds(row, 1), :] = piece_ref[mask % HALF, DH : DH + 1, :]


def whole(*shape):
    return pl.BlockSpec(shape, lambda step: (0,) * len(shape))


def part_of(chain):
    return pl.BlockSpec((BLOCK, WIDE), lambda step: (0, chain))


MEMBER = pl.BlockSpec(memory_space=pltpu.SMEM)


def call(body, in_specs, out_specs, outs, flops, name, aliases=None):
    return pl.pallas_call(
        body,
        grid=(1,),
        in_specs=in_specs,
        out_specs=out_specs,
        out_shape=outs,
        input_output_aliases=aliases or {},
        compiler_params=pltpu.CompilerParams(vmem_limit_bytes=16 * 1024 * 1024),
        cost_estimate=pl.CostEstimate(flops=flops, bytes_accessed=2 << 20, transcendentals=0),
        name=name,
    )


def swap(array, axis, mask):
    if mask == 0:
        return array
    return lax.ppermute(array, axis, [(s, s ^ mask) for s in range(lax.axis_size(axis))])


def carried_in(kept, sent, axis, reverse):
    count, place = lax.axis_size(axis), lax.axis_index(axis)
    is_state = lax.broadcasted_iota(jnp.int32, kept.shape[1:], 0) < DH

    def later(mask):
        bit = (place & mask) != 0
        return bit != reverse

    other = swap(sent, axis, 1)
    row = kept + other
    beside = swap(row[1], axis, 2)
    total = row[0] + beside
    carried = jnp.where(is_state, 0.0, total)
    mask = 4
    while mask < count:
        arrived = swap(total, axis, mask)
        carried = carried + jnp.where(is_state & ~later(mask), 0.0, arrived)
        total = total + arrived
        mask *= 2
    back = swap(carried + jnp.where(is_state & ~later(2), row[0], 0.0), axis, 2)
    before = jnp.stack([carried + jnp.where(is_state & later(2), beside, 0.0), back])
    mine = before + jnp.where(is_state & later(1), other, 0.0)
    return mine, swap(before + jnp.where(is_state & ~later(1), kept, 0.0), axis, 1)


def local(queries, keys, values, out_gain, grad_out):
    full = queries.shape
    flat = (full[0] * full[1], full[2])
    assert flat == (BLOCK, HEADS * DH)
    query, key, value, grad = (a.reshape(flat) for a in (queries, keys, values, grad_out))
    gain = out_gain.reshape(1, HEADS * DH)
    assert lax.axis_size("seq") % CHAIN_HEADS == 0
    place = lax.axis_index("seq")
    member = ((place & 1) * 2 + ((place >> 1) & 1)).astype(jnp.int32).reshape(1)
    half = jax.ShapeDtypeStruct((HALF, DH, DH), jnp.float32)
    taller = jax.ShapeDtypeStruct((HALF, DH + GAIN_ROWS, DH), jnp.float32)
    wide_float = jax.ShapeDtypeStruct((BLOCK, WIDE), jnp.float32)
    wide_low = jax.ShapeDtypeStruct((BLOCK, WIDE), jnp.bfloat16)
    full_low = jax.ShapeDtypeStruct(flat, jnp.bfloat16)
    halves = [whole(*half.shape)] * 2
    tallers = [whole(*taller.shape)] * 2
    wide = whole(BLOCK, WIDE)
    spot = pl.BlockSpec(memory_space=pl.ANY)
    unit = 2 * BLOCK * DH * DH * CHAIN_HEADS

    states, inner = [], []
    for chain in range(CHAINS):
        cols = part_of(chain)
        kept, sent = call(delta_body, [MEMBER, cols, cols], halves, [half] * 2, 6 * unit, "delta")(member, key, value)
        states.append(carried_in(kept, sent, "seq", False))
        inner.append(call(inner_body, [cols] * 3, wide, wide_float, 16 * unit, "inner")(query, key, value))

    later, parts, grad_query = [], [], []
    for chain in range(CHAINS):
        cols = part_of(chain)
        attn, kept, sent = call(
            norm_body,
            [MEMBER, cols, cols, wide, pl.BlockSpec((1, WIDE), lambda step, c=chain: (0, c))] + halves,
            [wide] + tallers,
            [wide_low] + [taller] * 2,
            16 * unit,
            "norm",
        )(member, query, grad, inner[chain], gain, *states[chain])
        later.append(carried_in(kept, sent, "seq", True))
        *grad_query, key_part, value_part = call(
            partial_body,
            [MEMBER, cols, cols, cols, wide] + halves + [spot] * len(grad_query),
            [cols, wide, wide],
            [full_low, wide_float, wide_float],
            48 * unit,
            "partial",
            {7: 0} if grad_query else None,
        )(member, query, key, value, attn, *states[chain], *grad_query)
        parts.append((key_part, value_part))

    gain_terms = call(
        gain_body, [MEMBER] + tallers * CHAINS, whole(HEADS, DH),
        jax.ShapeDtypeStruct((HEADS, DH), jnp.float32), unit, "gain",
    )(member, *[piece for chain in later for piece in chain])
    mask = 1
    while mask < lax.axis_size("dp"):
        gain_terms = gain_terms + swap(gain_terms, "dp", mask)
        mask *= 2
    grads = []
    for chain in range(CHAINS):
        cols = part_of(chain)
        grads = call(
            final_body,
            [MEMBER, cols, cols, wide, wide] + tallers + [spot] * len(grads),
            [cols] * 2,
            [full_low] * 2,
            16 * unit,
            "final",
            {7: 0, 8: 1} if grads else None,
        )(member, key, value, *parts[chain], *later[chain], *grads)
    grad_key, grad_value = grads
    positions = lax.axis_size("seq") * lax.axis_size("dp") * BLOCK
    grad_gain = gain_terms.reshape(HEADS * DH) / math.sqrt(positions)
    return (grad_query[0].reshape(full), grad_key.reshape(full), grad_value.reshape(full), grad_gain)


def solution(mesh):
    sharded = P("dp", "seq", None)
    return jax.shard_map(
        local,
        mesh=mesh,
        in_specs=(sharded, sharded, sharded, P(), sharded),
        out_specs=(sharded, sharded, sharded, P()),
        check_vma=False,
    )
```

time: 77.5 us -> 79.5 us (1.026)
  waiting for transfers between devices: 8 us -> 29 us
  starting transfers between devices: 45.1 us -> 34.8 us
  local copies, waits for them, and re-layouts: 12.4 us -> 3.17 us
    ppermute x33 -> x25, waiting for transfers between devices: 8 us -> 29 us  [swap(): lax.ppermute(array, axis, [(s, s ^ mask) for s in range(lax.axis_size(axi...]
    ppermute x33 -> x25, starting transfers between devices: 45.1 us -> 34.8 us  [swap(): lax.ppermute(array, axis, [(s, s ^ mask) for s in range(lax.axis_size(axi...]
    unnamed x50 -> x16, local copies, waits for them, and re-layouts: 12.4 us -> 3.15 us
    pallas_call x9 -> x11, Pallas kernels: 9.28 us -> 9.91 us  [the longest x2 4.08 us: local(): call(partial_body, [MEMBER, cols, cols, cols, wide] + halves + [spot] * l...]
  transfers between devices with their start and end apart: 33 -> 25, of which waited for: 10 -> 19; matrix products, arithmetic and copies ran while one was open for 1% -> 0% of each run, Pallas kernels for 12% -> 12%
where the time goes in v4:
time: 79.5 us; the launch traced here: 79.2 us
  starting transfers between devices  34.8 us (44%)
  waiting for transfers between devices  29 us (36%)
  Pallas kernels  9.91 us (12%)
  local copies, waits for them, and re-layouts  3.17 us (4%)
  other arithmetic  1.34 us (2%)
  between operations  0.93 us (1%)
    ppermute x25, starting transfers between devices, swap(): lax.ppermute(array, axis, [(s, s ^ mask) for s in range(lax.axis_size(axi...  34.8 us
    ppermute x25, waiting for transfers between devices, swap(): lax.ppermute(array, axis, [(s, s ^ mask) for s in range(lax.axis_size(axi...  29 us
    pallas_call x2, Pallas kernels, local(): call(partial_body, [MEMBER, cols, cols, cols, wide] + halves + [spot] * l...  4.08 us
    unnamed x16, local copies, waits for them, and re-layouts  3.15 us
    pallas_call x2, Pallas kernels, local(): call(final_body, [MEMBER, cols, cols, wide, wide] + tallers + [spot] * le...  2.18 us
    pallas_call x2, Pallas kernels, local(): call(norm_body, [MEMBER, cols, cols, wide, pl.BlockSpec((1, WIDE), lambda...  1.7 us
  transfers between devices with their start and end apart: 25, of which 19 were waited for; matrix products, arithmetic and copies ran while one was open for 0% of the time, Pallas kernels for 12%

profile of v4, /device:TPU:0, one launch (start us, length us, event | category | flops | bytes accessed | tf_op | source)
XLA Modules:
  0.0 79.2 jit_solution(12594549813955420444)
XLA Ops:
  3.0 3.0 %collective-permute-start.6 = (f32[2,128,128]{2,1,0:T(8,128)S(1)}, f32[2,128,128]{2,1,0:T(8,128)S(1)}, u32[]{:S(2)}, u32[]{:S(2)}) collective-permute-start(f32[2,128,128]{2,1,0:T(8,128)S(1)} %get-tuple-element.28), channel_id=1, source_target_pairs={{0,2},{2,0},{4,6},{6,4},{8,10},{10,8},{12,14},{14,12},{16,18},{18,... | collective-permute-start | bytes 393224 | tf_op jit(solution)/shard_map/ppermute | solution.py:132
  6.5 3.9 %collective-permute-done.6 = f32[2,128,128]{2,1,0:T(8,128)S(1)} collective-permute-done((f32[2,128,128]{2,1,0:T(8,128)S(1)}, f32[2,128,128]{2,1,0:T(8,128)S(1)}, u32[]{:S(2)}, u32[]{:S(2)}) %collective-permute-start.6) | collective-permute-done | bytes 131104 | tf_op jit(solution)/shard_map/ppermute | solution.py:132
  10.4 2.1 %collective-permute-start.7 = (f32[128,128]{1,0:T(8,128)S(1)}, f32[128,128]{1,0:T(8,128)S(1)}, u32[]{:S(2)}, u32[]{:S(2)}) collective-permute-start(f32[128,128]{1,0:T(8,128)S(1)} %slice_bitcast_fusion.4), channel_id=1, source_target_pairs={{0,4},{2,6},{4,0},{6,2},{8,12},{10,14},{12,8},{14,10},{16,20},{18,... | collective-permute-start | bytes 196616 | tf_op jit(solution)/shard_map/ppermute | solution.py:132
  12.6 1.6 %collective-permute-start.1 = (f32[128,128]{1,0:T(8,128)S(1)}, f32[128,128]{1,0:T(8,128)S(1)}, u32[]{:S(2)}, u32[]{:S(2)}) collective-permute-start(f32[128,128]{1,0:T(8,128)S(1)} %slice_bitcast_fusion.6), channel_id=1, source_target_pairs={{0,4},{2,6},{4,0},{6,2},{8,12},{10,14},{12,8},{14,10},{16,20},{18,... | collective-permute-start | bytes 196616 | tf_op jit(solution)/shard_map/ppermute | solution.py:132
  14.2 1.1 %collective-permute-done.7 = f32[128,128]{1,0:T(8,128)S(1)} collective-permute-done((f32[128,128]{1,0:T(8,128)S(1)}, f32[128,128]{1,0:T(8,128)S(1)}, u32[]{:S(2)}, u32[]{:S(2)}) %collective-permute-start.7) | collective-permute-done | bytes 65568 | tf_op jit(solution)/shard_map/ppermute | solution.py:132
  15.3 2.0 %collective-permute-start.8 = (f32[128,128]{1,0:T(8,128)S(1)}, f32[128,128]{1,0:T(8,128)S(1)}, u32[]{:S(2)}, u32[]{:S(2)}) collective-permute-start(f32[128,128]{1,0:T(8,128)S(1)} %fusion.3), channel_id=1, source_target_pairs={{0,8},{2,10},{4,12},{6,14},{8,0},{10,2},{12,4},{14,6},{16,24},{18,... | collective-permute-start | bytes 196616 | tf_op jit(solution)/shard_map/ppermute | solution.py:132
  17.3 1.3 %collective-permute-start.2 = (f32[128,128]{1,0:T(8,128)S(1)}, f32[128,128]{1,0:T(8,128)S(1)}, u32[]{:S(2)}, u32[]{:S(2)}) collective-permute-start(f32[128,128]{1,0:T(8,128)S(1)} %fusion.2), channel_id=1, source_target_pairs={{0,8},{2,10},{4,12},{6,14},{8,0},{10,2},{12,4},{14,6},{16,24},{18,... | collective-permute-start | bytes 196616 | tf_op jit(solution)/shard_map/ppermute | solution.py:132
  19.6 3.4 %collective-permute-start.9 = (f32[128,128]{1,0:T(8,128)S(1)}, f32[128,128]{1,0:T(8,128)S(1)}, u32[]{:S(2)}, u32[]{:S(2)}) collective-permute-start(f32[128,128]{1,0:T(8,128)S(1)} %add.127), channel_id=1, source_target_pairs={{0,16},{2,18},{4,20},{6,22},{8,24},{10,26},{12,28},{14,30},{16,0},... | collective-permute-start | bytes 196616 | tf_op jit(solution)/shard_map/ppermute | solution.py:132
  23.1 1.6 %collective-permute-start.3 = (f32[128,128]{1,0:T(8,128)S(1)}, f32[128,128]{1,0:T(8,128)S(1)}, u32[]{:S(2)}, u32[]{:S(2)}) collective-permute-start(f32[128,128]{1,0:T(8,128)S(1)} %add.118), channel_id=1, source_target_pairs={{0,16},{2,18},{4,20},{6,22},{8,24},{10,26},{12,28},{14,30},{16,0},... | collective-permute-start | bytes 196616 | tf_op jit(solution)/shard_map/ppermute | solution.py:132
  25.3 3.0 %collective-permute-done.3 = f32[128,128]{1,0:T(8,128)S(1)} collective-permute-done((f32[128,128]{1,0:T(8,128)S(1)}, f32[128,128]{1,0:T(8,128)S(1)}, u32[]{:S(2)}, u32[]{:S(2)}) %collective-permute-start.3) | collective-permute-done | bytes 65568 | tf_op jit(solution)/shard_map/ppermute | solution.py:132
  28.5 1.4 %collective-permute-start.10 = (f32[128,128]{1,0:T(8,128)S(1)}, f32[128,128]{1,0:T(8,128)S(1)}, u32[]{:S(2)}, u32[]{:S(2)}) collective-permute-start(f32[128,128]{1,0:T(8,128)S(1)} %get-tuple-element.60), channel_id=1, source_target_pairs={{0,4},{2,6},{4,0},{6,2},{8,12},{10,14},{12,8},{14,10},{16,20},{18,... | collective-permute-start | bytes 196616 | tf_op jit(solution)/shard_map/ppermute | solution.py:132
  31.3 1.5 %collective-permute-done.10 = f32[128,128]{1,0:T(8,128)S(1)} collective-permute-done((f32[128,128]{1,0:T(8,128)S(1)}, f32[128,128]{1,0:T(8,128)S(1)}, u32[]{:S(2)}, u32[]{:S(2)}) %collective-permute-start.10) | collective-permute-done | bytes 65568 | tf_op jit(solution)/shard_map/ppermute | solution.py:132
  32.8 1.3 %collective-permute-done.4 = f32[128,128]{1,0:T(8,128)S(1)} collective-permute-done((f32[128,128]{1,0:T(8,128)S(1)}, f32[128,128]{1,0:T(8,128)S(1)}, u32[]{:S(2)}, u32[]{:S(2)}) %collective-permute-start.4) | collective-permute-done | bytes 65568 | tf_op jit(solution)/shard_map/ppermute | solution.py:132
  34.3 1.6 %collective-permute-start.11 = (f32[2,128,128]{2,1,0:T(8,128)S(1)}, f32[2,128,128]{2,1,0:T(8,128)S(1)}, u32[]{:S(2)}, u32[]{:S(2)}) collective-permute-start(f32[2,128,128]{2,1,0:T(8,128)S(1)} %get-tuple-element.65), channel_id=1, source_target_pairs={{0,2},{2,0},{4,6},{6,4},{8,10},{10,8},{12,14},{14,12},{16,18},{18,... | collective-permute-start | bytes 393224 | tf_op jit(solution)/shard_map/ppermute | solution.py:132
  37.2 3.5 %collective-permute-done.11.refs_1_ = f32[2,128,128]{2,1,0:T(8,128)S(1)} collective-permute-done((f32[2,128,128]{2,1,0:T(8,128)S(1)}, f32[2,128,128]{2,1,0:T(8,128)S(1)}, u32[]{:S(2)}, u32[]{:S(2)}) %collective-permute-start.11) | collective-permute-done | bytes 131104 | tf_op jit(solution)/shard_map/ppermute | solution.py:132
  42.6 1.6 %collective-permute-start.18 = (f32[2,136,128]{2,1,0:T(8,128)S(1)}, f32[2,136,128]{2,1,0:T(8,128)S(1)}, u32[]{:S(2)}, u32[]{:S(2)}) collective-permute-start(f32[2,136,128]{2,1,0:T(8,128)S(1)} %get-tuple-element.39), channel_id=1, source_target_pairs={{0,2},{2,0},{4,6},{6,4},{8,10},{10,8},{12,14},{14,12},{16,18},{18,... | collective-permute-start | bytes 417800 | tf_op jit(solution)/shard_map/ppermute | solution.py:132
  45.6 2.1 %collective-permute-done.18 = f32[2,136,128]{2,1,0:T(8,128)S(1)} collective-permute-done((f32[2,136,128]{2,1,0:T(8,128)S(1)}, f32[2,136,128]{2,1,0:T(8,128)S(1)}, u32[]{:S(2)}, u32[]{:S(2)}) %collective-permute-start.18) | collective-permute-done | bytes 139296 | tf_op jit(solution)/shard_map/ppermute | solution.py:132
  48.5 1.6 %collective-permute-done.12 = f32[2,136,128]{2,1,0:T(8,128)S(1)} collective-permute-done((f32[2,136,128]{2,1,0:T(8,128)S(1)}, f32[2,136,128]{2,1,0:T(8,128)S(1)}, u32[]{:S(2)}, u32[]{:S(2)}) %collective-permute-start.12) | collective-permute-done | bytes 139296 | tf_op jit(solution)/shard_map/ppermute | solution.py:132
  51.0 1.1 %collective-permute-done.19 = f32[136,128]{1,0:T(8,128)S(1)} collective-permute-done((f32[136,128]{1,0:T(8,128)S(1)}, f32[136,128]{1,0:T(8,128)S(1)}, u32[]{:S(2)}, u32[]{:S(2)}) %collective-permute-start.19) | collective-permute-done | bytes 69664 | tf_op jit(solution)/shard_map/ppermute | solution.py:132
  52.1 1.7 %collective-permute-start.20 = (f32[136,128]{1,0:T(8,128)S(1)}, f32[136,128]{1,0:T(8,128)S(1)}, u32[]{:S(2)}, u32[]{:S(2)}) collective-permute-start(f32[136,128]{1,0:T(8,128)S(1)} %fusion.1), channel_id=1, source_target_pairs={{0,8},{2,10},{4,12},{6,14},{8,0},{10,2},{12,4},{14,6},{16,24},{18,... | collective-permute-start | bytes 208904 | tf_op jit(solution)/shard_map/ppermute | solution.py:132
  54.5 2.2 %collective-permute-start.14 = (f32[136,128]{1,0:T(8,128)S(1)}, f32[136,128]{1,0:T(8,128)S(1)}, u32[]{:S(2)}, u32[]{:S(2)}) collective-permute-start(f32[136,128]{1,0:T(8,128)S(1)} %fusion), channel_id=1, source_target_pairs={{0,8},{2,10},{4,12},{6,14},{8,0},{10,2},{12,4},{14,6},{16,24},{18,... | collective-permute-start | bytes 208904 | tf_op jit(solution)/shard_map/ppermute | solution.py:132
  56.8 1.5 %collective-permute-start.21 = (f32[136,128]{1,0:T(8,128)S(1)}, f32[136,128]{1,0:T(8,128)S(1)}, u32[]{:S(2)}, u32[]{:S(2)}) collective-permute-start(f32[136,128]{1,0:T(8,128)S(1)} %add.145), channel_id=1, source_target_pairs={{0,16},{2,18},{4,20},{6,22},{8,24},{10,26},{12,28},{14,30},{16,0},... | collective-permute-start | bytes 208904 | tf_op jit(solution)/shard_map/ppermute | solution.py:132
  59.1 1.9 %collective-permute-start.15 = (f32[136,128]{1,0:T(8,128)S(1)}, f32[136,128]{1,0:T(8,128)S(1)}, u32[]{:S(2)}, u32[]{:S(2)}) collective-permute-start(f32[136,128]{1,0:T(8,128)S(1)} %add.136), channel_id=1, source_target_pairs={{0,16},{2,18},{4,20},{6,22},{8,24},{10,26},{12,28},{14,30},{16,0},... | collective-permute-start | bytes 208904 | tf_op jit(solution)/shard_map/ppermute | solution.py:132
  61.0 1.1 %collective-permute-done.21 = f32[136,128]{1,0:T(8,128)S(1)} collective-permute-done((f32[136,128]{1,0:T(8,128)S(1)}, f32[136,128]{1,0:T(8,128)S(1)}, u32[]{:S(2)}, u32[]{:S(2)}) %collective-permute-start.21) | collective-permute-done | bytes 69664 | tf_op jit(solution)/shard_map/ppermute | solution.py:132
  62.1 2.3 %collective-permute-done.15 = f32[136,128]{1,0:T(8,128)S(1)} collective-permute-done((f32[136,128]{1,0:T(8,128)S(1)}, f32[136,128]{1,0:T(8,128)S(1)}, u32[]{:S(2)}, u32[]{:S(2)}) %collective-permute-start.15) | collective-permute-done | bytes 69664 | tf_op jit(solution)/shard_map/ppermute | solution.py:132
  65.2 1.4 %collective-permute-start.22 = (f32[136,128]{1,0:T(8,128)S(1)}, f32[136,128]{1,0:T(8,128)S(1)}, u32[]{:S(2)}, u32[]{:S(2)}) collective-permute-start(f32[136,128]{1,0:T(8,128)S(1)} %get-tuple-element.62), channel_id=1, source_target_pairs={{0,4},{2,6},{4,0},{6,2},{8,12},{10,14},{12,8},{14,10},{16,20},{18,... | collective-permute-start | bytes 208904 | tf_op jit(solution)/shard_map/ppermute | solution.py:132
  66.6 2.0 %partial.2 = (bf16[256,1024]{1,0:T(8,128)(2,1)}, f32[256,512]{1,0:T(8,128)S(1)}, f32[256,512]{1,0:T(8,128)S(1)}) custom-call(s32[1]{0:T(128)} %bitcast.member_ref, bf16[256,1024]{1,0:T(8,128)(2,1)S(1)} %bitcast.75, bf16[256,1024]{1,0:T(8,128)(2,1)S(1)} %bitcast.59, bf16[256,1024]{1,0:T(8,128)(2,1)S(1)} %bitcast.67, ...), custom_call_target="tpu_custom_call" | custom-call | flops 1610612736 | bytes 2097152 | tf_op jit(solution)/shard_map/partial/pallas_call | solution.py:199
  69.8 1.3 %collective-permute-start.17 = (f32[2,136,128]{2,1,0:T(8,128)S(1)}, f32[2,136,128]{2,1,0:T(8,128)S(1)}, u32[]{:S(2)}, u32[]{:S(2)}) collective-permute-start(f32[2,136,128]{2,1,0:T(8,128)S(1)} %get-tuple-element.54), channel_id=1, source_target_pairs={{0,2},{2,0},{4,6},{6,4},{8,10},{10,8},{12,14},{14,12},{16,18},{18,... | collective-permute-start | bytes 417800 | tf_op jit(solution)/shard_map/ppermute | solution.py:132
  71.9 2.0 %partial.3 = (bf16[256,1024]{1,0:T(8,128)(2,1)}, f32[256,512]{1,0:T(8,128)S(1)}, f32[256,512]{1,0:T(8,128)S(1)}) custom-call(s32[1]{0:T(128)} %bitcast.member_ref, bf16[256,1024]{1,0:T(8,128)(2,1)S(1)} %bitcast.76, bf16[256,1024]{1,0:T(8,128)(2,1)S(1)} %bitcast.60, bf16[256,1024]{1,0:T(8,128)(2,1)S(1)} %bitcast.68, ...), custom_call_target="tpu_custom_call", output_to_operand_aliasing={{0}: (7, {})} | custom-call | flops 1610612736 | bytes 2097152 | tf_op jit(solution)/shard_map/partial/pallas_call | solution.py:199
  74.9 1.5 %collective-permute-done.23.refs_1_ = f32[2,136,128]{2,1,0:T(8,128)S(1)} collective-permute-done((f32[2,136,128]{2,1,0:T(8,128)S(1)}, f32[2,136,128]{2,1,0:T(8,128)S(1)}, u32[]{:S(2)}, u32[]{:S(2)}) %collective-permute-start.23) | collective-permute-done | bytes 139296 | tf_op jit(solution)/shard_map/ppermute | solution.py:132
  76.4 1.1 %final.2 = (bf16[256,1024]{1,0:T(8,128)(2,1)}, bf16[256,1024]{1,0:T(8,128)(2,1)}) custom-call(s32[1]{0:T(128)} %bitcast.member_ref, bf16[256,1024]{1,0:T(8,128)(2,1)S(1)} %bitcast.61, bf16[256,1024]{1,0:T(8,128)(2,1)S(1)} %bitcast.69, f32[256,512]{1,0:T(8,128)S(1)} %get-tuple-element.36.key_part_ref, f32[256,512]{1,0:T(8,128)S(1)} %get-tuple-element.37.value_part_ref, ...), custom_call_target="tpu_custom_call" | custom-call | flops 536870912 | bytes 2097152 | tf_op jit(solution)/shard_map/final/pallas_call | solution.py:221
  77.5 1.1 %final.3 = (bf16[256,1024]{1,0:T(8,128)(2,1)}, bf16[256,1024]{1,0:T(8,128)(2,1)}) custom-call(s32[1]{0:T(128)} %bitcast.member_ref, bf16[256,1024]{1,0:T(8,128)(2,1)S(1)} %bitcast.62, bf16[256,1024]{1,0:T(8,128)(2,1)S(1)} %bitcast.70, f32[256,512]{1,0:T(8,128)S(1)} %get-tuple-element.32.key_part_ref, ...), custom_call_target="tpu_custom_call", output_to_operand_aliasing={{0}: (7, {}), {1}: (8, {})} | custom-call | flops 536870912 | bytes 2097152 | tf_op jit(solution)/shard_map/final/pallas_call | solution.py:221
  (74 shorter events, 18.2 us)
Async XLA Ops:
  0.6 1.0 %copy-start = (bf16[1,256,1024]{2,1,0:T(8,128)(2,1)S(1)}, bf16[1,256,1024]{2,1,0:T(8,128)(2,1)}, u32[]{:S(2)}) copy-start(bf16[1,256,1024]{2,1,0:T(8,128)(2,1)} %param.6) | copy-start | bytes 1572868
  3.0 7.3 %collective-permute-start.6 = (f32[2,128,128]{2,1,0:T(8,128)S(1)}, f32[2,128,128]{2,1,0:T(8,128)S(1)}, u32[]{:S(2)}, u32[]{:S(2)}) collective-permute-start(f32[2,128,128]{2,1,0:T(8,128)S(1)} %get-tuple-element.28), channel_id=1, source_target_pairs={{0,2},{2,0},{4,6},{6,4},{8,10},{10,8},{12,14},{14,12},{16,18},{18,... | collective-permute-start | bytes 393224 | tf_op jit(solution)/shard_map/ppermute | solution.py:132
  6.3 6.2 %collective-permute-start = (f32[2,128,128]{2,1,0:T(8,128)S(1)}, f32[2,128,128]{2,1,0:T(8,128)S(1)}, u32[]{:S(2)}, u32[]{:S(2)}) collective-permute-start(f32[2,128,128]{2,1,0:T(8,128)S(1)} %get-tuple-element.25), channel_id=1, source_target_pairs={{0,2},{2,0},{4,6},{6,4},{8,10},{10,8},{12,14},{14,12},{16,18},{18,... | collective-permute-start | bytes 393224 | tf_op jit(solution)/shard_map/ppermute | solution.py:132
  10.4 4.9 %collective-permute-start.7 = (f32[128,128]{1,0:T(8,128)S(1)}, f32[128,128]{1,0:T(8,128)S(1)}, u32[]{:S(2)}, u32[]{:S(2)}) collective-permute-start(f32[128,128]{1,0:T(8,128)S(1)} %slice_bitcast_fusion.4), channel_id=1, source_target_pairs={{0,4},{2,6},{4,0},{6,2},{8,12},{10,14},{12,8},{14,10},{16,20},{18,... | collective-permute-start | bytes 196616 | tf_op jit(solution)/shard_map/ppermute | solution.py:132
  12.6 4.7 %collective-permute-start.1 = (f32[128,128]{1,0:T(8,128)S(1)}, f32[128,128]{1,0:T(8,128)S(1)}, u32[]{:S(2)}, u32[]{:S(2)}) collective-permute-start(f32[128,128]{1,0:T(8,128)S(1)} %slice_bitcast_fusion.6), channel_id=1, source_target_pairs={{0,4},{2,6},{4,0},{6,2},{8,12},{10,14},{12,8},{14,10},{16,20},{18,... | collective-permute-start | bytes 196616 | tf_op jit(solution)/shard_map/ppermute | solution.py:132
  15.3 15.3 %copy-start.4 = (bf16[1,256,1024]{2,1,0:T(8,128)(2,1)S(1)}, bf16[1,256,1024]{2,1,0:T(8,128)(2,1)}, u32[]{:S(2)}) copy-start(bf16[1,256,1024]{2,1,0:T(8,128)(2,1)} %param.5) | copy-start | bytes 1572868
  15.3 4.3 %collective-permute-start.8 = (f32[128,128]{1,0:T(8,128)S(1)}, f32[128,128]{1,0:T(8,128)S(1)}, u32[]{:S(2)}, u32[]{:S(2)}) collective-permute-start(f32[128,128]{1,0:T(8,128)S(1)} %fusion.3), channel_id=1, source_target_pairs={{0,8},{2,10},{4,12},{6,14},{8,0},{10,2},{12,4},{14,6},{16,24},{18,... | collective-permute-start | bytes 196616 | tf_op jit(solution)/shard_map/ppermute | solution.py:132
  17.3 5.7 %collective-permute-start.2 = (f32[128,128]{1,0:T(8,128)S(1)}, f32[128,128]{1,0:T(8,128)S(1)}, u32[]{:S(2)}, u32[]{:S(2)}) collective-permute-start(f32[128,128]{1,0:T(8,128)S(1)} %fusion.2), channel_id=1, source_target_pairs={{0,8},{2,10},{4,12},{6,14},{8,0},{10,2},{12,4},{14,6},{16,24},{18,... | collective-permute-start | bytes 196616 | tf_op jit(solution)/shard_map/ppermute | solution.py:132
  19.6 11.0 %copy-start.1 = (bf16[1,256,1024]{2,1,0:T(8,128)(2,1)S(1)}, bf16[1,256,1024]{2,1,0:T(8,128)(2,1)}, u32[]{:S(2)}) copy-start(bf16[1,256,1024]{2,1,0:T(8,128)(2,1)} %param.6) | copy-start | bytes 1572868
  19.6 11.0 %copy-start.3 = (bf16[1,256,1024]{2,1,0:T(8,128)(2,1)S(1)}, bf16[1,256,1024]{2,1,0:T(8,128)(2,1)}, u32[]{:S(2)}) copy-start(bf16[1,256,1024]{2,1,0:T(8,128)(2,1)} %param.7) | copy-start | bytes 1572868
  19.6 5.7 %collective-permute-start.9 = (f32[128,128]{1,0:T(8,128)S(1)}, f32[128,128]{1,0:T(8,128)S(1)}, u32[]{:S(2)}, u32[]{:S(2)}) collective-permute-start(f32[128,128]{1,0:T(8,128)S(1)} %add.127), channel_id=1, source_target_pairs={{0,16},{2,18},{4,20},{6,22},{8,24},{10,26},{12,28},{14,30},{16,0},... | collective-permute-start | bytes 196616 | tf_op jit(solution)/shard_map/ppermute | solution.py:132
  23.1 5.2 %collective-permute-start.3 = (f32[128,128]{1,0:T(8,128)S(1)}, f32[128,128]{1,0:T(8,128)S(1)}, u32[]{:S(2)}, u32[]{:S(2)}) collective-permute-start(f32[128,128]{1,0:T(8,128)S(1)} %add.118), channel_id=1, source_target_pairs={{0,16},{2,18},{4,20},{6,22},{8,24},{10,26},{12,28},{14,30},{16,0},... | collective-permute-start | bytes 196616 | tf_op jit(solution)/shard_map/ppermute | solution.py:132
  28.5 4.3 %collective-permute-start.10 = (f32[128,128]{1,0:T(8,128)S(1)}, f32[128,128]{1,0:T(8,128)S(1)}, u32[]{:S(2)}, u32[]{:S(2)}) collective-permute-start(f32[128,128]{1,0:T(8,128)S(1)} %get-tuple-element.60), channel_id=1, source_target_pairs={{0,4},{2,6},{4,0},{6,2},{8,12},{10,14},{12,8},{14,10},{16,20},{18,... | collective-permute-start | bytes 196616 | tf_op jit(solution)/shard_map/ppermute | solution.py:132
  29.9 4.3 %collective-permute-start.4 = (f32[128,128]{1,0:T(8,128)S(1)}, f32[128,128]{1,0:T(8,128)S(1)}, u32[]{:S(2)}, u32[]{:S(2)}) collective-permute-start(f32[128,128]{1,0:T(8,128)S(1)} %get-tuple-element.51), channel_id=1, source_target_pairs={{0,4},{2,6},{4,0},{6,2},{8,12},{10,14},{12,8},{14,10},{16,20},{18,... | collective-permute-start | bytes 196616 | tf_op jit(solution)/shard_map/ppermute | solution.py:132
  34.3 6.4 %collective-permute-start.11 = (f32[2,128,128]{2,1,0:T(8,128)S(1)}, f32[2,128,128]{2,1,0:T(8,128)S(1)}, u32[]{:S(2)}, u32[]{:S(2)}) collective-permute-start(f32[2,128,128]{2,1,0:T(8,128)S(1)} %get-tuple-element.65), channel_id=1, source_target_pairs={{0,2},{2,0},{4,6},{6,4},{8,10},{10,8},{12,14},{14,12},{16,18},{18,... | collective-permute-start | bytes 393224 | tf_op jit(solution)/shard_map/ppermute | solution.py:132
  36.6 4.1 %copy-start.7 = (f32[1024]{0:T(1024)S(1)}, f32[1024]{0:T(1024)}, u32[]{:S(2)}) copy-start(f32[1024]{0:T(1024)} %param.8) | copy-start | bytes 12292
  36.6 7.5 %collective-permute-start.5 = (f32[2,128,128]{2,1,0:T(8,128)S(1)}, f32[2,128,128]{2,1,0:T(8,128)S(1)}, u32[]{:S(2)}, u32[]{:S(2)}) collective-permute-start(f32[2,128,128]{2,1,0:T(8,128)S(1)} %get-tuple-element.58), channel_id=1, source_target_pairs={{0,2},{2,0},{4,6},{6,4},{8,10},{10,8},{12,14},{14,12},{16,18},{18,... | collective-permute-start | bytes 393224 | tf_op jit(solution)/shard_map/ppermute | solution.py:132
  40.7 1.0 %copy-start.5 = (bf16[1,256,1024]{2,1,0:T(8,128)(2,1)S(1)}, bf16[1,256,1024]{2,1,0:T(8,128)(2,1)}, u32[]{:S(2)}) copy-start(bf16[1,256,1024]{2,1,0:T(8,128)(2,1)} %param.9) | copy-start | bytes 1572868
  41.7 2.4 %copy-start.6 = (bf16[1,256,1024]{2,1,0:T(8,128)(2,1)S(1)}, bf16[1,256,1024]{2,1,0:T(8,128)(2,1)}, u32[]{:S(2)}) copy-start(bf16[1,256,1024]{2,1,0:T(8,128)(2,1)} %param.9) | copy-start | bytes 1572868
  42.6 5.1 %collective-permute-start.18 = (f32[2,136,128]{2,1,0:T(8,128)S(1)}, f32[2,136,128]{2,1,0:T(8,128)S(1)}, u32[]{:S(2)}, u32[]{:S(2)}) collective-permute-start(f32[2,136,128]{2,1,0:T(8,128)S(1)} %get-tuple-element.39), channel_id=1, source_target_pairs={{0,2},{2,0},{4,6},{6,4},{8,10},{10,8},{12,14},{14,12},{16,18},{18,... | collective-permute-start | bytes 417800 | tf_op jit(solution)/shard_map/ppermute | solution.py:132
  45.0 5.1 %collective-permute-start.12 = (f32[2,136,128]{2,1,0:T(8,128)S(1)}, f32[2,136,128]{2,1,0:T(8,128)S(1)}, u32[]{:S(2)}, u32[]{:S(2)}) collective-permute-start(f32[2,136,128]{2,1,0:T(8,128)S(1)} %get-tuple-element.35), channel_id=1, source_target_pairs={{0,2},{2,0},{4,6},{6,4},{8,10},{10,8},{12,14},{14,12},{16,18},{18,... | collective-permute-start | bytes 417800 | tf_op jit(solution)/shard_map/ppermute | solution.py:132
  47.7 4.4 %collective-permute-start.19 = (f32[136,128]{1,0:T(8,128)S(1)}, f32[136,128]{1,0:T(8,128)S(1)}, u32[]{:S(2)}, u32[]{:S(2)}) collective-permute-start(f32[136,128]{1,0:T(8,128)S(1)} %slice_bitcast_fusion), channel_id=1, source_target_pairs={{0,4},{2,6},{4,0},{6,2},{8,12},{10,14},{12,8},{14,10},{16,20},{18,... | collective-permute-start | bytes 208904 | tf_op jit(solution)/shard_map/ppermute | solution.py:132
  50.2 4.4 %collective-permute-start.13 = (f32[136,128]{1,0:T(8,128)S(1)}, f32[136,128]{1,0:T(8,128)S(1)}, u32[]{:S(2)}, u32[]{:S(2)}) collective-permute-start(f32[136,128]{1,0:T(8,128)S(1)} %slice_bitcast_fusion.2), channel_id=1, source_target_pairs={{0,4},{2,6},{4,0},{6,2},{8,12},{10,14},{12,8},{14,10},{16,20},{18,... | collective-permute-start | bytes 208904 | tf_op jit(solution)/shard_map/ppermute | solution.py:132
  52.1 4.7 %collective-permute-start.20 = (f32[136,128]{1,0:T(8,128)S(1)}, f32[136,128]{1,0:T(8,128)S(1)}, u32[]{:S(2)}, u32[]{:S(2)}) collective-permute-start(f32[136,128]{1,0:T(8,128)S(1)} %fusion.1), channel_id=1, source_target_pairs={{0,8},{2,10},{4,12},{6,14},{8,0},{10,2},{12,4},{14,6},{16,24},{18,... | collective-permute-start | bytes 208904 | tf_op jit(solution)/shard_map/ppermute | solution.py:132
  54.5 4.5 %collective-permute-start.14 = (f32[136,128]{1,0:T(8,128)S(1)}, f32[136,128]{1,0:T(8,128)S(1)}, u32[]{:S(2)}, u32[]{:S(2)}) collective-permute-start(f32[136,128]{1,0:T(8,128)S(1)} %fusion), channel_id=1, source_target_pairs={{0,8},{2,10},{4,12},{6,14},{8,0},{10,2},{12,4},{14,6},{16,24},{18,... | collective-permute-start | bytes 208904 | tf_op jit(solution)/shard_map/ppermute | solution.py:132
  56.8 5.3 %collective-permute-start.21 = (f32[136,128]{1,0:T(8,128)S(1)}, f32[136,128]{1,0:T(8,128)S(1)}, u32[]{:S(2)}, u32[]{:S(2)}) collective-permute-start(f32[136,128]{1,0:T(8,128)S(1)} %add.145), channel_id=1, source_target_pairs={{0,16},{2,18},{4,20},{6,22},{8,24},{10,26},{12,28},{14,30},{16,0},... | collective-permute-start | bytes 208904 | tf_op jit(solution)/shard_map/ppermute | solution.py:132
  59.1 5.3 %collective-permute-start.15 = (f32[136,128]{1,0:T(8,128)S(1)}, f32[136,128]{1,0:T(8,128)S(1)}, u32[]{:S(2)}, u32[]{:S(2)}) collective-permute-start(f32[136,128]{1,0:T(8,128)S(1)} %add.136), channel_id=1, source_target_pairs={{0,16},{2,18},{4,20},{6,22},{8,24},{10,26},{12,28},{14,30},{16,0},... | collective-permute-start | bytes 208904 | tf_op jit(solution)/shard_map/ppermute | solution.py:132
  64.5 4.4 %collective-permute-start.16 = (f32[136,128]{1,0:T(8,128)S(1)}, f32[136,128]{1,0:T(8,128)S(1)}, u32[]{:S(2)}, u32[]{:S(2)}) collective-permute-start(f32[136,128]{1,0:T(8,128)S(1)} %get-tuple-element.47), channel_id=1, source_target_pairs={{0,4},{2,6},{4,0},{6,2},{8,12},{10,14},{12,8},{14,10},{16,20},{18,... | collective-permute-start | bytes 208904 | tf_op jit(solution)/shard_map/ppermute | solution.py:132
  65.2 4.5 %collective-permute-start.22 = (f32[136,128]{1,0:T(8,128)S(1)}, f32[136,128]{1,0:T(8,128)S(1)}, u32[]{:S(2)}, u32[]{:S(2)}) collective-permute-start(f32[136,128]{1,0:T(8,128)S(1)} %get-tuple-element.62), channel_id=1, source_target_pairs={{0,4},{2,6},{4,0},{6,2},{8,12},{10,14},{12,8},{14,10},{16,20},{18,... | collective-permute-start | bytes 208904 | tf_op jit(solution)/shard_map/ppermute | solution.py:132
  69.8 5.1 %collective-permute-start.17 = (f32[2,136,128]{2,1,0:T(8,128)S(1)}, f32[2,136,128]{2,1,0:T(8,128)S(1)}, u32[]{:S(2)}, u32[]{:S(2)}) collective-permute-start(f32[2,136,128]{2,1,0:T(8,128)S(1)} %get-tuple-element.54), channel_id=1, source_target_pairs={{0,2},{2,0},{4,6},{6,4},{8,10},{10,8},{12,14},{14,12},{16,18},{18,... | collective-permute-start | bytes 417800 | tf_op jit(solution)/shard_map/ppermute | solution.py:132
  71.1 5.3 %collective-permute-start.23 = (f32[2,136,128]{2,1,0:T(8,128)S(1)}, f32[2,136,128]{2,1,0:T(8,128)S(1)}, u32[]{:S(2)}, u32[]{:S(2)}) collective-permute-start(f32[2,136,128]{2,1,0:T(8,128)S(1)} %get-tuple-element.67), channel_id=1, source_target_pairs={{0,2},{2,0},{4,6},{6,4},{8,10},{10,8},{12,14},{14,12},{16,18},{18,... | collective-permute-start | bytes 417800 | tf_op jit(solution)/shard_map/ppermute | solution.py:132
  76.4 2.2 %collective-permute-start.24 = (f32[8,128]{1,0:T(8,128)S(1)}, f32[8,128]{1,0:T(8,128)S(1)}, u32[]{:S(2)}, u32[]{:S(2)}) collective-permute-start(f32[8,128]{1,0:T(8,128)S(1)} %gain.1), channel_id=1, source_target_pairs={{0,1},{1,0},{2,3},{3,2},{4,5},{5,4},{6,7},{7,6},{8,9},{9,8},{10,11... | collective-permute-start | bytes 12296 | tf_op jit(solution)/shard_map/ppermute | solution.py:132
  (1 other events, 1.0 us)

commit v5 on v4

v5 whole, which is shorter than its diff:
```python
import functools
import math

import jax
import jax.numpy as jnp
from jax import lax
from jax.experimental import pallas as pl
from jax.experimental.pallas import tpu as pltpu
from jax.sharding import PartitionSpec as P

HEADS = 8
DH = 128
BLOCK = 256
GROUP = 8
CHUNKS = 2
CHUNK_HEADS = HEADS // CHUNKS
WIDE = CHUNK_HEADS * DH
GAIN_ROWS = 8
EPSILON = 1e-06

NT = (((1,), (1,)), ((), ()))
TN = (((0,), (0,)), ((), ()))
NN = (((1,), (0,)), ((), ()))


def dot(left, right, dims):
    return lax.dot_general(left, right, dims, preferred_element_type=jnp.float32)


def columns(member, mask):
    return pl.ds(pl.multiple_of((member ^ mask) * DH, DH), DH)


def causal():
    shape = (BLOCK, BLOCK)
    return lax.broadcasted_iota(jnp.int32, shape, 0) >= lax.broadcasted_iota(jnp.int32, shape, 1)


def delta_body(member_ref, key_ref, value_ref, *delta_refs):
    for mask, delta_ref in enumerate(delta_refs):
        at = columns(member_ref[0], mask)
        delta_ref[...] = dot(key_ref[:, at], value_ref[:, at], TN)


def inner_body(query_ref, key_ref, value_ref, inner_ref):
    keep = causal()
    for head in range(HEADS):
        at = pl.ds(head * DH, DH)
        raw = dot(query_ref[:, at], key_ref[:, at], NT)
        scores = jnp.where(keep, raw, 0.0).astype(jnp.bfloat16)
        inner_ref[:, at] = dot(scores, value_ref[:, at], NN)


def norm_body(member_ref, query_ref, grad_ref, inner_ref, gain_ref, *refs):
    state_refs, (attn_ref, low_ref, *delta_refs) = refs[:GROUP], refs[GROUP:]
    for mask, (state_ref, delta_ref) in enumerate(zip(state_refs, delta_refs)):
        at = columns(member_ref[0], mask)
        query = query_ref[:, at]
        state = state_ref[...].astype(jnp.bfloat16)
        low_ref[pl.ds(member_ref[0] ^ mask, 1)] = state[None]
        attn = inner_ref[:, at] + dot(query, state, NN)
        root = jnp.sqrt(jnp.mean(attn * attn, axis=-1, keepdims=True) + EPSILON)
        normed = attn / root
        cotangent = grad_ref[:, at].astype(jnp.float32)
        scaled = gain_ref[:, at] * cotangent
        shared = jnp.mean(normed * scaled, axis=-1, keepdims=True)
        grad_attn = ((scaled - normed * shared) / root).astype(jnp.bfloat16)
        attn_ref[:, at] = grad_attn
        terms = jnp.sum(normed * cotangent, axis=0, keepdims=True)
        delta_ref[:DH] = dot(query, grad_attn, TN)
        delta_ref[DH:] = jnp.broadcast_to(terms, (GAIN_ROWS, DH))


def partial_body(query_ref, key_ref, value_ref, attn_ref, state_ref, *refs):
    grad_query_ref, key_part_ref, value_part_ref = refs[-3:]
    keep = causal()
    for head in range(CHUNK_HEADS):
        at = pl.ds(head * DH, DH)
        query, key, value, grad_attn = query_ref[:, at], key_ref[:, at], value_ref[:, at], attn_ref[:, at]
        scores = jnp.where(keep, dot(query, key, NT), 0.0).astype(jnp.bfloat16)
        grad_scores = jnp.where(keep, dot(grad_attn, value, NT), 0.0).astype(jnp.bfloat16)
        carried = dot(grad_attn, state_ref[head], NT)
        grad_query_ref[:, at] = (dot(grad_scores, key, NN) + carried).astype(jnp.bfloat16)
        key_part_ref[:, at] = dot(grad_scores, query, TN)
        value_part_ref[:, at] = dot(scores, grad_attn, TN)


def final_body(member_ref, key_ref, value_ref, key_part_ref, value_part_ref, *refs):
    state_refs, (grad_key_ref, grad_value_ref) = refs[:GROUP], refs[GROUP:]
    for mask, state_ref in enumerate(state_refs):
        at = columns(member_ref[0], mask)
        state = state_ref[:DH].astype(jnp.bfloat16)
        grad_key_ref[:, at] = (key_part_ref[:, at] + dot(value_ref[:, at], state, NT)).astype(jnp.bfloat16)
        grad_value_ref[:, at] = (value_part_ref[:, at] + dot(key_ref[:, at], state, NN)).astype(jnp.bfloat16)


def prefix_body(reverse, member_ref, carried_ref, total_ref, *refs):
    held_refs, back_refs, ahead = refs[:GROUP], refs[GROUP:-1], refs[-1]
    for mask, held_ref in enumerate(held_refs):
        ahead[pl.ds(member_ref[0] ^ mask, 1)] = held_ref[:DH][None]
    running = carried_ref[:DH]
    for member in reversed(range(GROUP)) if reverse else range(GROUP):
        own = ahead[member]
        ahead[member] = running
        running = running + own
    for mask, back_ref in enumerate(back_refs):
        back_ref[:DH] = ahead[pl.ds(member_ref[0] ^ mask, 1)][0]
        if back_ref.shape[0] > DH:
            back_ref[DH:] = total_ref[DH:]


def gain_body(member_ref, *refs):
    for mask, piece_ref in enumerate(refs[:-1]):
        refs[-1][pl.ds(member_ref[0] ^ mask, 1), :] = piece_ref[DH : DH + 1, :]


def whole(*shape):
    return pl.BlockSpec(shape, lambda step: (0,) * len(shape))


def part_of(chain):
    return pl.BlockSpec((BLOCK, WIDE), lambda step: (0, chain))


MEMBER = pl.BlockSpec(memory_space=pltpu.SMEM)


def call(body, in_specs, out_specs, outs, flops, name, aliases=None, scratch=()):
    return pl.pallas_call(
        body,
        grid=(1,),
        in_specs=in_specs,
        out_specs=out_specs,
        out_shape=outs,
        input_output_aliases=aliases or {},
        scratch_shapes=scratch,
        compiler_params=pltpu.CompilerParams(vmem_limit_bytes=16 * 1024 * 1024),
        cost_estimate=pl.CostEstimate(flops=flops, bytes_accessed=2 << 20, transcendentals=0),
        name=name,
    )


def swap(array, axis, mask):
    if mask == 0:
        return array
    return lax.ppermute(array, axis, [(s, s ^ mask) for s in range(lax.axis_size(axis))])


def carried_in(held, axis, member, reverse):
    count, place = lax.axis_size(axis), lax.axis_index(axis)
    held = [swap(piece, axis, mask) for mask, piece in enumerate(held)]
    total = sum(held[1:], held[0])
    carried = jnp.zeros_like(total)
    mask = GROUP
    while mask < count:
        arrived = swap(total, axis, mask)
        later = ((place & mask) != 0) != reverse
        carried = carried + jnp.where(later, arrived, 0.0)
        total = total + arrived
        mask *= 2
    specs = [whole(*total.shape)] * GROUP
    back = call(
        functools.partial(prefix_body, reverse),
        [MEMBER] + specs[:2] + specs,
        specs,
        [jax.ShapeDtypeStruct(total.shape, jnp.float32)] * GROUP,
        1 << 24,
        "prefix",
        scratch=[pltpu.VMEM((GROUP, DH, DH), jnp.float32)],
    )(member, carried, total, *held)
    return [swap(piece, axis, mask) for mask, piece in enumerate(back)]


def local(queries, keys, values, out_gain, grad_out):
    full = queries.shape
    flat = (full[0] * full[1], full[2])
    assert flat == (BLOCK, HEADS * DH)
    query, key, value, grad = (a.reshape(flat) for a in (queries, keys, values, grad_out))
    gain = out_gain.reshape(1, HEADS * DH)
    assert lax.axis_size("seq") % GROUP == 0
    member = lax.rem(lax.axis_index("seq"), GROUP).astype(jnp.int32).reshape(1)
    square = jax.ShapeDtypeStruct((DH, DH), jnp.float32)
    taller = jax.ShapeDtypeStruct((DH + GAIN_ROWS, DH), jnp.float32)
    full_float = jax.ShapeDtypeStruct(flat, jnp.float32)
    full_low = jax.ShapeDtypeStruct(flat, jnp.bfloat16)
    states_low = jax.ShapeDtypeStruct((HEADS, DH, DH), jnp.bfloat16)
    squares = [whole(*square.shape)] * GROUP
    tallers = [whole(*taller.shape)] * GROUP
    wide = whole(*flat)
    spot = pl.BlockSpec(memory_space=pl.ANY)
    unit = 2 * BLOCK * DH * DH * HEADS

    deltas = call(delta_body, [MEMBER, wide, wide], squares, [square] * GROUP, 6 * unit, "delta")(member, key, value)
    states = carried_in(deltas, "seq", member, False)
    inner = call(inner_body, [wide] * 3, wide, full_float, 16 * unit, "inner")(query, key, value)
    attn, low, *deltas = call(
        norm_body,
        [MEMBER, wide, wide, wide, whole(1, HEADS * DH)] + squares,
        [wide, whole(*states_low.shape)] + tallers,
        [full_low, states_low] + [taller] * GROUP,
        16 * unit,
        "norm",
    )(member, query, grad, inner, gain, *states)
    later = carried_in(deltas, "seq", member, True)
    parts = []
    for chunk in range(CHUNKS):
        cols = part_of(chunk)
        parts = call(
            partial_body,
            [cols] * 4 + [pl.BlockSpec((CHUNK_HEADS, DH, DH), lambda step, c=chunk: (c, 0, 0))] + [spot] * len(parts),
            [cols] * 3,
            [full_low, full_float, full_float],
            24 * unit,
            "partial",
            {5: 0, 6: 1, 7: 2} if parts else None,
        )(query, key, value, attn, low, *parts)
    grad_query, *parts = parts

    gain_terms = call(
        gain_body, [MEMBER] + tallers, whole(HEADS, DH), jax.ShapeDtypeStruct((HEADS, DH), jnp.float32), unit, "gain"
    )(member, *later)
    mask = 1
    while mask < lax.axis_size("dp"):
        gain_terms = gain_terms + swap(gain_terms, "dp", mask)
        mask *= 2
    grad_key, grad_value = call(
        final_body, [MEMBER] + [wide] * 4 + tallers, [wide] * 2, [full_low] * 2, 16 * unit, "final"
    )(member, key, value, *parts, *later)
    positions = lax.axis_size("seq") * lax.axis_size("dp") * BLOCK
    grad_gain = gain_terms.reshape(HEADS * DH) / math.sqrt(positions)
    return (grad_query.reshape(full), grad_key.reshape(full), grad_value.reshape(full), grad_gain)


def solution(mesh):
    sharded = P("dp", "seq", None)
    return jax.shard_map(
        local,
        mesh=mesh,
        in_specs=(sharded, sharded, sharded, P(), sharded),
        out_specs=(sharded, sharded, sharded, P()),
        check_vma=False,
    )
```

time: 79.5 us -> 76 us (0.956)
  waiting for transfers between devices: 29 us -> 18.3 us
  starting transfers between devices: 34.8 us -> 45.1 us
  Pallas kernels: 9.91 us -> 8.79 us
  local copies, waits for them, and re-layouts: 3.17 us -> 2.1 us
    ppermute x25 -> x31, waiting for transfers between devices: 29 us -> 18.3 us  [swap(): lax.ppermute(array, axis, [(s, s ^ mask) for s in range(lax.axis_size(axi...]
    ppermute x25 -> x31, starting transfers between devices: 34.8 us -> 45.1 us  [swap(): lax.ppermute(array, axis, [(s, s ^ mask) for s in range(lax.axis_size(axi...]
    pallas_call x11 -> x9, Pallas kernels: 9.91 us -> 8.79 us  [the longest x2 4.08 us: local(): call(partial_body, [cols] * 4 + [pl.BlockSpec((CHUNK_HEADS, DH, DH), lamb...]
    unnamed x16 -> x14, local copies, waits for them, and re-layouts: 3.15 us -> 2.1 us
  transfers between devices with their start and end apart: 25 -> 31, of which waited for: 19 -> 13; matrix products, arithmetic and copies ran while one was open for 0% -> 0% of each run, Pallas kernels for 12% -> 9%
where the time goes in v5:
time: 76 us; the launch traced here: 75.8 us
  starting transfers between devices  45.1 us (59%)
  waiting for transfers between devices  18.3 us (24%)
  Pallas kernels  8.79 us (12%)
  local copies, waits for them, and re-layouts  2.1 us (3%)
  between operations  0.8 us (1%)
    ppermute x31, starting transfers between devices, swap(): lax.ppermute(array, axis, [(s, s ^ mask) for s in range(lax.axis_size(axi...  45.1 us
    ppermute x31, waiting for transfers between devices, swap(): lax.ppermute(array, axis, [(s, s ^ mask) for s in range(lax.axis_size(axi...  18.3 us
    pallas_call x2, Pallas kernels, local(): call(partial_body, [cols] * 4 + [pl.BlockSpec((CHUNK_HEADS, DH, DH), lamb...  4.08 us
    unnamed x14, local copies, waits for them, and re-layouts  2.1 us
    pallas_call x1, Pallas kernels, local(): call(final_body, [MEMBER] + [wide] * 4 + tallers, [wide] * 2, [full_low]...  1.56 us
  transfers between devices with their start and end apart: 31, of which 13 were waited for; matrix products, arithmetic and copies ran while one was open for 0% of the time, Pallas kernels for 9%

profile of v5, /device:TPU:0, one launch (start us, length us, event | category | flops | bytes accessed | tf_op | source)
XLA Modules:
  0.0 75.8 jit_solution(17934613042750913791)
XLA Ops:
  0.6 1.0 %copy-done.2 = bf16[1,256,1024]{2,1,0:T(8,128)(2,1)S(1)} copy-done((bf16[1,256,1024]{2,1,0:T(8,128)(2,1)S(1)}, bf16[1,256,1024]{2,1,0:T(8,128)(2,1)}, u32[]{:S(2)}) %copy-start.2) | copy-done | bytes 524312
  1.7 1.0 %copy-done.4 = bf16[1,256,1024]{2,1,0:T(8,128)(2,1)S(1)} copy-done((bf16[1,256,1024]{2,1,0:T(8,128)(2,1)S(1)}, bf16[1,256,1024]{2,1,0:T(8,128)(2,1)}, u32[]{:S(2)}) %copy-start.4) | copy-done | bytes 524312
  3.2 5.0 %collective-permute-start.6 = (f32[128,128]{1,0:T(8,128)S(1)}, f32[128,128]{1,0:T(8,128)S(1)}, u32[]{:S(2)}, u32[]{:S(2)}) collective-permute-start(f32[128,128]{1,0:T(8,128)S(1)} %get-tuple-element.53), channel_id=1, source_target_pairs={{0,14},{2,12},{4,10},{6,8},{8,6},{10,4},{12,2},{14,0},{16,30},{18,... | collective-permute-start | bytes 196616 | tf_op jit(solution)/shard_map/ppermute | solution.py:146
  8.6 1.5 %collective-permute-start.4 = (f32[128,128]{1,0:T(8,128)S(1)}, f32[128,128]{1,0:T(8,128)S(1)}, u32[]{:S(2)}, u32[]{:S(2)}) collective-permute-start(f32[128,128]{1,0:T(8,128)S(1)} %get-tuple-element.51), channel_id=1, source_target_pairs={{0,10},{2,8},{4,14},{6,12},{8,2},{10,0},{12,6},{14,4},{16,26},{18,... | collective-permute-start | bytes 196616 | tf_op jit(solution)/shard_map/ppermute | solution.py:146
  10.3 2.7 %collective-permute-start.2 = (f32[128,128]{1,0:T(8,128)S(1)}, f32[128,128]{1,0:T(8,128)S(1)}, u32[]{:S(2)}, u32[]{:S(2)}) collective-permute-start(f32[128,128]{1,0:T(8,128)S(1)} %get-tuple-element.49), channel_id=1, source_target_pairs={{0,6},{2,4},{4,2},{6,0},{8,14},{10,12},{12,10},{14,8},{16,22},{18,... | collective-permute-start | bytes 196616 | tf_op jit(solution)/shard_map/ppermute | solution.py:146
  15.1 1.2 %collective-permute-done.2.refs_3_ = f32[128,128]{1,0:T(8,128)S(1)} collective-permute-done((f32[128,128]{1,0:T(8,128)S(1)}, f32[128,128]{1,0:T(8,128)S(1)}, u32[]{:S(2)}, u32[]{:S(2)}) %collective-permute-start.2) | collective-permute-done | bytes 65568 | tf_op jit(solution)/shard_map/ppermute | solution.py:146
  16.3 1.0 %collective-permute-done.1.refs_2_ = f32[128,128]{1,0:T(8,128)S(1)} collective-permute-done((f32[128,128]{1,0:T(8,128)S(1)}, f32[128,128]{1,0:T(8,128)S(1)}, u32[]{:S(2)}, u32[]{:S(2)}) %collective-permute-start.1) | collective-permute-done | bytes 65568 | tf_op jit(solution)/shard_map/ppermute | solution.py:146
  17.3 1.1 %collective-permute-done.refs_1_ = f32[128,128]{1,0:T(8,128)S(1)} collective-permute-done((f32[128,128]{1,0:T(8,128)S(1)}, f32[128,128]{1,0:T(8,128)S(1)}, u32[]{:S(2)}, u32[]{:S(2)}) %collective-permute-start) | collective-permute-done | bytes 65568 | tf_op jit(solution)/shard_map/ppermute | solution.py:146
  18.4 2.7 %collective-permute-start.7 = (f32[128,128]{1,0:T(8,128)S(1)}, f32[128,128]{1,0:T(8,128)S(1)}, u32[]{:S(2)}, u32[]{:S(2)}) collective-permute-start(f32[128,128]{1,0:T(8,128)S(1)} %add_add_fusion.1), channel_id=1, source_target_pairs={{0,16},{2,18},{4,20},{6,22},{8,24},{10,26},{12,28},{14,30},{16,0},... | collective-permute-start | bytes 196616 | tf_op jit(solution)/shard_map/ppermute | solution.py:146
  21.1 3.3 %collective-permute-done.7 = f32[128,128]{1,0:T(8,128)S(1)} collective-permute-done((f32[128,128]{1,0:T(8,128)S(1)}, f32[128,128]{1,0:T(8,128)S(1)}, u32[]{:S(2)}, u32[]{:S(2)}) %collective-permute-start.7) | collective-permute-done | bytes 65568 | tf_op jit(solution)/shard_map/ppermute | solution.py:146
  25.3 2.7 %collective-permute-start.10 = (f32[128,128]{1,0:T(8,128)S(1)}, f32[128,128]{1,0:T(8,128)S(1)}, u32[]{:S(2)}, u32[]{:S(2)}) collective-permute-start(f32[128,128]{1,0:T(8,128)S(1)} %get-tuple-element.57), channel_id=1, source_target_pairs={{0,6},{2,4},{4,2},{6,0},{8,14},{10,12},{12,10},{14,8},{16,22},{18,... | collective-permute-start | bytes 196616 | tf_op jit(solution)/shard_map/ppermute | solution.py:146
  28.4 1.1 %collective-permute-start.12 = (f32[128,128]{1,0:T(8,128)S(1)}, f32[128,128]{1,0:T(8,128)S(1)}, u32[]{:S(2)}, u32[]{:S(2)}) collective-permute-start(f32[128,128]{1,0:T(8,128)S(1)} %get-tuple-element.59), channel_id=1, source_target_pairs={{0,10},{2,8},{4,14},{6,12},{8,2},{10,0},{12,6},{14,4},{16,26},{18,... | collective-permute-start | bytes 196616 | tf_op jit(solution)/shard_map/ppermute | solution.py:146
  29.6 1.7 %collective-permute-start.13 = (f32[128,128]{1,0:T(8,128)S(1)}, f32[128,128]{1,0:T(8,128)S(1)}, u32[]{:S(2)}, u32[]{:S(2)}) collective-permute-start(f32[128,128]{1,0:T(8,128)S(1)} %get-tuple-element.60), channel_id=1, source_target_pairs={{0,12},{2,14},{4,8},{6,10},{8,4},{10,6},{12,0},{14,2},{16,28},{18,... | collective-permute-start | bytes 196616 | tf_op jit(solution)/shard_map/ppermute | solution.py:146
  31.3 2.6 %collective-permute-start.14 = (f32[128,128]{1,0:T(8,128)S(1)}, f32[128,128]{1,0:T(8,128)S(1)}, u32[]{:S(2)}, u32[]{:S(2)}) collective-permute-start(f32[128,128]{1,0:T(8,128)S(1)} %get-tuple-element.61), channel_id=1, source_target_pairs={{0,14},{2,12},{4,10},{6,8},{8,6},{10,4},{12,2},{14,0},{16,30},{18,... | collective-permute-start | bytes 196616 | tf_op jit(solution)/shard_map/ppermute | solution.py:146
  34.9 2.6 %collective-permute-done.14.refs_7_ = f32[128,128]{1,0:T(8,128)S(1)} collective-permute-done((f32[128,128]{1,0:T(8,128)S(1)}, f32[128,128]{1,0:T(8,128)S(1)}, u32[]{:S(2)}, u32[]{:S(2)}) %collective-permute-start.14) | collective-permute-done | bytes 65568 | tf_op jit(solution)/shard_map/ppermute | solution.py:146
  37.5 1.5 %norm.1 = (bf16[256,1024]{1,0:T(8,128)(2,1)S(1)}, bf16[8,128,128]{2,1,0:T(8,128)(2,1)S(1)}, f32[136,128]{1,0:T(8,128)S(1)}, f32[136,128]{1,0:T(8,128)S(1)}, f32[...) custom-call(s32[1]{0:T(128)} %bitcast.3.member_ref, ...), custom_call_target="tpu_custom_call" | custom-call | flops 1073741824 | bytes 2097152 | tf_op jit(solution)/shard_map/norm/pallas_call | solution.py:196
  39.0 3.0 %collective-permute-start.21 = (f32[136,128]{1,0:T(8,128)S(1)}, f32[136,128]{1,0:T(8,128)S(1)}, u32[]{:S(2)}, u32[]{:S(2)}) collective-permute-start(f32[136,128]{1,0:T(8,128)S(1)} %get-tuple-element.77), channel_id=1, source_target_pairs={{0,14},{2,12},{4,10},{6,8},{8,6},{10,4},{12,2},{14,0},{16,30},{18,... | collective-permute-start | bytes 208904 | tf_op jit(solution)/shard_map/ppermute | solution.py:146
  42.0 1.0 %collective-permute-start.20 = (f32[136,128]{1,0:T(8,128)S(1)}, f32[136,128]{1,0:T(8,128)S(1)}, u32[]{:S(2)}, u32[]{:S(2)}) collective-permute-start(f32[136,128]{1,0:T(8,128)S(1)} %get-tuple-element.76), channel_id=1, source_target_pairs={{0,12},{2,14},{4,8},{6,10},{8,4},{10,6},{12,0},{14,2},{16,28},{18,... | collective-permute-start | bytes 208904 | tf_op jit(solution)/shard_map/ppermute | solution.py:146
  43.2 1.7 %collective-permute-start.18 = (f32[136,128]{1,0:T(8,128)S(1)}, f32[136,128]{1,0:T(8,128)S(1)}, u32[]{:S(2)}, u32[]{:S(2)}) collective-permute-start(f32[136,128]{1,0:T(8,128)S(1)} %get-tuple-element.74), channel_id=1, source_target_pairs={{0,8},{2,10},{4,12},{6,14},{8,0},{10,2},{12,4},{14,6},{16,24},{18,... | collective-permute-start | bytes 208904 | tf_op jit(solution)/shard_map/ppermute | solution.py:146
  44.9 1.9 %collective-permute-start.17 = (f32[136,128]{1,0:T(8,128)S(1)}, f32[136,128]{1,0:T(8,128)S(1)}, u32[]{:S(2)}, u32[]{:S(2)}) collective-permute-start(f32[136,128]{1,0:T(8,128)S(1)} %get-tuple-element.73), channel_id=1, source_target_pairs={{0,6},{2,4},{4,2},{6,0},{8,14},{10,12},{12,10},{14,8},{16,22},{18,... | collective-permute-start | bytes 208904 | tf_op jit(solution)/shard_map/ppermute | solution.py:146
  46.8 1.1 %collective-permute-start.16 = (f32[136,128]{1,0:T(8,128)S(1)}, f32[136,128]{1,0:T(8,128)S(1)}, u32[]{:S(2)}, u32[]{:S(2)}) collective-permute-start(f32[136,128]{1,0:T(8,128)S(1)} %get-tuple-element.72), channel_id=1, source_target_pairs={{0,4},{2,6},{4,0},{6,2},{8,12},{10,14},{12,8},{14,10},{16,20},{18,... | collective-permute-start | bytes 208904 | tf_op jit(solution)/shard_map/ppermute | solution.py:146
  48.5 1.6 %collective-permute-done.17.refs_3_ = f32[136,128]{1,0:T(8,128)S(1)} collective-permute-done((f32[136,128]{1,0:T(8,128)S(1)}, f32[136,128]{1,0:T(8,128)S(1)}, u32[]{:S(2)}, u32[]{:S(2)}) %collective-permute-start.17) | collective-permute-done | bytes 69664 | tf_op jit(solution)/shard_map/ppermute | solution.py:146
  51.1 1.1 %collective-permute-done.15.refs_1_ = f32[136,128]{1,0:T(8,128)S(1)} collective-permute-done((f32[136,128]{1,0:T(8,128)S(1)}, f32[136,128]{1,0:T(8,128)S(1)}, u32[]{:S(2)}, u32[]{:S(2)}) %collective-permute-start.15) | collective-permute-done | bytes 69664 | tf_op jit(solution)/shard_map/ppermute | solution.py:146
  52.3 3.6 %collective-permute-start.22 = (f32[136,128]{1,0:T(8,128)S(1)}, f32[136,128]{1,0:T(8,128)S(1)}, u32[]{:S(2)}, u32[]{:S(2)}) collective-permute-start(f32[136,128]{1,0:T(8,128)S(1)} %add_add_fusion), channel_id=1, source_target_pairs={{0,16},{2,18},{4,20},{6,22},{8,24},{10,26},{12,28},{14,30},{16,0},... | collective-permute-start | bytes 208904 | tf_op jit(solution)/shard_map/ppermute | solution.py:146
  55.8 3.1 %collective-permute-done.22 = f32[136,128]{1,0:T(8,128)S(1)} collective-permute-done((f32[136,128]{1,0:T(8,128)S(1)}, f32[136,128]{1,0:T(8,128)S(1)}, u32[]{:S(2)}, u32[]{:S(2)}) %collective-permute-start.22) | collective-permute-done | bytes 69664 | tf_op jit(solution)/shard_map/ppermute | solution.py:146
  59.8 1.2 %collective-permute-start.24 = (f32[136,128]{1,0:T(8,128)S(1)}, f32[136,128]{1,0:T(8,128)S(1)}, u32[]{:S(2)}, u32[]{:S(2)}) collective-permute-start(f32[136,128]{1,0:T(8,128)S(1)} %get-tuple-element.80), channel_id=1, source_target_pairs={{0,4},{2,6},{4,0},{6,2},{8,12},{10,14},{12,8},{14,10},{16,20},{18,... | collective-permute-start | bytes 208904 | tf_op jit(solution)/shard_map/ppermute | solution.py:146
  60.9 2.0 %partial.2 = (bf16[256,1024]{1,0:T(8,128)(2,1)}, f32[256,1024]{1,0:T(8,128)S(1)}, f32[256,1024]{1,0:T(8,128)S(1)}) custom-call(bf16[256,1024]{1,0:T(8,128)(2,1)S(1)} %bitcast.14, bf16[256,1024]{1,0:T(8,128)(2,1)S(1)} %bitcast.18, bf16[256,1024]{1,0:T(8,128)(2,1)S(1)} %bitcast.23, bf16[256,1024]{1,0:T(8,128)(2,1)S(1)} %get-tuple-element.62.attn_ref, ...), custom_call_target="tpu_custom_call" | custom-call | flops 1610612736 | bytes 2097152 | tf_op jit(solution)/shard_map/partial/pallas_call | solution.py:208
  63.0 1.7 %collective-permute-start.25 = (f32[136,128]{1,0:T(8,128)S(1)}, f32[136,128]{1,0:T(8,128)S(1)}, u32[]{:S(2)}, u32[]{:S(2)}) collective-permute-start(f32[136,128]{1,0:T(8,128)S(1)} %get-tuple-element.81), channel_id=1, source_target_pairs={{0,6},{2,4},{4,2},{6,0},{8,14},{10,12},{12,10},{14,8},{16,22},{18,... | collective-permute-start | bytes 208904 | tf_op jit(solution)/shard_map/ppermute | solution.py:146
  64.7 2.1 %collective-permute-start.27 = (f32[136,128]{1,0:T(8,128)S(1)}, f32[136,128]{1,0:T(8,128)S(1)}, u32[]{:S(2)}, u32[]{:S(2)}) collective-permute-start(f32[136,128]{1,0:T(8,128)S(1)} %get-tuple-element.83), channel_id=1, source_target_pairs={{0,10},{2,8},{4,14},{6,12},{8,2},{10,0},{12,6},{14,4},{16,26},{18,... | collective-permute-start | bytes 208904 | tf_op jit(solution)/shard_map/ppermute | solution.py:146
  67.4 3.2 %collective-permute-start.29 = (f32[136,128]{1,0:T(8,128)S(1)}, f32[136,128]{1,0:T(8,128)S(1)}, u32[]{:S(2)}, u32[]{:S(2)}) collective-permute-start(f32[136,128]{1,0:T(8,128)S(1)} %get-tuple-element.85), channel_id=1, source_target_pairs={{0,14},{2,12},{4,10},{6,8},{8,6},{10,4},{12,2},{14,0},{16,30},{18,... | collective-permute-start | bytes 208904 | tf_op jit(solution)/shard_map/ppermute | solution.py:146
  70.6 2.0 %partial.3 = (bf16[256,1024]{1,0:T(8,128)(2,1)}, f32[256,1024]{1,0:T(8,128)S(1)}, f32[256,1024]{1,0:T(8,128)S(1)}) custom-call(bf16[256,1024]{1,0:T(8,128)(2,1)S(1)} %bitcast.15, bf16[256,1024]{1,0:T(8,128)(2,1)S(1)} %bitcast.19, bf16[256,1024]{1,0:T(8,128)(2,1)S(1)} %bitcast.24, ...), custom_call_target="tpu_custom_call", output_to_operand_aliasing={{0}: (5, {}), {1}: (6, {}), {2}: (7, {})} | custom-call | flops 1610612736 | bytes 2097152 | tf_op jit(solution)/shard_map/partial/pallas_call | solution.py:208
  73.6 1.6 %final.1 = (bf16[256,1024]{1,0:T(8,128)(2,1)}, bf16[256,1024]{1,0:T(8,128)(2,1)}) custom-call(s32[1]{0:T(128)} %bitcast.3.member_ref, bf16[256,1024]{1,0:T(8,128)(2,1)S(1)} %bitcast.20, bf16[256,1024]{1,0:T(8,128)(2,1)S(1)} %bitcast.25, f32[256,1024]{1,0:T(8,128)S(1)} %get-tuple-element.68.key_part_ref, f32[256,1024]{1,0:T(8,128)S(1)} %get-tuple-element.69.value_part_ref, ...), custom_call_target="tpu_custom_call" | custom-call | flops 1073741824 | bytes 2097152 | tf_op jit(solution)/shard_map/final/pallas_call | solution.py:226
  (58 shorter events, 10.4 us)
Async XLA Ops:
  2.7 31.2 %copy-start.5 = (bf16[1,256,1024]{2,1,0:T(8,128)(2,1)S(1)}, bf16[1,256,1024]{2,1,0:T(8,128)(2,1)}, u32[]{:S(2)}) copy-start(bf16[1,256,1024]{2,1,0:T(8,128)(2,1)} %param.7) | copy-start | bytes 1572868
  3.2 9.8 %collective-permute-start.6 = (f32[128,128]{1,0:T(8,128)S(1)}, f32[128,128]{1,0:T(8,128)S(1)}, u32[]{:S(2)}, u32[]{:S(2)}) collective-permute-start(f32[128,128]{1,0:T(8,128)S(1)} %get-tuple-element.53), channel_id=1, source_target_pairs={{0,14},{2,12},{4,10},{6,8},{8,6},{10,4},{12,2},{14,0},{16,30},{18,... | collective-permute-start | bytes 196616 | tf_op jit(solution)/shard_map/ppermute | solution.py:146
  8.2 5.9 %collective-permute-start.5 = (f32[128,128]{1,0:T(8,128)S(1)}, f32[128,128]{1,0:T(8,128)S(1)}, u32[]{:S(2)}, u32[]{:S(2)}) collective-permute-start(f32[128,128]{1,0:T(8,128)S(1)} %get-tuple-element.52), channel_id=1, source_target_pairs={{0,12},{2,14},{4,8},{6,10},{8,4},{10,6},{12,0},{14,2},{16,28},{18,... | collective-permute-start | bytes 196616 | tf_op jit(solution)/shard_map/ppermute | solution.py:146
  8.6 5.9 %collective-permute-start.4 = (f32[128,128]{1,0:T(8,128)S(1)}, f32[128,128]{1,0:T(8,128)S(1)}, u32[]{:S(2)}, u32[]{:S(2)}) collective-permute-start(f32[128,128]{1,0:T(8,128)S(1)} %get-tuple-element.51), channel_id=1, source_target_pairs={{0,10},{2,8},{4,14},{6,12},{8,2},{10,0},{12,6},{14,4},{16,26},{18,... | collective-permute-start | bytes 196616 | tf_op jit(solution)/shard_map/ppermute | solution.py:146
  10.1 5.0 %collective-permute-start.3 = (f32[128,128]{1,0:T(8,128)S(1)}, f32[128,128]{1,0:T(8,128)S(1)}, u32[]{:S(2)}, u32[]{:S(2)}) collective-permute-start(f32[128,128]{1,0:T(8,128)S(1)} %get-tuple-element.50), channel_id=1, source_target_pairs={{0,8},{2,10},{4,12},{6,14},{8,0},{10,2},{12,4},{14,6},{16,24},{18,... | collective-permute-start | bytes 196616 | tf_op jit(solution)/shard_map/ppermute | solution.py:146
  10.3 6.0 %collective-permute-start.2 = (f32[128,128]{1,0:T(8,128)S(1)}, f32[128,128]{1,0:T(8,128)S(1)}, u32[]{:S(2)}, u32[]{:S(2)}) collective-permute-start(f32[128,128]{1,0:T(8,128)S(1)} %get-tuple-element.49), channel_id=1, source_target_pairs={{0,6},{2,4},{4,2},{6,0},{8,14},{10,12},{12,10},{14,8},{16,22},{18,... | collective-permute-start | bytes 196616 | tf_op jit(solution)/shard_map/ppermute | solution.py:146
  13.0 4.3 %collective-permute-start.1 = (f32[128,128]{1,0:T(8,128)S(1)}, f32[128,128]{1,0:T(8,128)S(1)}, u32[]{:S(2)}, u32[]{:S(2)}) collective-permute-start(f32[128,128]{1,0:T(8,128)S(1)} %get-tuple-element.48), channel_id=1, source_target_pairs={{0,4},{2,6},{4,0},{6,2},{8,12},{10,14},{12,8},{14,10},{16,20},{18,... | collective-permute-start | bytes 196616 | tf_op jit(solution)/shard_map/ppermute | solution.py:146
  14.1 4.3 %collective-permute-start = (f32[128,128]{1,0:T(8,128)S(1)}, f32[128,128]{1,0:T(8,128)S(1)}, u32[]{:S(2)}, u32[]{:S(2)}) collective-permute-start(f32[128,128]{1,0:T(8,128)S(1)} %get-tuple-element.47), channel_id=1, source_target_pairs={{0,2},{2,0},{4,6},{6,4},{8,10},{10,8},{12,14},{14,12},{16,18},{18,... | collective-permute-start | bytes 196616 | tf_op jit(solution)/shard_map/ppermute | solution.py:146
  18.4 5.9 %collective-permute-start.7 = (f32[128,128]{1,0:T(8,128)S(1)}, f32[128,128]{1,0:T(8,128)S(1)}, u32[]{:S(2)}, u32[]{:S(2)}) collective-permute-start(f32[128,128]{1,0:T(8,128)S(1)} %add_add_fusion.1), channel_id=1, source_target_pairs={{0,16},{2,18},{4,20},{6,22},{8,24},{10,26},{12,28},{14,30},{16,0},... | collective-permute-start | bytes 196616 | tf_op jit(solution)/shard_map/ppermute | solution.py:146
  24.5 5.1 %collective-permute-start.8 = (f32[128,128]{1,0:T(8,128)S(1)}, f32[128,128]{1,0:T(8,128)S(1)}, u32[]{:S(2)}, u32[]{:S(2)}) collective-permute-start(f32[128,128]{1,0:T(8,128)S(1)} %get-tuple-element.55), channel_id=1, source_target_pairs={{0,2},{2,0},{4,6},{6,4},{8,10},{10,8},{12,14},{14,12},{16,18},{18,... | collective-permute-start | bytes 196616 | tf_op jit(solution)/shard_map/ppermute | solution.py:146
  24.6 6.7 %collective-permute-start.9 = (f32[128,128]{1,0:T(8,128)S(1)}, f32[128,128]{1,0:T(8,128)S(1)}, u32[]{:S(2)}, u32[]{:S(2)}) collective-permute-start(f32[128,128]{1,0:T(8,128)S(1)} %get-tuple-element.56), channel_id=1, source_target_pairs={{0,4},{2,6},{4,0},{6,2},{8,12},{10,14},{12,8},{14,10},{16,20},{18,... | collective-permute-start | bytes 196616 | tf_op jit(solution)/shard_map/ppermute | solution.py:146
  25.3 9.5 %collective-permute-start.10 = (f32[128,128]{1,0:T(8,128)S(1)}, f32[128,128]{1,0:T(8,128)S(1)}, u32[]{:S(2)}, u32[]{:S(2)}) collective-permute-start(f32[128,128]{1,0:T(8,128)S(1)} %get-tuple-element.57), channel_id=1, source_target_pairs={{0,6},{2,4},{4,2},{6,0},{8,14},{10,12},{12,10},{14,8},{16,22},{18,... | collective-permute-start | bytes 196616 | tf_op jit(solution)/shard_map/ppermute | solution.py:146
  28.0 6.8 %collective-permute-start.11 = (f32[128,128]{1,0:T(8,128)S(1)}, f32[128,128]{1,0:T(8,128)S(1)}, u32[]{:S(2)}, u32[]{:S(2)}) collective-permute-start(f32[128,128]{1,0:T(8,128)S(1)} %get-tuple-element.58), channel_id=1, source_target_pairs={{0,8},{2,10},{4,12},{6,14},{8,0},{10,2},{12,4},{14,6},{16,24},{18,... | collective-permute-start | bytes 196616 | tf_op jit(solution)/shard_map/ppermute | solution.py:146
  28.4 6.4 %collective-permute-start.12 = (f32[128,128]{1,0:T(8,128)S(1)}, f32[128,128]{1,0:T(8,128)S(1)}, u32[]{:S(2)}, u32[]{:S(2)}) collective-permute-start(f32[128,128]{1,0:T(8,128)S(1)} %get-tuple-element.59), channel_id=1, source_target_pairs={{0,10},{2,8},{4,14},{6,12},{8,2},{10,0},{12,6},{14,4},{16,26},{18,... | collective-permute-start | bytes 196616 | tf_op jit(solution)/shard_map/ppermute | solution.py:146
  29.6 5.3 %collective-permute-start.13 = (f32[128,128]{1,0:T(8,128)S(1)}, f32[128,128]{1,0:T(8,128)S(1)}, u32[]{:S(2)}, u32[]{:S(2)}) collective-permute-start(f32[128,128]{1,0:T(8,128)S(1)} %get-tuple-element.60), channel_id=1, source_target_pairs={{0,12},{2,14},{4,8},{6,10},{8,4},{10,6},{12,0},{14,2},{16,28},{18,... | collective-permute-start | bytes 196616 | tf_op jit(solution)/shard_map/ppermute | solution.py:146
  31.3 6.2 %collective-permute-start.14 = (f32[128,128]{1,0:T(8,128)S(1)}, f32[128,128]{1,0:T(8,128)S(1)}, u32[]{:S(2)}, u32[]{:S(2)}) collective-permute-start(f32[128,128]{1,0:T(8,128)S(1)} %get-tuple-element.61), channel_id=1, source_target_pairs={{0,14},{2,12},{4,10},{6,8},{8,6},{10,4},{12,2},{14,0},{16,30},{18,... | collective-permute-start | bytes 196616 | tf_op jit(solution)/shard_map/ppermute | solution.py:146
  39.0 7.8 %collective-permute-start.21 = (f32[136,128]{1,0:T(8,128)S(1)}, f32[136,128]{1,0:T(8,128)S(1)}, u32[]{:S(2)}, u32[]{:S(2)}) collective-permute-start(f32[136,128]{1,0:T(8,128)S(1)} %get-tuple-element.77), channel_id=1, source_target_pairs={{0,14},{2,12},{4,10},{6,8},{8,6},{10,4},{12,2},{14,0},{16,30},{18,... | collective-permute-start | bytes 208904 | tf_op jit(solution)/shard_map/ppermute | solution.py:146
  42.0 6.0 %collective-permute-start.20 = (f32[136,128]{1,0:T(8,128)S(1)}, f32[136,128]{1,0:T(8,128)S(1)}, u32[]{:S(2)}, u32[]{:S(2)}) collective-permute-start(f32[136,128]{1,0:T(8,128)S(1)} %get-tuple-element.76), channel_id=1, source_target_pairs={{0,12},{2,14},{4,8},{6,10},{8,4},{10,6},{12,0},{14,2},{16,28},{18,... | collective-permute-start | bytes 208904 | tf_op jit(solution)/shard_map/ppermute | solution.py:146
  42.9 5.6 %collective-permute-start.19 = (f32[136,128]{1,0:T(8,128)S(1)}, f32[136,128]{1,0:T(8,128)S(1)}, u32[]{:S(2)}, u32[]{:S(2)}) collective-permute-start(f32[136,128]{1,0:T(8,128)S(1)} %get-tuple-element.75), channel_id=1, source_target_pairs={{0,10},{2,8},{4,14},{6,12},{8,2},{10,0},{12,6},{14,4},{16,26},{18,... | collective-permute-start | bytes 208904 | tf_op jit(solution)/shard_map/ppermute | solution.py:146
  43.2 5.3 %collective-permute-start.18 = (f32[136,128]{1,0:T(8,128)S(1)}, f32[136,128]{1,0:T(8,128)S(1)}, u32[]{:S(2)}, u32[]{:S(2)}) collective-permute-start(f32[136,128]{1,0:T(8,128)S(1)} %get-tuple-element.74), channel_id=1, source_target_pairs={{0,8},{2,10},{4,12},{6,14},{8,0},{10,2},{12,4},{14,6},{16,24},{18,... | collective-permute-start | bytes 208904 | tf_op jit(solution)/shard_map/ppermute | solution.py:146
  44.9 5.2 %collective-permute-start.17 = (f32[136,128]{1,0:T(8,128)S(1)}, f32[136,128]{1,0:T(8,128)S(1)}, u32[]{:S(2)}, u32[]{:S(2)}) collective-permute-start(f32[136,128]{1,0:T(8,128)S(1)} %get-tuple-element.73), channel_id=1, source_target_pairs={{0,6},{2,4},{4,2},{6,0},{8,14},{10,12},{12,10},{14,8},{16,22},{18,... | collective-permute-start | bytes 208904 | tf_op jit(solution)/shard_map/ppermute | solution.py:146
  46.8 4.3 %collective-permute-start.16 = (f32[136,128]{1,0:T(8,128)S(1)}, f32[136,128]{1,0:T(8,128)S(1)}, u32[]{:S(2)}, u32[]{:S(2)}) collective-permute-start(f32[136,128]{1,0:T(8,128)S(1)} %get-tuple-element.72), channel_id=1, source_target_pairs={{0,4},{2,6},{4,0},{6,2},{8,12},{10,14},{12,8},{14,10},{16,20},{18,... | collective-permute-start | bytes 208904 | tf_op jit(solution)/shard_map/ppermute | solution.py:146
  47.9 4.3 %collective-permute-start.15 = (f32[136,128]{1,0:T(8,128)S(1)}, f32[136,128]{1,0:T(8,128)S(1)}, u32[]{:S(2)}, u32[]{:S(2)}) collective-permute-start(f32[136,128]{1,0:T(8,128)S(1)} %get-tuple-element.71), channel_id=1, source_target_pairs={{0,2},{2,0},{4,6},{6,4},{8,10},{10,8},{12,14},{14,12},{16,18},{18,... | collective-permute-start | bytes 208904 | tf_op jit(solution)/shard_map/ppermute | solution.py:146
  52.3 6.7 %collective-permute-start.22 = (f32[136,128]{1,0:T(8,128)S(1)}, f32[136,128]{1,0:T(8,128)S(1)}, u32[]{:S(2)}, u32[]{:S(2)}) collective-permute-start(f32[136,128]{1,0:T(8,128)S(1)} %add_add_fusion), channel_id=1, source_target_pairs={{0,16},{2,18},{4,20},{6,22},{8,24},{10,26},{12,28},{14,30},{16,0},... | collective-permute-start | bytes 208904 | tf_op jit(solution)/shard_map/ppermute | solution.py:146
  59.1 7.7 %collective-permute-start.23 = (f32[136,128]{1,0:T(8,128)S(1)}, f32[136,128]{1,0:T(8,128)S(1)}, u32[]{:S(2)}, u32[]{:S(2)}) collective-permute-start(f32[136,128]{1,0:T(8,128)S(1)} %get-tuple-element.79), channel_id=1, source_target_pairs={{0,2},{2,0},{4,6},{6,4},{8,10},{10,8},{12,14},{14,12},{16,18},{18,... | collective-permute-start | bytes 208904 | tf_op jit(solution)/shard_map/ppermute | solution.py:146
  59.8 7.6 %collective-permute-start.24 = (f32[136,128]{1,0:T(8,128)S(1)}, f32[136,128]{1,0:T(8,128)S(1)}, u32[]{:S(2)}, u32[]{:S(2)}) collective-permute-start(f32[136,128]{1,0:T(8,128)S(1)} %get-tuple-element.80), channel_id=1, source_target_pairs={{0,4},{2,6},{4,0},{6,2},{8,12},{10,14},{12,8},{14,10},{16,20},{18,... | collective-permute-start | bytes 208904 | tf_op jit(solution)/shard_map/ppermute | solution.py:146
  63.0 9.6 %collective-permute-start.25 = (f32[136,128]{1,0:T(8,128)S(1)}, f32[136,128]{1,0:T(8,128)S(1)}, u32[]{:S(2)}, u32[]{:S(2)}) collective-permute-start(f32[136,128]{1,0:T(8,128)S(1)} %get-tuple-element.81), channel_id=1, source_target_pairs={{0,6},{2,4},{4,2},{6,0},{8,14},{10,12},{12,10},{14,8},{16,22},{18,... | collective-permute-start | bytes 208904 | tf_op jit(solution)/shard_map/ppermute | solution.py:146
  64.7 7.9 %collective-permute-start.26 = (f32[136,128]{1,0:T(8,128)S(1)}, f32[136,128]{1,0:T(8,128)S(1)}, u32[]{:S(2)}, u32[]{:S(2)}) collective-permute-start(f32[136,128]{1,0:T(8,128)S(1)} %get-tuple-element.82), channel_id=1, source_target_pairs={{0,8},{2,10},{4,12},{6,14},{8,0},{10,2},{12,4},{14,6},{16,24},{18,... | collective-permute-start | bytes 208904 | tf_op jit(solution)/shard_map/ppermute | solution.py:146
  64.7 7.9 %collective-permute-start.27 = (f32[136,128]{1,0:T(8,128)S(1)}, f32[136,128]{1,0:T(8,128)S(1)}, u32[]{:S(2)}, u32[]{:S(2)}) collective-permute-start(f32[136,128]{1,0:T(8,128)S(1)} %get-tuple-element.83), channel_id=1, source_target_pairs={{0,10},{2,8},{4,14},{6,12},{8,2},{10,0},{12,6},{14,4},{16,26},{18,... | collective-permute-start | bytes 208904 | tf_op jit(solution)/shard_map/ppermute | solution.py:146
  66.8 5.8 %collective-permute-start.28 = (f32[136,128]{1,0:T(8,128)S(1)}, f32[136,128]{1,0:T(8,128)S(1)}, u32[]{:S(2)}, u32[]{:S(2)}) collective-permute-start(f32[136,128]{1,0:T(8,128)S(1)} %get-tuple-element.84), channel_id=1, source_target_pairs={{0,12},{2,14},{4,8},{6,10},{8,4},{10,6},{12,0},{14,2},{16,28},{18,... | collective-permute-start | bytes 208904 | tf_op jit(solution)/shard_map/ppermute | solution.py:146
  67.4 6.2 %collective-permute-start.29 = (f32[136,128]{1,0:T(8,128)S(1)}, f32[136,128]{1,0:T(8,128)S(1)}, u32[]{:S(2)}, u32[]{:S(2)}) collective-permute-start(f32[136,128]{1,0:T(8,128)S(1)} %get-tuple-element.85), channel_id=1, source_target_pairs={{0,14},{2,12},{4,10},{6,8},{8,6},{10,4},{12,2},{14,0},{16,30},{18,... | collective-permute-start | bytes 208904 | tf_op jit(solution)/shard_map/ppermute | solution.py:146
  73.6 1.6 %collective-permute-start.30 = (f32[8,128]{1,0:T(8,128)S(1)}, f32[8,128]{1,0:T(8,128)S(1)}, u32[]{:S(2)}, u32[]{:S(2)}) collective-permute-start(f32[8,128]{1,0:T(8,128)S(1)} %gain.1), channel_id=1, source_target_pairs={{0,1},{1,0},{2,3},{3,2},{4,5},{5,4},{6,7},{7,6},{8,9},{9,8},{10,11... | collective-permute-start | bytes 12296 | tf_op jit(solution)/shard_map/ppermute | solution.py:146
  (6 other events, 39.4 us)

commit v6 on v4

v6 whole, which is shorter than its diff:
```python
import functools
import math

import jax
import jax.numpy as jnp
from jax import lax
from jax.experimental import pallas as pl
from jax.experimental.pallas import tpu as pltpu
from jax.sharding import PartitionSpec as P

HEADS = 8
DH = 128
BLOCK = 256
GROUP = 8
CHAINS = 2
CHAIN_HEADS = HEADS // CHAINS
WIDE = CHAIN_HEADS * DH
OWNED = WIDE // GROUP
SHARES = DH // OWNED
GAIN_ROWS = 8
EPSILON = 1e-06

NT = (((1,), (1,)), ((), ()))
TN = (((0,), (0,)), ((), ()))
NN = (((1,), (0,)), ((), ()))


def dot(left, right, dims):
    return lax.dot_general(left, right, dims, preferred_element_type=jnp.float32)


def columns(head):
    return pl.ds(head * DH, DH)


def causal():
    shape = (BLOCK, BLOCK)
    return lax.broadcasted_iota(jnp.int32, shape, 0) >= lax.broadcasted_iota(jnp.int32, shape, 1)


def put(delta_ref, head, delta):
    for share in range(SHARES):
        delta_ref[head * SHARES + share, :OWNED] = delta[share * OWNED : (share + 1) * OWNED]


def delta_body(key_ref, value_ref, delta_ref):
    for head in range(CHAIN_HEADS):
        at = columns(head)
        put(delta_ref, head, dot(key_ref[:, at], value_ref[:, at], TN))


def state_of(state_ref, head):
    shares = [state_ref[head * SHARES + share, :OWNED] for share in range(SHARES)]
    return jnp.concatenate(shares, axis=0).astype(jnp.bfloat16)


def inner_body(query_ref, key_ref, value_ref, inner_ref):
    keep = causal()
    for head in range(CHAIN_HEADS):
        at = columns(head)
        raw = dot(query_ref[:, at], key_ref[:, at], NT)
        scores = jnp.where(keep, raw, 0.0).astype(jnp.bfloat16)
        inner_ref[:, at] = dot(scores, value_ref[:, at], NN)


def norm_body(query_ref, grad_ref, inner_ref, gain_ref, state_ref, attn_ref, delta_ref):
    for head in range(CHAIN_HEADS):
        at = columns(head)
        query = query_ref[:, at]
        attn = inner_ref[:, at] + dot(query, state_of(state_ref, head), NN)
        root = jnp.sqrt(jnp.mean(attn * attn, axis=-1, keepdims=True) + EPSILON)
        normed = attn / root
        cotangent = grad_ref[:, at].astype(jnp.float32)
        scaled = gain_ref[:, at] * cotangent
        shared = jnp.mean(normed * scaled, axis=-1, keepdims=True)
        grad_attn = ((scaled - normed * shared) / root).astype(jnp.bfloat16)
        attn_ref[:, at] = grad_attn
        terms = jnp.sum(normed * cotangent, axis=0, keepdims=True)
        put(delta_ref, head, dot(query, grad_attn, TN))
        for share in range(SHARES):
            delta_ref[head * SHARES + share, OWNED:] = jnp.broadcast_to(terms, (GAIN_ROWS, DH))


def partial_body(query_ref, key_ref, value_ref, attn_ref, state_ref, *refs):
    grad_query_ref, key_part_ref, value_part_ref = refs[-3:]
    keep = causal()
    for head in range(CHAIN_HEADS):
        at = columns(head)
        query, key, value, grad_attn = query_ref[:, at], key_ref[:, at], value_ref[:, at], attn_ref[:, at]
        scores = jnp.where(keep, dot(query, key, NT), 0.0).astype(jnp.bfloat16)
        grad_scores = jnp.where(keep, dot(grad_attn, value, NT), 0.0).astype(jnp.bfloat16)
        carried = dot(grad_attn, state_of(state_ref, head), NT)
        grad_query_ref[:, at] = (dot(grad_scores, key, NN) + carried).astype(jnp.bfloat16)
        key_part_ref[:, at] = dot(grad_scores, query, TN)
        value_part_ref[:, at] = dot(scores, grad_attn, TN)


def final_body(key_ref, value_ref, key_part_ref, value_part_ref, state_ref, *refs):
    grad_key_ref, grad_value_ref = refs[-2:]
    for head in range(CHAIN_HEADS):
        at = columns(head)
        state = state_of(state_ref, head)
        grad_key_ref[:, at] = (key_part_ref[:, at] + dot(value_ref[:, at], state, NT)).astype(jnp.bfloat16)
        grad_value_ref[:, at] = (value_part_ref[:, at] + dot(key_ref[:, at], state, NN)).astype(jnp.bfloat16)


def gain_body(*refs):
    for chain, state_ref in enumerate(refs[:-1]):
        for head in range(CHAIN_HEADS):
            row = chain * CHAIN_HEADS + head
            refs[-1][row : row + 1, :] = state_ref[head * SHARES, OWNED : OWNED + 1, :]


def prefix_body(reverse, carried_ref, total_ref, held_ref, back_ref):
    running = carried_ref[:OWNED]
    for member in reversed(range(GROUP)) if reverse else range(GROUP):
        back_ref[member, :OWNED] = running
        running = running + held_ref[member, :OWNED]
        if back_ref.shape[1] > OWNED:
            back_ref[member, OWNED:] = total_ref[OWNED:]


def whole(*shape):
    return pl.BlockSpec(shape, lambda step: (0,) * len(shape))


def part_of(chain):
    return pl.BlockSpec((BLOCK, WIDE), lambda step: (0, chain))


def call(body, in_specs, out_specs, outs, flops, name, aliases=None):
    return pl.pallas_call(
        body,
        grid=(1,),
        in_specs=in_specs,
        out_specs=out_specs,
        out_shape=outs,
        input_output_aliases=aliases or {},
        compiler_params=pltpu.CompilerParams(vmem_limit_bytes=16 * 1024 * 1024),
        cost_estimate=pl.CostEstimate(flops=flops, bytes_accessed=2 << 20, transcendentals=0),
        name=name,
    )


def swap(array, axis, mask):
    if mask == 0:
        return array
    return lax.ppermute(array, axis, [(s, s ^ mask) for s in range(lax.axis_size(axis))])


def carried_in(parts, axis, reverse):
    count, place = lax.axis_size(axis), lax.axis_index(axis)
    teams = [list(range(first, first + GROUP)) for first in range(0, count, GROUP)]
    held = lax.all_to_all(parts, axis, 0, 0, axis_index_groups=teams)
    total = jnp.sum(held, axis=0)
    carried = jnp.zeros_like(total)
    mask = GROUP
    while mask < count:
        arrived = swap(total, axis, mask)
        later = ((place & mask) != 0) != reverse
        carried = carried + jnp.where(later, arrived, 0.0)
        total = total + arrived
        mask *= 2
    single, stacked = whole(*total.shape), whole(*held.shape)
    back = call(
        functools.partial(prefix_body, reverse),
        [single, single, stacked],
        stacked,
        jax.ShapeDtypeStruct(held.shape, jnp.float32),
        1 << 24,
        "prefix",
    )(carried, total, held)
    return lax.all_to_all(back, axis, 0, 0, axis_index_groups=teams)


def local(queries, keys, values, out_gain, grad_out):
    full = queries.shape
    flat = (full[0] * full[1], full[2])
    assert flat == (BLOCK, HEADS * DH)
    query, key, value, grad = (a.reshape(flat) for a in (queries, keys, values, grad_out))
    gain = out_gain.reshape(1, HEADS * DH)
    assert lax.axis_size("seq") % GROUP == 0
    plain = jax.ShapeDtypeStruct((GROUP, OWNED, DH), jnp.float32)
    taller = jax.ShapeDtypeStruct((GROUP, OWNED + GAIN_ROWS, DH), jnp.float32)
    wide_float = jax.ShapeDtypeStruct((BLOCK, WIDE), jnp.float32)
    wide_low = jax.ShapeDtypeStruct((BLOCK, WIDE), jnp.bfloat16)
    full_low = jax.ShapeDtypeStruct(flat, jnp.bfloat16)
    short, tall, wide = whole(*plain.shape), whole(*taller.shape), whole(BLOCK, WIDE)
    spot = pl.BlockSpec(memory_space=pl.ANY)
    unit = 2 * BLOCK * DH * DH * CHAIN_HEADS

    states, inner = [], []
    for chain in range(CHAINS):
        cols = part_of(chain)
        delta = call(delta_body, [cols, cols], short, plain, 6 * unit, "delta")(key, value)
        states.append(carried_in(delta, "seq", False))
        inner.append(call(inner_body, [cols] * 3, wide, wide_float, 16 * unit, "inner")(query, key, value))

    later, parts, grad_query = [], [], []
    for chain in range(CHAINS):
        cols = part_of(chain)
        attn, delta = call(
            norm_body,
            [cols, cols, wide, pl.BlockSpec((1, WIDE), lambda step, c=chain: (0, c)), short],
            [wide, tall],
            [wide_low, taller],
            16 * unit,
            "norm",
        )(query, grad, inner[chain], gain, states[chain])
        later.append(carried_in(delta, "seq", True))
        *grad_query, key_part, value_part = call(
            partial_body,
            [cols, cols, cols, wide, short] + [spot] * len(grad_query),
            [cols, wide, wide],
            [full_low, wide_float, wide_float],
            48 * unit,
            "partial",
            {5: 0} if grad_query else None,
        )(query, key, value, attn, states[chain], *grad_query)
        parts.append((key_part, value_part))

    gain_terms = call(
        gain_body, [tall] * CHAINS, whole(HEADS, DH), jax.ShapeDtypeStruct((HEADS, DH), jnp.float32), unit, "gain"
    )(*later)
    mask = 1
    while mask < lax.axis_size("dp"):
        gain_terms = gain_terms + swap(gain_terms, "dp", mask)
        mask *= 2
    grads = []
    for chain in range(CHAINS):
        cols = part_of(chain)
        grads = call(
            final_body,
            [cols, cols, wide, wide, tall] + [spot] * len(grads),
            [cols] * 2,
            [full_low] * 2,
            16 * unit,
            "final",
            {5: 0, 6: 1} if grads else None,
        )(key, value, *parts[chain], later[chain], *grads)
    grad_key, grad_value = grads
    positions = lax.axis_size("seq") * lax.axis_size("dp") * BLOCK
    grad_gain = gain_terms.reshape(HEADS * DH) / math.sqrt(positions)
    return (grad_query[0].reshape(full), grad_key.reshape(full), grad_value.reshape(full), grad_gain)


def solution(mesh):
    sharded = P("dp", "seq", None)
    return jax.shard_map(
        local,
        mesh=mesh,
        in_specs=(sharded, sharded, sharded, P(), sharded),
        out_specs=(sharded, sharded, sharded, P()),
        check_vma=False,
    )
```

time: 79.5 us -> 98.9 us (1.24)
  starting transfers between devices: 34.8 us -> 42.7 us
  Pallas kernels: 9.91 us -> 15.6 us
  local copies, waits for them, and re-layouts: 3.17 us -> 6.47 us
  waiting for transfers between devices: 29 us -> 31.5 us
    all_to_all x0 -> x8, starting transfers between devices: none -> 35.3 us  [the longest x4 18.7 us: carried_in(): return lax.all_to_all(back, axis, 0, 0, axis_index_groups=teams)]
    ppermute x25 -> x5, starting transfers between devices: 34.8 us -> 7.4 us  [swap(): lax.ppermute(array, axis, [(s, s ^ mask) for s in range(lax.axis_size(axi...]
    all_to_all x0 -> x8, waiting for transfers between devices: none -> 18.9 us  [the longest x4 11.1 us: carried_in(): held = lax.all_to_all(parts, axis, 0, 0, axis_index_groups=teams)]
    ppermute x25 -> x5, waiting for transfers between devices: 29 us -> 12.6 us  [swap(): lax.ppermute(array, axis, [(s, s ^ mask) for s in range(lax.axis_size(axi...]
    pallas_call x9 -> x13, Pallas kernels: 8.54 us -> 14.2 us  [the longest x2 4.07 us: local(): call(partial_body, [cols, cols, cols, wide, short] + [spot] * len(grad_qu...]
    unnamed x16 -> x30, local copies, waits for them, and re-layouts: 3.15 us -> 6.47 us
  transfers between devices with their start and end apart: 25 -> 13, of which waited for: 19 -> 12; matrix products, arithmetic and copies ran while one was open for 0% -> 0% of each run, Pallas kernels for 12% -> 15%
where the time goes in v6:
time: 98.9 us; the launch traced here: 97.7 us
  starting transfers between devices  42.7 us (43%)
  waiting for transfers between devices  31.5 us (32%)
  Pallas kernels  15.6 us (16%)
  local copies, waits for them, and re-layouts  6.47 us (7%)
    all_to_all x4, starting transfers between devices, carried_in(): return lax.all_to_all(back, axis, 0, 0, axis_index_groups=teams)  18.7 us
    all_to_all x4, starting transfers between devices, carried_in(): held = lax.all_to_all(parts, axis, 0, 0, axis_index_groups=teams)  16.6 us
    ppermute x5, waiting for transfers between devices, swap(): lax.ppermute(array, axis, [(s, s ^ mask) for s in range(lax.axis_size(axi...  12.6 us
    all_to_all x4, waiting for transfers between devices, carried_in(): held = lax.all_to_all(parts, axis, 0, 0, axis_index_groups=teams)  11.1 us
    all_to_all x4, waiting for transfers between devices, carried_in(): return lax.all_to_all(back, axis, 0, 0, axis_index_groups=teams)  7.81 us
    ppermute x5, starting transfers between devices, swap(): lax.ppermute(array, axis, [(s, s ^ mask) for s in range(lax.axis_size(axi...  7.4 us
    unnamed x30, local copies, waits for them, and re-layouts  6.47 us
    pallas_call x2, Pallas kernels, local(): call(partial_body, [cols, cols, cols, wide, short] + [spot] * len(grad_qu...  4.07 us
  transfers between devices with their start and end apart: 13, of which 12 were waited for; matrix products, arithmetic and copies ran while one was open for 0% of the time, Pallas kernels for 15%

profile of v6, /device:TPU:0, one launch (start us, length us, event | category | flops | bytes accessed | tf_op | source)
XLA Modules:
  0.0 97.7 jit_solution(3975964487869058983)
XLA Ops:
  0.6 1.0 %copy-done = bf16[1,256,1024]{2,1,0:T(8,128)(2,1)S(1)} copy-done((bf16[1,256,1024]{2,1,0:T(8,128)(2,1)S(1)}, bf16[1,256,1024]{2,1,0:T(8,128)(2,1)}, u32[]{:S(2)}) %copy-start) | copy-done | bytes 524312
  1.7 1.0 %copy-done.2 = bf16[1,256,1024]{2,1,0:T(8,128)(2,1)S(1)} copy-done((bf16[1,256,1024]{2,1,0:T(8,128)(2,1)S(1)}, bf16[1,256,1024]{2,1,0:T(8,128)(2,1)}, u32[]{:S(2)}) %copy-start.2) | copy-done | bytes 524312
  2.7 1.0 %delta.3 = f32[8,64,128]{2,1,0:T(8,128)} custom-call(bf16[256,1024]{1,0:T(8,128)(2,1)S(1)} %bitcast.10, bf16[256,1024]{1,0:T(8,128)(2,1)S(1)} %bitcast.18), custom_call_target="tpu_custom_call" | custom-call | flops 201326592 | bytes 2097152 | tf_op jit(solution)/shard_map/delta/pallas_call | solution.py:195
  3.7 6.3 %all-to-all-start.2 = ((f32[8,64,128]{2,1,0:T(8,128)}), f32[8,64,128]{2,1,0:T(8,128)S(1)}, u32[]{:S(2)}, u32[]{:S(2)}) async-start(f32[8,64,128]{2,1,0:T(8,128)} %delta.3), calls=%async_computation.2 | async-start | bytes 524288 | tf_op jit(solution)/shard_map/all_to_all | solution.py:154
  10.0 1.0 %delta.2 = f32[8,64,128]{2,1,0:T(8,128)} custom-call(bf16[256,1024]{1,0:T(8,128)(2,1)S(1)} %bitcast.11, bf16[256,1024]{1,0:T(8,128)(2,1)S(1)} %bitcast.19), custom_call_target="tpu_custom_call" | custom-call | flops 201326592 | bytes 2097152 | tf_op jit(solution)/shard_map/delta/pallas_call | solution.py:195
  11.0 5.6 %all-to-all-done.2.held_ref = f32[8,64,128]{2,1,0:T(8,128)S(1)} async-done(((f32[8,64,128]{2,1,0:T(8,128)}), f32[8,64,128]{2,1,0:T(8,128)S(1)}, u32[]{:S(2)}, u32[]{:S(2)}) %all-to-all-start.2) | async-done | bytes 262176 | tf_op jit(solution)/shard_map/all_to_all | solution.py:154
  16.7 3.4 %all-to-all-start = ((f32[8,64,128]{2,1,0:T(8,128)}), f32[8,64,128]{2,1,0:T(8,128)S(1)}, u32[]{:S(2)}, u32[]{:S(2)}) async-start(f32[8,64,128]{2,1,0:T(8,128)} %delta.2), calls=%async_computation | async-start | bytes 524288 | tf_op jit(solution)/shard_map/all_to_all | solution.py:154
  20.1 2.7 %collective-permute-start.1 = (f32[64,128]{1,0:T(8,128)S(1)}, f32[64,128]{1,0:T(8,128)S(1)}, u32[]{:S(2)}, u32[]{:S(2)}) collective-permute-start(f32[64,128]{1,0:T(8,128)S(1)} %reduce_sum.37), channel_id=1, source_target_pairs={{0,16},{2,18},{4,20},{6,22},{8,24},{10,26},{12,28},{14,30},{16,0},... | collective-permute-start | bytes 98312 | tf_op jit(solution)/shard_map/ppermute | solution.py:148
  22.8 2.3 %collective-permute-done.1 = f32[64,128]{1,0:T(8,128)S(1)} collective-permute-done((f32[64,128]{1,0:T(8,128)S(1)}, f32[64,128]{1,0:T(8,128)S(1)}, u32[]{:S(2)}, u32[]{:S(2)}) %collective-permute-start.1) | collective-permute-done | bytes 32800 | tf_op jit(solution)/shard_map/ppermute | solution.py:148
  26.6 5.3 %all-to-all-start.3 = ((f32[8,64,128]{2,1,0:T(8,128)}), f32[8,64,128]{2,1,0:T(8,128)S(1)}, u32[]{:S(2)}, u32[]{:S(2)}) async-start(f32[8,64,128]{2,1,0:T(8,128)} %prefix.5), calls=%async_computation.3 | async-start | bytes 524288 | tf_op jit(solution)/shard_map/all_to_all | solution.py:173
  32.0 1.8 %collective-permute-start = (f32[64,128]{1,0:T(8,128)S(1)}, f32[64,128]{1,0:T(8,128)S(1)}, u32[]{:S(2)}, u32[]{:S(2)}) collective-permute-start(f32[64,128]{1,0:T(8,128)S(1)} %reduce_sum.36), channel_id=1, source_target_pairs={{0,16},{2,18},{4,20},{6,22},{8,24},{10,26},{12,28},{14,30},{16,0},... | collective-permute-start | bytes 98312 | tf_op jit(solution)/shard_map/ppermute | solution.py:148
  33.7 3.2 %collective-permute-done = f32[64,128]{1,0:T(8,128)S(1)} collective-permute-done((f32[64,128]{1,0:T(8,128)S(1)}, f32[64,128]{1,0:T(8,128)S(1)}, u32[]{:S(2)}, u32[]{:S(2)}) %collective-permute-start) | collective-permute-done | bytes 32800 | tf_op jit(solution)/shard_map/ppermute | solution.py:148
  38.6 4.4 %all-to-all-start.1 = ((f32[8,64,128]{2,1,0:T(8,128)}), f32[8,64,128]{2,1,0:T(8,128)S(1)}, u32[]{:S(2)}, u32[]{:S(2)}) async-start(f32[8,64,128]{2,1,0:T(8,128)} %prefix.4), calls=%async_computation.1 | async-start | bytes 524288 | tf_op jit(solution)/shard_map/all_to_all | solution.py:173
  44.1 1.6 %norm.3 = (bf16[256,512]{1,0:T(8,128)(2,1)S(1)}, f32[8,72,128]{2,1,0:T(8,128)}) custom-call(bf16[256,1024]{1,0:T(8,128)(2,1)S(1)} %bitcast.27, bf16[256,1024]{1,0:T(8,128)(2,1)S(1)} %bitcast.32, f32[256,512]{1,0:T(8,128)S(1)} %inner.3.inner_ref, f32[1,1024]{1,0:T(1,128)S(1)} %bitcast.34, f32[8,64,128]{2,1,0:T(8,128)S(1)} %all-to-all-done.3.state_ref), custom_call_target="tpu_custom_call" | custom-call | flops 536870912 | bytes 2097152 | tf_op jit(solution)/shard_map/norm/pallas_call | solution.py:202
  46.3 3.3 %all-to-all-done.1.state_ref = f32[8,64,128]{2,1,0:T(8,128)S(1)} async-done(((f32[8,64,128]{2,1,0:T(8,128)}), f32[8,64,128]{2,1,0:T(8,128)S(1)}, u32[]{:S(2)}, u32[]{:S(2)}) %all-to-all-start.1) | async-done | bytes 262176 | tf_op jit(solution)/shard_map/all_to_all | solution.py:173
  49.6 3.4 %all-to-all-start.6 = ((f32[8,72,128]{2,1,0:T(8,128)}), f32[8,72,128]{2,1,0:T(8,128)S(1)}, u32[]{:S(2)}, u32[]{:S(2)}) async-start(f32[8,72,128]{2,1,0:T(8,128)} %get-tuple-element.27), calls=%async_computation.6 | async-start | bytes 589824 | tf_op jit(solution)/shard_map/all_to_all | solution.py:154
  53.7 1.6 %norm.2 = (bf16[256,512]{1,0:T(8,128)(2,1)S(1)}, f32[8,72,128]{2,1,0:T(8,128)}) custom-call(bf16[256,1024]{1,0:T(8,128)(2,1)S(1)} %bitcast.29, bf16[256,1024]{1,0:T(8,128)(2,1)S(1)} %bitcast.33, f32[256,512]{1,0:T(8,128)S(1)} %inner.2.inner_ref, f32[1,1024]{1,0:T(1,128)S(1)} %bitcast.35, f32[8,64,128]{2,1,0:T(8,128)S(1)} %all-to-all-done.1.state_ref), custom_call_target="tpu_custom_call" | custom-call | flops 536870912 | bytes 2097152 | tf_op jit(solution)/shard_map/norm/pallas_call | solution.py:202
  56.0 3.8 %all-to-all-done.6.held_ref = f32[8,72,128]{2,1,0:T(8,128)S(1)} async-done(((f32[8,72,128]{2,1,0:T(8,128)}), f32[8,72,128]{2,1,0:T(8,128)S(1)}, u32[]{:S(2)}, u32[]{:S(2)}) %all-to-all-start.6) | async-done | bytes 294944 | tf_op jit(solution)/shard_map/all_to_all | solution.py:154
  59.8 3.4 %all-to-all-start.4 = ((f32[8,72,128]{2,1,0:T(8,128)}), f32[8,72,128]{2,1,0:T(8,128)S(1)}, u32[]{:S(2)}, u32[]{:S(2)}) async-start(f32[8,72,128]{2,1,0:T(8,128)} %get-tuple-element.24), calls=%async_computation.4 | async-start | bytes 589824 | tf_op jit(solution)/shard_map/all_to_all | solution.py:154
  63.2 1.9 %collective-permute-start.3 = (f32[72,128]{1,0:T(8,128)S(1)}, f32[72,128]{1,0:T(8,128)S(1)}, u32[]{:S(2)}, u32[]{:S(2)}) collective-permute-start(f32[72,128]{1,0:T(8,128)S(1)} %reduce_sum.39), channel_id=1, source_target_pairs={{0,16},{2,18},{4,20},{6,22},{8,24},{10,26},{12,28},{14,30},{16,0},... | collective-permute-start | bytes 110600 | tf_op jit(solution)/shard_map/ppermute | solution.py:148
  65.1 3.1 %collective-permute-done.3 = f32[72,128]{1,0:T(8,128)S(1)} collective-permute-done((f32[72,128]{1,0:T(8,128)S(1)}, f32[72,128]{1,0:T(8,128)S(1)}, u32[]{:S(2)}, u32[]{:S(2)}) %collective-permute-start.3) | collective-permute-done | bytes 36896 | tf_op jit(solution)/shard_map/ppermute | solution.py:148
  69.9 5.3 %all-to-all-start.7 = ((f32[8,72,128]{2,1,0:T(8,128)}), f32[8,72,128]{2,1,0:T(8,128)S(1)}, u32[]{:S(2)}, u32[]{:S(2)}) async-start(f32[8,72,128]{2,1,0:T(8,128)} %prefix.7), calls=%async_computation.7 | async-start | bytes 589824 | tf_op jit(solution)/shard_map/all_to_all | solution.py:173
  75.2 1.1 %collective-permute-start.2 = (f32[72,128]{1,0:T(8,128)S(1)}, f32[72,128]{1,0:T(8,128)S(1)}, u32[]{:S(2)}, u32[]{:S(2)}) collective-permute-start(f32[72,128]{1,0:T(8,128)S(1)} %reduce_sum.38), channel_id=1, source_target_pairs={{0,16},{2,18},{4,20},{6,22},{8,24},{10,26},{12,28},{14,30},{16,0},... | collective-permute-start | bytes 110600 | tf_op jit(solution)/shard_map/ppermute | solution.py:148
  76.3 4.0 %collective-permute-done.2 = f32[72,128]{1,0:T(8,128)S(1)} collective-permute-done((f32[72,128]{1,0:T(8,128)S(1)}, f32[72,128]{1,0:T(8,128)S(1)}, u32[]{:S(2)}, u32[]{:S(2)}) %collective-permute-start.2) | collective-permute-done | bytes 36896 | tf_op jit(solution)/shard_map/ppermute | solution.py:148
  81.0 2.5 %all-to-all-done.7.state_ref.refs_0_ = f32[8,72,128]{2,1,0:T(8,128)S(1)} async-done(((f32[8,72,128]{2,1,0:T(8,128)}), f32[8,72,128]{2,1,0:T(8,128)S(1)}, u32[]{:S(2)}, u32[]{:S(2)}) %all-to-all-start.7) | async-done | bytes 294944 | tf_op jit(solution)/shard_map/all_to_all | solution.py:173
  83.6 3.6 %all-to-all-start.5 = ((f32[8,72,128]{2,1,0:T(8,128)}), f32[8,72,128]{2,1,0:T(8,128)S(1)}, u32[]{:S(2)}, u32[]{:S(2)}) async-start(f32[8,72,128]{2,1,0:T(8,128)} %prefix.6), calls=%async_computation.5 | async-start | bytes 589824 | tf_op jit(solution)/shard_map/all_to_all | solution.py:173
  87.2 2.0 %partial.2 = (bf16[256,1024]{1,0:T(8,128)(2,1)}, f32[256,512]{1,0:T(8,128)S(1)}, f32[256,512]{1,0:T(8,128)S(1)}) custom-call(bf16[256,1024]{1,0:T(8,128)(2,1)S(1)} %bitcast.30, bf16[256,1024]{1,0:T(8,128)(2,1)S(1)} %bitcast.14, bf16[256,1024]{1,0:T(8,128)(2,1)S(1)} %bitcast.22, bf16[256,512]{1,0:T(8,128)(2,1)S(1)} %copy-done.12, ...), custom_call_target="tpu_custom_call" | custom-call | flops 1610612736 | bytes 2097152 | tf_op jit(solution)/shard_map/partial/pallas_call | solution.py:211
  90.8 2.0 %partial.3 = (bf16[256,1024]{1,0:T(8,128)(2,1)}, f32[256,512]{1,0:T(8,128)S(1)}, f32[256,512]{1,0:T(8,128)S(1)}) custom-call(bf16[256,1024]{1,0:T(8,128)(2,1)S(1)} %bitcast.31, bf16[256,1024]{1,0:T(8,128)(2,1)S(1)} %bitcast.15, bf16[256,1024]{1,0:T(8,128)(2,1)S(1)} %bitcast.23, bf16[256,512]{1,0:T(8,128)(2,1)S(1)} %copy-done.14, ...), custom_call_target="tpu_custom_call", output_to_operand_aliasing={{0}: (5, {})} | custom-call | flops 1610612736 | bytes 2097152 | tf_op jit(solution)/shard_map/partial/pallas_call | solution.py:211
  92.9 1.1 %all-to-all-done.5.state_ref.refs_1_ = f32[8,72,128]{2,1,0:T(8,128)S(1)} async-done(((f32[8,72,128]{2,1,0:T(8,128)}), f32[8,72,128]{2,1,0:T(8,128)S(1)}, u32[]{:S(2)}, u32[]{:S(2)}) %all-to-all-start.5) | async-done | bytes 294944 | tf_op jit(solution)/shard_map/all_to_all | solution.py:173
  94.0 1.0 %copy-done.8 = f32[256,512]{1,0:T(8,128)S(1)} copy-done((f32[256,512]{1,0:T(8,128)S(1)}, f32[256,512]{1,0:T(8,128)}, u32[]{:S(2)}) %copy-start.8) | copy-done | bytes 524312
  95.0 1.1 %final.2 = (bf16[256,1024]{1,0:T(8,128)(2,1)}, bf16[256,1024]{1,0:T(8,128)(2,1)}) custom-call(bf16[256,1024]{1,0:T(8,128)(2,1)S(1)} %bitcast.16, bf16[256,1024]{1,0:T(8,128)(2,1)S(1)} %bitcast.24, f32[256,512]{1,0:T(8,128)S(1)} %copy-done.6, f32[256,512]{1,0:T(8,128)S(1)} %copy-done.8, f32[8,72,128]{2,1,0:T(8,128)S(1)} %all-to-all-done.7.state_ref.refs_0_), custom_call_target="tpu_custom_call" | custom-call | flops 536870912 | bytes 2097152 | tf_op jit(solution)/shard_map/final/pallas_call | solution.py:232
  96.1 1.1 %final.3 = (bf16[256,1024]{1,0:T(8,128)(2,1)}, bf16[256,1024]{1,0:T(8,128)(2,1)}) custom-call(bf16[256,1024]{1,0:T(8,128)(2,1)S(1)} %bitcast.17, bf16[256,1024]{1,0:T(8,128)(2,1)S(1)} %bitcast.25, f32[256,512]{1,0:T(8,128)S(1)} %get-tuple-element.22.key_part_ref, ...), custom_call_target="tpu_custom_call", output_to_operand_aliasing={{0}: (5, {}), {1}: (6, {})} | custom-call | flops 536870912 | bytes 2097152 | tf_op jit(solution)/shard_map/final/pallas_call | solution.py:232
  (48 shorter events, 10.9 us)
Async XLA Ops:
  0.6 1.0 %copy-start = (bf16[1,256,1024]{2,1,0:T(8,128)(2,1)S(1)}, bf16[1,256,1024]{2,1,0:T(8,128)(2,1)}, u32[]{:S(2)}) copy-start(bf16[1,256,1024]{2,1,0:T(8,128)(2,1)} %param.6) | copy-start | bytes 1572868
  1.7 1.0 %copy-start.2 = (bf16[1,256,1024]{2,1,0:T(8,128)(2,1)S(1)}, bf16[1,256,1024]{2,1,0:T(8,128)(2,1)}, u32[]{:S(2)}) copy-start(bf16[1,256,1024]{2,1,0:T(8,128)(2,1)} %param.7) | copy-start | bytes 1572868
  2.7 7.3 %copy-start.3 = (bf16[1,256,1024]{2,1,0:T(8,128)(2,1)S(1)}, bf16[1,256,1024]{2,1,0:T(8,128)(2,1)}, u32[]{:S(2)}) copy-start(bf16[1,256,1024]{2,1,0:T(8,128)(2,1)} %param.7) | copy-start | bytes 1572868
  3.7 6.3 %copy-start.1 = (bf16[1,256,1024]{2,1,0:T(8,128)(2,1)S(1)}, bf16[1,256,1024]{2,1,0:T(8,128)(2,1)}, u32[]{:S(2)}) copy-start(bf16[1,256,1024]{2,1,0:T(8,128)(2,1)} %param.6) | copy-start | bytes 1572868
  3.7 12.9 %all-to-all-start.2 = ((f32[8,64,128]{2,1,0:T(8,128)}), f32[8,64,128]{2,1,0:T(8,128)S(1)}, u32[]{:S(2)}, u32[]{:S(2)}) async-start(f32[8,64,128]{2,1,0:T(8,128)} %delta.3), calls=%async_computation.2 | async-start | bytes 524288 | tf_op jit(solution)/shard_map/all_to_all | solution.py:154
  16.7 10.0 %all-to-all-start = ((f32[8,64,128]{2,1,0:T(8,128)}), f32[8,64,128]{2,1,0:T(8,128)S(1)}, u32[]{:S(2)}, u32[]{:S(2)}) async-start(f32[8,64,128]{2,1,0:T(8,128)} %delta.2), calls=%async_computation | async-start | bytes 524288 | tf_op jit(solution)/shard_map/all_to_all | solution.py:154
  20.1 5.0 %collective-permute-start.1 = (f32[64,128]{1,0:T(8,128)S(1)}, f32[64,128]{1,0:T(8,128)S(1)}, u32[]{:S(2)}, u32[]{:S(2)}) collective-permute-start(f32[64,128]{1,0:T(8,128)S(1)} %reduce_sum.37), channel_id=1, source_target_pairs={{0,16},{2,18},{4,20},{6,22},{8,24},{10,26},{12,28},{14,30},{16,0},... | collective-permute-start | bytes 98312 | tf_op jit(solution)/shard_map/ppermute | solution.py:148
  26.6 11.9 %all-to-all-start.3 = ((f32[8,64,128]{2,1,0:T(8,128)}), f32[8,64,128]{2,1,0:T(8,128)S(1)}, u32[]{:S(2)}, u32[]{:S(2)}) async-start(f32[8,64,128]{2,1,0:T(8,128)} %prefix.5), calls=%async_computation.3 | async-start | bytes 524288 | tf_op jit(solution)/shard_map/all_to_all | solution.py:173
  32.0 5.0 %collective-permute-start = (f32[64,128]{1,0:T(8,128)S(1)}, f32[64,128]{1,0:T(8,128)S(1)}, u32[]{:S(2)}, u32[]{:S(2)}) collective-permute-start(f32[64,128]{1,0:T(8,128)S(1)} %reduce_sum.36), channel_id=1, source_target_pairs={{0,16},{2,18},{4,20},{6,22},{8,24},{10,26},{12,28},{14,30},{16,0},... | collective-permute-start | bytes 98312 | tf_op jit(solution)/shard_map/ppermute | solution.py:148
  36.9 6.1 %copy-start.4 = (bf16[1,256,1024]{2,1,0:T(8,128)(2,1)S(1)}, bf16[1,256,1024]{2,1,0:T(8,128)(2,1)}, u32[]{:S(2)}) copy-start(bf16[1,256,1024]{2,1,0:T(8,128)(2,1)} %param.5) | copy-start | bytes 1572868
  38.6 11.1 %all-to-all-start.1 = ((f32[8,64,128]{2,1,0:T(8,128)}), f32[8,64,128]{2,1,0:T(8,128)S(1)}, u32[]{:S(2)}, u32[]{:S(2)}) async-start(f32[8,64,128]{2,1,0:T(8,128)} %prefix.4), calls=%async_computation.1 | async-start | bytes 524288 | tf_op jit(solution)/shard_map/all_to_all | solution.py:173
  43.0 1.0 %copy-start.9 = (bf16[1,256,1024]{2,1,0:T(8,128)(2,1)S(1)}, bf16[1,256,1024]{2,1,0:T(8,128)(2,1)}, u32[]{:S(2)}) copy-start(bf16[1,256,1024]{2,1,0:T(8,128)(2,1)} %param.9) | copy-start | bytes 1572868
  43.0 1.0 %copy-start.10 = (f32[1024]{0:T(1024)S(1)}, f32[1024]{0:T(1024)}, u32[]{:S(2)}) copy-start(f32[1024]{0:T(1024)} %param.8) | copy-start | bytes 12292
  45.6 0.7 copy-start.11
  49.6 10.2 %all-to-all-start.6 = ((f32[8,72,128]{2,1,0:T(8,128)}), f32[8,72,128]{2,1,0:T(8,128)S(1)}, u32[]{:S(2)}, u32[]{:S(2)}) async-start(f32[8,72,128]{2,1,0:T(8,128)} %get-tuple-element.27), calls=%async_computation.6 | async-start | bytes 589824 | tf_op jit(solution)/shard_map/all_to_all | solution.py:154
  55.3 0.7 copy-start.13
  59.8 10.1 %all-to-all-start.4 = ((f32[8,72,128]{2,1,0:T(8,128)}), f32[8,72,128]{2,1,0:T(8,128)S(1)}, u32[]{:S(2)}, u32[]{:S(2)}) async-start(f32[8,72,128]{2,1,0:T(8,128)} %get-tuple-element.24), calls=%async_computation.4 | async-start | bytes 589824 | tf_op jit(solution)/shard_map/all_to_all | solution.py:154
  63.2 5.0 %collective-permute-start.3 = (f32[72,128]{1,0:T(8,128)S(1)}, f32[72,128]{1,0:T(8,128)S(1)}, u32[]{:S(2)}, u32[]{:S(2)}) collective-permute-start(f32[72,128]{1,0:T(8,128)S(1)} %reduce_sum.39), channel_id=1, source_target_pairs={{0,16},{2,18},{4,20},{6,22},{8,24},{10,26},{12,28},{14,30},{16,0},... | collective-permute-start | bytes 110600 | tf_op jit(solution)/shard_map/ppermute | solution.py:148
  69.9 13.7 %all-to-all-start.7 = ((f32[8,72,128]{2,1,0:T(8,128)}), f32[8,72,128]{2,1,0:T(8,128)S(1)}, u32[]{:S(2)}, u32[]{:S(2)}) async-start(f32[8,72,128]{2,1,0:T(8,128)} %prefix.7), calls=%async_computation.7 | async-start | bytes 589824 | tf_op jit(solution)/shard_map/all_to_all | solution.py:173
  75.2 5.0 %collective-permute-start.2 = (f32[72,128]{1,0:T(8,128)S(1)}, f32[72,128]{1,0:T(8,128)S(1)}, u32[]{:S(2)}, u32[]{:S(2)}) collective-permute-start(f32[72,128]{1,0:T(8,128)S(1)} %reduce_sum.38), channel_id=1, source_target_pairs={{0,16},{2,18},{4,20},{6,22},{8,24},{10,26},{12,28},{14,30},{16,0},... | collective-permute-start | bytes 110600 | tf_op jit(solution)/shard_map/ppermute | solution.py:148
  81.0 6.2 %copy-start.12 = (bf16[256,512]{1,0:T(8,128)(2,1)S(1)}, bf16[256,512]{1,0:T(8,128)(2,1)}, u32[]{:S(2)}) copy-start(bf16[256,512]{1,0:T(8,128)(2,1)} %copy-done.11) | copy-start | bytes 786436
  83.6 10.4 %all-to-all-start.5 = ((f32[8,72,128]{2,1,0:T(8,128)}), f32[8,72,128]{2,1,0:T(8,128)S(1)}, u32[]{:S(2)}, u32[]{:S(2)}) async-start(f32[8,72,128]{2,1,0:T(8,128)} %prefix.6), calls=%async_computation.5 | async-start | bytes 589824 | tf_op jit(solution)/shard_map/all_to_all | solution.py:173
  87.2 3.6 %copy-start.14 = (bf16[256,512]{1,0:T(8,128)(2,1)S(1)}, bf16[256,512]{1,0:T(8,128)(2,1)}, u32[]{:S(2)}) copy-start(bf16[256,512]{1,0:T(8,128)(2,1)} %copy-done.13) | copy-start | bytes 786436
  89.2 0.8 copy-start.5
  90.0 0.8 copy-start.7
  92.9 1.1 %copy-start.6 = (f32[256,512]{1,0:T(8,128)S(1)}, f32[256,512]{1,0:T(8,128)}, u32[]{:S(2)}) copy-start(f32[256,512]{1,0:T(8,128)} %copy-done.5) | copy-start | bytes 1572868
  93.9 3.2 %collective-permute-start.4 = (f32[8,128]{1,0:T(8,128)S(1)}, f32[8,128]{1,0:T(8,128)S(1)}, u32[]{:S(2)}, u32[]{:S(2)}) collective-permute-start(f32[8,128]{1,0:T(8,128)S(1)} %gain.1), channel_id=1, source_target_pairs={{0,1},{1,0},{2,3},{3,2},{4,5},{5,4},{6,7},{7,6},{8,9},{9,8},{10,11... | collective-permute-start | bytes 12296 | tf_op jit(solution)/shard_map/ppermute | solution.py:148
  93.9 1.0 %copy-start.8 = (f32[256,512]{1,0:T(8,128)S(1)}, f32[256,512]{1,0:T(8,128)}, u32[]{:S(2)}) copy-start(f32[256,512]{1,0:T(8,128)} %copy-done.7) | copy-start | bytes 1572868

commit v7 on v6

v7 whole, which is shorter than its diff:
```python
import functools
import math

import jax
import jax.numpy as jnp
from jax import lax
from jax.experimental import pallas as pl
from jax.experimental.pallas import tpu as pltpu
from jax.sharding import PartitionSpec as P

HEADS = 8
DH = 128
BLOCK = 256
GROUP = 8
GAIN_ROWS = 8
STEPS = 4
STEP_HEADS = HEADS // STEPS
EPSILON = 1e-06

NT = (((1,), (1,)), ((), ()))
TN = (((0,), (0,)), ((), ()))
NN = (((1,), (0,)), ((), ()))


def dot(left, right, dims):
    return lax.dot_general(left, right, dims, preferred_element_type=jnp.float32)


def columns(head):
    return pl.ds(head * DH, DH)


def causal():
    shape = (BLOCK, BLOCK)
    return lax.broadcasted_iota(jnp.int32, shape, 0) >= lax.broadcasted_iota(jnp.int32, shape, 1)


def delta_body(key_ref, value_ref, delta_ref, key_here, value_here, sems):
    copies = []
    for head in range(HEADS):
        at = columns(head)
        copies.append(
            [
                pltpu.make_async_copy(source.at[:, at], here.at[:, at], sems.at[side, head])
                for side, (source, here) in enumerate(((key_ref, key_here), (value_ref, value_here)))
            ]
        )
        for copy in copies[-1]:
            copy.start()
    for head in range(HEADS):
        at = columns(head)
        for copy in copies[head]:
            copy.wait()
        delta_ref[head] = dot(key_here[:, at], value_here[:, at], TN)


def inner_body(query_ref, key_ref, value_ref, inner_ref):
    keep = causal()
    for head in range(HEADS):
        at = columns(head)
        raw = dot(query_ref[:, at], key_ref[:, at], NT)
        scores = jnp.where(keep, raw, 0.0).astype(jnp.bfloat16)
        inner_ref[:, at] = dot(scores, value_ref[:, at], NN)


def norm_body(query_ref, grad_ref, inner_ref, gain_ref, state_ref, attn_ref, delta_ref):
    for head in range(HEADS):
        at = columns(head)
        query = query_ref[:, at]
        attn = inner_ref[:, at] + dot(query, state_ref[head].astype(jnp.bfloat16), NN)
        per_root = lax.rsqrt(jnp.mean(attn * attn, axis=-1, keepdims=True) + EPSILON)
        normed = attn * per_root
        cotangent = grad_ref[:, at].astype(jnp.float32)
        product = normed * cotangent
        gain = gain_ref[:, at]
        shared = jnp.mean(product * gain, axis=-1, keepdims=True)
        grad_attn = ((gain * cotangent - normed * shared) * per_root).astype(jnp.bfloat16)
        attn_ref[:, at] = grad_attn
        terms = jnp.sum(product, axis=0, keepdims=True)
        delta_ref[head, :DH] = dot(query, grad_attn, TN)
        delta_ref[head, DH:] = jnp.broadcast_to(terms, (GAIN_ROWS, DH))


def partial_body(query_ref, key_ref, value_ref, attn_ref, state_ref, grad_query_ref, key_part_ref, value_part_ref):
    keep = causal()
    for head in range(HEADS):
        at = columns(head)
        query, key, value, grad_attn = query_ref[:, at], key_ref[:, at], value_ref[:, at], attn_ref[:, at]
        scores = jnp.where(keep, dot(query, key, NT), 0.0).astype(jnp.bfloat16)
        grad_scores = jnp.where(keep, dot(grad_attn, value, NT), 0.0).astype(jnp.bfloat16)
        carried = dot(grad_attn, state_ref[head].astype(jnp.bfloat16), NT)
        grad_query_ref[:, at] = (dot(grad_scores, key, NN) + carried).astype(jnp.bfloat16)
        key_part_ref[:, at] = dot(grad_scores, query, TN)
        value_part_ref[:, at] = dot(scores, grad_attn, TN)


def final_body(key_ref, value_ref, key_part_ref, value_part_ref, state_ref, grad_key_ref, grad_value_ref):
    step = pl.program_id(0)
    for head in range(STEP_HEADS):
        whole_head = step * STEP_HEADS + head
        wide = pl.ds(pl.multiple_of(whole_head * DH, DH), DH)
        at = columns(head)
        state = state_ref[whole_head, :DH].astype(jnp.bfloat16)
        grad_key_ref[:, at] = (key_part_ref[:, wide] + dot(value_ref[:, wide], state, NT)).astype(jnp.bfloat16)
        grad_value_ref[:, at] = (value_part_ref[:, wide] + dot(key_ref[:, wide], state, NN)).astype(jnp.bfloat16)


def gain_body(state_ref, gain_ref):
    for head in range(HEADS):
        gain_ref[head : head + 1, :] = state_ref[head, DH : DH + 1]


def prefix_body(reverse, carried_ref, total_ref, held_ref, back_ref):
    running = carried_ref[:DH]
    for member in reversed(range(GROUP)) if reverse else range(GROUP):
        back_ref[member, :DH] = running
        running = running + held_ref[member, :DH]
        if back_ref.shape[1] > DH:
            back_ref[member, DH:] = total_ref[DH:]


def whole(*shape):
    return pl.BlockSpec(shape, lambda step: (0,) * len(shape))


def call(body, in_specs, out_specs, outs, flops, name, steps=1, scratch=()):
    return pl.pallas_call(
        body,
        grid=(steps,),
        in_specs=in_specs,
        out_specs=out_specs,
        out_shape=outs,
        scratch_shapes=scratch,
        compiler_params=pltpu.CompilerParams(vmem_limit_bytes=16 * 1024 * 1024),
        cost_estimate=pl.CostEstimate(flops=flops, bytes_accessed=2 << 20, transcendentals=0),
        name=name,
    )


def carried_in(parts, reverse):
    count, place = lax.axis_size("seq"), lax.axis_index("seq")
    teams = [list(range(first, first + GROUP)) for first in range(0, count, GROUP)]
    held = lax.all_to_all(parts, "seq", 0, 0, axis_index_groups=teams)
    total = jnp.sum(held, axis=0)
    carried = jnp.zeros_like(total)
    mask = GROUP
    while mask < count:
        arrived = lax.ppermute(total, "seq", [(s, s ^ mask) for s in range(count)])
        later = ((place & mask) != 0) != reverse
        carried = carried + jnp.where(later, arrived, 0.0)
        total = total + arrived
        mask *= 2
    single, stacked = whole(*total.shape), whole(*held.shape)
    back = call(
        functools.partial(prefix_body, reverse),
        [single, single, stacked],
        stacked,
        jax.ShapeDtypeStruct(held.shape, jnp.float32),
        1 << 24,
        "prefix",
    )(carried, total, held)
    return lax.all_to_all(back, "seq", 0, 0, axis_index_groups=teams)


def local(queries, keys, values, out_gain, grad_out):
    full = queries.shape
    flat = (full[0] * full[1], full[2])
    assert flat == (BLOCK, HEADS * DH) and lax.axis_size("seq") % GROUP == 0 and GROUP == HEADS
    query, key, value, grad = (a.reshape(flat) for a in (queries, keys, values, grad_out))
    gain = out_gain.reshape(1, HEADS * DH)
    plain = jax.ShapeDtypeStruct((GROUP, DH, DH), jnp.float32)
    taller = jax.ShapeDtypeStruct((GROUP, DH + GAIN_ROWS, DH), jnp.float32)
    full_float = jax.ShapeDtypeStruct(flat, jnp.float32)
    full_low = jax.ShapeDtypeStruct(flat, jnp.bfloat16)
    short, tall, wide = whole(*plain.shape), whole(*taller.shape), whole(*flat)
    unit = 2 * BLOCK * DH * DH * HEADS

    delta = call(
        delta_body,
        [pl.BlockSpec(memory_space=pltpu.HBM)] * 2,
        short,
        plain,
        6 * unit,
        "delta",
        scratch=[pltpu.VMEM(flat, jnp.bfloat16)] * 2 + [pltpu.SemaphoreType.DMA((2, HEADS))],
    )(*[pltpu.with_memory_space_constraint(a, pltpu.HBM) for a in (key, value)])
    states = carried_in(delta, False)
    inner = call(inner_body, [wide] * 3, wide, full_float, 16 * unit, "inner")(query, key, value)
    attn, delta = call(
        norm_body, [wide, wide, wide, whole(1, HEADS * DH), short], [wide, tall], [full_low, taller], 16 * unit, "norm"
    )(query, grad, inner, gain, states)
    later = carried_in(delta, True)
    grad_query, key_part, value_part = call(
        partial_body, [wide] * 4 + [short], [wide] * 3, [full_low, full_float, full_float], 48 * unit, "partial"
    )(query, key, value, attn, states)
    gain_terms = call(
        gain_body, [tall], whole(HEADS, DH), jax.ShapeDtypeStruct((HEADS, DH), jnp.float32), unit, "gain"
    )(later)
    docs, mask = lax.axis_size("dp"), 1
    while mask < docs:
        gain_terms = gain_terms + lax.ppermute(gain_terms, "dp", [(d, d ^ mask) for d in range(docs)])
        mask *= 2
    chunk = pl.BlockSpec((BLOCK, STEP_HEADS * DH), lambda step: (0, step))
    grad_key, grad_value = call(
        final_body, [wide] * 4 + [tall], [chunk] * 2, [full_low] * 2, 16 * unit, "final", steps=STEPS
    )(key, value, key_part, value_part, later)
    grad_gain = gain_terms / math.sqrt(lax.axis_size("seq") * docs * BLOCK)
    return (
        grad_query.reshape(full),
        grad_key.reshape(full),
        grad_value.reshape(full),
        grad_gain.reshape(HEADS * DH),
    )


def solution(mesh):
    sharded = P("dp", "seq", None)
    return jax.shard_map(
        local,
        mesh=mesh,
        in_specs=(sharded, sharded, sharded, P(), sharded),
        out_specs=(sharded, sharded, sharded, P()),
        check_vma=False,
    )
```

time: 98.9 us -> 75 us (0.76)
  starting transfers between devices: 42.7 us -> 11.2 us
  blocking collectives: 0 us -> 27 us
  waiting for transfers between devices: 31.5 us -> 16 us
  Pallas kernels: 15.6 us -> 12.1 us
    all_to_all x8 -> x2, starting transfers between devices: 35.3 us -> 7.16 us  [carried_in(): return lax.all_to_all(back, 'seq', 0, 0, axis_index_groups=teams)]
    all_to_all x0 -> x2, blocking collectives: none -> 27 us  [carried_in(): held = lax.all_to_all(parts, 'seq', 0, 0, axis_index_groups=teams)]
    all_to_all x8 -> x2, waiting for transfers between devices: 18.9 us -> 8.05 us  [carried_in(): return lax.all_to_all(back, 'seq', 0, 0, axis_index_groups=teams)]
    ppermute x5 -> x3, waiting for transfers between devices: 12.6 us -> 7.96 us  [the longest x2 7.96 us: carried_in(): arrived = lax.ppermute(total, 'seq', [(s, s ^ mask) for s in range(count)])]
    ppermute x5 -> x3, starting transfers between devices: 7.4 us -> 4.05 us  [the longest x2 4.05 us: carried_in(): arrived = lax.ppermute(total, 'seq', [(s, s ^ mask) for s in range(count)])]
    pallas_call x11 -> x6, Pallas kernels: 12.7 us -> 10.4 us  [the longest x1 3.34 us: local(): call(partial_body, [wide] * 4 + [short], [wide] * 3, [full_low, full_floa...]
    pallas_call x4 -> x2, Pallas kernels: 2.9 us -> 1.68 us  [carried_in(): call(functools.partial(prefix_body, reverse), [single, single, stacked],...]
    unnamed x30 -> x22, local copies, waits for them, and re-layouts: 6.47 us -> 6.66 us
  transfers between devices with their start and end apart: 13 -> 5, of which waited for: 12 -> 4; matrix products, arithmetic and copies ran while one was open for 0% -> 0% of each run, Pallas kernels for 15% -> 9%
where the time goes in v7:
time: 75 us; the launch traced here: 74.5 us
  blocking collectives  27 us (36%)
  waiting for transfers between devices  16 us (21%)
  Pallas kernels  12.1 us (16%)
  starting transfers between devices  11.2 us (15%)
  local copies, waits for them, and re-layouts  6.66 us (9%)
  between operations  0.75 us (1%)
    all_to_all x2, blocking collectives, carried_in(): held = lax.all_to_all(parts, 'seq', 0, 0, axis_index_groups=teams)  27 us
    all_to_all x2, waiting for transfers between devices, carried_in(): return lax.all_to_all(back, 'seq', 0, 0, axis_index_groups=teams)  8.05 us
    ppermute x2, waiting for transfers between devices, carried_in(): arrived = lax.ppermute(total, 'seq', [(s, s ^ mask) for s in range(count)])  7.96 us
    all_to_all x2, starting transfers between devices, carried_in(): return lax.all_to_all(back, 'seq', 0, 0, axis_index_groups=teams)  7.16 us
    unnamed x22, local copies, waits for them, and re-layouts  6.66 us
    ppermute x2, starting transfers between devices, carried_in(): arrived = lax.ppermute(total, 'seq', [(s, s ^ mask) for s in range(count)])  4.05 us
    pallas_call x1, Pallas kernels, local(): call(partial_body, [wide] * 4 + [short], [wide] * 3, [full_low, full_floa...  3.34 us
    pallas_call x1, Pallas kernels, local(): call(delta_body, [pl.BlockSpec(memory_space=pltpu.HBM)] * 2, short, plain...  2.76 us
  transfers between devices with their start and end apart: 5, of which 4 were waited for; matrix products, arithmetic and copies ran while one was open for 0% of the time, Pallas kernels for 9%

profile of v7, /device:TPU:0, one launch (start us, length us, event | category | flops | bytes accessed | tf_op | source)
XLA Modules:
  0.0 74.5 jit_solution(16695492882435682421)
XLA Ops:
  0.6 2.8 %delta.1 = f32[8,128,128]{2,1,0:T(8,128)S(1)} custom-call(bf16[256,1024]{1,0:T(8,128)(2,1)} %bitcast.10, bf16[256,1024]{1,0:T(8,128)(2,1)} %bitcast.14), custom_call_target="tpu_custom_call" | custom-call | flops 402653184 | bytes 2097152 | tf_op jit(solution)/shard_map/delta/pallas_call | solution.py:178
  3.4 15.4 %all_to_all.20.held_ref = f32[8,128,128]{2,1,0:T(8,128)S(1)} all-to-all(f32[8,128,128]{2,1,0:T(8,128)S(1)} %delta.1), channel_id=1, replica_groups={{0,2,4,6,8,10,12,14},{16,18,20,22,24,26,28,30},{1,3,5,7,9,11,13,15},{17..., dimensions={0} | all-to-all | bytes 1048576 | tf_op jit(solution)/shard_map/all_to_all | solution.py:143
  18.8 2.7 %collective-permute-start = (f32[128,128]{1,0:T(8,128)S(1)}, f32[128,128]{1,0:T(8,128)S(1)}, u32[]{:S(2)}, u32[]{:S(2)}) collective-permute-start(f32[128,128]{1,0:T(8,128)S(1)} %reduce_sum.18), channel_id=1, source_target_pairs={{0,16},{2,18},{4,20},{6,22},{8,24},{10,26},{12,28},{14,30},{16,0},... | collective-permute-start | bytes 196616 | tf_op jit(solution)/shard_map/ppermute | solution.py:148
  21.5 3.3 %collective-permute-done = f32[128,128]{1,0:T(8,128)S(1)} collective-permute-done((f32[128,128]{1,0:T(8,128)S(1)}, f32[128,128]{1,0:T(8,128)S(1)}, u32[]{:S(2)}, u32[]{:S(2)}) %collective-permute-start) | collective-permute-done | bytes 65568 | tf_op jit(solution)/shard_map/ppermute | solution.py:148
  24.8 0.0 copy-start.3
  24.8 0.8 %prefix.2 = f32[8,128,128]{2,1,0:T(8,128)} custom-call(f32[128,128]{1,0:T(8,128)S(1)} %get-tuple-element.21.carried_ref, f32[128,128]{1,0:T(8,128)S(1)} %get-tuple-element.20.total_ref, f32[8,128,128]{2,1,0:T(8,128)S(1)} %all_to_all.20.held_ref), custom_call_target="tpu_custom_call" | custom-call | flops 16777216 | bytes 2097152 | tf_op jit(solution)/shard_map/prefix/pallas_call | solution.py:154
  25.6 3.6 %all-to-all-start.1 = ((f32[8,128,128]{2,1,0:T(8,128)}), f32[8,128,128]{2,1,0:T(8,128)S(1)}, u32[]{:S(2)}, u32[]{:S(2)}) async-start(f32[8,128,128]{2,1,0:T(8,128)} %prefix.2), calls=%async_computation.1 | async-start | bytes 1048576 | tf_op jit(solution)/shard_map/all_to_all | solution.py:162
  29.3 0.0 copy-done.3
  29.3 0.0 copy-done
  29.3 0.0 copy-start.2
  29.3 0.0 copy-start.4
  29.3 0.9 %inner.1.inner_ref = f32[256,1024]{1,0:T(8,128)S(1)} custom-call(bf16[256,1024]{1,0:T(8,128)(2,1)S(1)} %bitcast.19, bf16[256,1024]{1,0:T(8,128)(2,1)S(1)} %bitcast.11, bf16[256,1024]{1,0:T(8,128)(2,1)S(1)} %bitcast.15), custom_call_target="tpu_custom_call" | custom-call | flops 1073741824 | bytes 2097152 | tf_op jit(solution)/shard_map/inner/pallas_call | solution.py:188
  30.3 1.0 %copy-done.9 = f32[256,1024]{1,0:T(8,128)} copy-done((f32[256,1024]{1,0:T(8,128)}, f32[256,1024]{1,0:T(8,128)S(1)}, u32[]{:S(2)}) %copy-start.9) | copy-done | bytes 1048600
  31.2 5.6 %all-to-all-done.1.state_ref = f32[8,128,128]{2,1,0:T(8,128)S(1)} async-done(((f32[8,128,128]{2,1,0:T(8,128)}), f32[8,128,128]{2,1,0:T(8,128)S(1)}, u32[]{:S(2)}, u32[]{:S(2)}) %all-to-all-start.1) | async-done | bytes 524320 | tf_op jit(solution)/shard_map/all_to_all | solution.py:162
  36.9 0.0 copy-done.2
  36.9 1.2 %copy-done.10 = f32[256,1024]{1,0:T(8,128)S(1)} copy-done((f32[256,1024]{1,0:T(8,128)S(1)}, f32[256,1024]{1,0:T(8,128)}, u32[]{:S(2)}) %copy-start.10) | copy-done | bytes 1048600
  38.1 1.3 %norm.1 = (bf16[256,1024]{1,0:T(8,128)(2,1)S(1)}, f32[8,136,128]{2,1,0:T(8,128)S(1)}) custom-call(bf16[256,1024]{1,0:T(8,128)(2,1)S(1)} %bitcast.20, bf16[256,1024]{1,0:T(8,128)(2,1)S(1)} %bitcast.18, f32[256,1024]{1,0:T(8,128)S(1)} %copy-done.10, f32[1,1024]{1,0:T(1,128)S(1)} %bitcast.22, f32[8,128,128]{2,1,0:T(8,128)S(1)} %all-to-all-done.1.state_ref), custom_call_target="tpu_custom_call" | custom-call | flops 1073741824 | bytes 2097152 | tf_op jit(solution)/shard_map/norm/pallas_call | solution.py:189
  39.4 11.6 %all_to_all.21.held_ref = f32[8,136,128]{2,1,0:T(8,128)S(1)} all-to-all(f32[8,136,128]{2,1,0:T(8,128)S(1)} %get-tuple-element.15), channel_id=1, replica_groups={{0,2,4,6,8,10,12,14},{16,18,20,22,24,26,28,30},{1,3,5,7,9,11,13,15},{17..., dimensions={0} | all-to-all | bytes 1114112 | tf_op jit(solution)/shard_map/all_to_all | solution.py:143
  51.1 1.4 %collective-permute-start.1 = (f32[136,128]{1,0:T(8,128)S(1)}, f32[136,128]{1,0:T(8,128)S(1)}, u32[]{:S(2)}, u32[]{:S(2)}) collective-permute-start(f32[136,128]{1,0:T(8,128)S(1)} %reduce_sum.19), channel_id=1, source_target_pairs={{0,16},{2,18},{4,20},{6,22},{8,24},{10,26},{12,28},{14,30},{16,0},... | collective-permute-start | bytes 208904 | tf_op jit(solution)/shard_map/ppermute | solution.py:148
  52.5 4.7 %collective-permute-done.1 = f32[136,128]{1,0:T(8,128)S(1)} collective-permute-done((f32[136,128]{1,0:T(8,128)S(1)}, f32[136,128]{1,0:T(8,128)S(1)}, u32[]{:S(2)}, u32[]{:S(2)}) %collective-permute-start.1) | collective-permute-done | bytes 69664 | tf_op jit(solution)/shard_map/ppermute | solution.py:148
  57.2 0.9 %prefix.3 = f32[8,136,128]{2,1,0:T(8,128)} custom-call(f32[136,128]{1,0:T(8,128)S(1)} %get-tuple-element.19.carried_ref, f32[136,128]{1,0:T(8,128)S(1)} %get-tuple-element.18.total_ref, f32[8,136,128]{2,1,0:T(8,128)S(1)} %all_to_all.21.held_ref), custom_call_target="tpu_custom_call" | custom-call | flops 16777216 | bytes 2097152 | tf_op jit(solution)/shard_map/prefix/pallas_call | solution.py:154
  58.1 3.5 %all-to-all-start.3 = ((f32[8,136,128]{2,1,0:T(8,128)}), f32[8,136,128]{2,1,0:T(8,128)S(1)}, u32[]{:S(2)}, u32[]{:S(2)}) async-start(f32[8,136,128]{2,1,0:T(8,128)} %prefix.3), calls=%async_computation.3 | async-start | bytes 1114112 | tf_op jit(solution)/shard_map/all_to_all | solution.py:162
  61.6 3.3 %partial.1 = (bf16[256,1024]{1,0:T(8,128)(2,1)}, f32[256,1024]{1,0:T(8,128)S(1)}, f32[256,1024]{1,0:T(8,128)S(1)}) custom-call(bf16[256,1024]{1,0:T(8,128)(2,1)S(1)} %bitcast.21, bf16[256,1024]{1,0:T(8,128)(2,1)S(1)} %bitcast.12, bf16[256,1024]{1,0:T(8,128)(2,1)S(1)} %bitcast.16, bf16[256,1024]{1,0:T(8,128)(2,1)S(1)} %get-tuple-element.11.attn_ref, ...), custom_call_target="tpu_custom_call" | custom-call | flops 3221225472 | bytes 2097152 | tf_op jit(solution)/shard_map/partial/pallas_call | solution.py:193
  64.9 1.0 %copy-done.5 = f32[256,1024]{1,0:T(8,128)} copy-done((f32[256,1024]{1,0:T(8,128)}, f32[256,1024]{1,0:T(8,128)S(1)}, u32[]{:S(2)}) %copy-start.5) | copy-done | bytes 1048600
  65.9 1.0 %copy-done.7 = f32[256,1024]{1,0:T(8,128)} copy-done((f32[256,1024]{1,0:T(8,128)}, f32[256,1024]{1,0:T(8,128)S(1)}, u32[]{:S(2)}) %copy-start.7) | copy-done | bytes 1048600
  66.9 2.4 %all-to-all-done.3.state_ref = f32[8,136,128]{2,1,0:T(8,128)S(1)} async-done(((f32[8,136,128]{2,1,0:T(8,128)}), f32[8,136,128]{2,1,0:T(8,128)S(1)}, u32[]{:S(2)}, u32[]{:S(2)}) %all-to-all-start.3) | async-done | bytes 557088 | tf_op jit(solution)/shard_map/all_to_all | solution.py:162
  69.3 0.0 collective-permute-start.2
  69.4 1.2 %copy-done.6 = f32[256,1024]{1,0:T(8,128)S(1)} copy-done((f32[256,1024]{1,0:T(8,128)S(1)}, f32[256,1024]{1,0:T(8,128)}, u32[]{:S(2)}) %copy-start.6) | copy-done | bytes 1048600
  70.6 1.2 %copy-done.8 = f32[256,1024]{1,0:T(8,128)S(1)} copy-done((f32[256,1024]{1,0:T(8,128)S(1)}, f32[256,1024]{1,0:T(8,128)}, u32[]{:S(2)}) %copy-start.8) | copy-done | bytes 1048600
  71.8 2.1 %final.1 = (bf16[256,1024]{1,0:T(8,128)(2,1)}, bf16[256,1024]{1,0:T(8,128)(2,1)}) custom-call(bf16[256,1024]{1,0:T(8,128)(2,1)S(1)} %bitcast.13, bf16[256,1024]{1,0:T(8,128)(2,1)S(1)} %bitcast.17, f32[256,1024]{1,0:T(8,128)S(1)} %copy-done.6, f32[256,1024]{1,0:T(8,128)S(1)} %copy-done.8, f32[8,136,128]{2,1,0:T(8,128)S(1)} %all-to-all-done.3.state_ref), custom_call_target="tpu_custom_call" | custom-call | flops 1073741824 | bytes 2097152 | tf_op jit(solution)/shard_map/final/pallas_call | solution.py:204
  73.9 0.0 collective-permute-done.2
  73.9 0.6 multiply_bitcast_fusion
  (15 shorter events, 0.1 us)
Async XLA Ops:
  18.8 5.9 %collective-permute-start = (f32[128,128]{1,0:T(8,128)S(1)}, f32[128,128]{1,0:T(8,128)S(1)}, u32[]{:S(2)}, u32[]{:S(2)}) collective-permute-start(f32[128,128]{1,0:T(8,128)S(1)} %reduce_sum.18), channel_id=1, source_target_pairs={{0,16},{2,18},{4,20},{6,22},{8,24},{10,26},{12,28},{14,30},{16,0},... | collective-permute-start | bytes 196616 | tf_op jit(solution)/shard_map/ppermute | solution.py:148
  24.8 4.5 %copy-start.3 = (bf16[1,256,1024]{2,1,0:T(8,128)(2,1)S(1)}, bf16[1,256,1024]{2,1,0:T(8,128)(2,1)}, u32[]{:S(2)}) copy-start(bf16[1,256,1024]{2,1,0:T(8,128)(2,1)} %param.5) | copy-start | bytes 1572868
  25.6 3.6 %copy-start = (bf16[1,256,1024]{2,1,0:T(8,128)(2,1)S(1)}, bf16[1,256,1024]{2,1,0:T(8,128)(2,1)}, u32[]{:S(2)}) copy-start(bf16[1,256,1024]{2,1,0:T(8,128)(2,1)} %param.6) | copy-start | bytes 1572868
  25.6 3.7 %copy-start.1 = (bf16[1,256,1024]{2,1,0:T(8,128)(2,1)S(1)}, bf16[1,256,1024]{2,1,0:T(8,128)(2,1)}, u32[]{:S(2)}) copy-start(bf16[1,256,1024]{2,1,0:T(8,128)(2,1)} %param.7) | copy-start | bytes 1572868
  25.6 11.2 %all-to-all-start.1 = ((f32[8,128,128]{2,1,0:T(8,128)}), f32[8,128,128]{2,1,0:T(8,128)S(1)}, u32[]{:S(2)}, u32[]{:S(2)}) async-start(f32[8,128,128]{2,1,0:T(8,128)} %prefix.2), calls=%async_computation.1 | async-start | bytes 1048576 | tf_op jit(solution)/shard_map/all_to_all | solution.py:162
  29.3 7.6 %copy-start.2 = (bf16[1,256,1024]{2,1,0:T(8,128)(2,1)S(1)}, bf16[1,256,1024]{2,1,0:T(8,128)(2,1)}, u32[]{:S(2)}) copy-start(bf16[1,256,1024]{2,1,0:T(8,128)(2,1)} %param.9) | copy-start | bytes 1572868
  29.3 7.6 %copy-start.4 = (f32[1024]{0:T(1024)S(1)}, f32[1024]{0:T(1024)}, u32[]{:S(2)}) copy-start(f32[1024]{0:T(1024)} %param.8) | copy-start | bytes 12292
  30.2 1.0 %copy-start.9 = (f32[256,1024]{1,0:T(8,128)}, f32[256,1024]{1,0:T(8,128)S(1)}, u32[]{:S(2)}) copy-start(f32[256,1024]{1,0:T(8,128)S(1)} %inner.1.inner_ref) | copy-start | bytes 3145732
  36.9 1.2 %copy-start.10 = (f32[256,1024]{1,0:T(8,128)S(1)}, f32[256,1024]{1,0:T(8,128)}, u32[]{:S(2)}) copy-start(f32[256,1024]{1,0:T(8,128)} %copy-done.9) | copy-start | bytes 3145732
  51.1 6.1 %collective-permute-start.1 = (f32[136,128]{1,0:T(8,128)S(1)}, f32[136,128]{1,0:T(8,128)S(1)}, u32[]{:S(2)}, u32[]{:S(2)}) collective-permute-start(f32[136,128]{1,0:T(8,128)S(1)} %reduce_sum.19), channel_id=1, source_target_pairs={{0,16},{2,18},{4,20},{6,22},{8,24},{10,26},{12,28},{14,30},{16,0},... | collective-permute-start | bytes 208904 | tf_op jit(solution)/shard_map/ppermute | solution.py:148
  58.1 11.3 %all-to-all-start.3 = ((f32[8,136,128]{2,1,0:T(8,128)}), f32[8,136,128]{2,1,0:T(8,128)S(1)}, u32[]{:S(2)}, u32[]{:S(2)}) async-start(f32[8,136,128]{2,1,0:T(8,128)} %prefix.3), calls=%async_computation.3 | async-start | bytes 1114112 | tf_op jit(solution)/shard_map/all_to_all | solution.py:162
  64.9 1.0 %copy-start.5 = (f32[256,1024]{1,0:T(8,128)}, f32[256,1024]{1,0:T(8,128)S(1)}, u32[]{:S(2)}) copy-start(f32[256,1024]{1,0:T(8,128)S(1)} %get-tuple-element.13.key_part_ref) | copy-start | bytes 3145732
  65.9 1.0 %copy-start.7 = (f32[256,1024]{1,0:T(8,128)}, f32[256,1024]{1,0:T(8,128)S(1)}, u32[]{:S(2)}) copy-start(f32[256,1024]{1,0:T(8,128)S(1)} %get-tuple-element.14.value_part_ref) | copy-start | bytes 3145732
  69.3 4.5 %collective-permute-start.2 = (f32[8,128]{1,0:T(8,128)S(1)}, f32[8,128]{1,0:T(8,128)S(1)}, u32[]{:S(2)}, u32[]{:S(2)}) collective-permute-start(f32[8,128]{1,0:T(8,128)S(1)} %gain.1), channel_id=1, source_target_pairs={{0,1},{1,0},{2,3},{3,2},{4,5},{5,4},{6,7},{7,6},{8,9},{9,8},{10,11... | collective-permute-start | bytes 12296 | tf_op jit(solution)/shard_map/ppermute | solution.py:201
  69.3 1.2 %copy-start.6 = (f32[256,1024]{1,0:T(8,128)S(1)}, f32[256,1024]{1,0:T(8,128)}, u32[]{:S(2)}) copy-start(f32[256,1024]{1,0:T(8,128)} %copy-done.5) | copy-start | bytes 3145732
  70.6 1.2 %copy-start.8 = (f32[256,1024]{1,0:T(8,128)S(1)}, f32[256,1024]{1,0:T(8,128)}, u32[]{:S(2)}) copy-start(f32[256,1024]{1,0:T(8,128)} %copy-done.7) | copy-start | bytes 3145732

commit v8 on v7

--- a/solution.py
+++ b/solution.py
@@ -13,8 +13,8 @@
 BLOCK = 256
 GROUP = 8
 GAIN_ROWS = 8
-STEPS = 4
-STEP_HEADS = HEADS // STEPS
+PARTS = 2
+PART_ROWS = BLOCK // PARTS
 EPSILON = 1e-06
 
 NT = (((1,), (1,)), ((), ()))
@@ -37,21 +37,19 @@
 
 def delta_body(key_ref, value_ref, delta_ref, key_here, value_here, sems):
     copies = []
-    for head in range(HEADS):
-        at = columns(head)
-        copies.append(
-            [
-                pltpu.make_async_copy(source.at[:, at], here.at[:, at], sems.at[side, head])
-                for side, (source, here) in enumerate(((key_ref, key_here), (value_ref, value_here)))
-            ]
-        )
-        for copy in copies[-1]:
-            copy.start()
-    for head in range(HEADS):
-        at = columns(head)
-        for copy in copies[head]:
+    for part in range(PARTS):
+        rows = pl.ds(part * PART_ROWS, PART_ROWS)
+        for side, (source, here) in enumerate(((key_ref, key_here), (value_ref, value_here))):
+            copies.append(pltpu.make_async_copy(source.at[rows], here.at[rows], sems.at[part, side]))
+            copies[-1].start()
+    for part in range(PARTS):
+        rows = pl.ds(part * PART_ROWS, PART_ROWS)
+        for copy in copies[2 * part : 2 * part + 2]:
             copy.wait()
-        delta_ref[head] = dot(key_here[:, at], value_here[:, at], TN)
+        for head in range(HEADS):
+            at = columns(head)
+            delta = dot(key_here[rows, at], value_here[rows, at], TN)
+            delta_ref[head] = delta if part == 0 else delta_ref[head] + delta
 
 
 def inner_body(query_ref, key_ref, value_ref, inner_ref):
@@ -95,14 +93,12 @@
 
 
 def final_body(key_ref, value_ref, key_part_ref, value_part_ref, state_ref, grad_key_ref, grad_value_ref):
-    step = pl.program_id(0)
-    for head in range(STEP_HEADS):
-        whole_head = step * STEP_HEADS + head
-        wide = pl.ds(pl.multiple_of(whole_head * DH, DH), DH)
-        at = columns(head)
-        state = state_ref[whole_head, :DH].astype(jnp.bfloat16)
-        grad_key_ref[:, at] = (key_part_ref[:, wide] + dot(value_ref[:, wide], state, NT)).astype(jnp.bfloat16)
-        grad_value_ref[:, at] = (value_part_ref[:, wide] + dot(key_ref[:, wide], state, NN)).astype(jnp.bfloat16)
+    rows = pl.ds(pl.multiple_of(pl.program_id(0) * PART_ROWS, PART_ROWS), PART_ROWS)
+    for head in range(HEADS):
+        at = columns(head)
+        state = state_ref[head, :DH].astype(jnp.bfloat16)
+        grad_key_ref[:, at] = (key_part_ref[rows, at] + dot(value_ref[rows, at], state, NT)).astype(jnp.bfloat16)
+        grad_value_ref[:, at] = (value_part_ref[rows, at] + dot(key_ref[rows, at], state, NN)).astype(jnp.bfloat16)
 
 
 def gain_body(state_ref, gain_ref):
@@ -137,10 +133,12 @@
     )
 
 
-def carried_in(parts, reverse):
+def carried_in(parts, reverse, beside, operands):
     count, place = lax.axis_size("seq"), lax.axis_index("seq")
     teams = [list(range(first, first + GROUP)) for first in range(0, count, GROUP)]
     held = lax.all_to_all(parts, "seq", 0, 0, axis_index_groups=teams)
+    held, *operands = lax.optimization_barrier((held, *operands))
+    aside = beside(*operands)
     total = jnp.sum(held, axis=0)
     carried = jnp.zeros_like(total)
     mask = GROUP
@@ -159,7 +157,8 @@
         1 << 24,
         "prefix",
     )(carried, total, held)
-    return lax.all_to_all(back, "seq", 0, 0, axis_index_groups=teams)
+    back, aside = lax.optimization_barrier((back, aside))
+    return lax.all_to_all(back, "seq", 0, 0, axis_index_groups=teams), aside
 
 
 def local(queries, keys, values, out_gain, grad_out):
@@ -182,17 +181,18 @@
         plain,
         6 * unit,
         "delta",
-        scratch=[pltpu.VMEM(flat, jnp.bfloat16)] * 2 + [pltpu.SemaphoreType.DMA((2, HEADS))],
+        scratch=[pltpu.VMEM(flat, jnp.bfloat16)] * 2 + [pltpu.SemaphoreType.DMA((PARTS, 2))],
     )(*[pltpu.with_memory_space_constraint(a, pltpu.HBM) for a in (key, value)])
-    states = carried_in(delta, False)
-    inner = call(inner_body, [wide] * 3, wide, full_float, 16 * unit, "inner")(query, key, value)
+    inner_call = call(inner_body, [wide] * 3, wide, full_float, 16 * unit, "inner")
+    states, inner = carried_in(delta, False, inner_call, (query, key, value))
     attn, delta = call(
         norm_body, [wide, wide, wide, whole(1, HEADS * DH), short], [wide, tall], [full_low, taller], 16 * unit, "norm"
     )(query, grad, inner, gain, states)
-    later = carried_in(delta, True)
-    grad_query, key_part, value_part = call(
+    partial_call = call(
         partial_body, [wide] * 4 + [short], [wide] * 3, [full_low, full_float, full_float], 48 * unit, "partial"
-    )(query, key, value, attn, states)
+    )
+    later, parts = carried_in(delta, True, partial_call, (query, key, value, attn, states))
+    grad_query, key_part, value_part = parts
     gain_terms = call(
         gain_body, [tall], whole(HEADS, DH), jax.ShapeDtypeStruct((HEADS, DH), jnp.float32), unit, "gain"
     )(later)
@@ -200,9 +200,9 @@
     while mask < docs:
         gain_terms = gain_terms + lax.ppermute(gain_terms, "dp", [(d, d ^ mask) for d in range(docs)])
         mask *= 2
-    chunk = pl.BlockSpec((BLOCK, STEP_HEADS * DH), lambda step: (0, step))
+    chunk = pl.BlockSpec((PART_ROWS, HEADS * DH), lambda step: (step, 0))
     grad_key, grad_value = call(
-        final_body, [wide] * 4 + [tall], [chunk] * 2, [full_low] * 2, 16 * unit, "final", steps=STEPS
+        final_body, [wide] * 4 + [tall], [chunk] * 2, [full_low] * 2, 16 * unit, "final", steps=PARTS
     )(key, value, key_part, value_part, later)
     grad_gain = gain_terms / math.sqrt(lax.axis_size("seq") * docs * BLOCK)
     return (

time: 75 us -> 70.2 us (0.936)
  local copies, waits for them, and re-layouts: 6.66 us -> 0.03 us
  starting transfers between devices: 11.2 us -> 16.9 us
  blocking collectives: 27 us -> 22.5 us
  waiting for transfers between devices: 16 us -> 18.5 us
  Pallas kernels: 12.1 us -> 10.4 us
    all_to_all x2, waiting for transfers between devices: 8.05 us -> 16.8 us  [carried_in(): held = lax.all_to_all(parts, 'seq', 0, 0, axis_index_groups=teams)]
    unnamed x22 -> x10, local copies, waits for them, and re-layouts: 6.66 us -> 0.03 us
    ppermute x2, waiting for transfers between devices: 7.96 us -> 1.64 us  [carried_in(): arrived = lax.ppermute(total, 'seq', [(s, s ^ mask) for s in range(count)])]
    all_to_all x2, blocking collectives: 27 us -> 22.5 us  [carried_in(): return (lax.all_to_all(back, 'seq', 0, 0, axis_index_groups=teams), aside)]
    ppermute x2, starting transfers between devices: 4.05 us -> 7.05 us  [carried_in(): arrived = lax.ppermute(total, 'seq', [(s, s ^ mask) for s in range(count)])]
    all_to_all x2, starting transfers between devices: 7.16 us -> 9.86 us  [carried_in(): held = lax.all_to_all(parts, 'seq', 0, 0, axis_index_groups=teams)]
    pallas_call x2, Pallas kernels: 1.68 us -> 0.08 us  [carried_in(): call(functools.partial(prefix_body, reverse), [single, single, stacked],...]
    pallas_call x1, Pallas kernels: 1.33 us -> 2.16 us  [local(): call(norm_body, [wide, wide, wide, whole(1, HEADS * DH), short], [wide, t...]
  transfers between devices with their start and end apart: 5 -> 5, of which waited for: 4 -> 3; matrix products, arithmetic and copies ran while one was open for 0% -> 0% of each run, Pallas kernels for 9% -> 8%
where the time goes in v8:
time: 70.2 us; the launch traced here: 69.8 us
  blocking collectives  22.5 us (32%)
  waiting for transfers between devices  18.5 us (26%)
  starting transfers between devices  16.9 us (24%)
  Pallas kernels  10.4 us (15%)
  between operations  0.74 us (1%)
    all_to_all x2, blocking collectives, carried_in(): return (lax.all_to_all(back, 'seq', 0, 0, axis_index_groups=teams), aside)  22.5 us
    all_to_all x2, waiting for transfers between devices, carried_in(): held = lax.all_to_all(parts, 'seq', 0, 0, axis_index_groups=teams)  16.8 us
    all_to_all x2, starting transfers between devices, carried_in(): held = lax.all_to_all(parts, 'seq', 0, 0, axis_index_groups=teams)  9.86 us
    ppermute x2, starting transfers between devices, carried_in(): arrived = lax.ppermute(total, 'seq', [(s, s ^ mask) for s in range(count)])  7.05 us
    pallas_call x2, Pallas kernels, carried_in(): aside = beside(*operands)  4.27 us
    pallas_call x1, Pallas kernels, local(): call(delta_body, [pl.BlockSpec(memory_space=pltpu.HBM)] * 2, short, plain...  2.28 us
    pallas_call x1, Pallas kernels, local(): call(norm_body, [wide, wide, wide, whole(1, HEADS * DH), short], [wide, t...  2.16 us
    ppermute x2, waiting for transfers between devices, carried_in(): arrived = lax.ppermute(total, 'seq', [(s, s ^ mask) for s in range(count)])  1.64 us
  transfers between devices with their start and end apart: 5, of which 3 were waited for; matrix products, arithmetic and copies ran while one was open for 0% of the time, Pallas kernels for 8%

profile of v8, /device:TPU:0, one launch (start us, length us, event | category | flops | bytes accessed | tf_op | source)
XLA Modules:
  0.0 69.8 jit_solution(10289642624812269348)
XLA Ops:
  0.6 2.3 %delta.1 = f32[8,128,128]{2,1,0:T(8,128)} custom-call(bf16[256,1024]{1,0:T(8,128)(2,1)} %bitcast.10, bf16[256,1024]{1,0:T(8,128)(2,1)} %bitcast.14), custom_call_target="tpu_custom_call" | custom-call | flops 402653184 | bytes 2097152 | tf_op jit(solution)/shard_map/delta/pallas_call | solution.py:177
  2.9 0.0 copy-start.1
  2.9 0.0 copy-start.3
  2.9 6.3 %all-to-all-start = ((f32[8,128,128]{2,1,0:T(8,128)}), f32[8,128,128]{2,1,0:T(8,128)S(1)}, u32[]{:S(2)}, u32[]{:S(2)}) async-start(f32[8,128,128]{2,1,0:T(8,128)} %delta.1), calls=%async_computation | async-start | bytes 1048576 | tf_op jit(solution)/shard_map/all_to_all | solution.py:139
  9.3 0.0 copy-start
  9.3 9.1 %all-to-all-done.held_ref = f32[8,128,128]{2,1,0:T(8,128)S(1)} async-done(((f32[8,128,128]{2,1,0:T(8,128)}), f32[8,128,128]{2,1,0:T(8,128)S(1)}, u32[]{:S(2)}, u32[]{:S(2)}) %all-to-all-start) | async-done | bytes 524320 | tf_op jit(solution)/shard_map/all_to_all | solution.py:139
  18.4 2.7 %collective-permute-start = (f32[128,128]{1,0:T(8,128)S(1)}, f32[128,128]{1,0:T(8,128)S(1)}, u32[]{:S(2)}, u32[]{:S(2)}) collective-permute-start(f32[128,128]{1,0:T(8,128)S(1)} %reduce_sum.18), channel_id=1, source_target_pairs={{0,16},{2,18},{4,20},{6,22},{8,24},{10,26},{12,28},{14,30},{16,0},... | collective-permute-start | bytes 196616 | tf_op jit(solution)/shard_map/ppermute | solution.py:146
  21.1 0.0 copy-done.1
  21.1 0.0 copy-done.3
  21.1 0.0 copy-done
  21.1 0.9 %inner.1.inner_ref = f32[256,1024]{1,0:T(8,128)S(1)} custom-call(bf16[256,1024]{1,0:T(8,128)(2,1)S(1)} %bitcast.19, bf16[256,1024]{1,0:T(8,128)(2,1)S(1)} %bitcast.11, bf16[256,1024]{1,0:T(8,128)(2,1)S(1)} %bitcast.15), custom_call_target="tpu_custom_call" | custom-call | flops 1073741824 | bytes 2097152 | tf_op jit(solution)/shard_map/inner/pallas_call | solution.py:141
  22.0 1.6 %collective-permute-done = f32[128,128]{1,0:T(8,128)S(1)} collective-permute-done((f32[128,128]{1,0:T(8,128)S(1)}, f32[128,128]{1,0:T(8,128)S(1)}, u32[]{:S(2)}, u32[]{:S(2)}) %collective-permute-start) | collective-permute-done | bytes 65568 | tf_op jit(solution)/shard_map/ppermute | solution.py:146
  23.7 0.0 copy-start.2
  23.7 0.0 copy-start.4
  23.7 11.2 %all_to_all.20.state_ref = f32[8,128,128]{2,1,0:T(8,128)S(1)} all-to-all(f32[8,128,128]{2,1,0:T(8,128)S(1)} %prefix.2), channel_id=1, replica_groups={{0,2,4,6,8,10,12,14},{16,18,20,22,24,26,28,30},{1,3,5,7,9,11,13,15},{17..., dimensions={0} | all-to-all | bytes 1048576 | tf_op jit(solution)/shard_map/all_to_all | solution.py:161
  34.9 0.0 copy-done.2
  34.9 0.0 copy-done.4
  34.9 2.2 %norm.1 = (bf16[256,1024]{1,0:T(8,128)(2,1)S(1)}, f32[8,136,128]{2,1,0:T(8,128)}) custom-call(bf16[256,1024]{1,0:T(8,128)(2,1)S(1)} %bitcast.20, bf16[256,1024]{1,0:T(8,128)(2,1)S(1)} %bitcast.18, f32[256,1024]{1,0:T(8,128)S(1)} %inner.1.inner_ref, f32[1,1024]{1,0:T(1,128)S(1)} %bitcast.22, f32[8,128,128]{2,1,0:T(8,128)S(1)} %all_to_all.20.state_ref), custom_call_target="tpu_custom_call" | custom-call | flops 1073741824 | bytes 2097152 | tf_op jit(solution)/shard_map/norm/pallas_call | solution.py:188
  37.1 3.5 %all-to-all-start.2 = ((f32[8,136,128]{2,1,0:T(8,128)}), f32[8,136,128]{2,1,0:T(8,128)S(1)}, u32[]{:S(2)}, u32[]{:S(2)}) async-start(f32[8,136,128]{2,1,0:T(8,128)} %get-tuple-element.33), calls=%async_computation.2 | async-start | bytes 1114112 | tf_op jit(solution)/shard_map/all_to_all | solution.py:139
  40.6 7.7 %all-to-all-done.2.held_ref = f32[8,136,128]{2,1,0:T(8,128)S(1)} async-done(((f32[8,136,128]{2,1,0:T(8,128)}), f32[8,136,128]{2,1,0:T(8,128)S(1)}, u32[]{:S(2)}, u32[]{:S(2)}) %all-to-all-start.2) | async-done | bytes 557088 | tf_op jit(solution)/shard_map/all_to_all | solution.py:139
  48.4 4.4 %collective-permute-start.1 = (f32[136,128]{1,0:T(8,128)S(1)}, f32[136,128]{1,0:T(8,128)S(1)}, u32[]{:S(2)}, u32[]{:S(2)}) collective-permute-start(f32[136,128]{1,0:T(8,128)S(1)} %reduce_sum.19), channel_id=1, source_target_pairs={{0,16},{2,18},{4,20},{6,22},{8,24},{10,26},{12,28},{14,30},{16,0},... | collective-permute-start | bytes 208904 | tf_op jit(solution)/shard_map/ppermute | solution.py:146
  52.8 3.3 %partial.1 = (bf16[256,1024]{1,0:T(8,128)(2,1)}, f32[256,1024]{1,0:T(8,128)S(1)}, f32[256,1024]{1,0:T(8,128)S(1)}) custom-call(bf16[256,1024]{1,0:T(8,128)(2,1)S(1)} %bitcast.21, bf16[256,1024]{1,0:T(8,128)(2,1)S(1)} %bitcast.12, bf16[256,1024]{1,0:T(8,128)(2,1)S(1)} %bitcast.16, bf16[256,1024]{1,0:T(8,128)(2,1)S(1)} %get-tuple-element.39.attn_ref, ...), custom_call_target="tpu_custom_call" | custom-call | flops 3221225472 | bytes 2097152 | tf_op jit(solution)/shard_map/partial/pallas_call | solution.py:141
  56.2 0.0 collective-permute-done.1
  56.2 11.3 %all_to_all.21.state_ref = f32[8,136,128]{2,1,0:T(8,128)S(1)} all-to-all(f32[8,136,128]{2,1,0:T(8,128)S(1)} %prefix.3), channel_id=1, replica_groups={{0,2,4,6,8,10,12,14},{16,18,20,22,24,26,28,30},{1,3,5,7,9,11,13,15},{17..., dimensions={0} | all-to-all | bytes 1114112 | tf_op jit(solution)/shard_map/all_to_all | solution.py:161
  67.6 0.0 collective-permute-start.2
  67.6 1.6 %final.1 = (bf16[256,1024]{1,0:T(8,128)(2,1)}, bf16[256,1024]{1,0:T(8,128)(2,1)}) custom-call(bf16[256,1024]{1,0:T(8,128)(2,1)S(1)} %bitcast.13, bf16[256,1024]{1,0:T(8,128)(2,1)S(1)} %bitcast.17, f32[256,1024]{1,0:T(8,128)S(1)} %get-tuple-element.45.key_part_ref, f32[256,1024]{1,0:T(8,128)S(1)} %get-tuple-element.46.value_part_ref, ...), custom_call_target="tpu_custom_call" | custom-call | flops 1073741824 | bytes 2097152 | tf_op jit(solution)/shard_map/final/pallas_call | solution.py:204
  69.1 0.0 collective-permute-done.2
  69.2 0.6 multiply_bitcast_fusion
  (7 shorter events, 0.2 us)
Async XLA Ops:
  2.9 18.2 %copy-start.1 = (bf16[1,256,1024]{2,1,0:T(8,128)(2,1)S(1)}, bf16[1,256,1024]{2,1,0:T(8,128)(2,1)}, u32[]{:S(2)}) copy-start(bf16[1,256,1024]{2,1,0:T(8,128)(2,1)} %param.7) | copy-start | bytes 1572868
  2.9 18.1 %copy-start.3 = (bf16[1,256,1024]{2,1,0:T(8,128)(2,1)S(1)}, bf16[1,256,1024]{2,1,0:T(8,128)(2,1)}, u32[]{:S(2)}) copy-start(bf16[1,256,1024]{2,1,0:T(8,128)(2,1)} %param.5) | copy-start | bytes 1572868
  2.9 15.4 %all-to-all-start = ((f32[8,128,128]{2,1,0:T(8,128)}), f32[8,128,128]{2,1,0:T(8,128)S(1)}, u32[]{:S(2)}, u32[]{:S(2)}) async-start(f32[8,128,128]{2,1,0:T(8,128)} %delta.1), calls=%async_computation | async-start | bytes 1048576 | tf_op jit(solution)/shard_map/all_to_all | solution.py:139
  9.3 11.8 %copy-start = (bf16[1,256,1024]{2,1,0:T(8,128)(2,1)S(1)}, bf16[1,256,1024]{2,1,0:T(8,128)(2,1)}, u32[]{:S(2)}) copy-start(bf16[1,256,1024]{2,1,0:T(8,128)(2,1)} %param.6) | copy-start | bytes 1572868
  18.4 5.2 %collective-permute-start = (f32[128,128]{1,0:T(8,128)S(1)}, f32[128,128]{1,0:T(8,128)S(1)}, u32[]{:S(2)}, u32[]{:S(2)}) collective-permute-start(f32[128,128]{1,0:T(8,128)S(1)} %reduce_sum.18), channel_id=1, source_target_pairs={{0,16},{2,18},{4,20},{6,22},{8,24},{10,26},{12,28},{14,30},{16,0},... | collective-permute-start | bytes 196616 | tf_op jit(solution)/shard_map/ppermute | solution.py:146
  23.7 11.2 %copy-start.2 = (bf16[1,256,1024]{2,1,0:T(8,128)(2,1)S(1)}, bf16[1,256,1024]{2,1,0:T(8,128)(2,1)}, u32[]{:S(2)}) copy-start(bf16[1,256,1024]{2,1,0:T(8,128)(2,1)} %param.9) | copy-start | bytes 1572868
  23.7 11.2 %copy-start.4 = (f32[1024]{0:T(1024)S(1)}, f32[1024]{0:T(1024)}, u32[]{:S(2)}) copy-start(f32[1024]{0:T(1024)} %param.8) | copy-start | bytes 12292
  37.1 11.3 %all-to-all-start.2 = ((f32[8,136,128]{2,1,0:T(8,128)}), f32[8,136,128]{2,1,0:T(8,128)S(1)}, u32[]{:S(2)}, u32[]{:S(2)}) async-start(f32[8,136,128]{2,1,0:T(8,128)} %get-tuple-element.33), calls=%async_computation.2 | async-start | bytes 1114112 | tf_op jit(solution)/shard_map/all_to_all | solution.py:139
  48.4 7.7 %collective-permute-start.1 = (f32[136,128]{1,0:T(8,128)S(1)}, f32[136,128]{1,0:T(8,128)S(1)}, u32[]{:S(2)}, u32[]{:S(2)}) collective-permute-start(f32[136,128]{1,0:T(8,128)S(1)} %reduce_sum.19), channel_id=1, source_target_pairs={{0,16},{2,18},{4,20},{6,22},{8,24},{10,26},{12,28},{14,30},{16,0},... | collective-permute-start | bytes 208904 | tf_op jit(solution)/shard_map/ppermute | solution.py:146
  67.6 1.6 %collective-permute-start.2 = (f32[8,128]{1,0:T(8,128)S(1)}, f32[8,128]{1,0:T(8,128)S(1)}, u32[]{:S(2)}, u32[]{:S(2)}) collective-permute-start(f32[8,128]{1,0:T(8,128)S(1)} %gain.1), channel_id=1, source_target_pairs={{0,1},{1,0},{2,3},{3,2},{4,5},{5,4},{6,7},{7,6},{8,9},{9,8},{10,11... | collective-permute-start | bytes 12296 | tf_op jit(solution)/shard_map/ppermute | solution.py:201

commit v9 on v8

--- a/solution.py
+++ b/solution.py
@@ -30,12 +30,12 @@
     return pl.ds(head * DH, DH)
 
 
-def causal():
-    shape = (BLOCK, BLOCK)
-    return lax.broadcasted_iota(jnp.int32, shape, 0) >= lax.broadcasted_iota(jnp.int32, shape, 1)
-
-
-def delta_body(key_ref, value_ref, delta_ref, key_here, value_here, sems):
+def causal(turned=False):
+    shape, first = (BLOCK, BLOCK), int(turned)
+    return lax.broadcasted_iota(jnp.int32, shape, first) >= lax.broadcasted_iota(jnp.int32, shape, 1 - first)
+
+
+def delta_body(flags_ref, key_ref, value_ref, delta_ref, key_here, value_here, sems):
     copies = []
     for part in range(PARTS):
         rows = pl.ds(part * PART_ROWS, PART_ROWS)
@@ -52,13 +52,14 @@
             delta_ref[head] = delta if part == 0 else delta_ref[head] + delta
 
 
-def inner_body(query_ref, key_ref, value_ref, inner_ref):
-    keep = causal()
-    for head in range(HEADS):
-        at = columns(head)
-        raw = dot(query_ref[:, at], key_ref[:, at], NT)
-        scores = jnp.where(keep, raw, 0.0).astype(jnp.bfloat16)
+def inner_body(query_ref, key_ref, value_ref, inner_ref, turned_ref):
+    keep, kept = causal(), causal(True)
+    for head in range(HEADS):
+        at = columns(head)
+        query, key = query_ref[:, at], key_ref[:, at]
+        scores = jnp.where(keep, dot(query, key, NT), 0.0).astype(jnp.bfloat16)
         inner_ref[:, at] = dot(scores, value_ref[:, at], NN)
+        turned_ref[head] = jnp.where(kept, dot(key, query, NT), 0.0).astype(jnp.bfloat16)
 
 
 def norm_body(query_ref, grad_ref, inner_ref, gain_ref, state_ref, attn_ref, delta_ref):
@@ -79,17 +80,19 @@
         delta_ref[head, DH:] = jnp.broadcast_to(terms, (GAIN_ROWS, DH))
 
 
-def partial_body(query_ref, key_ref, value_ref, attn_ref, state_ref, grad_query_ref, key_part_ref, value_part_ref):
-    keep = causal()
-    for head in range(HEADS):
-        at = columns(head)
-        query, key, value, grad_attn = query_ref[:, at], key_ref[:, at], value_ref[:, at], attn_ref[:, at]
-        scores = jnp.where(keep, dot(query, key, NT), 0.0).astype(jnp.bfloat16)
+def partial_body(
+    query_ref, key_ref, value_ref, turned_ref, attn_ref, state_ref, grad_query_ref, key_part_ref, value_part_ref
+):
+    keep, kept = causal(), causal(True)
+    for head in range(HEADS):
+        at = columns(head)
+        key, value, grad_attn = key_ref[:, at], value_ref[:, at], attn_ref[:, at]
         grad_scores = jnp.where(keep, dot(grad_attn, value, NT), 0.0).astype(jnp.bfloat16)
+        turned_grad = jnp.where(kept, dot(value, grad_attn, NT), 0.0).astype(jnp.bfloat16)
         carried = dot(grad_attn, state_ref[head].astype(jnp.bfloat16), NT)
         grad_query_ref[:, at] = (dot(grad_scores, key, NN) + carried).astype(jnp.bfloat16)
-        key_part_ref[:, at] = dot(grad_scores, query, TN)
-        value_part_ref[:, at] = dot(scores, grad_attn, TN)
+        key_part_ref[:, at] = dot(turned_grad, query_ref[:, at], NN)
+        value_part_ref[:, at] = dot(turned_ref[head], grad_attn, NN)
 
 
 def final_body(key_ref, value_ref, key_part_ref, value_part_ref, state_ref, grad_key_ref, grad_value_ref):
@@ -106,8 +109,12 @@
         gain_ref[head : head + 1, :] = state_ref[head, DH : DH + 1]
 
 
-def prefix_body(reverse, carried_ref, total_ref, held_ref, back_ref):
-    running = carried_ref[:DH]
+def prefix_body(reverse, flags_ref, *refs):
+    *arrived_refs, total_ref, held_ref, back_ref = refs
+    running = jnp.zeros((DH, DH), jnp.float32)
+    for step, arrived_ref in enumerate(arrived_refs):
+        later = (flags_ref[step] != 0) != reverse
+        running = running + jnp.where(later, arrived_ref[:DH], 0.0)
     for member in reversed(range(GROUP)) if reverse else range(GROUP):
         back_ref[member, :DH] = running
         running = running + held_ref[member, :DH]
@@ -117,6 +124,9 @@
 
 def whole(*shape):
     return pl.BlockSpec(shape, lambda step: (0,) * len(shape))
+
+
+FLAGS = pl.BlockSpec(memory_space=pltpu.SMEM)
 
 
 def call(body, in_specs, out_specs, outs, flops, name, steps=1, scratch=()):
@@ -133,30 +143,33 @@
     )
 
 
-def carried_in(parts, reverse, beside, operands):
-    count, place = lax.axis_size("seq"), lax.axis_index("seq")
+def exchange_masks():
+    masks = [GROUP]
+    while masks[-1] * 2 < lax.axis_size("seq"):
+        masks.append(masks[-1] * 2)
+    return masks if lax.axis_size("seq") > GROUP else []
+
+
+def carried_in(parts, reverse, flags, beside, operands):
+    count = lax.axis_size("seq")
     teams = [list(range(first, first + GROUP)) for first in range(0, count, GROUP)]
     held = lax.all_to_all(parts, "seq", 0, 0, axis_index_groups=teams)
     held, *operands = lax.optimization_barrier((held, *operands))
     aside = beside(*operands)
     total = jnp.sum(held, axis=0)
-    carried = jnp.zeros_like(total)
-    mask = GROUP
-    while mask < count:
-        arrived = lax.ppermute(total, "seq", [(s, s ^ mask) for s in range(count)])
-        later = ((place & mask) != 0) != reverse
-        carried = carried + jnp.where(later, arrived, 0.0)
-        total = total + arrived
-        mask *= 2
+    arrived = []
+    for mask in exchange_masks():
+        arrived.append(lax.ppermute(total, "seq", [(s, s ^ mask) for s in range(count)]))
+        total = total + arrived[-1]
     single, stacked = whole(*total.shape), whole(*held.shape)
     back = call(
         functools.partial(prefix_body, reverse),
-        [single, single, stacked],
+        [FLAGS] + [single] * (len(arrived) + 1) + [stacked],
         stacked,
         jax.ShapeDtypeStruct(held.shape, jnp.float32),
         1 << 24,
         "prefix",
-    )(carried, total, held)
+    )(flags, *arrived, total, held)
     back, aside = lax.optimization_barrier((back, aside))
     return lax.all_to_all(back, "seq", 0, 0, axis_index_groups=teams), aside
 
@@ -174,24 +187,27 @@
     short, tall, wide = whole(*plain.shape), whole(*taller.shape), whole(*flat)
     unit = 2 * BLOCK * DH * DH * HEADS
 
+    place = lax.axis_index("seq")
+    flags = jnp.stack([place & mask for mask in exchange_masks()] or [place]).astype(jnp.int32)
     delta = call(
         delta_body,
-        [pl.BlockSpec(memory_space=pltpu.HBM)] * 2,
+        [FLAGS] + [pl.BlockSpec(memory_space=pltpu.HBM)] * 2,
         short,
         plain,
         6 * unit,
         "delta",
         scratch=[pltpu.VMEM(flat, jnp.bfloat16)] * 2 + [pltpu.SemaphoreType.DMA((PARTS, 2))],
-    )(*[pltpu.with_memory_space_constraint(a, pltpu.HBM) for a in (key, value)])
-    inner_call = call(inner_body, [wide] * 3, wide, full_float, 16 * unit, "inner")
-    states, inner = carried_in(delta, False, inner_call, (query, key, value))
+    )(flags, *[pltpu.with_memory_space_constraint(a, pltpu.HBM) for a in (key, value)])
+    square = jax.ShapeDtypeStruct((HEADS, BLOCK, BLOCK), jnp.bfloat16)
+    inner_call = call(inner_body, [wide] * 3, [wide, whole(*square.shape)], [full_float, square], 16 * unit, "inner")
+    states, (inner, turned) = carried_in(delta, False, flags, inner_call, (query, key, value))
     attn, delta = call(
         norm_body, [wide, wide, wide, whole(1, HEADS * DH), short], [wide, tall], [full_low, taller], 16 * unit, "norm"
     )(query, grad, inner, gain, states)
     partial_call = call(
-        partial_body, [wide] * 4 + [short], [wide] * 3, [full_low, full_float, full_float], 48 * unit, "partial"
-    )
-    later, parts = carried_in(delta, True, partial_call, (query, key, value, attn, states))
+        partial_body, [wide] * 3 + [whole(*square.shape), wide, short], [wide] * 3, [full_low, full_float, full_float], 48 * unit, "partial"
+    )
+    later, parts = carried_in(delta, True, flags, partial_call, (query, key, value, turned, attn, states))
     grad_query, key_part, value_part = parts
     gain_terms = call(
         gain_body, [tall], whole(HEADS, DH), jax.ShapeDtypeStruct((HEADS, DH), jnp.float32), unit, "gain"

time: 70.2 us -> 67 us (0.954)
  blocking collectives: 22.5 us -> 48.6 us
  waiting for transfers between devices: 18.5 us -> 1.66 us
  starting transfers between devices: 16.9 us -> 4.86 us
  Pallas kernels: 10.4 us -> 8.79 us
  local copies, waits for them, and re-layouts: 0.03 us -> 1.26 us
    all_to_all x0 -> x2, blocking collectives: none -> 27.2 us  [carried_in(): held = lax.all_to_all(parts, 'seq', 0, 0, axis_index_groups=teams)]
    all_to_all x2 -> x0, waiting for transfers between devices: 16.8 us -> none  [carried_in(): held = lax.all_to_all(parts, 'seq', 0, 0, axis_index_groups=teams)]
    all_to_all x2 -> x0, starting transfers between devices: 9.86 us -> none  [carried_in(): held = lax.all_to_all(parts, 'seq', 0, 0, axis_index_groups=teams)]
    ppermute x2, starting transfers between devices: 7.05 us -> 4.86 us  [carried_in(): lax.ppermute(total, 'seq', [(s, s ^ mask) for s in range(count)])]
    unnamed x10 -> x14, local copies, waits for them, and re-layouts: 0.03 us -> 1.26 us
    all_to_all x2, blocking collectives: 22.5 us -> 21.5 us  [carried_in(): return (lax.all_to_all(back, 'seq', 0, 0, axis_index_groups=teams), aside)]
    pallas_call x1, Pallas kernels: 2.16 us -> 1.35 us  [local(): call(norm_body, [wide, wide, wide, whole(1, HEADS * DH), short], [wide, t...]
    pallas_call x3, Pallas kernels: 2.35 us -> 1.58 us  [the longest x1 1.49 us: local(): call(delta_body, [FLAGS] + [pl.BlockSpec(memory_space=pltpu.HBM)] * 2, sh...]
  transfers between devices with their start and end apart: 5 -> 3, of which waited for: 3 -> 1; matrix products, arithmetic and copies ran while one was open for 0% -> 0% of each run, Pallas kernels for 8% -> 9%
where the time goes in v9:
time: 67 us; the launch traced here: 66.6 us
  blocking collectives  48.6 us (73%)
  Pallas kernels  8.79 us (13%)
  starting transfers between devices  4.86 us (7%)
  waiting for transfers between devices  1.66 us (2%)
  local copies, waits for them, and re-layouts  1.26 us (2%)
  between operations  0.74 us (1%)
  other arithmetic  0.68 us (1%)
    all_to_all x2, blocking collectives, carried_in(): held = lax.all_to_all(parts, 'seq', 0, 0, axis_index_groups=teams)  27.2 us
    all_to_all x2, blocking collectives, carried_in(): return (lax.all_to_all(back, 'seq', 0, 0, axis_index_groups=teams), aside)  21.5 us
    ppermute x2, starting transfers between devices, carried_in(): lax.ppermute(total, 'seq', [(s, s ^ mask) for s in range(count)])  4.86 us
    pallas_call x2, Pallas kernels, carried_in(): aside = beside(*operands)  4.31 us
    ppermute x2, waiting for transfers between devices, carried_in(): lax.ppermute(total, 'seq', [(s, s ^ mask) for s in range(count)])  1.66 us
    pallas_call x1, Pallas kernels, local(): call(final_body, [wide] * 4 + [tall], [chunk] * 2, [full_low] * 2, 16 * u...  1.55 us
    pallas_call x1, Pallas kernels, local(): call(delta_body, [FLAGS] + [pl.BlockSpec(memory_space=pltpu.HBM)] * 2, sh...  1.49 us
    pallas_call x1, Pallas kernels, local(): call(norm_body, [wide, wide, wide, whole(1, HEADS * DH), short], [wide, t...  1.35 us
  transfers between devices with their start and end apart: 3, of which 1 were waited for; matrix products, arithmetic and copies ran while one was open for 0% of the time, Pallas kernels for 9%

profile of v9, /device:TPU:0, one launch (start us, length us, event | category | flops | bytes accessed | tf_op | source)
XLA Modules:
  0.0 66.6 jit_solution(7119071542994896963)
XLA Ops:
  0.6 1.5 %delta.1 = f32[8,128,128]{2,1,0:T(8,128)S(1)} custom-call(s32[1]{0:T(128)} %bitcast.flags_ref, bf16[256,1024]{1,0:T(8,128)(2,1)} %bitcast.11, bf16[256,1024]{1,0:T(8,128)(2,1)} %bitcast.15), custom_call_target="tpu_custom_call" | custom-call | flops 402653184 | bytes 2097152 | tf_op jit(solution)/shard_map/delta/pallas_call | solution.py:192
  2.1 0.0 copy-start.1
  2.1 0.0 copy-start.3
  2.2 15.5 %all_to_all.20.refs_2_ = f32[8,128,128]{2,1,0:T(8,128)S(1)} all-to-all(f32[8,128,128]{2,1,0:T(8,128)S(1)} %delta.1), channel_id=1, replica_groups={{0,2,4,6,8,10,12,14},{16,18,20,22,24,26,28,30},{1,3,5,7,9,11,13,15},{17..., dimensions={0} | all-to-all | bytes 1048576 | tf_op jit(solution)/shard_map/all_to_all | solution.py:156
  17.7 0.0 copy-start
  17.7 2.7 %collective-permute-start = (f32[128,128]{1,0:T(8,128)S(1)}, f32[128,128]{1,0:T(8,128)S(1)}, u32[]{:S(2)}, u32[]{:S(2)}) collective-permute-start(f32[128,128]{1,0:T(8,128)S(1)} %reduce_sum.18), channel_id=1, source_target_pairs={{0,16},{2,18},{4,20},{6,22},{8,24},{10,26},{12,28},{14,30},{16,0},... | collective-permute-start | bytes 196616 | tf_op jit(solution)/shard_map/ppermute | solution.py:162
  20.4 0.0 copy-done.1
  20.4 0.0 copy-done.3
  20.4 0.0 copy-done
  20.4 1.6 %inner.1 = (f32[256,1024]{1,0:T(8,128)S(1)}, bf16[8,256,256]{2,1,0:T(8,128)(2,1)S(1)}) custom-call(bf16[256,1024]{1,0:T(8,128)(2,1)S(1)} %bitcast.20, bf16[256,1024]{1,0:T(8,128)(2,1)S(1)} %bitcast.12, bf16[256,1024]{1,0:T(8,128)(2,1)S(1)} %bitcast.16), custom_call_target="tpu_custom_call" | custom-call | flops 1073741824 | bytes 2097152 | tf_op jit(solution)/shard_map/inner/pallas_call | solution.py:158
  22.0 0.0 copy-start.5
  22.0 1.7 %collective-permute-done.refs_0_ = f32[128,128]{1,0:T(8,128)S(1)} collective-permute-done((f32[128,128]{1,0:T(8,128)S(1)}, f32[128,128]{1,0:T(8,128)S(1)}, u32[]{:S(2)}, u32[]{:S(2)}) %collective-permute-start) | collective-permute-done | bytes 65568 | tf_op jit(solution)/shard_map/ppermute | solution.py:162
  23.7 0.0 copy-done.5
  23.7 0.0 copy-start.2
  23.7 0.0 copy-start.4
  23.8 10.6 %all_to_all.21.state_ref = f32[8,128,128]{2,1,0:T(8,128)S(1)} all-to-all(f32[8,128,128]{2,1,0:T(8,128)S(1)} %prefix.2), channel_id=1, replica_groups={{0,2,4,6,8,10,12,14},{16,18,20,22,24,26,28,30},{1,3,5,7,9,11,13,15},{17..., dimensions={0} | all-to-all | bytes 1048576 | tf_op jit(solution)/shard_map/all_to_all | solution.py:174
  34.3 0.0 copy-done.2
  34.3 0.0 copy-done.4
  34.3 1.3 %norm.1 = (bf16[256,1024]{1,0:T(8,128)(2,1)S(1)}, f32[8,136,128]{2,1,0:T(8,128)S(1)}) custom-call(bf16[256,1024]{1,0:T(8,128)(2,1)S(1)} %bitcast.21, bf16[256,1024]{1,0:T(8,128)(2,1)S(1)} %bitcast.19, f32[256,1024]{1,0:T(8,128)S(1)} %get-tuple-element.37.inner_ref, f32[1,1024]{1,0:T(1,128)S(1)} %bitcast.23, f32[8,128,128]{2,1,0:T(8,128)S(1)} %all_to_all.21.state_ref), custom_call_target="tpu_custom_call" | custom-call | flops 1073741824 | bytes 2097152 | tf_op jit(solution)/shard_map/norm/pallas_call | solution.py:204
  35.7 11.6 %all_to_all.22.refs_2_ = f32[8,136,128]{2,1,0:T(8,128)S(1)} all-to-all(f32[8,136,128]{2,1,0:T(8,128)S(1)} %get-tuple-element.39), channel_id=1, replica_groups={{0,2,4,6,8,10,12,14},{16,18,20,22,24,26,28,30},{1,3,5,7,9,11,13,15},{17..., dimensions={0} | all-to-all | bytes 1114112 | tf_op jit(solution)/shard_map/all_to_all | solution.py:156
  47.4 2.2 %collective-permute-start.1 = (f32[136,128]{1,0:T(8,128)S(1)}, f32[136,128]{1,0:T(8,128)S(1)}, u32[]{:S(2)}, u32[]{:S(2)}) collective-permute-start(f32[136,128]{1,0:T(8,128)S(1)} %reduce_sum.19), channel_id=1, source_target_pairs={{0,16},{2,18},{4,20},{6,22},{8,24},{10,26},{12,28},{14,30},{16,0},... | collective-permute-start | bytes 208904 | tf_op jit(solution)/shard_map/ppermute | solution.py:162
  49.6 0.0 copy-start.6
  49.6 1.2 %copy-done.6 = bf16[8,256,256]{2,1,0:T(8,128)(2,1)S(1)} copy-done((bf16[8,256,256]{2,1,0:T(8,128)(2,1)S(1)}, bf16[8,256,256]{2,1,0:T(8,128)(2,1)}, u32[]{:S(2)}) %copy-start.6) | copy-done | bytes 1048600
  50.8 2.7 %partial.1 = (bf16[256,1024]{1,0:T(8,128)(2,1)}, f32[256,1024]{1,0:T(8,128)S(1)}, f32[256,1024]{1,0:T(8,128)S(1)}) custom-call(bf16[256,1024]{1,0:T(8,128)(2,1)S(1)} %bitcast.22, bf16[256,1024]{1,0:T(8,128)(2,1)S(1)} %bitcast.13, bf16[256,1024]{1,0:T(8,128)(2,1)S(1)} %bitcast.17, bf16[8,256,256]{2,1,0:T(8,128)(2,1)S(1)} %copy-done.6, ...), custom_call_target="tpu_custom_call" | custom-call | flops 3221225472 | bytes 2097152 | tf_op jit(solution)/shard_map/partial/pallas_call | solution.py:158
  53.5 0.0 collective-permute-done.1.refs_0_
  53.6 10.9 %all_to_all.23.state_ref = f32[8,136,128]{2,1,0:T(8,128)S(1)} all-to-all(f32[8,136,128]{2,1,0:T(8,128)S(1)} %prefix.3), channel_id=1, replica_groups={{0,2,4,6,8,10,12,14},{16,18,20,22,24,26,28,30},{1,3,5,7,9,11,13,15},{17..., dimensions={0} | all-to-all | bytes 1114112 | tf_op jit(solution)/shard_map/all_to_all | solution.py:174
  64.5 0.0 collective-permute-start.2
  64.5 1.5 %final.1 = (bf16[256,1024]{1,0:T(8,128)(2,1)}, bf16[256,1024]{1,0:T(8,128)(2,1)}) custom-call(bf16[256,1024]{1,0:T(8,128)(2,1)S(1)} %bitcast.14, bf16[256,1024]{1,0:T(8,128)(2,1)S(1)} %bitcast.18, f32[256,1024]{1,0:T(8,128)S(1)} %get-tuple-element.53.key_part_ref, f32[256,1024]{1,0:T(8,128)S(1)} %get-tuple-element.54.value_part_ref, ...), custom_call_target="tpu_custom_call" | custom-call | flops 1073741824 | bytes 2097152 | tf_op jit(solution)/shard_map/final/pallas_call | solution.py:220
  66.0 0.0 collective-permute-done.2
  66.0 0.6 multiply_bitcast_fusion
  (7 shorter events, 0.2 us)
Async XLA Ops:
  2.1 18.2 %copy-start.1 = (bf16[1,256,1024]{2,1,0:T(8,128)(2,1)S(1)}, bf16[1,256,1024]{2,1,0:T(8,128)(2,1)}, u32[]{:S(2)}) copy-start(bf16[1,256,1024]{2,1,0:T(8,128)(2,1)} %param.7) | copy-start | bytes 1572868
  2.1 18.2 %copy-start.3 = (bf16[1,256,1024]{2,1,0:T(8,128)(2,1)S(1)}, bf16[1,256,1024]{2,1,0:T(8,128)(2,1)}, u32[]{:S(2)}) copy-start(bf16[1,256,1024]{2,1,0:T(8,128)(2,1)} %param.5) | copy-start | bytes 1572868
  17.7 2.7 %copy-start = (bf16[1,256,1024]{2,1,0:T(8,128)(2,1)S(1)}, bf16[1,256,1024]{2,1,0:T(8,128)(2,1)}, u32[]{:S(2)}) copy-start(bf16[1,256,1024]{2,1,0:T(8,128)(2,1)} %param.6) | copy-start | bytes 1572868
  17.7 5.9 %collective-permute-start = (f32[128,128]{1,0:T(8,128)S(1)}, f32[128,128]{1,0:T(8,128)S(1)}, u32[]{:S(2)}, u32[]{:S(2)}) collective-permute-start(f32[128,128]{1,0:T(8,128)S(1)} %reduce_sum.18), channel_id=1, source_target_pairs={{0,16},{2,18},{4,20},{6,22},{8,24},{10,26},{12,28},{14,30},{16,0},... | collective-permute-start | bytes 196616 | tf_op jit(solution)/shard_map/ppermute | solution.py:162
  22.0 1.7 %copy-start.5 = (bf16[8,256,256]{2,1,0:T(8,128)(2,1)}, bf16[8,256,256]{2,1,0:T(8,128)(2,1)S(1)}, u32[]{:S(2)}) copy-start(bf16[8,256,256]{2,1,0:T(8,128)(2,1)S(1)} %get-tuple-element.46.turned_ref) | copy-start | bytes 3145732
  23.7 10.6 %copy-start.2 = (bf16[1,256,1024]{2,1,0:T(8,128)(2,1)S(1)}, bf16[1,256,1024]{2,1,0:T(8,128)(2,1)}, u32[]{:S(2)}) copy-start(bf16[1,256,1024]{2,1,0:T(8,128)(2,1)} %param.9) | copy-start | bytes 1572868
  23.7 10.6 %copy-start.4 = (f32[1024]{0:T(1024)S(1)}, f32[1024]{0:T(1024)}, u32[]{:S(2)}) copy-start(f32[1024]{0:T(1024)} %param.8) | copy-start | bytes 12292
  47.4 6.1 %collective-permute-start.1 = (f32[136,128]{1,0:T(8,128)S(1)}, f32[136,128]{1,0:T(8,128)S(1)}, u32[]{:S(2)}, u32[]{:S(2)}) collective-permute-start(f32[136,128]{1,0:T(8,128)S(1)} %reduce_sum.19), channel_id=1, source_target_pairs={{0,16},{2,18},{4,20},{6,22},{8,24},{10,26},{12,28},{14,30},{16,0},... | collective-permute-start | bytes 208904 | tf_op jit(solution)/shard_map/ppermute | solution.py:162
  49.6 1.2 %copy-start.6 = (bf16[8,256,256]{2,1,0:T(8,128)(2,1)S(1)}, bf16[8,256,256]{2,1,0:T(8,128)(2,1)}, u32[]{:S(2)}) copy-start(bf16[8,256,256]{2,1,0:T(8,128)(2,1)} %copy-done.5) | copy-start | bytes 3145732
  64.5 1.6 %collective-permute-start.2 = (f32[8,128]{1,0:T(8,128)S(1)}, f32[8,128]{1,0:T(8,128)S(1)}, u32[]{:S(2)}, u32[]{:S(2)}) collective-permute-start(f32[8,128]{1,0:T(8,128)S(1)} %gain.1), channel_id=1, source_target_pairs={{0,1},{1,0},{2,3},{3,2},{4,5},{5,4},{6,7},{7,6},{8,9},{9,8},{10,11... | collective-permute-start | bytes 12296 | tf_op jit(solution)/shard_map/ppermute | solution.py:217

commit v10 on v9

v10 whole, which is shorter than its diff:
```python
import functools
import math

import jax
import jax.numpy as jnp
from jax import lax
from jax.experimental import pallas as pl
from jax.experimental.pallas import tpu as pltpu
from jax.sharding import PartitionSpec as P

HEADS = 8
DH = 128
BLOCK = 256
GROUP = 4
CHAINS = HEADS // GROUP
WIDE = GROUP * DH
GAIN_ROWS = 8
PARTS = 2
PART_ROWS = BLOCK // PARTS
EPSILON = 1e-06

NT = (((1,), (1,)), ((), ()))
TN = (((0,), (0,)), ((), ()))
NN = (((1,), (0,)), ((), ()))


def dot(left, right, dims):
    return lax.dot_general(left, right, dims, preferred_element_type=jnp.float32)


def columns(head):
    return pl.ds(head * DH, DH)


def own_columns(place_ref, mask, chain=0):
    return pl.ds(pl.multiple_of(chain * WIDE + (place_ref[0] ^ mask) * DH, DH), DH)


def causal(turned=False):
    shape, first = (BLOCK, BLOCK), int(turned)
    return lax.broadcasted_iota(jnp.int32, shape, first) >= lax.broadcasted_iota(jnp.int32, shape, 1 - first)


def delta_body(place_ref, key_ref, value_ref, *refs):
    delta_refs, (key_here, value_here, sems) = refs[:HEADS], refs[HEADS:]
    copies = []
    for part in range(PARTS):
        rows = pl.ds(part * PART_ROWS, PART_ROWS)
        for side, (source, here) in enumerate(((key_ref, key_here), (value_ref, value_here))):
            copies.append(pltpu.make_async_copy(source.at[rows], here.at[rows], sems.at[part, side]))
            copies[-1].start()
    for part in range(PARTS):
        rows = pl.ds(part * PART_ROWS, PART_ROWS)
        for copy in copies[2 * part : 2 * part + 2]:
            copy.wait()
        for at_head, delta_ref in enumerate(delta_refs):
            at = own_columns(place_ref, at_head % GROUP, at_head // GROUP)
            delta = dot(key_here[rows, at], value_here[rows, at], TN)
            delta_ref[...] = delta if part == 0 else delta_ref[...] + delta


def inner_body(query_ref, key_ref, value_ref, inner_ref):
    keep = causal()
    for head in range(HEADS):
        at = columns(head)
        scores = jnp.where(keep, dot(query_ref[:, at], key_ref[:, at], NT), 0.0).astype(jnp.bfloat16)
        inner_ref[:, at] = dot(scores, value_ref[:, at], NN)


def norm_body(chain, place_ref, query_ref, grad_ref, inner_ref, gain_ref, *refs):
    state_refs, (attn_ref, *delta_refs) = refs[:GROUP], refs[GROUP:]
    for mask, (state_ref, delta_ref) in enumerate(zip(state_refs, delta_refs)):
        at = own_columns(place_ref, mask, chain)
        query = query_ref[:, at]
        attn = inner_ref[:, at] + dot(query, state_ref[...].astype(jnp.bfloat16), NN)
        per_root = lax.rsqrt(jnp.mean(attn * attn, axis=-1, keepdims=True) + EPSILON)
        normed = attn * per_root
        cotangent = grad_ref[:, at].astype(jnp.float32)
        product = normed * cotangent
        gain = gain_ref[:, at]
        shared = jnp.mean(product * gain, axis=-1, keepdims=True)
        grad_attn = ((gain * cotangent - normed * shared) * per_root).astype(jnp.bfloat16)
        attn_ref[:, own_columns(place_ref, mask)] = grad_attn
        delta_ref[:DH] = dot(query, grad_attn, TN)
        delta_ref[DH:] = jnp.broadcast_to(jnp.sum(product, axis=0, keepdims=True), (GAIN_ROWS, DH))


def partial_body(place_ref, query_ref, key_ref, value_ref, *refs):
    attn_refs, state_refs = refs[:CHAINS], refs[CHAINS : CHAINS + HEADS]
    grad_query_ref, key_part_ref, value_part_ref = refs[-3:]
    keep, kept = causal(), causal(True)
    for at_head, state_ref in enumerate(state_refs):
        chain, mask = at_head // GROUP, at_head % GROUP
        at = own_columns(place_ref, mask, chain)
        query, key, value = query_ref[:, at], key_ref[:, at], value_ref[:, at]
        grad_attn = attn_refs[chain][:, own_columns(place_ref, mask)]
        turned = jnp.where(kept, dot(key, query, NT), 0.0).astype(jnp.bfloat16)
        grad_scores = jnp.where(keep, dot(grad_attn, value, NT), 0.0).astype(jnp.bfloat16)
        turned_grad = jnp.where(kept, dot(value, grad_attn, NT), 0.0).astype(jnp.bfloat16)
        carried = dot(grad_attn, state_ref[...].astype(jnp.bfloat16), NT)
        grad_query_ref[:, at] = (dot(grad_scores, key, NN) + carried).astype(jnp.bfloat16)
        key_part_ref[:, at] = dot(turned_grad, query, NN)
        value_part_ref[:, at] = dot(turned, grad_attn, NN)


def final_body(place_ref, key_ref, value_ref, key_part_ref, value_part_ref, *refs):
    state_refs, (grad_key_ref, grad_value_ref) = refs[:HEADS], refs[HEADS:]
    rows = pl.ds(pl.multiple_of(pl.program_id(0) * PART_ROWS, PART_ROWS), PART_ROWS)
    for at_head, state_ref in enumerate(state_refs):
        at = own_columns(place_ref, at_head % GROUP, at_head // GROUP)
        state = state_ref[:DH].astype(jnp.bfloat16)
        grad_key_ref[:, at] = (key_part_ref[rows, at] + dot(value_ref[rows, at], state, NT)).astype(jnp.bfloat16)
        grad_value_ref[:, at] = (value_part_ref[rows, at] + dot(key_ref[rows, at], state, NN)).astype(jnp.bfloat16)


def gain_body(place_ref, *refs):
    for at_head, state_ref in enumerate(refs[:-1]):
        row = (at_head // GROUP) * GROUP + (place_ref[0] ^ (at_head % GROUP))
        refs[-1][pl.ds(row, 1), :] = state_ref[DH : DH + 1]


def prefix_body(reverse, place_ref, *refs):
    (total_ref, *arrived_refs), (*back_refs, ahead) = refs[: -2 * GROUP - 1], refs[-GROUP - 1 :]
    held_refs = refs[-2 * GROUP - 1 : -GROUP - 1]
    for mask, held_ref in enumerate(held_refs):
        ahead[pl.ds(place_ref[0] ^ mask, 1)] = held_ref[:DH][None]
    running = jnp.zeros((DH, DH), jnp.float32)
    for step, arrived_ref in enumerate(arrived_refs):
        later = (place_ref[step + 1] != 0) != reverse
        running = running + jnp.where(later, arrived_ref[:DH], 0.0)
    for member in reversed(range(GROUP)) if reverse else range(GROUP):
        own = ahead[member]
        ahead[member] = running
        running = running + own
    for mask, back_ref in enumerate(back_refs):
        back_ref[:DH] = ahead[pl.ds(place_ref[0] ^ mask, 1)][0]
        if back_ref.shape[0] > DH:
            back_ref[DH:] = total_ref[DH:]


def whole(*shape):
    return pl.BlockSpec(shape, lambda step: (0,) * len(shape))


PLACE = pl.BlockSpec(memory_space=pltpu.SMEM)


def call(body, in_specs, out_specs, outs, flops, name, steps=1, scratch=()):
    return pl.pallas_call(
        body,
        grid=(steps,),
        in_specs=[PLACE] + in_specs,
        out_specs=out_specs,
        out_shape=outs,
        scratch_shapes=scratch,
        compiler_params=pltpu.CompilerParams(vmem_limit_bytes=16 * 1024 * 1024),
        cost_estimate=pl.CostEstimate(flops=flops, bytes_accessed=2 << 20, transcendentals=0),
        name=name,
    )


def exchange_masks():
    masks = [GROUP]
    while masks[-1] * 2 < lax.axis_size("seq"):
        masks.append(masks[-1] * 2)
    return masks if lax.axis_size("seq") > GROUP else []


def swap(array, mask):
    if mask == 0:
        return array
    return lax.ppermute(array, "seq", [(s, s ^ mask) for s in range(lax.axis_size("seq"))])


def carried_in(pieces, reverse, place):
    held = [swap(piece, mask) for mask, piece in enumerate(pieces)]
    total = sum(held[1:], held[0])
    arrived = []
    for mask in exchange_masks():
        arrived.append(swap(total, mask))
        total = total + arrived[-1]
    single = whole(*total.shape)
    back = call(
        functools.partial(prefix_body, reverse),
        [single] * (1 + len(arrived) + GROUP),
        [single] * GROUP,
        [jax.ShapeDtypeStruct(total.shape, jnp.float32)] * GROUP,
        1 << 24,
        "prefix",
        scratch=[pltpu.VMEM((GROUP, DH, DH), jnp.float32)],
    )(place, total, *arrived, *held)
    return [swap(piece, mask) for mask, piece in enumerate(back)]


def local(queries, keys, values, out_gain, grad_out):
    full = queries.shape
    flat = (full[0] * full[1], full[2])
    assert flat == (BLOCK, HEADS * DH) and lax.axis_size("seq") % GROUP == 0
    query, key, value, grad = (a.reshape(flat) for a in (queries, keys, values, grad_out))
    gain = out_gain.reshape(1, HEADS * DH)
    square = jax.ShapeDtypeStruct((DH, DH), jnp.float32)
    taller = jax.ShapeDtypeStruct((DH + GAIN_ROWS, DH), jnp.float32)
    full_float = jax.ShapeDtypeStruct(flat, jnp.float32)
    full_low = jax.ShapeDtypeStruct(flat, jnp.bfloat16)
    half_low = jax.ShapeDtypeStruct((BLOCK, WIDE), jnp.bfloat16)
    short, tall, wide, half = whole(*square.shape), whole(*taller.shape), whole(*flat), whole(BLOCK, WIDE)
    unit = 2 * BLOCK * DH * DH * HEADS

    at = lax.axis_index("seq")
    place = jnp.stack([lax.rem(at, GROUP)] + [at & mask for mask in exchange_masks()]).astype(jnp.int32)
    deltas = call(
        delta_body,
        [pl.BlockSpec(memory_space=pltpu.HBM)] * 2,
        [short] * HEADS,
        [square] * HEADS,
        6 * unit,
        "delta",
        scratch=[pltpu.VMEM(flat, jnp.bfloat16)] * 2 + [pltpu.SemaphoreType.DMA((PARTS, 2))],
    )(place, *[pltpu.with_memory_space_constraint(a, pltpu.HBM) for a in (key, value)])
    chains = [slice(chain * GROUP, (chain + 1) * GROUP) for chain in range(CHAINS)]
    states = [carried_in(deltas[chain], False, place) for chain in chains]
    inner = call(
        lambda place_ref, *refs: inner_body(*refs), [wide] * 3, wide, full_float, 16 * unit, "inner"
    )(place, query, key, value)
    attns, later = [], []
    for chain in range(CHAINS):
        attn, *deltas = call(
            functools.partial(norm_body, chain),
            [wide, wide, wide, whole(1, HEADS * DH)] + [short] * GROUP,
            [half] + [tall] * GROUP,
            [half_low] + [taller] * GROUP,
            8 * unit,
            "norm",
        )(place, query, grad, inner, gain, *states[chain])
        attns.append(attn)
        later += carried_in(deltas, True, place)
    grad_query, key_part, value_part = call(
        partial_body,
        [wide] * 3 + [half] * CHAINS + [short] * HEADS,
        [wide] * 3,
        [full_low, full_float, full_float],
        48 * unit,
        "partial",
    )(place, query, key, value, *attns, *[state for chain in states for state in chain])
    gain_terms = call(
        gain_body, [tall] * HEADS, whole(HEADS, DH), jax.ShapeDtypeStruct((HEADS, DH), jnp.float32), unit, "gain"
    )(place, *later)
    docs, mask = lax.axis_size("dp"), 1
    while mask < docs:
        gain_terms = gain_terms + lax.ppermute(gain_terms, "dp", [(d, d ^ mask) for d in range(docs)])
        mask *= 2
    chunk = pl.BlockSpec((PART_ROWS, HEADS * DH), lambda step: (step, 0))
    grad_key, grad_value = call(
        final_body, [wide] * 4 + [tall] * HEADS, [chunk] * 2, [full_low] * 2, 16 * unit, "final", steps=PARTS
    )(place, key, value, key_part, value_part, *later)
    grad_gain = gain_terms / math.sqrt(lax.axis_size("seq") * docs * BLOCK)
    return (
        grad_query.reshape(full),
        grad_key.reshape(full),
        grad_value.reshape(full),
        grad_gain.reshape(HEADS * DH),
    )


def solution(mesh):
    sharded = P("dp", "seq", None)
    return jax.shard_map(
        local,
        mesh=mesh,
        in_specs=(sharded, sharded, sharded, P(), sharded),
        out_specs=(sharded, sharded, sharded, P()),
        check_vma=False,
    )
```

time: 67 us -> 69.7 us (1.040)
  blocking collectives: 48.6 us -> 0 us
  starting transfers between devices: 4.86 us -> 43.7 us
  waiting for transfers between devices: 1.66 us -> 9.25 us
  Pallas kernels: 8.79 us -> 14.9 us
  local copies, waits for them, and re-layouts: 1.26 us -> 0.03 us
    all_to_all x4 -> x0, blocking collectives: 48.6 us -> none  [the longest x2 27.2 us: carried_in(): held = lax.all_to_all(parts, 'seq', 0, 0, axis_index_groups=teams)]
    ppermute x2 -> x32, starting transfers between devices: 4.86 us -> 43.6 us  [swap(): lax.ppermute(array, 'seq', [(s, s ^ mask) for s in range(lax.axis_size('s...]
    ppermute x2 -> x32, waiting for transfers between devices: 1.66 us -> 9.24 us  [swap(): lax.ppermute(array, 'seq', [(s, s ^ mask) for s in range(lax.axis_size('s...]
    pallas_call x8 -> x11, Pallas kernels: 8.79 us -> 14.9 us  [the longest x1 3.64 us: local(): call(partial_body, [wide] * 3 + [half] * CHAINS + [short] * HEADS, [wide]...]
    unnamed x14 -> x10, local copies, waits for them, and re-layouts: 1.26 us -> 0.03 us
  transfers between devices with their start and end apart: 3 -> 33, of which waited for: 1 -> 13; matrix products, arithmetic and copies ran while one was open for 0% -> 0% of each run, Pallas kernels for 9% -> 18%
where the time goes in v10:
time: 69.7 us; the launch traced here: 69.5 us
  starting transfers between devices  43.7 us (63%)
  Pallas kernels  14.9 us (21%)
  waiting for transfers between devices  9.25 us (13%)
  other arithmetic  0.83 us (1%)
  between operations  0.83 us (1%)
    ppermute x32, starting transfers between devices, swap(): lax.ppermute(array, 'seq', [(s, s ^ mask) for s in range(lax.axis_size('s...  43.6 us
    ppermute x32, waiting for transfers between devices, swap(): lax.ppermute(array, 'seq', [(s, s ^ mask) for s in range(lax.axis_size('s...  9.24 us
    pallas_call x1, Pallas kernels, local(): call(partial_body, [wide] * 3 + [half] * CHAINS + [short] * HEADS, [wide]...  3.64 us
    pallas_call x2, Pallas kernels, local(): call(functools.partial(norm_body, chain), [wide, wide, wide, whole(1, HEA...  2.55 us
    pallas_call x4, Pallas kernels, carried_in(): call(functools.partial(prefix_body, reverse), [single] * (1 + len(arrived...  2.42 us
    pallas_call x1, Pallas kernels, local(): call(final_body, [wide] * 4 + [tall] * HEADS, [chunk] * 2, [full_low] * 2...  2.18 us
    pallas_call x1, Pallas kernels, local(): call(delta_body, [pl.BlockSpec(memory_space=pltpu.HBM)] * 2, [short] * HE...  2.07 us
    pallas_call x1, Pallas kernels, local(): call(lambda place_ref, *refs: inner_body(*refs), [wide] * 3, wide, full_f...  1.47 us
  transfers between devices with their start and end apart: 33, of which 13 were waited for; matrix products, arithmetic and copies ran while one was open for 0% of the time, Pallas kernels for 18%

profile of v10, /device:TPU:0, one launch (start us, length us, event | category | flops | bytes accessed | tf_op | source)
XLA Modules:
  0.0 69.5 jit_solution(9285428315344650478)
XLA Ops:
  0.7 2.1 %delta.1 = (f32[128,128]{1,0:T(8,128)S(1)}, f32[128,128]{1,0:T(8,128)S(1)}, f32[128,128]{1,0:T(8,128)S(1)}, f32[128,128]{1,0:T(8,128)S(1)}, f32[128,128]{1,0:T(8...) custom-call(s32[3]{0:T(128)S(1)} %pad_add_fusion.place_ref, ...), custom_call_target="tpu_custom_call" | custom-call | flops 402653184 | bytes 2097152 | tf_op jit(solution)/shard_map/delta/pallas_call | solution.py:211
  2.8 4.0 %collective-permute-start.2 = (f32[128,128]{1,0:T(8,128)S(1)}, f32[128,128]{1,0:T(8,128)S(1)}, u32[]{:S(2)}, u32[]{:S(2)}) collective-permute-start(f32[128,128]{1,0:T(8,128)S(1)} %get-tuple-element.46), channel_id=1, source_target_pairs={{0,6},{2,4},{4,2},{6,0},{8,14},{10,12},{12,10},{14,8},{16,22},{18,... | collective-permute-start | bytes 196616 | tf_op jit(solution)/shard_map/ppermute | solution.py:172
  7.4 2.8 %collective-permute-start.10 = (f32[128,128]{1,0:T(8,128)S(1)}, f32[128,128]{1,0:T(8,128)S(1)}, u32[]{:S(2)}, u32[]{:S(2)}) collective-permute-start(f32[128,128]{1,0:T(8,128)S(1)} %get-tuple-element.55), channel_id=1, source_target_pairs={{0,6},{2,4},{4,2},{6,0},{8,14},{10,12},{12,10},{14,8},{16,22},{18,... | collective-permute-start | bytes 196616 | tf_op jit(solution)/shard_map/ppermute | solution.py:172
  11.8 1.6 %collective-permute-start.3 = (f32[128,128]{1,0:T(8,128)S(1)}, f32[128,128]{1,0:T(8,128)S(1)}, u32[]{:S(2)}, u32[]{:S(2)}) collective-permute-start(f32[128,128]{1,0:T(8,128)S(1)} %add_add_fusion.3), channel_id=1, source_target_pairs={{0,8},{2,10},{4,12},{6,14},{8,0},{10,2},{12,4},{14,6},{16,24},{18,... | collective-permute-start | bytes 196616 | tf_op jit(solution)/shard_map/ppermute | solution.py:172
  15.0 1.6 %collective-permute-start.11 = (f32[128,128]{1,0:T(8,128)S(1)}, f32[128,128]{1,0:T(8,128)S(1)}, u32[]{:S(2)}, u32[]{:S(2)}) collective-permute-start(f32[128,128]{1,0:T(8,128)S(1)} %add_add_fusion.2), channel_id=1, source_target_pairs={{0,8},{2,10},{4,12},{6,14},{8,0},{10,2},{12,4},{14,6},{16,24},{18,... | collective-permute-start | bytes 196616 | tf_op jit(solution)/shard_map/ppermute | solution.py:172
  16.9 2.7 %collective-permute-start.4 = (f32[128,128]{1,0:T(8,128)S(1)}, f32[128,128]{1,0:T(8,128)S(1)}, u32[]{:S(2)}, u32[]{:S(2)}) collective-permute-start(f32[128,128]{1,0:T(8,128)S(1)} %add.66), channel_id=1, source_target_pairs={{0,16},{2,18},{4,20},{6,22},{8,24},{10,26},{12,28},{14,30},{16,0},... | collective-permute-start | bytes 196616 | tf_op jit(solution)/shard_map/ppermute | solution.py:172
  19.5 2.5 %collective-permute-start.12 = (f32[128,128]{1,0:T(8,128)S(1)}, f32[128,128]{1,0:T(8,128)S(1)}, u32[]{:S(2)}, u32[]{:S(2)}) collective-permute-start(f32[128,128]{1,0:T(8,128)S(1)} %add.71), channel_id=1, source_target_pairs={{0,16},{2,18},{4,20},{6,22},{8,24},{10,26},{12,28},{14,30},{16,0},... | collective-permute-start | bytes 196616 | tf_op jit(solution)/shard_map/ppermute | solution.py:172
  22.0 1.4 %collective-permute-done.4.refs_2_ = f32[128,128]{1,0:T(8,128)S(1)} collective-permute-done((f32[128,128]{1,0:T(8,128)S(1)}, f32[128,128]{1,0:T(8,128)S(1)}, u32[]{:S(2)}, u32[]{:S(2)}) %collective-permute-start.4) | collective-permute-done | bytes 65568 | tf_op jit(solution)/shard_map/ppermute | solution.py:172
  24.6 1.5 %collective-permute-start.6 = (f32[128,128]{1,0:T(8,128)S(1)}, f32[128,128]{1,0:T(8,128)S(1)}, u32[]{:S(2)}, u32[]{:S(2)}) collective-permute-start(f32[128,128]{1,0:T(8,128)S(1)} %get-tuple-element.49), channel_id=1, source_target_pairs={{0,4},{2,6},{4,0},{6,2},{8,12},{10,14},{12,8},{14,10},{16,20},{18,... | collective-permute-start | bytes 196616 | tf_op jit(solution)/shard_map/ppermute | solution.py:172
  26.1 1.6 %collective-permute-start.7 = (f32[128,128]{1,0:T(8,128)S(1)}, f32[128,128]{1,0:T(8,128)S(1)}, u32[]{:S(2)}, u32[]{:S(2)}) collective-permute-start(f32[128,128]{1,0:T(8,128)S(1)} %get-tuple-element.50), channel_id=1, source_target_pairs={{0,6},{2,4},{4,2},{6,0},{8,14},{10,12},{12,10},{14,8},{16,22},{18,... | collective-permute-start | bytes 196616 | tf_op jit(solution)/shard_map/ppermute | solution.py:172
  28.8 1.5 %inner.1.inner_ref = f32[256,1024]{1,0:T(8,128)S(1)} custom-call(s32[3]{0:T(128)S(1)} %pad_add_fusion.place_ref, bf16[256,1024]{1,0:T(8,128)(2,1)S(1)} %bitcast.15, bf16[256,1024]{1,0:T(8,128)(2,1)S(1)} %bitcast.22, bf16[256,1024]{1,0:T(8,128)(2,1)S(1)} %bitcast.26), custom_call_target="tpu_custom_call" | custom-call | flops 1073741824 | bytes 2097152 | tf_op jit(solution)/shard_map/inner/pallas_call | solution.py:222
  30.3 1.6 %collective-permute-start.14 = (f32[128,128]{1,0:T(8,128)S(1)}, f32[128,128]{1,0:T(8,128)S(1)}, u32[]{:S(2)}, u32[]{:S(2)}) collective-permute-start(f32[128,128]{1,0:T(8,128)S(1)} %get-tuple-element.58), channel_id=1, source_target_pairs={{0,4},{2,6},{4,0},{6,2},{8,12},{10,14},{12,8},{14,10},{16,20},{18,... | collective-permute-start | bytes 196616 | tf_op jit(solution)/shard_map/ppermute | solution.py:172
  31.8 1.6 %collective-permute-start.15 = (f32[128,128]{1,0:T(8,128)S(1)}, f32[128,128]{1,0:T(8,128)S(1)}, u32[]{:S(2)}, u32[]{:S(2)}) collective-permute-start(f32[128,128]{1,0:T(8,128)S(1)} %get-tuple-element.59), channel_id=1, source_target_pairs={{0,6},{2,4},{4,2},{6,0},{8,14},{10,12},{12,10},{14,8},{16,22},{18,... | collective-permute-start | bytes 196616 | tf_op jit(solution)/shard_map/ppermute | solution.py:172
  33.5 1.3 %norm.2 = (bf16[256,512]{1,0:T(8,128)(2,1)S(1)}, f32[136,128]{1,0:T(8,128)S(1)}, f32[136,128]{1,0:T(8,128)S(1)}, f32[136,128]{1,0:T(8,128)S(1)}, f32[136,128]{1,0:T(8,128)S(1)}) custom-call(s32[3]{0:T(128)S(1)} %pad_add_fusion.place_ref, bf16[256,1024]{1,0:T(8,128)(2,1)S(1)} %bitcast.16, bf16[256,1024]{1,0:T(8,128)(2,1)S(1)} %bitcast.13, ...), custom_call_target="tpu_custom_call" | custom-call | flops 536870912 | bytes 2097152 | tf_op jit(solution)/shard_map/norm/pallas_call | solution.py:227
  34.7 1.4 %collective-permute-start.18 = (f32[136,128]{1,0:T(8,128)S(1)}, f32[136,128]{1,0:T(8,128)S(1)}, u32[]{:S(2)}, u32[]{:S(2)}) collective-permute-start(f32[136,128]{1,0:T(8,128)S(1)} %get-tuple-element.67), channel_id=1, source_target_pairs={{0,6},{2,4},{4,2},{6,0},{8,14},{10,12},{12,10},{14,8},{16,22},{18,... | collective-permute-start | bytes 208904 | tf_op jit(solution)/shard_map/ppermute | solution.py:172
  36.7 1.6 %collective-permute-start.16 = (f32[136,128]{1,0:T(8,128)S(1)}, f32[136,128]{1,0:T(8,128)S(1)}, u32[]{:S(2)}, u32[]{:S(2)}) collective-permute-start(f32[136,128]{1,0:T(8,128)S(1)} %get-tuple-element.65), channel_id=1, source_target_pairs={{0,2},{2,0},{4,6},{6,4},{8,10},{10,8},{12,14},{14,12},{16,18},{18,... | collective-permute-start | bytes 208904 | tf_op jit(solution)/shard_map/ppermute | solution.py:172
  38.3 1.3 %norm.3 = (bf16[256,512]{1,0:T(8,128)(2,1)S(1)}, f32[136,128]{1,0:T(8,128)S(1)}, f32[136,128]{1,0:T(8,128)S(1)}, f32[136,128]{1,0:T(8,128)S(1)}, f32[136,128]{1,0:T(8,128)S(1)}) custom-call(s32[3]{0:T(128)S(1)} %pad_add_fusion.place_ref, bf16[256,1024]{1,0:T(8,128)(2,1)S(1)} %bitcast.17, bf16[256,1024]{1,0:T(8,128)(2,1)S(1)} %bitcast.14, ...), custom_call_target="tpu_custom_call" | custom-call | flops 536870912 | bytes 2097152 | tf_op jit(solution)/shard_map/norm/pallas_call | solution.py:227
  39.6 1.4 %collective-permute-start.26 = (f32[136,128]{1,0:T(8,128)S(1)}, f32[136,128]{1,0:T(8,128)S(1)}, u32[]{:S(2)}, u32[]{:S(2)}) collective-permute-start(f32[136,128]{1,0:T(8,128)S(1)} %get-tuple-element.75), channel_id=1, source_target_pairs={{0,6},{2,4},{4,2},{6,0},{8,14},{10,12},{12,10},{14,8},{16,22},{18,... | collective-permute-start | bytes 208904 | tf_op jit(solution)/shard_map/ppermute | solution.py:172
  41.5 1.6 %collective-permute-start.24 = (f32[136,128]{1,0:T(8,128)S(1)}, f32[136,128]{1,0:T(8,128)S(1)}, u32[]{:S(2)}, u32[]{:S(2)}) collective-permute-start(f32[136,128]{1,0:T(8,128)S(1)} %get-tuple-element.73), channel_id=1, source_target_pairs={{0,2},{2,0},{4,6},{6,4},{8,10},{10,8},{12,14},{14,12},{16,18},{18,... | collective-permute-start | bytes 208904 | tf_op jit(solution)/shard_map/ppermute | solution.py:172
  43.8 1.1 %collective-permute-done.26.refs_6_ = f32[136,128]{1,0:T(8,128)S(1)} collective-permute-done((f32[136,128]{1,0:T(8,128)S(1)}, f32[136,128]{1,0:T(8,128)S(1)}, u32[]{:S(2)}, u32[]{:S(2)}) %collective-permute-start.26) | collective-permute-done | bytes 69664 | tf_op jit(solution)/shard_map/ppermute | solution.py:172
  46.6 0.9 %collective-permute-done.19.refs_1_ = f32[136,128]{1,0:T(8,128)S(1)} collective-permute-done((f32[136,128]{1,0:T(8,128)S(1)}, f32[136,128]{1,0:T(8,128)S(1)}, u32[]{:S(2)}, u32[]{:S(2)}) %collective-permute-start.19) | collective-permute-done | bytes 69664 | tf_op jit(solution)/shard_map/ppermute | solution.py:172
  47.6 2.1 %collective-permute-start.20 = (f32[136,128]{1,0:T(8,128)S(1)}, f32[136,128]{1,0:T(8,128)S(1)}, u32[]{:S(2)}, u32[]{:S(2)}) collective-permute-start(f32[136,128]{1,0:T(8,128)S(1)} %add.76), channel_id=1, source_target_pairs={{0,16},{2,18},{4,20},{6,22},{8,24},{10,26},{12,28},{14,30},{16,0},... | collective-permute-start | bytes 208904 | tf_op jit(solution)/shard_map/ppermute | solution.py:172
  50.2 1.7 %collective-permute-start.28 = (f32[136,128]{1,0:T(8,128)S(1)}, f32[136,128]{1,0:T(8,128)S(1)}, u32[]{:S(2)}, u32[]{:S(2)}) collective-permute-start(f32[136,128]{1,0:T(8,128)S(1)} %add.81), channel_id=1, source_target_pairs={{0,16},{2,18},{4,20},{6,22},{8,24},{10,26},{12,28},{14,30},{16,0},... | collective-permute-start | bytes 208904 | tf_op jit(solution)/shard_map/ppermute | solution.py:172
  52.0 1.6 %collective-permute-done.20.refs_2_ = f32[136,128]{1,0:T(8,128)S(1)} collective-permute-done((f32[136,128]{1,0:T(8,128)S(1)}, f32[136,128]{1,0:T(8,128)S(1)}, u32[]{:S(2)}, u32[]{:S(2)}) %collective-permute-start.20) | collective-permute-done | bytes 69664 | tf_op jit(solution)/shard_map/ppermute | solution.py:172
  54.2 1.0 %collective-permute-start.21 = (f32[136,128]{1,0:T(8,128)S(1)}, f32[136,128]{1,0:T(8,128)S(1)}, u32[]{:S(2)}, u32[]{:S(2)}) collective-permute-start(f32[136,128]{1,0:T(8,128)S(1)} %get-tuple-element.69), channel_id=1, source_target_pairs={{0,2},{2,0},{4,6},{6,4},{8,10},{10,8},{12,14},{14,12},{16,18},{18,... | collective-permute-start | bytes 208904 | tf_op jit(solution)/shard_map/ppermute | solution.py:172
  55.3 1.5 %collective-permute-start.22 = (f32[136,128]{1,0:T(8,128)S(1)}, f32[136,128]{1,0:T(8,128)S(1)}, u32[]{:S(2)}, u32[]{:S(2)}) collective-permute-start(f32[136,128]{1,0:T(8,128)S(1)} %get-tuple-element.70), channel_id=1, source_target_pairs={{0,4},{2,6},{4,0},{6,2},{8,12},{10,14},{12,8},{14,10},{16,20},{18,... | collective-permute-start | bytes 208904 | tf_op jit(solution)/shard_map/ppermute | solution.py:172
  56.7 1.1 %collective-permute-start.23 = (f32[136,128]{1,0:T(8,128)S(1)}, f32[136,128]{1,0:T(8,128)S(1)}, u32[]{:S(2)}, u32[]{:S(2)}) collective-permute-start(f32[136,128]{1,0:T(8,128)S(1)} %get-tuple-element.71), channel_id=1, source_target_pairs={{0,6},{2,4},{4,2},{6,0},{8,14},{10,12},{12,10},{14,8},{16,22},{18,... | collective-permute-start | bytes 208904 | tf_op jit(solution)/shard_map/ppermute | solution.py:172
  58.4 1.0 %collective-permute-start.29 = (f32[136,128]{1,0:T(8,128)S(1)}, f32[136,128]{1,0:T(8,128)S(1)}, u32[]{:S(2)}, u32[]{:S(2)}) collective-permute-start(f32[136,128]{1,0:T(8,128)S(1)} %get-tuple-element.77), channel_id=1, source_target_pairs={{0,2},{2,0},{4,6},{6,4},{8,10},{10,8},{12,14},{14,12},{16,18},{18,... | collective-permute-start | bytes 208904 | tf_op jit(solution)/shard_map/ppermute | solution.py:172
  59.4 1.5 %collective-permute-start.30 = (f32[136,128]{1,0:T(8,128)S(1)}, f32[136,128]{1,0:T(8,128)S(1)}, u32[]{:S(2)}, u32[]{:S(2)}) collective-permute-start(f32[136,128]{1,0:T(8,128)S(1)} %get-tuple-element.78), channel_id=1, source_target_pairs={{0,4},{2,6},{4,0},{6,2},{8,12},{10,14},{12,8},{14,10},{16,20},{18,... | collective-permute-start | bytes 208904 | tf_op jit(solution)/shard_map/ppermute | solution.py:172
  60.9 1.1 %collective-permute-start.31 = (f32[136,128]{1,0:T(8,128)S(1)}, f32[136,128]{1,0:T(8,128)S(1)}, u32[]{:S(2)}, u32[]{:S(2)}) collective-permute-start(f32[136,128]{1,0:T(8,128)S(1)} %get-tuple-element.79), channel_id=1, source_target_pairs={{0,6},{2,4},{4,2},{6,0},{8,14},{10,12},{12,10},{14,8},{16,22},{18,... | collective-permute-start | bytes 208904 | tf_op jit(solution)/shard_map/ppermute | solution.py:172
  62.0 3.6 %partial.1 = (bf16[256,1024]{1,0:T(8,128)(2,1)}, f32[256,1024]{1,0:T(8,128)S(1)}, f32[256,1024]{1,0:T(8,128)S(1)}) custom-call(s32[3]{0:T(128)S(1)} %pad_add_fusion.place_ref, bf16[256,1024]{1,0:T(8,128)(2,1)S(1)} %bitcast.18, bf16[256,1024]{1,0:T(8,128)(2,1)S(1)} %bitcast.23, bf16[256,1024]{1,0:T(8,128)(2,1)S(1)} %bitcast.27, ...), custom_call_target="tpu_custom_call" | custom-call | flops 3221225472 | bytes 2097152 | tf_op jit(solution)/shard_map/partial/pallas_call | solution.py:237
  66.7 2.2 %final.1 = (bf16[256,1024]{1,0:T(8,128)(2,1)}, bf16[256,1024]{1,0:T(8,128)(2,1)}) custom-call(s32[3]{0:T(128)S(1)} %pad_add_fusion.place_ref, bf16[256,1024]{1,0:T(8,128)(2,1)S(1)} %bitcast.24, bf16[256,1024]{1,0:T(8,128)(2,1)S(1)} %bitcast.28, f32[256,1024]{1,0:T(8,128)S(1)} %get-tuple-element.62.key_part_ref, ...), custom_call_target="tpu_custom_call" | custom-call | flops 1073741824 | bytes 2097152 | tf_op jit(solution)/shard_map/final/pallas_call | solution.py:253
  (69 shorter events, 13.1 us)
Async XLA Ops:
  2.8 8.0 %collective-permute-start.2 = (f32[128,128]{1,0:T(8,128)S(1)}, f32[128,128]{1,0:T(8,128)S(1)}, u32[]{:S(2)}, u32[]{:S(2)}) collective-permute-start(f32[128,128]{1,0:T(8,128)S(1)} %get-tuple-element.46), channel_id=1, source_target_pairs={{0,6},{2,4},{4,2},{6,0},{8,14},{10,12},{12,10},{14,8},{16,22},{18,... | collective-permute-start | bytes 196616 | tf_op jit(solution)/shard_map/ppermute | solution.py:172
  6.8 5.1 %collective-permute-start.1 = (f32[128,128]{1,0:T(8,128)S(1)}, f32[128,128]{1,0:T(8,128)S(1)}, u32[]{:S(2)}, u32[]{:S(2)}) collective-permute-start(f32[128,128]{1,0:T(8,128)S(1)} %get-tuple-element.45), channel_id=1, source_target_pairs={{0,4},{2,6},{4,0},{6,2},{8,12},{10,14},{12,8},{14,10},{16,20},{18,... | collective-permute-start | bytes 196616 | tf_op jit(solution)/shard_map/ppermute | solution.py:172
  7.3 4.6 %collective-permute-start = (f32[128,128]{1,0:T(8,128)S(1)}, f32[128,128]{1,0:T(8,128)S(1)}, u32[]{:S(2)}, u32[]{:S(2)}) collective-permute-start(f32[128,128]{1,0:T(8,128)S(1)} %get-tuple-element.44), channel_id=1, source_target_pairs={{0,2},{2,0},{4,6},{6,4},{8,10},{10,8},{12,14},{14,12},{16,18},{18,... | collective-permute-start | bytes 196616 | tf_op jit(solution)/shard_map/ppermute | solution.py:172
  7.4 6.2 %collective-permute-start.10 = (f32[128,128]{1,0:T(8,128)S(1)}, f32[128,128]{1,0:T(8,128)S(1)}, u32[]{:S(2)}, u32[]{:S(2)}) collective-permute-start(f32[128,128]{1,0:T(8,128)S(1)} %get-tuple-element.55), channel_id=1, source_target_pairs={{0,6},{2,4},{4,2},{6,0},{8,14},{10,12},{12,10},{14,8},{16,22},{18,... | collective-permute-start | bytes 196616 | tf_op jit(solution)/shard_map/ppermute | solution.py:172
  10.2 4.3 %collective-permute-start.9 = (f32[128,128]{1,0:T(8,128)S(1)}, f32[128,128]{1,0:T(8,128)S(1)}, u32[]{:S(2)}, u32[]{:S(2)}) collective-permute-start(f32[128,128]{1,0:T(8,128)S(1)} %get-tuple-element.54), channel_id=1, source_target_pairs={{0,4},{2,6},{4,0},{6,2},{8,12},{10,14},{12,8},{14,10},{16,20},{18,... | collective-permute-start | bytes 196616 | tf_op jit(solution)/shard_map/ppermute | solution.py:172
  10.8 4.3 %collective-permute-start.8 = (f32[128,128]{1,0:T(8,128)S(1)}, f32[128,128]{1,0:T(8,128)S(1)}, u32[]{:S(2)}, u32[]{:S(2)}) collective-permute-start(f32[128,128]{1,0:T(8,128)S(1)} %get-tuple-element.53), channel_id=1, source_target_pairs={{0,2},{2,0},{4,6},{6,4},{8,10},{10,8},{12,14},{14,12},{16,18},{18,... | collective-permute-start | bytes 196616 | tf_op jit(solution)/shard_map/ppermute | solution.py:172
  11.8 5.0 %collective-permute-start.3 = (f32[128,128]{1,0:T(8,128)S(1)}, f32[128,128]{1,0:T(8,128)S(1)}, u32[]{:S(2)}, u32[]{:S(2)}) collective-permute-start(f32[128,128]{1,0:T(8,128)S(1)} %add_add_fusion.3), channel_id=1, source_target_pairs={{0,8},{2,10},{4,12},{6,14},{8,0},{10,2},{12,4},{14,6},{16,24},{18,... | collective-permute-start | bytes 196616 | tf_op jit(solution)/shard_map/ppermute | solution.py:172
  15.0 4.5 %collective-permute-start.11 = (f32[128,128]{1,0:T(8,128)S(1)}, f32[128,128]{1,0:T(8,128)S(1)}, u32[]{:S(2)}, u32[]{:S(2)}) collective-permute-start(f32[128,128]{1,0:T(8,128)S(1)} %add_add_fusion.2), channel_id=1, source_target_pairs={{0,8},{2,10},{4,12},{6,14},{8,0},{10,2},{12,4},{14,6},{16,24},{18,... | collective-permute-start | bytes 196616 | tf_op jit(solution)/shard_map/ppermute | solution.py:172
  16.9 6.6 %collective-permute-start.4 = (f32[128,128]{1,0:T(8,128)S(1)}, f32[128,128]{1,0:T(8,128)S(1)}, u32[]{:S(2)}, u32[]{:S(2)}) collective-permute-start(f32[128,128]{1,0:T(8,128)S(1)} %add.66), channel_id=1, source_target_pairs={{0,16},{2,18},{4,20},{6,22},{8,24},{10,26},{12,28},{14,30},{16,0},... | collective-permute-start | bytes 196616 | tf_op jit(solution)/shard_map/ppermute | solution.py:172
  19.5 8.2 %collective-permute-start.12 = (f32[128,128]{1,0:T(8,128)S(1)}, f32[128,128]{1,0:T(8,128)S(1)}, u32[]{:S(2)}, u32[]{:S(2)}) collective-permute-start(f32[128,128]{1,0:T(8,128)S(1)} %add.71), channel_id=1, source_target_pairs={{0,16},{2,18},{4,20},{6,22},{8,24},{10,26},{12,28},{14,30},{16,0},... | collective-permute-start | bytes 196616 | tf_op jit(solution)/shard_map/ppermute | solution.py:172
  24.1 7.7 %collective-permute-start.5 = (f32[128,128]{1,0:T(8,128)S(1)}, f32[128,128]{1,0:T(8,128)S(1)}, u32[]{:S(2)}, u32[]{:S(2)}) collective-permute-start(f32[128,128]{1,0:T(8,128)S(1)} %get-tuple-element.48), channel_id=1, source_target_pairs={{0,2},{2,0},{4,6},{6,4},{8,10},{10,8},{12,14},{14,12},{16,18},{18,... | collective-permute-start | bytes 196616 | tf_op jit(solution)/shard_map/ppermute | solution.py:172
  24.6 8.9 %collective-permute-start.6 = (f32[128,128]{1,0:T(8,128)S(1)}, f32[128,128]{1,0:T(8,128)S(1)}, u32[]{:S(2)}, u32[]{:S(2)}) collective-permute-start(f32[128,128]{1,0:T(8,128)S(1)} %get-tuple-element.49), channel_id=1, source_target_pairs={{0,4},{2,6},{4,0},{6,2},{8,12},{10,14},{12,8},{14,10},{16,20},{18,... | collective-permute-start | bytes 196616 | tf_op jit(solution)/shard_map/ppermute | solution.py:172
  26.1 7.4 %collective-permute-start.7 = (f32[128,128]{1,0:T(8,128)S(1)}, f32[128,128]{1,0:T(8,128)S(1)}, u32[]{:S(2)}, u32[]{:S(2)}) collective-permute-start(f32[128,128]{1,0:T(8,128)S(1)} %get-tuple-element.50), channel_id=1, source_target_pairs={{0,6},{2,4},{4,2},{6,0},{8,14},{10,12},{12,10},{14,8},{16,22},{18,... | collective-permute-start | bytes 196616 | tf_op jit(solution)/shard_map/ppermute | solution.py:172
  28.3 8.4 %collective-permute-start.13 = (f32[128,128]{1,0:T(8,128)S(1)}, f32[128,128]{1,0:T(8,128)S(1)}, u32[]{:S(2)}, u32[]{:S(2)}) collective-permute-start(f32[128,128]{1,0:T(8,128)S(1)} %get-tuple-element.57), channel_id=1, source_target_pairs={{0,2},{2,0},{4,6},{6,4},{8,10},{10,8},{12,14},{14,12},{16,18},{18,... | collective-permute-start | bytes 196616 | tf_op jit(solution)/shard_map/ppermute | solution.py:172
  30.3 8.0 %collective-permute-start.14 = (f32[128,128]{1,0:T(8,128)S(1)}, f32[128,128]{1,0:T(8,128)S(1)}, u32[]{:S(2)}, u32[]{:S(2)}) collective-permute-start(f32[128,128]{1,0:T(8,128)S(1)} %get-tuple-element.58), channel_id=1, source_target_pairs={{0,4},{2,6},{4,0},{6,2},{8,12},{10,14},{12,8},{14,10},{16,20},{18,... | collective-permute-start | bytes 196616 | tf_op jit(solution)/shard_map/ppermute | solution.py:172
  31.8 6.5 %collective-permute-start.15 = (f32[128,128]{1,0:T(8,128)S(1)}, f32[128,128]{1,0:T(8,128)S(1)}, u32[]{:S(2)}, u32[]{:S(2)}) collective-permute-start(f32[128,128]{1,0:T(8,128)S(1)} %get-tuple-element.59), channel_id=1, source_target_pairs={{0,6},{2,4},{4,2},{6,0},{8,14},{10,12},{12,10},{14,8},{16,22},{18,... | collective-permute-start | bytes 196616 | tf_op jit(solution)/shard_map/ppermute | solution.py:172
  34.7 6.8 %collective-permute-start.18 = (f32[136,128]{1,0:T(8,128)S(1)}, f32[136,128]{1,0:T(8,128)S(1)}, u32[]{:S(2)}, u32[]{:S(2)}) collective-permute-start(f32[136,128]{1,0:T(8,128)S(1)} %get-tuple-element.67), channel_id=1, source_target_pairs={{0,6},{2,4},{4,2},{6,0},{8,14},{10,12},{12,10},{14,8},{16,22},{18,... | collective-permute-start | bytes 208904 | tf_op jit(solution)/shard_map/ppermute | solution.py:172
  36.1 7.0 %collective-permute-start.17 = (f32[136,128]{1,0:T(8,128)S(1)}, f32[136,128]{1,0:T(8,128)S(1)}, u32[]{:S(2)}, u32[]{:S(2)}) collective-permute-start(f32[136,128]{1,0:T(8,128)S(1)} %get-tuple-element.66), channel_id=1, source_target_pairs={{0,4},{2,6},{4,0},{6,2},{8,12},{10,14},{12,8},{14,10},{16,20},{18,... | collective-permute-start | bytes 208904 | tf_op jit(solution)/shard_map/ppermute | solution.py:172
  36.7 6.5 %collective-permute-start.16 = (f32[136,128]{1,0:T(8,128)S(1)}, f32[136,128]{1,0:T(8,128)S(1)}, u32[]{:S(2)}, u32[]{:S(2)}) collective-permute-start(f32[136,128]{1,0:T(8,128)S(1)} %get-tuple-element.65), channel_id=1, source_target_pairs={{0,2},{2,0},{4,6},{6,4},{8,10},{10,8},{12,14},{14,12},{16,18},{18,... | collective-permute-start | bytes 208904 | tf_op jit(solution)/shard_map/ppermute | solution.py:172
  39.6 5.3 %collective-permute-start.26 = (f32[136,128]{1,0:T(8,128)S(1)}, f32[136,128]{1,0:T(8,128)S(1)}, u32[]{:S(2)}, u32[]{:S(2)}) collective-permute-start(f32[136,128]{1,0:T(8,128)S(1)} %get-tuple-element.75), channel_id=1, source_target_pairs={{0,6},{2,4},{4,2},{6,0},{8,14},{10,12},{12,10},{14,8},{16,22},{18,... | collective-permute-start | bytes 208904 | tf_op jit(solution)/shard_map/ppermute | solution.py:172
  41.0 4.6 %collective-permute-start.25 = (f32[136,128]{1,0:T(8,128)S(1)}, f32[136,128]{1,0:T(8,128)S(1)}, u32[]{:S(2)}, u32[]{:S(2)}) collective-permute-start(f32[136,128]{1,0:T(8,128)S(1)} %get-tuple-element.74), channel_id=1, source_target_pairs={{0,4},{2,6},{4,0},{6,2},{8,12},{10,14},{12,8},{14,10},{16,20},{18,... | collective-permute-start | bytes 208904 | tf_op jit(solution)/shard_map/ppermute | solution.py:172
  41.5 4.3 %collective-permute-start.24 = (f32[136,128]{1,0:T(8,128)S(1)}, f32[136,128]{1,0:T(8,128)S(1)}, u32[]{:S(2)}, u32[]{:S(2)}) collective-permute-start(f32[136,128]{1,0:T(8,128)S(1)} %get-tuple-element.73), channel_id=1, source_target_pairs={{0,2},{2,0},{4,6},{6,4},{8,10},{10,8},{12,14},{14,12},{16,18},{18,... | collective-permute-start | bytes 208904 | tf_op jit(solution)/shard_map/ppermute | solution.py:172
  43.2 4.4 %collective-permute-start.19 = (f32[136,128]{1,0:T(8,128)S(1)}, f32[136,128]{1,0:T(8,128)S(1)}, u32[]{:S(2)}, u32[]{:S(2)}) collective-permute-start(f32[136,128]{1,0:T(8,128)S(1)} %add_add_fusion.1), channel_id=1, source_target_pairs={{0,8},{2,10},{4,12},{6,14},{8,0},{10,2},{12,4},{14,6},{16,24},{18,... | collective-permute-start | bytes 208904 | tf_op jit(solution)/shard_map/ppermute | solution.py:172
  45.8 4.4 %collective-permute-start.27 = (f32[136,128]{1,0:T(8,128)S(1)}, f32[136,128]{1,0:T(8,128)S(1)}, u32[]{:S(2)}, u32[]{:S(2)}) collective-permute-start(f32[136,128]{1,0:T(8,128)S(1)} %add_add_fusion), channel_id=1, source_target_pairs={{0,8},{2,10},{4,12},{6,14},{8,0},{10,2},{12,4},{14,6},{16,24},{18,... | collective-permute-start | bytes 208904 | tf_op jit(solution)/shard_map/ppermute | solution.py:172
  47.6 6.0 %collective-permute-start.20 = (f32[136,128]{1,0:T(8,128)S(1)}, f32[136,128]{1,0:T(8,128)S(1)}, u32[]{:S(2)}, u32[]{:S(2)}) collective-permute-start(f32[136,128]{1,0:T(8,128)S(1)} %add.76), channel_id=1, source_target_pairs={{0,16},{2,18},{4,20},{6,22},{8,24},{10,26},{12,28},{14,30},{16,0},... | collective-permute-start | bytes 208904 | tf_op jit(solution)/shard_map/ppermute | solution.py:172
  50.2 7.5 %collective-permute-start.28 = (f32[136,128]{1,0:T(8,128)S(1)}, f32[136,128]{1,0:T(8,128)S(1)}, u32[]{:S(2)}, u32[]{:S(2)}) collective-permute-start(f32[136,128]{1,0:T(8,128)S(1)} %add.81), channel_id=1, source_target_pairs={{0,16},{2,18},{4,20},{6,22},{8,24},{10,26},{12,28},{14,30},{16,0},... | collective-permute-start | bytes 208904 | tf_op jit(solution)/shard_map/ppermute | solution.py:172
  54.2 6.7 %collective-permute-start.21 = (f32[136,128]{1,0:T(8,128)S(1)}, f32[136,128]{1,0:T(8,128)S(1)}, u32[]{:S(2)}, u32[]{:S(2)}) collective-permute-start(f32[136,128]{1,0:T(8,128)S(1)} %get-tuple-element.69), channel_id=1, source_target_pairs={{0,2},{2,0},{4,6},{6,4},{8,10},{10,8},{12,14},{14,12},{16,18},{18,... | collective-permute-start | bytes 208904 | tf_op jit(solution)/shard_map/ppermute | solution.py:172
  55.3 10.3 %collective-permute-start.22 = (f32[136,128]{1,0:T(8,128)S(1)}, f32[136,128]{1,0:T(8,128)S(1)}, u32[]{:S(2)}, u32[]{:S(2)}) collective-permute-start(f32[136,128]{1,0:T(8,128)S(1)} %get-tuple-element.70), channel_id=1, source_target_pairs={{0,4},{2,6},{4,0},{6,2},{8,12},{10,14},{12,8},{14,10},{16,20},{18,... | collective-permute-start | bytes 208904 | tf_op jit(solution)/shard_map/ppermute | solution.py:172
  56.7 8.9 %collective-permute-start.23 = (f32[136,128]{1,0:T(8,128)S(1)}, f32[136,128]{1,0:T(8,128)S(1)}, u32[]{:S(2)}, u32[]{:S(2)}) collective-permute-start(f32[136,128]{1,0:T(8,128)S(1)} %get-tuple-element.71), channel_id=1, source_target_pairs={{0,6},{2,4},{4,2},{6,0},{8,14},{10,12},{12,10},{14,8},{16,22},{18,... | collective-permute-start | bytes 208904 | tf_op jit(solution)/shard_map/ppermute | solution.py:172
  58.4 7.2 %collective-permute-start.29 = (f32[136,128]{1,0:T(8,128)S(1)}, f32[136,128]{1,0:T(8,128)S(1)}, u32[]{:S(2)}, u32[]{:S(2)}) collective-permute-start(f32[136,128]{1,0:T(8,128)S(1)} %get-tuple-element.77), channel_id=1, source_target_pairs={{0,2},{2,0},{4,6},{6,4},{8,10},{10,8},{12,14},{14,12},{16,18},{18,... | collective-permute-start | bytes 208904 | tf_op jit(solution)/shard_map/ppermute | solution.py:172
  59.4 6.2 %collective-permute-start.30 = (f32[136,128]{1,0:T(8,128)S(1)}, f32[136,128]{1,0:T(8,128)S(1)}, u32[]{:S(2)}, u32[]{:S(2)}) collective-permute-start(f32[136,128]{1,0:T(8,128)S(1)} %get-tuple-element.78), channel_id=1, source_target_pairs={{0,4},{2,6},{4,0},{6,2},{8,12},{10,14},{12,8},{14,10},{16,20},{18,... | collective-permute-start | bytes 208904 | tf_op jit(solution)/shard_map/ppermute | solution.py:172
  60.9 5.2 %collective-permute-start.31 = (f32[136,128]{1,0:T(8,128)S(1)}, f32[136,128]{1,0:T(8,128)S(1)}, u32[]{:S(2)}, u32[]{:S(2)}) collective-permute-start(f32[136,128]{1,0:T(8,128)S(1)} %get-tuple-element.79), channel_id=1, source_target_pairs={{0,6},{2,4},{4,2},{6,0},{8,14},{10,12},{12,10},{14,8},{16,22},{18,... | collective-permute-start | bytes 208904 | tf_op jit(solution)/shard_map/ppermute | solution.py:172
  (6 other events, 32.6 us)

commit v11 on v10

--- a/solution.py
+++ b/solution.py
@@ -33,7 +33,7 @@
 
 
 def own_columns(place_ref, mask, chain=0):
-    return pl.ds(pl.multiple_of(chain * WIDE + (place_ref[0] ^ mask) * DH, DH), DH)
+    return pl.ds(pl.multiple_of(chain * WIDE + (place_ref[0] & (GROUP - 1) ^ mask) * DH, DH), DH)
 
 
 def causal(turned=False):
@@ -115,25 +115,25 @@
 
 def gain_body(place_ref, *refs):
     for at_head, state_ref in enumerate(refs[:-1]):
-        row = (at_head // GROUP) * GROUP + (place_ref[0] ^ (at_head % GROUP))
+        row = (at_head // GROUP) * GROUP + (place_ref[0] & (GROUP - 1) ^ (at_head % GROUP))
         refs[-1][pl.ds(row, 1), :] = state_ref[DH : DH + 1]
 
 
-def prefix_body(reverse, place_ref, *refs):
+def prefix_body(reverse, masks, place_ref, *refs):
     (total_ref, *arrived_refs), (*back_refs, ahead) = refs[: -2 * GROUP - 1], refs[-GROUP - 1 :]
     held_refs = refs[-2 * GROUP - 1 : -GROUP - 1]
     for mask, held_ref in enumerate(held_refs):
-        ahead[pl.ds(place_ref[0] ^ mask, 1)] = held_ref[:DH][None]
+        ahead[pl.ds(place_ref[0] & (GROUP - 1) ^ mask, 1)] = held_ref[:DH][None]
     running = jnp.zeros((DH, DH), jnp.float32)
-    for step, arrived_ref in enumerate(arrived_refs):
-        later = (place_ref[step + 1] != 0) != reverse
+    for mask, arrived_ref in zip(masks, arrived_refs):
+        later = (place_ref[0] & mask == 0) == reverse
         running = running + jnp.where(later, arrived_ref[:DH], 0.0)
     for member in reversed(range(GROUP)) if reverse else range(GROUP):
         own = ahead[member]
         ahead[member] = running
         running = running + own
     for mask, back_ref in enumerate(back_refs):
-        back_ref[:DH] = ahead[pl.ds(place_ref[0] ^ mask, 1)][0]
+        back_ref[:DH] = ahead[pl.ds(place_ref[0] & (GROUP - 1) ^ mask, 1)][0]
         if back_ref.shape[0] > DH:
             back_ref[DH:] = total_ref[DH:]
 
@@ -181,7 +181,7 @@
         total = total + arrived[-1]
     single = whole(*total.shape)
     back = call(
-        functools.partial(prefix_body, reverse),
+        functools.partial(prefix_body, reverse, exchange_masks()),
         [single] * (1 + len(arrived) + GROUP),
         [single] * GROUP,
         [jax.ShapeDtypeStruct(total.shape, jnp.float32)] * GROUP,
@@ -206,8 +206,7 @@
     short, tall, wide, half = whole(*square.shape), whole(*taller.shape), whole(*flat), whole(BLOCK, WIDE)
     unit = 2 * BLOCK * DH * DH * HEADS
 
-    at = lax.axis_index("seq")
-    place = jnp.stack([lax.rem(at, GROUP)] + [at & mask for mask in exchange_masks()]).astype(jnp.int32)
+    place = lax.axis_index("seq").astype(jnp.int32).reshape(1)
     deltas = call(
         delta_body,
         [pl.BlockSpec(memory_space=pltpu.HBM)] * 2,

time: 69.7 us -> 63.7 us (0.914)
  Pallas kernels: 14.9 us -> 8.97 us
    pallas_call x4, Pallas kernels: 2.42 us -> 0.32 us  [carried_in(): call(functools.partial(prefix_body, reverse, exchange_masks()), [single]...]
    pallas_call x2, Pallas kernels: 2.55 us -> 1.48 us  [local(): call(functools.partial(norm_body, chain), [wide, wide, wide, whole(1, HEA...]
  transfers between devices with their start and end apart: 33 -> 33, of which waited for: 13 -> 12; matrix products, arithmetic and copies ran while one was open for 0% -> 0% of each run, Pallas kernels for 18% -> 12%
where the time goes in v11:
time: 63.7 us; the launch traced here: 63.5 us
  starting transfers between devices  44 us (69%)
  Pallas kernels  8.97 us (14%)
  waiting for transfers between devices  8.96 us (14%)
  between operations  0.83 us (1%)
  other arithmetic  0.75 us (1%)
    ppermute x32, starting transfers between devices, swap(): lax.ppermute(array, 'seq', [(s, s ^ mask) for s in range(lax.axis_size('s...  43.9 us
    ppermute x32, waiting for transfers between devices, swap(): lax.ppermute(array, 'seq', [(s, s ^ mask) for s in range(lax.axis_size('s...  8.96 us
    pallas_call x1, Pallas kernels, local(): call(partial_body, [wide] * 3 + [half] * CHAINS + [short] * HEADS, [wide]...  3.09 us
    pallas_call x1, Pallas kernels, local(): call(final_body, [wide] * 4 + [tall] * HEADS, [chunk] * 2, [full_low] * 2...  1.61 us
    pallas_call x1, Pallas kernels, local(): call(delta_body, [pl.BlockSpec(memory_space=pltpu.HBM)] * 2, [short] * HE...  1.53 us
    pallas_call x2, Pallas kernels, local(): call(functools.partial(norm_body, chain), [wide, wide, wide, whole(1, HEA...  1.48 us
  transfers between devices with their start and end apart: 33, of which 12 were waited for; matrix products, arithmetic and copies ran while one was open for 0% of the time, Pallas kernels for 12%

profile of v11, /device:TPU:0, one launch (start us, length us, event | category | flops | bytes accessed | tf_op | source)
XLA Modules:
  0.0 63.5 jit_solution(1751634351450172735)
XLA Ops:
  0.6 1.5 %delta.1 = (f32[128,128]{1,0:T(8,128)S(1)}, f32[128,128]{1,0:T(8,128)S(1)}, f32[128,128]{1,0:T(8,128)S(1)}, f32[128,128]{1,0:T(8,128)S(1)}, f32[128,128]{1,0:T(8...) custom-call(s32[1]{0:T(128)} %bitcast.place_ref, bf16[256,1024]{1,0:T(8,128)(2,1)} %bitcast.19, ...), custom_call_target="tpu_custom_call" | custom-call | flops 402653184 | bytes 2097152 | tf_op jit(solution)/shard_map/delta/pallas_call | solution.py:210
  2.2 4.0 %collective-permute-start.2 = (f32[128,128]{1,0:T(8,128)S(1)}, f32[128,128]{1,0:T(8,128)S(1)}, u32[]{:S(2)}, u32[]{:S(2)}) collective-permute-start(f32[128,128]{1,0:T(8,128)S(1)} %get-tuple-element.46), channel_id=1, source_target_pairs={{0,6},{2,4},{4,2},{6,0},{8,14},{10,12},{12,10},{14,8},{16,22},{18,... | collective-permute-start | bytes 196616 | tf_op jit(solution)/shard_map/ppermute | solution.py:172
  6.8 2.8 %collective-permute-start.10 = (f32[128,128]{1,0:T(8,128)S(1)}, f32[128,128]{1,0:T(8,128)S(1)}, u32[]{:S(2)}, u32[]{:S(2)}) collective-permute-start(f32[128,128]{1,0:T(8,128)S(1)} %get-tuple-element.55), channel_id=1, source_target_pairs={{0,6},{2,4},{4,2},{6,0},{8,14},{10,12},{12,10},{14,8},{16,22},{18,... | collective-permute-start | bytes 196616 | tf_op jit(solution)/shard_map/ppermute | solution.py:172
  11.2 1.7 %collective-permute-start.3 = (f32[128,128]{1,0:T(8,128)S(1)}, f32[128,128]{1,0:T(8,128)S(1)}, u32[]{:S(2)}, u32[]{:S(2)}) collective-permute-start(f32[128,128]{1,0:T(8,128)S(1)} %add_add_fusion.3), channel_id=1, source_target_pairs={{0,8},{2,10},{4,12},{6,14},{8,0},{10,2},{12,4},{14,6},{16,24},{18,... | collective-permute-start | bytes 196616 | tf_op jit(solution)/shard_map/ppermute | solution.py:172
  13.0 0.9 %collective-permute-done.9.refs_5_ = f32[128,128]{1,0:T(8,128)S(1)} collective-permute-done((f32[128,128]{1,0:T(8,128)S(1)}, f32[128,128]{1,0:T(8,128)S(1)}, u32[]{:S(2)}, u32[]{:S(2)}) %collective-permute-start.9) | collective-permute-done | bytes 65568 | tf_op jit(solution)/shard_map/ppermute | solution.py:172
  14.4 1.6 %collective-permute-start.11 = (f32[128,128]{1,0:T(8,128)S(1)}, f32[128,128]{1,0:T(8,128)S(1)}, u32[]{:S(2)}, u32[]{:S(2)}) collective-permute-start(f32[128,128]{1,0:T(8,128)S(1)} %add_add_fusion.2), channel_id=1, source_target_pairs={{0,8},{2,10},{4,12},{6,14},{8,0},{10,2},{12,4},{14,6},{16,24},{18,... | collective-permute-start | bytes 196616 | tf_op jit(solution)/shard_map/ppermute | solution.py:172
  16.2 2.6 %collective-permute-start.4 = (f32[128,128]{1,0:T(8,128)S(1)}, f32[128,128]{1,0:T(8,128)S(1)}, u32[]{:S(2)}, u32[]{:S(2)}) collective-permute-start(f32[128,128]{1,0:T(8,128)S(1)} %add.66), channel_id=1, source_target_pairs={{0,16},{2,18},{4,20},{6,22},{8,24},{10,26},{12,28},{14,30},{16,0},... | collective-permute-start | bytes 196616 | tf_op jit(solution)/shard_map/ppermute | solution.py:172
  18.9 2.5 %collective-permute-start.12 = (f32[128,128]{1,0:T(8,128)S(1)}, f32[128,128]{1,0:T(8,128)S(1)}, u32[]{:S(2)}, u32[]{:S(2)}) collective-permute-start(f32[128,128]{1,0:T(8,128)S(1)} %add.71), channel_id=1, source_target_pairs={{0,16},{2,18},{4,20},{6,22},{8,24},{10,26},{12,28},{14,30},{16,0},... | collective-permute-start | bytes 196616 | tf_op jit(solution)/shard_map/ppermute | solution.py:172
  21.4 1.5 %collective-permute-done.4.refs_2_ = f32[128,128]{1,0:T(8,128)S(1)} collective-permute-done((f32[128,128]{1,0:T(8,128)S(1)}, f32[128,128]{1,0:T(8,128)S(1)}, u32[]{:S(2)}, u32[]{:S(2)}) %collective-permute-start.4) | collective-permute-done | bytes 65568 | tf_op jit(solution)/shard_map/ppermute | solution.py:172
  23.4 1.5 %collective-permute-start.6 = (f32[128,128]{1,0:T(8,128)S(1)}, f32[128,128]{1,0:T(8,128)S(1)}, u32[]{:S(2)}, u32[]{:S(2)}) collective-permute-start(f32[128,128]{1,0:T(8,128)S(1)} %get-tuple-element.49), channel_id=1, source_target_pairs={{0,4},{2,6},{4,0},{6,2},{8,12},{10,14},{12,8},{14,10},{16,20},{18,... | collective-permute-start | bytes 196616 | tf_op jit(solution)/shard_map/ppermute | solution.py:172
  24.9 1.6 %collective-permute-start.7 = (f32[128,128]{1,0:T(8,128)S(1)}, f32[128,128]{1,0:T(8,128)S(1)}, u32[]{:S(2)}, u32[]{:S(2)}) collective-permute-start(f32[128,128]{1,0:T(8,128)S(1)} %get-tuple-element.50), channel_id=1, source_target_pairs={{0,6},{2,4},{4,2},{6,0},{8,14},{10,12},{12,10},{14,8},{16,22},{18,... | collective-permute-start | bytes 196616 | tf_op jit(solution)/shard_map/ppermute | solution.py:172
  27.1 0.9 %inner.1.inner_ref = f32[256,1024]{1,0:T(8,128)S(1)} custom-call(s32[1]{0:T(128)} %bitcast.place_ref, bf16[256,1024]{1,0:T(8,128)(2,1)S(1)} %bitcast.13, bf16[256,1024]{1,0:T(8,128)(2,1)S(1)} %bitcast.20, bf16[256,1024]{1,0:T(8,128)(2,1)S(1)} %bitcast.24), custom_call_target="tpu_custom_call" | custom-call | flops 1073741824 | bytes 2097152 | tf_op jit(solution)/shard_map/inner/pallas_call | solution.py:221
  28.1 1.5 %collective-permute-start.14 = (f32[128,128]{1,0:T(8,128)S(1)}, f32[128,128]{1,0:T(8,128)S(1)}, u32[]{:S(2)}, u32[]{:S(2)}) collective-permute-start(f32[128,128]{1,0:T(8,128)S(1)} %get-tuple-element.58), channel_id=1, source_target_pairs={{0,4},{2,6},{4,0},{6,2},{8,12},{10,14},{12,8},{14,10},{16,20},{18,... | collective-permute-start | bytes 196616 | tf_op jit(solution)/shard_map/ppermute | solution.py:172
  29.6 1.6 %collective-permute-start.15 = (f32[128,128]{1,0:T(8,128)S(1)}, f32[128,128]{1,0:T(8,128)S(1)}, u32[]{:S(2)}, u32[]{:S(2)}) collective-permute-start(f32[128,128]{1,0:T(8,128)S(1)} %get-tuple-element.59), channel_id=1, source_target_pairs={{0,6},{2,4},{4,2},{6,0},{8,14},{10,12},{12,10},{14,8},{16,22},{18,... | collective-permute-start | bytes 196616 | tf_op jit(solution)/shard_map/ppermute | solution.py:172
  31.3 0.7 %norm.2 = (bf16[256,512]{1,0:T(8,128)(2,1)S(1)}, f32[136,128]{1,0:T(8,128)S(1)}, f32[136,128]{1,0:T(8,128)S(1)}, f32[136,128]{1,0:T(8,128)S(1)}, f32[136,128]{1,0:T(8,128)S(1)}) custom-call(s32[1]{0:T(128)} %bitcast.place_ref, bf16[256,1024]{1,0:T(8,128)(2,1)S(1)} %bitcast.14, bf16[256,1024]{1,0:T(8,128)(2,1)S(1)} %bitcast.11, ...), custom_call_target="tpu_custom_call" | custom-call | flops 536870912 | bytes 2097152 | tf_op jit(solution)/shard_map/norm/pallas_call | solution.py:226
  32.0 1.4 %collective-permute-start.18 = (f32[136,128]{1,0:T(8,128)S(1)}, f32[136,128]{1,0:T(8,128)S(1)}, u32[]{:S(2)}, u32[]{:S(2)}) collective-permute-start(f32[136,128]{1,0:T(8,128)S(1)} %get-tuple-element.67), channel_id=1, source_target_pairs={{0,6},{2,4},{4,2},{6,0},{8,14},{10,12},{12,10},{14,8},{16,22},{18,... | collective-permute-start | bytes 208904 | tf_op jit(solution)/shard_map/ppermute | solution.py:172
  33.9 1.6 %collective-permute-start.16 = (f32[136,128]{1,0:T(8,128)S(1)}, f32[136,128]{1,0:T(8,128)S(1)}, u32[]{:S(2)}, u32[]{:S(2)}) collective-permute-start(f32[136,128]{1,0:T(8,128)S(1)} %get-tuple-element.65), channel_id=1, source_target_pairs={{0,2},{2,0},{4,6},{6,4},{8,10},{10,8},{12,14},{14,12},{16,18},{18,... | collective-permute-start | bytes 208904 | tf_op jit(solution)/shard_map/ppermute | solution.py:172
  35.6 0.7 %norm.3 = (bf16[256,512]{1,0:T(8,128)(2,1)S(1)}, f32[136,128]{1,0:T(8,128)S(1)}, f32[136,128]{1,0:T(8,128)S(1)}, f32[136,128]{1,0:T(8,128)S(1)}, f32[136,128]{1,0:T(8,128)S(1)}) custom-call(s32[1]{0:T(128)} %bitcast.place_ref, bf16[256,1024]{1,0:T(8,128)(2,1)S(1)} %bitcast.15, bf16[256,1024]{1,0:T(8,128)(2,1)S(1)} %bitcast.12, ...), custom_call_target="tpu_custom_call" | custom-call | flops 536870912 | bytes 2097152 | tf_op jit(solution)/shard_map/norm/pallas_call | solution.py:226
  36.3 1.4 %collective-permute-start.26 = (f32[136,128]{1,0:T(8,128)S(1)}, f32[136,128]{1,0:T(8,128)S(1)}, u32[]{:S(2)}, u32[]{:S(2)}) collective-permute-start(f32[136,128]{1,0:T(8,128)S(1)} %get-tuple-element.75), channel_id=1, source_target_pairs={{0,6},{2,4},{4,2},{6,0},{8,14},{10,12},{12,10},{14,8},{16,22},{18,... | collective-permute-start | bytes 208904 | tf_op jit(solution)/shard_map/ppermute | solution.py:172
  37.7 0.9 %collective-permute-start.25 = (f32[136,128]{1,0:T(8,128)S(1)}, f32[136,128]{1,0:T(8,128)S(1)}, u32[]{:S(2)}, u32[]{:S(2)}) collective-permute-start(f32[136,128]{1,0:T(8,128)S(1)} %get-tuple-element.74), channel_id=1, source_target_pairs={{0,4},{2,6},{4,0},{6,2},{8,12},{10,14},{12,8},{14,10},{16,20},{18,... | collective-permute-start | bytes 208904 | tf_op jit(solution)/shard_map/ppermute | solution.py:172
  38.6 1.3 %collective-permute-start.24 = (f32[136,128]{1,0:T(8,128)S(1)}, f32[136,128]{1,0:T(8,128)S(1)}, u32[]{:S(2)}, u32[]{:S(2)}) collective-permute-start(f32[136,128]{1,0:T(8,128)S(1)} %get-tuple-element.73), channel_id=1, source_target_pairs={{0,2},{2,0},{4,6},{6,4},{8,10},{10,8},{12,14},{14,12},{16,18},{18,... | collective-permute-start | bytes 208904 | tf_op jit(solution)/shard_map/ppermute | solution.py:172
  40.5 1.1 %collective-permute-done.26.refs_6_ = f32[136,128]{1,0:T(8,128)S(1)} collective-permute-done((f32[136,128]{1,0:T(8,128)S(1)}, f32[136,128]{1,0:T(8,128)S(1)}, u32[]{:S(2)}, u32[]{:S(2)}) %collective-permute-start.26) | collective-permute-done | bytes 69664 | tf_op jit(solution)/shard_map/ppermute | solution.py:172
  41.6 0.7 %collective-permute-done.25.refs_5_ = f32[136,128]{1,0:T(8,128)S(1)} collective-permute-done((f32[136,128]{1,0:T(8,128)S(1)}, f32[136,128]{1,0:T(8,128)S(1)}, u32[]{:S(2)}, u32[]{:S(2)}) %collective-permute-start.25) | collective-permute-done | bytes 69664 | tf_op jit(solution)/shard_map/ppermute | solution.py:172
  43.5 1.2 %collective-permute-done.19.refs_1_ = f32[136,128]{1,0:T(8,128)S(1)} collective-permute-done((f32[136,128]{1,0:T(8,128)S(1)}, f32[136,128]{1,0:T(8,128)S(1)}, u32[]{:S(2)}, u32[]{:S(2)}) %collective-permute-start.19) | collective-permute-done | bytes 69664 | tf_op jit(solution)/shard_map/ppermute | solution.py:172
  44.8 2.3 %collective-permute-start.20 = (f32[136,128]{1,0:T(8,128)S(1)}, f32[136,128]{1,0:T(8,128)S(1)}, u32[]{:S(2)}, u32[]{:S(2)}) collective-permute-start(f32[136,128]{1,0:T(8,128)S(1)} %add.76), channel_id=1, source_target_pairs={{0,16},{2,18},{4,20},{6,22},{8,24},{10,26},{12,28},{14,30},{16,0},... | collective-permute-start | bytes 208904 | tf_op jit(solution)/shard_map/ppermute | solution.py:172
  47.3 2.0 %collective-permute-start.28 = (f32[136,128]{1,0:T(8,128)S(1)}, f32[136,128]{1,0:T(8,128)S(1)}, u32[]{:S(2)}, u32[]{:S(2)}) collective-permute-start(f32[136,128]{1,0:T(8,128)S(1)} %add.81), channel_id=1, source_target_pairs={{0,16},{2,18},{4,20},{6,22},{8,24},{10,26},{12,28},{14,30},{16,0},... | collective-permute-start | bytes 208904 | tf_op jit(solution)/shard_map/ppermute | solution.py:172
  49.4 1.4 %collective-permute-done.20.refs_2_ = f32[136,128]{1,0:T(8,128)S(1)} collective-permute-done((f32[136,128]{1,0:T(8,128)S(1)}, f32[136,128]{1,0:T(8,128)S(1)}, u32[]{:S(2)}, u32[]{:S(2)}) %collective-permute-start.20) | collective-permute-done | bytes 69664 | tf_op jit(solution)/shard_map/ppermute | solution.py:172
  51.9 2.6 %collective-permute-start.23 = (f32[136,128]{1,0:T(8,128)S(1)}, f32[136,128]{1,0:T(8,128)S(1)}, u32[]{:S(2)}, u32[]{:S(2)}) collective-permute-start(f32[136,128]{1,0:T(8,128)S(1)} %get-tuple-element.71), channel_id=1, source_target_pairs={{0,6},{2,4},{4,2},{6,0},{8,14},{10,12},{12,10},{14,8},{16,22},{18,... | collective-permute-start | bytes 208904 | tf_op jit(solution)/shard_map/ppermute | solution.py:172
  55.1 0.9 %collective-permute-start.30 = (f32[136,128]{1,0:T(8,128)S(1)}, f32[136,128]{1,0:T(8,128)S(1)}, u32[]{:S(2)}, u32[]{:S(2)}) collective-permute-start(f32[136,128]{1,0:T(8,128)S(1)} %get-tuple-element.78), channel_id=1, source_target_pairs={{0,4},{2,6},{4,0},{6,2},{8,12},{10,14},{12,8},{14,10},{16,20},{18,... | collective-permute-start | bytes 208904 | tf_op jit(solution)/shard_map/ppermute | solution.py:172
  56.0 2.1 %collective-permute-start.31 = (f32[136,128]{1,0:T(8,128)S(1)}, f32[136,128]{1,0:T(8,128)S(1)}, u32[]{:S(2)}, u32[]{:S(2)}) collective-permute-start(f32[136,128]{1,0:T(8,128)S(1)} %get-tuple-element.79), channel_id=1, source_target_pairs={{0,6},{2,4},{4,2},{6,0},{8,14},{10,12},{12,10},{14,8},{16,22},{18,... | collective-permute-start | bytes 208904 | tf_op jit(solution)/shard_map/ppermute | solution.py:172
  58.1 3.1 %partial.1 = (bf16[256,1024]{1,0:T(8,128)(2,1)}, f32[256,1024]{1,0:T(8,128)S(1)}, f32[256,1024]{1,0:T(8,128)S(1)}) custom-call(s32[1]{0:T(128)} %bitcast.place_ref, bf16[256,1024]{1,0:T(8,128)(2,1)S(1)} %bitcast.16, bf16[256,1024]{1,0:T(8,128)(2,1)S(1)} %bitcast.21, bf16[256,1024]{1,0:T(8,128)(2,1)S(1)} %bitcast.25, ...), custom_call_target="tpu_custom_call" | custom-call | flops 3221225472 | bytes 2097152 | tf_op jit(solution)/shard_map/partial/pallas_call | solution.py:236
  61.3 1.6 %final.1 = (bf16[256,1024]{1,0:T(8,128)(2,1)}, bf16[256,1024]{1,0:T(8,128)(2,1)}) custom-call(s32[1]{0:T(128)} %bitcast.place_ref, bf16[256,1024]{1,0:T(8,128)(2,1)S(1)} %bitcast.22, bf16[256,1024]{1,0:T(8,128)(2,1)S(1)} %bitcast.26, f32[256,1024]{1,0:T(8,128)S(1)} %get-tuple-element.62.key_part_ref, f32[256,1024]{1,0:T(8,128)S(1)} %get-tuple-element.63.value_part_ref, ...), custom_call_target="tpu_custom_call" | custom-call | flops 1073741824 | bytes 2097152 | tf_op jit(solution)/shard_map/final/pallas_call | solution.py:252
  (68 shorter events, 9.2 us)
Async XLA Ops:
  2.2 8.0 %collective-permute-start.2 = (f32[128,128]{1,0:T(8,128)S(1)}, f32[128,128]{1,0:T(8,128)S(1)}, u32[]{:S(2)}, u32[]{:S(2)}) collective-permute-start(f32[128,128]{1,0:T(8,128)S(1)} %get-tuple-element.46), channel_id=1, source_target_pairs={{0,6},{2,4},{4,2},{6,0},{8,14},{10,12},{12,10},{14,8},{16,22},{18,... | collective-permute-start | bytes 196616 | tf_op jit(solution)/shard_map/ppermute | solution.py:172
  6.1 5.1 %collective-permute-start.1 = (f32[128,128]{1,0:T(8,128)S(1)}, f32[128,128]{1,0:T(8,128)S(1)}, u32[]{:S(2)}, u32[]{:S(2)}) collective-permute-start(f32[128,128]{1,0:T(8,128)S(1)} %get-tuple-element.45), channel_id=1, source_target_pairs={{0,4},{2,6},{4,0},{6,2},{8,12},{10,14},{12,8},{14,10},{16,20},{18,... | collective-permute-start | bytes 196616 | tf_op jit(solution)/shard_map/ppermute | solution.py:172
  6.6 4.6 %collective-permute-start = (f32[128,128]{1,0:T(8,128)S(1)}, f32[128,128]{1,0:T(8,128)S(1)}, u32[]{:S(2)}, u32[]{:S(2)}) collective-permute-start(f32[128,128]{1,0:T(8,128)S(1)} %get-tuple-element.44), channel_id=1, source_target_pairs={{0,2},{2,0},{4,6},{6,4},{8,10},{10,8},{12,14},{14,12},{16,18},{18,... | collective-permute-start | bytes 196616 | tf_op jit(solution)/shard_map/ppermute | solution.py:172
  6.8 6.2 %collective-permute-start.10 = (f32[128,128]{1,0:T(8,128)S(1)}, f32[128,128]{1,0:T(8,128)S(1)}, u32[]{:S(2)}, u32[]{:S(2)}) collective-permute-start(f32[128,128]{1,0:T(8,128)S(1)} %get-tuple-element.55), channel_id=1, source_target_pairs={{0,6},{2,4},{4,2},{6,0},{8,14},{10,12},{12,10},{14,8},{16,22},{18,... | collective-permute-start | bytes 196616 | tf_op jit(solution)/shard_map/ppermute | solution.py:172
  9.6 4.3 %collective-permute-start.9 = (f32[128,128]{1,0:T(8,128)S(1)}, f32[128,128]{1,0:T(8,128)S(1)}, u32[]{:S(2)}, u32[]{:S(2)}) collective-permute-start(f32[128,128]{1,0:T(8,128)S(1)} %get-tuple-element.54), channel_id=1, source_target_pairs={{0,4},{2,6},{4,0},{6,2},{8,12},{10,14},{12,8},{14,10},{16,20},{18,... | collective-permute-start | bytes 196616 | tf_op jit(solution)/shard_map/ppermute | solution.py:172
  10.1 4.3 %collective-permute-start.8 = (f32[128,128]{1,0:T(8,128)S(1)}, f32[128,128]{1,0:T(8,128)S(1)}, u32[]{:S(2)}, u32[]{:S(2)}) collective-permute-start(f32[128,128]{1,0:T(8,128)S(1)} %get-tuple-element.53), channel_id=1, source_target_pairs={{0,2},{2,0},{4,6},{6,4},{8,10},{10,8},{12,14},{14,12},{16,18},{18,... | collective-permute-start | bytes 196616 | tf_op jit(solution)/shard_map/ppermute | solution.py:172
  11.2 5.0 %collective-permute-start.3 = (f32[128,128]{1,0:T(8,128)S(1)}, f32[128,128]{1,0:T(8,128)S(1)}, u32[]{:S(2)}, u32[]{:S(2)}) collective-permute-start(f32[128,128]{1,0:T(8,128)S(1)} %add_add_fusion.3), channel_id=1, source_target_pairs={{0,8},{2,10},{4,12},{6,14},{8,0},{10,2},{12,4},{14,6},{16,24},{18,... | collective-permute-start | bytes 196616 | tf_op jit(solution)/shard_map/ppermute | solution.py:172
  14.4 4.5 %collective-permute-start.11 = (f32[128,128]{1,0:T(8,128)S(1)}, f32[128,128]{1,0:T(8,128)S(1)}, u32[]{:S(2)}, u32[]{:S(2)}) collective-permute-start(f32[128,128]{1,0:T(8,128)S(1)} %add_add_fusion.2), channel_id=1, source_target_pairs={{0,8},{2,10},{4,12},{6,14},{8,0},{10,2},{12,4},{14,6},{16,24},{18,... | collective-permute-start | bytes 196616 | tf_op jit(solution)/shard_map/ppermute | solution.py:172
  16.2 6.6 %collective-permute-start.4 = (f32[128,128]{1,0:T(8,128)S(1)}, f32[128,128]{1,0:T(8,128)S(1)}, u32[]{:S(2)}, u32[]{:S(2)}) collective-permute-start(f32[128,128]{1,0:T(8,128)S(1)} %add.66), channel_id=1, source_target_pairs={{0,16},{2,18},{4,20},{6,22},{8,24},{10,26},{12,28},{14,30},{16,0},... | collective-permute-start | bytes 196616 | tf_op jit(solution)/shard_map/ppermute | solution.py:172
  18.9 7.6 %collective-permute-start.12 = (f32[128,128]{1,0:T(8,128)S(1)}, f32[128,128]{1,0:T(8,128)S(1)}, u32[]{:S(2)}, u32[]{:S(2)}) collective-permute-start(f32[128,128]{1,0:T(8,128)S(1)} %add.71), channel_id=1, source_target_pairs={{0,16},{2,18},{4,20},{6,22},{8,24},{10,26},{12,28},{14,30},{16,0},... | collective-permute-start | bytes 196616 | tf_op jit(solution)/shard_map/ppermute | solution.py:172
  23.0 6.6 %collective-permute-start.5 = (f32[128,128]{1,0:T(8,128)S(1)}, f32[128,128]{1,0:T(8,128)S(1)}, u32[]{:S(2)}, u32[]{:S(2)}) collective-permute-start(f32[128,128]{1,0:T(8,128)S(1)} %get-tuple-element.48), channel_id=1, source_target_pairs={{0,2},{2,0},{4,6},{6,4},{8,10},{10,8},{12,14},{14,12},{16,18},{18,... | collective-permute-start | bytes 196616 | tf_op jit(solution)/shard_map/ppermute | solution.py:172
  23.4 7.8 %collective-permute-start.6 = (f32[128,128]{1,0:T(8,128)S(1)}, f32[128,128]{1,0:T(8,128)S(1)}, u32[]{:S(2)}, u32[]{:S(2)}) collective-permute-start(f32[128,128]{1,0:T(8,128)S(1)} %get-tuple-element.49), channel_id=1, source_target_pairs={{0,4},{2,6},{4,0},{6,2},{8,12},{10,14},{12,8},{14,10},{16,20},{18,... | collective-permute-start | bytes 196616 | tf_op jit(solution)/shard_map/ppermute | solution.py:172
  24.9 6.3 %collective-permute-start.7 = (f32[128,128]{1,0:T(8,128)S(1)}, f32[128,128]{1,0:T(8,128)S(1)}, u32[]{:S(2)}, u32[]{:S(2)}) collective-permute-start(f32[128,128]{1,0:T(8,128)S(1)} %get-tuple-element.50), channel_id=1, source_target_pairs={{0,6},{2,4},{4,2},{6,0},{8,14},{10,12},{12,10},{14,8},{16,22},{18,... | collective-permute-start | bytes 196616 | tf_op jit(solution)/shard_map/ppermute | solution.py:172
  26.6 7.3 %collective-permute-start.13 = (f32[128,128]{1,0:T(8,128)S(1)}, f32[128,128]{1,0:T(8,128)S(1)}, u32[]{:S(2)}, u32[]{:S(2)}) collective-permute-start(f32[128,128]{1,0:T(8,128)S(1)} %get-tuple-element.57), channel_id=1, source_target_pairs={{0,2},{2,0},{4,6},{6,4},{8,10},{10,8},{12,14},{14,12},{16,18},{18,... | collective-permute-start | bytes 196616 | tf_op jit(solution)/shard_map/ppermute | solution.py:172
  28.1 7.5 %collective-permute-start.14 = (f32[128,128]{1,0:T(8,128)S(1)}, f32[128,128]{1,0:T(8,128)S(1)}, u32[]{:S(2)}, u32[]{:S(2)}) collective-permute-start(f32[128,128]{1,0:T(8,128)S(1)} %get-tuple-element.58), channel_id=1, source_target_pairs={{0,4},{2,6},{4,0},{6,2},{8,12},{10,14},{12,8},{14,10},{16,20},{18,... | collective-permute-start | bytes 196616 | tf_op jit(solution)/shard_map/ppermute | solution.py:172
  29.6 6.0 %collective-permute-start.15 = (f32[128,128]{1,0:T(8,128)S(1)}, f32[128,128]{1,0:T(8,128)S(1)}, u32[]{:S(2)}, u32[]{:S(2)}) collective-permute-start(f32[128,128]{1,0:T(8,128)S(1)} %get-tuple-element.59), channel_id=1, source_target_pairs={{0,6},{2,4},{4,2},{6,0},{8,14},{10,12},{12,10},{14,8},{16,22},{18,... | collective-permute-start | bytes 196616 | tf_op jit(solution)/shard_map/ppermute | solution.py:172
  32.0 6.6 %collective-permute-start.18 = (f32[136,128]{1,0:T(8,128)S(1)}, f32[136,128]{1,0:T(8,128)S(1)}, u32[]{:S(2)}, u32[]{:S(2)}) collective-permute-start(f32[136,128]{1,0:T(8,128)S(1)} %get-tuple-element.67), channel_id=1, source_target_pairs={{0,6},{2,4},{4,2},{6,0},{8,14},{10,12},{12,10},{14,8},{16,22},{18,... | collective-permute-start | bytes 208904 | tf_op jit(solution)/shard_map/ppermute | solution.py:172
  33.4 6.5 %collective-permute-start.17 = (f32[136,128]{1,0:T(8,128)S(1)}, f32[136,128]{1,0:T(8,128)S(1)}, u32[]{:S(2)}, u32[]{:S(2)}) collective-permute-start(f32[136,128]{1,0:T(8,128)S(1)} %get-tuple-element.66), channel_id=1, source_target_pairs={{0,4},{2,6},{4,0},{6,2},{8,12},{10,14},{12,8},{14,10},{16,20},{18,... | collective-permute-start | bytes 208904 | tf_op jit(solution)/shard_map/ppermute | solution.py:172
  33.9 6.0 %collective-permute-start.16 = (f32[136,128]{1,0:T(8,128)S(1)}, f32[136,128]{1,0:T(8,128)S(1)}, u32[]{:S(2)}, u32[]{:S(2)}) collective-permute-start(f32[136,128]{1,0:T(8,128)S(1)} %get-tuple-element.65), channel_id=1, source_target_pairs={{0,2},{2,0},{4,6},{6,4},{8,10},{10,8},{12,14},{14,12},{16,18},{18,... | collective-permute-start | bytes 208904 | tf_op jit(solution)/shard_map/ppermute | solution.py:172
  36.3 5.3 %collective-permute-start.26 = (f32[136,128]{1,0:T(8,128)S(1)}, f32[136,128]{1,0:T(8,128)S(1)}, u32[]{:S(2)}, u32[]{:S(2)}) collective-permute-start(f32[136,128]{1,0:T(8,128)S(1)} %get-tuple-element.75), channel_id=1, source_target_pairs={{0,6},{2,4},{4,2},{6,0},{8,14},{10,12},{12,10},{14,8},{16,22},{18,... | collective-permute-start | bytes 208904 | tf_op jit(solution)/shard_map/ppermute | solution.py:172
  37.7 4.6 %collective-permute-start.25 = (f32[136,128]{1,0:T(8,128)S(1)}, f32[136,128]{1,0:T(8,128)S(1)}, u32[]{:S(2)}, u32[]{:S(2)}) collective-permute-start(f32[136,128]{1,0:T(8,128)S(1)} %get-tuple-element.74), channel_id=1, source_target_pairs={{0,4},{2,6},{4,0},{6,2},{8,12},{10,14},{12,8},{14,10},{16,20},{18,... | collective-permute-start | bytes 208904 | tf_op jit(solution)/shard_map/ppermute | solution.py:172
  38.6 4.3 %collective-permute-start.24 = (f32[136,128]{1,0:T(8,128)S(1)}, f32[136,128]{1,0:T(8,128)S(1)}, u32[]{:S(2)}, u32[]{:S(2)}) collective-permute-start(f32[136,128]{1,0:T(8,128)S(1)} %get-tuple-element.73), channel_id=1, source_target_pairs={{0,2},{2,0},{4,6},{6,4},{8,10},{10,8},{12,14},{14,12},{16,18},{18,... | collective-permute-start | bytes 208904 | tf_op jit(solution)/shard_map/ppermute | solution.py:172
  39.9 4.9 %collective-permute-start.19 = (f32[136,128]{1,0:T(8,128)S(1)}, f32[136,128]{1,0:T(8,128)S(1)}, u32[]{:S(2)}, u32[]{:S(2)}) collective-permute-start(f32[136,128]{1,0:T(8,128)S(1)} %add_add_fusion.1), channel_id=1, source_target_pairs={{0,8},{2,10},{4,12},{6,14},{8,0},{10,2},{12,4},{14,6},{16,24},{18,... | collective-permute-start | bytes 208904 | tf_op jit(solution)/shard_map/ppermute | solution.py:172
  42.9 4.4 %collective-permute-start.27 = (f32[136,128]{1,0:T(8,128)S(1)}, f32[136,128]{1,0:T(8,128)S(1)}, u32[]{:S(2)}, u32[]{:S(2)}) collective-permute-start(f32[136,128]{1,0:T(8,128)S(1)} %add_add_fusion), channel_id=1, source_target_pairs={{0,8},{2,10},{4,12},{6,14},{8,0},{10,2},{12,4},{14,6},{16,24},{18,... | collective-permute-start | bytes 208904 | tf_op jit(solution)/shard_map/ppermute | solution.py:172
  44.8 6.0 %collective-permute-start.20 = (f32[136,128]{1,0:T(8,128)S(1)}, f32[136,128]{1,0:T(8,128)S(1)}, u32[]{:S(2)}, u32[]{:S(2)}) collective-permute-start(f32[136,128]{1,0:T(8,128)S(1)} %add.76), channel_id=1, source_target_pairs={{0,16},{2,18},{4,20},{6,22},{8,24},{10,26},{12,28},{14,30},{16,0},... | collective-permute-start | bytes 208904 | tf_op jit(solution)/shard_map/ppermute | solution.py:172
  47.3 7.1 %collective-permute-start.28 = (f32[136,128]{1,0:T(8,128)S(1)}, f32[136,128]{1,0:T(8,128)S(1)}, u32[]{:S(2)}, u32[]{:S(2)}) collective-permute-start(f32[136,128]{1,0:T(8,128)S(1)} %add.81), channel_id=1, source_target_pairs={{0,16},{2,18},{4,20},{6,22},{8,24},{10,26},{12,28},{14,30},{16,0},... | collective-permute-start | bytes 208904 | tf_op jit(solution)/shard_map/ppermute | solution.py:172
  50.9 5.1 %collective-permute-start.21 = (f32[136,128]{1,0:T(8,128)S(1)}, f32[136,128]{1,0:T(8,128)S(1)}, u32[]{:S(2)}, u32[]{:S(2)}) collective-permute-start(f32[136,128]{1,0:T(8,128)S(1)} %get-tuple-element.69), channel_id=1, source_target_pairs={{0,2},{2,0},{4,6},{6,4},{8,10},{10,8},{12,14},{14,12},{16,18},{18,... | collective-permute-start | bytes 208904 | tf_op jit(solution)/shard_map/ppermute | solution.py:172
  51.4 9.8 %collective-permute-start.22 = (f32[136,128]{1,0:T(8,128)S(1)}, f32[136,128]{1,0:T(8,128)S(1)}, u32[]{:S(2)}, u32[]{:S(2)}) collective-permute-start(f32[136,128]{1,0:T(8,128)S(1)} %get-tuple-element.70), channel_id=1, source_target_pairs={{0,4},{2,6},{4,0},{6,2},{8,12},{10,14},{12,8},{14,10},{16,20},{18,... | collective-permute-start | bytes 208904 | tf_op jit(solution)/shard_map/ppermute | solution.py:172
  51.9 9.3 %collective-permute-start.23 = (f32[136,128]{1,0:T(8,128)S(1)}, f32[136,128]{1,0:T(8,128)S(1)}, u32[]{:S(2)}, u32[]{:S(2)}) collective-permute-start(f32[136,128]{1,0:T(8,128)S(1)} %get-tuple-element.71), channel_id=1, source_target_pairs={{0,6},{2,4},{4,2},{6,0},{8,14},{10,12},{12,10},{14,8},{16,22},{18,... | collective-permute-start | bytes 208904 | tf_op jit(solution)/shard_map/ppermute | solution.py:172
  54.5 6.7 %collective-permute-start.29 = (f32[136,128]{1,0:T(8,128)S(1)}, f32[136,128]{1,0:T(8,128)S(1)}, u32[]{:S(2)}, u32[]{:S(2)}) collective-permute-start(f32[136,128]{1,0:T(8,128)S(1)} %get-tuple-element.77), channel_id=1, source_target_pairs={{0,2},{2,0},{4,6},{6,4},{8,10},{10,8},{12,14},{14,12},{16,18},{18,... | collective-permute-start | bytes 208904 | tf_op jit(solution)/shard_map/ppermute | solution.py:172
  55.1 6.1 %collective-permute-start.30 = (f32[136,128]{1,0:T(8,128)S(1)}, f32[136,128]{1,0:T(8,128)S(1)}, u32[]{:S(2)}, u32[]{:S(2)}) collective-permute-start(f32[136,128]{1,0:T(8,128)S(1)} %get-tuple-element.78), channel_id=1, source_target_pairs={{0,4},{2,6},{4,0},{6,2},{8,12},{10,14},{12,8},{14,10},{16,20},{18,... | collective-permute-start | bytes 208904 | tf_op jit(solution)/shard_map/ppermute | solution.py:172
  56.0 5.2 %collective-permute-start.31 = (f32[136,128]{1,0:T(8,128)S(1)}, f32[136,128]{1,0:T(8,128)S(1)}, u32[]{:S(2)}, u32[]{:S(2)}) collective-permute-start(f32[136,128]{1,0:T(8,128)S(1)} %get-tuple-element.79), channel_id=1, source_target_pairs={{0,6},{2,4},{4,2},{6,0},{8,14},{10,12},{12,10},{14,8},{16,22},{18,... | collective-permute-start | bytes 208904 | tf_op jit(solution)/shard_map/ppermute | solution.py:172
  (6 other events, 28.3 us)

commit v12 on v11

--- a/solution.py
+++ b/solution.py
@@ -85,32 +85,31 @@
         delta_ref[DH:] = jnp.broadcast_to(jnp.sum(product, axis=0, keepdims=True), (GAIN_ROWS, DH))
 
 
-def partial_body(place_ref, query_ref, key_ref, value_ref, *refs):
-    attn_refs, state_refs = refs[:CHAINS], refs[CHAINS : CHAINS + HEADS]
-    grad_query_ref, key_part_ref, value_part_ref = refs[-3:]
+def partial_body(chain, place_ref, query_ref, key_ref, value_ref, attn_ref, *refs):
+    state_refs, (grad_query_ref, key_part_ref, value_part_ref) = refs[:GROUP], refs[-3:]
     keep, kept = causal(), causal(True)
-    for at_head, state_ref in enumerate(state_refs):
-        chain, mask = at_head // GROUP, at_head % GROUP
-        at = own_columns(place_ref, mask, chain)
-        query, key, value = query_ref[:, at], key_ref[:, at], value_ref[:, at]
-        grad_attn = attn_refs[chain][:, own_columns(place_ref, mask)]
+    for mask, state_ref in enumerate(state_refs):
+        at, here = own_columns(place_ref, mask, chain), own_columns(place_ref, mask)
+        query, key, value, grad_attn = query_ref[:, at], key_ref[:, at], value_ref[:, at], attn_ref[:, here]
         turned = jnp.where(kept, dot(key, query, NT), 0.0).astype(jnp.bfloat16)
         grad_scores = jnp.where(keep, dot(grad_attn, value, NT), 0.0).astype(jnp.bfloat16)
         turned_grad = jnp.where(kept, dot(value, grad_attn, NT), 0.0).astype(jnp.bfloat16)
         carried = dot(grad_attn, state_ref[...].astype(jnp.bfloat16), NT)
-        grad_query_ref[:, at] = (dot(grad_scores, key, NN) + carried).astype(jnp.bfloat16)
-        key_part_ref[:, at] = dot(turned_grad, query, NN)
-        value_part_ref[:, at] = dot(turned, grad_attn, NN)
-
-
-def final_body(place_ref, key_ref, value_ref, key_part_ref, value_part_ref, *refs):
-    state_refs, (grad_key_ref, grad_value_ref) = refs[:HEADS], refs[HEADS:]
+        grad_query_ref[:, here] = (dot(grad_scores, key, NN) + carried).astype(jnp.bfloat16)
+        key_part_ref[:, here] = dot(turned_grad, query, NN)
+        value_part_ref[:, here] = dot(turned, grad_attn, NN)
+
+
+def final_body(place_ref, key_ref, value_ref, *refs):
+    part_refs, state_refs, (grad_key_ref, grad_value_ref) = refs[: 2 * CHAINS], refs[2 * CHAINS : -2], refs[-2:]
     rows = pl.ds(pl.multiple_of(pl.program_id(0) * PART_ROWS, PART_ROWS), PART_ROWS)
     for at_head, state_ref in enumerate(state_refs):
-        at = own_columns(place_ref, at_head % GROUP, at_head // GROUP)
+        chain, mask = at_head // GROUP, at_head % GROUP
+        at, here = own_columns(place_ref, mask, chain), own_columns(place_ref, mask)
         state = state_ref[:DH].astype(jnp.bfloat16)
-        grad_key_ref[:, at] = (key_part_ref[rows, at] + dot(value_ref[rows, at], state, NT)).astype(jnp.bfloat16)
-        grad_value_ref[:, at] = (value_part_ref[rows, at] + dot(key_ref[rows, at], state, NN)).astype(jnp.bfloat16)
+        key_part, value_part = part_refs[2 * chain][rows, here], part_refs[2 * chain + 1][rows, here]
+        grad_key_ref[:, at] = (key_part + dot(value_ref[rows, at], state, NT)).astype(jnp.bfloat16)
+        grad_value_ref[:, at] = (value_part + dot(key_ref[rows, at], state, NN)).astype(jnp.bfloat16)
 
 
 def gain_body(place_ref, *refs):
@@ -145,7 +144,7 @@
 PLACE = pl.BlockSpec(memory_space=pltpu.SMEM)
 
 
-def call(body, in_specs, out_specs, outs, flops, name, steps=1, scratch=()):
+def call(body, in_specs, out_specs, outs, flops, name, steps=1, scratch=(), aliases=None):
     return pl.pallas_call(
         body,
         grid=(steps,),
@@ -153,6 +152,7 @@
         out_specs=out_specs,
         out_shape=outs,
         scratch_shapes=scratch,
+        input_output_aliases=aliases or {},
         compiler_params=pltpu.CompilerParams(vmem_limit_bytes=16 * 1024 * 1024),
         cost_estimate=pl.CostEstimate(flops=flops, bytes_accessed=2 << 20, transcendentals=0),
         name=name,
@@ -172,13 +172,18 @@
     return lax.ppermute(array, "seq", [(s, s ^ mask) for s in range(lax.axis_size("seq"))])
 
 
-def carried_in(pieces, reverse, place):
+def carried_in(pieces, reverse, place, beside=None, operands=()):
     held = [swap(piece, mask) for mask, piece in enumerate(pieces)]
-    total = sum(held[1:], held[0])
+    total, aside = sum(held[1:], held[0]), None
+    if beside:
+        total, operands = lax.optimization_barrier((total, operands))
+        aside = beside(*operands)
     arrived = []
     for mask in exchange_masks():
         arrived.append(swap(total, mask))
         total = total + arrived[-1]
+        if beside and len(arrived) == 1:
+            total, aside = lax.optimization_barrier((total, aside))
     single = whole(*total.shape)
     back = call(
         functools.partial(prefix_body, reverse, exchange_masks()),
@@ -189,7 +194,7 @@
         "prefix",
         scratch=[pltpu.VMEM((GROUP, DH, DH), jnp.float32)],
     )(place, total, *arrived, *held)
-    return [swap(piece, mask) for mask, piece in enumerate(back)]
+    return [swap(piece, mask) for mask, piece in enumerate(back)], aside
 
 
 def local(queries, keys, values, out_gain, grad_out):
@@ -202,6 +207,7 @@
     taller = jax.ShapeDtypeStruct((DH + GAIN_ROWS, DH), jnp.float32)
     full_float = jax.ShapeDtypeStruct(flat, jnp.float32)
     full_low = jax.ShapeDtypeStruct(flat, jnp.bfloat16)
+    half_float = jax.ShapeDtypeStruct((BLOCK, WIDE), jnp.float32)
     half_low = jax.ShapeDtypeStruct((BLOCK, WIDE), jnp.bfloat16)
     short, tall, wide, half = whole(*square.shape), whole(*taller.shape), whole(*flat), whole(BLOCK, WIDE)
     unit = 2 * BLOCK * DH * DH * HEADS
@@ -217,11 +223,12 @@
         scratch=[pltpu.VMEM(flat, jnp.bfloat16)] * 2 + [pltpu.SemaphoreType.DMA((PARTS, 2))],
     )(place, *[pltpu.with_memory_space_constraint(a, pltpu.HBM) for a in (key, value)])
     chains = [slice(chain * GROUP, (chain + 1) * GROUP) for chain in range(CHAINS)]
-    states = [carried_in(deltas[chain], False, place) for chain in chains]
-    inner = call(
+    inner_call = call(
         lambda place_ref, *refs: inner_body(*refs), [wide] * 3, wide, full_float, 16 * unit, "inner"
-    )(place, query, key, value)
-    attns, later = [], []
+    )
+    first, inner = carried_in(deltas[chains[0]], False, place, inner_call, (place, query, key, value))
+    states = [first] + [carried_in(deltas[chain], False, place)[0] for chain in chains[1:]]
+    later, parts, grad_query = [], [], []
     for chain in range(CHAINS):
         attn, *deltas = call(
             functools.partial(norm_body, chain),
@@ -231,16 +238,24 @@
             8 * unit,
             "norm",
         )(place, query, grad, inner, gain, *states[chain])
-        attns.append(attn)
-        later += carried_in(deltas, True, place)
-    grad_query, key_part, value_part = call(
-        partial_body,
-        [wide] * 3 + [half] * CHAINS + [short] * HEADS,
-        [wide] * 3,
-        [full_low, full_float, full_float],
-        48 * unit,
-        "partial",
-    )(place, query, key, value, *attns, *[state for chain in states for state in chain])
+        partial_call = call(
+            functools.partial(partial_body, chain),
+            [wide] * 3 + [half] + [short] * GROUP + [pl.BlockSpec(memory_space=pl.ANY)] * len(grad_query),
+            [pl.BlockSpec((BLOCK, WIDE), lambda step, chain=chain: (0, chain)), half, half],
+            [full_low, half_float, half_float],
+            24 * unit,
+            "partial",
+            aliases={5 + GROUP: 0} if grad_query else None,
+        )
+        operands = (place, query, key, value, attn, *states[chain], *grad_query)
+        if chain == 0:
+            pieces, aside = carried_in(deltas, True, place, partial_call, operands)
+        else:
+            pieces, aside = carried_in(deltas, True, place)[0], partial_call(*operands)
+        *grad_query, key_part, value_part = aside
+        later += pieces
+        parts += [key_part, value_part]
+    (grad_query,) = grad_query
     gain_terms = call(
         gain_body, [tall] * HEADS, whole(HEADS, DH), jax.ShapeDtypeStruct((HEADS, DH), jnp.float32), unit, "gain"
     )(place, *later)
@@ -250,8 +265,8 @@
         mask *= 2
     chunk = pl.BlockSpec((PART_ROWS, HEADS * DH), lambda step: (step, 0))
     grad_key, grad_value = call(
-        final_body, [wide] * 4 + [tall] * HEADS, [chunk] * 2, [full_low] * 2, 16 * unit, "final", steps=PARTS
-    )(place, key, value, key_part, value_part, *later)
+        final_body, [wide] * 2 + [half] * (2 * CHAINS) + [tall] * HEADS, [chunk] * 2, [full_low] * 2, 16 * unit, "final", steps=PARTS
+    )(place, key, value, *parts, *later)
     grad_gain = gain_terms / math.sqrt(lax.axis_size("seq") * docs * BLOCK)
     return (
         grad_query.reshape(full),

time: 63.7 us -> 64.9 us (1.019)
  waiting for transfers between devices: 8.96 us -> 12.2 us
  starting transfers between devices: 44 us -> 41.2 us
  Pallas kernels: 8.97 us -> 9.8 us
    ppermute x32, waiting for transfers between devices: 8.96 us -> 12.2 us  [swap(): lax.ppermute(array, 'seq', [(s, s ^ mask) for s in range(lax.axis_size('s...]
    ppermute x32, starting transfers between devices: 43.9 us -> 41.2 us  [swap(): lax.ppermute(array, 'seq', [(s, s ^ mask) for s in range(lax.axis_size('s...]
    pallas_call x3 -> x4, Pallas kernels: 5.64 us -> 6.4 us  [the longest x2 2.86 us: carried_in(): aside = beside(*operands)]
  transfers between devices with their start and end apart: 33 -> 33, of which waited for: 12 -> 10; matrix products, arithmetic and copies ran while one was open for 0% -> 0% of each run, Pallas kernels for 12% -> 13%
where the time goes in v12:
time: 64.9 us; the launch traced here: 64.8 us
  starting transfers between devices  41.2 us (63%)
  waiting for transfers between devices  12.2 us (19%)
  Pallas kernels  9.8 us (15%)
  between operations  0.85 us (1%)
  other arithmetic  0.75 us (1%)
    ppermute x32, starting transfers between devices, swap(): lax.ppermute(array, 'seq', [(s, s ^ mask) for s in range(lax.axis_size('s...  41.2 us
    ppermute x32, waiting for transfers between devices, swap(): lax.ppermute(array, 'seq', [(s, s ^ mask) for s in range(lax.axis_size('s...  12.2 us
    pallas_call x2, Pallas kernels, carried_in(): aside = beside(*operands)  2.86 us
    pallas_call x1, Pallas kernels, local(): partial_call(*operands)  1.91 us
    pallas_call x1, Pallas kernels, local(): call(final_body, [wide] * 2 + [half] * (2 * CHAINS) + [tall] * HEADS, [ch...  1.63 us
    pallas_call x1, Pallas kernels, local(): call(delta_body, [pl.BlockSpec(memory_space=pltpu.HBM)] * 2, [short] * HE...  1.61 us
    pallas_call x2, Pallas kernels, local(): call(functools.partial(norm_body, chain), [wide, wide, wide, whole(1, HEA...  1.47 us
  transfers between devices with their start and end apart: 33, of which 10 were waited for; matrix products, arithmetic and copies ran while one was open for 0% of the time, Pallas kernels for 13%

profile of v12, /device:TPU:0, one launch (start us, length us, event | category | flops | bytes accessed | tf_op | source)
XLA Modules:
  0.0 64.8 jit_solution(4233668180982229499)
XLA Ops:
  0.7 1.6 %delta.1 = (f32[128,128]{1,0:T(8,128)S(1)}, f32[128,128]{1,0:T(8,128)S(1)}, f32[128,128]{1,0:T(8,128)S(1)}, f32[128,128]{1,0:T(8,128)S(1)}, f32[128,128]{1,0:T(8...) custom-call(s32[1]{0:T(128)} %bitcast.place_ref, bf16[256,1024]{1,0:T(8,128)(2,1)} %bitcast.20, ...), custom_call_target="tpu_custom_call" | custom-call | flops 402653184 | bytes 2097152 | tf_op jit(solution)/shard_map/delta/pallas_call | solution.py:216
  2.3 3.0 %collective-permute-start.4 = (f32[128,128]{1,0:T(8,128)S(1)}, f32[128,128]{1,0:T(8,128)S(1)}, u32[]{:S(2)}, u32[]{:S(2)}) collective-permute-start(f32[128,128]{1,0:T(8,128)S(1)} %get-tuple-element.78), channel_id=1, source_target_pairs={{0,2},{2,0},{4,6},{6,4},{8,10},{10,8},{12,14},{14,12},{16,18},{18,... | collective-permute-start | bytes 196616 | tf_op jit(solution)/shard_map/ppermute | solution.py:172
  5.3 1.5 %collective-permute-start.5 = (f32[128,128]{1,0:T(8,128)S(1)}, f32[128,128]{1,0:T(8,128)S(1)}, u32[]{:S(2)}, u32[]{:S(2)}) collective-permute-start(f32[128,128]{1,0:T(8,128)S(1)} %get-tuple-element.79), channel_id=1, source_target_pairs={{0,4},{2,6},{4,0},{6,2},{8,12},{10,14},{12,8},{14,10},{16,20},{18,... | collective-permute-start | bytes 196616 | tf_op jit(solution)/shard_map/ppermute | solution.py:172
  6.8 1.9 %collective-permute-start = (f32[128,128]{1,0:T(8,128)S(1)}, f32[128,128]{1,0:T(8,128)S(1)}, u32[]{:S(2)}, u32[]{:S(2)}) collective-permute-start(f32[128,128]{1,0:T(8,128)S(1)} %get-tuple-element.68), channel_id=1, source_target_pairs={{0,2},{2,0},{4,6},{6,4},{8,10},{10,8},{12,14},{14,12},{16,18},{18,... | collective-permute-start | bytes 196616 | tf_op jit(solution)/shard_map/ppermute | solution.py:172
  8.8 1.5 %collective-permute-start.1 = (f32[128,128]{1,0:T(8,128)S(1)}, f32[128,128]{1,0:T(8,128)S(1)}, u32[]{:S(2)}, u32[]{:S(2)}) collective-permute-start(f32[128,128]{1,0:T(8,128)S(1)} %get-tuple-element.69), channel_id=1, source_target_pairs={{0,4},{2,6},{4,0},{6,2},{8,12},{10,14},{12,8},{14,10},{16,20},{18,... | collective-permute-start | bytes 196616 | tf_op jit(solution)/shard_map/ppermute | solution.py:172
  10.9 1.1 %collective-permute-done.6.refs_6_ = f32[128,128]{1,0:T(8,128)S(1)} collective-permute-done((f32[128,128]{1,0:T(8,128)S(1)}, f32[128,128]{1,0:T(8,128)S(1)}, u32[]{:S(2)}, u32[]{:S(2)}) %collective-permute-start.6) | collective-permute-done | bytes 65568 | tf_op jit(solution)/shard_map/ppermute | solution.py:172
  12.0 1.6 %collective-permute-start.7 = (f32[128,128]{1,0:T(8,128)S(1)}, f32[128,128]{1,0:T(8,128)S(1)}, u32[]{:S(2)}, u32[]{:S(2)}) collective-permute-start(f32[128,128]{1,0:T(8,128)S(1)} %add_add_fusion.2), channel_id=1, source_target_pairs={{0,8},{2,10},{4,12},{6,14},{8,0},{10,2},{12,4},{14,6},{16,24},{18,... | collective-permute-start | bytes 196616 | tf_op jit(solution)/shard_map/ppermute | solution.py:172
  13.7 1.8 %collective-permute-done.2.refs_6_ = f32[128,128]{1,0:T(8,128)S(1)} collective-permute-done((f32[128,128]{1,0:T(8,128)S(1)}, f32[128,128]{1,0:T(8,128)S(1)}, u32[]{:S(2)}, u32[]{:S(2)}) %collective-permute-start.2) | collective-permute-done | bytes 65568 | tf_op jit(solution)/shard_map/ppermute | solution.py:172
  15.5 1.6 %collective-permute-start.3 = (f32[128,128]{1,0:T(8,128)S(1)}, f32[128,128]{1,0:T(8,128)S(1)}, u32[]{:S(2)}, u32[]{:S(2)}) collective-permute-start(f32[128,128]{1,0:T(8,128)S(1)} %add_add_fusion.3), channel_id=1, source_target_pairs={{0,8},{2,10},{4,12},{6,14},{8,0},{10,2},{12,4},{14,6},{16,24},{18,... | collective-permute-start | bytes 196616 | tf_op jit(solution)/shard_map/ppermute | solution.py:172
  17.1 2.7 %collective-permute-start.8 = (f32[128,128]{1,0:T(8,128)S(1)}, f32[128,128]{1,0:T(8,128)S(1)}, u32[]{:S(2)}, u32[]{:S(2)}) collective-permute-start(f32[128,128]{1,0:T(8,128)S(1)} %add.70), channel_id=1, source_target_pairs={{0,16},{2,18},{4,20},{6,22},{8,24},{10,26},{12,28},{14,30},{16,0},... | collective-permute-start | bytes 196616 | tf_op jit(solution)/shard_map/ppermute | solution.py:172
  19.8 0.9 %inner.1.inner_ref = f32[256,1024]{1,0:T(8,128)S(1)} custom-call(s32[1]{0:T(128)} %bitcast.place_ref, bf16[256,1024]{1,0:T(8,128)(2,1)S(1)} %bitcast.13, bf16[256,1024]{1,0:T(8,128)(2,1)S(1)} %bitcast.21, bf16[256,1024]{1,0:T(8,128)(2,1)S(1)} %bitcast.26), custom_call_target="tpu_custom_call" | custom-call | flops 1073741824 | bytes 2097152 | tf_op jit(solution)/shard_map/inner/pallas_call | solution.py:180
  20.8 2.1 %collective-permute-start.12 = (f32[128,128]{1,0:T(8,128)S(1)}, f32[128,128]{1,0:T(8,128)S(1)}, u32[]{:S(2)}, u32[]{:S(2)}) collective-permute-start(f32[128,128]{1,0:T(8,128)S(1)} %add.66), channel_id=1, source_target_pairs={{0,16},{2,18},{4,20},{6,22},{8,24},{10,26},{12,28},{14,30},{16,0},... | collective-permute-start | bytes 196616 | tf_op jit(solution)/shard_map/ppermute | solution.py:172
  22.9 1.5 %collective-permute-done.8.refs_2_ = f32[128,128]{1,0:T(8,128)S(1)} collective-permute-done((f32[128,128]{1,0:T(8,128)S(1)}, f32[128,128]{1,0:T(8,128)S(1)}, u32[]{:S(2)}, u32[]{:S(2)}) %collective-permute-start.8) | collective-permute-done | bytes 65568 | tf_op jit(solution)/shard_map/ppermute | solution.py:172
  25.7 2.3 %collective-permute-start.11 = (f32[128,128]{1,0:T(8,128)S(1)}, f32[128,128]{1,0:T(8,128)S(1)}, u32[]{:S(2)}, u32[]{:S(2)}) collective-permute-start(f32[128,128]{1,0:T(8,128)S(1)} %get-tuple-element.84), channel_id=1, source_target_pairs={{0,6},{2,4},{4,2},{6,0},{8,14},{10,12},{12,10},{14,8},{16,22},{18,... | collective-permute-start | bytes 196616 | tf_op jit(solution)/shard_map/ppermute | solution.py:172
  29.3 2.3 %collective-permute-start.15 = (f32[128,128]{1,0:T(8,128)S(1)}, f32[128,128]{1,0:T(8,128)S(1)}, u32[]{:S(2)}, u32[]{:S(2)}) collective-permute-start(f32[128,128]{1,0:T(8,128)S(1)} %get-tuple-element.90), channel_id=1, source_target_pairs={{0,6},{2,4},{4,2},{6,0},{8,14},{10,12},{12,10},{14,8},{16,22},{18,... | collective-permute-start | bytes 196616 | tf_op jit(solution)/shard_map/ppermute | solution.py:172
  33.3 1.5 %collective-permute-start.25 = (f32[136,128]{1,0:T(8,128)S(1)}, f32[136,128]{1,0:T(8,128)S(1)}, u32[]{:S(2)}, u32[]{:S(2)}) collective-permute-start(f32[136,128]{1,0:T(8,128)S(1)} %get-tuple-element.122), channel_id=1, source_target_pairs={{0,4},{2,6},{4,0},{6,2},{8,12},{10,14},{12,8},{14,10},{16,20},{18,... | collective-permute-start | bytes 208904 | tf_op jit(solution)/shard_map/ppermute | solution.py:172
  34.8 1.2 %collective-permute-start.26 = (f32[136,128]{1,0:T(8,128)S(1)}, f32[136,128]{1,0:T(8,128)S(1)}, u32[]{:S(2)}, u32[]{:S(2)}) collective-permute-start(f32[136,128]{1,0:T(8,128)S(1)} %get-tuple-element.123), channel_id=1, source_target_pairs={{0,6},{2,4},{4,2},{6,0},{8,14},{10,12},{12,10},{14,8},{16,22},{18,... | collective-permute-start | bytes 208904 | tf_op jit(solution)/shard_map/ppermute | solution.py:172
  37.6 1.5 %collective-permute-start.17 = (f32[136,128]{1,0:T(8,128)S(1)}, f32[136,128]{1,0:T(8,128)S(1)}, u32[]{:S(2)}, u32[]{:S(2)}) collective-permute-start(f32[136,128]{1,0:T(8,128)S(1)} %get-tuple-element.93), channel_id=1, source_target_pairs={{0,4},{2,6},{4,0},{6,2},{8,12},{10,14},{12,8},{14,10},{16,20},{18,... | collective-permute-start | bytes 208904 | tf_op jit(solution)/shard_map/ppermute | solution.py:172
  39.1 1.2 %collective-permute-start.18 = (f32[136,128]{1,0:T(8,128)S(1)}, f32[136,128]{1,0:T(8,128)S(1)}, u32[]{:S(2)}, u32[]{:S(2)}) collective-permute-start(f32[136,128]{1,0:T(8,128)S(1)} %get-tuple-element.94), channel_id=1, source_target_pairs={{0,6},{2,4},{4,2},{6,0},{8,14},{10,12},{12,10},{14,8},{16,22},{18,... | collective-permute-start | bytes 208904 | tf_op jit(solution)/shard_map/ppermute | solution.py:172
  41.9 2.5 %collective-permute-done.18.refs_6_ = f32[136,128]{1,0:T(8,128)S(1)} collective-permute-done((f32[136,128]{1,0:T(8,128)S(1)}, f32[136,128]{1,0:T(8,128)S(1)}, u32[]{:S(2)}, u32[]{:S(2)}) %collective-permute-start.18) | collective-permute-done | bytes 69664 | tf_op jit(solution)/shard_map/ppermute | solution.py:172
  44.4 1.0 %collective-permute-done.27.refs_1_ = f32[136,128]{1,0:T(8,128)S(1)} collective-permute-done((f32[136,128]{1,0:T(8,128)S(1)}, f32[136,128]{1,0:T(8,128)S(1)}, u32[]{:S(2)}, u32[]{:S(2)}) %collective-permute-start.27) | collective-permute-done | bytes 69664 | tf_op jit(solution)/shard_map/ppermute | solution.py:172
  45.5 1.9 %collective-permute-start.28 = (f32[136,128]{1,0:T(8,128)S(1)}, f32[136,128]{1,0:T(8,128)S(1)}, u32[]{:S(2)}, u32[]{:S(2)}) collective-permute-start(f32[136,128]{1,0:T(8,128)S(1)} %add.81), channel_id=1, source_target_pairs={{0,16},{2,18},{4,20},{6,22},{8,24},{10,26},{12,28},{14,30},{16,0},... | collective-permute-start | bytes 208904 | tf_op jit(solution)/shard_map/ppermute | solution.py:172
  47.3 1.9 %partial.2 = (bf16[256,1024]{1,0:T(8,128)(2,1)}, f32[256,512]{1,0:T(8,128)S(1)}, f32[256,512]{1,0:T(8,128)S(1)}) custom-call(s32[1]{0:T(128)} %bitcast.place_ref, bf16[256,1024]{1,0:T(8,128)(2,1)S(1)} %bitcast.16, bf16[256,1024]{1,0:T(8,128)(2,1)S(1)} %bitcast.22, bf16[256,1024]{1,0:T(8,128)(2,1)S(1)} %bitcast.27, ...), custom_call_target="tpu_custom_call" | custom-call | flops 1610612736 | bytes 2097152 | tf_op jit(solution)/shard_map/partial/pallas_call | solution.py:180
  49.3 1.2 %collective-permute-start.20 = (f32[136,128]{1,0:T(8,128)S(1)}, f32[136,128]{1,0:T(8,128)S(1)}, u32[]{:S(2)}, u32[]{:S(2)}) collective-permute-start(f32[136,128]{1,0:T(8,128)S(1)} %add.76), channel_id=1, source_target_pairs={{0,16},{2,18},{4,20},{6,22},{8,24},{10,26},{12,28},{14,30},{16,0},... | collective-permute-start | bytes 208904 | tf_op jit(solution)/shard_map/ppermute | solution.py:172
  50.5 1.0 %collective-permute-done.28.refs_2_ = f32[136,128]{1,0:T(8,128)S(1)} collective-permute-done((f32[136,128]{1,0:T(8,128)S(1)}, f32[136,128]{1,0:T(8,128)S(1)}, u32[]{:S(2)}, u32[]{:S(2)}) %collective-permute-start.28) | collective-permute-done | bytes 69664 | tf_op jit(solution)/shard_map/ppermute | solution.py:172
  51.7 1.5 %collective-permute-start.30 = (f32[136,128]{1,0:T(8,128)S(1)}, f32[136,128]{1,0:T(8,128)S(1)}, u32[]{:S(2)}, u32[]{:S(2)}) collective-permute-start(f32[136,128]{1,0:T(8,128)S(1)} %get-tuple-element.126), channel_id=1, source_target_pairs={{0,4},{2,6},{4,0},{6,2},{8,12},{10,14},{12,8},{14,10},{16,20},{18,... | collective-permute-start | bytes 208904 | tf_op jit(solution)/shard_map/ppermute | solution.py:172
  53.2 1.9 %collective-permute-start.31 = (f32[136,128]{1,0:T(8,128)S(1)}, f32[136,128]{1,0:T(8,128)S(1)}, u32[]{:S(2)}, u32[]{:S(2)}) collective-permute-start(f32[136,128]{1,0:T(8,128)S(1)} %get-tuple-element.127), channel_id=1, source_target_pairs={{0,6},{2,4},{4,2},{6,0},{8,14},{10,12},{12,10},{14,8},{16,22},{18,... | collective-permute-start | bytes 208904 | tf_op jit(solution)/shard_map/ppermute | solution.py:172
  56.2 1.1 %collective-permute-start.22 = (f32[136,128]{1,0:T(8,128)S(1)}, f32[136,128]{1,0:T(8,128)S(1)}, u32[]{:S(2)}, u32[]{:S(2)}) collective-permute-start(f32[136,128]{1,0:T(8,128)S(1)} %get-tuple-element.118), channel_id=1, source_target_pairs={{0,4},{2,6},{4,0},{6,2},{8,12},{10,14},{12,8},{14,10},{16,20},{18,... | collective-permute-start | bytes 208904 | tf_op jit(solution)/shard_map/ppermute | solution.py:172
  57.3 1.6 %collective-permute-start.23 = (f32[136,128]{1,0:T(8,128)S(1)}, f32[136,128]{1,0:T(8,128)S(1)}, u32[]{:S(2)}, u32[]{:S(2)}) collective-permute-start(f32[136,128]{1,0:T(8,128)S(1)} %get-tuple-element.119), channel_id=1, source_target_pairs={{0,6},{2,4},{4,2},{6,0},{8,14},{10,12},{12,10},{14,8},{16,22},{18,... | collective-permute-start | bytes 208904 | tf_op jit(solution)/shard_map/ppermute | solution.py:172
  59.0 1.9 %partial.3 = (bf16[256,1024]{1,0:T(8,128)(2,1)}, f32[256,512]{1,0:T(8,128)S(1)}, f32[256,512]{1,0:T(8,128)S(1)}) custom-call(s32[1]{0:T(128)} %bitcast.place_ref, bf16[256,1024]{1,0:T(8,128)(2,1)S(1)} %bitcast.17, bf16[256,1024]{1,0:T(8,128)(2,1)S(1)} %bitcast.23, bf16[256,1024]{1,0:T(8,128)(2,1)S(1)} %bitcast.28, ...), custom_call_target="tpu_custom_call", output_to_operand_aliasing={{0}: (9, {})} | custom-call | flops 1610612736 | bytes 2097152 | tf_op jit(solution)/shard_map/partial/pallas_call | solution.py:254
  60.9 1.6 %collective-permute-done.23.refs_7_.refs_3_ = f32[136,128]{1,0:T(8,128)S(1)} collective-permute-done((f32[136,128]{1,0:T(8,128)S(1)}, f32[136,128]{1,0:T(8,128)S(1)}, u32[]{:S(2)}, u32[]{:S(2)}) %collective-permute-start.23) | collective-permute-done | bytes 69664 | tf_op jit(solution)/shard_map/ppermute | solution.py:172
  62.6 1.6 %final.1 = (bf16[256,1024]{1,0:T(8,128)(2,1)}, bf16[256,1024]{1,0:T(8,128)(2,1)}) custom-call(s32[1]{0:T(128)} %bitcast.place_ref, bf16[256,1024]{1,0:T(8,128)(2,1)S(1)} %bitcast.24, bf16[256,1024]{1,0:T(8,128)(2,1)S(1)} %bitcast.29, f32[256,512]{1,0:T(8,128)S(1)} %get-tuple-element.111.refs_0_, f32[256,512]{1,0:T(8,128)S(1)} %get-tuple-element.112.refs_1_, ...), custom_call_target="tpu_custom_call" | custom-call | flops 1073741824 | bytes 2097152 | tf_op jit(solution)/shard_map/final/pallas_call | solution.py:267
  (69 shorter events, 10.1 us)
Async XLA Ops:
  2.3 8.0 %collective-permute-start.4 = (f32[128,128]{1,0:T(8,128)S(1)}, f32[128,128]{1,0:T(8,128)S(1)}, u32[]{:S(2)}, u32[]{:S(2)}) collective-permute-start(f32[128,128]{1,0:T(8,128)S(1)} %get-tuple-element.78), channel_id=1, source_target_pairs={{0,2},{2,0},{4,6},{6,4},{8,10},{10,8},{12,14},{14,12},{16,18},{18,... | collective-permute-start | bytes 196616 | tf_op jit(solution)/shard_map/ppermute | solution.py:172
  5.3 5.6 %collective-permute-start.5 = (f32[128,128]{1,0:T(8,128)S(1)}, f32[128,128]{1,0:T(8,128)S(1)}, u32[]{:S(2)}, u32[]{:S(2)}) collective-permute-start(f32[128,128]{1,0:T(8,128)S(1)} %get-tuple-element.79), channel_id=1, source_target_pairs={{0,4},{2,6},{4,0},{6,2},{8,12},{10,14},{12,8},{14,10},{16,20},{18,... | collective-permute-start | bytes 196616 | tf_op jit(solution)/shard_map/ppermute | solution.py:172
  6.8 5.2 %collective-permute-start.6 = (f32[128,128]{1,0:T(8,128)S(1)}, f32[128,128]{1,0:T(8,128)S(1)}, u32[]{:S(2)}, u32[]{:S(2)}) collective-permute-start(f32[128,128]{1,0:T(8,128)S(1)} %get-tuple-element.80), channel_id=1, source_target_pairs={{0,6},{2,4},{4,2},{6,0},{8,14},{10,12},{12,10},{14,8},{16,22},{18,... | collective-permute-start | bytes 196616 | tf_op jit(solution)/shard_map/ppermute | solution.py:172
  6.8 6.8 %collective-permute-start = (f32[128,128]{1,0:T(8,128)S(1)}, f32[128,128]{1,0:T(8,128)S(1)}, u32[]{:S(2)}, u32[]{:S(2)}) collective-permute-start(f32[128,128]{1,0:T(8,128)S(1)} %get-tuple-element.68), channel_id=1, source_target_pairs={{0,2},{2,0},{4,6},{6,4},{8,10},{10,8},{12,14},{14,12},{16,18},{18,... | collective-permute-start | bytes 196616 | tf_op jit(solution)/shard_map/ppermute | solution.py:172
  8.8 4.9 %collective-permute-start.1 = (f32[128,128]{1,0:T(8,128)S(1)}, f32[128,128]{1,0:T(8,128)S(1)}, u32[]{:S(2)}, u32[]{:S(2)}) collective-permute-start(f32[128,128]{1,0:T(8,128)S(1)} %get-tuple-element.69), channel_id=1, source_target_pairs={{0,4},{2,6},{4,0},{6,2},{8,12},{10,14},{12,8},{14,10},{16,20},{18,... | collective-permute-start | bytes 196616 | tf_op jit(solution)/shard_map/ppermute | solution.py:172
  10.3 5.2 %collective-permute-start.2 = (f32[128,128]{1,0:T(8,128)S(1)}, f32[128,128]{1,0:T(8,128)S(1)}, u32[]{:S(2)}, u32[]{:S(2)}) collective-permute-start(f32[128,128]{1,0:T(8,128)S(1)} %get-tuple-element.70), channel_id=1, source_target_pairs={{0,6},{2,4},{4,2},{6,0},{8,14},{10,12},{12,10},{14,8},{16,22},{18,... | collective-permute-start | bytes 196616 | tf_op jit(solution)/shard_map/ppermute | solution.py:172
  12.0 5.1 %collective-permute-start.7 = (f32[128,128]{1,0:T(8,128)S(1)}, f32[128,128]{1,0:T(8,128)S(1)}, u32[]{:S(2)}, u32[]{:S(2)}) collective-permute-start(f32[128,128]{1,0:T(8,128)S(1)} %add_add_fusion.2), channel_id=1, source_target_pairs={{0,8},{2,10},{4,12},{6,14},{8,0},{10,2},{12,4},{14,6},{16,24},{18,... | collective-permute-start | bytes 196616 | tf_op jit(solution)/shard_map/ppermute | solution.py:172
  15.5 5.3 %collective-permute-start.3 = (f32[128,128]{1,0:T(8,128)S(1)}, f32[128,128]{1,0:T(8,128)S(1)}, u32[]{:S(2)}, u32[]{:S(2)}) collective-permute-start(f32[128,128]{1,0:T(8,128)S(1)} %add_add_fusion.3), channel_id=1, source_target_pairs={{0,8},{2,10},{4,12},{6,14},{8,0},{10,2},{12,4},{14,6},{16,24},{18,... | collective-permute-start | bytes 196616 | tf_op jit(solution)/shard_map/ppermute | solution.py:172
  17.1 7.2 %collective-permute-start.8 = (f32[128,128]{1,0:T(8,128)S(1)}, f32[128,128]{1,0:T(8,128)S(1)}, u32[]{:S(2)}, u32[]{:S(2)}) collective-permute-start(f32[128,128]{1,0:T(8,128)S(1)} %add.70), channel_id=1, source_target_pairs={{0,16},{2,18},{4,20},{6,22},{8,24},{10,26},{12,28},{14,30},{16,0},... | collective-permute-start | bytes 196616 | tf_op jit(solution)/shard_map/ppermute | solution.py:172
  20.8 7.2 %collective-permute-start.12 = (f32[128,128]{1,0:T(8,128)S(1)}, f32[128,128]{1,0:T(8,128)S(1)}, u32[]{:S(2)}, u32[]{:S(2)}) collective-permute-start(f32[128,128]{1,0:T(8,128)S(1)} %add.66), channel_id=1, source_target_pairs={{0,16},{2,18},{4,20},{6,22},{8,24},{10,26},{12,28},{14,30},{16,0},... | collective-permute-start | bytes 196616 | tf_op jit(solution)/shard_map/ppermute | solution.py:172
  24.5 4.9 %collective-permute-start.9 = (f32[128,128]{1,0:T(8,128)S(1)}, f32[128,128]{1,0:T(8,128)S(1)}, u32[]{:S(2)}, u32[]{:S(2)}) collective-permute-start(f32[128,128]{1,0:T(8,128)S(1)} %get-tuple-element.82), channel_id=1, source_target_pairs={{0,2},{2,0},{4,6},{6,4},{8,10},{10,8},{12,14},{14,12},{16,18},{18,... | collective-permute-start | bytes 196616 | tf_op jit(solution)/shard_map/ppermute | solution.py:172
  24.8 6.9 %collective-permute-start.10 = (f32[128,128]{1,0:T(8,128)S(1)}, f32[128,128]{1,0:T(8,128)S(1)}, u32[]{:S(2)}, u32[]{:S(2)}) collective-permute-start(f32[128,128]{1,0:T(8,128)S(1)} %get-tuple-element.83), channel_id=1, source_target_pairs={{0,4},{2,6},{4,0},{6,2},{8,12},{10,14},{12,8},{14,10},{16,20},{18,... | collective-permute-start | bytes 196616 | tf_op jit(solution)/shard_map/ppermute | solution.py:172
  25.7 6.0 %collective-permute-start.11 = (f32[128,128]{1,0:T(8,128)S(1)}, f32[128,128]{1,0:T(8,128)S(1)}, u32[]{:S(2)}, u32[]{:S(2)}) collective-permute-start(f32[128,128]{1,0:T(8,128)S(1)} %get-tuple-element.84), channel_id=1, source_target_pairs={{0,6},{2,4},{4,2},{6,0},{8,14},{10,12},{12,10},{14,8},{16,22},{18,... | collective-permute-start | bytes 196616 | tf_op jit(solution)/shard_map/ppermute | solution.py:172
  28.1 6.7 %collective-permute-start.13 = (f32[128,128]{1,0:T(8,128)S(1)}, f32[128,128]{1,0:T(8,128)S(1)}, u32[]{:S(2)}, u32[]{:S(2)}) collective-permute-start(f32[128,128]{1,0:T(8,128)S(1)} %get-tuple-element.88), channel_id=1, source_target_pairs={{0,2},{2,0},{4,6},{6,4},{8,10},{10,8},{12,14},{14,12},{16,18},{18,... | collective-permute-start | bytes 196616 | tf_op jit(solution)/shard_map/ppermute | solution.py:172
  28.5 7.5 %collective-permute-start.14 = (f32[128,128]{1,0:T(8,128)S(1)}, f32[128,128]{1,0:T(8,128)S(1)}, u32[]{:S(2)}, u32[]{:S(2)}) collective-permute-start(f32[128,128]{1,0:T(8,128)S(1)} %get-tuple-element.89), channel_id=1, source_target_pairs={{0,4},{2,6},{4,0},{6,2},{8,12},{10,14},{12,8},{14,10},{16,20},{18,... | collective-permute-start | bytes 196616 | tf_op jit(solution)/shard_map/ppermute | solution.py:172
  29.3 6.7 %collective-permute-start.15 = (f32[128,128]{1,0:T(8,128)S(1)}, f32[128,128]{1,0:T(8,128)S(1)}, u32[]{:S(2)}, u32[]{:S(2)}) collective-permute-start(f32[128,128]{1,0:T(8,128)S(1)} %get-tuple-element.90), channel_id=1, source_target_pairs={{0,6},{2,4},{4,2},{6,0},{8,14},{10,12},{12,10},{14,8},{16,22},{18,... | collective-permute-start | bytes 196616 | tf_op jit(solution)/shard_map/ppermute | solution.py:172
  32.4 6.7 %collective-permute-start.24 = (f32[136,128]{1,0:T(8,128)S(1)}, f32[136,128]{1,0:T(8,128)S(1)}, u32[]{:S(2)}, u32[]{:S(2)}) collective-permute-start(f32[136,128]{1,0:T(8,128)S(1)} %get-tuple-element.121), channel_id=1, source_target_pairs={{0,2},{2,0},{4,6},{6,4},{8,10},{10,8},{12,14},{14,12},{16,18},{18,... | collective-permute-start | bytes 208904 | tf_op jit(solution)/shard_map/ppermute | solution.py:172
  33.3 7.0 %collective-permute-start.25 = (f32[136,128]{1,0:T(8,128)S(1)}, f32[136,128]{1,0:T(8,128)S(1)}, u32[]{:S(2)}, u32[]{:S(2)}) collective-permute-start(f32[136,128]{1,0:T(8,128)S(1)} %get-tuple-element.122), channel_id=1, source_target_pairs={{0,4},{2,6},{4,0},{6,2},{8,12},{10,14},{12,8},{14,10},{16,20},{18,... | collective-permute-start | bytes 208904 | tf_op jit(solution)/shard_map/ppermute | solution.py:172
  34.8 5.5 %collective-permute-start.26 = (f32[136,128]{1,0:T(8,128)S(1)}, f32[136,128]{1,0:T(8,128)S(1)}, u32[]{:S(2)}, u32[]{:S(2)}) collective-permute-start(f32[136,128]{1,0:T(8,128)S(1)} %get-tuple-element.123), channel_id=1, source_target_pairs={{0,6},{2,4},{4,2},{6,0},{8,14},{10,12},{12,10},{14,8},{16,22},{18,... | collective-permute-start | bytes 208904 | tf_op jit(solution)/shard_map/ppermute | solution.py:172
  36.7 4.4 %collective-permute-start.16 = (f32[136,128]{1,0:T(8,128)S(1)}, f32[136,128]{1,0:T(8,128)S(1)}, u32[]{:S(2)}, u32[]{:S(2)}) collective-permute-start(f32[136,128]{1,0:T(8,128)S(1)} %get-tuple-element.92), channel_id=1, source_target_pairs={{0,2},{2,0},{4,6},{6,4},{8,10},{10,8},{12,14},{14,12},{16,18},{18,... | collective-permute-start | bytes 208904 | tf_op jit(solution)/shard_map/ppermute | solution.py:172
  37.6 4.3 %collective-permute-start.17 = (f32[136,128]{1,0:T(8,128)S(1)}, f32[136,128]{1,0:T(8,128)S(1)}, u32[]{:S(2)}, u32[]{:S(2)}) collective-permute-start(f32[136,128]{1,0:T(8,128)S(1)} %get-tuple-element.93), channel_id=1, source_target_pairs={{0,4},{2,6},{4,0},{6,2},{8,12},{10,14},{12,8},{14,10},{16,20},{18,... | collective-permute-start | bytes 208904 | tf_op jit(solution)/shard_map/ppermute | solution.py:172
  39.1 5.2 %collective-permute-start.18 = (f32[136,128]{1,0:T(8,128)S(1)}, f32[136,128]{1,0:T(8,128)S(1)}, u32[]{:S(2)}, u32[]{:S(2)}) collective-permute-start(f32[136,128]{1,0:T(8,128)S(1)} %get-tuple-element.94), channel_id=1, source_target_pairs={{0,6},{2,4},{4,2},{6,0},{8,14},{10,12},{12,10},{14,8},{16,22},{18,... | collective-permute-start | bytes 208904 | tf_op jit(solution)/shard_map/ppermute | solution.py:172
  40.3 5.1 %collective-permute-start.27 = (f32[136,128]{1,0:T(8,128)S(1)}, f32[136,128]{1,0:T(8,128)S(1)}, u32[]{:S(2)}, u32[]{:S(2)}) collective-permute-start(f32[136,128]{1,0:T(8,128)S(1)} %add_add_fusion), channel_id=1, source_target_pairs={{0,8},{2,10},{4,12},{6,14},{8,0},{10,2},{12,4},{14,6},{16,24},{18,... | collective-permute-start | bytes 208904 | tf_op jit(solution)/shard_map/ppermute | solution.py:172
  44.4 4.9 %collective-permute-start.19 = (f32[136,128]{1,0:T(8,128)S(1)}, f32[136,128]{1,0:T(8,128)S(1)}, u32[]{:S(2)}, u32[]{:S(2)}) collective-permute-start(f32[136,128]{1,0:T(8,128)S(1)} %add_add_fusion.1), channel_id=1, source_target_pairs={{0,8},{2,10},{4,12},{6,14},{8,0},{10,2},{12,4},{14,6},{16,24},{18,... | collective-permute-start | bytes 208904 | tf_op jit(solution)/shard_map/ppermute | solution.py:172
  45.5 6.0 %collective-permute-start.28 = (f32[136,128]{1,0:T(8,128)S(1)}, f32[136,128]{1,0:T(8,128)S(1)}, u32[]{:S(2)}, u32[]{:S(2)}) collective-permute-start(f32[136,128]{1,0:T(8,128)S(1)} %add.81), channel_id=1, source_target_pairs={{0,16},{2,18},{4,20},{6,22},{8,24},{10,26},{12,28},{14,30},{16,0},... | collective-permute-start | bytes 208904 | tf_op jit(solution)/shard_map/ppermute | solution.py:172
  49.3 6.0 %collective-permute-start.20 = (f32[136,128]{1,0:T(8,128)S(1)}, f32[136,128]{1,0:T(8,128)S(1)}, u32[]{:S(2)}, u32[]{:S(2)}) collective-permute-start(f32[136,128]{1,0:T(8,128)S(1)} %add.76), channel_id=1, source_target_pairs={{0,16},{2,18},{4,20},{6,22},{8,24},{10,26},{12,28},{14,30},{16,0},... | collective-permute-start | bytes 208904 | tf_op jit(solution)/shard_map/ppermute | solution.py:172
  51.6 5.7 %collective-permute-start.29 = (f32[136,128]{1,0:T(8,128)S(1)}, f32[136,128]{1,0:T(8,128)S(1)}, u32[]{:S(2)}, u32[]{:S(2)}) collective-permute-start(f32[136,128]{1,0:T(8,128)S(1)} %get-tuple-element.125), channel_id=1, source_target_pairs={{0,2},{2,0},{4,6},{6,4},{8,10},{10,8},{12,14},{14,12},{16,18},{18,... | collective-permute-start | bytes 208904 | tf_op jit(solution)/shard_map/ppermute | solution.py:172
  51.7 9.2 %collective-permute-start.30 = (f32[136,128]{1,0:T(8,128)S(1)}, f32[136,128]{1,0:T(8,128)S(1)}, u32[]{:S(2)}, u32[]{:S(2)}) collective-permute-start(f32[136,128]{1,0:T(8,128)S(1)} %get-tuple-element.126), channel_id=1, source_target_pairs={{0,4},{2,6},{4,0},{6,2},{8,12},{10,14},{12,8},{14,10},{16,20},{18,... | collective-permute-start | bytes 208904 | tf_op jit(solution)/shard_map/ppermute | solution.py:172
  53.2 7.6 %collective-permute-start.31 = (f32[136,128]{1,0:T(8,128)S(1)}, f32[136,128]{1,0:T(8,128)S(1)}, u32[]{:S(2)}, u32[]{:S(2)}) collective-permute-start(f32[136,128]{1,0:T(8,128)S(1)} %get-tuple-element.127), channel_id=1, source_target_pairs={{0,6},{2,4},{4,2},{6,0},{8,14},{10,12},{12,10},{14,8},{16,22},{18,... | collective-permute-start | bytes 208904 | tf_op jit(solution)/shard_map/ppermute | solution.py:172
  55.4 5.5 %collective-permute-start.21 = (f32[136,128]{1,0:T(8,128)S(1)}, f32[136,128]{1,0:T(8,128)S(1)}, u32[]{:S(2)}, u32[]{:S(2)}) collective-permute-start(f32[136,128]{1,0:T(8,128)S(1)} %get-tuple-element.117), channel_id=1, source_target_pairs={{0,2},{2,0},{4,6},{6,4},{8,10},{10,8},{12,14},{14,12},{16,18},{18,... | collective-permute-start | bytes 208904 | tf_op jit(solution)/shard_map/ppermute | solution.py:172
  56.2 4.7 %collective-permute-start.22 = (f32[136,128]{1,0:T(8,128)S(1)}, f32[136,128]{1,0:T(8,128)S(1)}, u32[]{:S(2)}, u32[]{:S(2)}) collective-permute-start(f32[136,128]{1,0:T(8,128)S(1)} %get-tuple-element.118), channel_id=1, source_target_pairs={{0,4},{2,6},{4,0},{6,2},{8,12},{10,14},{12,8},{14,10},{16,20},{18,... | collective-permute-start | bytes 208904 | tf_op jit(solution)/shard_map/ppermute | solution.py:172
  57.3 5.2 %collective-permute-start.23 = (f32[136,128]{1,0:T(8,128)S(1)}, f32[136,128]{1,0:T(8,128)S(1)}, u32[]{:S(2)}, u32[]{:S(2)}) collective-permute-start(f32[136,128]{1,0:T(8,128)S(1)} %get-tuple-element.119), channel_id=1, source_target_pairs={{0,6},{2,4},{4,2},{6,0},{8,14},{10,12},{12,10},{14,8},{16,22},{18,... | collective-permute-start | bytes 208904 | tf_op jit(solution)/shard_map/ppermute | solution.py:172
  (6 other events, 68.1 us)

commit v13 on v12

--- a/solution.py
+++ b/solution.py
@@ -172,18 +172,23 @@
     return lax.ppermute(array, "seq", [(s, s ^ mask) for s in range(lax.axis_size("seq"))])
 
 
-def carried_in(pieces, reverse, place, beside=None, operands=()):
-    held = [swap(piece, mask) for mask, piece in enumerate(pieces)]
-    total, aside = sum(held[1:], held[0]), None
-    if beside:
-        total, operands = lax.optimization_barrier((total, operands))
-        aside = beside(*operands)
+def plane_swap(pieces):
+    return [swap(piece, mask) for mask, piece in enumerate(pieces)]
+
+
+def beside(function, operands, first, second):
+    total = sum(first[1:], first[0])
+    total, operands = lax.optimization_barrier((total, operands))
+    result = function(*operands)
+    second, result = lax.optimization_barrier((second, result))
+    return [(first, total), (second, sum(second[1:], second[0]))], result
+
+
+def carried_in(held, total, reverse, place):
     arrived = []
     for mask in exchange_masks():
         arrived.append(swap(total, mask))
         total = total + arrived[-1]
-        if beside and len(arrived) == 1:
-            total, aside = lax.optimization_barrier((total, aside))
     single = whole(*total.shape)
     back = call(
         functools.partial(prefix_body, reverse, exchange_masks()),
@@ -194,7 +199,7 @@
         "prefix",
         scratch=[pltpu.VMEM((GROUP, DH, DH), jnp.float32)],
     )(place, total, *arrived, *held)
-    return [swap(piece, mask) for mask, piece in enumerate(back)], aside
+    return [swap(piece, mask) for mask, piece in enumerate(back)]
 
 
 def local(queries, keys, values, out_gain, grad_out):
@@ -226,9 +231,9 @@
     inner_call = call(
         lambda place_ref, *refs: inner_body(*refs), [wide] * 3, wide, full_float, 16 * unit, "inner"
     )
-    first, inner = carried_in(deltas[chains[0]], False, place, inner_call, (place, query, key, value))
-    states = [first] + [carried_in(deltas[chain], False, place)[0] for chain in chains[1:]]
-    later, parts, grad_query = [], [], []
+    sums, inner = beside(inner_call, (place, query, key, value), *[plane_swap(deltas[chain]) for chain in chains])
+    states = [carried_in(held, total, False, place) for held, total in sums]
+    attns, helds = [], []
     for chain in range(CHAINS):
         attn, *deltas = call(
             functools.partial(norm_body, chain),
@@ -238,24 +243,25 @@
             8 * unit,
             "norm",
         )(place, query, grad, inner, gain, *states[chain])
-        partial_call = call(
+        attns.append(attn)
+        helds.append(plane_swap(deltas))
+
+    def partial_call(chain, *operands):
+        return call(
             functools.partial(partial_body, chain),
-            [wide] * 3 + [half] + [short] * GROUP + [pl.BlockSpec(memory_space=pl.ANY)] * len(grad_query),
-            [pl.BlockSpec((BLOCK, WIDE), lambda step, chain=chain: (0, chain)), half, half],
+            [wide] * 3 + [half] + [short] * GROUP + [pl.BlockSpec(memory_space=pl.ANY)] * chain,
+            [pl.BlockSpec((BLOCK, WIDE), lambda step: (0, chain)), half, half],
             [full_low, half_float, half_float],
             24 * unit,
             "partial",
-            aliases={5 + GROUP: 0} if grad_query else None,
-        )
-        operands = (place, query, key, value, attn, *states[chain], *grad_query)
-        if chain == 0:
-            pieces, aside = carried_in(deltas, True, place, partial_call, operands)
-        else:
-            pieces, aside = carried_in(deltas, True, place)[0], partial_call(*operands)
-        *grad_query, key_part, value_part = aside
-        later += pieces
-        parts += [key_part, value_part]
-    (grad_query,) = grad_query
+            aliases={5 + GROUP: 0} if chain else None,
+        )(*operands)
+
+    operands = [(place, query, key, value, attns[chain], *states[chain]) for chain in range(CHAINS)]
+    sums, (grad_query, *parts) = beside(functools.partial(partial_call, 0), operands[0], *helds)
+    later = [piece for held, total in sums for piece in carried_in(held, total, True, place)]
+    grad_query, *rest = partial_call(1, *operands[1], grad_query)
+    parts += rest
     gain_terms = call(
         gain_body, [tall] * HEADS, whole(HEADS, DH), jax.ShapeDtypeStruct((HEADS, DH), jnp.float32), unit, "gain"
     )(place, *later)

time: 64.9 us -> 64.4 us (level)
  waiting for transfers between devices: 12.2 us -> 8.49 us
  starting transfers between devices: 41.2 us -> 44.4 us
    ppermute x32, waiting for transfers between devices: 12.2 us -> 8.49 us  [swap(): lax.ppermute(array, 'seq', [(s, s ^ mask) for s in range(lax.axis_size('s...]
    ppermute x32, starting transfers between devices: 41.2 us -> 44.4 us  [swap(): lax.ppermute(array, 'seq', [(s, s ^ mask) for s in range(lax.axis_size('s...]
  transfers between devices with their start and end apart: 33 -> 33, of which waited for: 10 -> 8; matrix products, arithmetic and copies ran while one was open for 0% -> 0% of each run, Pallas kernels for 13% -> 13%
where the time goes in v13:
time: 64.4 us; the launch traced here: 64.3 us
  starting transfers between devices  44.4 us (69%)
  Pallas kernels  9.81 us (15%)
  waiting for transfers between devices  8.49 us (13%)
  between operations  0.83 us (1%)
  other arithmetic  0.75 us (1%)
    ppermute x32, starting transfers between devices, swap(): lax.ppermute(array, 'seq', [(s, s ^ mask) for s in range(lax.axis_size('s...  44.4 us
    ppermute x32, waiting for transfers between devices, swap(): lax.ppermute(array, 'seq', [(s, s ^ mask) for s in range(lax.axis_size('s...  8.49 us
    pallas_call x2, Pallas kernels, partial_call(): call(functools.partial(partial_body, chain), [wide] * 3 + [half] + [short...  3.83 us
    pallas_call x1, Pallas kernels, local(): call(delta_body, [pl.BlockSpec(memory_space=pltpu.HBM)] * 2, [short] * HE...  1.64 us
    pallas_call x1, Pallas kernels, local(): call(final_body, [wide] * 2 + [half] * (2 * CHAINS) + [tall] * HEADS, [ch...  1.62 us
    pallas_call x2, Pallas kernels, local(): call(functools.partial(norm_body, chain), [wide, wide, wide, whole(1, HEA...  1.47 us
  transfers between devices with their start and end apart: 33, of which 8 were waited for; matrix products, arithmetic and copies ran while one was open for 0% of the time, Pallas kernels for 13%

profile of v13, /device:TPU:0, one launch (start us, length us, event | category | flops | bytes accessed | tf_op | source)
XLA Modules:
  0.0 64.3 jit_solution(8757283031757801277)
XLA Ops:
  0.7 1.6 %delta.1 = (f32[128,128]{1,0:T(8,128)S(1)}, f32[128,128]{1,0:T(8,128)S(1)}, f32[128,128]{1,0:T(8,128)S(1)}, f32[128,128]{1,0:T(8,128)S(1)}, f32[128,128]{1,0:T(8...) custom-call(s32[1]{0:T(128)} %bitcast.place_ref, bf16[256,1024]{1,0:T(8,128)(2,1)} %bitcast.20, ...), custom_call_target="tpu_custom_call" | custom-call | flops 402653184 | bytes 2097152 | tf_op jit(solution)/shard_map/delta/pallas_call | solution.py:221
  2.3 3.0 %collective-permute-start.3 = (f32[128,128]{1,0:T(8,128)S(1)}, f32[128,128]{1,0:T(8,128)S(1)}, u32[]{:S(2)}, u32[]{:S(2)}) collective-permute-start(f32[128,128]{1,0:T(8,128)S(1)} %get-tuple-element.78), channel_id=1, source_target_pairs={{0,2},{2,0},{4,6},{6,4},{8,10},{10,8},{12,14},{14,12},{16,18},{18,... | collective-permute-start | bytes 196616 | tf_op jit(solution)/shard_map/ppermute | solution.py:172
  5.3 1.5 %collective-permute-start.4 = (f32[128,128]{1,0:T(8,128)S(1)}, f32[128,128]{1,0:T(8,128)S(1)}, u32[]{:S(2)}, u32[]{:S(2)}) collective-permute-start(f32[128,128]{1,0:T(8,128)S(1)} %get-tuple-element.79), channel_id=1, source_target_pairs={{0,4},{2,6},{4,0},{6,2},{8,12},{10,14},{12,8},{14,10},{16,20},{18,... | collective-permute-start | bytes 196616 | tf_op jit(solution)/shard_map/ppermute | solution.py:172
  6.9 1.9 %collective-permute-start = (f32[128,128]{1,0:T(8,128)S(1)}, f32[128,128]{1,0:T(8,128)S(1)}, u32[]{:S(2)}, u32[]{:S(2)}) collective-permute-start(f32[128,128]{1,0:T(8,128)S(1)} %get-tuple-element.74), channel_id=1, source_target_pairs={{0,2},{2,0},{4,6},{6,4},{8,10},{10,8},{12,14},{14,12},{16,18},{18,... | collective-permute-start | bytes 196616 | tf_op jit(solution)/shard_map/ppermute | solution.py:172
  8.8 1.5 %collective-permute-start.1 = (f32[128,128]{1,0:T(8,128)S(1)}, f32[128,128]{1,0:T(8,128)S(1)}, u32[]{:S(2)}, u32[]{:S(2)}) collective-permute-start(f32[128,128]{1,0:T(8,128)S(1)} %get-tuple-element.75), channel_id=1, source_target_pairs={{0,4},{2,6},{4,0},{6,2},{8,12},{10,14},{12,8},{14,10},{16,20},{18,... | collective-permute-start | bytes 196616 | tf_op jit(solution)/shard_map/ppermute | solution.py:172
  10.9 1.1 %collective-permute-done.5.refs_6_ = f32[128,128]{1,0:T(8,128)S(1)} collective-permute-done((f32[128,128]{1,0:T(8,128)S(1)}, f32[128,128]{1,0:T(8,128)S(1)}, u32[]{:S(2)}, u32[]{:S(2)}) %collective-permute-start.5) | collective-permute-done | bytes 65568 | tf_op jit(solution)/shard_map/ppermute | solution.py:172
  12.0 1.6 %collective-permute-start.14 = (f32[128,128]{1,0:T(8,128)S(1)}, f32[128,128]{1,0:T(8,128)S(1)}, u32[]{:S(2)}, u32[]{:S(2)}) collective-permute-start(f32[128,128]{1,0:T(8,128)S(1)} %add_add_fusion.3), channel_id=1, source_target_pairs={{0,8},{2,10},{4,12},{6,14},{8,0},{10,2},{12,4},{14,6},{16,24},{18,... | collective-permute-start | bytes 196616 | tf_op jit(solution)/shard_map/ppermute | solution.py:172
  13.7 0.9 %inner.1.inner_ref = f32[256,1024]{1,0:T(8,128)S(1)} custom-call(s32[1]{0:T(128)} %bitcast.place_ref, bf16[256,1024]{1,0:T(8,128)(2,1)S(1)} %bitcast.13, bf16[256,1024]{1,0:T(8,128)(2,1)S(1)} %bitcast.21, bf16[256,1024]{1,0:T(8,128)(2,1)S(1)} %bitcast.26), custom_call_target="tpu_custom_call" | custom-call | flops 1073741824 | bytes 2097152 | tf_op jit(solution)/shard_map/inner/pallas_call | solution.py:182
  14.6 0.9 %collective-permute-done.2.refs_6_ = f32[128,128]{1,0:T(8,128)S(1)} collective-permute-done((f32[128,128]{1,0:T(8,128)S(1)}, f32[128,128]{1,0:T(8,128)S(1)}, u32[]{:S(2)}, u32[]{:S(2)}) %collective-permute-start.2) | collective-permute-done | bytes 65568 | tf_op jit(solution)/shard_map/ppermute | solution.py:172
  15.5 1.6 %collective-permute-start.6 = (f32[128,128]{1,0:T(8,128)S(1)}, f32[128,128]{1,0:T(8,128)S(1)}, u32[]{:S(2)}, u32[]{:S(2)}) collective-permute-start(f32[128,128]{1,0:T(8,128)S(1)} %add_add_fusion.2), channel_id=1, source_target_pairs={{0,8},{2,10},{4,12},{6,14},{8,0},{10,2},{12,4},{14,6},{16,24},{18,... | collective-permute-start | bytes 196616 | tf_op jit(solution)/shard_map/ppermute | solution.py:172
  17.2 2.7 %collective-permute-start.15 = (f32[128,128]{1,0:T(8,128)S(1)}, f32[128,128]{1,0:T(8,128)S(1)}, u32[]{:S(2)}, u32[]{:S(2)}) collective-permute-start(f32[128,128]{1,0:T(8,128)S(1)} %add.71), channel_id=1, source_target_pairs={{0,16},{2,18},{4,20},{6,22},{8,24},{10,26},{12,28},{14,30},{16,0},... | collective-permute-start | bytes 196616 | tf_op jit(solution)/shard_map/ppermute | solution.py:172
  19.9 3.0 %collective-permute-start.7 = (f32[128,128]{1,0:T(8,128)S(1)}, f32[128,128]{1,0:T(8,128)S(1)}, u32[]{:S(2)}, u32[]{:S(2)}) collective-permute-start(f32[128,128]{1,0:T(8,128)S(1)} %add.69), channel_id=1, source_target_pairs={{0,16},{2,18},{4,20},{6,22},{8,24},{10,26},{12,28},{14,30},{16,0},... | collective-permute-start | bytes 196616 | tf_op jit(solution)/shard_map/ppermute | solution.py:172
  25.2 2.2 %collective-permute-start.18 = (f32[128,128]{1,0:T(8,128)S(1)}, f32[128,128]{1,0:T(8,128)S(1)}, u32[]{:S(2)}, u32[]{:S(2)}) collective-permute-start(f32[128,128]{1,0:T(8,128)S(1)} %get-tuple-element.103), channel_id=1, source_target_pairs={{0,6},{2,4},{4,2},{6,0},{8,14},{10,12},{12,10},{14,8},{16,22},{18,... | collective-permute-start | bytes 196616 | tf_op jit(solution)/shard_map/ppermute | solution.py:172
  28.9 2.2 %collective-permute-start.10 = (f32[128,128]{1,0:T(8,128)S(1)}, f32[128,128]{1,0:T(8,128)S(1)}, u32[]{:S(2)}, u32[]{:S(2)}) collective-permute-start(f32[128,128]{1,0:T(8,128)S(1)} %get-tuple-element.93), channel_id=1, source_target_pairs={{0,6},{2,4},{4,2},{6,0},{8,14},{10,12},{12,10},{14,8},{16,22},{18,... | collective-permute-start | bytes 196616 | tf_op jit(solution)/shard_map/ppermute | solution.py:172
  31.8 1.0 %collective-permute-start.19 = (f32[136,128]{1,0:T(8,128)S(1)}, f32[136,128]{1,0:T(8,128)S(1)}, u32[]{:S(2)}, u32[]{:S(2)}) collective-permute-start(f32[136,128]{1,0:T(8,128)S(1)} %get-tuple-element.105), channel_id=1, source_target_pairs={{0,2},{2,0},{4,6},{6,4},{8,10},{10,8},{12,14},{14,12},{16,18},{18,... | collective-permute-start | bytes 208904 | tf_op jit(solution)/shard_map/ppermute | solution.py:172
  32.7 1.6 %collective-permute-start.20 = (f32[136,128]{1,0:T(8,128)S(1)}, f32[136,128]{1,0:T(8,128)S(1)}, u32[]{:S(2)}, u32[]{:S(2)}) collective-permute-start(f32[136,128]{1,0:T(8,128)S(1)} %get-tuple-element.106), channel_id=1, source_target_pairs={{0,4},{2,6},{4,0},{6,2},{8,12},{10,14},{12,8},{14,10},{16,20},{18,... | collective-permute-start | bytes 208904 | tf_op jit(solution)/shard_map/ppermute | solution.py:172
  34.3 1.0 %collective-permute-start.21 = (f32[136,128]{1,0:T(8,128)S(1)}, f32[136,128]{1,0:T(8,128)S(1)}, u32[]{:S(2)}, u32[]{:S(2)}) collective-permute-start(f32[136,128]{1,0:T(8,128)S(1)} %get-tuple-element.107), channel_id=1, source_target_pairs={{0,6},{2,4},{4,2},{6,0},{8,14},{10,12},{12,10},{14,8},{16,22},{18,... | collective-permute-start | bytes 208904 | tf_op jit(solution)/shard_map/ppermute | solution.py:172
  36.1 1.0 %collective-permute-start.11 = (f32[136,128]{1,0:T(8,128)S(1)}, f32[136,128]{1,0:T(8,128)S(1)}, u32[]{:S(2)}, u32[]{:S(2)}) collective-permute-start(f32[136,128]{1,0:T(8,128)S(1)} %get-tuple-element.96), channel_id=1, source_target_pairs={{0,2},{2,0},{4,6},{6,4},{8,10},{10,8},{12,14},{14,12},{16,18},{18,... | collective-permute-start | bytes 208904 | tf_op jit(solution)/shard_map/ppermute | solution.py:172
  37.0 1.6 %collective-permute-start.12 = (f32[136,128]{1,0:T(8,128)S(1)}, f32[136,128]{1,0:T(8,128)S(1)}, u32[]{:S(2)}, u32[]{:S(2)}) collective-permute-start(f32[136,128]{1,0:T(8,128)S(1)} %get-tuple-element.97), channel_id=1, source_target_pairs={{0,4},{2,6},{4,0},{6,2},{8,12},{10,14},{12,8},{14,10},{16,20},{18,... | collective-permute-start | bytes 208904 | tf_op jit(solution)/shard_map/ppermute | solution.py:172
  38.6 1.0 %collective-permute-start.13 = (f32[136,128]{1,0:T(8,128)S(1)}, f32[136,128]{1,0:T(8,128)S(1)}, u32[]{:S(2)}, u32[]{:S(2)}) collective-permute-start(f32[136,128]{1,0:T(8,128)S(1)} %get-tuple-element.98), channel_id=1, source_target_pairs={{0,6},{2,4},{4,2},{6,0},{8,14},{10,12},{12,10},{14,8},{16,22},{18,... | collective-permute-start | bytes 208904 | tf_op jit(solution)/shard_map/ppermute | solution.py:172
  40.1 1.9 %partial.2 = (bf16[256,1024]{1,0:T(8,128)(2,1)}, f32[256,512]{1,0:T(8,128)S(1)}, f32[256,512]{1,0:T(8,128)S(1)}) custom-call(s32[1]{0:T(128)} %bitcast.place_ref, bf16[256,1024]{1,0:T(8,128)(2,1)S(1)} %bitcast.16, bf16[256,1024]{1,0:T(8,128)(2,1)S(1)} %bitcast.22, bf16[256,1024]{1,0:T(8,128)(2,1)S(1)} %bitcast.27, ...), custom_call_target="tpu_custom_call" | custom-call | flops 1610612736 | bytes 2097152 | tf_op jit(solution)/shard_map/partial/pallas_call | solution.py:250
  42.1 1.8 %collective-permute-done.13.refs_6_ = f32[136,128]{1,0:T(8,128)S(1)} collective-permute-done((f32[136,128]{1,0:T(8,128)S(1)}, f32[136,128]{1,0:T(8,128)S(1)}, u32[]{:S(2)}, u32[]{:S(2)}) %collective-permute-start.13) | collective-permute-done | bytes 69664 | tf_op jit(solution)/shard_map/ppermute | solution.py:172
  44.2 3.2 %collective-permute-start.23 = (f32[136,128]{1,0:T(8,128)S(1)}, f32[136,128]{1,0:T(8,128)S(1)}, u32[]{:S(2)}, u32[]{:S(2)}) collective-permute-start(f32[136,128]{1,0:T(8,128)S(1)} %add.76), channel_id=1, source_target_pairs={{0,16},{2,18},{4,20},{6,22},{8,24},{10,26},{12,28},{14,30},{16,0},... | collective-permute-start | bytes 208904 | tf_op jit(solution)/shard_map/ppermute | solution.py:172
  48.3 1.5 %collective-permute-start.28 = (f32[136,128]{1,0:T(8,128)S(1)}, f32[136,128]{1,0:T(8,128)S(1)}, u32[]{:S(2)}, u32[]{:S(2)}) collective-permute-start(f32[136,128]{1,0:T(8,128)S(1)} %add.81), channel_id=1, source_target_pairs={{0,16},{2,18},{4,20},{6,22},{8,24},{10,26},{12,28},{14,30},{16,0},... | collective-permute-start | bytes 208904 | tf_op jit(solution)/shard_map/ppermute | solution.py:172
  49.9 1.7 %collective-permute-start.24 = (f32[136,128]{1,0:T(8,128)S(1)}, f32[136,128]{1,0:T(8,128)S(1)}, u32[]{:S(2)}, u32[]{:S(2)}) collective-permute-start(f32[136,128]{1,0:T(8,128)S(1)} %get-tuple-element.129), channel_id=1, source_target_pairs={{0,2},{2,0},{4,6},{6,4},{8,10},{10,8},{12,14},{14,12},{16,18},{18,... | collective-permute-start | bytes 208904 | tf_op jit(solution)/shard_map/ppermute | solution.py:172
  51.6 1.6 %collective-permute-start.25 = (f32[136,128]{1,0:T(8,128)S(1)}, f32[136,128]{1,0:T(8,128)S(1)}, u32[]{:S(2)}, u32[]{:S(2)}) collective-permute-start(f32[136,128]{1,0:T(8,128)S(1)} %get-tuple-element.130), channel_id=1, source_target_pairs={{0,4},{2,6},{4,0},{6,2},{8,12},{10,14},{12,8},{14,10},{16,20},{18,... | collective-permute-start | bytes 208904 | tf_op jit(solution)/shard_map/ppermute | solution.py:172
  54.3 0.9 %collective-permute-start.29 = (f32[136,128]{1,0:T(8,128)S(1)}, f32[136,128]{1,0:T(8,128)S(1)}, u32[]{:S(2)}, u32[]{:S(2)}) collective-permute-start(f32[136,128]{1,0:T(8,128)S(1)} %get-tuple-element.137), channel_id=1, source_target_pairs={{0,2},{2,0},{4,6},{6,4},{8,10},{10,8},{12,14},{14,12},{16,18},{18,... | collective-permute-start | bytes 208904 | tf_op jit(solution)/shard_map/ppermute | solution.py:172
  55.2 1.6 %collective-permute-start.30 = (f32[136,128]{1,0:T(8,128)S(1)}, f32[136,128]{1,0:T(8,128)S(1)}, u32[]{:S(2)}, u32[]{:S(2)}) collective-permute-start(f32[136,128]{1,0:T(8,128)S(1)} %get-tuple-element.138), channel_id=1, source_target_pairs={{0,4},{2,6},{4,0},{6,2},{8,12},{10,14},{12,8},{14,10},{16,20},{18,... | collective-permute-start | bytes 208904 | tf_op jit(solution)/shard_map/ppermute | solution.py:172
  56.8 1.0 %collective-permute-start.31 = (f32[136,128]{1,0:T(8,128)S(1)}, f32[136,128]{1,0:T(8,128)S(1)}, u32[]{:S(2)}, u32[]{:S(2)}) collective-permute-start(f32[136,128]{1,0:T(8,128)S(1)} %get-tuple-element.139), channel_id=1, source_target_pairs={{0,6},{2,4},{4,2},{6,0},{8,14},{10,12},{12,10},{14,8},{16,22},{18,... | collective-permute-start | bytes 208904 | tf_op jit(solution)/shard_map/ppermute | solution.py:172
  57.8 1.9 %partial.3 = (bf16[256,1024]{1,0:T(8,128)(2,1)}, f32[256,512]{1,0:T(8,128)S(1)}, f32[256,512]{1,0:T(8,128)S(1)}) custom-call(s32[1]{0:T(128)} %bitcast.place_ref, bf16[256,1024]{1,0:T(8,128)(2,1)S(1)} %bitcast.17, bf16[256,1024]{1,0:T(8,128)(2,1)S(1)} %bitcast.23, bf16[256,1024]{1,0:T(8,128)(2,1)S(1)} %bitcast.28, ...), custom_call_target="tpu_custom_call", output_to_operand_aliasing={{0}: (9, {})} | custom-call | flops 1610612736 | bytes 2097152 | tf_op jit(solution)/shard_map/partial/pallas_call | solution.py:250
  59.8 2.3 %collective-permute-done.31.refs_11_.refs_7_ = f32[136,128]{1,0:T(8,128)S(1)} collective-permute-done((f32[136,128]{1,0:T(8,128)S(1)}, f32[136,128]{1,0:T(8,128)S(1)}, u32[]{:S(2)}, u32[]{:S(2)}) %collective-permute-start.31) | collective-permute-done | bytes 69664 | tf_op jit(solution)/shard_map/ppermute | solution.py:172
  62.1 1.6 %final.1 = (bf16[256,1024]{1,0:T(8,128)(2,1)}, bf16[256,1024]{1,0:T(8,128)(2,1)}) custom-call(s32[1]{0:T(128)} %bitcast.place_ref, bf16[256,1024]{1,0:T(8,128)(2,1)S(1)} %bitcast.24, bf16[256,1024]{1,0:T(8,128)(2,1)S(1)} %bitcast.29, f32[256,512]{1,0:T(8,128)S(1)} %get-tuple-element.123.refs_0_, f32[256,512]{1,0:T(8,128)S(1)} %get-tuple-element.124.refs_1_, ...), custom_call_target="tpu_custom_call" | custom-call | flops 1073741824 | bytes 2097152 | tf_op jit(solution)/shard_map/final/pallas_call | solution.py:273
  (69 shorter events, 9.5 us)
Async XLA Ops:
  2.3 8.0 %collective-permute-start.3 = (f32[128,128]{1,0:T(8,128)S(1)}, f32[128,128]{1,0:T(8,128)S(1)}, u32[]{:S(2)}, u32[]{:S(2)}) collective-permute-start(f32[128,128]{1,0:T(8,128)S(1)} %get-tuple-element.78), channel_id=1, source_target_pairs={{0,2},{2,0},{4,6},{6,4},{8,10},{10,8},{12,14},{14,12},{16,18},{18,... | collective-permute-start | bytes 196616 | tf_op jit(solution)/shard_map/ppermute | solution.py:172
  5.3 5.6 %collective-permute-start.4 = (f32[128,128]{1,0:T(8,128)S(1)}, f32[128,128]{1,0:T(8,128)S(1)}, u32[]{:S(2)}, u32[]{:S(2)}) collective-permute-start(f32[128,128]{1,0:T(8,128)S(1)} %get-tuple-element.79), channel_id=1, source_target_pairs={{0,4},{2,6},{4,0},{6,2},{8,12},{10,14},{12,8},{14,10},{16,20},{18,... | collective-permute-start | bytes 196616 | tf_op jit(solution)/shard_map/ppermute | solution.py:172
  6.8 5.2 %collective-permute-start.5 = (f32[128,128]{1,0:T(8,128)S(1)}, f32[128,128]{1,0:T(8,128)S(1)}, u32[]{:S(2)}, u32[]{:S(2)}) collective-permute-start(f32[128,128]{1,0:T(8,128)S(1)} %get-tuple-element.80), channel_id=1, source_target_pairs={{0,6},{2,4},{4,2},{6,0},{8,14},{10,12},{12,10},{14,8},{16,22},{18,... | collective-permute-start | bytes 196616 | tf_op jit(solution)/shard_map/ppermute | solution.py:172
  6.9 7.8 %collective-permute-start = (f32[128,128]{1,0:T(8,128)S(1)}, f32[128,128]{1,0:T(8,128)S(1)}, u32[]{:S(2)}, u32[]{:S(2)}) collective-permute-start(f32[128,128]{1,0:T(8,128)S(1)} %get-tuple-element.74), channel_id=1, source_target_pairs={{0,2},{2,0},{4,6},{6,4},{8,10},{10,8},{12,14},{14,12},{16,18},{18,... | collective-permute-start | bytes 196616 | tf_op jit(solution)/shard_map/ppermute | solution.py:172
  8.8 5.8 %collective-permute-start.1 = (f32[128,128]{1,0:T(8,128)S(1)}, f32[128,128]{1,0:T(8,128)S(1)}, u32[]{:S(2)}, u32[]{:S(2)}) collective-permute-start(f32[128,128]{1,0:T(8,128)S(1)} %get-tuple-element.75), channel_id=1, source_target_pairs={{0,4},{2,6},{4,0},{6,2},{8,12},{10,14},{12,8},{14,10},{16,20},{18,... | collective-permute-start | bytes 196616 | tf_op jit(solution)/shard_map/ppermute | solution.py:172
  10.3 5.2 %collective-permute-start.2 = (f32[128,128]{1,0:T(8,128)S(1)}, f32[128,128]{1,0:T(8,128)S(1)}, u32[]{:S(2)}, u32[]{:S(2)}) collective-permute-start(f32[128,128]{1,0:T(8,128)S(1)} %get-tuple-element.76), channel_id=1, source_target_pairs={{0,6},{2,4},{4,2},{6,0},{8,14},{10,12},{12,10},{14,8},{16,22},{18,... | collective-permute-start | bytes 196616 | tf_op jit(solution)/shard_map/ppermute | solution.py:172
  12.0 5.1 %collective-permute-start.14 = (f32[128,128]{1,0:T(8,128)S(1)}, f32[128,128]{1,0:T(8,128)S(1)}, u32[]{:S(2)}, u32[]{:S(2)}) collective-permute-start(f32[128,128]{1,0:T(8,128)S(1)} %add_add_fusion.3), channel_id=1, source_target_pairs={{0,8},{2,10},{4,12},{6,14},{8,0},{10,2},{12,4},{14,6},{16,24},{18,... | collective-permute-start | bytes 196616 | tf_op jit(solution)/shard_map/ppermute | solution.py:172
  15.5 4.3 %collective-permute-start.6 = (f32[128,128]{1,0:T(8,128)S(1)}, f32[128,128]{1,0:T(8,128)S(1)}, u32[]{:S(2)}, u32[]{:S(2)}) collective-permute-start(f32[128,128]{1,0:T(8,128)S(1)} %add_add_fusion.2), channel_id=1, source_target_pairs={{0,8},{2,10},{4,12},{6,14},{8,0},{10,2},{12,4},{14,6},{16,24},{18,... | collective-permute-start | bytes 196616 | tf_op jit(solution)/shard_map/ppermute | solution.py:172
  17.2 6.5 %collective-permute-start.15 = (f32[128,128]{1,0:T(8,128)S(1)}, f32[128,128]{1,0:T(8,128)S(1)}, u32[]{:S(2)}, u32[]{:S(2)}) collective-permute-start(f32[128,128]{1,0:T(8,128)S(1)} %add.71), channel_id=1, source_target_pairs={{0,16},{2,18},{4,20},{6,22},{8,24},{10,26},{12,28},{14,30},{16,0},... | collective-permute-start | bytes 196616 | tf_op jit(solution)/shard_map/ppermute | solution.py:172
  19.9 7.5 %collective-permute-start.7 = (f32[128,128]{1,0:T(8,128)S(1)}, f32[128,128]{1,0:T(8,128)S(1)}, u32[]{:S(2)}, u32[]{:S(2)}) collective-permute-start(f32[128,128]{1,0:T(8,128)S(1)} %add.69), channel_id=1, source_target_pairs={{0,16},{2,18},{4,20},{6,22},{8,24},{10,26},{12,28},{14,30},{16,0},... | collective-permute-start | bytes 196616 | tf_op jit(solution)/shard_map/ppermute | solution.py:172
  23.8 5.1 %collective-permute-start.16 = (f32[128,128]{1,0:T(8,128)S(1)}, f32[128,128]{1,0:T(8,128)S(1)}, u32[]{:S(2)}, u32[]{:S(2)}) collective-permute-start(f32[128,128]{1,0:T(8,128)S(1)} %get-tuple-element.101), channel_id=1, source_target_pairs={{0,2},{2,0},{4,6},{6,4},{8,10},{10,8},{12,14},{14,12},{16,18},{18,... | collective-permute-start | bytes 196616 | tf_op jit(solution)/shard_map/ppermute | solution.py:172
  24.4 6.6 %collective-permute-start.17 = (f32[128,128]{1,0:T(8,128)S(1)}, f32[128,128]{1,0:T(8,128)S(1)}, u32[]{:S(2)}, u32[]{:S(2)}) collective-permute-start(f32[128,128]{1,0:T(8,128)S(1)} %get-tuple-element.102), channel_id=1, source_target_pairs={{0,4},{2,6},{4,0},{6,2},{8,12},{10,14},{12,8},{14,10},{16,20},{18,... | collective-permute-start | bytes 196616 | tf_op jit(solution)/shard_map/ppermute | solution.py:172
  25.2 5.8 %collective-permute-start.18 = (f32[128,128]{1,0:T(8,128)S(1)}, f32[128,128]{1,0:T(8,128)S(1)}, u32[]{:S(2)}, u32[]{:S(2)}) collective-permute-start(f32[128,128]{1,0:T(8,128)S(1)} %get-tuple-element.103), channel_id=1, source_target_pairs={{0,6},{2,4},{4,2},{6,0},{8,14},{10,12},{12,10},{14,8},{16,22},{18,... | collective-permute-start | bytes 196616 | tf_op jit(solution)/shard_map/ppermute | solution.py:172
  27.5 6.9 %collective-permute-start.8 = (f32[128,128]{1,0:T(8,128)S(1)}, f32[128,128]{1,0:T(8,128)S(1)}, u32[]{:S(2)}, u32[]{:S(2)}) collective-permute-start(f32[128,128]{1,0:T(8,128)S(1)} %get-tuple-element.91), channel_id=1, source_target_pairs={{0,2},{2,0},{4,6},{6,4},{8,10},{10,8},{12,14},{14,12},{16,18},{18,... | collective-permute-start | bytes 196616 | tf_op jit(solution)/shard_map/ppermute | solution.py:172
  28.1 7.3 %collective-permute-start.9 = (f32[128,128]{1,0:T(8,128)S(1)}, f32[128,128]{1,0:T(8,128)S(1)}, u32[]{:S(2)}, u32[]{:S(2)}) collective-permute-start(f32[128,128]{1,0:T(8,128)S(1)} %get-tuple-element.92), channel_id=1, source_target_pairs={{0,4},{2,6},{4,0},{6,2},{8,12},{10,14},{12,8},{14,10},{16,20},{18,... | collective-permute-start | bytes 196616 | tf_op jit(solution)/shard_map/ppermute | solution.py:172
  28.9 6.5 %collective-permute-start.10 = (f32[128,128]{1,0:T(8,128)S(1)}, f32[128,128]{1,0:T(8,128)S(1)}, u32[]{:S(2)}, u32[]{:S(2)}) collective-permute-start(f32[128,128]{1,0:T(8,128)S(1)} %get-tuple-element.93), channel_id=1, source_target_pairs={{0,6},{2,4},{4,2},{6,0},{8,14},{10,12},{12,10},{14,8},{16,22},{18,... | collective-permute-start | bytes 196616 | tf_op jit(solution)/shard_map/ppermute | solution.py:172
  31.8 6.8 %collective-permute-start.19 = (f32[136,128]{1,0:T(8,128)S(1)}, f32[136,128]{1,0:T(8,128)S(1)}, u32[]{:S(2)}, u32[]{:S(2)}) collective-permute-start(f32[136,128]{1,0:T(8,128)S(1)} %get-tuple-element.105), channel_id=1, source_target_pairs={{0,2},{2,0},{4,6},{6,4},{8,10},{10,8},{12,14},{14,12},{16,18},{18,... | collective-permute-start | bytes 208904 | tf_op jit(solution)/shard_map/ppermute | solution.py:172
  32.7 6.9 %collective-permute-start.20 = (f32[136,128]{1,0:T(8,128)S(1)}, f32[136,128]{1,0:T(8,128)S(1)}, u32[]{:S(2)}, u32[]{:S(2)}) collective-permute-start(f32[136,128]{1,0:T(8,128)S(1)} %get-tuple-element.106), channel_id=1, source_target_pairs={{0,4},{2,6},{4,0},{6,2},{8,12},{10,14},{12,8},{14,10},{16,20},{18,... | collective-permute-start | bytes 208904 | tf_op jit(solution)/shard_map/ppermute | solution.py:172
  34.3 5.3 %collective-permute-start.21 = (f32[136,128]{1,0:T(8,128)S(1)}, f32[136,128]{1,0:T(8,128)S(1)}, u32[]{:S(2)}, u32[]{:S(2)}) collective-permute-start(f32[136,128]{1,0:T(8,128)S(1)} %get-tuple-element.107), channel_id=1, source_target_pairs={{0,6},{2,4},{4,2},{6,0},{8,14},{10,12},{12,10},{14,8},{16,22},{18,... | collective-permute-start | bytes 208904 | tf_op jit(solution)/shard_map/ppermute | solution.py:172
  36.1 6.0 %collective-permute-start.11 = (f32[136,128]{1,0:T(8,128)S(1)}, f32[136,128]{1,0:T(8,128)S(1)}, u32[]{:S(2)}, u32[]{:S(2)}) collective-permute-start(f32[136,128]{1,0:T(8,128)S(1)} %get-tuple-element.96), channel_id=1, source_target_pairs={{0,2},{2,0},{4,6},{6,4},{8,10},{10,8},{12,14},{14,12},{16,18},{18,... | collective-permute-start | bytes 208904 | tf_op jit(solution)/shard_map/ppermute | solution.py:172
  37.0 5.0 %collective-permute-start.12 = (f32[136,128]{1,0:T(8,128)S(1)}, f32[136,128]{1,0:T(8,128)S(1)}, u32[]{:S(2)}, u32[]{:S(2)}) collective-permute-start(f32[136,128]{1,0:T(8,128)S(1)} %get-tuple-element.97), channel_id=1, source_target_pairs={{0,4},{2,6},{4,0},{6,2},{8,12},{10,14},{12,8},{14,10},{16,20},{18,... | collective-permute-start | bytes 208904 | tf_op jit(solution)/shard_map/ppermute | solution.py:172
  38.6 5.2 %collective-permute-start.13 = (f32[136,128]{1,0:T(8,128)S(1)}, f32[136,128]{1,0:T(8,128)S(1)}, u32[]{:S(2)}, u32[]{:S(2)}) collective-permute-start(f32[136,128]{1,0:T(8,128)S(1)} %get-tuple-element.98), channel_id=1, source_target_pairs={{0,6},{2,4},{4,2},{6,0},{8,14},{10,12},{12,10},{14,8},{16,22},{18,... | collective-permute-start | bytes 208904 | tf_op jit(solution)/shard_map/ppermute | solution.py:172
  39.7 4.5 %collective-permute-start.22 = (f32[136,128]{1,0:T(8,128)S(1)}, f32[136,128]{1,0:T(8,128)S(1)}, u32[]{:S(2)}, u32[]{:S(2)}) collective-permute-start(f32[136,128]{1,0:T(8,128)S(1)} %add_add_fusion.1), channel_id=1, source_target_pairs={{0,8},{2,10},{4,12},{6,14},{8,0},{10,2},{12,4},{14,6},{16,24},{18,... | collective-permute-start | bytes 208904 | tf_op jit(solution)/shard_map/ppermute | solution.py:172
  43.9 4.4 %collective-permute-start.27 = (f32[136,128]{1,0:T(8,128)S(1)}, f32[136,128]{1,0:T(8,128)S(1)}, u32[]{:S(2)}, u32[]{:S(2)}) collective-permute-start(f32[136,128]{1,0:T(8,128)S(1)} %add_add_fusion), channel_id=1, source_target_pairs={{0,8},{2,10},{4,12},{6,14},{8,0},{10,2},{12,4},{14,6},{16,24},{18,... | collective-permute-start | bytes 208904 | tf_op jit(solution)/shard_map/ppermute | solution.py:172
  44.2 5.6 %collective-permute-start.23 = (f32[136,128]{1,0:T(8,128)S(1)}, f32[136,128]{1,0:T(8,128)S(1)}, u32[]{:S(2)}, u32[]{:S(2)}) collective-permute-start(f32[136,128]{1,0:T(8,128)S(1)} %add.76), channel_id=1, source_target_pairs={{0,16},{2,18},{4,20},{6,22},{8,24},{10,26},{12,28},{14,30},{16,0},... | collective-permute-start | bytes 208904 | tf_op jit(solution)/shard_map/ppermute | solution.py:172
  48.3 5.9 %collective-permute-start.28 = (f32[136,128]{1,0:T(8,128)S(1)}, f32[136,128]{1,0:T(8,128)S(1)}, u32[]{:S(2)}, u32[]{:S(2)}) collective-permute-start(f32[136,128]{1,0:T(8,128)S(1)} %add.81), channel_id=1, source_target_pairs={{0,16},{2,18},{4,20},{6,22},{8,24},{10,26},{12,28},{14,30},{16,0},... | collective-permute-start | bytes 208904 | tf_op jit(solution)/shard_map/ppermute | solution.py:172
  49.9 6.9 %collective-permute-start.24 = (f32[136,128]{1,0:T(8,128)S(1)}, f32[136,128]{1,0:T(8,128)S(1)}, u32[]{:S(2)}, u32[]{:S(2)}) collective-permute-start(f32[136,128]{1,0:T(8,128)S(1)} %get-tuple-element.129), channel_id=1, source_target_pairs={{0,2},{2,0},{4,6},{6,4},{8,10},{10,8},{12,14},{14,12},{16,18},{18,... | collective-permute-start | bytes 208904 | tf_op jit(solution)/shard_map/ppermute | solution.py:172
  51.6 8.2 %collective-permute-start.25 = (f32[136,128]{1,0:T(8,128)S(1)}, f32[136,128]{1,0:T(8,128)S(1)}, u32[]{:S(2)}, u32[]{:S(2)}) collective-permute-start(f32[136,128]{1,0:T(8,128)S(1)} %get-tuple-element.130), channel_id=1, source_target_pairs={{0,4},{2,6},{4,0},{6,2},{8,12},{10,14},{12,8},{14,10},{16,20},{18,... | collective-permute-start | bytes 208904 | tf_op jit(solution)/shard_map/ppermute | solution.py:172
  53.2 6.6 %collective-permute-start.26 = (f32[136,128]{1,0:T(8,128)S(1)}, f32[136,128]{1,0:T(8,128)S(1)}, u32[]{:S(2)}, u32[]{:S(2)}) collective-permute-start(f32[136,128]{1,0:T(8,128)S(1)} %get-tuple-element.131), channel_id=1, source_target_pairs={{0,6},{2,4},{4,2},{6,0},{8,14},{10,12},{12,10},{14,8},{16,22},{18,... | collective-permute-start | bytes 208904 | tf_op jit(solution)/shard_map/ppermute | solution.py:172
  54.3 5.5 %collective-permute-start.29 = (f32[136,128]{1,0:T(8,128)S(1)}, f32[136,128]{1,0:T(8,128)S(1)}, u32[]{:S(2)}, u32[]{:S(2)}) collective-permute-start(f32[136,128]{1,0:T(8,128)S(1)} %get-tuple-element.137), channel_id=1, source_target_pairs={{0,2},{2,0},{4,6},{6,4},{8,10},{10,8},{12,14},{14,12},{16,18},{18,... | collective-permute-start | bytes 208904 | tf_op jit(solution)/shard_map/ppermute | solution.py:172
  55.2 4.5 %collective-permute-start.30 = (f32[136,128]{1,0:T(8,128)S(1)}, f32[136,128]{1,0:T(8,128)S(1)}, u32[]{:S(2)}, u32[]{:S(2)}) collective-permute-start(f32[136,128]{1,0:T(8,128)S(1)} %get-tuple-element.138), channel_id=1, source_target_pairs={{0,4},{2,6},{4,0},{6,2},{8,12},{10,14},{12,8},{14,10},{16,20},{18,... | collective-permute-start | bytes 208904 | tf_op jit(solution)/shard_map/ppermute | solution.py:172
  56.8 5.2 %collective-permute-start.31 = (f32[136,128]{1,0:T(8,128)S(1)}, f32[136,128]{1,0:T(8,128)S(1)}, u32[]{:S(2)}, u32[]{:S(2)}) collective-permute-start(f32[136,128]{1,0:T(8,128)S(1)} %get-tuple-element.139), channel_id=1, source_target_pairs={{0,6},{2,4},{4,2},{6,0},{8,14},{10,12},{12,10},{14,8},{16,22},{18,... | collective-permute-start | bytes 208904 | tf_op jit(solution)/shard_map/ppermute | solution.py:172
  (6 other events, 51.0 us)

commit v14 on v13

--- a/solution.py
+++ b/solution.py
@@ -15,6 +15,7 @@
 CHAINS = HEADS // GROUP
 WIDE = GROUP * DH
 GAIN_ROWS = 8
+ORDER = (0, 3, 2, 1)
 PARTS = 2
 PART_ROWS = BLOCK // PARTS
 EPSILON = 1e-06
@@ -54,7 +55,7 @@
         for copy in copies[2 * part : 2 * part + 2]:
             copy.wait()
         for at_head, delta_ref in enumerate(delta_refs):
-            at = own_columns(place_ref, at_head % GROUP, at_head // GROUP)
+            at = own_columns(place_ref, ORDER[at_head % GROUP], at_head // GROUP)
             delta = dot(key_here[rows, at], value_here[rows, at], TN)
             delta_ref[...] = delta if part == 0 else delta_ref[...] + delta
 
@@ -69,7 +70,7 @@
 
 def norm_body(chain, place_ref, query_ref, grad_ref, inner_ref, gain_ref, *refs):
     state_refs, (attn_ref, *delta_refs) = refs[:GROUP], refs[GROUP:]
-    for mask, (state_ref, delta_ref) in enumerate(zip(state_refs, delta_refs)):
+    for mask, state_ref, delta_ref in zip(ORDER, state_refs, delta_refs):
         at = own_columns(place_ref, mask, chain)
         query = query_ref[:, at]
         attn = inner_ref[:, at] + dot(query, state_ref[...].astype(jnp.bfloat16), NN)
@@ -88,7 +89,7 @@
 def partial_body(chain, place_ref, query_ref, key_ref, value_ref, attn_ref, *refs):
     state_refs, (grad_query_ref, key_part_ref, value_part_ref) = refs[:GROUP], refs[-3:]
     keep, kept = causal(), causal(True)
-    for mask, state_ref in enumerate(state_refs):
+    for mask, state_ref in zip(ORDER, state_refs):
         at, here = own_columns(place_ref, mask, chain), own_columns(place_ref, mask)
         query, key, value, grad_attn = query_ref[:, at], key_ref[:, at], value_ref[:, at], attn_ref[:, here]
         turned = jnp.where(kept, dot(key, query, NT), 0.0).astype(jnp.bfloat16)
@@ -104,7 +105,7 @@
     part_refs, state_refs, (grad_key_ref, grad_value_ref) = refs[: 2 * CHAINS], refs[2 * CHAINS : -2], refs[-2:]
     rows = pl.ds(pl.multiple_of(pl.program_id(0) * PART_ROWS, PART_ROWS), PART_ROWS)
     for at_head, state_ref in enumerate(state_refs):
-        chain, mask = at_head // GROUP, at_head % GROUP
+        chain, mask = at_head // GROUP, ORDER[at_head % GROUP]
         at, here = own_columns(place_ref, mask, chain), own_columns(place_ref, mask)
         state = state_ref[:DH].astype(jnp.bfloat16)
         key_part, value_part = part_refs[2 * chain][rows, here], part_refs[2 * chain + 1][rows, here]
@@ -114,14 +115,14 @@
 
 def gain_body(place_ref, *refs):
     for at_head, state_ref in enumerate(refs[:-1]):
-        row = (at_head // GROUP) * GROUP + (place_ref[0] & (GROUP - 1) ^ (at_head % GROUP))
+        row = (at_head // GROUP) * GROUP + (place_ref[0] & (GROUP - 1) ^ ORDER[at_head % GROUP])
         refs[-1][pl.ds(row, 1), :] = state_ref[DH : DH + 1]
 
 
 def prefix_body(reverse, masks, place_ref, *refs):
     (total_ref, *arrived_refs), (*back_refs, ahead) = refs[: -2 * GROUP - 1], refs[-GROUP - 1 :]
     held_refs = refs[-2 * GROUP - 1 : -GROUP - 1]
-    for mask, held_ref in enumerate(held_refs):
+    for mask, held_ref in zip(ORDER, held_refs):
         ahead[pl.ds(place_ref[0] & (GROUP - 1) ^ mask, 1)] = held_ref[:DH][None]
     running = jnp.zeros((DH, DH), jnp.float32)
     for mask, arrived_ref in zip(masks, arrived_refs):
@@ -131,7 +132,7 @@
         own = ahead[member]
         ahead[member] = running
         running = running + own
-    for mask, back_ref in enumerate(back_refs):
+    for mask, back_ref in zip(ORDER, back_refs):
         back_ref[:DH] = ahead[pl.ds(place_ref[0] & (GROUP - 1) ^ mask, 1)][0]
         if back_ref.shape[0] > DH:
             back_ref[DH:] = total_ref[DH:]
@@ -173,7 +174,7 @@
 
 
 def plane_swap(pieces):
-    return [swap(piece, mask) for mask, piece in enumerate(pieces)]
+    return [swap(piece, mask) for mask, piece in zip(ORDER, pieces)]
 
 
 def beside(function, operands, first, second):
@@ -199,7 +200,7 @@
         "prefix",
         scratch=[pltpu.VMEM((GROUP, DH, DH), jnp.float32)],
     )(place, total, *arrived, *held)
-    return [swap(piece, mask) for mask, piece in enumerate(back)]
+    return plane_swap(back)
 
 
 def local(queries, keys, values, out_gain, grad_out):

time: 64.4 us -> 62.7 us (0.974)
  waiting for transfers between devices: 8.49 us -> 5.74 us
  starting transfers between devices: 44.4 us -> 45.4 us
    ppermute x32, waiting for transfers between devices: 8.49 us -> 5.74 us  [swap(): lax.ppermute(array, 'seq', [(s, s ^ mask) for s in range(lax.axis_size('s...]
    ppermute x32, starting transfers between devices: 44.4 us -> 45.4 us  [swap(): lax.ppermute(array, 'seq', [(s, s ^ mask) for s in range(lax.axis_size('s...]
  transfers between devices with their start and end apart: 33 -> 33, of which waited for: 8 -> 11; matrix products, arithmetic and copies ran while one was open for 0% -> 0% of each run, Pallas kernels for 13% -> 13%
where the time goes in v14:
time: 62.7 us; the launch traced here: 62.6 us
  starting transfers between devices  45.4 us (72%)
  Pallas kernels  9.81 us (16%)
  waiting for transfers between devices  5.74 us (9%)
  between operations  0.82 us (1%)
  other arithmetic  0.75 us (1%)
    ppermute x32, starting transfers between devices, swap(): lax.ppermute(array, 'seq', [(s, s ^ mask) for s in range(lax.axis_size('s...  45.4 us
    ppermute x32, waiting for transfers between devices, swap(): lax.ppermute(array, 'seq', [(s, s ^ mask) for s in range(lax.axis_size('s...  5.74 us
    pallas_call x2, Pallas kernels, partial_call(): call(functools.partial(partial_body, chain), [wide] * 3 + [half] + [short...  3.82 us
    pallas_call x1, Pallas kernels, local(): call(delta_body, [pl.BlockSpec(memory_space=pltpu.HBM)] * 2, [short] * HE...  1.64 us
    pallas_call x1, Pallas kernels, local(): call(final_body, [wide] * 2 + [half] * (2 * CHAINS) + [tall] * HEADS, [ch...  1.62 us
    pallas_call x2, Pallas kernels, local(): call(functools.partial(norm_body, chain), [wide, wide, wide, whole(1, HEA...  1.48 us
  transfers between devices with their start and end apart: 33, of which 11 were waited for; matrix products, arithmetic and copies ran while one was open for 0% of the time, Pallas kernels for 13%

profile of v14, /device:TPU:0, one launch (start us, length us, event | category | flops | bytes accessed | tf_op | source)
XLA Modules:
  0.0 62.6 jit_solution(13466035352908431986)
XLA Ops:
  0.7 1.6 %delta.1 = (f32[128,128]{1,0:T(8,128)S(1)}, f32[128,128]{1,0:T(8,128)S(1)}, f32[128,128]{1,0:T(8,128)S(1)}, f32[128,128]{1,0:T(8,128)S(1)}, f32[128,128]{1,0:T(8...) custom-call(s32[1]{0:T(128)} %bitcast.place_ref, bf16[256,1024]{1,0:T(8,128)(2,1)} %bitcast.20, ...), custom_call_target="tpu_custom_call" | custom-call | flops 402653184 | bytes 2097152 | tf_op jit(solution)/shard_map/delta/pallas_call | solution.py:222
  2.3 4.0 %collective-permute-start.3 = (f32[128,128]{1,0:T(8,128)S(1)}, f32[128,128]{1,0:T(8,128)S(1)}, u32[]{:S(2)}, u32[]{:S(2)}) collective-permute-start(f32[128,128]{1,0:T(8,128)S(1)} %get-tuple-element.78), channel_id=1, source_target_pairs={{0,6},{2,4},{4,2},{6,0},{8,14},{10,12},{12,10},{14,8},{16,22},{18,... | collective-permute-start | bytes 196616 | tf_op jit(solution)/shard_map/ppermute | solution.py:173
  6.9 2.8 %collective-permute-start = (f32[128,128]{1,0:T(8,128)S(1)}, f32[128,128]{1,0:T(8,128)S(1)}, u32[]{:S(2)}, u32[]{:S(2)}) collective-permute-start(f32[128,128]{1,0:T(8,128)S(1)} %get-tuple-element.74), channel_id=1, source_target_pairs={{0,6},{2,4},{4,2},{6,0},{8,14},{10,12},{12,10},{14,8},{16,22},{18,... | collective-permute-start | bytes 196616 | tf_op jit(solution)/shard_map/ppermute | solution.py:173
  11.4 1.6 %collective-permute-start.14 = (f32[128,128]{1,0:T(8,128)S(1)}, f32[128,128]{1,0:T(8,128)S(1)}, u32[]{:S(2)}, u32[]{:S(2)}) collective-permute-start(f32[128,128]{1,0:T(8,128)S(1)} %add_add_fusion.3), channel_id=1, source_target_pairs={{0,8},{2,10},{4,12},{6,14},{8,0},{10,2},{12,4},{14,6},{16,24},{18,... | collective-permute-start | bytes 196616 | tf_op jit(solution)/shard_map/ppermute | solution.py:173
  13.0 0.9 %inner.1.inner_ref = f32[256,1024]{1,0:T(8,128)S(1)} custom-call(s32[1]{0:T(128)} %bitcast.place_ref, bf16[256,1024]{1,0:T(8,128)(2,1)S(1)} %bitcast.13, bf16[256,1024]{1,0:T(8,128)(2,1)S(1)} %bitcast.21, bf16[256,1024]{1,0:T(8,128)(2,1)S(1)} %bitcast.26), custom_call_target="tpu_custom_call" | custom-call | flops 1073741824 | bytes 2097152 | tf_op jit(solution)/shard_map/inner/pallas_call | solution.py:183
  14.6 1.6 %collective-permute-start.6 = (f32[128,128]{1,0:T(8,128)S(1)}, f32[128,128]{1,0:T(8,128)S(1)}, u32[]{:S(2)}, u32[]{:S(2)}) collective-permute-start(f32[128,128]{1,0:T(8,128)S(1)} %add_add_fusion.2), channel_id=1, source_target_pairs={{0,8},{2,10},{4,12},{6,14},{8,0},{10,2},{12,4},{14,6},{16,24},{18,... | collective-permute-start | bytes 196616 | tf_op jit(solution)/shard_map/ppermute | solution.py:173
  16.4 2.7 %collective-permute-start.15 = (f32[128,128]{1,0:T(8,128)S(1)}, f32[128,128]{1,0:T(8,128)S(1)}, u32[]{:S(2)}, u32[]{:S(2)}) collective-permute-start(f32[128,128]{1,0:T(8,128)S(1)} %add.71), channel_id=1, source_target_pairs={{0,16},{2,18},{4,20},{6,22},{8,24},{10,26},{12,28},{14,30},{16,0},... | collective-permute-start | bytes 196616 | tf_op jit(solution)/shard_map/ppermute | solution.py:173
  19.0 2.5 %collective-permute-start.7 = (f32[128,128]{1,0:T(8,128)S(1)}, f32[128,128]{1,0:T(8,128)S(1)}, u32[]{:S(2)}, u32[]{:S(2)}) collective-permute-start(f32[128,128]{1,0:T(8,128)S(1)} %add.69), channel_id=1, source_target_pairs={{0,16},{2,18},{4,20},{6,22},{8,24},{10,26},{12,28},{14,30},{16,0},... | collective-permute-start | bytes 196616 | tf_op jit(solution)/shard_map/ppermute | solution.py:173
  21.6 1.4 %collective-permute-done.15.refs_2_ = f32[128,128]{1,0:T(8,128)S(1)} collective-permute-done((f32[128,128]{1,0:T(8,128)S(1)}, f32[128,128]{1,0:T(8,128)S(1)}, u32[]{:S(2)}, u32[]{:S(2)}) %collective-permute-start.15) | collective-permute-done | bytes 65568 | tf_op jit(solution)/shard_map/ppermute | solution.py:173
  23.1 1.4 %collective-permute-start.16 = (f32[128,128]{1,0:T(8,128)S(1)}, f32[128,128]{1,0:T(8,128)S(1)}, u32[]{:S(2)}, u32[]{:S(2)}) collective-permute-start(f32[128,128]{1,0:T(8,128)S(1)} %get-tuple-element.101), channel_id=1, source_target_pairs={{0,6},{2,4},{4,2},{6,0},{8,14},{10,12},{12,10},{14,8},{16,22},{18,... | collective-permute-start | bytes 196616 | tf_op jit(solution)/shard_map/ppermute | solution.py:173
  24.5 0.8 %collective-permute-start.17 = (f32[128,128]{1,0:T(8,128)S(1)}, f32[128,128]{1,0:T(8,128)S(1)}, u32[]{:S(2)}, u32[]{:S(2)}) collective-permute-start(f32[128,128]{1,0:T(8,128)S(1)} %get-tuple-element.102), channel_id=1, source_target_pairs={{0,4},{2,6},{4,0},{6,2},{8,12},{10,14},{12,8},{14,10},{16,20},{18,... | collective-permute-start | bytes 196616 | tf_op jit(solution)/shard_map/ppermute | solution.py:173
  25.3 1.4 %collective-permute-start.18 = (f32[128,128]{1,0:T(8,128)S(1)}, f32[128,128]{1,0:T(8,128)S(1)}, u32[]{:S(2)}, u32[]{:S(2)}) collective-permute-start(f32[128,128]{1,0:T(8,128)S(1)} %get-tuple-element.103), channel_id=1, source_target_pairs={{0,2},{2,0},{4,6},{6,4},{8,10},{10,8},{12,14},{14,12},{16,18},{18,... | collective-permute-start | bytes 196616 | tf_op jit(solution)/shard_map/ppermute | solution.py:173
  26.8 1.4 %collective-permute-start.8 = (f32[128,128]{1,0:T(8,128)S(1)}, f32[128,128]{1,0:T(8,128)S(1)}, u32[]{:S(2)}, u32[]{:S(2)}) collective-permute-start(f32[128,128]{1,0:T(8,128)S(1)} %get-tuple-element.91), channel_id=1, source_target_pairs={{0,6},{2,4},{4,2},{6,0},{8,14},{10,12},{12,10},{14,8},{16,22},{18,... | collective-permute-start | bytes 196616 | tf_op jit(solution)/shard_map/ppermute | solution.py:173
  28.1 0.8 %collective-permute-start.9 = (f32[128,128]{1,0:T(8,128)S(1)}, f32[128,128]{1,0:T(8,128)S(1)}, u32[]{:S(2)}, u32[]{:S(2)}) collective-permute-start(f32[128,128]{1,0:T(8,128)S(1)} %get-tuple-element.92), channel_id=1, source_target_pairs={{0,4},{2,6},{4,0},{6,2},{8,12},{10,14},{12,8},{14,10},{16,20},{18,... | collective-permute-start | bytes 196616 | tf_op jit(solution)/shard_map/ppermute | solution.py:173
  28.9 1.4 %collective-permute-start.10 = (f32[128,128]{1,0:T(8,128)S(1)}, f32[128,128]{1,0:T(8,128)S(1)}, u32[]{:S(2)}, u32[]{:S(2)}) collective-permute-start(f32[128,128]{1,0:T(8,128)S(1)} %get-tuple-element.93), channel_id=1, source_target_pairs={{0,2},{2,0},{4,6},{6,4},{8,10},{10,8},{12,14},{14,12},{16,18},{18,... | collective-permute-start | bytes 196616 | tf_op jit(solution)/shard_map/ppermute | solution.py:173
  31.1 1.8 %collective-permute-start.19 = (f32[136,128]{1,0:T(8,128)S(1)}, f32[136,128]{1,0:T(8,128)S(1)}, u32[]{:S(2)}, u32[]{:S(2)}) collective-permute-start(f32[136,128]{1,0:T(8,128)S(1)} %get-tuple-element.105), channel_id=1, source_target_pairs={{0,6},{2,4},{4,2},{6,0},{8,14},{10,12},{12,10},{14,8},{16,22},{18,... | collective-permute-start | bytes 208904 | tf_op jit(solution)/shard_map/ppermute | solution.py:173
  33.6 1.1 %collective-permute-start.21 = (f32[136,128]{1,0:T(8,128)S(1)}, f32[136,128]{1,0:T(8,128)S(1)}, u32[]{:S(2)}, u32[]{:S(2)}) collective-permute-start(f32[136,128]{1,0:T(8,128)S(1)} %get-tuple-element.107), channel_id=1, source_target_pairs={{0,2},{2,0},{4,6},{6,4},{8,10},{10,8},{12,14},{14,12},{16,18},{18,... | collective-permute-start | bytes 208904 | tf_op jit(solution)/shard_map/ppermute | solution.py:173
  35.4 1.8 %collective-permute-start.11 = (f32[136,128]{1,0:T(8,128)S(1)}, f32[136,128]{1,0:T(8,128)S(1)}, u32[]{:S(2)}, u32[]{:S(2)}) collective-permute-start(f32[136,128]{1,0:T(8,128)S(1)} %get-tuple-element.96), channel_id=1, source_target_pairs={{0,6},{2,4},{4,2},{6,0},{8,14},{10,12},{12,10},{14,8},{16,22},{18,... | collective-permute-start | bytes 208904 | tf_op jit(solution)/shard_map/ppermute | solution.py:173
  37.9 1.1 %collective-permute-start.13 = (f32[136,128]{1,0:T(8,128)S(1)}, f32[136,128]{1,0:T(8,128)S(1)}, u32[]{:S(2)}, u32[]{:S(2)}) collective-permute-start(f32[136,128]{1,0:T(8,128)S(1)} %get-tuple-element.98), channel_id=1, source_target_pairs={{0,2},{2,0},{4,6},{6,4},{8,10},{10,8},{12,14},{14,12},{16,18},{18,... | collective-permute-start | bytes 208904 | tf_op jit(solution)/shard_map/ppermute | solution.py:173
  39.6 1.9 %partial.2 = (bf16[256,1024]{1,0:T(8,128)(2,1)}, f32[256,512]{1,0:T(8,128)S(1)}, f32[256,512]{1,0:T(8,128)S(1)}) custom-call(s32[1]{0:T(128)} %bitcast.place_ref, bf16[256,1024]{1,0:T(8,128)(2,1)S(1)} %bitcast.16, bf16[256,1024]{1,0:T(8,128)(2,1)S(1)} %bitcast.22, bf16[256,1024]{1,0:T(8,128)(2,1)S(1)} %bitcast.27, ...), custom_call_target="tpu_custom_call" | custom-call | flops 1610612736 | bytes 2097152 | tf_op jit(solution)/shard_map/partial/pallas_call | solution.py:251
  42.2 0.9 %collective-permute-start.27 = (f32[136,128]{1,0:T(8,128)S(1)}, f32[136,128]{1,0:T(8,128)S(1)}, u32[]{:S(2)}, u32[]{:S(2)}) collective-permute-start(f32[136,128]{1,0:T(8,128)S(1)} %add_add_fusion), channel_id=1, source_target_pairs={{0,8},{2,10},{4,12},{6,14},{8,0},{10,2},{12,4},{14,6},{16,24},{18,... | collective-permute-start | bytes 208904 | tf_op jit(solution)/shard_map/ppermute | solution.py:173
  43.7 2.7 %collective-permute-start.23 = (f32[136,128]{1,0:T(8,128)S(1)}, f32[136,128]{1,0:T(8,128)S(1)}, u32[]{:S(2)}, u32[]{:S(2)}) collective-permute-start(f32[136,128]{1,0:T(8,128)S(1)} %add.76), channel_id=1, source_target_pairs={{0,16},{2,18},{4,20},{6,22},{8,24},{10,26},{12,28},{14,30},{16,0},... | collective-permute-start | bytes 208904 | tf_op jit(solution)/shard_map/ppermute | solution.py:173
  46.6 2.8 %collective-permute-start.28 = (f32[136,128]{1,0:T(8,128)S(1)}, f32[136,128]{1,0:T(8,128)S(1)}, u32[]{:S(2)}, u32[]{:S(2)}) collective-permute-start(f32[136,128]{1,0:T(8,128)S(1)} %add.81), channel_id=1, source_target_pairs={{0,16},{2,18},{4,20},{6,22},{8,24},{10,26},{12,28},{14,30},{16,0},... | collective-permute-start | bytes 208904 | tf_op jit(solution)/shard_map/ppermute | solution.py:173
  49.8 1.6 %collective-permute-start.24 = (f32[136,128]{1,0:T(8,128)S(1)}, f32[136,128]{1,0:T(8,128)S(1)}, u32[]{:S(2)}, u32[]{:S(2)}) collective-permute-start(f32[136,128]{1,0:T(8,128)S(1)} %get-tuple-element.129), channel_id=1, source_target_pairs={{0,6},{2,4},{4,2},{6,0},{8,14},{10,12},{12,10},{14,8},{16,22},{18,... | collective-permute-start | bytes 208904 | tf_op jit(solution)/shard_map/ppermute | solution.py:173
  51.4 1.0 %collective-permute-start.25 = (f32[136,128]{1,0:T(8,128)S(1)}, f32[136,128]{1,0:T(8,128)S(1)}, u32[]{:S(2)}, u32[]{:S(2)}) collective-permute-start(f32[136,128]{1,0:T(8,128)S(1)} %get-tuple-element.130), channel_id=1, source_target_pairs={{0,4},{2,6},{4,0},{6,2},{8,12},{10,14},{12,8},{14,10},{16,20},{18,... | collective-permute-start | bytes 208904 | tf_op jit(solution)/shard_map/ppermute | solution.py:173
  52.4 1.0 %collective-permute-start.26 = (f32[136,128]{1,0:T(8,128)S(1)}, f32[136,128]{1,0:T(8,128)S(1)}, u32[]{:S(2)}, u32[]{:S(2)}) collective-permute-start(f32[136,128]{1,0:T(8,128)S(1)} %get-tuple-element.131), channel_id=1, source_target_pairs={{0,2},{2,0},{4,6},{6,4},{8,10},{10,8},{12,14},{14,12},{16,18},{18,... | collective-permute-start | bytes 208904 | tf_op jit(solution)/shard_map/ppermute | solution.py:173
  53.4 1.6 %collective-permute-start.29 = (f32[136,128]{1,0:T(8,128)S(1)}, f32[136,128]{1,0:T(8,128)S(1)}, u32[]{:S(2)}, u32[]{:S(2)}) collective-permute-start(f32[136,128]{1,0:T(8,128)S(1)} %get-tuple-element.137), channel_id=1, source_target_pairs={{0,6},{2,4},{4,2},{6,0},{8,14},{10,12},{12,10},{14,8},{16,22},{18,... | collective-permute-start | bytes 208904 | tf_op jit(solution)/shard_map/ppermute | solution.py:173
  55.0 1.0 %collective-permute-start.30 = (f32[136,128]{1,0:T(8,128)S(1)}, f32[136,128]{1,0:T(8,128)S(1)}, u32[]{:S(2)}, u32[]{:S(2)}) collective-permute-start(f32[136,128]{1,0:T(8,128)S(1)} %get-tuple-element.138), channel_id=1, source_target_pairs={{0,4},{2,6},{4,0},{6,2},{8,12},{10,14},{12,8},{14,10},{16,20},{18,... | collective-permute-start | bytes 208904 | tf_op jit(solution)/shard_map/ppermute | solution.py:173
  56.0 1.0 %collective-permute-start.31 = (f32[136,128]{1,0:T(8,128)S(1)}, f32[136,128]{1,0:T(8,128)S(1)}, u32[]{:S(2)}, u32[]{:S(2)}) collective-permute-start(f32[136,128]{1,0:T(8,128)S(1)} %get-tuple-element.139), channel_id=1, source_target_pairs={{0,2},{2,0},{4,6},{6,4},{8,10},{10,8},{12,14},{14,12},{16,18},{18,... | collective-permute-start | bytes 208904 | tf_op jit(solution)/shard_map/ppermute | solution.py:173
  57.0 1.9 %partial.3 = (bf16[256,1024]{1,0:T(8,128)(2,1)}, f32[256,512]{1,0:T(8,128)S(1)}, f32[256,512]{1,0:T(8,128)S(1)}) custom-call(s32[1]{0:T(128)} %bitcast.place_ref, bf16[256,1024]{1,0:T(8,128)(2,1)S(1)} %bitcast.17, bf16[256,1024]{1,0:T(8,128)(2,1)S(1)} %bitcast.23, bf16[256,1024]{1,0:T(8,128)(2,1)S(1)} %bitcast.28, ...), custom_call_target="tpu_custom_call", output_to_operand_aliasing={{0}: (9, {})} | custom-call | flops 1610612736 | bytes 2097152 | tf_op jit(solution)/shard_map/partial/pallas_call | solution.py:251
  59.5 0.9 %collective-permute-done.31.refs_11_.refs_7_ = f32[136,128]{1,0:T(8,128)S(1)} collective-permute-done((f32[136,128]{1,0:T(8,128)S(1)}, f32[136,128]{1,0:T(8,128)S(1)}, u32[]{:S(2)}, u32[]{:S(2)}) %collective-permute-start.31) | collective-permute-done | bytes 69664 | tf_op jit(solution)/shard_map/ppermute | solution.py:173
  60.4 1.6 %final.1 = (bf16[256,1024]{1,0:T(8,128)(2,1)}, bf16[256,1024]{1,0:T(8,128)(2,1)}) custom-call(s32[1]{0:T(128)} %bitcast.place_ref, bf16[256,1024]{1,0:T(8,128)(2,1)S(1)} %bitcast.24, bf16[256,1024]{1,0:T(8,128)(2,1)S(1)} %bitcast.29, f32[256,512]{1,0:T(8,128)S(1)} %get-tuple-element.123.refs_0_, f32[256,512]{1,0:T(8,128)S(1)} %get-tuple-element.124.refs_1_, ...), custom_call_target="tpu_custom_call" | custom-call | flops 1073741824 | bytes 2097152 | tf_op jit(solution)/shard_map/final/pallas_call | solution.py:274
  (69 shorter events, 9.7 us)
Async XLA Ops:
  2.3 8.0 %collective-permute-start.3 = (f32[128,128]{1,0:T(8,128)S(1)}, f32[128,128]{1,0:T(8,128)S(1)}, u32[]{:S(2)}, u32[]{:S(2)}) collective-permute-start(f32[128,128]{1,0:T(8,128)S(1)} %get-tuple-element.78), channel_id=1, source_target_pairs={{0,6},{2,4},{4,2},{6,0},{8,14},{10,12},{12,10},{14,8},{16,22},{18,... | collective-permute-start | bytes 196616 | tf_op jit(solution)/shard_map/ppermute | solution.py:173
  6.3 5.1 %collective-permute-start.4 = (f32[128,128]{1,0:T(8,128)S(1)}, f32[128,128]{1,0:T(8,128)S(1)}, u32[]{:S(2)}, u32[]{:S(2)}) collective-permute-start(f32[128,128]{1,0:T(8,128)S(1)} %get-tuple-element.79), channel_id=1, source_target_pairs={{0,4},{2,6},{4,0},{6,2},{8,12},{10,14},{12,8},{14,10},{16,20},{18,... | collective-permute-start | bytes 196616 | tf_op jit(solution)/shard_map/ppermute | solution.py:173
  6.8 4.6 %collective-permute-start.5 = (f32[128,128]{1,0:T(8,128)S(1)}, f32[128,128]{1,0:T(8,128)S(1)}, u32[]{:S(2)}, u32[]{:S(2)}) collective-permute-start(f32[128,128]{1,0:T(8,128)S(1)} %get-tuple-element.80), channel_id=1, source_target_pairs={{0,2},{2,0},{4,6},{6,4},{8,10},{10,8},{12,14},{14,12},{16,18},{18,... | collective-permute-start | bytes 196616 | tf_op jit(solution)/shard_map/ppermute | solution.py:173
  6.9 7.0 %collective-permute-start = (f32[128,128]{1,0:T(8,128)S(1)}, f32[128,128]{1,0:T(8,128)S(1)}, u32[]{:S(2)}, u32[]{:S(2)}) collective-permute-start(f32[128,128]{1,0:T(8,128)S(1)} %get-tuple-element.74), channel_id=1, source_target_pairs={{0,6},{2,4},{4,2},{6,0},{8,14},{10,12},{12,10},{14,8},{16,22},{18,... | collective-permute-start | bytes 196616 | tf_op jit(solution)/shard_map/ppermute | solution.py:173
  9.8 4.3 %collective-permute-start.1 = (f32[128,128]{1,0:T(8,128)S(1)}, f32[128,128]{1,0:T(8,128)S(1)}, u32[]{:S(2)}, u32[]{:S(2)}) collective-permute-start(f32[128,128]{1,0:T(8,128)S(1)} %get-tuple-element.75), channel_id=1, source_target_pairs={{0,4},{2,6},{4,0},{6,2},{8,12},{10,14},{12,8},{14,10},{16,20},{18,... | collective-permute-start | bytes 196616 | tf_op jit(solution)/shard_map/ppermute | solution.py:173
  10.3 4.3 %collective-permute-start.2 = (f32[128,128]{1,0:T(8,128)S(1)}, f32[128,128]{1,0:T(8,128)S(1)}, u32[]{:S(2)}, u32[]{:S(2)}) collective-permute-start(f32[128,128]{1,0:T(8,128)S(1)} %get-tuple-element.76), channel_id=1, source_target_pairs={{0,2},{2,0},{4,6},{6,4},{8,10},{10,8},{12,14},{14,12},{16,18},{18,... | collective-permute-start | bytes 196616 | tf_op jit(solution)/shard_map/ppermute | solution.py:173
  11.4 5.0 %collective-permute-start.14 = (f32[128,128]{1,0:T(8,128)S(1)}, f32[128,128]{1,0:T(8,128)S(1)}, u32[]{:S(2)}, u32[]{:S(2)}) collective-permute-start(f32[128,128]{1,0:T(8,128)S(1)} %add_add_fusion.3), channel_id=1, source_target_pairs={{0,8},{2,10},{4,12},{6,14},{8,0},{10,2},{12,4},{14,6},{16,24},{18,... | collective-permute-start | bytes 196616 | tf_op jit(solution)/shard_map/ppermute | solution.py:173
  14.6 4.5 %collective-permute-start.6 = (f32[128,128]{1,0:T(8,128)S(1)}, f32[128,128]{1,0:T(8,128)S(1)}, u32[]{:S(2)}, u32[]{:S(2)}) collective-permute-start(f32[128,128]{1,0:T(8,128)S(1)} %add_add_fusion.2), channel_id=1, source_target_pairs={{0,8},{2,10},{4,12},{6,14},{8,0},{10,2},{12,4},{14,6},{16,24},{18,... | collective-permute-start | bytes 196616 | tf_op jit(solution)/shard_map/ppermute | solution.py:173
  16.4 6.6 %collective-permute-start.15 = (f32[128,128]{1,0:T(8,128)S(1)}, f32[128,128]{1,0:T(8,128)S(1)}, u32[]{:S(2)}, u32[]{:S(2)}) collective-permute-start(f32[128,128]{1,0:T(8,128)S(1)} %add.71), channel_id=1, source_target_pairs={{0,16},{2,18},{4,20},{6,22},{8,24},{10,26},{12,28},{14,30},{16,0},... | collective-permute-start | bytes 196616 | tf_op jit(solution)/shard_map/ppermute | solution.py:173
  19.0 7.6 %collective-permute-start.7 = (f32[128,128]{1,0:T(8,128)S(1)}, f32[128,128]{1,0:T(8,128)S(1)}, u32[]{:S(2)}, u32[]{:S(2)}) collective-permute-start(f32[128,128]{1,0:T(8,128)S(1)} %add.69), channel_id=1, source_target_pairs={{0,16},{2,18},{4,20},{6,22},{8,24},{10,26},{12,28},{14,30},{16,0},... | collective-permute-start | bytes 196616 | tf_op jit(solution)/shard_map/ppermute | solution.py:173
  23.1 5.8 %collective-permute-start.16 = (f32[128,128]{1,0:T(8,128)S(1)}, f32[128,128]{1,0:T(8,128)S(1)}, u32[]{:S(2)}, u32[]{:S(2)}) collective-permute-start(f32[128,128]{1,0:T(8,128)S(1)} %get-tuple-element.101), channel_id=1, source_target_pairs={{0,6},{2,4},{4,2},{6,0},{8,14},{10,12},{12,10},{14,8},{16,22},{18,... | collective-permute-start | bytes 196616 | tf_op jit(solution)/shard_map/ppermute | solution.py:173
  24.5 5.8 %collective-permute-start.17 = (f32[128,128]{1,0:T(8,128)S(1)}, f32[128,128]{1,0:T(8,128)S(1)}, u32[]{:S(2)}, u32[]{:S(2)}) collective-permute-start(f32[128,128]{1,0:T(8,128)S(1)} %get-tuple-element.102), channel_id=1, source_target_pairs={{0,4},{2,6},{4,0},{6,2},{8,12},{10,14},{12,8},{14,10},{16,20},{18,... | collective-permute-start | bytes 196616 | tf_op jit(solution)/shard_map/ppermute | solution.py:173
  25.3 5.1 %collective-permute-start.18 = (f32[128,128]{1,0:T(8,128)S(1)}, f32[128,128]{1,0:T(8,128)S(1)}, u32[]{:S(2)}, u32[]{:S(2)}) collective-permute-start(f32[128,128]{1,0:T(8,128)S(1)} %get-tuple-element.103), channel_id=1, source_target_pairs={{0,2},{2,0},{4,6},{6,4},{8,10},{10,8},{12,14},{14,12},{16,18},{18,... | collective-permute-start | bytes 196616 | tf_op jit(solution)/shard_map/ppermute | solution.py:173
  26.8 6.8 %collective-permute-start.8 = (f32[128,128]{1,0:T(8,128)S(1)}, f32[128,128]{1,0:T(8,128)S(1)}, u32[]{:S(2)}, u32[]{:S(2)}) collective-permute-start(f32[128,128]{1,0:T(8,128)S(1)} %get-tuple-element.91), channel_id=1, source_target_pairs={{0,6},{2,4},{4,2},{6,0},{8,14},{10,12},{12,10},{14,8},{16,22},{18,... | collective-permute-start | bytes 196616 | tf_op jit(solution)/shard_map/ppermute | solution.py:173
  28.1 6.5 %collective-permute-start.9 = (f32[128,128]{1,0:T(8,128)S(1)}, f32[128,128]{1,0:T(8,128)S(1)}, u32[]{:S(2)}, u32[]{:S(2)}) collective-permute-start(f32[128,128]{1,0:T(8,128)S(1)} %get-tuple-element.92), channel_id=1, source_target_pairs={{0,4},{2,6},{4,0},{6,2},{8,12},{10,14},{12,8},{14,10},{16,20},{18,... | collective-permute-start | bytes 196616 | tf_op jit(solution)/shard_map/ppermute | solution.py:173
  28.9 5.8 %collective-permute-start.10 = (f32[128,128]{1,0:T(8,128)S(1)}, f32[128,128]{1,0:T(8,128)S(1)}, u32[]{:S(2)}, u32[]{:S(2)}) collective-permute-start(f32[128,128]{1,0:T(8,128)S(1)} %get-tuple-element.93), channel_id=1, source_target_pairs={{0,2},{2,0},{4,6},{6,4},{8,10},{10,8},{12,14},{14,12},{16,18},{18,... | collective-permute-start | bytes 196616 | tf_op jit(solution)/shard_map/ppermute | solution.py:173
  31.1 6.8 %collective-permute-start.19 = (f32[136,128]{1,0:T(8,128)S(1)}, f32[136,128]{1,0:T(8,128)S(1)}, u32[]{:S(2)}, u32[]{:S(2)}) collective-permute-start(f32[136,128]{1,0:T(8,128)S(1)} %get-tuple-element.105), channel_id=1, source_target_pairs={{0,6},{2,4},{4,2},{6,0},{8,14},{10,12},{12,10},{14,8},{16,22},{18,... | collective-permute-start | bytes 208904 | tf_op jit(solution)/shard_map/ppermute | solution.py:173
  32.9 6.1 %collective-permute-start.20 = (f32[136,128]{1,0:T(8,128)S(1)}, f32[136,128]{1,0:T(8,128)S(1)}, u32[]{:S(2)}, u32[]{:S(2)}) collective-permute-start(f32[136,128]{1,0:T(8,128)S(1)} %get-tuple-element.106), channel_id=1, source_target_pairs={{0,4},{2,6},{4,0},{6,2},{8,12},{10,14},{12,8},{14,10},{16,20},{18,... | collective-permute-start | bytes 208904 | tf_op jit(solution)/shard_map/ppermute | solution.py:173
  33.6 5.4 %collective-permute-start.21 = (f32[136,128]{1,0:T(8,128)S(1)}, f32[136,128]{1,0:T(8,128)S(1)}, u32[]{:S(2)}, u32[]{:S(2)}) collective-permute-start(f32[136,128]{1,0:T(8,128)S(1)} %get-tuple-element.107), channel_id=1, source_target_pairs={{0,2},{2,0},{4,6},{6,4},{8,10},{10,8},{12,14},{14,12},{16,18},{18,... | collective-permute-start | bytes 208904 | tf_op jit(solution)/shard_map/ppermute | solution.py:173
  35.4 6.1 %collective-permute-start.11 = (f32[136,128]{1,0:T(8,128)S(1)}, f32[136,128]{1,0:T(8,128)S(1)}, u32[]{:S(2)}, u32[]{:S(2)}) collective-permute-start(f32[136,128]{1,0:T(8,128)S(1)} %get-tuple-element.96), channel_id=1, source_target_pairs={{0,6},{2,4},{4,2},{6,0},{8,14},{10,12},{12,10},{14,8},{16,22},{18,... | collective-permute-start | bytes 208904 | tf_op jit(solution)/shard_map/ppermute | solution.py:173
  37.2 4.3 %collective-permute-start.12 = (f32[136,128]{1,0:T(8,128)S(1)}, f32[136,128]{1,0:T(8,128)S(1)}, u32[]{:S(2)}, u32[]{:S(2)}) collective-permute-start(f32[136,128]{1,0:T(8,128)S(1)} %get-tuple-element.97), channel_id=1, source_target_pairs={{0,4},{2,6},{4,0},{6,2},{8,12},{10,14},{12,8},{14,10},{16,20},{18,... | collective-permute-start | bytes 208904 | tf_op jit(solution)/shard_map/ppermute | solution.py:173
  37.9 4.3 %collective-permute-start.13 = (f32[136,128]{1,0:T(8,128)S(1)}, f32[136,128]{1,0:T(8,128)S(1)}, u32[]{:S(2)}, u32[]{:S(2)}) collective-permute-start(f32[136,128]{1,0:T(8,128)S(1)} %get-tuple-element.98), channel_id=1, source_target_pairs={{0,2},{2,0},{4,6},{6,4},{8,10},{10,8},{12,14},{14,12},{16,18},{18,... | collective-permute-start | bytes 208904 | tf_op jit(solution)/shard_map/ppermute | solution.py:173
  39.0 4.6 %collective-permute-start.22 = (f32[136,128]{1,0:T(8,128)S(1)}, f32[136,128]{1,0:T(8,128)S(1)}, u32[]{:S(2)}, u32[]{:S(2)}) collective-permute-start(f32[136,128]{1,0:T(8,128)S(1)} %add_add_fusion.1), channel_id=1, source_target_pairs={{0,8},{2,10},{4,12},{6,14},{8,0},{10,2},{12,4},{14,6},{16,24},{18,... | collective-permute-start | bytes 208904 | tf_op jit(solution)/shard_map/ppermute | solution.py:173
  42.2 4.4 %collective-permute-start.27 = (f32[136,128]{1,0:T(8,128)S(1)}, f32[136,128]{1,0:T(8,128)S(1)}, u32[]{:S(2)}, u32[]{:S(2)}) collective-permute-start(f32[136,128]{1,0:T(8,128)S(1)} %add_add_fusion), channel_id=1, source_target_pairs={{0,8},{2,10},{4,12},{6,14},{8,0},{10,2},{12,4},{14,6},{16,24},{18,... | collective-permute-start | bytes 208904 | tf_op jit(solution)/shard_map/ppermute | solution.py:173
  43.7 6.0 %collective-permute-start.23 = (f32[136,128]{1,0:T(8,128)S(1)}, f32[136,128]{1,0:T(8,128)S(1)}, u32[]{:S(2)}, u32[]{:S(2)}) collective-permute-start(f32[136,128]{1,0:T(8,128)S(1)} %add.76), channel_id=1, source_target_pairs={{0,16},{2,18},{4,20},{6,22},{8,24},{10,26},{12,28},{14,30},{16,0},... | collective-permute-start | bytes 208904 | tf_op jit(solution)/shard_map/ppermute | solution.py:173
  46.6 6.8 %collective-permute-start.28 = (f32[136,128]{1,0:T(8,128)S(1)}, f32[136,128]{1,0:T(8,128)S(1)}, u32[]{:S(2)}, u32[]{:S(2)}) collective-permute-start(f32[136,128]{1,0:T(8,128)S(1)} %add.81), channel_id=1, source_target_pairs={{0,16},{2,18},{4,20},{6,22},{8,24},{10,26},{12,28},{14,30},{16,0},... | collective-permute-start | bytes 208904 | tf_op jit(solution)/shard_map/ppermute | solution.py:173
  49.8 6.2 %collective-permute-start.24 = (f32[136,128]{1,0:T(8,128)S(1)}, f32[136,128]{1,0:T(8,128)S(1)}, u32[]{:S(2)}, u32[]{:S(2)}) collective-permute-start(f32[136,128]{1,0:T(8,128)S(1)} %get-tuple-element.129), channel_id=1, source_target_pairs={{0,6},{2,4},{4,2},{6,0},{8,14},{10,12},{12,10},{14,8},{16,22},{18,... | collective-permute-start | bytes 208904 | tf_op jit(solution)/shard_map/ppermute | solution.py:173
  51.4 7.5 %collective-permute-start.25 = (f32[136,128]{1,0:T(8,128)S(1)}, f32[136,128]{1,0:T(8,128)S(1)}, u32[]{:S(2)}, u32[]{:S(2)}) collective-permute-start(f32[136,128]{1,0:T(8,128)S(1)} %get-tuple-element.130), channel_id=1, source_target_pairs={{0,4},{2,6},{4,0},{6,2},{8,12},{10,14},{12,8},{14,10},{16,20},{18,... | collective-permute-start | bytes 208904 | tf_op jit(solution)/shard_map/ppermute | solution.py:173
  52.4 6.5 %collective-permute-start.26 = (f32[136,128]{1,0:T(8,128)S(1)}, f32[136,128]{1,0:T(8,128)S(1)}, u32[]{:S(2)}, u32[]{:S(2)}) collective-permute-start(f32[136,128]{1,0:T(8,128)S(1)} %get-tuple-element.131), channel_id=1, source_target_pairs={{0,2},{2,0},{4,6},{6,4},{8,10},{10,8},{12,14},{14,12},{16,18},{18,... | collective-permute-start | bytes 208904 | tf_op jit(solution)/shard_map/ppermute | solution.py:173
  53.4 5.5 %collective-permute-start.29 = (f32[136,128]{1,0:T(8,128)S(1)}, f32[136,128]{1,0:T(8,128)S(1)}, u32[]{:S(2)}, u32[]{:S(2)}) collective-permute-start(f32[136,128]{1,0:T(8,128)S(1)} %get-tuple-element.137), channel_id=1, source_target_pairs={{0,6},{2,4},{4,2},{6,0},{8,14},{10,12},{12,10},{14,8},{16,22},{18,... | collective-permute-start | bytes 208904 | tf_op jit(solution)/shard_map/ppermute | solution.py:173
  55.0 4.4 %collective-permute-start.30 = (f32[136,128]{1,0:T(8,128)S(1)}, f32[136,128]{1,0:T(8,128)S(1)}, u32[]{:S(2)}, u32[]{:S(2)}) collective-permute-start(f32[136,128]{1,0:T(8,128)S(1)} %get-tuple-element.138), channel_id=1, source_target_pairs={{0,4},{2,6},{4,0},{6,2},{8,12},{10,14},{12,8},{14,10},{16,20},{18,... | collective-permute-start | bytes 208904 | tf_op jit(solution)/shard_map/ppermute | solution.py:173
  56.0 4.3 %collective-permute-start.31 = (f32[136,128]{1,0:T(8,128)S(1)}, f32[136,128]{1,0:T(8,128)S(1)}, u32[]{:S(2)}, u32[]{:S(2)}) collective-permute-start(f32[136,128]{1,0:T(8,128)S(1)} %get-tuple-element.139), channel_id=1, source_target_pairs={{0,2},{2,0},{4,6},{6,4},{8,10},{10,8},{12,14},{14,12},{16,18},{18,... | collective-permute-start | bytes 208904 | tf_op jit(solution)/shard_map/ppermute | solution.py:173
  (6 other events, 48.3 us)

commit v15 on v14

--- a/solution.py
+++ b/solution.py
@@ -126,7 +126,7 @@
         ahead[pl.ds(place_ref[0] & (GROUP - 1) ^ mask, 1)] = held_ref[:DH][None]
     running = jnp.zeros((DH, DH), jnp.float32)
     for mask, arrived_ref in zip(masks, arrived_refs):
-        later = (place_ref[0] & mask == 0) == reverse
+        later = (place_ref[0] ^ mask < place_ref[0]) != reverse
         running = running + jnp.where(later, arrived_ref[:DH], 0.0)
     for member in reversed(range(GROUP)) if reverse else range(GROUP):
         own = ahead[member]
@@ -160,11 +160,13 @@
     )
 
 
-def exchange_masks():
-    masks = [GROUP]
-    while masks[-1] * 2 < lax.axis_size("seq"):
-        masks.append(masks[-1] * 2)
-    return masks if lax.axis_size("seq") > GROUP else []
+def exchange_steps():
+    count, base, steps = lax.axis_size("seq"), GROUP, []
+    while base < count:
+        masks = [base, 2 * base, 3 * base] if 4 * base <= count else [base]
+        steps.append(masks)
+        base *= len(masks) + 1
+    return steps
 
 
 def swap(array, mask):
@@ -187,12 +189,12 @@
 
 def carried_in(held, total, reverse, place):
     arrived = []
-    for mask in exchange_masks():
-        arrived.append(swap(total, mask))
-        total = total + arrived[-1]
+    for masks in exchange_steps():
+        arrived += [swap(total, mask) for mask in masks]
+        total = sum(arrived[-len(masks) :], total)
     single = whole(*total.shape)
     back = call(
-        functools.partial(prefix_body, reverse, exchange_masks()),
+        functools.partial(prefix_body, reverse, sum(exchange_steps(), [])),
         [single] * (1 + len(arrived) + GROUP),
         [single] * GROUP,
         [jax.ShapeDtypeStruct(total.shape, jnp.float32)] * GROUP,

time: 62.7 us -> 62.5 us (level)
  waiting for transfers between devices: 5.74 us -> 3.15 us
  starting transfers between devices: 45.4 us -> 47.8 us
    ppermute x32 -> x36, waiting for transfers between devices: 5.74 us -> 3.15 us  [swap(): lax.ppermute(array, 'seq', [(s, s ^ mask) for s in range(lax.axis_size('s...]
    ppermute x32 -> x36, starting transfers between devices: 45.4 us -> 47.8 us  [swap(): lax.ppermute(array, 'seq', [(s, s ^ mask) for s in range(lax.axis_size('s...]
  transfers between devices with their start and end apart: 33 -> 37, of which waited for: 11 -> 5; matrix products, arithmetic and copies ran while one was open for 0% -> 0% of each run, Pallas kernels for 13% -> 13%
where the time goes in v15:
time: 62.5 us; the launch traced here: 62.4 us
  starting transfers between devices  47.8 us (76%)
  Pallas kernels  9.84 us (16%)
  waiting for transfers between devices  3.15 us (5%)
  between operations  0.82 us (1%)
  other arithmetic  0.75 us (1%)
    ppermute x36, starting transfers between devices, swap(): lax.ppermute(array, 'seq', [(s, s ^ mask) for s in range(lax.axis_size('s...  47.8 us
    pallas_call x2, Pallas kernels, partial_call(): call(functools.partial(partial_body, chain), [wide] * 3 + [half] + [short...  3.83 us
    ppermute x36, waiting for transfers between devices, swap(): lax.ppermute(array, 'seq', [(s, s ^ mask) for s in range(lax.axis_size('s...  3.15 us
    pallas_call x1, Pallas kernels, local(): call(delta_body, [pl.BlockSpec(memory_space=pltpu.HBM)] * 2, [short] * HE...  1.64 us
    pallas_call x1, Pallas kernels, local(): call(final_body, [wide] * 2 + [half] * (2 * CHAINS) + [tall] * HEADS, [ch...  1.63 us
    pallas_call x2, Pallas kernels, local(): call(functools.partial(norm_body, chain), [wide, wide, wide, whole(1, HEA...  1.48 us
  transfers between devices with their start and end apart: 37, of which 5 were waited for; matrix products, arithmetic and copies ran while one was open for 0% of the time, Pallas kernels for 13%

profile of v15, /device:TPU:0, one launch (start us, length us, event | category | flops | bytes accessed | tf_op | source)
XLA Modules:
  0.0 62.4 jit_solution(2955036372769447573)
XLA Ops:
  0.7 1.6 %delta.1 = (f32[128,128]{1,0:T(8,128)S(1)}, f32[128,128]{1,0:T(8,128)S(1)}, f32[128,128]{1,0:T(8,128)S(1)}, f32[128,128]{1,0:T(8,128)S(1)}, f32[128,128]{1,0:T(8...) custom-call(s32[1]{0:T(128)} %bitcast.place_ref, bf16[256,1024]{1,0:T(8,128)(2,1)} %bitcast.20, ...), custom_call_target="tpu_custom_call" | custom-call | flops 402653184 | bytes 2097152 | tf_op jit(solution)/shard_map/delta/pallas_call | solution.py:224
  2.3 4.0 %collective-permute-start.3 = (f32[128,128]{1,0:T(8,128)S(1)}, f32[128,128]{1,0:T(8,128)S(1)}, u32[]{:S(2)}, u32[]{:S(2)}) collective-permute-start(f32[128,128]{1,0:T(8,128)S(1)} %get-tuple-element.78), channel_id=1, source_target_pairs={{0,6},{2,4},{4,2},{6,0},{8,14},{10,12},{12,10},{14,8},{16,22},{18,... | collective-permute-start | bytes 196616 | tf_op jit(solution)/shard_map/ppermute | solution.py:175
  6.9 2.8 %collective-permute-start = (f32[128,128]{1,0:T(8,128)S(1)}, f32[128,128]{1,0:T(8,128)S(1)}, u32[]{:S(2)}, u32[]{:S(2)}) collective-permute-start(f32[128,128]{1,0:T(8,128)S(1)} %get-tuple-element.74), channel_id=1, source_target_pairs={{0,6},{2,4},{4,2},{6,0},{8,14},{10,12},{12,10},{14,8},{16,22},{18,... | collective-permute-start | bytes 196616 | tf_op jit(solution)/shard_map/ppermute | solution.py:175
  10.3 0.6 %collective-permute-start.2 = (f32[128,128]{1,0:T(8,128)S(1)}, f32[128,128]{1,0:T(8,128)S(1)}, u32[]{:S(2)}, u32[]{:S(2)}) collective-permute-start(f32[128,128]{1,0:T(8,128)S(1)} %get-tuple-element.76), channel_id=1, source_target_pairs={{0,2},{2,0},{4,6},{6,4},{8,10},{10,8},{12,14},{14,12},{16,18},{18,... | collective-permute-start | bytes 196616 | tf_op jit(solution)/shard_map/ppermute | solution.py:175
  11.4 3.7 %collective-permute-start.17 = (f32[128,128]{1,0:T(8,128)S(1)}, f32[128,128]{1,0:T(8,128)S(1)}, u32[]{:S(2)}, u32[]{:S(2)}) collective-permute-start(f32[128,128]{1,0:T(8,128)S(1)} %add_add_fusion.7), channel_id=1, source_target_pairs={{0,24},{2,26},{4,28},{6,30},{8,16},{10,18},{12,20},{14,22},{16,8},... | collective-permute-start | bytes 196616 | tf_op jit(solution)/shard_map/ppermute | solution.py:175
  15.1 0.9 %inner.1.inner_ref = f32[256,1024]{1,0:T(8,128)S(1)} custom-call(s32[1]{0:T(128)} %bitcast.place_ref, bf16[256,1024]{1,0:T(8,128)(2,1)S(1)} %bitcast.13, bf16[256,1024]{1,0:T(8,128)(2,1)S(1)} %bitcast.21, bf16[256,1024]{1,0:T(8,128)(2,1)S(1)} %bitcast.26), custom_call_target="tpu_custom_call" | custom-call | flops 1073741824 | bytes 2097152 | tf_op jit(solution)/shard_map/inner/pallas_call | solution.py:185
  16.0 0.8 %collective-permute-start.15 = (f32[128,128]{1,0:T(8,128)S(1)}, f32[128,128]{1,0:T(8,128)S(1)}, u32[]{:S(2)}, u32[]{:S(2)}) collective-permute-start(f32[128,128]{1,0:T(8,128)S(1)} %add_add_fusion.7), channel_id=1, source_target_pairs={{0,8},{2,10},{4,12},{6,14},{8,0},{10,2},{12,4},{14,6},{16,24},{18,... | collective-permute-start | bytes 196616 | tf_op jit(solution)/shard_map/ppermute | solution.py:175
  16.9 3.7 %collective-permute-start.8 = (f32[128,128]{1,0:T(8,128)S(1)}, f32[128,128]{1,0:T(8,128)S(1)}, u32[]{:S(2)}, u32[]{:S(2)}) collective-permute-start(f32[128,128]{1,0:T(8,128)S(1)} %add_add_fusion.6), channel_id=1, source_target_pairs={{0,24},{2,26},{4,28},{6,30},{8,16},{10,18},{12,20},{14,22},{16,8},... | collective-permute-start | bytes 196616 | tf_op jit(solution)/shard_map/ppermute | solution.py:175
  20.5 0.8 %collective-permute-start.6 = (f32[128,128]{1,0:T(8,128)S(1)}, f32[128,128]{1,0:T(8,128)S(1)}, u32[]{:S(2)}, u32[]{:S(2)}) collective-permute-start(f32[128,128]{1,0:T(8,128)S(1)} %add_add_fusion.6), channel_id=1, source_target_pairs={{0,8},{2,10},{4,12},{6,14},{8,0},{10,2},{12,4},{14,6},{16,24},{18,... | collective-permute-start | bytes 196616 | tf_op jit(solution)/shard_map/ppermute | solution.py:175
  21.3 1.0 %collective-permute-done.16.refs_2_ = f32[128,128]{1,0:T(8,128)S(1)} collective-permute-done((f32[128,128]{1,0:T(8,128)S(1)}, f32[128,128]{1,0:T(8,128)S(1)}, u32[]{:S(2)}, u32[]{:S(2)}) %collective-permute-start.16) | collective-permute-done | bytes 65568 | tf_op jit(solution)/shard_map/ppermute | solution.py:175
  23.1 1.9 %collective-permute-start.18 = (f32[128,128]{1,0:T(8,128)S(1)}, f32[128,128]{1,0:T(8,128)S(1)}, u32[]{:S(2)}, u32[]{:S(2)}) collective-permute-start(f32[128,128]{1,0:T(8,128)S(1)} %get-tuple-element.101), channel_id=1, source_target_pairs={{0,6},{2,4},{4,2},{6,0},{8,14},{10,12},{12,10},{14,8},{16,22},{18,... | collective-permute-start | bytes 196616 | tf_op jit(solution)/shard_map/ppermute | solution.py:175
  25.2 1.4 %collective-permute-start.20 = (f32[128,128]{1,0:T(8,128)S(1)}, f32[128,128]{1,0:T(8,128)S(1)}, u32[]{:S(2)}, u32[]{:S(2)}) collective-permute-start(f32[128,128]{1,0:T(8,128)S(1)} %get-tuple-element.103), channel_id=1, source_target_pairs={{0,2},{2,0},{4,6},{6,4},{8,10},{10,8},{12,14},{14,12},{16,18},{18,... | collective-permute-start | bytes 196616 | tf_op jit(solution)/shard_map/ppermute | solution.py:175
  26.8 1.9 %collective-permute-start.9 = (f32[128,128]{1,0:T(8,128)S(1)}, f32[128,128]{1,0:T(8,128)S(1)}, u32[]{:S(2)}, u32[]{:S(2)}) collective-permute-start(f32[128,128]{1,0:T(8,128)S(1)} %get-tuple-element.91), channel_id=1, source_target_pairs={{0,6},{2,4},{4,2},{6,0},{8,14},{10,12},{12,10},{14,8},{16,22},{18,... | collective-permute-start | bytes 196616 | tf_op jit(solution)/shard_map/ppermute | solution.py:175
  28.9 1.4 %collective-permute-start.11 = (f32[128,128]{1,0:T(8,128)S(1)}, f32[128,128]{1,0:T(8,128)S(1)}, u32[]{:S(2)}, u32[]{:S(2)}) collective-permute-start(f32[128,128]{1,0:T(8,128)S(1)} %get-tuple-element.93), channel_id=1, source_target_pairs={{0,2},{2,0},{4,6},{6,4},{8,10},{10,8},{12,14},{14,12},{16,18},{18,... | collective-permute-start | bytes 196616 | tf_op jit(solution)/shard_map/ppermute | solution.py:175
  30.4 0.7 %norm.3 = (bf16[256,512]{1,0:T(8,128)(2,1)S(1)}, f32[136,128]{1,0:T(8,128)S(1)}, f32[136,128]{1,0:T(8,128)S(1)}, f32[136,128]{1,0:T(8,128)S(1)}, f32[136,128]{1,0:T(8,128)S(1)}) custom-call(s32[1]{0:T(128)} %bitcast.place_ref, bf16[256,1024]{1,0:T(8,128)(2,1)S(1)} %bitcast.14, bf16[256,1024]{1,0:T(8,128)(2,1)S(1)} %bitcast.11, ...), custom_call_target="tpu_custom_call" | custom-call | flops 536870912 | bytes 2097152 | tf_op jit(solution)/shard_map/norm/pallas_call | solution.py:241
  31.1 1.9 %collective-permute-start.21 = (f32[136,128]{1,0:T(8,128)S(1)}, f32[136,128]{1,0:T(8,128)S(1)}, u32[]{:S(2)}, u32[]{:S(2)}) collective-permute-start(f32[136,128]{1,0:T(8,128)S(1)} %get-tuple-element.105), channel_id=1, source_target_pairs={{0,6},{2,4},{4,2},{6,0},{8,14},{10,12},{12,10},{14,8},{16,22},{18,... | collective-permute-start | bytes 208904 | tf_op jit(solution)/shard_map/ppermute | solution.py:175
  33.3 1.4 %collective-permute-start.23 = (f32[136,128]{1,0:T(8,128)S(1)}, f32[136,128]{1,0:T(8,128)S(1)}, u32[]{:S(2)}, u32[]{:S(2)}) collective-permute-start(f32[136,128]{1,0:T(8,128)S(1)} %get-tuple-element.107), channel_id=1, source_target_pairs={{0,2},{2,0},{4,6},{6,4},{8,10},{10,8},{12,14},{14,12},{16,18},{18,... | collective-permute-start | bytes 208904 | tf_op jit(solution)/shard_map/ppermute | solution.py:175
  34.7 0.7 %norm.2 = (bf16[256,512]{1,0:T(8,128)(2,1)S(1)}, f32[136,128]{1,0:T(8,128)S(1)}, f32[136,128]{1,0:T(8,128)S(1)}, f32[136,128]{1,0:T(8,128)S(1)}, f32[136,128]{1,0:T(8,128)S(1)}) custom-call(s32[1]{0:T(128)} %bitcast.place_ref, bf16[256,1024]{1,0:T(8,128)(2,1)S(1)} %bitcast.15, bf16[256,1024]{1,0:T(8,128)(2,1)S(1)} %bitcast.12, ...), custom_call_target="tpu_custom_call" | custom-call | flops 536870912 | bytes 2097152 | tf_op jit(solution)/shard_map/norm/pallas_call | solution.py:241
  35.4 1.9 %collective-permute-start.12 = (f32[136,128]{1,0:T(8,128)S(1)}, f32[136,128]{1,0:T(8,128)S(1)}, u32[]{:S(2)}, u32[]{:S(2)}) collective-permute-start(f32[136,128]{1,0:T(8,128)S(1)} %get-tuple-element.96), channel_id=1, source_target_pairs={{0,6},{2,4},{4,2},{6,0},{8,14},{10,12},{12,10},{14,8},{16,22},{18,... | collective-permute-start | bytes 208904 | tf_op jit(solution)/shard_map/ppermute | solution.py:175
  37.6 1.4 %collective-permute-start.14 = (f32[136,128]{1,0:T(8,128)S(1)}, f32[136,128]{1,0:T(8,128)S(1)}, u32[]{:S(2)}, u32[]{:S(2)}) collective-permute-start(f32[136,128]{1,0:T(8,128)S(1)} %get-tuple-element.98), channel_id=1, source_target_pairs={{0,2},{2,0},{4,6},{6,4},{8,10},{10,8},{12,14},{14,12},{16,18},{18,... | collective-permute-start | bytes 208904 | tf_op jit(solution)/shard_map/ppermute | solution.py:175
  39.0 2.0 %collective-permute-start.26 = (f32[136,128]{1,0:T(8,128)S(1)}, f32[136,128]{1,0:T(8,128)S(1)}, u32[]{:S(2)}, u32[]{:S(2)}) collective-permute-start(f32[136,128]{1,0:T(8,128)S(1)} %add_add_fusion.3), channel_id=1, source_target_pairs={{0,24},{2,26},{4,28},{6,30},{8,16},{10,18},{12,20},{14,22},{16,8},... | collective-permute-start | bytes 208904 | tf_op jit(solution)/shard_map/ppermute | solution.py:175
  41.0 1.9 %partial.2 = (bf16[256,1024]{1,0:T(8,128)(2,1)}, f32[256,512]{1,0:T(8,128)S(1)}, f32[256,512]{1,0:T(8,128)S(1)}) custom-call(s32[1]{0:T(128)} %bitcast.place_ref, bf16[256,1024]{1,0:T(8,128)(2,1)S(1)} %bitcast.16, bf16[256,1024]{1,0:T(8,128)(2,1)S(1)} %bitcast.22, bf16[256,1024]{1,0:T(8,128)(2,1)S(1)} %bitcast.27, ...), custom_call_target="tpu_custom_call" | custom-call | flops 1610612736 | bytes 2097152 | tf_op jit(solution)/shard_map/partial/pallas_call | solution.py:253
  42.9 2.4 %collective-permute-start.24 = (f32[136,128]{1,0:T(8,128)S(1)}, f32[136,128]{1,0:T(8,128)S(1)}, u32[]{:S(2)}, u32[]{:S(2)}) collective-permute-start(f32[136,128]{1,0:T(8,128)S(1)} %add_add_fusion.3), channel_id=1, source_target_pairs={{0,8},{2,10},{4,12},{6,14},{8,0},{10,2},{12,4},{14,6},{16,24},{18,... | collective-permute-start | bytes 208904 | tf_op jit(solution)/shard_map/ppermute | solution.py:175
  45.4 2.0 %collective-permute-start.32 = (f32[136,128]{1,0:T(8,128)S(1)}, f32[136,128]{1,0:T(8,128)S(1)}, u32[]{:S(2)}, u32[]{:S(2)}) collective-permute-start(f32[136,128]{1,0:T(8,128)S(1)} %add_add_fusion.1), channel_id=1, source_target_pairs={{0,24},{2,26},{4,28},{6,30},{8,16},{10,18},{12,20},{14,22},{16,8},... | collective-permute-start | bytes 208904 | tf_op jit(solution)/shard_map/ppermute | solution.py:175
  47.4 2.4 %collective-permute-start.30 = (f32[136,128]{1,0:T(8,128)S(1)}, f32[136,128]{1,0:T(8,128)S(1)}, u32[]{:S(2)}, u32[]{:S(2)}) collective-permute-start(f32[136,128]{1,0:T(8,128)S(1)} %add_add_fusion.1), channel_id=1, source_target_pairs={{0,8},{2,10},{4,12},{6,14},{8,0},{10,2},{12,4},{14,6},{16,24},{18,... | collective-permute-start | bytes 208904 | tf_op jit(solution)/shard_map/ppermute | solution.py:175
  50.0 1.9 %collective-permute-start.27 = (f32[136,128]{1,0:T(8,128)S(1)}, f32[136,128]{1,0:T(8,128)S(1)}, u32[]{:S(2)}, u32[]{:S(2)}) collective-permute-start(f32[136,128]{1,0:T(8,128)S(1)} %get-tuple-element.129), channel_id=1, source_target_pairs={{0,6},{2,4},{4,2},{6,0},{8,14},{10,12},{12,10},{14,8},{16,22},{18,... | collective-permute-start | bytes 208904 | tf_op jit(solution)/shard_map/ppermute | solution.py:175
  52.1 1.4 %collective-permute-start.29 = (f32[136,128]{1,0:T(8,128)S(1)}, f32[136,128]{1,0:T(8,128)S(1)}, u32[]{:S(2)}, u32[]{:S(2)}) collective-permute-start(f32[136,128]{1,0:T(8,128)S(1)} %get-tuple-element.131), channel_id=1, source_target_pairs={{0,2},{2,0},{4,6},{6,4},{8,10},{10,8},{12,14},{14,12},{16,18},{18,... | collective-permute-start | bytes 208904 | tf_op jit(solution)/shard_map/ppermute | solution.py:175
  53.7 1.9 %collective-permute-start.33 = (f32[136,128]{1,0:T(8,128)S(1)}, f32[136,128]{1,0:T(8,128)S(1)}, u32[]{:S(2)}, u32[]{:S(2)}) collective-permute-start(f32[136,128]{1,0:T(8,128)S(1)} %get-tuple-element.137), channel_id=1, source_target_pairs={{0,6},{2,4},{4,2},{6,0},{8,14},{10,12},{12,10},{14,8},{16,22},{18,... | collective-permute-start | bytes 208904 | tf_op jit(solution)/shard_map/ppermute | solution.py:175
  55.8 1.4 %collective-permute-start.35 = (f32[136,128]{1,0:T(8,128)S(1)}, f32[136,128]{1,0:T(8,128)S(1)}, u32[]{:S(2)}, u32[]{:S(2)}) collective-permute-start(f32[136,128]{1,0:T(8,128)S(1)} %get-tuple-element.139), channel_id=1, source_target_pairs={{0,2},{2,0},{4,6},{6,4},{8,10},{10,8},{12,14},{14,12},{16,18},{18,... | collective-permute-start | bytes 208904 | tf_op jit(solution)/shard_map/ppermute | solution.py:175
  57.2 1.9 %partial.3 = (bf16[256,1024]{1,0:T(8,128)(2,1)}, f32[256,512]{1,0:T(8,128)S(1)}, f32[256,512]{1,0:T(8,128)S(1)}) custom-call(s32[1]{0:T(128)} %bitcast.place_ref, bf16[256,1024]{1,0:T(8,128)(2,1)S(1)} %bitcast.17, bf16[256,1024]{1,0:T(8,128)(2,1)S(1)} %bitcast.23, bf16[256,1024]{1,0:T(8,128)(2,1)S(1)} %bitcast.28, ...), custom_call_target="tpu_custom_call", output_to_operand_aliasing={{0}: (9, {})} | custom-call | flops 1610612736 | bytes 2097152 | tf_op jit(solution)/shard_map/partial/pallas_call | solution.py:253
  59.2 0.7 %collective-permute-done.34.refs_10_.refs_6_ = f32[136,128]{1,0:T(8,128)S(1)} collective-permute-done((f32[136,128]{1,0:T(8,128)S(1)}, f32[136,128]{1,0:T(8,128)S(1)}, u32[]{:S(2)}, u32[]{:S(2)}) %collective-permute-start.34) | collective-permute-done | bytes 69664 | tf_op jit(solution)/shard_map/ppermute | solution.py:175
  60.1 1.6 %final.1 = (bf16[256,1024]{1,0:T(8,128)(2,1)}, bf16[256,1024]{1,0:T(8,128)(2,1)}) custom-call(s32[1]{0:T(128)} %bitcast.place_ref, bf16[256,1024]{1,0:T(8,128)(2,1)S(1)} %bitcast.24, bf16[256,1024]{1,0:T(8,128)(2,1)S(1)} %bitcast.29, f32[256,512]{1,0:T(8,128)S(1)} %get-tuple-element.123.refs_0_, f32[256,512]{1,0:T(8,128)S(1)} %get-tuple-element.124.refs_1_, ...), custom_call_target="tpu_custom_call" | custom-call | flops 1073741824 | bytes 2097152 | tf_op jit(solution)/shard_map/final/pallas_call | solution.py:276
  (73 shorter events, 5.2 us)
Async XLA Ops:
  2.3 8.0 %collective-permute-start.3 = (f32[128,128]{1,0:T(8,128)S(1)}, f32[128,128]{1,0:T(8,128)S(1)}, u32[]{:S(2)}, u32[]{:S(2)}) collective-permute-start(f32[128,128]{1,0:T(8,128)S(1)} %get-tuple-element.78), channel_id=1, source_target_pairs={{0,6},{2,4},{4,2},{6,0},{8,14},{10,12},{12,10},{14,8},{16,22},{18,... | collective-permute-start | bytes 196616 | tf_op jit(solution)/shard_map/ppermute | solution.py:175
  6.9 9.1 %collective-permute-start = (f32[128,128]{1,0:T(8,128)S(1)}, f32[128,128]{1,0:T(8,128)S(1)}, u32[]{:S(2)}, u32[]{:S(2)}) collective-permute-start(f32[128,128]{1,0:T(8,128)S(1)} %get-tuple-element.74), channel_id=1, source_target_pairs={{0,6},{2,4},{4,2},{6,0},{8,14},{10,12},{12,10},{14,8},{16,22},{18,... | collective-permute-start | bytes 196616 | tf_op jit(solution)/shard_map/ppermute | solution.py:175
  9.8 7.1 %collective-permute-start.1 = (f32[128,128]{1,0:T(8,128)S(1)}, f32[128,128]{1,0:T(8,128)S(1)}, u32[]{:S(2)}, u32[]{:S(2)}) collective-permute-start(f32[128,128]{1,0:T(8,128)S(1)} %get-tuple-element.75), channel_id=1, source_target_pairs={{0,4},{2,6},{4,0},{6,2},{8,12},{10,14},{12,8},{14,10},{16,20},{18,... | collective-permute-start | bytes 196616 | tf_op jit(solution)/shard_map/ppermute | solution.py:175
  10.3 6.6 %collective-permute-start.2 = (f32[128,128]{1,0:T(8,128)S(1)}, f32[128,128]{1,0:T(8,128)S(1)}, u32[]{:S(2)}, u32[]{:S(2)}) collective-permute-start(f32[128,128]{1,0:T(8,128)S(1)} %get-tuple-element.76), channel_id=1, source_target_pairs={{0,2},{2,0},{4,6},{6,4},{8,10},{10,8},{12,14},{14,12},{16,18},{18,... | collective-permute-start | bytes 196616 | tf_op jit(solution)/shard_map/ppermute | solution.py:175
  11.4 9.2 %collective-permute-start.17 = (f32[128,128]{1,0:T(8,128)S(1)}, f32[128,128]{1,0:T(8,128)S(1)}, u32[]{:S(2)}, u32[]{:S(2)}) collective-permute-start(f32[128,128]{1,0:T(8,128)S(1)} %add_add_fusion.7), channel_id=1, source_target_pairs={{0,24},{2,26},{4,28},{6,30},{8,16},{10,18},{12,20},{14,22},{16,8},... | collective-permute-start | bytes 196616 | tf_op jit(solution)/shard_map/ppermute | solution.py:175
  15.0 7.3 %collective-permute-start.16 = (f32[128,128]{1,0:T(8,128)S(1)}, f32[128,128]{1,0:T(8,128)S(1)}, u32[]{:S(2)}, u32[]{:S(2)}) collective-permute-start(f32[128,128]{1,0:T(8,128)S(1)} %add_add_fusion.7), channel_id=1, source_target_pairs={{0,16},{2,18},{4,20},{6,22},{8,24},{10,26},{12,28},{14,30},{16,0},... | collective-permute-start | bytes 196616 | tf_op jit(solution)/shard_map/ppermute | solution.py:175
  16.0 7.0 %collective-permute-start.15 = (f32[128,128]{1,0:T(8,128)S(1)}, f32[128,128]{1,0:T(8,128)S(1)}, u32[]{:S(2)}, u32[]{:S(2)}) collective-permute-start(f32[128,128]{1,0:T(8,128)S(1)} %add_add_fusion.7), channel_id=1, source_target_pairs={{0,8},{2,10},{4,12},{6,14},{8,0},{10,2},{12,4},{14,6},{16,24},{18,... | collective-permute-start | bytes 196616 | tf_op jit(solution)/shard_map/ppermute | solution.py:175
  16.9 8.4 %collective-permute-start.8 = (f32[128,128]{1,0:T(8,128)S(1)}, f32[128,128]{1,0:T(8,128)S(1)}, u32[]{:S(2)}, u32[]{:S(2)}) collective-permute-start(f32[128,128]{1,0:T(8,128)S(1)} %add_add_fusion.6), channel_id=1, source_target_pairs={{0,24},{2,26},{4,28},{6,30},{8,16},{10,18},{12,20},{14,22},{16,8},... | collective-permute-start | bytes 196616 | tf_op jit(solution)/shard_map/ppermute | solution.py:175
  20.5 6.1 %collective-permute-start.7 = (f32[128,128]{1,0:T(8,128)S(1)}, f32[128,128]{1,0:T(8,128)S(1)}, u32[]{:S(2)}, u32[]{:S(2)}) collective-permute-start(f32[128,128]{1,0:T(8,128)S(1)} %add_add_fusion.6), channel_id=1, source_target_pairs={{0,16},{2,18},{4,20},{6,22},{8,24},{10,26},{12,28},{14,30},{16,0},... | collective-permute-start | bytes 196616 | tf_op jit(solution)/shard_map/ppermute | solution.py:175
  20.5 6.1 %collective-permute-start.6 = (f32[128,128]{1,0:T(8,128)S(1)}, f32[128,128]{1,0:T(8,128)S(1)}, u32[]{:S(2)}, u32[]{:S(2)}) collective-permute-start(f32[128,128]{1,0:T(8,128)S(1)} %add_add_fusion.6), channel_id=1, source_target_pairs={{0,8},{2,10},{4,12},{6,14},{8,0},{10,2},{12,4},{14,6},{16,24},{18,... | collective-permute-start | bytes 196616 | tf_op jit(solution)/shard_map/ppermute | solution.py:175
  23.1 5.8 %collective-permute-start.18 = (f32[128,128]{1,0:T(8,128)S(1)}, f32[128,128]{1,0:T(8,128)S(1)}, u32[]{:S(2)}, u32[]{:S(2)}) collective-permute-start(f32[128,128]{1,0:T(8,128)S(1)} %get-tuple-element.101), channel_id=1, source_target_pairs={{0,6},{2,4},{4,2},{6,0},{8,14},{10,12},{12,10},{14,8},{16,22},{18,... | collective-permute-start | bytes 196616 | tf_op jit(solution)/shard_map/ppermute | solution.py:175
  25.0 5.3 %collective-permute-start.19 = (f32[128,128]{1,0:T(8,128)S(1)}, f32[128,128]{1,0:T(8,128)S(1)}, u32[]{:S(2)}, u32[]{:S(2)}) collective-permute-start(f32[128,128]{1,0:T(8,128)S(1)} %get-tuple-element.102), channel_id=1, source_target_pairs={{0,4},{2,6},{4,0},{6,2},{8,12},{10,14},{12,8},{14,10},{16,20},{18,... | collective-permute-start | bytes 196616 | tf_op jit(solution)/shard_map/ppermute | solution.py:175
  25.2 5.1 %collective-permute-start.20 = (f32[128,128]{1,0:T(8,128)S(1)}, f32[128,128]{1,0:T(8,128)S(1)}, u32[]{:S(2)}, u32[]{:S(2)}) collective-permute-start(f32[128,128]{1,0:T(8,128)S(1)} %get-tuple-element.103), channel_id=1, source_target_pairs={{0,2},{2,0},{4,6},{6,4},{8,10},{10,8},{12,14},{14,12},{16,18},{18,... | collective-permute-start | bytes 196616 | tf_op jit(solution)/shard_map/ppermute | solution.py:175
  26.8 6.5 %collective-permute-start.9 = (f32[128,128]{1,0:T(8,128)S(1)}, f32[128,128]{1,0:T(8,128)S(1)}, u32[]{:S(2)}, u32[]{:S(2)}) collective-permute-start(f32[128,128]{1,0:T(8,128)S(1)} %get-tuple-element.91), channel_id=1, source_target_pairs={{0,6},{2,4},{4,2},{6,0},{8,14},{10,12},{12,10},{14,8},{16,22},{18,... | collective-permute-start | bytes 196616 | tf_op jit(solution)/shard_map/ppermute | solution.py:175
  28.7 6.0 %collective-permute-start.10 = (f32[128,128]{1,0:T(8,128)S(1)}, f32[128,128]{1,0:T(8,128)S(1)}, u32[]{:S(2)}, u32[]{:S(2)}) collective-permute-start(f32[128,128]{1,0:T(8,128)S(1)} %get-tuple-element.92), channel_id=1, source_target_pairs={{0,4},{2,6},{4,0},{6,2},{8,12},{10,14},{12,8},{14,10},{16,20},{18,... | collective-permute-start | bytes 196616 | tf_op jit(solution)/shard_map/ppermute | solution.py:175
  28.9 5.8 %collective-permute-start.11 = (f32[128,128]{1,0:T(8,128)S(1)}, f32[128,128]{1,0:T(8,128)S(1)}, u32[]{:S(2)}, u32[]{:S(2)}) collective-permute-start(f32[128,128]{1,0:T(8,128)S(1)} %get-tuple-element.93), channel_id=1, source_target_pairs={{0,2},{2,0},{4,6},{6,4},{8,10},{10,8},{12,14},{14,12},{16,18},{18,... | collective-permute-start | bytes 196616 | tf_op jit(solution)/shard_map/ppermute | solution.py:175
  31.1 6.5 %collective-permute-start.21 = (f32[136,128]{1,0:T(8,128)S(1)}, f32[136,128]{1,0:T(8,128)S(1)}, u32[]{:S(2)}, u32[]{:S(2)}) collective-permute-start(f32[136,128]{1,0:T(8,128)S(1)} %get-tuple-element.105), channel_id=1, source_target_pairs={{0,6},{2,4},{4,2},{6,0},{8,14},{10,12},{12,10},{14,8},{16,22},{18,... | collective-permute-start | bytes 208904 | tf_op jit(solution)/shard_map/ppermute | solution.py:175
  33.0 6.0 %collective-permute-start.22 = (f32[136,128]{1,0:T(8,128)S(1)}, f32[136,128]{1,0:T(8,128)S(1)}, u32[]{:S(2)}, u32[]{:S(2)}) collective-permute-start(f32[136,128]{1,0:T(8,128)S(1)} %get-tuple-element.106), channel_id=1, source_target_pairs={{0,4},{2,6},{4,0},{6,2},{8,12},{10,14},{12,8},{14,10},{16,20},{18,... | collective-permute-start | bytes 208904 | tf_op jit(solution)/shard_map/ppermute | solution.py:175
  33.3 5.7 %collective-permute-start.23 = (f32[136,128]{1,0:T(8,128)S(1)}, f32[136,128]{1,0:T(8,128)S(1)}, u32[]{:S(2)}, u32[]{:S(2)}) collective-permute-start(f32[136,128]{1,0:T(8,128)S(1)} %get-tuple-element.107), channel_id=1, source_target_pairs={{0,2},{2,0},{4,6},{6,4},{8,10},{10,8},{12,14},{14,12},{16,18},{18,... | collective-permute-start | bytes 208904 | tf_op jit(solution)/shard_map/ppermute | solution.py:175
  35.4 7.5 %collective-permute-start.12 = (f32[136,128]{1,0:T(8,128)S(1)}, f32[136,128]{1,0:T(8,128)S(1)}, u32[]{:S(2)}, u32[]{:S(2)}) collective-permute-start(f32[136,128]{1,0:T(8,128)S(1)} %get-tuple-element.96), channel_id=1, source_target_pairs={{0,6},{2,4},{4,2},{6,0},{8,14},{10,12},{12,10},{14,8},{16,22},{18,... | collective-permute-start | bytes 208904 | tf_op jit(solution)/shard_map/ppermute | solution.py:175
  37.3 8.1 %collective-permute-start.13 = (f32[136,128]{1,0:T(8,128)S(1)}, f32[136,128]{1,0:T(8,128)S(1)}, u32[]{:S(2)}, u32[]{:S(2)}) collective-permute-start(f32[136,128]{1,0:T(8,128)S(1)} %get-tuple-element.97), channel_id=1, source_target_pairs={{0,4},{2,6},{4,0},{6,2},{8,12},{10,14},{12,8},{14,10},{16,20},{18,... | collective-permute-start | bytes 208904 | tf_op jit(solution)/shard_map/ppermute | solution.py:175
  37.6 7.8 %collective-permute-start.14 = (f32[136,128]{1,0:T(8,128)S(1)}, f32[136,128]{1,0:T(8,128)S(1)}, u32[]{:S(2)}, u32[]{:S(2)}) collective-permute-start(f32[136,128]{1,0:T(8,128)S(1)} %get-tuple-element.98), channel_id=1, source_target_pairs={{0,2},{2,0},{4,6},{6,4},{8,10},{10,8},{12,14},{14,12},{16,18},{18,... | collective-permute-start | bytes 208904 | tf_op jit(solution)/shard_map/ppermute | solution.py:175
  39.0 8.4 %collective-permute-start.26 = (f32[136,128]{1,0:T(8,128)S(1)}, f32[136,128]{1,0:T(8,128)S(1)}, u32[]{:S(2)}, u32[]{:S(2)}) collective-permute-start(f32[136,128]{1,0:T(8,128)S(1)} %add_add_fusion.3), channel_id=1, source_target_pairs={{0,24},{2,26},{4,28},{6,30},{8,16},{10,18},{12,20},{14,22},{16,8},... | collective-permute-start | bytes 208904 | tf_op jit(solution)/shard_map/ppermute | solution.py:175
  41.0 8.9 %collective-permute-start.25 = (f32[136,128]{1,0:T(8,128)S(1)}, f32[136,128]{1,0:T(8,128)S(1)}, u32[]{:S(2)}, u32[]{:S(2)}) collective-permute-start(f32[136,128]{1,0:T(8,128)S(1)} %add_add_fusion.3), channel_id=1, source_target_pairs={{0,16},{2,18},{4,20},{6,22},{8,24},{10,26},{12,28},{14,30},{16,0},... | collective-permute-start | bytes 208904 | tf_op jit(solution)/shard_map/ppermute | solution.py:175
  42.9 6.9 %collective-permute-start.24 = (f32[136,128]{1,0:T(8,128)S(1)}, f32[136,128]{1,0:T(8,128)S(1)}, u32[]{:S(2)}, u32[]{:S(2)}) collective-permute-start(f32[136,128]{1,0:T(8,128)S(1)} %add_add_fusion.3), channel_id=1, source_target_pairs={{0,8},{2,10},{4,12},{6,14},{8,0},{10,2},{12,4},{14,6},{16,24},{18,... | collective-permute-start | bytes 208904 | tf_op jit(solution)/shard_map/ppermute | solution.py:175
  45.4 6.7 %collective-permute-start.32 = (f32[136,128]{1,0:T(8,128)S(1)}, f32[136,128]{1,0:T(8,128)S(1)}, u32[]{:S(2)}, u32[]{:S(2)}) collective-permute-start(f32[136,128]{1,0:T(8,128)S(1)} %add_add_fusion.1), channel_id=1, source_target_pairs={{0,24},{2,26},{4,28},{6,30},{8,16},{10,18},{12,20},{14,22},{16,8},... | collective-permute-start | bytes 208904 | tf_op jit(solution)/shard_map/ppermute | solution.py:175
  47.4 6.1 %collective-permute-start.31 = (f32[136,128]{1,0:T(8,128)S(1)}, f32[136,128]{1,0:T(8,128)S(1)}, u32[]{:S(2)}, u32[]{:S(2)}) collective-permute-start(f32[136,128]{1,0:T(8,128)S(1)} %add_add_fusion.1), channel_id=1, source_target_pairs={{0,16},{2,18},{4,20},{6,22},{8,24},{10,26},{12,28},{14,30},{16,0},... | collective-permute-start | bytes 208904 | tf_op jit(solution)/shard_map/ppermute | solution.py:175
  47.4 6.1 %collective-permute-start.30 = (f32[136,128]{1,0:T(8,128)S(1)}, f32[136,128]{1,0:T(8,128)S(1)}, u32[]{:S(2)}, u32[]{:S(2)}) collective-permute-start(f32[136,128]{1,0:T(8,128)S(1)} %add_add_fusion.1), channel_id=1, source_target_pairs={{0,8},{2,10},{4,12},{6,14},{8,0},{10,2},{12,4},{14,6},{16,24},{18,... | collective-permute-start | bytes 208904 | tf_op jit(solution)/shard_map/ppermute | solution.py:175
  50.0 5.8 %collective-permute-start.27 = (f32[136,128]{1,0:T(8,128)S(1)}, f32[136,128]{1,0:T(8,128)S(1)}, u32[]{:S(2)}, u32[]{:S(2)}) collective-permute-start(f32[136,128]{1,0:T(8,128)S(1)} %get-tuple-element.129), channel_id=1, source_target_pairs={{0,6},{2,4},{4,2},{6,0},{8,14},{10,12},{12,10},{14,8},{16,22},{18,... | collective-permute-start | bytes 208904 | tf_op jit(solution)/shard_map/ppermute | solution.py:175
  51.9 7.3 %collective-permute-start.28 = (f32[136,128]{1,0:T(8,128)S(1)}, f32[136,128]{1,0:T(8,128)S(1)}, u32[]{:S(2)}, u32[]{:S(2)}) collective-permute-start(f32[136,128]{1,0:T(8,128)S(1)} %get-tuple-element.130), channel_id=1, source_target_pairs={{0,4},{2,6},{4,0},{6,2},{8,12},{10,14},{12,8},{14,10},{16,20},{18,... | collective-permute-start | bytes 208904 | tf_op jit(solution)/shard_map/ppermute | solution.py:175
  52.1 7.0 %collective-permute-start.29 = (f32[136,128]{1,0:T(8,128)S(1)}, f32[136,128]{1,0:T(8,128)S(1)}, u32[]{:S(2)}, u32[]{:S(2)}) collective-permute-start(f32[136,128]{1,0:T(8,128)S(1)} %get-tuple-element.131), channel_id=1, source_target_pairs={{0,2},{2,0},{4,6},{6,4},{8,10},{10,8},{12,14},{14,12},{16,18},{18,... | collective-permute-start | bytes 208904 | tf_op jit(solution)/shard_map/ppermute | solution.py:175
  53.7 5.5 %collective-permute-start.33 = (f32[136,128]{1,0:T(8,128)S(1)}, f32[136,128]{1,0:T(8,128)S(1)}, u32[]{:S(2)}, u32[]{:S(2)}) collective-permute-start(f32[136,128]{1,0:T(8,128)S(1)} %get-tuple-element.137), channel_id=1, source_target_pairs={{0,6},{2,4},{4,2},{6,0},{8,14},{10,12},{12,10},{14,8},{16,22},{18,... | collective-permute-start | bytes 208904 | tf_op jit(solution)/shard_map/ppermute | solution.py:175
  (10 other events, 72.0 us)

commit v16 on v11

--- a/solution.py
+++ b/solution.py
@@ -15,6 +15,7 @@
 CHAINS = HEADS // GROUP
 WIDE = GROUP * DH
 GAIN_ROWS = 8
+ORDER = (0, 3, 2, 1)
 PARTS = 2
 PART_ROWS = BLOCK // PARTS
 EPSILON = 1e-06
@@ -54,7 +55,7 @@
         for copy in copies[2 * part : 2 * part + 2]:
             copy.wait()
         for at_head, delta_ref in enumerate(delta_refs):
-            at = own_columns(place_ref, at_head % GROUP, at_head // GROUP)
+            at = own_columns(place_ref, ORDER[at_head % GROUP], at_head // GROUP)
             delta = dot(key_here[rows, at], value_here[rows, at], TN)
             delta_ref[...] = delta if part == 0 else delta_ref[...] + delta
 
@@ -69,7 +70,7 @@
 
 def norm_body(chain, place_ref, query_ref, grad_ref, inner_ref, gain_ref, *refs):
     state_refs, (attn_ref, *delta_refs) = refs[:GROUP], refs[GROUP:]
-    for mask, (state_ref, delta_ref) in enumerate(zip(state_refs, delta_refs)):
+    for mask, state_ref, delta_ref in zip(ORDER, state_refs, delta_refs):
         at = own_columns(place_ref, mask, chain)
         query = query_ref[:, at]
         attn = inner_ref[:, at] + dot(query, state_ref[...].astype(jnp.bfloat16), NN)
@@ -90,10 +91,9 @@
     grad_query_ref, key_part_ref, value_part_ref = refs[-3:]
     keep, kept = causal(), causal(True)
     for at_head, state_ref in enumerate(state_refs):
-        chain, mask = at_head // GROUP, at_head % GROUP
-        at = own_columns(place_ref, mask, chain)
-        query, key, value = query_ref[:, at], key_ref[:, at], value_ref[:, at]
-        grad_attn = attn_refs[chain][:, own_columns(place_ref, mask)]
+        chain, mask = at_head // GROUP, ORDER[at_head % GROUP]
+        at, here = own_columns(place_ref, mask, chain), own_columns(place_ref, mask)
+        query, key, value, grad_attn = query_ref[:, at], key_ref[:, at], value_ref[:, at], attn_refs[chain][:, here]
         turned = jnp.where(kept, dot(key, query, NT), 0.0).astype(jnp.bfloat16)
         grad_scores = jnp.where(keep, dot(grad_attn, value, NT), 0.0).astype(jnp.bfloat16)
         turned_grad = jnp.where(kept, dot(value, grad_attn, NT), 0.0).astype(jnp.bfloat16)
@@ -107,7 +107,7 @@
     state_refs, (grad_key_ref, grad_value_ref) = refs[:HEADS], refs[HEADS:]
     rows = pl.ds(pl.multiple_of(pl.program_id(0) * PART_ROWS, PART_ROWS), PART_ROWS)
     for at_head, state_ref in enumerate(state_refs):
-        at = own_columns(place_ref, at_head % GROUP, at_head // GROUP)
+        at = own_columns(place_ref, ORDER[at_head % GROUP], at_head // GROUP)
         state = state_ref[:DH].astype(jnp.bfloat16)
         grad_key_ref[:, at] = (key_part_ref[rows, at] + dot(value_ref[rows, at], state, NT)).astype(jnp.bfloat16)
         grad_value_ref[:, at] = (value_part_ref[rows, at] + dot(key_ref[rows, at], state, NN)).astype(jnp.bfloat16)
@@ -115,24 +115,24 @@
 
 def gain_body(place_ref, *refs):
     for at_head, state_ref in enumerate(refs[:-1]):
-        row = (at_head // GROUP) * GROUP + (place_ref[0] & (GROUP - 1) ^ (at_head % GROUP))
+        row = (at_head // GROUP) * GROUP + (place_ref[0] & (GROUP - 1) ^ ORDER[at_head % GROUP])
         refs[-1][pl.ds(row, 1), :] = state_ref[DH : DH + 1]
 
 
 def prefix_body(reverse, masks, place_ref, *refs):
     (total_ref, *arrived_refs), (*back_refs, ahead) = refs[: -2 * GROUP - 1], refs[-GROUP - 1 :]
     held_refs = refs[-2 * GROUP - 1 : -GROUP - 1]
-    for mask, held_ref in enumerate(held_refs):
+    for mask, held_ref in zip(ORDER, held_refs):
         ahead[pl.ds(place_ref[0] & (GROUP - 1) ^ mask, 1)] = held_ref[:DH][None]
     running = jnp.zeros((DH, DH), jnp.float32)
     for mask, arrived_ref in zip(masks, arrived_refs):
-        later = (place_ref[0] & mask == 0) == reverse
+        later = (place_ref[0] ^ mask < place_ref[0]) != reverse
         running = running + jnp.where(later, arrived_ref[:DH], 0.0)
     for member in reversed(range(GROUP)) if reverse else range(GROUP):
         own = ahead[member]
         ahead[member] = running
         running = running + own
-    for mask, back_ref in enumerate(back_refs):
+    for mask, back_ref in zip(ORDER, back_refs):
         back_ref[:DH] = ahead[pl.ds(place_ref[0] & (GROUP - 1) ^ mask, 1)][0]
         if back_ref.shape[0] > DH:
             back_ref[DH:] = total_ref[DH:]
@@ -159,11 +159,13 @@
     )
 
 
-def exchange_masks():
-    masks = [GROUP]
-    while masks[-1] * 2 < lax.axis_size("seq"):
-        masks.append(masks[-1] * 2)
-    return masks if lax.axis_size("seq") > GROUP else []
+def exchange_steps():
+    count, base, steps = lax.axis_size("seq"), GROUP, []
+    while base < count:
+        masks = [base, 3 * base, 2 * base] if 4 * base <= count else [base]
+        steps.append(masks)
+        base *= len(masks) + 1
+    return steps
 
 
 def swap(array, mask):
@@ -172,16 +174,22 @@
     return lax.ppermute(array, "seq", [(s, s ^ mask) for s in range(lax.axis_size("seq"))])
 
 
-def carried_in(pieces, reverse, place):
-    held = [swap(piece, mask) for mask, piece in enumerate(pieces)]
-    total = sum(held[1:], held[0])
-    arrived = []
-    for mask in exchange_masks():
-        arrived.append(swap(total, mask))
-        total = total + arrived[-1]
+def plane_swap(pieces):
+    return lax.optimization_barrier([swap(piece, mask) for mask, piece in zip(ORDER, pieces)])
+
+
+def exchange(held):
+    total, arrived = sum(held[1:], held[0]), []
+    for masks in exchange_steps():
+        arrived += lax.optimization_barrier([swap(total, mask) for mask in masks])
+        total = sum(arrived[-len(masks) :], total)
+    return total, arrived
+
+
+def carried_in(held, total, arrived, reverse, place):
     single = whole(*total.shape)
     back = call(
-        functools.partial(prefix_body, reverse, exchange_masks()),
+        functools.partial(prefix_body, reverse, sum(exchange_steps(), [])),
         [single] * (1 + len(arrived) + GROUP),
         [single] * GROUP,
         [jax.ShapeDtypeStruct(total.shape, jnp.float32)] * GROUP,
@@ -189,7 +197,7 @@
         "prefix",
         scratch=[pltpu.VMEM((GROUP, DH, DH), jnp.float32)],
     )(place, total, *arrived, *held)
-    return [swap(piece, mask) for mask, piece in enumerate(back)]
+    return plane_swap(back)
 
 
 def local(queries, keys, values, out_gain, grad_out):
@@ -217,10 +225,14 @@
         scratch=[pltpu.VMEM(flat, jnp.bfloat16)] * 2 + [pltpu.SemaphoreType.DMA((PARTS, 2))],
     )(place, *[pltpu.with_memory_space_constraint(a, pltpu.HBM) for a in (key, value)])
     chains = [slice(chain * GROUP, (chain + 1) * GROUP) for chain in range(CHAINS)]
-    states = [carried_in(deltas[chain], False, place) for chain in chains]
-    inner = call(
+    inner_call = call(
         lambda place_ref, *refs: inner_body(*refs), [wide] * 3, wide, full_float, 16 * unit, "inner"
-    )(place, query, key, value)
+    )
+    helds = [plane_swap(deltas[chain]) for chain in chains]
+    helds[1], operands = lax.optimization_barrier((helds[1], (place, query, key, value)))
+    (total, arrived), *others = [exchange(held) for held in helds]
+    arrived, inner = lax.optimization_barrier((arrived, inner_call(*operands)))
+    states = [carried_in(*sums, False, place) for sums in zip(helds, *zip((total, arrived), *others))]
     attns, later = [], []
     for chain in range(CHAINS):
         attn, *deltas = call(
@@ -232,7 +244,8 @@
             "norm",
         )(place, query, grad, inner, gain, *states[chain])
         attns.append(attn)
-        later += carried_in(deltas, True, place)
+        held = plane_swap(deltas)
+        later += carried_in(held, *exchange(held), True, place)
     grad_query, key_part, value_part = call(
         partial_body,
         [wide] * 3 + [half] * CHAINS + [short] * HEADS,

time: 63.7 us -> 62.7 us (0.984)
  waiting for transfers between devices: 8.96 us -> 6.18 us
  starting transfers between devices: 44 us -> 45.7 us
    ppermute x32 -> x36, waiting for transfers between devices: 8.96 us -> 6.18 us  [swap(): lax.ppermute(array, 'seq', [(s, s ^ mask) for s in range(lax.axis_size('s...]
    ppermute x32 -> x36, starting transfers between devices: 43.9 us -> 45.7 us  [swap(): lax.ppermute(array, 'seq', [(s, s ^ mask) for s in range(lax.axis_size('s...]
  transfers between devices with their start and end apart: 33 -> 37, of which waited for: 12 -> 7; matrix products, arithmetic and copies ran while one was open for 0% -> 0% of each run, Pallas kernels for 12% -> 12%
where the time goes in v16:
time: 62.7 us; the launch traced here: 62.5 us
  starting transfers between devices  45.7 us (73%)
  Pallas kernels  9.05 us (14%)
  waiting for transfers between devices  6.18 us (10%)
  between operations  0.83 us (1%)
  other arithmetic  0.75 us (1%)
    ppermute x36, starting transfers between devices, swap(): lax.ppermute(array, 'seq', [(s, s ^ mask) for s in range(lax.axis_size('s...  45.7 us
    ppermute x36, waiting for transfers between devices, swap(): lax.ppermute(array, 'seq', [(s, s ^ mask) for s in range(lax.axis_size('s...  6.18 us
    pallas_call x1, Pallas kernels, local(): call(partial_body, [wide] * 3 + [half] * CHAINS + [short] * HEADS, [wide]...  3.09 us
    pallas_call x1, Pallas kernels, local(): call(delta_body, [pl.BlockSpec(memory_space=pltpu.HBM)] * 2, [short] * HE...  1.61 us
    pallas_call x1, Pallas kernels, local(): call(final_body, [wide] * 4 + [tall] * HEADS, [chunk] * 2, [full_low] * 2...  1.61 us
    pallas_call x2, Pallas kernels, local(): call(functools.partial(norm_body, chain), [wide, wide, wide, whole(1, HEA...  1.47 us
  transfers between devices with their start and end apart: 37, of which 7 were waited for; matrix products, arithmetic and copies ran while one was open for 0% of the time, Pallas kernels for 12%

profile of v16, /device:TPU:0, one launch (start us, length us, event | category | flops | bytes accessed | tf_op | source)
XLA Modules:
  0.0 62.5 jit_solution(5296373154982760818)
XLA Ops:
  0.7 1.6 %delta.1 = (f32[128,128]{1,0:T(8,128)S(1)}, f32[128,128]{1,0:T(8,128)S(1)}, f32[128,128]{1,0:T(8,128)S(1)}, f32[128,128]{1,0:T(8,128)S(1)}, f32[128,128]{1,0:T(8...) custom-call(s32[1]{0:T(128)} %bitcast.place_ref, bf16[256,1024]{1,0:T(8,128)(2,1)} %bitcast.19, ...), custom_call_target="tpu_custom_call" | custom-call | flops 402653184 | bytes 2097152 | tf_op jit(solution)/shard_map/delta/pallas_call | solution.py:218
  2.3 4.0 %collective-permute-start = (f32[128,128]{1,0:T(8,128)S(1)}, f32[128,128]{1,0:T(8,128)S(1)}, u32[]{:S(2)}, u32[]{:S(2)}) collective-permute-start(f32[128,128]{1,0:T(8,128)S(1)} %get-tuple-element.100), channel_id=1, source_target_pairs={{0,6},{2,4},{4,2},{6,0},{8,14},{10,12},{12,10},{14,8},{16,22},{18,... | collective-permute-start | bytes 196616 | tf_op jit(solution)/shard_map/ppermute | solution.py:174
  6.9 2.8 %collective-permute-start.6 = (f32[128,128]{1,0:T(8,128)S(1)}, f32[128,128]{1,0:T(8,128)S(1)}, u32[]{:S(2)}, u32[]{:S(2)}) collective-permute-start(f32[128,128]{1,0:T(8,128)S(1)} %get-tuple-element.111), channel_id=1, source_target_pairs={{0,6},{2,4},{4,2},{6,0},{8,14},{10,12},{12,10},{14,8},{16,22},{18,... | collective-permute-start | bytes 196616 | tf_op jit(solution)/shard_map/ppermute | solution.py:174
  11.3 1.6 %collective-permute-start.3 = (f32[128,128]{1,0:T(8,128)S(1)}, f32[128,128]{1,0:T(8,128)S(1)}, u32[]{:S(2)}, u32[]{:S(2)}) collective-permute-start(f32[128,128]{1,0:T(8,128)S(1)} %add_add_fusion.7), channel_id=1, source_target_pairs={{0,8},{2,10},{4,12},{6,14},{8,0},{10,2},{12,4},{14,6},{16,24},{18,... | collective-permute-start | bytes 196616 | tf_op jit(solution)/shard_map/ppermute | solution.py:174
  13.0 2.5 %collective-permute-start.4 = (f32[128,128]{1,0:T(8,128)S(1)}, f32[128,128]{1,0:T(8,128)S(1)}, u32[]{:S(2)}, u32[]{:S(2)}) collective-permute-start(f32[128,128]{1,0:T(8,128)S(1)} %add_add_fusion.7), channel_id=1, source_target_pairs={{0,24},{2,26},{4,28},{6,30},{8,16},{10,18},{12,20},{14,22},{16,8},... | collective-permute-start | bytes 196616 | tf_op jit(solution)/shard_map/ppermute | solution.py:174
  15.7 1.7 %collective-permute-start.12 = (f32[128,128]{1,0:T(8,128)S(1)}, f32[128,128]{1,0:T(8,128)S(1)}, u32[]{:S(2)}, u32[]{:S(2)}) collective-permute-start(f32[128,128]{1,0:T(8,128)S(1)} %add_add_fusion.5), channel_id=1, source_target_pairs={{0,8},{2,10},{4,12},{6,14},{8,0},{10,2},{12,4},{14,6},{16,24},{18,... | collective-permute-start | bytes 196616 | tf_op jit(solution)/shard_map/ppermute | solution.py:174
  17.5 2.5 %collective-permute-start.13 = (f32[128,128]{1,0:T(8,128)S(1)}, f32[128,128]{1,0:T(8,128)S(1)}, u32[]{:S(2)}, u32[]{:S(2)}) collective-permute-start(f32[128,128]{1,0:T(8,128)S(1)} %add_add_fusion.5), channel_id=1, source_target_pairs={{0,24},{2,26},{4,28},{6,30},{8,16},{10,18},{12,20},{14,22},{16,8},... | collective-permute-start | bytes 196616 | tf_op jit(solution)/shard_map/ppermute | solution.py:174
  19.9 0.9 %inner.1.inner_ref = f32[256,1024]{1,0:T(8,128)S(1)} custom-call(s32[1]{0:T(128)} %bitcast.place_ref, bf16[256,1024]{1,0:T(8,128)(2,1)S(1)} %bitcast.13, bf16[256,1024]{1,0:T(8,128)(2,1)S(1)} %bitcast.20, bf16[256,1024]{1,0:T(8,128)(2,1)S(1)} %bitcast.24), custom_call_target="tpu_custom_call" | custom-call | flops 1073741824 | bytes 2097152 | tf_op jit(solution)/shard_map/inner/pallas_call | solution.py:234
  21.0 2.9 %collective-permute-done.5.refs_3_ = f32[128,128]{1,0:T(8,128)S(1)} collective-permute-done((f32[128,128]{1,0:T(8,128)S(1)}, f32[128,128]{1,0:T(8,128)S(1)}, u32[]{:S(2)}, u32[]{:S(2)}) %collective-permute-start.5) | collective-permute-done | bytes 65568 | tf_op jit(solution)/shard_map/ppermute | solution.py:174
  24.0 1.9 %collective-permute-start.9 = (f32[128,128]{1,0:T(8,128)S(1)}, f32[128,128]{1,0:T(8,128)S(1)}, u32[]{:S(2)}, u32[]{:S(2)}) collective-permute-start(f32[128,128]{1,0:T(8,128)S(1)} %get-tuple-element.127), channel_id=1, source_target_pairs={{0,6},{2,4},{4,2},{6,0},{8,14},{10,12},{12,10},{14,8},{16,22},{18,... | collective-permute-start | bytes 196616 | tf_op jit(solution)/shard_map/ppermute | solution.py:174
  25.9 0.8 %collective-permute-start.10 = (f32[128,128]{1,0:T(8,128)S(1)}, f32[128,128]{1,0:T(8,128)S(1)}, u32[]{:S(2)}, u32[]{:S(2)}) collective-permute-start(f32[128,128]{1,0:T(8,128)S(1)} %get-tuple-element.128), channel_id=1, source_target_pairs={{0,4},{2,6},{4,0},{6,2},{8,12},{10,14},{12,8},{14,10},{16,20},{18,... | collective-permute-start | bytes 196616 | tf_op jit(solution)/shard_map/ppermute | solution.py:174
  26.8 0.8 %collective-permute-start.11 = (f32[128,128]{1,0:T(8,128)S(1)}, f32[128,128]{1,0:T(8,128)S(1)}, u32[]{:S(2)}, u32[]{:S(2)}) collective-permute-start(f32[128,128]{1,0:T(8,128)S(1)} %get-tuple-element.129), channel_id=1, source_target_pairs={{0,2},{2,0},{4,6},{6,4},{8,10},{10,8},{12,14},{14,12},{16,18},{18,... | collective-permute-start | bytes 196616 | tf_op jit(solution)/shard_map/ppermute | solution.py:174
  27.7 1.9 %collective-permute-start.15 = (f32[128,128]{1,0:T(8,128)S(1)}, f32[128,128]{1,0:T(8,128)S(1)}, u32[]{:S(2)}, u32[]{:S(2)}) collective-permute-start(f32[128,128]{1,0:T(8,128)S(1)} %get-tuple-element.143), channel_id=1, source_target_pairs={{0,6},{2,4},{4,2},{6,0},{8,14},{10,12},{12,10},{14,8},{16,22},{18,... | collective-permute-start | bytes 196616 | tf_op jit(solution)/shard_map/ppermute | solution.py:174
  29.7 0.8 %collective-permute-start.16 = (f32[128,128]{1,0:T(8,128)S(1)}, f32[128,128]{1,0:T(8,128)S(1)}, u32[]{:S(2)}, u32[]{:S(2)}) collective-permute-start(f32[128,128]{1,0:T(8,128)S(1)} %get-tuple-element.144), channel_id=1, source_target_pairs={{0,4},{2,6},{4,0},{6,2},{8,12},{10,14},{12,8},{14,10},{16,20},{18,... | collective-permute-start | bytes 196616 | tf_op jit(solution)/shard_map/ppermute | solution.py:174
  30.5 0.8 %collective-permute-start.17 = (f32[128,128]{1,0:T(8,128)S(1)}, f32[128,128]{1,0:T(8,128)S(1)}, u32[]{:S(2)}, u32[]{:S(2)}) collective-permute-start(f32[128,128]{1,0:T(8,128)S(1)} %get-tuple-element.145), channel_id=1, source_target_pairs={{0,2},{2,0},{4,6},{6,4},{8,10},{10,8},{12,14},{14,12},{16,18},{18,... | collective-permute-start | bytes 196616 | tf_op jit(solution)/shard_map/ppermute | solution.py:174
  31.6 0.7 %norm.2 = (bf16[256,512]{1,0:T(8,128)(2,1)S(1)}, f32[136,128]{1,0:T(8,128)S(1)}, f32[136,128]{1,0:T(8,128)S(1)}, f32[136,128]{1,0:T(8,128)S(1)}, f32[136,128]{1,0:T(8,128)S(1)}) custom-call(s32[1]{0:T(128)} %bitcast.place_ref, bf16[256,1024]{1,0:T(8,128)(2,1)S(1)} %bitcast.14, bf16[256,1024]{1,0:T(8,128)(2,1)S(1)} %bitcast.11, ...), custom_call_target="tpu_custom_call" | custom-call | flops 536870912 | bytes 2097152 | tf_op jit(solution)/shard_map/norm/pallas_call | solution.py:238
  32.3 1.8 %collective-permute-start.18 = (f32[136,128]{1,0:T(8,128)S(1)}, f32[136,128]{1,0:T(8,128)S(1)}, u32[]{:S(2)}, u32[]{:S(2)}) collective-permute-start(f32[136,128]{1,0:T(8,128)S(1)} %get-tuple-element.155), channel_id=1, source_target_pairs={{0,6},{2,4},{4,2},{6,0},{8,14},{10,12},{12,10},{14,8},{16,22},{18,... | collective-permute-start | bytes 208904 | tf_op jit(solution)/shard_map/ppermute | solution.py:174
  34.9 1.0 %collective-permute-start.20 = (f32[136,128]{1,0:T(8,128)S(1)}, f32[136,128]{1,0:T(8,128)S(1)}, u32[]{:S(2)}, u32[]{:S(2)}) collective-permute-start(f32[136,128]{1,0:T(8,128)S(1)} %get-tuple-element.157), channel_id=1, source_target_pairs={{0,2},{2,0},{4,6},{6,4},{8,10},{10,8},{12,14},{14,12},{16,18},{18,... | collective-permute-start | bytes 208904 | tf_op jit(solution)/shard_map/ppermute | solution.py:174
  36.6 1.8 %collective-permute-start.27 = (f32[136,128]{1,0:T(8,128)S(1)}, f32[136,128]{1,0:T(8,128)S(1)}, u32[]{:S(2)}, u32[]{:S(2)}) collective-permute-start(f32[136,128]{1,0:T(8,128)S(1)} %get-tuple-element.174), channel_id=1, source_target_pairs={{0,6},{2,4},{4,2},{6,0},{8,14},{10,12},{12,10},{14,8},{16,22},{18,... | collective-permute-start | bytes 208904 | tf_op jit(solution)/shard_map/ppermute | solution.py:174
  38.4 0.7 %collective-permute-start.28 = (f32[136,128]{1,0:T(8,128)S(1)}, f32[136,128]{1,0:T(8,128)S(1)}, u32[]{:S(2)}, u32[]{:S(2)}) collective-permute-start(f32[136,128]{1,0:T(8,128)S(1)} %get-tuple-element.175), channel_id=1, source_target_pairs={{0,4},{2,6},{4,0},{6,2},{8,12},{10,14},{12,8},{14,10},{16,20},{18,... | collective-permute-start | bytes 208904 | tf_op jit(solution)/shard_map/ppermute | solution.py:174
  39.2 1.0 %collective-permute-start.29 = (f32[136,128]{1,0:T(8,128)S(1)}, f32[136,128]{1,0:T(8,128)S(1)}, u32[]{:S(2)}, u32[]{:S(2)}) collective-permute-start(f32[136,128]{1,0:T(8,128)S(1)} %get-tuple-element.176), channel_id=1, source_target_pairs={{0,2},{2,0},{4,6},{6,4},{8,10},{10,8},{12,14},{14,12},{16,18},{18,... | collective-permute-start | bytes 208904 | tf_op jit(solution)/shard_map/ppermute | solution.py:174
  40.3 2.5 %collective-permute-start.22 = (f32[136,128]{1,0:T(8,128)S(1)}, f32[136,128]{1,0:T(8,128)S(1)}, u32[]{:S(2)}, u32[]{:S(2)}) collective-permute-start(f32[136,128]{1,0:T(8,128)S(1)} %add_add_fusion.3), channel_id=1, source_target_pairs={{0,24},{2,26},{4,28},{6,30},{8,16},{10,18},{12,20},{14,22},{16,8},... | collective-permute-start | bytes 208904 | tf_op jit(solution)/shard_map/ppermute | solution.py:174
  42.8 0.9 %collective-permute-start.23 = (f32[136,128]{1,0:T(8,128)S(1)}, f32[136,128]{1,0:T(8,128)S(1)}, u32[]{:S(2)}, u32[]{:S(2)}) collective-permute-start(f32[136,128]{1,0:T(8,128)S(1)} %add_add_fusion.3), channel_id=1, source_target_pairs={{0,16},{2,18},{4,20},{6,22},{8,24},{10,26},{12,28},{14,30},{16,0},... | collective-permute-start | bytes 208904 | tf_op jit(solution)/shard_map/ppermute | solution.py:174
  43.8 1.3 %collective-permute-start.30 = (f32[136,128]{1,0:T(8,128)S(1)}, f32[136,128]{1,0:T(8,128)S(1)}, u32[]{:S(2)}, u32[]{:S(2)}) collective-permute-start(f32[136,128]{1,0:T(8,128)S(1)} %add_add_fusion.1), channel_id=1, source_target_pairs={{0,8},{2,10},{4,12},{6,14},{8,0},{10,2},{12,4},{14,6},{16,24},{18,... | collective-permute-start | bytes 208904 | tf_op jit(solution)/shard_map/ppermute | solution.py:174
  45.1 2.3 %collective-permute-start.31 = (f32[136,128]{1,0:T(8,128)S(1)}, f32[136,128]{1,0:T(8,128)S(1)}, u32[]{:S(2)}, u32[]{:S(2)}) collective-permute-start(f32[136,128]{1,0:T(8,128)S(1)} %add_add_fusion.1), channel_id=1, source_target_pairs={{0,24},{2,26},{4,28},{6,30},{8,16},{10,18},{12,20},{14,22},{16,8},... | collective-permute-start | bytes 208904 | tf_op jit(solution)/shard_map/ppermute | solution.py:174
  47.4 1.4 %collective-permute-done.23.refs_3_ = f32[136,128]{1,0:T(8,128)S(1)} collective-permute-done((f32[136,128]{1,0:T(8,128)S(1)}, f32[136,128]{1,0:T(8,128)S(1)}, u32[]{:S(2)}, u32[]{:S(2)}) %collective-permute-start.23) | collective-permute-done | bytes 69664 | tf_op jit(solution)/shard_map/ppermute | solution.py:174
  48.9 1.7 %collective-permute-start.24 = (f32[136,128]{1,0:T(8,128)S(1)}, f32[136,128]{1,0:T(8,128)S(1)}, u32[]{:S(2)}, u32[]{:S(2)}) collective-permute-start(f32[136,128]{1,0:T(8,128)S(1)} %get-tuple-element.166), channel_id=1, source_target_pairs={{0,6},{2,4},{4,2},{6,0},{8,14},{10,12},{12,10},{14,8},{16,22},{18,... | collective-permute-start | bytes 208904 | tf_op jit(solution)/shard_map/ppermute | solution.py:174
  50.6 1.3 %collective-permute-start.25 = (f32[136,128]{1,0:T(8,128)S(1)}, f32[136,128]{1,0:T(8,128)S(1)}, u32[]{:S(2)}, u32[]{:S(2)}) collective-permute-start(f32[136,128]{1,0:T(8,128)S(1)} %get-tuple-element.167), channel_id=1, source_target_pairs={{0,4},{2,6},{4,0},{6,2},{8,12},{10,14},{12,8},{14,10},{16,20},{18,... | collective-permute-start | bytes 208904 | tf_op jit(solution)/shard_map/ppermute | solution.py:174
  53.1 1.3 %collective-permute-start.33 = (f32[136,128]{1,0:T(8,128)S(1)}, f32[136,128]{1,0:T(8,128)S(1)}, u32[]{:S(2)}, u32[]{:S(2)}) collective-permute-start(f32[136,128]{1,0:T(8,128)S(1)} %get-tuple-element.185), channel_id=1, source_target_pairs={{0,6},{2,4},{4,2},{6,0},{8,14},{10,12},{12,10},{14,8},{16,22},{18,... | collective-permute-start | bytes 208904 | tf_op jit(solution)/shard_map/ppermute | solution.py:174
  54.5 1.5 %collective-permute-start.34 = (f32[136,128]{1,0:T(8,128)S(1)}, f32[136,128]{1,0:T(8,128)S(1)}, u32[]{:S(2)}, u32[]{:S(2)}) collective-permute-start(f32[136,128]{1,0:T(8,128)S(1)} %get-tuple-element.186), channel_id=1, source_target_pairs={{0,4},{2,6},{4,0},{6,2},{8,12},{10,14},{12,8},{14,10},{16,20},{18,... | collective-permute-start | bytes 208904 | tf_op jit(solution)/shard_map/ppermute | solution.py:174
  56.7 3.1 %partial.1 = (bf16[256,1024]{1,0:T(8,128)(2,1)}, f32[256,1024]{1,0:T(8,128)S(1)}, f32[256,1024]{1,0:T(8,128)S(1)}) custom-call(s32[1]{0:T(128)} %bitcast.place_ref, bf16[256,1024]{1,0:T(8,128)(2,1)S(1)} %bitcast.16, bf16[256,1024]{1,0:T(8,128)(2,1)S(1)} %bitcast.21, bf16[256,1024]{1,0:T(8,128)(2,1)S(1)} %bitcast.25, ...), custom_call_target="tpu_custom_call" | custom-call | flops 3221225472 | bytes 2097152 | tf_op jit(solution)/shard_map/partial/pallas_call | solution.py:249
  60.3 1.6 %final.1 = (bf16[256,1024]{1,0:T(8,128)(2,1)}, bf16[256,1024]{1,0:T(8,128)(2,1)}) custom-call(s32[1]{0:T(128)} %bitcast.place_ref, bf16[256,1024]{1,0:T(8,128)(2,1)S(1)} %bitcast.22, bf16[256,1024]{1,0:T(8,128)(2,1)S(1)} %bitcast.26, f32[256,1024]{1,0:T(8,128)S(1)} %get-tuple-element.152.key_part_ref, f32[256,1024]{1,0:T(8,128)S(1)} %get-tuple-element.153.value_part_ref, ...), custom_call_target="tpu_custom_call" | custom-call | flops 1073741824 | bytes 2097152 | tf_op jit(solution)/shard_map/final/pallas_call | solution.py:265
  (72 shorter events, 7.9 us)
Async XLA Ops:
  2.3 8.0 %collective-permute-start = (f32[128,128]{1,0:T(8,128)S(1)}, f32[128,128]{1,0:T(8,128)S(1)}, u32[]{:S(2)}, u32[]{:S(2)}) collective-permute-start(f32[128,128]{1,0:T(8,128)S(1)} %get-tuple-element.100), channel_id=1, source_target_pairs={{0,6},{2,4},{4,2},{6,0},{8,14},{10,12},{12,10},{14,8},{16,22},{18,... | collective-permute-start | bytes 196616 | tf_op jit(solution)/shard_map/ppermute | solution.py:174
  6.2 5.1 %collective-permute-start.1 = (f32[128,128]{1,0:T(8,128)S(1)}, f32[128,128]{1,0:T(8,128)S(1)}, u32[]{:S(2)}, u32[]{:S(2)}) collective-permute-start(f32[128,128]{1,0:T(8,128)S(1)} %get-tuple-element.101), channel_id=1, source_target_pairs={{0,4},{2,6},{4,0},{6,2},{8,12},{10,14},{12,8},{14,10},{16,20},{18,... | collective-permute-start | bytes 196616 | tf_op jit(solution)/shard_map/ppermute | solution.py:174
  6.9 8.6 %collective-permute-start.6 = (f32[128,128]{1,0:T(8,128)S(1)}, f32[128,128]{1,0:T(8,128)S(1)}, u32[]{:S(2)}, u32[]{:S(2)}) collective-permute-start(f32[128,128]{1,0:T(8,128)S(1)} %get-tuple-element.111), channel_id=1, source_target_pairs={{0,6},{2,4},{4,2},{6,0},{8,14},{10,12},{12,10},{14,8},{16,22},{18,... | collective-permute-start | bytes 196616 | tf_op jit(solution)/shard_map/ppermute | solution.py:174
  9.7 6.0 %collective-permute-start.7 = (f32[128,128]{1,0:T(8,128)S(1)}, f32[128,128]{1,0:T(8,128)S(1)}, u32[]{:S(2)}, u32[]{:S(2)}) collective-permute-start(f32[128,128]{1,0:T(8,128)S(1)} %get-tuple-element.112), channel_id=1, source_target_pairs={{0,4},{2,6},{4,0},{6,2},{8,12},{10,14},{12,8},{14,10},{16,20},{18,... | collective-permute-start | bytes 196616 | tf_op jit(solution)/shard_map/ppermute | solution.py:174
  10.2 5.5 %collective-permute-start.8 = (f32[128,128]{1,0:T(8,128)S(1)}, f32[128,128]{1,0:T(8,128)S(1)}, u32[]{:S(2)}, u32[]{:S(2)}) collective-permute-start(f32[128,128]{1,0:T(8,128)S(1)} %get-tuple-element.113), channel_id=1, source_target_pairs={{0,2},{2,0},{4,6},{6,4},{8,10},{10,8},{12,14},{14,12},{16,18},{18,... | collective-permute-start | bytes 196616 | tf_op jit(solution)/shard_map/ppermute | solution.py:174
  11.3 9.5 %collective-permute-start.3 = (f32[128,128]{1,0:T(8,128)S(1)}, f32[128,128]{1,0:T(8,128)S(1)}, u32[]{:S(2)}, u32[]{:S(2)}) collective-permute-start(f32[128,128]{1,0:T(8,128)S(1)} %add_add_fusion.7), channel_id=1, source_target_pairs={{0,8},{2,10},{4,12},{6,14},{8,0},{10,2},{12,4},{14,6},{16,24},{18,... | collective-permute-start | bytes 196616 | tf_op jit(solution)/shard_map/ppermute | solution.py:174
  13.0 8.0 %collective-permute-start.4 = (f32[128,128]{1,0:T(8,128)S(1)}, f32[128,128]{1,0:T(8,128)S(1)}, u32[]{:S(2)}, u32[]{:S(2)}) collective-permute-start(f32[128,128]{1,0:T(8,128)S(1)} %add_add_fusion.7), channel_id=1, source_target_pairs={{0,24},{2,26},{4,28},{6,30},{8,16},{10,18},{12,20},{14,22},{16,8},... | collective-permute-start | bytes 196616 | tf_op jit(solution)/shard_map/ppermute | solution.py:174
  15.5 8.5 %collective-permute-start.5 = (f32[128,128]{1,0:T(8,128)S(1)}, f32[128,128]{1,0:T(8,128)S(1)}, u32[]{:S(2)}, u32[]{:S(2)}) collective-permute-start(f32[128,128]{1,0:T(8,128)S(1)} %add_add_fusion.7), channel_id=1, source_target_pairs={{0,16},{2,18},{4,20},{6,22},{8,24},{10,26},{12,28},{14,30},{16,0},... | collective-permute-start | bytes 196616 | tf_op jit(solution)/shard_map/ppermute | solution.py:174
  15.7 11.0 %collective-permute-start.12 = (f32[128,128]{1,0:T(8,128)S(1)}, f32[128,128]{1,0:T(8,128)S(1)}, u32[]{:S(2)}, u32[]{:S(2)}) collective-permute-start(f32[128,128]{1,0:T(8,128)S(1)} %add_add_fusion.5), channel_id=1, source_target_pairs={{0,8},{2,10},{4,12},{6,14},{8,0},{10,2},{12,4},{14,6},{16,24},{18,... | collective-permute-start | bytes 196616 | tf_op jit(solution)/shard_map/ppermute | solution.py:174
  17.5 10.1 %collective-permute-start.13 = (f32[128,128]{1,0:T(8,128)S(1)}, f32[128,128]{1,0:T(8,128)S(1)}, u32[]{:S(2)}, u32[]{:S(2)}) collective-permute-start(f32[128,128]{1,0:T(8,128)S(1)} %add_add_fusion.5), channel_id=1, source_target_pairs={{0,24},{2,26},{4,28},{6,30},{8,16},{10,18},{12,20},{14,22},{16,8},... | collective-permute-start | bytes 196616 | tf_op jit(solution)/shard_map/ppermute | solution.py:174
  20.9 6.7 %collective-permute-start.14 = (f32[128,128]{1,0:T(8,128)S(1)}, f32[128,128]{1,0:T(8,128)S(1)}, u32[]{:S(2)}, u32[]{:S(2)}) collective-permute-start(f32[128,128]{1,0:T(8,128)S(1)} %add_add_fusion.5), channel_id=1, source_target_pairs={{0,16},{2,18},{4,20},{6,22},{8,24},{10,26},{12,28},{14,30},{16,0},... | collective-permute-start | bytes 196616 | tf_op jit(solution)/shard_map/ppermute | solution.py:174
  24.0 6.4 %collective-permute-start.9 = (f32[128,128]{1,0:T(8,128)S(1)}, f32[128,128]{1,0:T(8,128)S(1)}, u32[]{:S(2)}, u32[]{:S(2)}) collective-permute-start(f32[128,128]{1,0:T(8,128)S(1)} %get-tuple-element.127), channel_id=1, source_target_pairs={{0,6},{2,4},{4,2},{6,0},{8,14},{10,12},{12,10},{14,8},{16,22},{18,... | collective-permute-start | bytes 196616 | tf_op jit(solution)/shard_map/ppermute | solution.py:174
  25.9 5.4 %collective-permute-start.10 = (f32[128,128]{1,0:T(8,128)S(1)}, f32[128,128]{1,0:T(8,128)S(1)}, u32[]{:S(2)}, u32[]{:S(2)}) collective-permute-start(f32[128,128]{1,0:T(8,128)S(1)} %get-tuple-element.128), channel_id=1, source_target_pairs={{0,4},{2,6},{4,0},{6,2},{8,12},{10,14},{12,8},{14,10},{16,20},{18,... | collective-permute-start | bytes 196616 | tf_op jit(solution)/shard_map/ppermute | solution.py:174
  27.7 7.2 %collective-permute-start.15 = (f32[128,128]{1,0:T(8,128)S(1)}, f32[128,128]{1,0:T(8,128)S(1)}, u32[]{:S(2)}, u32[]{:S(2)}) collective-permute-start(f32[128,128]{1,0:T(8,128)S(1)} %get-tuple-element.143), channel_id=1, source_target_pairs={{0,6},{2,4},{4,2},{6,0},{8,14},{10,12},{12,10},{14,8},{16,22},{18,... | collective-permute-start | bytes 196616 | tf_op jit(solution)/shard_map/ppermute | solution.py:174
  29.7 6.2 %collective-permute-start.16 = (f32[128,128]{1,0:T(8,128)S(1)}, f32[128,128]{1,0:T(8,128)S(1)}, u32[]{:S(2)}, u32[]{:S(2)}) collective-permute-start(f32[128,128]{1,0:T(8,128)S(1)} %get-tuple-element.144), channel_id=1, source_target_pairs={{0,4},{2,6},{4,0},{6,2},{8,12},{10,14},{12,8},{14,10},{16,20},{18,... | collective-permute-start | bytes 196616 | tf_op jit(solution)/shard_map/ppermute | solution.py:174
  30.5 5.4 %collective-permute-start.17 = (f32[128,128]{1,0:T(8,128)S(1)}, f32[128,128]{1,0:T(8,128)S(1)}, u32[]{:S(2)}, u32[]{:S(2)}) collective-permute-start(f32[128,128]{1,0:T(8,128)S(1)} %get-tuple-element.145), channel_id=1, source_target_pairs={{0,2},{2,0},{4,6},{6,4},{8,10},{10,8},{12,14},{14,12},{16,18},{18,... | collective-permute-start | bytes 196616 | tf_op jit(solution)/shard_map/ppermute | solution.py:174
  32.3 6.9 %collective-permute-start.18 = (f32[136,128]{1,0:T(8,128)S(1)}, f32[136,128]{1,0:T(8,128)S(1)}, u32[]{:S(2)}, u32[]{:S(2)}) collective-permute-start(f32[136,128]{1,0:T(8,128)S(1)} %get-tuple-element.155), channel_id=1, source_target_pairs={{0,6},{2,4},{4,2},{6,0},{8,14},{10,12},{12,10},{14,8},{16,22},{18,... | collective-permute-start | bytes 208904 | tf_op jit(solution)/shard_map/ppermute | solution.py:174
  34.1 6.0 %collective-permute-start.19 = (f32[136,128]{1,0:T(8,128)S(1)}, f32[136,128]{1,0:T(8,128)S(1)}, u32[]{:S(2)}, u32[]{:S(2)}) collective-permute-start(f32[136,128]{1,0:T(8,128)S(1)} %get-tuple-element.156), channel_id=1, source_target_pairs={{0,4},{2,6},{4,0},{6,2},{8,12},{10,14},{12,8},{14,10},{16,20},{18,... | collective-permute-start | bytes 208904 | tf_op jit(solution)/shard_map/ppermute | solution.py:174
  34.9 5.3 %collective-permute-start.20 = (f32[136,128]{1,0:T(8,128)S(1)}, f32[136,128]{1,0:T(8,128)S(1)}, u32[]{:S(2)}, u32[]{:S(2)}) collective-permute-start(f32[136,128]{1,0:T(8,128)S(1)} %get-tuple-element.157), channel_id=1, source_target_pairs={{0,2},{2,0},{4,6},{6,4},{8,10},{10,8},{12,14},{14,12},{16,18},{18,... | collective-permute-start | bytes 208904 | tf_op jit(solution)/shard_map/ppermute | solution.py:174
  36.6 6.2 %collective-permute-start.27 = (f32[136,128]{1,0:T(8,128)S(1)}, f32[136,128]{1,0:T(8,128)S(1)}, u32[]{:S(2)}, u32[]{:S(2)}) collective-permute-start(f32[136,128]{1,0:T(8,128)S(1)} %get-tuple-element.174), channel_id=1, source_target_pairs={{0,6},{2,4},{4,2},{6,0},{8,14},{10,12},{12,10},{14,8},{16,22},{18,... | collective-permute-start | bytes 208904 | tf_op jit(solution)/shard_map/ppermute | solution.py:174
  38.4 5.3 %collective-permute-start.28 = (f32[136,128]{1,0:T(8,128)S(1)}, f32[136,128]{1,0:T(8,128)S(1)}, u32[]{:S(2)}, u32[]{:S(2)}) collective-permute-start(f32[136,128]{1,0:T(8,128)S(1)} %get-tuple-element.175), channel_id=1, source_target_pairs={{0,4},{2,6},{4,0},{6,2},{8,12},{10,14},{12,8},{14,10},{16,20},{18,... | collective-permute-start | bytes 208904 | tf_op jit(solution)/shard_map/ppermute | solution.py:174
  40.2 7.1 %collective-permute-start.21 = (f32[136,128]{1,0:T(8,128)S(1)}, f32[136,128]{1,0:T(8,128)S(1)}, u32[]{:S(2)}, u32[]{:S(2)}) collective-permute-start(f32[136,128]{1,0:T(8,128)S(1)} %add_add_fusion.3), channel_id=1, source_target_pairs={{0,8},{2,10},{4,12},{6,14},{8,0},{10,2},{12,4},{14,6},{16,24},{18,... | collective-permute-start | bytes 208904 | tf_op jit(solution)/shard_map/ppermute | solution.py:174
  40.3 7.1 %collective-permute-start.22 = (f32[136,128]{1,0:T(8,128)S(1)}, f32[136,128]{1,0:T(8,128)S(1)}, u32[]{:S(2)}, u32[]{:S(2)}) collective-permute-start(f32[136,128]{1,0:T(8,128)S(1)} %add_add_fusion.3), channel_id=1, source_target_pairs={{0,24},{2,26},{4,28},{6,30},{8,16},{10,18},{12,20},{14,22},{16,8},... | collective-permute-start | bytes 208904 | tf_op jit(solution)/shard_map/ppermute | solution.py:174
  42.8 6.0 %collective-permute-start.23 = (f32[136,128]{1,0:T(8,128)S(1)}, f32[136,128]{1,0:T(8,128)S(1)}, u32[]{:S(2)}, u32[]{:S(2)}) collective-permute-start(f32[136,128]{1,0:T(8,128)S(1)} %add_add_fusion.3), channel_id=1, source_target_pairs={{0,16},{2,18},{4,20},{6,22},{8,24},{10,26},{12,28},{14,30},{16,0},... | collective-permute-start | bytes 208904 | tf_op jit(solution)/shard_map/ppermute | solution.py:174
  43.8 8.1 %collective-permute-start.30 = (f32[136,128]{1,0:T(8,128)S(1)}, f32[136,128]{1,0:T(8,128)S(1)}, u32[]{:S(2)}, u32[]{:S(2)}) collective-permute-start(f32[136,128]{1,0:T(8,128)S(1)} %add_add_fusion.1), channel_id=1, source_target_pairs={{0,8},{2,10},{4,12},{6,14},{8,0},{10,2},{12,4},{14,6},{16,24},{18,... | collective-permute-start | bytes 208904 | tf_op jit(solution)/shard_map/ppermute | solution.py:174
  45.1 7.4 %collective-permute-start.31 = (f32[136,128]{1,0:T(8,128)S(1)}, f32[136,128]{1,0:T(8,128)S(1)}, u32[]{:S(2)}, u32[]{:S(2)}) collective-permute-start(f32[136,128]{1,0:T(8,128)S(1)} %add_add_fusion.1), channel_id=1, source_target_pairs={{0,24},{2,26},{4,28},{6,30},{8,16},{10,18},{12,20},{14,22},{16,8},... | collective-permute-start | bytes 208904 | tf_op jit(solution)/shard_map/ppermute | solution.py:174
  47.3 5.7 %collective-permute-start.32 = (f32[136,128]{1,0:T(8,128)S(1)}, f32[136,128]{1,0:T(8,128)S(1)}, u32[]{:S(2)}, u32[]{:S(2)}) collective-permute-start(f32[136,128]{1,0:T(8,128)S(1)} %add_add_fusion.1), channel_id=1, source_target_pairs={{0,16},{2,18},{4,20},{6,22},{8,24},{10,26},{12,28},{14,30},{16,0},... | collective-permute-start | bytes 208904 | tf_op jit(solution)/shard_map/ppermute | solution.py:174
  48.9 7.1 %collective-permute-start.24 = (f32[136,128]{1,0:T(8,128)S(1)}, f32[136,128]{1,0:T(8,128)S(1)}, u32[]{:S(2)}, u32[]{:S(2)}) collective-permute-start(f32[136,128]{1,0:T(8,128)S(1)} %get-tuple-element.166), channel_id=1, source_target_pairs={{0,6},{2,4},{4,2},{6,0},{8,14},{10,12},{12,10},{14,8},{16,22},{18,... | collective-permute-start | bytes 208904 | tf_op jit(solution)/shard_map/ppermute | solution.py:174
  50.6 9.2 %collective-permute-start.25 = (f32[136,128]{1,0:T(8,128)S(1)}, f32[136,128]{1,0:T(8,128)S(1)}, u32[]{:S(2)}, u32[]{:S(2)}) collective-permute-start(f32[136,128]{1,0:T(8,128)S(1)} %get-tuple-element.167), channel_id=1, source_target_pairs={{0,4},{2,6},{4,0},{6,2},{8,12},{10,14},{12,8},{14,10},{16,20},{18,... | collective-permute-start | bytes 208904 | tf_op jit(solution)/shard_map/ppermute | solution.py:174
  51.9 7.9 %collective-permute-start.26 = (f32[136,128]{1,0:T(8,128)S(1)}, f32[136,128]{1,0:T(8,128)S(1)}, u32[]{:S(2)}, u32[]{:S(2)}) collective-permute-start(f32[136,128]{1,0:T(8,128)S(1)} %get-tuple-element.168), channel_id=1, source_target_pairs={{0,2},{2,0},{4,6},{6,4},{8,10},{10,8},{12,14},{14,12},{16,18},{18,... | collective-permute-start | bytes 208904 | tf_op jit(solution)/shard_map/ppermute | solution.py:174
  53.1 6.7 %collective-permute-start.33 = (f32[136,128]{1,0:T(8,128)S(1)}, f32[136,128]{1,0:T(8,128)S(1)}, u32[]{:S(2)}, u32[]{:S(2)}) collective-permute-start(f32[136,128]{1,0:T(8,128)S(1)} %get-tuple-element.185), channel_id=1, source_target_pairs={{0,6},{2,4},{4,2},{6,0},{8,14},{10,12},{12,10},{14,8},{16,22},{18,... | collective-permute-start | bytes 208904 | tf_op jit(solution)/shard_map/ppermute | solution.py:174
  54.5 5.3 %collective-permute-start.34 = (f32[136,128]{1,0:T(8,128)S(1)}, f32[136,128]{1,0:T(8,128)S(1)}, u32[]{:S(2)}, u32[]{:S(2)}) collective-permute-start(f32[136,128]{1,0:T(8,128)S(1)} %get-tuple-element.186), channel_id=1, source_target_pairs={{0,4},{2,6},{4,0},{6,2},{8,12},{10,14},{12,8},{14,10},{16,20},{18,... | collective-permute-start | bytes 208904 | tf_op jit(solution)/shard_map/ppermute | solution.py:174
  (10 other events, 85.6 us)

commit v17 on v14

--- a/solution.py
+++ b/solution.py
@@ -42,21 +42,24 @@
     return lax.broadcasted_iota(jnp.int32, shape, first) >= lax.broadcasted_iota(jnp.int32, shape, 1 - first)
 
 
-def delta_body(place_ref, key_ref, value_ref, *refs):
-    delta_refs, (key_here, value_here, sems) = refs[:HEADS], refs[HEADS:]
-    copies = []
+def delta_body(chain, place_ref, key_ref, value_ref, *refs):
+    delta_refs, scratch = refs[:GROUP], refs[GROUP:]
+    if scratch:
+        copies, *heres, sems = [], *scratch
+        for part in range(PARTS):
+            rows = pl.ds(part * PART_ROWS, PART_ROWS)
+            for side, (source, here) in enumerate(zip((key_ref, value_ref), heres)):
+                chunk = source.at[rows, pl.ds(chain * WIDE, WIDE)]
+                copies.append(pltpu.make_async_copy(chunk, here.at[rows], sems.at[part, side]))
+                copies[-1].start()
+        chain, (key_ref, value_ref) = 0, heres
     for part in range(PARTS):
         rows = pl.ds(part * PART_ROWS, PART_ROWS)
-        for side, (source, here) in enumerate(((key_ref, key_here), (value_ref, value_here))):
-            copies.append(pltpu.make_async_copy(source.at[rows], here.at[rows], sems.at[part, side]))
-            copies[-1].start()
-    for part in range(PARTS):
-        rows = pl.ds(part * PART_ROWS, PART_ROWS)
-        for copy in copies[2 * part : 2 * part + 2]:
+        for copy in copies[2 * part : 2 * part + 2] if scratch else ():
             copy.wait()
-        for at_head, delta_ref in enumerate(delta_refs):
-            at = own_columns(place_ref, ORDER[at_head % GROUP], at_head // GROUP)
-            delta = dot(key_here[rows, at], value_here[rows, at], TN)
+        for mask, delta_ref in zip(ORDER, delta_refs):
+            at = own_columns(place_ref, mask, chain)
+            delta = dot(key_ref[rows, at], value_ref[rows, at], TN)
             delta_ref[...] = delta if part == 0 else delta_ref[...] + delta
 
 
@@ -101,16 +104,13 @@
         value_part_ref[:, here] = dot(turned, grad_attn, NN)
 
 
-def final_body(place_ref, key_ref, value_ref, *refs):
-    part_refs, state_refs, (grad_key_ref, grad_value_ref) = refs[: 2 * CHAINS], refs[2 * CHAINS : -2], refs[-2:]
-    rows = pl.ds(pl.multiple_of(pl.program_id(0) * PART_ROWS, PART_ROWS), PART_ROWS)
-    for at_head, state_ref in enumerate(state_refs):
-        chain, mask = at_head // GROUP, ORDER[at_head % GROUP]
+def final_body(chain, place_ref, key_ref, value_ref, key_part_ref, value_part_ref, *refs):
+    state_refs, (grad_key_ref, grad_value_ref) = refs[:GROUP], refs[-2:]
+    for mask, state_ref in zip(ORDER, state_refs):
         at, here = own_columns(place_ref, mask, chain), own_columns(place_ref, mask)
         state = state_ref[:DH].astype(jnp.bfloat16)
-        key_part, value_part = part_refs[2 * chain][rows, here], part_refs[2 * chain + 1][rows, here]
-        grad_key_ref[:, at] = (key_part + dot(value_ref[rows, at], state, NT)).astype(jnp.bfloat16)
-        grad_value_ref[:, at] = (value_part + dot(key_ref[rows, at], state, NN)).astype(jnp.bfloat16)
+        grad_key_ref[:, here] = (key_part_ref[:, here] + dot(value_ref[:, at], state, NT)).astype(jnp.bfloat16)
+        grad_value_ref[:, here] = (value_part_ref[:, here] + dot(key_ref[:, at], state, NN)).astype(jnp.bfloat16)
 
 
 def gain_body(place_ref, *refs):
@@ -219,20 +219,25 @@
     unit = 2 * BLOCK * DH * DH * HEADS
 
     place = lax.axis_index("seq").astype(jnp.int32).reshape(1)
-    deltas = call(
-        delta_body,
-        [pl.BlockSpec(memory_space=pltpu.HBM)] * 2,
-        [short] * HEADS,
-        [square] * HEADS,
-        6 * unit,
-        "delta",
-        scratch=[pltpu.VMEM(flat, jnp.bfloat16)] * 2 + [pltpu.SemaphoreType.DMA((PARTS, 2))],
-    )(place, *[pltpu.with_memory_space_constraint(a, pltpu.HBM) for a in (key, value)])
-    chains = [slice(chain * GROUP, (chain + 1) * GROUP) for chain in range(CHAINS)]
+    near = [pltpu.with_memory_space_constraint(a, pltpu.HBM) for a in (key, value)]
+    deltas = [
+        call(
+            functools.partial(delta_body, chain),
+            [pl.BlockSpec(memory_space=pltpu.HBM) if chain == 0 else wide] * 2,
+            [short] * GROUP,
+            [square] * GROUP,
+            3 * unit,
+            "delta",
+            scratch=[pltpu.VMEM((BLOCK, WIDE), jnp.bfloat16)] * 2 + [pltpu.SemaphoreType.DMA((PARTS, 2))]
+            if chain == 0
+            else (),
+        )(place, *(near if chain == 0 else (key, value)))
+        for chain in range(CHAINS)
+    ]
     inner_call = call(
         lambda place_ref, *refs: inner_body(*refs), [wide] * 3, wide, full_float, 16 * unit, "inner"
     )
-    sums, inner = beside(inner_call, (place, query, key, value), *[plane_swap(deltas[chain]) for chain in chains])
+    sums, inner = beside(inner_call, (place, query, key, value), *[plane_swap(delta) for delta in deltas])
     states = [carried_in(held, total, False, place) for held, total in sums]
     attns, helds = [], []
     for chain in range(CHAINS):
@@ -260,20 +265,29 @@
 
     operands = [(place, query, key, value, attns[chain], *states[chain]) for chain in range(CHAINS)]
     sums, (grad_query, *parts) = beside(functools.partial(partial_call, 0), operands[0], *helds)
-    later = [piece for held, total in sums for piece in carried_in(held, total, True, place)]
-    grad_query, *rest = partial_call(1, *operands[1], grad_query)
-    parts += rest
+    later = [carried_in(held, total, True, place) for held, total in sums]
+    grad_query, *other_parts = partial_call(1, *operands[1], grad_query)
+
+    def final_call(chain, parts, grads=()):
+        return call(
+            functools.partial(final_body, chain),
+            [wide] * 2 + [half] * 2 + [tall] * GROUP + [pl.BlockSpec(memory_space=pl.ANY)] * len(grads),
+            [pl.BlockSpec((BLOCK, WIDE), lambda step: (0, chain))] * 2,
+            [full_low] * 2,
+            8 * unit,
+            "final",
+            aliases={5 + GROUP: 0, 6 + GROUP: 1} if grads else None,
+        )(place, key, value, *parts, *later[chain], *grads)
+
+    later[1], grads = lax.optimization_barrier((later[1], final_call(0, parts)))
     gain_terms = call(
         gain_body, [tall] * HEADS, whole(HEADS, DH), jax.ShapeDtypeStruct((HEADS, DH), jnp.float32), unit, "gain"
-    )(place, *later)
+    )(place, *later[0], *later[1])
     docs, mask = lax.axis_size("dp"), 1
     while mask < docs:
         gain_terms = gain_terms + lax.ppermute(gain_terms, "dp", [(d, d ^ mask) for d in range(docs)])
         mask *= 2
-    chunk = pl.BlockSpec((PART_ROWS, HEADS * DH), lambda step: (step, 0))
-    grad_key, grad_value = call(
-        final_body, [wide] * 2 + [half] * (2 * CHAINS) + [tall] * HEADS, [chunk] * 2, [full_low] * 2, 16 * unit, "final", steps=PARTS
-    )(place, key, value, *parts, *later)
+    grad_key, grad_value = final_call(1, other_parts, grads)
     grad_gain = gain_terms / math.sqrt(lax.axis_size("seq") * docs * BLOCK)
     return (
         grad_query.reshape(full),

time: 62.7 us -> 62.8 us (level)
  starting transfers between devices: 45.4 us -> 44 us
  waiting for transfers between devices: 5.74 us -> 6.63 us
  Pallas kernels: 9.81 us -> 10.5 us
    ppermute x32, starting transfers between devices: 45.4 us -> 44 us  [swap(): lax.ppermute(array, 'seq', [(s, s ^ mask) for s in range(lax.axis_size('s...]
    ppermute x32, waiting for transfers between devices: 5.74 us -> 6.57 us  [swap(): lax.ppermute(array, 'seq', [(s, s ^ mask) for s in range(lax.axis_size('s...]
    pallas_call x2 -> x4, Pallas kernels: 3.26 us -> 3.91 us  [the longest x2 2.2 us: final_call(): call(functools.partial(final_body, chain), [wide] * 2 + [half] * 2 + [tal...]
  transfers between devices with their start and end apart: 33 -> 33, of which waited for: 11 -> 12; matrix products, arithmetic and copies ran while one was open for 0% -> 0% of each run, Pallas kernels for 13% -> 14%
where the time goes in v17:
time: 62.8 us; the launch traced here: 62.6 us
  starting transfers between devices  44 us (70%)
  Pallas kernels  10.5 us (17%)
  waiting for transfers between devices  6.63 us (11%)
  between operations  0.81 us (1%)
  other arithmetic  0.75 us (1%)
    ppermute x32, starting transfers between devices, swap(): lax.ppermute(array, 'seq', [(s, s ^ mask) for s in range(lax.axis_size('s...  44 us
    ppermute x32, waiting for transfers between devices, swap(): lax.ppermute(array, 'seq', [(s, s ^ mask) for s in range(lax.axis_size('s...  6.57 us
    pallas_call x2, Pallas kernels, partial_call(): call(functools.partial(partial_body, chain), [wide] * 3 + [half] + [short...  3.83 us
    pallas_call x2, Pallas kernels, final_call(): call(functools.partial(final_body, chain), [wide] * 2 + [half] * 2 + [tal...  2.2 us
    pallas_call x2, Pallas kernels, local(): call(functools.partial(delta_body, chain), [pl.BlockSpec(memory_space=plt...  1.71 us
    pallas_call x2, Pallas kernels, local(): call(functools.partial(norm_body, chain), [wide, wide, wide, whole(1, HEA...  1.48 us
  transfers between devices with their start and end apart: 33, of which 12 were waited for; matrix products, arithmetic and copies ran while one was open for 0% of the time, Pallas kernels for 14%

profile of v17, /device:TPU:0, one launch (start us, length us, event | category | flops | bytes accessed | tf_op | source)
XLA Modules:
  0.0 62.6 jit_solution(2908871859507026935)
XLA Ops:
  0.7 1.4 %delta.3 = (f32[128,128]{1,0:T(8,128)S(1)}, f32[128,128]{1,0:T(8,128)S(1)}, f32[128,128]{1,0:T(8,128)S(1)}, f32[128,128]{1,0:T(8,128)S(1)}) custom-call(s32[1]{0:T(128)} %bitcast.place_ref, bf16[256,1024]{1,0:T(8,128)(2,1)} %bitcast.11, bf16[256,1024]{1,0:T(8,128)(2,1)} %bitcast.18), custom_call_target="tpu_custom_call" | custom-call | flops 201326592 | bytes 2097152 | tf_op jit(solution)/shard_map/delta/pallas_call | solution.py:224
  2.1 4.0 %collective-permute-start.3 = (f32[128,128]{1,0:T(8,128)S(1)}, f32[128,128]{1,0:T(8,128)S(1)}, u32[]{:S(2)}, u32[]{:S(2)}) collective-permute-start(f32[128,128]{1,0:T(8,128)S(1)} %get-tuple-element.86), channel_id=1, source_target_pairs={{0,6},{2,4},{4,2},{6,0},{8,14},{10,12},{12,10},{14,8},{16,22},{18,... | collective-permute-start | bytes 196616 | tf_op jit(solution)/shard_map/ppermute | solution.py:173
  7.0 2.9 %collective-permute-start = (f32[128,128]{1,0:T(8,128)S(1)}, f32[128,128]{1,0:T(8,128)S(1)}, u32[]{:S(2)}, u32[]{:S(2)}) collective-permute-start(f32[128,128]{1,0:T(8,128)S(1)} %get-tuple-element.82), channel_id=1, source_target_pairs={{0,6},{2,4},{4,2},{6,0},{8,14},{10,12},{12,10},{14,8},{16,22},{18,... | collective-permute-start | bytes 196616 | tf_op jit(solution)/shard_map/ppermute | solution.py:173
  11.4 1.6 %collective-permute-start.14 = (f32[128,128]{1,0:T(8,128)S(1)}, f32[128,128]{1,0:T(8,128)S(1)}, u32[]{:S(2)}, u32[]{:S(2)}) collective-permute-start(f32[128,128]{1,0:T(8,128)S(1)} %add_add_fusion.3), channel_id=1, source_target_pairs={{0,8},{2,10},{4,12},{6,14},{8,0},{10,2},{12,4},{14,6},{16,24},{18,... | collective-permute-start | bytes 196616 | tf_op jit(solution)/shard_map/ppermute | solution.py:173
  13.1 0.9 %inner.1.inner_ref = f32[256,1024]{1,0:T(8,128)S(1)} custom-call(s32[1]{0:T(128)} %bitcast.place_ref, bf16[256,1024]{1,0:T(8,128)(2,1)S(1)} %bitcast.27, bf16[256,1024]{1,0:T(8,128)(2,1)S(1)} %bitcast.13, bf16[256,1024]{1,0:T(8,128)(2,1)S(1)} %bitcast.20), custom_call_target="tpu_custom_call" | custom-call | flops 1073741824 | bytes 2097152 | tf_op jit(solution)/shard_map/inner/pallas_call | solution.py:183
  14.7 1.6 %collective-permute-start.6 = (f32[128,128]{1,0:T(8,128)S(1)}, f32[128,128]{1,0:T(8,128)S(1)}, u32[]{:S(2)}, u32[]{:S(2)}) collective-permute-start(f32[128,128]{1,0:T(8,128)S(1)} %add_add_fusion.2), channel_id=1, source_target_pairs={{0,8},{2,10},{4,12},{6,14},{8,0},{10,2},{12,4},{14,6},{16,24},{18,... | collective-permute-start | bytes 196616 | tf_op jit(solution)/shard_map/ppermute | solution.py:173
  16.4 2.7 %collective-permute-start.15 = (f32[128,128]{1,0:T(8,128)S(1)}, f32[128,128]{1,0:T(8,128)S(1)}, u32[]{:S(2)}, u32[]{:S(2)}) collective-permute-start(f32[128,128]{1,0:T(8,128)S(1)} %add.71), channel_id=1, source_target_pairs={{0,16},{2,18},{4,20},{6,22},{8,24},{10,26},{12,28},{14,30},{16,0},... | collective-permute-start | bytes 196616 | tf_op jit(solution)/shard_map/ppermute | solution.py:173
  19.0 2.7 %collective-permute-start.7 = (f32[128,128]{1,0:T(8,128)S(1)}, f32[128,128]{1,0:T(8,128)S(1)}, u32[]{:S(2)}, u32[]{:S(2)}) collective-permute-start(f32[128,128]{1,0:T(8,128)S(1)} %add.69), channel_id=1, source_target_pairs={{0,16},{2,18},{4,20},{6,22},{8,24},{10,26},{12,28},{14,30},{16,0},... | collective-permute-start | bytes 196616 | tf_op jit(solution)/shard_map/ppermute | solution.py:173
  21.7 1.2 %collective-permute-done.15.refs_2_ = f32[128,128]{1,0:T(8,128)S(1)} collective-permute-done((f32[128,128]{1,0:T(8,128)S(1)}, f32[128,128]{1,0:T(8,128)S(1)}, u32[]{:S(2)}, u32[]{:S(2)}) %collective-permute-start.15) | collective-permute-done | bytes 65568 | tf_op jit(solution)/shard_map/ppermute | solution.py:173
  23.1 1.5 %collective-permute-start.16 = (f32[128,128]{1,0:T(8,128)S(1)}, f32[128,128]{1,0:T(8,128)S(1)}, u32[]{:S(2)}, u32[]{:S(2)}) collective-permute-start(f32[128,128]{1,0:T(8,128)S(1)} %get-tuple-element.109), channel_id=1, source_target_pairs={{0,6},{2,4},{4,2},{6,0},{8,14},{10,12},{12,10},{14,8},{16,22},{18,... | collective-permute-start | bytes 196616 | tf_op jit(solution)/shard_map/ppermute | solution.py:173
  25.1 1.6 %collective-permute-start.18 = (f32[128,128]{1,0:T(8,128)S(1)}, f32[128,128]{1,0:T(8,128)S(1)}, u32[]{:S(2)}, u32[]{:S(2)}) collective-permute-start(f32[128,128]{1,0:T(8,128)S(1)} %get-tuple-element.111), channel_id=1, source_target_pairs={{0,2},{2,0},{4,6},{6,4},{8,10},{10,8},{12,14},{14,12},{16,18},{18,... | collective-permute-start | bytes 196616 | tf_op jit(solution)/shard_map/ppermute | solution.py:173
  27.3 2.3 %collective-permute-start.8 = (f32[128,128]{1,0:T(8,128)S(1)}, f32[128,128]{1,0:T(8,128)S(1)}, u32[]{:S(2)}, u32[]{:S(2)}) collective-permute-start(f32[128,128]{1,0:T(8,128)S(1)} %get-tuple-element.99), channel_id=1, source_target_pairs={{0,6},{2,4},{4,2},{6,0},{8,14},{10,12},{12,10},{14,8},{16,22},{18,... | collective-permute-start | bytes 196616 | tf_op jit(solution)/shard_map/ppermute | solution.py:173
  30.3 0.7 %norm.3 = (bf16[256,512]{1,0:T(8,128)(2,1)S(1)}, f32[136,128]{1,0:T(8,128)S(1)}, f32[136,128]{1,0:T(8,128)S(1)}, f32[136,128]{1,0:T(8,128)S(1)}, f32[136,128]{1,0:T(8,128)S(1)}) custom-call(s32[1]{0:T(128)} %bitcast.place_ref, bf16[256,1024]{1,0:T(8,128)(2,1)S(1)} %bitcast.28, bf16[256,1024]{1,0:T(8,128)(2,1)S(1)} %bitcast.25, ...), custom_call_target="tpu_custom_call" | custom-call | flops 536870912 | bytes 2097152 | tf_op jit(solution)/shard_map/norm/pallas_call | solution.py:244
  31.1 1.5 %collective-permute-start.19 = (f32[136,128]{1,0:T(8,128)S(1)}, f32[136,128]{1,0:T(8,128)S(1)}, u32[]{:S(2)}, u32[]{:S(2)}) collective-permute-start(f32[136,128]{1,0:T(8,128)S(1)} %get-tuple-element.113), channel_id=1, source_target_pairs={{0,6},{2,4},{4,2},{6,0},{8,14},{10,12},{12,10},{14,8},{16,22},{18,... | collective-permute-start | bytes 208904 | tf_op jit(solution)/shard_map/ppermute | solution.py:173
  32.6 1.0 %collective-permute-start.20 = (f32[136,128]{1,0:T(8,128)S(1)}, f32[136,128]{1,0:T(8,128)S(1)}, u32[]{:S(2)}, u32[]{:S(2)}) collective-permute-start(f32[136,128]{1,0:T(8,128)S(1)} %get-tuple-element.114), channel_id=1, source_target_pairs={{0,4},{2,6},{4,0},{6,2},{8,12},{10,14},{12,8},{14,10},{16,20},{18,... | collective-permute-start | bytes 208904 | tf_op jit(solution)/shard_map/ppermute | solution.py:173
  33.6 1.0 %collective-permute-start.21 = (f32[136,128]{1,0:T(8,128)S(1)}, f32[136,128]{1,0:T(8,128)S(1)}, u32[]{:S(2)}, u32[]{:S(2)}) collective-permute-start(f32[136,128]{1,0:T(8,128)S(1)} %get-tuple-element.115), channel_id=1, source_target_pairs={{0,2},{2,0},{4,6},{6,4},{8,10},{10,8},{12,14},{14,12},{16,18},{18,... | collective-permute-start | bytes 208904 | tf_op jit(solution)/shard_map/ppermute | solution.py:173
  35.5 1.7 %collective-permute-start.11 = (f32[136,128]{1,0:T(8,128)S(1)}, f32[136,128]{1,0:T(8,128)S(1)}, u32[]{:S(2)}, u32[]{:S(2)}) collective-permute-start(f32[136,128]{1,0:T(8,128)S(1)} %get-tuple-element.104), channel_id=1, source_target_pairs={{0,6},{2,4},{4,2},{6,0},{8,14},{10,12},{12,10},{14,8},{16,22},{18,... | collective-permute-start | bytes 208904 | tf_op jit(solution)/shard_map/ppermute | solution.py:173
  37.2 1.2 %collective-permute-start.12 = (f32[136,128]{1,0:T(8,128)S(1)}, f32[136,128]{1,0:T(8,128)S(1)}, u32[]{:S(2)}, u32[]{:S(2)}) collective-permute-start(f32[136,128]{1,0:T(8,128)S(1)} %get-tuple-element.105), channel_id=1, source_target_pairs={{0,4},{2,6},{4,0},{6,2},{8,12},{10,14},{12,8},{14,10},{16,20},{18,... | collective-permute-start | bytes 208904 | tf_op jit(solution)/shard_map/ppermute | solution.py:173
  39.7 1.9 %partial.2 = (bf16[256,1024]{1,0:T(8,128)(2,1)}, f32[256,512]{1,0:T(8,128)S(1)}, f32[256,512]{1,0:T(8,128)S(1)}) custom-call(s32[1]{0:T(128)} %bitcast.place_ref, bf16[256,1024]{1,0:T(8,128)(2,1)S(1)} %bitcast.30, bf16[256,1024]{1,0:T(8,128)(2,1)S(1)} %bitcast.14, bf16[256,1024]{1,0:T(8,128)(2,1)S(1)} %bitcast.21, ...), custom_call_target="tpu_custom_call" | custom-call | flops 1610612736 | bytes 2097152 | tf_op jit(solution)/shard_map/partial/pallas_call | solution.py:256
  41.7 1.1 %collective-permute-done.13.refs_6_ = f32[136,128]{1,0:T(8,128)S(1)} collective-permute-done((f32[136,128]{1,0:T(8,128)S(1)}, f32[136,128]{1,0:T(8,128)S(1)}, u32[]{:S(2)}, u32[]{:S(2)}) %collective-permute-start.13) | collective-permute-done | bytes 69664 | tf_op jit(solution)/shard_map/ppermute | solution.py:173
  43.2 0.8 %collective-permute-done.27.refs_1_ = f32[136,128]{1,0:T(8,128)S(1)} collective-permute-done((f32[136,128]{1,0:T(8,128)S(1)}, f32[136,128]{1,0:T(8,128)S(1)}, u32[]{:S(2)}, u32[]{:S(2)}) %collective-permute-start.27) | collective-permute-done | bytes 69664 | tf_op jit(solution)/shard_map/ppermute | solution.py:173
  44.0 2.4 %collective-permute-start.28 = (f32[136,128]{1,0:T(8,128)S(1)}, f32[136,128]{1,0:T(8,128)S(1)}, u32[]{:S(2)}, u32[]{:S(2)}) collective-permute-start(f32[136,128]{1,0:T(8,128)S(1)} %add.81), channel_id=1, source_target_pairs={{0,16},{2,18},{4,20},{6,22},{8,24},{10,26},{12,28},{14,30},{16,0},... | collective-permute-start | bytes 208904 | tf_op jit(solution)/shard_map/ppermute | solution.py:173
  47.1 2.2 %collective-permute-start.23 = (f32[136,128]{1,0:T(8,128)S(1)}, f32[136,128]{1,0:T(8,128)S(1)}, u32[]{:S(2)}, u32[]{:S(2)}) collective-permute-start(f32[136,128]{1,0:T(8,128)S(1)} %add.79), channel_id=1, source_target_pairs={{0,16},{2,18},{4,20},{6,22},{8,24},{10,26},{12,28},{14,30},{16,0},... | collective-permute-start | bytes 208904 | tf_op jit(solution)/shard_map/ppermute | solution.py:173
  50.1 1.0 %collective-permute-start.29 = (f32[136,128]{1,0:T(8,128)S(1)}, f32[136,128]{1,0:T(8,128)S(1)}, u32[]{:S(2)}, u32[]{:S(2)}) collective-permute-start(f32[136,128]{1,0:T(8,128)S(1)} %get-tuple-element.145), channel_id=1, source_target_pairs={{0,6},{2,4},{4,2},{6,0},{8,14},{10,12},{12,10},{14,8},{16,22},{18,... | collective-permute-start | bytes 208904 | tf_op jit(solution)/shard_map/ppermute | solution.py:173
  51.1 1.8 %collective-permute-start.30 = (f32[136,128]{1,0:T(8,128)S(1)}, f32[136,128]{1,0:T(8,128)S(1)}, u32[]{:S(2)}, u32[]{:S(2)}) collective-permute-start(f32[136,128]{1,0:T(8,128)S(1)} %get-tuple-element.146), channel_id=1, source_target_pairs={{0,4},{2,6},{4,0},{6,2},{8,12},{10,14},{12,8},{14,10},{16,20},{18,... | collective-permute-start | bytes 208904 | tf_op jit(solution)/shard_map/ppermute | solution.py:173
  52.9 0.8 %collective-permute-start.31 = (f32[136,128]{1,0:T(8,128)S(1)}, f32[136,128]{1,0:T(8,128)S(1)}, u32[]{:S(2)}, u32[]{:S(2)}) collective-permute-start(f32[136,128]{1,0:T(8,128)S(1)} %get-tuple-element.147), channel_id=1, source_target_pairs={{0,2},{2,0},{4,6},{6,4},{8,10},{10,8},{12,14},{14,12},{16,18},{18,... | collective-permute-start | bytes 208904 | tf_op jit(solution)/shard_map/ppermute | solution.py:173
  53.8 1.0 %collective-permute-start.24 = (f32[136,128]{1,0:T(8,128)S(1)}, f32[136,128]{1,0:T(8,128)S(1)}, u32[]{:S(2)}, u32[]{:S(2)}) collective-permute-start(f32[136,128]{1,0:T(8,128)S(1)} %get-tuple-element.138), channel_id=1, source_target_pairs={{0,6},{2,4},{4,2},{6,0},{8,14},{10,12},{12,10},{14,8},{16,22},{18,... | collective-permute-start | bytes 208904 | tf_op jit(solution)/shard_map/ppermute | solution.py:173
  54.8 1.8 %collective-permute-start.25 = (f32[136,128]{1,0:T(8,128)S(1)}, f32[136,128]{1,0:T(8,128)S(1)}, u32[]{:S(2)}, u32[]{:S(2)}) collective-permute-start(f32[136,128]{1,0:T(8,128)S(1)} %get-tuple-element.139), channel_id=1, source_target_pairs={{0,4},{2,6},{4,0},{6,2},{8,12},{10,14},{12,8},{14,10},{16,20},{18,... | collective-permute-start | bytes 208904 | tf_op jit(solution)/shard_map/ppermute | solution.py:173
  56.6 0.8 %collective-permute-start.26 = (f32[136,128]{1,0:T(8,128)S(1)}, f32[136,128]{1,0:T(8,128)S(1)}, u32[]{:S(2)}, u32[]{:S(2)}) collective-permute-start(f32[136,128]{1,0:T(8,128)S(1)} %get-tuple-element.140), channel_id=1, source_target_pairs={{0,2},{2,0},{4,6},{6,4},{8,10},{10,8},{12,14},{14,12},{16,18},{18,... | collective-permute-start | bytes 208904 | tf_op jit(solution)/shard_map/ppermute | solution.py:173
  57.3 1.9 %partial.3 = (bf16[256,1024]{1,0:T(8,128)(2,1)}, f32[256,512]{1,0:T(8,128)S(1)}, f32[256,512]{1,0:T(8,128)S(1)}) custom-call(s32[1]{0:T(128)} %bitcast.place_ref, bf16[256,1024]{1,0:T(8,128)(2,1)S(1)} %bitcast.31, bf16[256,1024]{1,0:T(8,128)(2,1)S(1)} %bitcast.15, bf16[256,1024]{1,0:T(8,128)(2,1)S(1)} %bitcast.22, ...), custom_call_target="tpu_custom_call", output_to_operand_aliasing={{0}: (9, {})} | custom-call | flops 1610612736 | bytes 2097152 | tf_op jit(solution)/shard_map/partial/pallas_call | solution.py:256
  59.3 1.1 %final.2 = (bf16[256,1024]{1,0:T(8,128)(2,1)}, bf16[256,1024]{1,0:T(8,128)(2,1)}) custom-call(s32[1]{0:T(128)} %bitcast.place_ref, bf16[256,1024]{1,0:T(8,128)(2,1)S(1)} %bitcast.16, bf16[256,1024]{1,0:T(8,128)(2,1)S(1)} %bitcast.23, f32[256,512]{1,0:T(8,128)S(1)} %get-tuple-element.141.key_part_ref, f32[256,512]{1,0:T(8,128)S(1)} %get-tuple-element.142.value_part_ref, ...), custom_call_target="tpu_custom_call" | custom-call | flops 536870912 | bytes 2097152 | tf_op jit(solution)/shard_map/final/pallas_call | solution.py:272
  60.9 1.1 %final.3 = (bf16[256,1024]{1,0:T(8,128)(2,1)}, bf16[256,1024]{1,0:T(8,128)(2,1)}) custom-call(s32[1]{0:T(128)} %bitcast.place_ref, bf16[256,1024]{1,0:T(8,128)(2,1)S(1)} %bitcast.17, bf16[256,1024]{1,0:T(8,128)(2,1)S(1)} %bitcast.24, f32[256,512]{1,0:T(8,128)S(1)} %get-tuple-element.131.key_part_ref, ...), custom_call_target="tpu_custom_call", output_to_operand_aliasing={{0}: (9, {}), {1}: (10, {})} | custom-call | flops 536870912 | bytes 2097152 | tf_op jit(solution)/shard_map/final/pallas_call | solution.py:272
  (71 shorter events, 10.6 us)
Async XLA Ops:
  2.1 8.3 %collective-permute-start.3 = (f32[128,128]{1,0:T(8,128)S(1)}, f32[128,128]{1,0:T(8,128)S(1)}, u32[]{:S(2)}, u32[]{:S(2)}) collective-permute-start(f32[128,128]{1,0:T(8,128)S(1)} %get-tuple-element.86), channel_id=1, source_target_pairs={{0,6},{2,4},{4,2},{6,0},{8,14},{10,12},{12,10},{14,8},{16,22},{18,... | collective-permute-start | bytes 196616 | tf_op jit(solution)/shard_map/ppermute | solution.py:173
  6.1 5.0 %collective-permute-start.4 = (f32[128,128]{1,0:T(8,128)S(1)}, f32[128,128]{1,0:T(8,128)S(1)}, u32[]{:S(2)}, u32[]{:S(2)}) collective-permute-start(f32[128,128]{1,0:T(8,128)S(1)} %get-tuple-element.87), channel_id=1, source_target_pairs={{0,4},{2,6},{4,0},{6,2},{8,12},{10,14},{12,8},{14,10},{16,20},{18,... | collective-permute-start | bytes 196616 | tf_op jit(solution)/shard_map/ppermute | solution.py:173
  6.6 4.8 %collective-permute-start.5 = (f32[128,128]{1,0:T(8,128)S(1)}, f32[128,128]{1,0:T(8,128)S(1)}, u32[]{:S(2)}, u32[]{:S(2)}) collective-permute-start(f32[128,128]{1,0:T(8,128)S(1)} %get-tuple-element.88), channel_id=1, source_target_pairs={{0,2},{2,0},{4,6},{6,4},{8,10},{10,8},{12,14},{14,12},{16,18},{18,... | collective-permute-start | bytes 196616 | tf_op jit(solution)/shard_map/ppermute | solution.py:173
  7.0 7.0 %collective-permute-start = (f32[128,128]{1,0:T(8,128)S(1)}, f32[128,128]{1,0:T(8,128)S(1)}, u32[]{:S(2)}, u32[]{:S(2)}) collective-permute-start(f32[128,128]{1,0:T(8,128)S(1)} %get-tuple-element.82), channel_id=1, source_target_pairs={{0,6},{2,4},{4,2},{6,0},{8,14},{10,12},{12,10},{14,8},{16,22},{18,... | collective-permute-start | bytes 196616 | tf_op jit(solution)/shard_map/ppermute | solution.py:173
  9.9 4.3 %collective-permute-start.1 = (f32[128,128]{1,0:T(8,128)S(1)}, f32[128,128]{1,0:T(8,128)S(1)}, u32[]{:S(2)}, u32[]{:S(2)}) collective-permute-start(f32[128,128]{1,0:T(8,128)S(1)} %get-tuple-element.83), channel_id=1, source_target_pairs={{0,4},{2,6},{4,0},{6,2},{8,12},{10,14},{12,8},{14,10},{16,20},{18,... | collective-permute-start | bytes 196616 | tf_op jit(solution)/shard_map/ppermute | solution.py:173
  10.4 4.3 %collective-permute-start.2 = (f32[128,128]{1,0:T(8,128)S(1)}, f32[128,128]{1,0:T(8,128)S(1)}, u32[]{:S(2)}, u32[]{:S(2)}) collective-permute-start(f32[128,128]{1,0:T(8,128)S(1)} %get-tuple-element.84), channel_id=1, source_target_pairs={{0,2},{2,0},{4,6},{6,4},{8,10},{10,8},{12,14},{14,12},{16,18},{18,... | collective-permute-start | bytes 196616 | tf_op jit(solution)/shard_map/ppermute | solution.py:173
  11.4 4.9 %collective-permute-start.14 = (f32[128,128]{1,0:T(8,128)S(1)}, f32[128,128]{1,0:T(8,128)S(1)}, u32[]{:S(2)}, u32[]{:S(2)}) collective-permute-start(f32[128,128]{1,0:T(8,128)S(1)} %add_add_fusion.3), channel_id=1, source_target_pairs={{0,8},{2,10},{4,12},{6,14},{8,0},{10,2},{12,4},{14,6},{16,24},{18,... | collective-permute-start | bytes 196616 | tf_op jit(solution)/shard_map/ppermute | solution.py:173
  14.7 4.3 %collective-permute-start.6 = (f32[128,128]{1,0:T(8,128)S(1)}, f32[128,128]{1,0:T(8,128)S(1)}, u32[]{:S(2)}, u32[]{:S(2)}) collective-permute-start(f32[128,128]{1,0:T(8,128)S(1)} %add_add_fusion.2), channel_id=1, source_target_pairs={{0,8},{2,10},{4,12},{6,14},{8,0},{10,2},{12,4},{14,6},{16,24},{18,... | collective-permute-start | bytes 196616 | tf_op jit(solution)/shard_map/ppermute | solution.py:173
  16.4 6.6 %collective-permute-start.15 = (f32[128,128]{1,0:T(8,128)S(1)}, f32[128,128]{1,0:T(8,128)S(1)}, u32[]{:S(2)}, u32[]{:S(2)}) collective-permute-start(f32[128,128]{1,0:T(8,128)S(1)} %add.71), channel_id=1, source_target_pairs={{0,16},{2,18},{4,20},{6,22},{8,24},{10,26},{12,28},{14,30},{16,0},... | collective-permute-start | bytes 196616 | tf_op jit(solution)/shard_map/ppermute | solution.py:173
  19.0 7.6 %collective-permute-start.7 = (f32[128,128]{1,0:T(8,128)S(1)}, f32[128,128]{1,0:T(8,128)S(1)}, u32[]{:S(2)}, u32[]{:S(2)}) collective-permute-start(f32[128,128]{1,0:T(8,128)S(1)} %add.69), channel_id=1, source_target_pairs={{0,16},{2,18},{4,20},{6,22},{8,24},{10,26},{12,28},{14,30},{16,0},... | collective-permute-start | bytes 196616 | tf_op jit(solution)/shard_map/ppermute | solution.py:173
  23.1 6.5 %collective-permute-start.16 = (f32[128,128]{1,0:T(8,128)S(1)}, f32[128,128]{1,0:T(8,128)S(1)}, u32[]{:S(2)}, u32[]{:S(2)}) collective-permute-start(f32[128,128]{1,0:T(8,128)S(1)} %get-tuple-element.109), channel_id=1, source_target_pairs={{0,6},{2,4},{4,2},{6,0},{8,14},{10,12},{12,10},{14,8},{16,22},{18,... | collective-permute-start | bytes 196616 | tf_op jit(solution)/shard_map/ppermute | solution.py:173
  24.6 5.7 %collective-permute-start.17 = (f32[128,128]{1,0:T(8,128)S(1)}, f32[128,128]{1,0:T(8,128)S(1)}, u32[]{:S(2)}, u32[]{:S(2)}) collective-permute-start(f32[128,128]{1,0:T(8,128)S(1)} %get-tuple-element.110), channel_id=1, source_target_pairs={{0,4},{2,6},{4,0},{6,2},{8,12},{10,14},{12,8},{14,10},{16,20},{18,... | collective-permute-start | bytes 196616 | tf_op jit(solution)/shard_map/ppermute | solution.py:173
  25.1 5.2 %collective-permute-start.18 = (f32[128,128]{1,0:T(8,128)S(1)}, f32[128,128]{1,0:T(8,128)S(1)}, u32[]{:S(2)}, u32[]{:S(2)}) collective-permute-start(f32[128,128]{1,0:T(8,128)S(1)} %get-tuple-element.111), channel_id=1, source_target_pairs={{0,2},{2,0},{4,6},{6,4},{8,10},{10,8},{12,14},{14,12},{16,18},{18,... | collective-permute-start | bytes 196616 | tf_op jit(solution)/shard_map/ppermute | solution.py:173
  26.7 6.9 %collective-permute-start.10 = (f32[128,128]{1,0:T(8,128)S(1)}, f32[128,128]{1,0:T(8,128)S(1)}, u32[]{:S(2)}, u32[]{:S(2)}) collective-permute-start(f32[128,128]{1,0:T(8,128)S(1)} %get-tuple-element.101), channel_id=1, source_target_pairs={{0,2},{2,0},{4,6},{6,4},{8,10},{10,8},{12,14},{14,12},{16,18},{18,... | collective-permute-start | bytes 196616 | tf_op jit(solution)/shard_map/ppermute | solution.py:173
  27.3 7.4 %collective-permute-start.8 = (f32[128,128]{1,0:T(8,128)S(1)}, f32[128,128]{1,0:T(8,128)S(1)}, u32[]{:S(2)}, u32[]{:S(2)}) collective-permute-start(f32[128,128]{1,0:T(8,128)S(1)} %get-tuple-element.99), channel_id=1, source_target_pairs={{0,6},{2,4},{4,2},{6,0},{8,14},{10,12},{12,10},{14,8},{16,22},{18,... | collective-permute-start | bytes 196616 | tf_op jit(solution)/shard_map/ppermute | solution.py:173
  29.6 5.2 %collective-permute-start.9 = (f32[128,128]{1,0:T(8,128)S(1)}, f32[128,128]{1,0:T(8,128)S(1)}, u32[]{:S(2)}, u32[]{:S(2)}) collective-permute-start(f32[128,128]{1,0:T(8,128)S(1)} %get-tuple-element.100), channel_id=1, source_target_pairs={{0,4},{2,6},{4,0},{6,2},{8,12},{10,14},{12,8},{14,10},{16,20},{18,... | collective-permute-start | bytes 196616 | tf_op jit(solution)/shard_map/ppermute | solution.py:173
  31.1 7.3 %collective-permute-start.19 = (f32[136,128]{1,0:T(8,128)S(1)}, f32[136,128]{1,0:T(8,128)S(1)}, u32[]{:S(2)}, u32[]{:S(2)}) collective-permute-start(f32[136,128]{1,0:T(8,128)S(1)} %get-tuple-element.113), channel_id=1, source_target_pairs={{0,6},{2,4},{4,2},{6,0},{8,14},{10,12},{12,10},{14,8},{16,22},{18,... | collective-permute-start | bytes 208904 | tf_op jit(solution)/shard_map/ppermute | solution.py:173
  32.6 6.5 %collective-permute-start.20 = (f32[136,128]{1,0:T(8,128)S(1)}, f32[136,128]{1,0:T(8,128)S(1)}, u32[]{:S(2)}, u32[]{:S(2)}) collective-permute-start(f32[136,128]{1,0:T(8,128)S(1)} %get-tuple-element.114), channel_id=1, source_target_pairs={{0,4},{2,6},{4,0},{6,2},{8,12},{10,14},{12,8},{14,10},{16,20},{18,... | collective-permute-start | bytes 208904 | tf_op jit(solution)/shard_map/ppermute | solution.py:173
  33.6 5.5 %collective-permute-start.21 = (f32[136,128]{1,0:T(8,128)S(1)}, f32[136,128]{1,0:T(8,128)S(1)}, u32[]{:S(2)}, u32[]{:S(2)}) collective-permute-start(f32[136,128]{1,0:T(8,128)S(1)} %get-tuple-element.115), channel_id=1, source_target_pairs={{0,2},{2,0},{4,6},{6,4},{8,10},{10,8},{12,14},{14,12},{16,18},{18,... | collective-permute-start | bytes 208904 | tf_op jit(solution)/shard_map/ppermute | solution.py:173
  35.5 6.1 %collective-permute-start.11 = (f32[136,128]{1,0:T(8,128)S(1)}, f32[136,128]{1,0:T(8,128)S(1)}, u32[]{:S(2)}, u32[]{:S(2)}) collective-permute-start(f32[136,128]{1,0:T(8,128)S(1)} %get-tuple-element.104), channel_id=1, source_target_pairs={{0,6},{2,4},{4,2},{6,0},{8,14},{10,12},{12,10},{14,8},{16,22},{18,... | collective-permute-start | bytes 208904 | tf_op jit(solution)/shard_map/ppermute | solution.py:173
  37.2 4.5 %collective-permute-start.12 = (f32[136,128]{1,0:T(8,128)S(1)}, f32[136,128]{1,0:T(8,128)S(1)}, u32[]{:S(2)}, u32[]{:S(2)}) collective-permute-start(f32[136,128]{1,0:T(8,128)S(1)} %get-tuple-element.105), channel_id=1, source_target_pairs={{0,4},{2,6},{4,0},{6,2},{8,12},{10,14},{12,8},{14,10},{16,20},{18,... | collective-permute-start | bytes 208904 | tf_op jit(solution)/shard_map/ppermute | solution.py:173
  38.4 4.3 %collective-permute-start.13 = (f32[136,128]{1,0:T(8,128)S(1)}, f32[136,128]{1,0:T(8,128)S(1)}, u32[]{:S(2)}, u32[]{:S(2)}) collective-permute-start(f32[136,128]{1,0:T(8,128)S(1)} %get-tuple-element.106), channel_id=1, source_target_pairs={{0,2},{2,0},{4,6},{6,4},{8,10},{10,8},{12,14},{14,12},{16,18},{18,... | collective-permute-start | bytes 208904 | tf_op jit(solution)/shard_map/ppermute | solution.py:173
  39.1 4.9 %collective-permute-start.27 = (f32[136,128]{1,0:T(8,128)S(1)}, f32[136,128]{1,0:T(8,128)S(1)}, u32[]{:S(2)}, u32[]{:S(2)}) collective-permute-start(f32[136,128]{1,0:T(8,128)S(1)} %add_add_fusion.1), channel_id=1, source_target_pairs={{0,8},{2,10},{4,12},{6,14},{8,0},{10,2},{12,4},{14,6},{16,24},{18,... | collective-permute-start | bytes 208904 | tf_op jit(solution)/shard_map/ppermute | solution.py:173
  42.7 4.4 %collective-permute-start.22 = (f32[136,128]{1,0:T(8,128)S(1)}, f32[136,128]{1,0:T(8,128)S(1)}, u32[]{:S(2)}, u32[]{:S(2)}) collective-permute-start(f32[136,128]{1,0:T(8,128)S(1)} %add_add_fusion), channel_id=1, source_target_pairs={{0,8},{2,10},{4,12},{6,14},{8,0},{10,2},{12,4},{14,6},{16,24},{18,... | collective-permute-start | bytes 208904 | tf_op jit(solution)/shard_map/ppermute | solution.py:173
  44.0 6.0 %collective-permute-start.28 = (f32[136,128]{1,0:T(8,128)S(1)}, f32[136,128]{1,0:T(8,128)S(1)}, u32[]{:S(2)}, u32[]{:S(2)}) collective-permute-start(f32[136,128]{1,0:T(8,128)S(1)} %add.81), channel_id=1, source_target_pairs={{0,16},{2,18},{4,20},{6,22},{8,24},{10,26},{12,28},{14,30},{16,0},... | collective-permute-start | bytes 208904 | tf_op jit(solution)/shard_map/ppermute | solution.py:173
  47.1 6.5 %collective-permute-start.23 = (f32[136,128]{1,0:T(8,128)S(1)}, f32[136,128]{1,0:T(8,128)S(1)}, u32[]{:S(2)}, u32[]{:S(2)}) collective-permute-start(f32[136,128]{1,0:T(8,128)S(1)} %add.79), channel_id=1, source_target_pairs={{0,16},{2,18},{4,20},{6,22},{8,24},{10,26},{12,28},{14,30},{16,0},... | collective-permute-start | bytes 208904 | tf_op jit(solution)/shard_map/ppermute | solution.py:173
  50.1 6.5 %collective-permute-start.29 = (f32[136,128]{1,0:T(8,128)S(1)}, f32[136,128]{1,0:T(8,128)S(1)}, u32[]{:S(2)}, u32[]{:S(2)}) collective-permute-start(f32[136,128]{1,0:T(8,128)S(1)} %get-tuple-element.145), channel_id=1, source_target_pairs={{0,6},{2,4},{4,2},{6,0},{8,14},{10,12},{12,10},{14,8},{16,22},{18,... | collective-permute-start | bytes 208904 | tf_op jit(solution)/shard_map/ppermute | solution.py:173
  51.1 8.2 %collective-permute-start.30 = (f32[136,128]{1,0:T(8,128)S(1)}, f32[136,128]{1,0:T(8,128)S(1)}, u32[]{:S(2)}, u32[]{:S(2)}) collective-permute-start(f32[136,128]{1,0:T(8,128)S(1)} %get-tuple-element.146), channel_id=1, source_target_pairs={{0,4},{2,6},{4,0},{6,2},{8,12},{10,14},{12,8},{14,10},{16,20},{18,... | collective-permute-start | bytes 208904 | tf_op jit(solution)/shard_map/ppermute | solution.py:173
  52.9 6.4 %collective-permute-start.31 = (f32[136,128]{1,0:T(8,128)S(1)}, f32[136,128]{1,0:T(8,128)S(1)}, u32[]{:S(2)}, u32[]{:S(2)}) collective-permute-start(f32[136,128]{1,0:T(8,128)S(1)} %get-tuple-element.147), channel_id=1, source_target_pairs={{0,2},{2,0},{4,6},{6,4},{8,10},{10,8},{12,14},{14,12},{16,18},{18,... | collective-permute-start | bytes 208904 | tf_op jit(solution)/shard_map/ppermute | solution.py:173
  53.8 6.6 %collective-permute-start.24 = (f32[136,128]{1,0:T(8,128)S(1)}, f32[136,128]{1,0:T(8,128)S(1)}, u32[]{:S(2)}, u32[]{:S(2)}) collective-permute-start(f32[136,128]{1,0:T(8,128)S(1)} %get-tuple-element.138), channel_id=1, source_target_pairs={{0,6},{2,4},{4,2},{6,0},{8,14},{10,12},{12,10},{14,8},{16,22},{18,... | collective-permute-start | bytes 208904 | tf_op jit(solution)/shard_map/ppermute | solution.py:173
  54.8 5.6 %collective-permute-start.25 = (f32[136,128]{1,0:T(8,128)S(1)}, f32[136,128]{1,0:T(8,128)S(1)}, u32[]{:S(2)}, u32[]{:S(2)}) collective-permute-start(f32[136,128]{1,0:T(8,128)S(1)} %get-tuple-element.139), channel_id=1, source_target_pairs={{0,4},{2,6},{4,0},{6,2},{8,12},{10,14},{12,8},{14,10},{16,20},{18,... | collective-permute-start | bytes 208904 | tf_op jit(solution)/shard_map/ppermute | solution.py:173
  56.6 4.3 %collective-permute-start.26 = (f32[136,128]{1,0:T(8,128)S(1)}, f32[136,128]{1,0:T(8,128)S(1)}, u32[]{:S(2)}, u32[]{:S(2)}) collective-permute-start(f32[136,128]{1,0:T(8,128)S(1)} %get-tuple-element.140), channel_id=1, source_target_pairs={{0,2},{2,0},{4,6},{6,4},{8,10},{10,8},{12,14},{14,12},{16,18},{18,... | collective-permute-start | bytes 208904 | tf_op jit(solution)/shard_map/ppermute | solution.py:173
  (6 other events, 30.2 us)

commit v18 on v17

--- a/solution.py
+++ b/solution.py
@@ -72,8 +72,10 @@
 
 
 def norm_body(chain, place_ref, query_ref, grad_ref, inner_ref, gain_ref, *refs):
-    state_refs, (attn_ref, *delta_refs) = refs[:GROUP], refs[GROUP:]
-    for mask, state_ref, delta_ref in zip(ORDER, state_refs, delta_refs):
+    state_refs, (attn_ref, *delta_refs) = refs[:GROUP], refs[-GROUP - 1 - (chain == 0) :]
+    if chain == 0:
+        *delta_refs, terms_ref = delta_refs
+    for slot, (mask, state_ref, delta_ref) in enumerate(zip(ORDER, state_refs, delta_refs)):
         at = own_columns(place_ref, mask, chain)
         query = query_ref[:, at]
         attn = inner_ref[:, at] + dot(query, state_ref[...].astype(jnp.bfloat16), NN)
@@ -86,7 +88,12 @@
         grad_attn = ((gain * cotangent - normed * shared) * per_root).astype(jnp.bfloat16)
         attn_ref[:, own_columns(place_ref, mask)] = grad_attn
         delta_ref[:DH] = dot(query, grad_attn, TN)
-        delta_ref[DH:] = jnp.broadcast_to(jnp.sum(product, axis=0, keepdims=True), (GAIN_ROWS, DH))
+        terms = jnp.sum(product, axis=0, keepdims=True)
+        if chain == 0:
+            terms_ref[slot : slot + 1] = terms
+        else:
+            delta_ref[DH:] = jnp.broadcast_to(terms, (GAIN_ROWS, DH))
+            delta_ref[DH + 1 : DH + 2] = refs[GROUP][slot : slot + 1]
 
 
 def partial_body(chain, place_ref, query_ref, key_ref, value_ref, attn_ref, *refs):
@@ -114,9 +121,11 @@
 
 
 def gain_body(place_ref, *refs):
-    for at_head, state_ref in enumerate(refs[:-1]):
-        row = (at_head // GROUP) * GROUP + (place_ref[0] & (GROUP - 1) ^ ORDER[at_head % GROUP])
-        refs[-1][pl.ds(row, 1), :] = state_ref[DH : DH + 1]
+    for mask, state_ref in zip(ORDER, refs[:-1]):
+        member = place_ref[0] & (GROUP - 1) ^ mask
+        for chain in range(CHAINS):
+            row = DH + CHAINS - 1 - chain
+            refs[-1][pl.ds(chain * GROUP + member, 1), :] = state_ref[row : row + 1]
 
 
 def prefix_body(reverse, masks, place_ref, *refs):
@@ -239,18 +248,21 @@
     )
     sums, inner = beside(inner_call, (place, query, key, value), *[plane_swap(delta) for delta in deltas])
     states = [carried_in(held, total, False, place) for held, total in sums]
-    attns, helds = [], []
+    attns, helds, terms = [], [], ()
     for chain in range(CHAINS):
+        size, spec = (square, short) if chain == 0 else (taller, tall)
+        extra = [] if chain else [jax.ShapeDtypeStruct((GROUP, DH), jnp.float32)]
         attn, *deltas = call(
             functools.partial(norm_body, chain),
-            [wide, wide, wide, whole(1, HEADS * DH)] + [short] * GROUP,
-            [half] + [tall] * GROUP,
-            [half_low] + [taller] * GROUP,
+            [wide, wide, wide, whole(1, HEADS * DH)] + [short] * GROUP + [whole(GROUP, DH)] * chain,
+            [half] + [spec] * GROUP + [whole(*one.shape) for one in extra],
+            [half_low] + [size] * GROUP + extra,
             8 * unit,
             "norm",
-        )(place, query, grad, inner, gain, *states[chain])
+        )(place, query, grad, inner, gain, *states[chain], *terms)
         attns.append(attn)
-        helds.append(plane_swap(deltas))
+        helds.append(plane_swap(deltas[:GROUP]))
+        terms = deltas[GROUP:]
 
     def partial_call(chain, *operands):
         return call(
@@ -271,7 +283,7 @@
     def final_call(chain, parts, grads=()):
         return call(
             functools.partial(final_body, chain),
-            [wide] * 2 + [half] * 2 + [tall] * GROUP + [pl.BlockSpec(memory_space=pl.ANY)] * len(grads),
+            [wide] * 2 + [half] * 2 + [tall if chain else short] * GROUP + [pl.BlockSpec(memory_space=pl.ANY)] * len(grads),
             [pl.BlockSpec((BLOCK, WIDE), lambda step: (0, chain))] * 2,
             [full_low] * 2,
             8 * unit,
@@ -281,8 +293,8 @@
 
     later[1], grads = lax.optimization_barrier((later[1], final_call(0, parts)))
     gain_terms = call(
-        gain_body, [tall] * HEADS, whole(HEADS, DH), jax.ShapeDtypeStruct((HEADS, DH), jnp.float32), unit, "gain"
-    )(place, *later[0], *later[1])
+        gain_body, [tall] * GROUP, whole(HEADS, DH), jax.ShapeDtypeStruct((HEADS, DH), jnp.float32), unit, "gain"
+    )(place, *later[1])
     docs, mask = lax.axis_size("dp"), 1
     while mask < docs:
         gain_terms = gain_terms + lax.ppermute(gain_terms, "dp", [(d, d ^ mask) for d in range(docs)])

time: 62.8 us -> 62.7 us (level)
  no operation moved by 1% of the time
where the time goes in v18:
time: 62.7 us; the launch traced here: 62.5 us
  starting transfers between devices  43.9 us (70%)
  Pallas kernels  10.5 us (17%)
  waiting for transfers between devices  6.56 us (10%)
  between operations  0.81 us (1%)
  other arithmetic  0.74 us (1%)
    ppermute x32, starting transfers between devices, swap(): lax.ppermute(array, 'seq', [(s, s ^ mask) for s in range(lax.axis_size('s...  43.9 us
    ppermute x32, waiting for transfers between devices, swap(): lax.ppermute(array, 'seq', [(s, s ^ mask) for s in range(lax.axis_size('s...  6.5 us
    pallas_call x2, Pallas kernels, partial_call(): call(functools.partial(partial_body, chain), [wide] * 3 + [half] + [short...  3.83 us
    pallas_call x2, Pallas kernels, final_call(): call(functools.partial(final_body, chain), [wide] * 2 + [half] * 2 + [tal...  2.19 us
    pallas_call x2, Pallas kernels, local(): call(functools.partial(delta_body, chain), [pl.BlockSpec(memory_space=plt...  1.71 us
    pallas_call x2, Pallas kernels, local(): call(functools.partial(norm_body, chain), [wide, wide, wide, whole(1, HEA...  1.48 us
  transfers between devices with their start and end apart: 33, of which 12 were waited for; matrix products, arithmetic and copies ran while one was open for 0% of the time, Pallas kernels for 14%

profile of v18, /device:TPU:0, one launch (start us, length us, event | category | flops | bytes accessed | tf_op | source)
XLA Modules:
  0.0 62.5 jit_solution(10271852718157993136)
XLA Ops:
  0.7 1.4 %delta.3 = (f32[128,128]{1,0:T(8,128)S(1)}, f32[128,128]{1,0:T(8,128)S(1)}, f32[128,128]{1,0:T(8,128)S(1)}, f32[128,128]{1,0:T(8,128)S(1)}) custom-call(s32[1]{0:T(128)} %bitcast.place_ref, bf16[256,1024]{1,0:T(8,128)(2,1)} %bitcast.11, bf16[256,1024]{1,0:T(8,128)(2,1)} %bitcast.18), custom_call_target="tpu_custom_call" | custom-call | flops 201326592 | bytes 2097152 | tf_op jit(solution)/shard_map/delta/pallas_call | solution.py:233
  2.1 4.0 %collective-permute-start.3 = (f32[128,128]{1,0:T(8,128)S(1)}, f32[128,128]{1,0:T(8,128)S(1)}, u32[]{:S(2)}, u32[]{:S(2)}) collective-permute-start(f32[128,128]{1,0:T(8,128)S(1)} %get-tuple-element.87), channel_id=1, source_target_pairs={{0,6},{2,4},{4,2},{6,0},{8,14},{10,12},{12,10},{14,8},{16,22},{18,... | collective-permute-start | bytes 196616 | tf_op jit(solution)/shard_map/ppermute | solution.py:182
  7.0 2.9 %collective-permute-start = (f32[128,128]{1,0:T(8,128)S(1)}, f32[128,128]{1,0:T(8,128)S(1)}, u32[]{:S(2)}, u32[]{:S(2)}) collective-permute-start(f32[128,128]{1,0:T(8,128)S(1)} %get-tuple-element.83), channel_id=1, source_target_pairs={{0,6},{2,4},{4,2},{6,0},{8,14},{10,12},{12,10},{14,8},{16,22},{18,... | collective-permute-start | bytes 196616 | tf_op jit(solution)/shard_map/ppermute | solution.py:182
  11.4 1.6 %collective-permute-start.11 = (f32[128,128]{1,0:T(8,128)S(1)}, f32[128,128]{1,0:T(8,128)S(1)}, u32[]{:S(2)}, u32[]{:S(2)}) collective-permute-start(f32[128,128]{1,0:T(8,128)S(1)} %add_add_fusion.3), channel_id=1, source_target_pairs={{0,8},{2,10},{4,12},{6,14},{8,0},{10,2},{12,4},{14,6},{16,24},{18,... | collective-permute-start | bytes 196616 | tf_op jit(solution)/shard_map/ppermute | solution.py:182
  13.1 0.9 %inner.1.inner_ref = f32[256,1024]{1,0:T(8,128)S(1)} custom-call(s32[1]{0:T(128)} %bitcast.place_ref, bf16[256,1024]{1,0:T(8,128)(2,1)S(1)} %bitcast.27, bf16[256,1024]{1,0:T(8,128)(2,1)S(1)} %bitcast.13, bf16[256,1024]{1,0:T(8,128)(2,1)S(1)} %bitcast.20), custom_call_target="tpu_custom_call" | custom-call | flops 1073741824 | bytes 2097152 | tf_op jit(solution)/shard_map/inner/pallas_call | solution.py:192
  14.7 1.6 %collective-permute-start.6 = (f32[128,128]{1,0:T(8,128)S(1)}, f32[128,128]{1,0:T(8,128)S(1)}, u32[]{:S(2)}, u32[]{:S(2)}) collective-permute-start(f32[128,128]{1,0:T(8,128)S(1)} %add_add_fusion.2), channel_id=1, source_target_pairs={{0,8},{2,10},{4,12},{6,14},{8,0},{10,2},{12,4},{14,6},{16,24},{18,... | collective-permute-start | bytes 196616 | tf_op jit(solution)/shard_map/ppermute | solution.py:182
  16.4 2.7 %collective-permute-start.12 = (f32[128,128]{1,0:T(8,128)S(1)}, f32[128,128]{1,0:T(8,128)S(1)}, u32[]{:S(2)}, u32[]{:S(2)}) collective-permute-start(f32[128,128]{1,0:T(8,128)S(1)} %add.71), channel_id=1, source_target_pairs={{0,16},{2,18},{4,20},{6,22},{8,24},{10,26},{12,28},{14,30},{16,0},... | collective-permute-start | bytes 196616 | tf_op jit(solution)/shard_map/ppermute | solution.py:182
  19.0 2.7 %collective-permute-start.7 = (f32[128,128]{1,0:T(8,128)S(1)}, f32[128,128]{1,0:T(8,128)S(1)}, u32[]{:S(2)}, u32[]{:S(2)}) collective-permute-start(f32[128,128]{1,0:T(8,128)S(1)} %add.69), channel_id=1, source_target_pairs={{0,16},{2,18},{4,20},{6,22},{8,24},{10,26},{12,28},{14,30},{16,0},... | collective-permute-start | bytes 196616 | tf_op jit(solution)/shard_map/ppermute | solution.py:182
  21.7 1.2 %collective-permute-done.12.refs_2_ = f32[128,128]{1,0:T(8,128)S(1)} collective-permute-done((f32[128,128]{1,0:T(8,128)S(1)}, f32[128,128]{1,0:T(8,128)S(1)}, u32[]{:S(2)}, u32[]{:S(2)}) %collective-permute-start.12) | collective-permute-done | bytes 65568 | tf_op jit(solution)/shard_map/ppermute | solution.py:182
  23.1 1.5 %collective-permute-start.13 = (f32[128,128]{1,0:T(8,128)S(1)}, f32[128,128]{1,0:T(8,128)S(1)}, u32[]{:S(2)}, u32[]{:S(2)}) collective-permute-start(f32[128,128]{1,0:T(8,128)S(1)} %get-tuple-element.105), channel_id=1, source_target_pairs={{0,6},{2,4},{4,2},{6,0},{8,14},{10,12},{12,10},{14,8},{16,22},{18,... | collective-permute-start | bytes 196616 | tf_op jit(solution)/shard_map/ppermute | solution.py:182
  25.1 1.6 %collective-permute-start.15 = (f32[128,128]{1,0:T(8,128)S(1)}, f32[128,128]{1,0:T(8,128)S(1)}, u32[]{:S(2)}, u32[]{:S(2)}) collective-permute-start(f32[128,128]{1,0:T(8,128)S(1)} %get-tuple-element.107), channel_id=1, source_target_pairs={{0,2},{2,0},{4,6},{6,4},{8,10},{10,8},{12,14},{14,12},{16,18},{18,... | collective-permute-start | bytes 196616 | tf_op jit(solution)/shard_map/ppermute | solution.py:182
  27.3 2.3 %collective-permute-start.8 = (f32[128,128]{1,0:T(8,128)S(1)}, f32[128,128]{1,0:T(8,128)S(1)}, u32[]{:S(2)}, u32[]{:S(2)}) collective-permute-start(f32[128,128]{1,0:T(8,128)S(1)} %get-tuple-element.100), channel_id=1, source_target_pairs={{0,6},{2,4},{4,2},{6,0},{8,14},{10,12},{12,10},{14,8},{16,22},{18,... | collective-permute-start | bytes 196616 | tf_op jit(solution)/shard_map/ppermute | solution.py:182
  29.6 0.7 %collective-permute-start.9 = (f32[128,128]{1,0:T(8,128)S(1)}, f32[128,128]{1,0:T(8,128)S(1)}, u32[]{:S(2)}, u32[]{:S(2)}) collective-permute-start(f32[128,128]{1,0:T(8,128)S(1)} %get-tuple-element.101), channel_id=1, source_target_pairs={{0,4},{2,6},{4,0},{6,2},{8,12},{10,14},{12,8},{14,10},{16,20},{18,... | collective-permute-start | bytes 196616 | tf_op jit(solution)/shard_map/ppermute | solution.py:182
  30.3 0.7 %norm.2 = (bf16[256,512]{1,0:T(8,128)(2,1)S(1)}, f32[128,128]{1,0:T(8,128)S(1)}, f32[128,128]{1,0:T(8,128)S(1)}, f32[128,128]{1,0:T(8,128)S(1)}, f32[128,128]{1,0:T(8,128)S(1)}, /*index=5*/f32[4,128]{1,0:T(4,128)S(1)}) custom-call(s32[1]{0:T(128)} %bitcast.place_ref, bf16[256,1024]{1,0:T(8,128)(2,1)S(1)} %bitcast.28, bf16[256,1024]{1,0:T(8,128)(2,1)S(1)} %bitcast.25, ...), custom_call_target="tpu_custom_call" | custom-call | flops 536870912 | bytes 2097152 | tf_op jit(solution)/shard_map/norm/pallas_call | solution.py:255
  31.1 1.5 %collective-permute-start.19 = (f32[128,128]{1,0:T(8,128)S(1)}, f32[128,128]{1,0:T(8,128)S(1)}, u32[]{:S(2)}, u32[]{:S(2)}) collective-permute-start(f32[128,128]{1,0:T(8,128)S(1)} %get-tuple-element.115), channel_id=1, source_target_pairs={{0,6},{2,4},{4,2},{6,0},{8,14},{10,12},{12,10},{14,8},{16,22},{18,... | collective-permute-start | bytes 196616 | tf_op jit(solution)/shard_map/ppermute | solution.py:182
  32.6 0.9 %collective-permute-start.20 = (f32[128,128]{1,0:T(8,128)S(1)}, f32[128,128]{1,0:T(8,128)S(1)}, u32[]{:S(2)}, u32[]{:S(2)}) collective-permute-start(f32[128,128]{1,0:T(8,128)S(1)} %get-tuple-element.116), channel_id=1, source_target_pairs={{0,4},{2,6},{4,0},{6,2},{8,12},{10,14},{12,8},{14,10},{16,20},{18,... | collective-permute-start | bytes 196616 | tf_op jit(solution)/shard_map/ppermute | solution.py:182
  33.6 1.1 %collective-permute-start.21 = (f32[128,128]{1,0:T(8,128)S(1)}, f32[128,128]{1,0:T(8,128)S(1)}, u32[]{:S(2)}, u32[]{:S(2)}) collective-permute-start(f32[128,128]{1,0:T(8,128)S(1)} %get-tuple-element.117), channel_id=1, source_target_pairs={{0,2},{2,0},{4,6},{6,4},{8,10},{10,8},{12,14},{14,12},{16,18},{18,... | collective-permute-start | bytes 196616 | tf_op jit(solution)/shard_map/ppermute | solution.py:182
  34.7 0.7 %norm.3 = (bf16[256,512]{1,0:T(8,128)(2,1)S(1)}, f32[136,128]{1,0:T(8,128)S(1)}, f32[136,128]{1,0:T(8,128)S(1)}, f32[136,128]{1,0:T(8,128)S(1)}, f32[136,128]{1,0:T(8,128)S(1)}) custom-call(s32[1]{0:T(128)} %bitcast.place_ref, bf16[256,1024]{1,0:T(8,128)(2,1)S(1)} %bitcast.29, bf16[256,1024]{1,0:T(8,128)(2,1)S(1)} %bitcast.26, ...), custom_call_target="tpu_custom_call" | custom-call | flops 536870912 | bytes 2097152 | tf_op jit(solution)/shard_map/norm/pallas_call | solution.py:255
  35.5 1.7 %collective-permute-start.16 = (f32[136,128]{1,0:T(8,128)S(1)}, f32[136,128]{1,0:T(8,128)S(1)}, u32[]{:S(2)}, u32[]{:S(2)}) collective-permute-start(f32[136,128]{1,0:T(8,128)S(1)} %get-tuple-element.111), channel_id=1, source_target_pairs={{0,6},{2,4},{4,2},{6,0},{8,14},{10,12},{12,10},{14,8},{16,22},{18,... | collective-permute-start | bytes 208904 | tf_op jit(solution)/shard_map/ppermute | solution.py:182
  37.2 1.2 %collective-permute-start.17 = (f32[136,128]{1,0:T(8,128)S(1)}, f32[136,128]{1,0:T(8,128)S(1)}, u32[]{:S(2)}, u32[]{:S(2)}) collective-permute-start(f32[136,128]{1,0:T(8,128)S(1)} %get-tuple-element.112), channel_id=1, source_target_pairs={{0,4},{2,6},{4,0},{6,2},{8,12},{10,14},{12,8},{14,10},{16,20},{18,... | collective-permute-start | bytes 208904 | tf_op jit(solution)/shard_map/ppermute | solution.py:182
  39.6 1.9 %partial.2 = (bf16[256,1024]{1,0:T(8,128)(2,1)}, f32[256,512]{1,0:T(8,128)S(1)}, f32[256,512]{1,0:T(8,128)S(1)}) custom-call(s32[1]{0:T(128)} %bitcast.place_ref, bf16[256,1024]{1,0:T(8,128)(2,1)S(1)} %bitcast.30, bf16[256,1024]{1,0:T(8,128)(2,1)S(1)} %bitcast.14, bf16[256,1024]{1,0:T(8,128)(2,1)S(1)} %bitcast.21, ...), custom_call_target="tpu_custom_call" | custom-call | flops 1610612736 | bytes 2097152 | tf_op jit(solution)/shard_map/partial/pallas_call | solution.py:268
  41.5 1.2 %collective-permute-done.18.refs_6_ = f32[136,128]{1,0:T(8,128)S(1)} collective-permute-done((f32[136,128]{1,0:T(8,128)S(1)}, f32[136,128]{1,0:T(8,128)S(1)}, u32[]{:S(2)}, u32[]{:S(2)}) %collective-permute-start.18) | collective-permute-done | bytes 69664 | tf_op jit(solution)/shard_map/ppermute | solution.py:182
  43.9 2.5 %collective-permute-start.28 = (f32[128,128]{1,0:T(8,128)S(1)}, f32[128,128]{1,0:T(8,128)S(1)}, u32[]{:S(2)}, u32[]{:S(2)}) collective-permute-start(f32[128,128]{1,0:T(8,128)S(1)} %add.81), channel_id=1, source_target_pairs={{0,16},{2,18},{4,20},{6,22},{8,24},{10,26},{12,28},{14,30},{16,0},... | collective-permute-start | bytes 196616 | tf_op jit(solution)/shard_map/ppermute | solution.py:182
  46.4 0.8 %collective-permute-done.22.refs_1_ = f32[136,128]{1,0:T(8,128)S(1)} collective-permute-done((f32[136,128]{1,0:T(8,128)S(1)}, f32[136,128]{1,0:T(8,128)S(1)}, u32[]{:S(2)}, u32[]{:S(2)}) %collective-permute-start.22) | collective-permute-done | bytes 69664 | tf_op jit(solution)/shard_map/ppermute | solution.py:182
  47.1 2.2 %collective-permute-start.23 = (f32[136,128]{1,0:T(8,128)S(1)}, f32[136,128]{1,0:T(8,128)S(1)}, u32[]{:S(2)}, u32[]{:S(2)}) collective-permute-start(f32[136,128]{1,0:T(8,128)S(1)} %add.79), channel_id=1, source_target_pairs={{0,16},{2,18},{4,20},{6,22},{8,24},{10,26},{12,28},{14,30},{16,0},... | collective-permute-start | bytes 208904 | tf_op jit(solution)/shard_map/ppermute | solution.py:182
  49.9 1.1 %collective-permute-start.29 = (f32[128,128]{1,0:T(8,128)S(1)}, f32[128,128]{1,0:T(8,128)S(1)}, u32[]{:S(2)}, u32[]{:S(2)}) collective-permute-start(f32[128,128]{1,0:T(8,128)S(1)} %get-tuple-element.147), channel_id=1, source_target_pairs={{0,6},{2,4},{4,2},{6,0},{8,14},{10,12},{12,10},{14,8},{16,22},{18,... | collective-permute-start | bytes 196616 | tf_op jit(solution)/shard_map/ppermute | solution.py:182
  51.0 1.7 %collective-permute-start.30 = (f32[128,128]{1,0:T(8,128)S(1)}, f32[128,128]{1,0:T(8,128)S(1)}, u32[]{:S(2)}, u32[]{:S(2)}) collective-permute-start(f32[128,128]{1,0:T(8,128)S(1)} %get-tuple-element.148), channel_id=1, source_target_pairs={{0,4},{2,6},{4,0},{6,2},{8,12},{10,14},{12,8},{14,10},{16,20},{18,... | collective-permute-start | bytes 196616 | tf_op jit(solution)/shard_map/ppermute | solution.py:182
  53.6 1.2 %collective-permute-start.24 = (f32[136,128]{1,0:T(8,128)S(1)}, f32[136,128]{1,0:T(8,128)S(1)}, u32[]{:S(2)}, u32[]{:S(2)}) collective-permute-start(f32[136,128]{1,0:T(8,128)S(1)} %get-tuple-element.140), channel_id=1, source_target_pairs={{0,6},{2,4},{4,2},{6,0},{8,14},{10,12},{12,10},{14,8},{16,22},{18,... | collective-permute-start | bytes 208904 | tf_op jit(solution)/shard_map/ppermute | solution.py:182
  54.8 1.7 %collective-permute-start.25 = (f32[136,128]{1,0:T(8,128)S(1)}, f32[136,128]{1,0:T(8,128)S(1)}, u32[]{:S(2)}, u32[]{:S(2)}) collective-permute-start(f32[136,128]{1,0:T(8,128)S(1)} %get-tuple-element.141), channel_id=1, source_target_pairs={{0,4},{2,6},{4,0},{6,2},{8,12},{10,14},{12,8},{14,10},{16,20},{18,... | collective-permute-start | bytes 208904 | tf_op jit(solution)/shard_map/ppermute | solution.py:182
  57.1 1.9 %partial.3 = (bf16[256,1024]{1,0:T(8,128)(2,1)}, f32[256,512]{1,0:T(8,128)S(1)}, f32[256,512]{1,0:T(8,128)S(1)}) custom-call(s32[1]{0:T(128)} %bitcast.place_ref, bf16[256,1024]{1,0:T(8,128)(2,1)S(1)} %bitcast.31, bf16[256,1024]{1,0:T(8,128)(2,1)S(1)} %bitcast.15, bf16[256,1024]{1,0:T(8,128)(2,1)S(1)} %bitcast.22, ...), custom_call_target="tpu_custom_call", output_to_operand_aliasing={{0}: (9, {})} | custom-call | flops 1610612736 | bytes 2097152 | tf_op jit(solution)/shard_map/partial/pallas_call | solution.py:268
  59.1 1.1 %final.2 = (bf16[256,1024]{1,0:T(8,128)(2,1)}, bf16[256,1024]{1,0:T(8,128)(2,1)}) custom-call(s32[1]{0:T(128)} %bitcast.place_ref, bf16[256,1024]{1,0:T(8,128)(2,1)S(1)} %bitcast.16, bf16[256,1024]{1,0:T(8,128)(2,1)S(1)} %bitcast.23, f32[256,512]{1,0:T(8,128)S(1)} %get-tuple-element.143.key_part_ref, f32[256,512]{1,0:T(8,128)S(1)} %get-tuple-element.144.value_part_ref, ...), custom_call_target="tpu_custom_call" | custom-call | flops 536870912 | bytes 2097152 | tf_op jit(solution)/shard_map/final/pallas_call | solution.py:284
  60.8 1.1 %final.3 = (bf16[256,1024]{1,0:T(8,128)(2,1)}, bf16[256,1024]{1,0:T(8,128)(2,1)}) custom-call(s32[1]{0:T(128)} %bitcast.place_ref, bf16[256,1024]{1,0:T(8,128)(2,1)S(1)} %bitcast.17, bf16[256,1024]{1,0:T(8,128)(2,1)S(1)} %bitcast.24, f32[256,512]{1,0:T(8,128)S(1)} %get-tuple-element.133.key_part_ref, ...), custom_call_target="tpu_custom_call", output_to_operand_aliasing={{0}: (9, {}), {1}: (10, {})} | custom-call | flops 536870912 | bytes 2097152 | tf_op jit(solution)/shard_map/final/pallas_call | solution.py:284
  (71 shorter events, 10.2 us)
Async XLA Ops:
  2.1 8.3 %collective-permute-start.3 = (f32[128,128]{1,0:T(8,128)S(1)}, f32[128,128]{1,0:T(8,128)S(1)}, u32[]{:S(2)}, u32[]{:S(2)}) collective-permute-start(f32[128,128]{1,0:T(8,128)S(1)} %get-tuple-element.87), channel_id=1, source_target_pairs={{0,6},{2,4},{4,2},{6,0},{8,14},{10,12},{12,10},{14,8},{16,22},{18,... | collective-permute-start | bytes 196616 | tf_op jit(solution)/shard_map/ppermute | solution.py:182
  6.1 5.0 %collective-permute-start.4 = (f32[128,128]{1,0:T(8,128)S(1)}, f32[128,128]{1,0:T(8,128)S(1)}, u32[]{:S(2)}, u32[]{:S(2)}) collective-permute-start(f32[128,128]{1,0:T(8,128)S(1)} %get-tuple-element.88), channel_id=1, source_target_pairs={{0,4},{2,6},{4,0},{6,2},{8,12},{10,14},{12,8},{14,10},{16,20},{18,... | collective-permute-start | bytes 196616 | tf_op jit(solution)/shard_map/ppermute | solution.py:182
  6.6 4.8 %collective-permute-start.5 = (f32[128,128]{1,0:T(8,128)S(1)}, f32[128,128]{1,0:T(8,128)S(1)}, u32[]{:S(2)}, u32[]{:S(2)}) collective-permute-start(f32[128,128]{1,0:T(8,128)S(1)} %get-tuple-element.89), channel_id=1, source_target_pairs={{0,2},{2,0},{4,6},{6,4},{8,10},{10,8},{12,14},{14,12},{16,18},{18,... | collective-permute-start | bytes 196616 | tf_op jit(solution)/shard_map/ppermute | solution.py:182
  7.0 7.0 %collective-permute-start = (f32[128,128]{1,0:T(8,128)S(1)}, f32[128,128]{1,0:T(8,128)S(1)}, u32[]{:S(2)}, u32[]{:S(2)}) collective-permute-start(f32[128,128]{1,0:T(8,128)S(1)} %get-tuple-element.83), channel_id=1, source_target_pairs={{0,6},{2,4},{4,2},{6,0},{8,14},{10,12},{12,10},{14,8},{16,22},{18,... | collective-permute-start | bytes 196616 | tf_op jit(solution)/shard_map/ppermute | solution.py:182
  9.9 4.3 %collective-permute-start.1 = (f32[128,128]{1,0:T(8,128)S(1)}, f32[128,128]{1,0:T(8,128)S(1)}, u32[]{:S(2)}, u32[]{:S(2)}) collective-permute-start(f32[128,128]{1,0:T(8,128)S(1)} %get-tuple-element.84), channel_id=1, source_target_pairs={{0,4},{2,6},{4,0},{6,2},{8,12},{10,14},{12,8},{14,10},{16,20},{18,... | collective-permute-start | bytes 196616 | tf_op jit(solution)/shard_map/ppermute | solution.py:182
  10.4 4.3 %collective-permute-start.2 = (f32[128,128]{1,0:T(8,128)S(1)}, f32[128,128]{1,0:T(8,128)S(1)}, u32[]{:S(2)}, u32[]{:S(2)}) collective-permute-start(f32[128,128]{1,0:T(8,128)S(1)} %get-tuple-element.85), channel_id=1, source_target_pairs={{0,2},{2,0},{4,6},{6,4},{8,10},{10,8},{12,14},{14,12},{16,18},{18,... | collective-permute-start | bytes 196616 | tf_op jit(solution)/shard_map/ppermute | solution.py:182
  11.4 4.9 %collective-permute-start.11 = (f32[128,128]{1,0:T(8,128)S(1)}, f32[128,128]{1,0:T(8,128)S(1)}, u32[]{:S(2)}, u32[]{:S(2)}) collective-permute-start(f32[128,128]{1,0:T(8,128)S(1)} %add_add_fusion.3), channel_id=1, source_target_pairs={{0,8},{2,10},{4,12},{6,14},{8,0},{10,2},{12,4},{14,6},{16,24},{18,... | collective-permute-start | bytes 196616 | tf_op jit(solution)/shard_map/ppermute | solution.py:182
  14.7 4.3 %collective-permute-start.6 = (f32[128,128]{1,0:T(8,128)S(1)}, f32[128,128]{1,0:T(8,128)S(1)}, u32[]{:S(2)}, u32[]{:S(2)}) collective-permute-start(f32[128,128]{1,0:T(8,128)S(1)} %add_add_fusion.2), channel_id=1, source_target_pairs={{0,8},{2,10},{4,12},{6,14},{8,0},{10,2},{12,4},{14,6},{16,24},{18,... | collective-permute-start | bytes 196616 | tf_op jit(solution)/shard_map/ppermute | solution.py:182
  16.4 6.6 %collective-permute-start.12 = (f32[128,128]{1,0:T(8,128)S(1)}, f32[128,128]{1,0:T(8,128)S(1)}, u32[]{:S(2)}, u32[]{:S(2)}) collective-permute-start(f32[128,128]{1,0:T(8,128)S(1)} %add.71), channel_id=1, source_target_pairs={{0,16},{2,18},{4,20},{6,22},{8,24},{10,26},{12,28},{14,30},{16,0},... | collective-permute-start | bytes 196616 | tf_op jit(solution)/shard_map/ppermute | solution.py:182
  19.0 7.6 %collective-permute-start.7 = (f32[128,128]{1,0:T(8,128)S(1)}, f32[128,128]{1,0:T(8,128)S(1)}, u32[]{:S(2)}, u32[]{:S(2)}) collective-permute-start(f32[128,128]{1,0:T(8,128)S(1)} %add.69), channel_id=1, source_target_pairs={{0,16},{2,18},{4,20},{6,22},{8,24},{10,26},{12,28},{14,30},{16,0},... | collective-permute-start | bytes 196616 | tf_op jit(solution)/shard_map/ppermute | solution.py:182
  23.1 6.5 %collective-permute-start.13 = (f32[128,128]{1,0:T(8,128)S(1)}, f32[128,128]{1,0:T(8,128)S(1)}, u32[]{:S(2)}, u32[]{:S(2)}) collective-permute-start(f32[128,128]{1,0:T(8,128)S(1)} %get-tuple-element.105), channel_id=1, source_target_pairs={{0,6},{2,4},{4,2},{6,0},{8,14},{10,12},{12,10},{14,8},{16,22},{18,... | collective-permute-start | bytes 196616 | tf_op jit(solution)/shard_map/ppermute | solution.py:182
  24.6 5.7 %collective-permute-start.14 = (f32[128,128]{1,0:T(8,128)S(1)}, f32[128,128]{1,0:T(8,128)S(1)}, u32[]{:S(2)}, u32[]{:S(2)}) collective-permute-start(f32[128,128]{1,0:T(8,128)S(1)} %get-tuple-element.106), channel_id=1, source_target_pairs={{0,4},{2,6},{4,0},{6,2},{8,12},{10,14},{12,8},{14,10},{16,20},{18,... | collective-permute-start | bytes 196616 | tf_op jit(solution)/shard_map/ppermute | solution.py:182
  25.1 5.2 %collective-permute-start.15 = (f32[128,128]{1,0:T(8,128)S(1)}, f32[128,128]{1,0:T(8,128)S(1)}, u32[]{:S(2)}, u32[]{:S(2)}) collective-permute-start(f32[128,128]{1,0:T(8,128)S(1)} %get-tuple-element.107), channel_id=1, source_target_pairs={{0,2},{2,0},{4,6},{6,4},{8,10},{10,8},{12,14},{14,12},{16,18},{18,... | collective-permute-start | bytes 196616 | tf_op jit(solution)/shard_map/ppermute | solution.py:182
  26.7 6.8 %collective-permute-start.10 = (f32[128,128]{1,0:T(8,128)S(1)}, f32[128,128]{1,0:T(8,128)S(1)}, u32[]{:S(2)}, u32[]{:S(2)}) collective-permute-start(f32[128,128]{1,0:T(8,128)S(1)} %get-tuple-element.102), channel_id=1, source_target_pairs={{0,2},{2,0},{4,6},{6,4},{8,10},{10,8},{12,14},{14,12},{16,18},{18,... | collective-permute-start | bytes 196616 | tf_op jit(solution)/shard_map/ppermute | solution.py:182
  27.3 7.4 %collective-permute-start.8 = (f32[128,128]{1,0:T(8,128)S(1)}, f32[128,128]{1,0:T(8,128)S(1)}, u32[]{:S(2)}, u32[]{:S(2)}) collective-permute-start(f32[128,128]{1,0:T(8,128)S(1)} %get-tuple-element.100), channel_id=1, source_target_pairs={{0,6},{2,4},{4,2},{6,0},{8,14},{10,12},{12,10},{14,8},{16,22},{18,... | collective-permute-start | bytes 196616 | tf_op jit(solution)/shard_map/ppermute | solution.py:182
  29.6 5.2 %collective-permute-start.9 = (f32[128,128]{1,0:T(8,128)S(1)}, f32[128,128]{1,0:T(8,128)S(1)}, u32[]{:S(2)}, u32[]{:S(2)}) collective-permute-start(f32[128,128]{1,0:T(8,128)S(1)} %get-tuple-element.101), channel_id=1, source_target_pairs={{0,4},{2,6},{4,0},{6,2},{8,12},{10,14},{12,8},{14,10},{16,20},{18,... | collective-permute-start | bytes 196616 | tf_op jit(solution)/shard_map/ppermute | solution.py:182
  31.1 7.3 %collective-permute-start.19 = (f32[128,128]{1,0:T(8,128)S(1)}, f32[128,128]{1,0:T(8,128)S(1)}, u32[]{:S(2)}, u32[]{:S(2)}) collective-permute-start(f32[128,128]{1,0:T(8,128)S(1)} %get-tuple-element.115), channel_id=1, source_target_pairs={{0,6},{2,4},{4,2},{6,0},{8,14},{10,12},{12,10},{14,8},{16,22},{18,... | collective-permute-start | bytes 196616 | tf_op jit(solution)/shard_map/ppermute | solution.py:182
  32.6 6.4 %collective-permute-start.20 = (f32[128,128]{1,0:T(8,128)S(1)}, f32[128,128]{1,0:T(8,128)S(1)}, u32[]{:S(2)}, u32[]{:S(2)}) collective-permute-start(f32[128,128]{1,0:T(8,128)S(1)} %get-tuple-element.116), channel_id=1, source_target_pairs={{0,4},{2,6},{4,0},{6,2},{8,12},{10,14},{12,8},{14,10},{16,20},{18,... | collective-permute-start | bytes 196616 | tf_op jit(solution)/shard_map/ppermute | solution.py:182
  33.6 5.5 %collective-permute-start.21 = (f32[128,128]{1,0:T(8,128)S(1)}, f32[128,128]{1,0:T(8,128)S(1)}, u32[]{:S(2)}, u32[]{:S(2)}) collective-permute-start(f32[128,128]{1,0:T(8,128)S(1)} %get-tuple-element.117), channel_id=1, source_target_pairs={{0,2},{2,0},{4,6},{6,4},{8,10},{10,8},{12,14},{14,12},{16,18},{18,... | collective-permute-start | bytes 196616 | tf_op jit(solution)/shard_map/ppermute | solution.py:182
  35.5 6.1 %collective-permute-start.16 = (f32[136,128]{1,0:T(8,128)S(1)}, f32[136,128]{1,0:T(8,128)S(1)}, u32[]{:S(2)}, u32[]{:S(2)}) collective-permute-start(f32[136,128]{1,0:T(8,128)S(1)} %get-tuple-element.111), channel_id=1, source_target_pairs={{0,6},{2,4},{4,2},{6,0},{8,14},{10,12},{12,10},{14,8},{16,22},{18,... | collective-permute-start | bytes 208904 | tf_op jit(solution)/shard_map/ppermute | solution.py:182
  37.2 4.3 %collective-permute-start.17 = (f32[136,128]{1,0:T(8,128)S(1)}, f32[136,128]{1,0:T(8,128)S(1)}, u32[]{:S(2)}, u32[]{:S(2)}) collective-permute-start(f32[136,128]{1,0:T(8,128)S(1)} %get-tuple-element.112), channel_id=1, source_target_pairs={{0,4},{2,6},{4,0},{6,2},{8,12},{10,14},{12,8},{14,10},{16,20},{18,... | collective-permute-start | bytes 208904 | tf_op jit(solution)/shard_map/ppermute | solution.py:182
  38.4 4.3 %collective-permute-start.18 = (f32[136,128]{1,0:T(8,128)S(1)}, f32[136,128]{1,0:T(8,128)S(1)}, u32[]{:S(2)}, u32[]{:S(2)}) collective-permute-start(f32[136,128]{1,0:T(8,128)S(1)} %get-tuple-element.113), channel_id=1, source_target_pairs={{0,2},{2,0},{4,6},{6,4},{8,10},{10,8},{12,14},{14,12},{16,18},{18,... | collective-permute-start | bytes 208904 | tf_op jit(solution)/shard_map/ppermute | solution.py:182
  39.1 4.8 %collective-permute-start.27 = (f32[128,128]{1,0:T(8,128)S(1)}, f32[128,128]{1,0:T(8,128)S(1)}, u32[]{:S(2)}, u32[]{:S(2)}) collective-permute-start(f32[128,128]{1,0:T(8,128)S(1)} %add_add_fusion.1), channel_id=1, source_target_pairs={{0,8},{2,10},{4,12},{6,14},{8,0},{10,2},{12,4},{14,6},{16,24},{18,... | collective-permute-start | bytes 196616 | tf_op jit(solution)/shard_map/ppermute | solution.py:182
  42.7 4.4 %collective-permute-start.22 = (f32[136,128]{1,0:T(8,128)S(1)}, f32[136,128]{1,0:T(8,128)S(1)}, u32[]{:S(2)}, u32[]{:S(2)}) collective-permute-start(f32[136,128]{1,0:T(8,128)S(1)} %add_add_fusion), channel_id=1, source_target_pairs={{0,8},{2,10},{4,12},{6,14},{8,0},{10,2},{12,4},{14,6},{16,24},{18,... | collective-permute-start | bytes 208904 | tf_op jit(solution)/shard_map/ppermute | solution.py:182
  43.9 5.9 %collective-permute-start.28 = (f32[128,128]{1,0:T(8,128)S(1)}, f32[128,128]{1,0:T(8,128)S(1)}, u32[]{:S(2)}, u32[]{:S(2)}) collective-permute-start(f32[128,128]{1,0:T(8,128)S(1)} %add.81), channel_id=1, source_target_pairs={{0,16},{2,18},{4,20},{6,22},{8,24},{10,26},{12,28},{14,30},{16,0},... | collective-permute-start | bytes 196616 | tf_op jit(solution)/shard_map/ppermute | solution.py:182
  47.1 6.4 %collective-permute-start.23 = (f32[136,128]{1,0:T(8,128)S(1)}, f32[136,128]{1,0:T(8,128)S(1)}, u32[]{:S(2)}, u32[]{:S(2)}) collective-permute-start(f32[136,128]{1,0:T(8,128)S(1)} %add.79), channel_id=1, source_target_pairs={{0,16},{2,18},{4,20},{6,22},{8,24},{10,26},{12,28},{14,30},{16,0},... | collective-permute-start | bytes 208904 | tf_op jit(solution)/shard_map/ppermute | solution.py:182
  49.9 6.5 %collective-permute-start.29 = (f32[128,128]{1,0:T(8,128)S(1)}, f32[128,128]{1,0:T(8,128)S(1)}, u32[]{:S(2)}, u32[]{:S(2)}) collective-permute-start(f32[128,128]{1,0:T(8,128)S(1)} %get-tuple-element.147), channel_id=1, source_target_pairs={{0,6},{2,4},{4,2},{6,0},{8,14},{10,12},{12,10},{14,8},{16,22},{18,... | collective-permute-start | bytes 196616 | tf_op jit(solution)/shard_map/ppermute | solution.py:182
  51.0 8.0 %collective-permute-start.30 = (f32[128,128]{1,0:T(8,128)S(1)}, f32[128,128]{1,0:T(8,128)S(1)}, u32[]{:S(2)}, u32[]{:S(2)}) collective-permute-start(f32[128,128]{1,0:T(8,128)S(1)} %get-tuple-element.148), channel_id=1, source_target_pairs={{0,4},{2,6},{4,0},{6,2},{8,12},{10,14},{12,8},{14,10},{16,20},{18,... | collective-permute-start | bytes 196616 | tf_op jit(solution)/shard_map/ppermute | solution.py:182
  52.8 6.3 %collective-permute-start.31 = (f32[128,128]{1,0:T(8,128)S(1)}, f32[128,128]{1,0:T(8,128)S(1)}, u32[]{:S(2)}, u32[]{:S(2)}) collective-permute-start(f32[128,128]{1,0:T(8,128)S(1)} %get-tuple-element.149), channel_id=1, source_target_pairs={{0,2},{2,0},{4,6},{6,4},{8,10},{10,8},{12,14},{14,12},{16,18},{18,... | collective-permute-start | bytes 196616 | tf_op jit(solution)/shard_map/ppermute | solution.py:182
  53.6 6.6 %collective-permute-start.24 = (f32[136,128]{1,0:T(8,128)S(1)}, f32[136,128]{1,0:T(8,128)S(1)}, u32[]{:S(2)}, u32[]{:S(2)}) collective-permute-start(f32[136,128]{1,0:T(8,128)S(1)} %get-tuple-element.140), channel_id=1, source_target_pairs={{0,6},{2,4},{4,2},{6,0},{8,14},{10,12},{12,10},{14,8},{16,22},{18,... | collective-permute-start | bytes 208904 | tf_op jit(solution)/shard_map/ppermute | solution.py:182
  54.8 5.4 %collective-permute-start.25 = (f32[136,128]{1,0:T(8,128)S(1)}, f32[136,128]{1,0:T(8,128)S(1)}, u32[]{:S(2)}, u32[]{:S(2)}) collective-permute-start(f32[136,128]{1,0:T(8,128)S(1)} %get-tuple-element.141), channel_id=1, source_target_pairs={{0,4},{2,6},{4,0},{6,2},{8,12},{10,14},{12,8},{14,10},{16,20},{18,... | collective-permute-start | bytes 208904 | tf_op jit(solution)/shard_map/ppermute | solution.py:182
  56.4 4.3 %collective-permute-start.26 = (f32[136,128]{1,0:T(8,128)S(1)}, f32[136,128]{1,0:T(8,128)S(1)}, u32[]{:S(2)}, u32[]{:S(2)}) collective-permute-start(f32[136,128]{1,0:T(8,128)S(1)} %get-tuple-element.142), channel_id=1, source_target_pairs={{0,2},{2,0},{4,6},{6,4},{8,10},{10,8},{12,14},{14,12},{16,18},{18,... | collective-permute-start | bytes 208904 | tf_op jit(solution)/shard_map/ppermute | solution.py:182
  (6 other events, 30.2 us)

commit v19 on v16

--- a/solution.py
+++ b/solution.py
@@ -159,10 +159,10 @@
     )
 
 
-def exchange_steps():
+def exchange_steps(direct):
     count, base, steps = lax.axis_size("seq"), GROUP, []
     while base < count:
-        masks = [base, 3 * base, 2 * base] if 4 * base <= count else [base]
+        masks = [base, 3 * base, 2 * base] if direct and 4 * base <= count else [base]
         steps.append(masks)
         base *= len(masks) + 1
     return steps
@@ -175,21 +175,29 @@
 
 
 def plane_swap(pieces):
-    return lax.optimization_barrier([swap(piece, mask) for mask, piece in zip(ORDER, pieces)])
-
-
-def exchange(held):
-    total, arrived = sum(held[1:], held[0]), []
-    for masks in exchange_steps():
-        arrived += lax.optimization_barrier([swap(total, mask) for mask in masks])
-        total = sum(arrived[-len(masks) :], total)
-    return total, arrived
-
-
-def carried_in(held, total, arrived, reverse, place):
+    return [swap(piece, mask) for mask, piece in zip(ORDER, pieces)]
+
+
+def plane_sum(held):
+    return sum(held[1:], held[0])
+
+
+def carried_in(held, reverse, place, beside=None, operands=()):
+    total, arrived, steps, result = plane_sum(held), [], exchange_steps(reverse), None
+    for masks in steps:
+        if beside and masks == steps[-1]:
+            total, operands = lax.optimization_barrier((total, operands))
+            result = beside(*operands)
+        got = [swap(total, mask) for mask in masks]
+        if result is not None:
+            got, result = lax.optimization_barrier((got, result))
+        elif len(masks) > 1:
+            got = lax.optimization_barrier(got)
+        arrived += got
+        total = sum(got, total)
     single = whole(*total.shape)
     back = call(
-        functools.partial(prefix_body, reverse, sum(exchange_steps(), [])),
+        functools.partial(prefix_body, reverse, sum(steps, [])),
         [single] * (1 + len(arrived) + GROUP),
         [single] * GROUP,
         [jax.ShapeDtypeStruct(total.shape, jnp.float32)] * GROUP,
@@ -197,7 +205,7 @@
         "prefix",
         scratch=[pltpu.VMEM((GROUP, DH, DH), jnp.float32)],
     )(place, total, *arrived, *held)
-    return plane_swap(back)
+    return plane_swap(back), result
 
 
 def local(queries, keys, values, out_gain, grad_out):
@@ -228,11 +236,9 @@
     inner_call = call(
         lambda place_ref, *refs: inner_body(*refs), [wide] * 3, wide, full_float, 16 * unit, "inner"
     )
-    helds = [plane_swap(deltas[chain]) for chain in chains]
-    helds[1], operands = lax.optimization_barrier((helds[1], (place, query, key, value)))
-    (total, arrived), *others = [exchange(held) for held in helds]
-    arrived, inner = lax.optimization_barrier((arrived, inner_call(*operands)))
-    states = [carried_in(*sums, False, place) for sums in zip(helds, *zip((total, arrived), *others))]
+    first, second = [lax.optimization_barrier(plane_swap(deltas[chain])) for chain in chains]
+    state, inner = carried_in(first, False, place, inner_call, (place, query, key, value))
+    states = [state, carried_in(second, False, place)[0]]
     attns, later = [], []
     for chain in range(CHAINS):
         attn, *deltas = call(
@@ -244,8 +250,8 @@
             "norm",
         )(place, query, grad, inner, gain, *states[chain])
         attns.append(attn)
-        held = plane_swap(deltas)
-        later += carried_in(held, *exchange(held), True, place)
+        held = lax.optimization_barrier(plane_swap(deltas))
+        later += carried_in(held, True, place)[0]
     grad_query, key_part, value_part = call(
         partial_body,
         [wide] * 3 + [half] * CHAINS + [short] * HEADS,

time: 62.7 us -> 61.9 us (0.987)
  waiting for transfers between devices: 6.18 us -> 4.88 us
    ppermute x36 -> x34, waiting for transfers between devices: 6.18 us -> 4.88 us  [swap(): lax.ppermute(array, 'seq', [(s, s ^ mask) for s in range(lax.axis_size('s...]
    ppermute x36 -> x34, starting transfers between devices: 45.7 us -> 46.2 us  [swap(): lax.ppermute(array, 'seq', [(s, s ^ mask) for s in range(lax.axis_size('s...]
  transfers between devices with their start and end apart: 37 -> 35, of which waited for: 7 -> 9; matrix products, arithmetic and copies ran while one was open for 0% -> 0% of each run, Pallas kernels for 12% -> 12%
where the time goes in v19:
time: 61.9 us; the launch traced here: 61.7 us
  starting transfers between devices  46.2 us (75%)
  Pallas kernels  9.03 us (15%)
  waiting for transfers between devices  4.88 us (8%)
  between operations  0.8 us (1%)
  other arithmetic  0.76 us (1%)
    ppermute x34, starting transfers between devices, swap(): lax.ppermute(array, 'seq', [(s, s ^ mask) for s in range(lax.axis_size('s...  46.2 us
    ppermute x34, waiting for transfers between devices, swap(): lax.ppermute(array, 'seq', [(s, s ^ mask) for s in range(lax.axis_size('s...  4.88 us
    pallas_call x1, Pallas kernels, local(): call(partial_body, [wide] * 3 + [half] * CHAINS + [short] * HEADS, [wide]...  3.09 us
    pallas_call x1, Pallas kernels, local(): call(final_body, [wide] * 4 + [tall] * HEADS, [chunk] * 2, [full_low] * 2...  1.61 us
    pallas_call x1, Pallas kernels, local(): call(delta_body, [pl.BlockSpec(memory_space=pltpu.HBM)] * 2, [short] * HE...  1.59 us
    pallas_call x2, Pallas kernels, local(): call(functools.partial(norm_body, chain), [wide, wide, wide, whole(1, HEA...  1.48 us
  transfers between devices with their start and end apart: 35, of which 9 were waited for; matrix products, arithmetic and copies ran while one was open for 0% of the time, Pallas kernels for 12%

profile of v19, /device:TPU:0, one launch (start us, length us, event | category | flops | bytes accessed | tf_op | source)
XLA Modules:
  0.0 61.7 jit_solution(2825067156054509577)
XLA Ops:
  0.6 1.6 %delta.1 = (f32[128,128]{1,0:T(8,128)S(1)}, f32[128,128]{1,0:T(8,128)S(1)}, f32[128,128]{1,0:T(8,128)S(1)}, f32[128,128]{1,0:T(8,128)S(1)}, f32[128,128]{1,0:T(8...) custom-call(s32[1]{0:T(128)} %bitcast.place_ref, bf16[256,1024]{1,0:T(8,128)(2,1)} %bitcast.19, ...), custom_call_target="tpu_custom_call" | custom-call | flops 402653184 | bytes 2097152 | tf_op jit(solution)/shard_map/delta/pallas_call | solution.py:226
  2.2 4.0 %collective-permute-start = (f32[128,128]{1,0:T(8,128)S(1)}, f32[128,128]{1,0:T(8,128)S(1)}, u32[]{:S(2)}, u32[]{:S(2)}) collective-permute-start(f32[128,128]{1,0:T(8,128)S(1)} %get-tuple-element.73), channel_id=1, source_target_pairs={{0,6},{2,4},{4,2},{6,0},{8,14},{10,12},{12,10},{14,8},{16,22},{18,... | collective-permute-start | bytes 196616 | tf_op jit(solution)/shard_map/ppermute | solution.py:174
  6.8 2.8 %collective-permute-start.8 = (f32[128,128]{1,0:T(8,128)S(1)}, f32[128,128]{1,0:T(8,128)S(1)}, u32[]{:S(2)}, u32[]{:S(2)}) collective-permute-start(f32[128,128]{1,0:T(8,128)S(1)} %get-tuple-element.93), channel_id=1, source_target_pairs={{0,6},{2,4},{4,2},{6,0},{8,14},{10,12},{12,10},{14,8},{16,22},{18,... | collective-permute-start | bytes 196616 | tf_op jit(solution)/shard_map/ppermute | solution.py:174
  11.3 1.6 %collective-permute-start.3 = (f32[128,128]{1,0:T(8,128)S(1)}, f32[128,128]{1,0:T(8,128)S(1)}, u32[]{:S(2)}, u32[]{:S(2)}) collective-permute-start(f32[128,128]{1,0:T(8,128)S(1)} %add_add_fusion.5), channel_id=1, source_target_pairs={{0,8},{2,10},{4,12},{6,14},{8,0},{10,2},{12,4},{14,6},{16,24},{18,... | collective-permute-start | bytes 196616 | tf_op jit(solution)/shard_map/ppermute | solution.py:174
  13.1 0.9 %collective-permute-done.9.refs_5_ = f32[128,128]{1,0:T(8,128)S(1)} collective-permute-done((f32[128,128]{1,0:T(8,128)S(1)}, f32[128,128]{1,0:T(8,128)S(1)}, u32[]{:S(2)}, u32[]{:S(2)}) %collective-permute-start.9) | collective-permute-done | bytes 65568 | tf_op jit(solution)/shard_map/ppermute | solution.py:174
  14.5 1.6 %collective-permute-start.11 = (f32[128,128]{1,0:T(8,128)S(1)}, f32[128,128]{1,0:T(8,128)S(1)}, u32[]{:S(2)}, u32[]{:S(2)}) collective-permute-start(f32[128,128]{1,0:T(8,128)S(1)} %add_add_fusion.4), channel_id=1, source_target_pairs={{0,8},{2,10},{4,12},{6,14},{8,0},{10,2},{12,4},{14,6},{16,24},{18,... | collective-permute-start | bytes 196616 | tf_op jit(solution)/shard_map/ppermute | solution.py:174
  16.3 2.6 %collective-permute-start.4 = (f32[128,128]{1,0:T(8,128)S(1)}, f32[128,128]{1,0:T(8,128)S(1)}, u32[]{:S(2)}, u32[]{:S(2)}) collective-permute-start(f32[128,128]{1,0:T(8,128)S(1)} %add.72), channel_id=1, source_target_pairs={{0,16},{2,18},{4,20},{6,22},{8,24},{10,26},{12,28},{14,30},{16,0},... | collective-permute-start | bytes 196616 | tf_op jit(solution)/shard_map/ppermute | solution.py:174
  19.0 2.5 %collective-permute-start.12 = (f32[128,128]{1,0:T(8,128)S(1)}, f32[128,128]{1,0:T(8,128)S(1)}, u32[]{:S(2)}, u32[]{:S(2)}) collective-permute-start(f32[128,128]{1,0:T(8,128)S(1)} %add.77), channel_id=1, source_target_pairs={{0,16},{2,18},{4,20},{6,22},{8,24},{10,26},{12,28},{14,30},{16,0},... | collective-permute-start | bytes 196616 | tf_op jit(solution)/shard_map/ppermute | solution.py:174
  21.5 0.9 %inner.1.inner_ref = f32[256,1024]{1,0:T(8,128)S(1)} custom-call(s32[1]{0:T(128)} %bitcast.place_ref, bf16[256,1024]{1,0:T(8,128)(2,1)S(1)} %bitcast.13, bf16[256,1024]{1,0:T(8,128)(2,1)S(1)} %bitcast.20, bf16[256,1024]{1,0:T(8,128)(2,1)S(1)} %bitcast.24), custom_call_target="tpu_custom_call" | custom-call | flops 1073741824 | bytes 2097152 | tf_op jit(solution)/shard_map/inner/pallas_call | solution.py:190
  23.1 1.5 %collective-permute-start.5 = (f32[128,128]{1,0:T(8,128)S(1)}, f32[128,128]{1,0:T(8,128)S(1)}, u32[]{:S(2)}, u32[]{:S(2)}) collective-permute-start(f32[128,128]{1,0:T(8,128)S(1)} %get-tuple-element.88), channel_id=1, source_target_pairs={{0,6},{2,4},{4,2},{6,0},{8,14},{10,12},{12,10},{14,8},{16,22},{18,... | collective-permute-start | bytes 196616 | tf_op jit(solution)/shard_map/ppermute | solution.py:174
  25.1 1.6 %collective-permute-start.7 = (f32[128,128]{1,0:T(8,128)S(1)}, f32[128,128]{1,0:T(8,128)S(1)}, u32[]{:S(2)}, u32[]{:S(2)}) collective-permute-start(f32[128,128]{1,0:T(8,128)S(1)} %get-tuple-element.90), channel_id=1, source_target_pairs={{0,2},{2,0},{4,6},{6,4},{8,10},{10,8},{12,14},{14,12},{16,18},{18,... | collective-permute-start | bytes 196616 | tf_op jit(solution)/shard_map/ppermute | solution.py:174
  26.7 1.5 %collective-permute-start.13 = (f32[128,128]{1,0:T(8,128)S(1)}, f32[128,128]{1,0:T(8,128)S(1)}, u32[]{:S(2)}, u32[]{:S(2)}) collective-permute-start(f32[128,128]{1,0:T(8,128)S(1)} %get-tuple-element.101), channel_id=1, source_target_pairs={{0,6},{2,4},{4,2},{6,0},{8,14},{10,12},{12,10},{14,8},{16,22},{18,... | collective-permute-start | bytes 196616 | tf_op jit(solution)/shard_map/ppermute | solution.py:174
  28.7 1.6 %collective-permute-start.15 = (f32[128,128]{1,0:T(8,128)S(1)}, f32[128,128]{1,0:T(8,128)S(1)}, u32[]{:S(2)}, u32[]{:S(2)}) collective-permute-start(f32[128,128]{1,0:T(8,128)S(1)} %get-tuple-element.103), channel_id=1, source_target_pairs={{0,2},{2,0},{4,6},{6,4},{8,10},{10,8},{12,14},{14,12},{16,18},{18,... | collective-permute-start | bytes 196616 | tf_op jit(solution)/shard_map/ppermute | solution.py:174
  31.1 1.5 %collective-permute-start.16 = (f32[136,128]{1,0:T(8,128)S(1)}, f32[136,128]{1,0:T(8,128)S(1)}, u32[]{:S(2)}, u32[]{:S(2)}) collective-permute-start(f32[136,128]{1,0:T(8,128)S(1)} %get-tuple-element.109), channel_id=1, source_target_pairs={{0,6},{2,4},{4,2},{6,0},{8,14},{10,12},{12,10},{14,8},{16,22},{18,... | collective-permute-start | bytes 208904 | tf_op jit(solution)/shard_map/ppermute | solution.py:174
  32.6 1.0 %collective-permute-start.17 = (f32[136,128]{1,0:T(8,128)S(1)}, f32[136,128]{1,0:T(8,128)S(1)}, u32[]{:S(2)}, u32[]{:S(2)}) collective-permute-start(f32[136,128]{1,0:T(8,128)S(1)} %get-tuple-element.110), channel_id=1, source_target_pairs={{0,4},{2,6},{4,0},{6,2},{8,12},{10,14},{12,8},{14,10},{16,20},{18,... | collective-permute-start | bytes 208904 | tf_op jit(solution)/shard_map/ppermute | solution.py:174
  33.5 1.1 %collective-permute-start.18 = (f32[136,128]{1,0:T(8,128)S(1)}, f32[136,128]{1,0:T(8,128)S(1)}, u32[]{:S(2)}, u32[]{:S(2)}) collective-permute-start(f32[136,128]{1,0:T(8,128)S(1)} %get-tuple-element.111), channel_id=1, source_target_pairs={{0,2},{2,0},{4,6},{6,4},{8,10},{10,8},{12,14},{14,12},{16,18},{18,... | collective-permute-start | bytes 208904 | tf_op jit(solution)/shard_map/ppermute | solution.py:174
  35.4 1.5 %collective-permute-start.25 = (f32[136,128]{1,0:T(8,128)S(1)}, f32[136,128]{1,0:T(8,128)S(1)}, u32[]{:S(2)}, u32[]{:S(2)}) collective-permute-start(f32[136,128]{1,0:T(8,128)S(1)} %get-tuple-element.124), channel_id=1, source_target_pairs={{0,6},{2,4},{4,2},{6,0},{8,14},{10,12},{12,10},{14,8},{16,22},{18,... | collective-permute-start | bytes 208904 | tf_op jit(solution)/shard_map/ppermute | solution.py:174
  36.9 1.0 %collective-permute-start.26 = (f32[136,128]{1,0:T(8,128)S(1)}, f32[136,128]{1,0:T(8,128)S(1)}, u32[]{:S(2)}, u32[]{:S(2)}) collective-permute-start(f32[136,128]{1,0:T(8,128)S(1)} %get-tuple-element.125), channel_id=1, source_target_pairs={{0,4},{2,6},{4,0},{6,2},{8,12},{10,14},{12,8},{14,10},{16,20},{18,... | collective-permute-start | bytes 208904 | tf_op jit(solution)/shard_map/ppermute | solution.py:174
  37.9 1.1 %collective-permute-start.27 = (f32[136,128]{1,0:T(8,128)S(1)}, f32[136,128]{1,0:T(8,128)S(1)}, u32[]{:S(2)}, u32[]{:S(2)}) collective-permute-start(f32[136,128]{1,0:T(8,128)S(1)} %get-tuple-element.126), channel_id=1, source_target_pairs={{0,2},{2,0},{4,6},{6,4},{8,10},{10,8},{12,14},{14,12},{16,18},{18,... | collective-permute-start | bytes 208904 | tf_op jit(solution)/shard_map/ppermute | solution.py:174
  39.0 1.1 %collective-permute-start.19 = (f32[136,128]{1,0:T(8,128)S(1)}, f32[136,128]{1,0:T(8,128)S(1)}, u32[]{:S(2)}, u32[]{:S(2)}) collective-permute-start(f32[136,128]{1,0:T(8,128)S(1)} %add_add_fusion.3), channel_id=1, source_target_pairs={{0,8},{2,10},{4,12},{6,14},{8,0},{10,2},{12,4},{14,6},{16,24},{18,... | collective-permute-start | bytes 208904 | tf_op jit(solution)/shard_map/ppermute | solution.py:174
  40.1 2.3 %collective-permute-start.20 = (f32[136,128]{1,0:T(8,128)S(1)}, f32[136,128]{1,0:T(8,128)S(1)}, u32[]{:S(2)}, u32[]{:S(2)}) collective-permute-start(f32[136,128]{1,0:T(8,128)S(1)} %add_add_fusion.3), channel_id=1, source_target_pairs={{0,24},{2,26},{4,28},{6,30},{8,16},{10,18},{12,20},{14,22},{16,8},... | collective-permute-start | bytes 208904 | tf_op jit(solution)/shard_map/ppermute | solution.py:174
  42.9 1.7 %collective-permute-start.28 = (f32[136,128]{1,0:T(8,128)S(1)}, f32[136,128]{1,0:T(8,128)S(1)}, u32[]{:S(2)}, u32[]{:S(2)}) collective-permute-start(f32[136,128]{1,0:T(8,128)S(1)} %add_add_fusion.1), channel_id=1, source_target_pairs={{0,8},{2,10},{4,12},{6,14},{8,0},{10,2},{12,4},{14,6},{16,24},{18,... | collective-permute-start | bytes 208904 | tf_op jit(solution)/shard_map/ppermute | solution.py:174
  44.6 2.3 %collective-permute-start.29 = (f32[136,128]{1,0:T(8,128)S(1)}, f32[136,128]{1,0:T(8,128)S(1)}, u32[]{:S(2)}, u32[]{:S(2)}) collective-permute-start(f32[136,128]{1,0:T(8,128)S(1)} %add_add_fusion.1), channel_id=1, source_target_pairs={{0,24},{2,26},{4,28},{6,30},{8,16},{10,18},{12,20},{14,22},{16,8},... | collective-permute-start | bytes 208904 | tf_op jit(solution)/shard_map/ppermute | solution.py:174
  46.9 1.5 %collective-permute-done.21.refs_3_ = f32[136,128]{1,0:T(8,128)S(1)} collective-permute-done((f32[136,128]{1,0:T(8,128)S(1)}, f32[136,128]{1,0:T(8,128)S(1)}, u32[]{:S(2)}, u32[]{:S(2)}) %collective-permute-start.21) | collective-permute-done | bytes 69664 | tf_op jit(solution)/shard_map/ppermute | solution.py:174
  48.5 1.6 %collective-permute-start.22 = (f32[136,128]{1,0:T(8,128)S(1)}, f32[136,128]{1,0:T(8,128)S(1)}, u32[]{:S(2)}, u32[]{:S(2)}) collective-permute-start(f32[136,128]{1,0:T(8,128)S(1)} %get-tuple-element.120), channel_id=1, source_target_pairs={{0,6},{2,4},{4,2},{6,0},{8,14},{10,12},{12,10},{14,8},{16,22},{18,... | collective-permute-start | bytes 208904 | tf_op jit(solution)/shard_map/ppermute | solution.py:174
  50.1 1.0 %collective-permute-start.23 = (f32[136,128]{1,0:T(8,128)S(1)}, f32[136,128]{1,0:T(8,128)S(1)}, u32[]{:S(2)}, u32[]{:S(2)}) collective-permute-start(f32[136,128]{1,0:T(8,128)S(1)} %get-tuple-element.121), channel_id=1, source_target_pairs={{0,4},{2,6},{4,0},{6,2},{8,12},{10,14},{12,8},{14,10},{16,20},{18,... | collective-permute-start | bytes 208904 | tf_op jit(solution)/shard_map/ppermute | solution.py:174
  51.1 1.0 %collective-permute-start.24 = (f32[136,128]{1,0:T(8,128)S(1)}, f32[136,128]{1,0:T(8,128)S(1)}, u32[]{:S(2)}, u32[]{:S(2)}) collective-permute-start(f32[136,128]{1,0:T(8,128)S(1)} %get-tuple-element.122), channel_id=1, source_target_pairs={{0,2},{2,0},{4,6},{6,4},{8,10},{10,8},{12,14},{14,12},{16,18},{18,... | collective-permute-start | bytes 208904 | tf_op jit(solution)/shard_map/ppermute | solution.py:174
  52.6 1.8 %collective-permute-start.31 = (f32[136,128]{1,0:T(8,128)S(1)}, f32[136,128]{1,0:T(8,128)S(1)}, u32[]{:S(2)}, u32[]{:S(2)}) collective-permute-start(f32[136,128]{1,0:T(8,128)S(1)} %get-tuple-element.135), channel_id=1, source_target_pairs={{0,6},{2,4},{4,2},{6,0},{8,14},{10,12},{12,10},{14,8},{16,22},{18,... | collective-permute-start | bytes 208904 | tf_op jit(solution)/shard_map/ppermute | solution.py:174
  54.3 0.8 %collective-permute-start.32 = (f32[136,128]{1,0:T(8,128)S(1)}, f32[136,128]{1,0:T(8,128)S(1)}, u32[]{:S(2)}, u32[]{:S(2)}) collective-permute-start(f32[136,128]{1,0:T(8,128)S(1)} %get-tuple-element.136), channel_id=1, source_target_pairs={{0,4},{2,6},{4,0},{6,2},{8,12},{10,14},{12,8},{14,10},{16,20},{18,... | collective-permute-start | bytes 208904 | tf_op jit(solution)/shard_map/ppermute | solution.py:174
  55.2 1.0 %collective-permute-start.33 = (f32[136,128]{1,0:T(8,128)S(1)}, f32[136,128]{1,0:T(8,128)S(1)}, u32[]{:S(2)}, u32[]{:S(2)}) collective-permute-start(f32[136,128]{1,0:T(8,128)S(1)} %get-tuple-element.137), channel_id=1, source_target_pairs={{0,2},{2,0},{4,6},{6,4},{8,10},{10,8},{12,14},{14,12},{16,18},{18,... | collective-permute-start | bytes 208904 | tf_op jit(solution)/shard_map/ppermute | solution.py:174
  56.1 3.1 %partial.1 = (bf16[256,1024]{1,0:T(8,128)(2,1)}, f32[256,1024]{1,0:T(8,128)S(1)}, f32[256,1024]{1,0:T(8,128)S(1)}) custom-call(s32[1]{0:T(128)} %bitcast.place_ref, bf16[256,1024]{1,0:T(8,128)(2,1)S(1)} %bitcast.16, bf16[256,1024]{1,0:T(8,128)(2,1)S(1)} %bitcast.21, bf16[256,1024]{1,0:T(8,128)(2,1)S(1)} %bitcast.25, ...), custom_call_target="tpu_custom_call" | custom-call | flops 3221225472 | bytes 2097152 | tf_op jit(solution)/shard_map/partial/pallas_call | solution.py:255
  59.5 1.6 %final.1 = (bf16[256,1024]{1,0:T(8,128)(2,1)}, bf16[256,1024]{1,0:T(8,128)(2,1)}) custom-call(s32[1]{0:T(128)} %bitcast.place_ref, bf16[256,1024]{1,0:T(8,128)(2,1)S(1)} %bitcast.22, bf16[256,1024]{1,0:T(8,128)(2,1)S(1)} %bitcast.26, f32[256,1024]{1,0:T(8,128)S(1)} %get-tuple-element.106.key_part_ref, f32[256,1024]{1,0:T(8,128)S(1)} %get-tuple-element.107.value_part_ref, ...), custom_call_target="tpu_custom_call" | custom-call | flops 1073741824 | bytes 2097152 | tf_op jit(solution)/shard_map/final/pallas_call | solution.py:271
  (70 shorter events, 8.4 us)
Async XLA Ops:
  2.2 8.0 %collective-permute-start = (f32[128,128]{1,0:T(8,128)S(1)}, f32[128,128]{1,0:T(8,128)S(1)}, u32[]{:S(2)}, u32[]{:S(2)}) collective-permute-start(f32[128,128]{1,0:T(8,128)S(1)} %get-tuple-element.73), channel_id=1, source_target_pairs={{0,6},{2,4},{4,2},{6,0},{8,14},{10,12},{12,10},{14,8},{16,22},{18,... | collective-permute-start | bytes 196616 | tf_op jit(solution)/shard_map/ppermute | solution.py:174
  6.2 5.1 %collective-permute-start.1 = (f32[128,128]{1,0:T(8,128)S(1)}, f32[128,128]{1,0:T(8,128)S(1)}, u32[]{:S(2)}, u32[]{:S(2)}) collective-permute-start(f32[128,128]{1,0:T(8,128)S(1)} %get-tuple-element.74), channel_id=1, source_target_pairs={{0,4},{2,6},{4,0},{6,2},{8,12},{10,14},{12,8},{14,10},{16,20},{18,... | collective-permute-start | bytes 196616 | tf_op jit(solution)/shard_map/ppermute | solution.py:174
  6.7 4.6 %collective-permute-start.2 = (f32[128,128]{1,0:T(8,128)S(1)}, f32[128,128]{1,0:T(8,128)S(1)}, u32[]{:S(2)}, u32[]{:S(2)}) collective-permute-start(f32[128,128]{1,0:T(8,128)S(1)} %get-tuple-element.75), channel_id=1, source_target_pairs={{0,2},{2,0},{4,6},{6,4},{8,10},{10,8},{12,14},{14,12},{16,18},{18,... | collective-permute-start | bytes 196616 | tf_op jit(solution)/shard_map/ppermute | solution.py:174
  6.8 6.2 %collective-permute-start.8 = (f32[128,128]{1,0:T(8,128)S(1)}, f32[128,128]{1,0:T(8,128)S(1)}, u32[]{:S(2)}, u32[]{:S(2)}) collective-permute-start(f32[128,128]{1,0:T(8,128)S(1)} %get-tuple-element.93), channel_id=1, source_target_pairs={{0,6},{2,4},{4,2},{6,0},{8,14},{10,12},{12,10},{14,8},{16,22},{18,... | collective-permute-start | bytes 196616 | tf_op jit(solution)/shard_map/ppermute | solution.py:174
  11.3 5.0 %collective-permute-start.3 = (f32[128,128]{1,0:T(8,128)S(1)}, f32[128,128]{1,0:T(8,128)S(1)}, u32[]{:S(2)}, u32[]{:S(2)}) collective-permute-start(f32[128,128]{1,0:T(8,128)S(1)} %add_add_fusion.5), channel_id=1, source_target_pairs={{0,8},{2,10},{4,12},{6,14},{8,0},{10,2},{12,4},{14,6},{16,24},{18,... | collective-permute-start | bytes 196616 | tf_op jit(solution)/shard_map/ppermute | solution.py:174
  14.5 4.5 %collective-permute-start.11 = (f32[128,128]{1,0:T(8,128)S(1)}, f32[128,128]{1,0:T(8,128)S(1)}, u32[]{:S(2)}, u32[]{:S(2)}) collective-permute-start(f32[128,128]{1,0:T(8,128)S(1)} %add_add_fusion.4), channel_id=1, source_target_pairs={{0,8},{2,10},{4,12},{6,14},{8,0},{10,2},{12,4},{14,6},{16,24},{18,... | collective-permute-start | bytes 196616 | tf_op jit(solution)/shard_map/ppermute | solution.py:174
  16.3 6.6 %collective-permute-start.4 = (f32[128,128]{1,0:T(8,128)S(1)}, f32[128,128]{1,0:T(8,128)S(1)}, u32[]{:S(2)}, u32[]{:S(2)}) collective-permute-start(f32[128,128]{1,0:T(8,128)S(1)} %add.72), channel_id=1, source_target_pairs={{0,16},{2,18},{4,20},{6,22},{8,24},{10,26},{12,28},{14,30},{16,0},... | collective-permute-start | bytes 196616 | tf_op jit(solution)/shard_map/ppermute | solution.py:174
  19.0 7.7 %collective-permute-start.12 = (f32[128,128]{1,0:T(8,128)S(1)}, f32[128,128]{1,0:T(8,128)S(1)}, u32[]{:S(2)}, u32[]{:S(2)}) collective-permute-start(f32[128,128]{1,0:T(8,128)S(1)} %add.77), channel_id=1, source_target_pairs={{0,16},{2,18},{4,20},{6,22},{8,24},{10,26},{12,28},{14,30},{16,0},... | collective-permute-start | bytes 196616 | tf_op jit(solution)/shard_map/ppermute | solution.py:174
  23.1 5.7 %collective-permute-start.5 = (f32[128,128]{1,0:T(8,128)S(1)}, f32[128,128]{1,0:T(8,128)S(1)}, u32[]{:S(2)}, u32[]{:S(2)}) collective-permute-start(f32[128,128]{1,0:T(8,128)S(1)} %get-tuple-element.88), channel_id=1, source_target_pairs={{0,6},{2,4},{4,2},{6,0},{8,14},{10,12},{12,10},{14,8},{16,22},{18,... | collective-permute-start | bytes 196616 | tf_op jit(solution)/shard_map/ppermute | solution.py:174
  24.6 5.7 %collective-permute-start.6 = (f32[128,128]{1,0:T(8,128)S(1)}, f32[128,128]{1,0:T(8,128)S(1)}, u32[]{:S(2)}, u32[]{:S(2)}) collective-permute-start(f32[128,128]{1,0:T(8,128)S(1)} %get-tuple-element.89), channel_id=1, source_target_pairs={{0,4},{2,6},{4,0},{6,2},{8,12},{10,14},{12,8},{14,10},{16,20},{18,... | collective-permute-start | bytes 196616 | tf_op jit(solution)/shard_map/ppermute | solution.py:174
  25.1 5.2 %collective-permute-start.7 = (f32[128,128]{1,0:T(8,128)S(1)}, f32[128,128]{1,0:T(8,128)S(1)}, u32[]{:S(2)}, u32[]{:S(2)}) collective-permute-start(f32[128,128]{1,0:T(8,128)S(1)} %get-tuple-element.90), channel_id=1, source_target_pairs={{0,2},{2,0},{4,6},{6,4},{8,10},{10,8},{12,14},{14,12},{16,18},{18,... | collective-permute-start | bytes 196616 | tf_op jit(solution)/shard_map/ppermute | solution.py:174
  26.7 6.8 %collective-permute-start.13 = (f32[128,128]{1,0:T(8,128)S(1)}, f32[128,128]{1,0:T(8,128)S(1)}, u32[]{:S(2)}, u32[]{:S(2)}) collective-permute-start(f32[128,128]{1,0:T(8,128)S(1)} %get-tuple-element.101), channel_id=1, source_target_pairs={{0,6},{2,4},{4,2},{6,0},{8,14},{10,12},{12,10},{14,8},{16,22},{18,... | collective-permute-start | bytes 196616 | tf_op jit(solution)/shard_map/ppermute | solution.py:174
  28.3 6.4 %collective-permute-start.14 = (f32[128,128]{1,0:T(8,128)S(1)}, f32[128,128]{1,0:T(8,128)S(1)}, u32[]{:S(2)}, u32[]{:S(2)}) collective-permute-start(f32[128,128]{1,0:T(8,128)S(1)} %get-tuple-element.102), channel_id=1, source_target_pairs={{0,4},{2,6},{4,0},{6,2},{8,12},{10,14},{12,8},{14,10},{16,20},{18,... | collective-permute-start | bytes 196616 | tf_op jit(solution)/shard_map/ppermute | solution.py:174
  28.7 5.9 %collective-permute-start.15 = (f32[128,128]{1,0:T(8,128)S(1)}, f32[128,128]{1,0:T(8,128)S(1)}, u32[]{:S(2)}, u32[]{:S(2)}) collective-permute-start(f32[128,128]{1,0:T(8,128)S(1)} %get-tuple-element.103), channel_id=1, source_target_pairs={{0,2},{2,0},{4,6},{6,4},{8,10},{10,8},{12,14},{14,12},{16,18},{18,... | collective-permute-start | bytes 196616 | tf_op jit(solution)/shard_map/ppermute | solution.py:174
  31.1 6.8 %collective-permute-start.16 = (f32[136,128]{1,0:T(8,128)S(1)}, f32[136,128]{1,0:T(8,128)S(1)}, u32[]{:S(2)}, u32[]{:S(2)}) collective-permute-start(f32[136,128]{1,0:T(8,128)S(1)} %get-tuple-element.109), channel_id=1, source_target_pairs={{0,6},{2,4},{4,2},{6,0},{8,14},{10,12},{12,10},{14,8},{16,22},{18,... | collective-permute-start | bytes 208904 | tf_op jit(solution)/shard_map/ppermute | solution.py:174
  32.6 6.4 %collective-permute-start.17 = (f32[136,128]{1,0:T(8,128)S(1)}, f32[136,128]{1,0:T(8,128)S(1)}, u32[]{:S(2)}, u32[]{:S(2)}) collective-permute-start(f32[136,128]{1,0:T(8,128)S(1)} %get-tuple-element.110), channel_id=1, source_target_pairs={{0,4},{2,6},{4,0},{6,2},{8,12},{10,14},{12,8},{14,10},{16,20},{18,... | collective-permute-start | bytes 208904 | tf_op jit(solution)/shard_map/ppermute | solution.py:174
  33.5 5.4 %collective-permute-start.18 = (f32[136,128]{1,0:T(8,128)S(1)}, f32[136,128]{1,0:T(8,128)S(1)}, u32[]{:S(2)}, u32[]{:S(2)}) collective-permute-start(f32[136,128]{1,0:T(8,128)S(1)} %get-tuple-element.111), channel_id=1, source_target_pairs={{0,2},{2,0},{4,6},{6,4},{8,10},{10,8},{12,14},{14,12},{16,18},{18,... | collective-permute-start | bytes 208904 | tf_op jit(solution)/shard_map/ppermute | solution.py:174
  35.4 7.0 %collective-permute-start.25 = (f32[136,128]{1,0:T(8,128)S(1)}, f32[136,128]{1,0:T(8,128)S(1)}, u32[]{:S(2)}, u32[]{:S(2)}) collective-permute-start(f32[136,128]{1,0:T(8,128)S(1)} %get-tuple-element.124), channel_id=1, source_target_pairs={{0,6},{2,4},{4,2},{6,0},{8,14},{10,12},{12,10},{14,8},{16,22},{18,... | collective-permute-start | bytes 208904 | tf_op jit(solution)/shard_map/ppermute | solution.py:174
  36.9 6.0 %collective-permute-start.26 = (f32[136,128]{1,0:T(8,128)S(1)}, f32[136,128]{1,0:T(8,128)S(1)}, u32[]{:S(2)}, u32[]{:S(2)}) collective-permute-start(f32[136,128]{1,0:T(8,128)S(1)} %get-tuple-element.125), channel_id=1, source_target_pairs={{0,4},{2,6},{4,0},{6,2},{8,12},{10,14},{12,8},{14,10},{16,20},{18,... | collective-permute-start | bytes 208904 | tf_op jit(solution)/shard_map/ppermute | solution.py:174
  37.9 5.1 %collective-permute-start.27 = (f32[136,128]{1,0:T(8,128)S(1)}, f32[136,128]{1,0:T(8,128)S(1)}, u32[]{:S(2)}, u32[]{:S(2)}) collective-permute-start(f32[136,128]{1,0:T(8,128)S(1)} %get-tuple-element.126), channel_id=1, source_target_pairs={{0,2},{2,0},{4,6},{6,4},{8,10},{10,8},{12,14},{14,12},{16,18},{18,... | collective-permute-start | bytes 208904 | tf_op jit(solution)/shard_map/ppermute | solution.py:174
  39.0 7.9 %collective-permute-start.19 = (f32[136,128]{1,0:T(8,128)S(1)}, f32[136,128]{1,0:T(8,128)S(1)}, u32[]{:S(2)}, u32[]{:S(2)}) collective-permute-start(f32[136,128]{1,0:T(8,128)S(1)} %add_add_fusion.3), channel_id=1, source_target_pairs={{0,8},{2,10},{4,12},{6,14},{8,0},{10,2},{12,4},{14,6},{16,24},{18,... | collective-permute-start | bytes 208904 | tf_op jit(solution)/shard_map/ppermute | solution.py:174
  40.1 6.8 %collective-permute-start.20 = (f32[136,128]{1,0:T(8,128)S(1)}, f32[136,128]{1,0:T(8,128)S(1)}, u32[]{:S(2)}, u32[]{:S(2)}) collective-permute-start(f32[136,128]{1,0:T(8,128)S(1)} %add_add_fusion.3), channel_id=1, source_target_pairs={{0,24},{2,26},{4,28},{6,30},{8,16},{10,18},{12,20},{14,22},{16,8},... | collective-permute-start | bytes 208904 | tf_op jit(solution)/shard_map/ppermute | solution.py:174
  42.4 6.0 %collective-permute-start.21 = (f32[136,128]{1,0:T(8,128)S(1)}, f32[136,128]{1,0:T(8,128)S(1)}, u32[]{:S(2)}, u32[]{:S(2)}) collective-permute-start(f32[136,128]{1,0:T(8,128)S(1)} %add_add_fusion.3), channel_id=1, source_target_pairs={{0,16},{2,18},{4,20},{6,22},{8,24},{10,26},{12,28},{14,30},{16,0},... | collective-permute-start | bytes 208904 | tf_op jit(solution)/shard_map/ppermute | solution.py:174
  42.9 8.2 %collective-permute-start.28 = (f32[136,128]{1,0:T(8,128)S(1)}, f32[136,128]{1,0:T(8,128)S(1)}, u32[]{:S(2)}, u32[]{:S(2)}) collective-permute-start(f32[136,128]{1,0:T(8,128)S(1)} %add_add_fusion.1), channel_id=1, source_target_pairs={{0,8},{2,10},{4,12},{6,14},{8,0},{10,2},{12,4},{14,6},{16,24},{18,... | collective-permute-start | bytes 208904 | tf_op jit(solution)/shard_map/ppermute | solution.py:174
  44.6 7.4 %collective-permute-start.29 = (f32[136,128]{1,0:T(8,128)S(1)}, f32[136,128]{1,0:T(8,128)S(1)}, u32[]{:S(2)}, u32[]{:S(2)}) collective-permute-start(f32[136,128]{1,0:T(8,128)S(1)} %add_add_fusion.1), channel_id=1, source_target_pairs={{0,24},{2,26},{4,28},{6,30},{8,16},{10,18},{12,20},{14,22},{16,8},... | collective-permute-start | bytes 208904 | tf_op jit(solution)/shard_map/ppermute | solution.py:174
  46.9 5.5 %collective-permute-start.30 = (f32[136,128]{1,0:T(8,128)S(1)}, f32[136,128]{1,0:T(8,128)S(1)}, u32[]{:S(2)}, u32[]{:S(2)}) collective-permute-start(f32[136,128]{1,0:T(8,128)S(1)} %add_add_fusion.1), channel_id=1, source_target_pairs={{0,16},{2,18},{4,20},{6,22},{8,24},{10,26},{12,28},{14,30},{16,0},... | collective-permute-start | bytes 208904 | tf_op jit(solution)/shard_map/ppermute | solution.py:174
  48.5 6.7 %collective-permute-start.22 = (f32[136,128]{1,0:T(8,128)S(1)}, f32[136,128]{1,0:T(8,128)S(1)}, u32[]{:S(2)}, u32[]{:S(2)}) collective-permute-start(f32[136,128]{1,0:T(8,128)S(1)} %get-tuple-element.120), channel_id=1, source_target_pairs={{0,6},{2,4},{4,2},{6,0},{8,14},{10,12},{12,10},{14,8},{16,22},{18,... | collective-permute-start | bytes 208904 | tf_op jit(solution)/shard_map/ppermute | solution.py:174
  50.1 9.2 %collective-permute-start.23 = (f32[136,128]{1,0:T(8,128)S(1)}, f32[136,128]{1,0:T(8,128)S(1)}, u32[]{:S(2)}, u32[]{:S(2)}) collective-permute-start(f32[136,128]{1,0:T(8,128)S(1)} %get-tuple-element.121), channel_id=1, source_target_pairs={{0,4},{2,6},{4,0},{6,2},{8,12},{10,14},{12,8},{14,10},{16,20},{18,... | collective-permute-start | bytes 208904 | tf_op jit(solution)/shard_map/ppermute | solution.py:174
  51.1 8.1 %collective-permute-start.24 = (f32[136,128]{1,0:T(8,128)S(1)}, f32[136,128]{1,0:T(8,128)S(1)}, u32[]{:S(2)}, u32[]{:S(2)}) collective-permute-start(f32[136,128]{1,0:T(8,128)S(1)} %get-tuple-element.122), channel_id=1, source_target_pairs={{0,2},{2,0},{4,6},{6,4},{8,10},{10,8},{12,14},{14,12},{16,18},{18,... | collective-permute-start | bytes 208904 | tf_op jit(solution)/shard_map/ppermute | solution.py:174
  52.6 6.7 %collective-permute-start.31 = (f32[136,128]{1,0:T(8,128)S(1)}, f32[136,128]{1,0:T(8,128)S(1)}, u32[]{:S(2)}, u32[]{:S(2)}) collective-permute-start(f32[136,128]{1,0:T(8,128)S(1)} %get-tuple-element.135), channel_id=1, source_target_pairs={{0,6},{2,4},{4,2},{6,0},{8,14},{10,12},{12,10},{14,8},{16,22},{18,... | collective-permute-start | bytes 208904 | tf_op jit(solution)/shard_map/ppermute | solution.py:174
  54.3 4.9 %collective-permute-start.32 = (f32[136,128]{1,0:T(8,128)S(1)}, f32[136,128]{1,0:T(8,128)S(1)}, u32[]{:S(2)}, u32[]{:S(2)}) collective-permute-start(f32[136,128]{1,0:T(8,128)S(1)} %get-tuple-element.136), channel_id=1, source_target_pairs={{0,4},{2,6},{4,0},{6,2},{8,12},{10,14},{12,8},{14,10},{16,20},{18,... | collective-permute-start | bytes 208904 | tf_op jit(solution)/shard_map/ppermute | solution.py:174
  55.2 4.3 %collective-permute-start.33 = (f32[136,128]{1,0:T(8,128)S(1)}, f32[136,128]{1,0:T(8,128)S(1)}, u32[]{:S(2)}, u32[]{:S(2)}) collective-permute-start(f32[136,128]{1,0:T(8,128)S(1)} %get-tuple-element.137), channel_id=1, source_target_pairs={{0,2},{2,0},{4,6},{6,4},{8,10},{10,8},{12,14},{14,12},{16,18},{18,... | collective-permute-start | bytes 208904 | tf_op jit(solution)/shard_map/ppermute | solution.py:174
  (8 other events, 60.8 us)

commit v20 on v19

--- a/solution.py
+++ b/solution.py
@@ -69,8 +69,10 @@
 
 
 def norm_body(chain, place_ref, query_ref, grad_ref, inner_ref, gain_ref, *refs):
-    state_refs, (attn_ref, *delta_refs) = refs[:GROUP], refs[GROUP:]
-    for mask, state_ref, delta_ref in zip(ORDER, state_refs, delta_refs):
+    state_refs, (attn_ref, *delta_refs) = refs[:GROUP], refs[-GROUP - 1 - (chain == 0) :]
+    if chain == 0:
+        *delta_refs, terms_ref = delta_refs
+    for slot, (mask, state_ref, delta_ref) in enumerate(zip(ORDER, state_refs, delta_refs)):
         at = own_columns(place_ref, mask, chain)
         query = query_ref[:, at]
         attn = inner_ref[:, at] + dot(query, state_ref[...].astype(jnp.bfloat16), NN)
@@ -83,7 +85,12 @@
         grad_attn = ((gain * cotangent - normed * shared) * per_root).astype(jnp.bfloat16)
         attn_ref[:, own_columns(place_ref, mask)] = grad_attn
         delta_ref[:DH] = dot(query, grad_attn, TN)
-        delta_ref[DH:] = jnp.broadcast_to(jnp.sum(product, axis=0, keepdims=True), (GAIN_ROWS, DH))
+        terms = jnp.sum(product, axis=0, keepdims=True)
+        if chain == 0:
+            terms_ref[slot : slot + 1] = terms
+        else:
+            delta_ref[DH:] = jnp.broadcast_to(terms, (GAIN_ROWS, DH))
+            delta_ref[DH + 1 : DH + 2] = refs[GROUP][slot : slot + 1]
 
 
 def partial_body(place_ref, query_ref, key_ref, value_ref, *refs):
@@ -114,9 +121,11 @@
 
 
 def gain_body(place_ref, *refs):
-    for at_head, state_ref in enumerate(refs[:-1]):
-        row = (at_head // GROUP) * GROUP + (place_ref[0] & (GROUP - 1) ^ ORDER[at_head % GROUP])
-        refs[-1][pl.ds(row, 1), :] = state_ref[DH : DH + 1]
+    for mask, state_ref in zip(ORDER, refs[GROUP:-1]):
+        member = place_ref[0] & (GROUP - 1) ^ mask
+        for chain in range(CHAINS):
+            row = DH + CHAINS - 1 - chain
+            refs[-1][pl.ds(chain * GROUP + member, 1), :] = state_ref[row : row + 1]
 
 
 def prefix_body(reverse, masks, place_ref, *refs):
@@ -239,18 +248,20 @@
     first, second = [lax.optimization_barrier(plane_swap(deltas[chain])) for chain in chains]
     state, inner = carried_in(first, False, place, inner_call, (place, query, key, value))
     states = [state, carried_in(second, False, place)[0]]
-    attns, later = [], []
+    attns, later, terms = [], [], ()
     for chain in range(CHAINS):
+        size, spec = (square, short) if chain == 0 else (taller, tall)
+        extra = [] if chain else [jax.ShapeDtypeStruct((GROUP, DH), jnp.float32)]
         attn, *deltas = call(
             functools.partial(norm_body, chain),
-            [wide, wide, wide, whole(1, HEADS * DH)] + [short] * GROUP,
-            [half] + [tall] * GROUP,
-            [half_low] + [taller] * GROUP,
+            [wide, wide, wide, whole(1, HEADS * DH)] + [short] * GROUP + [whole(GROUP, DH)] * chain,
+            [half] + [spec] * GROUP + [whole(*one.shape) for one in extra],
+            [half_low] + [size] * GROUP + extra,
             8 * unit,
             "norm",
-        )(place, query, grad, inner, gain, *states[chain])
+        )(place, query, grad, inner, gain, *states[chain], *terms)
         attns.append(attn)
-        held = lax.optimization_barrier(plane_swap(deltas))
+        held, terms = lax.optimization_barrier(plane_swap(deltas[:GROUP])), deltas[GROUP:]
         later += carried_in(held, True, place)[0]
     grad_query, key_part, value_part = call(
         partial_body,
@@ -261,7 +272,7 @@
         "partial",
     )(place, query, key, value, *attns, *[state for chain in states for state in chain])
     gain_terms = call(
-        gain_body, [tall] * HEADS, whole(HEADS, DH), jax.ShapeDtypeStruct((HEADS, DH), jnp.float32), unit, "gain"
+        gain_body, [short] * GROUP + [tall] * GROUP, whole(HEADS, DH), jax.ShapeDtypeStruct((HEADS, DH), jnp.float32), unit, "gain"
     )(place, *later)
     docs, mask = lax.axis_size("dp"), 1
     while mask < docs:
@@ -269,7 +280,7 @@
         mask *= 2
     chunk = pl.BlockSpec((PART_ROWS, HEADS * DH), lambda step: (step, 0))
     grad_key, grad_value = call(
-        final_body, [wide] * 4 + [tall] * HEADS, [chunk] * 2, [full_low] * 2, 16 * unit, "final", steps=PARTS
+        final_body, [wide] * 4 + [short] * GROUP + [tall] * GROUP, [chunk] * 2, [full_low] * 2, 16 * unit, "final", steps=PARTS
     )(place, key, value, key_part, value_part, *later)
     grad_gain = gain_terms / math.sqrt(lax.axis_size("seq") * docs * BLOCK)
     return (

time: 61.9 us -> 62 us (level)
  no operation moved by 1% of the time
where the time goes in v20:
time: 62 us; the launch traced here: 61.8 us
  starting transfers between devices  46.2 us (75%)
  Pallas kernels  9 us (15%)
  waiting for transfers between devices  5 us (8%)
  between operations  0.79 us (1%)
  other arithmetic  0.76 us (1%)
    ppermute x34, starting transfers between devices, swap(): lax.ppermute(array, 'seq', [(s, s ^ mask) for s in range(lax.axis_size('s...  46.2 us
    ppermute x34, waiting for transfers between devices, swap(): lax.ppermute(array, 'seq', [(s, s ^ mask) for s in range(lax.axis_size('s...  5 us
    pallas_call x1, Pallas kernels, local(): call(partial_body, [wide] * 3 + [half] * CHAINS + [short] * HEADS, [wide]...  3.08 us
    pallas_call x1, Pallas kernels, local(): call(final_body, [wide] * 4 + [short] * GROUP + [tall] * GROUP, [chunk] *...  1.61 us
    pallas_call x1, Pallas kernels, local(): call(delta_body, [pl.BlockSpec(memory_space=pltpu.HBM)] * 2, [short] * HE...  1.59 us
    pallas_call x2, Pallas kernels, local(): call(functools.partial(norm_body, chain), [wide, wide, wide, whole(1, HEA...  1.47 us
  transfers between devices with their start and end apart: 35, of which 9 were waited for; matrix products, arithmetic and copies ran while one was open for 0% of the time, Pallas kernels for 12%

profile of v20, /device:TPU:0, one launch (start us, length us, event | category | flops | bytes accessed | tf_op | source)
XLA Modules:
  0.0 61.8 jit_solution(11636550681229280556)
XLA Ops:
  0.6 1.6 %delta.1 = (f32[128,128]{1,0:T(8,128)S(1)}, f32[128,128]{1,0:T(8,128)S(1)}, f32[128,128]{1,0:T(8,128)S(1)}, f32[128,128]{1,0:T(8,128)S(1)}, f32[128,128]{1,0:T(8...) custom-call(s32[1]{0:T(128)} %bitcast.place_ref, bf16[256,1024]{1,0:T(8,128)(2,1)} %bitcast.19, ...), custom_call_target="tpu_custom_call" | custom-call | flops 402653184 | bytes 2097152 | tf_op jit(solution)/shard_map/delta/pallas_call | solution.py:235
  2.2 4.0 %collective-permute-start = (f32[128,128]{1,0:T(8,128)S(1)}, f32[128,128]{1,0:T(8,128)S(1)}, u32[]{:S(2)}, u32[]{:S(2)}) collective-permute-start(f32[128,128]{1,0:T(8,128)S(1)} %get-tuple-element.74), channel_id=1, source_target_pairs={{0,6},{2,4},{4,2},{6,0},{8,14},{10,12},{12,10},{14,8},{16,22},{18,... | collective-permute-start | bytes 196616 | tf_op jit(solution)/shard_map/ppermute | solution.py:183
  6.8 2.8 %collective-permute-start.8 = (f32[128,128]{1,0:T(8,128)S(1)}, f32[128,128]{1,0:T(8,128)S(1)}, u32[]{:S(2)}, u32[]{:S(2)}) collective-permute-start(f32[128,128]{1,0:T(8,128)S(1)} %get-tuple-element.94), channel_id=1, source_target_pairs={{0,6},{2,4},{4,2},{6,0},{8,14},{10,12},{12,10},{14,8},{16,22},{18,... | collective-permute-start | bytes 196616 | tf_op jit(solution)/shard_map/ppermute | solution.py:183
  11.3 1.6 %collective-permute-start.3 = (f32[128,128]{1,0:T(8,128)S(1)}, f32[128,128]{1,0:T(8,128)S(1)}, u32[]{:S(2)}, u32[]{:S(2)}) collective-permute-start(f32[128,128]{1,0:T(8,128)S(1)} %add_add_fusion.5), channel_id=1, source_target_pairs={{0,8},{2,10},{4,12},{6,14},{8,0},{10,2},{12,4},{14,6},{16,24},{18,... | collective-permute-start | bytes 196616 | tf_op jit(solution)/shard_map/ppermute | solution.py:183
  13.1 0.9 %collective-permute-done.9.refs_5_ = f32[128,128]{1,0:T(8,128)S(1)} collective-permute-done((f32[128,128]{1,0:T(8,128)S(1)}, f32[128,128]{1,0:T(8,128)S(1)}, u32[]{:S(2)}, u32[]{:S(2)}) %collective-permute-start.9) | collective-permute-done | bytes 65568 | tf_op jit(solution)/shard_map/ppermute | solution.py:183
  14.5 1.6 %collective-permute-start.11 = (f32[128,128]{1,0:T(8,128)S(1)}, f32[128,128]{1,0:T(8,128)S(1)}, u32[]{:S(2)}, u32[]{:S(2)}) collective-permute-start(f32[128,128]{1,0:T(8,128)S(1)} %add_add_fusion.4), channel_id=1, source_target_pairs={{0,8},{2,10},{4,12},{6,14},{8,0},{10,2},{12,4},{14,6},{16,24},{18,... | collective-permute-start | bytes 196616 | tf_op jit(solution)/shard_map/ppermute | solution.py:183
  16.3 2.6 %collective-permute-start.4 = (f32[128,128]{1,0:T(8,128)S(1)}, f32[128,128]{1,0:T(8,128)S(1)}, u32[]{:S(2)}, u32[]{:S(2)}) collective-permute-start(f32[128,128]{1,0:T(8,128)S(1)} %add.72), channel_id=1, source_target_pairs={{0,16},{2,18},{4,20},{6,22},{8,24},{10,26},{12,28},{14,30},{16,0},... | collective-permute-start | bytes 196616 | tf_op jit(solution)/shard_map/ppermute | solution.py:183
  19.0 2.5 %collective-permute-start.12 = (f32[128,128]{1,0:T(8,128)S(1)}, f32[128,128]{1,0:T(8,128)S(1)}, u32[]{:S(2)}, u32[]{:S(2)}) collective-permute-start(f32[128,128]{1,0:T(8,128)S(1)} %add.77), channel_id=1, source_target_pairs={{0,16},{2,18},{4,20},{6,22},{8,24},{10,26},{12,28},{14,30},{16,0},... | collective-permute-start | bytes 196616 | tf_op jit(solution)/shard_map/ppermute | solution.py:183
  21.5 0.9 %inner.1.inner_ref = f32[256,1024]{1,0:T(8,128)S(1)} custom-call(s32[1]{0:T(128)} %bitcast.place_ref, bf16[256,1024]{1,0:T(8,128)(2,1)S(1)} %bitcast.13, bf16[256,1024]{1,0:T(8,128)(2,1)S(1)} %bitcast.20, bf16[256,1024]{1,0:T(8,128)(2,1)S(1)} %bitcast.24), custom_call_target="tpu_custom_call" | custom-call | flops 1073741824 | bytes 2097152 | tf_op jit(solution)/shard_map/inner/pallas_call | solution.py:199
  23.1 1.5 %collective-permute-start.5 = (f32[128,128]{1,0:T(8,128)S(1)}, f32[128,128]{1,0:T(8,128)S(1)}, u32[]{:S(2)}, u32[]{:S(2)}) collective-permute-start(f32[128,128]{1,0:T(8,128)S(1)} %get-tuple-element.89), channel_id=1, source_target_pairs={{0,6},{2,4},{4,2},{6,0},{8,14},{10,12},{12,10},{14,8},{16,22},{18,... | collective-permute-start | bytes 196616 | tf_op jit(solution)/shard_map/ppermute | solution.py:183
  25.1 1.6 %collective-permute-start.7 = (f32[128,128]{1,0:T(8,128)S(1)}, f32[128,128]{1,0:T(8,128)S(1)}, u32[]{:S(2)}, u32[]{:S(2)}) collective-permute-start(f32[128,128]{1,0:T(8,128)S(1)} %get-tuple-element.91), channel_id=1, source_target_pairs={{0,2},{2,0},{4,6},{6,4},{8,10},{10,8},{12,14},{14,12},{16,18},{18,... | collective-permute-start | bytes 196616 | tf_op jit(solution)/shard_map/ppermute | solution.py:183
  26.7 1.5 %collective-permute-start.13 = (f32[128,128]{1,0:T(8,128)S(1)}, f32[128,128]{1,0:T(8,128)S(1)}, u32[]{:S(2)}, u32[]{:S(2)}) collective-permute-start(f32[128,128]{1,0:T(8,128)S(1)} %get-tuple-element.102), channel_id=1, source_target_pairs={{0,6},{2,4},{4,2},{6,0},{8,14},{10,12},{12,10},{14,8},{16,22},{18,... | collective-permute-start | bytes 196616 | tf_op jit(solution)/shard_map/ppermute | solution.py:183
  28.7 1.6 %collective-permute-start.15 = (f32[128,128]{1,0:T(8,128)S(1)}, f32[128,128]{1,0:T(8,128)S(1)}, u32[]{:S(2)}, u32[]{:S(2)}) collective-permute-start(f32[128,128]{1,0:T(8,128)S(1)} %get-tuple-element.104), channel_id=1, source_target_pairs={{0,2},{2,0},{4,6},{6,4},{8,10},{10,8},{12,14},{14,12},{16,18},{18,... | collective-permute-start | bytes 196616 | tf_op jit(solution)/shard_map/ppermute | solution.py:183
  31.1 1.5 %collective-permute-start.16 = (f32[128,128]{1,0:T(8,128)S(1)}, f32[128,128]{1,0:T(8,128)S(1)}, u32[]{:S(2)}, u32[]{:S(2)}) collective-permute-start(f32[128,128]{1,0:T(8,128)S(1)} %get-tuple-element.111), channel_id=1, source_target_pairs={{0,6},{2,4},{4,2},{6,0},{8,14},{10,12},{12,10},{14,8},{16,22},{18,... | collective-permute-start | bytes 196616 | tf_op jit(solution)/shard_map/ppermute | solution.py:183
  32.6 0.9 %collective-permute-start.17 = (f32[128,128]{1,0:T(8,128)S(1)}, f32[128,128]{1,0:T(8,128)S(1)}, u32[]{:S(2)}, u32[]{:S(2)}) collective-permute-start(f32[128,128]{1,0:T(8,128)S(1)} %get-tuple-element.112), channel_id=1, source_target_pairs={{0,4},{2,6},{4,0},{6,2},{8,12},{10,14},{12,8},{14,10},{16,20},{18,... | collective-permute-start | bytes 196616 | tf_op jit(solution)/shard_map/ppermute | solution.py:183
  33.5 1.1 %collective-permute-start.18 = (f32[128,128]{1,0:T(8,128)S(1)}, f32[128,128]{1,0:T(8,128)S(1)}, u32[]{:S(2)}, u32[]{:S(2)}) collective-permute-start(f32[128,128]{1,0:T(8,128)S(1)} %get-tuple-element.113), channel_id=1, source_target_pairs={{0,2},{2,0},{4,6},{6,4},{8,10},{10,8},{12,14},{14,12},{16,18},{18,... | collective-permute-start | bytes 196616 | tf_op jit(solution)/shard_map/ppermute | solution.py:183
  35.4 1.5 %collective-permute-start.25 = (f32[136,128]{1,0:T(8,128)S(1)}, f32[136,128]{1,0:T(8,128)S(1)}, u32[]{:S(2)}, u32[]{:S(2)}) collective-permute-start(f32[136,128]{1,0:T(8,128)S(1)} %get-tuple-element.126), channel_id=1, source_target_pairs={{0,6},{2,4},{4,2},{6,0},{8,14},{10,12},{12,10},{14,8},{16,22},{18,... | collective-permute-start | bytes 208904 | tf_op jit(solution)/shard_map/ppermute | solution.py:183
  36.9 0.9 %collective-permute-start.26 = (f32[136,128]{1,0:T(8,128)S(1)}, f32[136,128]{1,0:T(8,128)S(1)}, u32[]{:S(2)}, u32[]{:S(2)}) collective-permute-start(f32[136,128]{1,0:T(8,128)S(1)} %get-tuple-element.127), channel_id=1, source_target_pairs={{0,4},{2,6},{4,0},{6,2},{8,12},{10,14},{12,8},{14,10},{16,20},{18,... | collective-permute-start | bytes 208904 | tf_op jit(solution)/shard_map/ppermute | solution.py:183
  37.8 1.1 %collective-permute-start.27 = (f32[136,128]{1,0:T(8,128)S(1)}, f32[136,128]{1,0:T(8,128)S(1)}, u32[]{:S(2)}, u32[]{:S(2)}) collective-permute-start(f32[136,128]{1,0:T(8,128)S(1)} %get-tuple-element.128), channel_id=1, source_target_pairs={{0,2},{2,0},{4,6},{6,4},{8,10},{10,8},{12,14},{14,12},{16,18},{18,... | collective-permute-start | bytes 208904 | tf_op jit(solution)/shard_map/ppermute | solution.py:183
  39.0 1.1 %collective-permute-start.19 = (f32[128,128]{1,0:T(8,128)S(1)}, f32[128,128]{1,0:T(8,128)S(1)}, u32[]{:S(2)}, u32[]{:S(2)}) collective-permute-start(f32[128,128]{1,0:T(8,128)S(1)} %add_add_fusion.3), channel_id=1, source_target_pairs={{0,8},{2,10},{4,12},{6,14},{8,0},{10,2},{12,4},{14,6},{16,24},{18,... | collective-permute-start | bytes 196616 | tf_op jit(solution)/shard_map/ppermute | solution.py:183
  40.1 2.3 %collective-permute-start.20 = (f32[128,128]{1,0:T(8,128)S(1)}, f32[128,128]{1,0:T(8,128)S(1)}, u32[]{:S(2)}, u32[]{:S(2)}) collective-permute-start(f32[128,128]{1,0:T(8,128)S(1)} %add_add_fusion.3), channel_id=1, source_target_pairs={{0,24},{2,26},{4,28},{6,30},{8,16},{10,18},{12,20},{14,22},{16,8},... | collective-permute-start | bytes 196616 | tf_op jit(solution)/shard_map/ppermute | solution.py:183
  42.9 1.7 %collective-permute-start.28 = (f32[136,128]{1,0:T(8,128)S(1)}, f32[136,128]{1,0:T(8,128)S(1)}, u32[]{:S(2)}, u32[]{:S(2)}) collective-permute-start(f32[136,128]{1,0:T(8,128)S(1)} %add_add_fusion.1), channel_id=1, source_target_pairs={{0,8},{2,10},{4,12},{6,14},{8,0},{10,2},{12,4},{14,6},{16,24},{18,... | collective-permute-start | bytes 208904 | tf_op jit(solution)/shard_map/ppermute | solution.py:183
  44.6 2.3 %collective-permute-start.29 = (f32[136,128]{1,0:T(8,128)S(1)}, f32[136,128]{1,0:T(8,128)S(1)}, u32[]{:S(2)}, u32[]{:S(2)}) collective-permute-start(f32[136,128]{1,0:T(8,128)S(1)} %add_add_fusion.1), channel_id=1, source_target_pairs={{0,24},{2,26},{4,28},{6,30},{8,16},{10,18},{12,20},{14,22},{16,8},... | collective-permute-start | bytes 208904 | tf_op jit(solution)/shard_map/ppermute | solution.py:183
  46.9 1.4 %collective-permute-done.21.refs_3_ = f32[128,128]{1,0:T(8,128)S(1)} collective-permute-done((f32[128,128]{1,0:T(8,128)S(1)}, f32[128,128]{1,0:T(8,128)S(1)}, u32[]{:S(2)}, u32[]{:S(2)}) %collective-permute-start.21) | collective-permute-done | bytes 65568 | tf_op jit(solution)/shard_map/ppermute | solution.py:183
  48.4 1.5 %collective-permute-start.22 = (f32[128,128]{1,0:T(8,128)S(1)}, f32[128,128]{1,0:T(8,128)S(1)}, u32[]{:S(2)}, u32[]{:S(2)}) collective-permute-start(f32[128,128]{1,0:T(8,128)S(1)} %get-tuple-element.122), channel_id=1, source_target_pairs={{0,6},{2,4},{4,2},{6,0},{8,14},{10,12},{12,10},{14,8},{16,22},{18,... | collective-permute-start | bytes 196616 | tf_op jit(solution)/shard_map/ppermute | solution.py:183
  49.9 1.0 %collective-permute-start.23 = (f32[128,128]{1,0:T(8,128)S(1)}, f32[128,128]{1,0:T(8,128)S(1)}, u32[]{:S(2)}, u32[]{:S(2)}) collective-permute-start(f32[128,128]{1,0:T(8,128)S(1)} %get-tuple-element.123), channel_id=1, source_target_pairs={{0,4},{2,6},{4,0},{6,2},{8,12},{10,14},{12,8},{14,10},{16,20},{18,... | collective-permute-start | bytes 196616 | tf_op jit(solution)/shard_map/ppermute | solution.py:183
  51.0 1.0 %collective-permute-start.24 = (f32[128,128]{1,0:T(8,128)S(1)}, f32[128,128]{1,0:T(8,128)S(1)}, u32[]{:S(2)}, u32[]{:S(2)}) collective-permute-start(f32[128,128]{1,0:T(8,128)S(1)} %get-tuple-element.124), channel_id=1, source_target_pairs={{0,2},{2,0},{4,6},{6,4},{8,10},{10,8},{12,14},{14,12},{16,18},{18,... | collective-permute-start | bytes 196616 | tf_op jit(solution)/shard_map/ppermute | solution.py:183
  52.6 1.7 %collective-permute-start.31 = (f32[136,128]{1,0:T(8,128)S(1)}, f32[136,128]{1,0:T(8,128)S(1)}, u32[]{:S(2)}, u32[]{:S(2)}) collective-permute-start(f32[136,128]{1,0:T(8,128)S(1)} %get-tuple-element.137), channel_id=1, source_target_pairs={{0,6},{2,4},{4,2},{6,0},{8,14},{10,12},{12,10},{14,8},{16,22},{18,... | collective-permute-start | bytes 208904 | tf_op jit(solution)/shard_map/ppermute | solution.py:183
  54.3 1.0 %collective-permute-start.32 = (f32[136,128]{1,0:T(8,128)S(1)}, f32[136,128]{1,0:T(8,128)S(1)}, u32[]{:S(2)}, u32[]{:S(2)}) collective-permute-start(f32[136,128]{1,0:T(8,128)S(1)} %get-tuple-element.138), channel_id=1, source_target_pairs={{0,4},{2,6},{4,0},{6,2},{8,12},{10,14},{12,8},{14,10},{16,20},{18,... | collective-permute-start | bytes 208904 | tf_op jit(solution)/shard_map/ppermute | solution.py:183
  55.3 0.8 %collective-permute-start.33 = (f32[136,128]{1,0:T(8,128)S(1)}, f32[136,128]{1,0:T(8,128)S(1)}, u32[]{:S(2)}, u32[]{:S(2)}) collective-permute-start(f32[136,128]{1,0:T(8,128)S(1)} %get-tuple-element.139), channel_id=1, source_target_pairs={{0,2},{2,0},{4,6},{6,4},{8,10},{10,8},{12,14},{14,12},{16,18},{18,... | collective-permute-start | bytes 208904 | tf_op jit(solution)/shard_map/ppermute | solution.py:183
  56.1 3.1 %partial.1 = (bf16[256,1024]{1,0:T(8,128)(2,1)}, f32[256,1024]{1,0:T(8,128)S(1)}, f32[256,1024]{1,0:T(8,128)S(1)}) custom-call(s32[1]{0:T(128)} %bitcast.place_ref, bf16[256,1024]{1,0:T(8,128)(2,1)S(1)} %bitcast.16, bf16[256,1024]{1,0:T(8,128)(2,1)S(1)} %bitcast.21, bf16[256,1024]{1,0:T(8,128)(2,1)S(1)} %bitcast.25, ...), custom_call_target="tpu_custom_call" | custom-call | flops 3221225472 | bytes 2097152 | tf_op jit(solution)/shard_map/partial/pallas_call | solution.py:266
  59.6 1.6 %final.1 = (bf16[256,1024]{1,0:T(8,128)(2,1)}, bf16[256,1024]{1,0:T(8,128)(2,1)}) custom-call(s32[1]{0:T(128)} %bitcast.place_ref, bf16[256,1024]{1,0:T(8,128)(2,1)S(1)} %bitcast.22, bf16[256,1024]{1,0:T(8,128)(2,1)S(1)} %bitcast.26, f32[256,1024]{1,0:T(8,128)S(1)} %get-tuple-element.108.key_part_ref, f32[256,1024]{1,0:T(8,128)S(1)} %get-tuple-element.109.value_part_ref, ...), custom_call_target="tpu_custom_call" | custom-call | flops 1073741824 | bytes 2097152 | tf_op jit(solution)/shard_map/final/pallas_call | solution.py:282
  (70 shorter events, 8.6 us)
Async XLA Ops:
  2.2 8.0 %collective-permute-start = (f32[128,128]{1,0:T(8,128)S(1)}, f32[128,128]{1,0:T(8,128)S(1)}, u32[]{:S(2)}, u32[]{:S(2)}) collective-permute-start(f32[128,128]{1,0:T(8,128)S(1)} %get-tuple-element.74), channel_id=1, source_target_pairs={{0,6},{2,4},{4,2},{6,0},{8,14},{10,12},{12,10},{14,8},{16,22},{18,... | collective-permute-start | bytes 196616 | tf_op jit(solution)/shard_map/ppermute | solution.py:183
  6.2 5.1 %collective-permute-start.1 = (f32[128,128]{1,0:T(8,128)S(1)}, f32[128,128]{1,0:T(8,128)S(1)}, u32[]{:S(2)}, u32[]{:S(2)}) collective-permute-start(f32[128,128]{1,0:T(8,128)S(1)} %get-tuple-element.75), channel_id=1, source_target_pairs={{0,4},{2,6},{4,0},{6,2},{8,12},{10,14},{12,8},{14,10},{16,20},{18,... | collective-permute-start | bytes 196616 | tf_op jit(solution)/shard_map/ppermute | solution.py:183
  6.7 4.6 %collective-permute-start.2 = (f32[128,128]{1,0:T(8,128)S(1)}, f32[128,128]{1,0:T(8,128)S(1)}, u32[]{:S(2)}, u32[]{:S(2)}) collective-permute-start(f32[128,128]{1,0:T(8,128)S(1)} %get-tuple-element.76), channel_id=1, source_target_pairs={{0,2},{2,0},{4,6},{6,4},{8,10},{10,8},{12,14},{14,12},{16,18},{18,... | collective-permute-start | bytes 196616 | tf_op jit(solution)/shard_map/ppermute | solution.py:183
  6.8 6.2 %collective-permute-start.8 = (f32[128,128]{1,0:T(8,128)S(1)}, f32[128,128]{1,0:T(8,128)S(1)}, u32[]{:S(2)}, u32[]{:S(2)}) collective-permute-start(f32[128,128]{1,0:T(8,128)S(1)} %get-tuple-element.94), channel_id=1, source_target_pairs={{0,6},{2,4},{4,2},{6,0},{8,14},{10,12},{12,10},{14,8},{16,22},{18,... | collective-permute-start | bytes 196616 | tf_op jit(solution)/shard_map/ppermute | solution.py:183
  11.3 5.0 %collective-permute-start.3 = (f32[128,128]{1,0:T(8,128)S(1)}, f32[128,128]{1,0:T(8,128)S(1)}, u32[]{:S(2)}, u32[]{:S(2)}) collective-permute-start(f32[128,128]{1,0:T(8,128)S(1)} %add_add_fusion.5), channel_id=1, source_target_pairs={{0,8},{2,10},{4,12},{6,14},{8,0},{10,2},{12,4},{14,6},{16,24},{18,... | collective-permute-start | bytes 196616 | tf_op jit(solution)/shard_map/ppermute | solution.py:183
  14.5 4.5 %collective-permute-start.11 = (f32[128,128]{1,0:T(8,128)S(1)}, f32[128,128]{1,0:T(8,128)S(1)}, u32[]{:S(2)}, u32[]{:S(2)}) collective-permute-start(f32[128,128]{1,0:T(8,128)S(1)} %add_add_fusion.4), channel_id=1, source_target_pairs={{0,8},{2,10},{4,12},{6,14},{8,0},{10,2},{12,4},{14,6},{16,24},{18,... | collective-permute-start | bytes 196616 | tf_op jit(solution)/shard_map/ppermute | solution.py:183
  16.3 6.6 %collective-permute-start.4 = (f32[128,128]{1,0:T(8,128)S(1)}, f32[128,128]{1,0:T(8,128)S(1)}, u32[]{:S(2)}, u32[]{:S(2)}) collective-permute-start(f32[128,128]{1,0:T(8,128)S(1)} %add.72), channel_id=1, source_target_pairs={{0,16},{2,18},{4,20},{6,22},{8,24},{10,26},{12,28},{14,30},{16,0},... | collective-permute-start | bytes 196616 | tf_op jit(solution)/shard_map/ppermute | solution.py:183
  19.0 7.7 %collective-permute-start.12 = (f32[128,128]{1,0:T(8,128)S(1)}, f32[128,128]{1,0:T(8,128)S(1)}, u32[]{:S(2)}, u32[]{:S(2)}) collective-permute-start(f32[128,128]{1,0:T(8,128)S(1)} %add.77), channel_id=1, source_target_pairs={{0,16},{2,18},{4,20},{6,22},{8,24},{10,26},{12,28},{14,30},{16,0},... | collective-permute-start | bytes 196616 | tf_op jit(solution)/shard_map/ppermute | solution.py:183
  23.1 5.7 %collective-permute-start.5 = (f32[128,128]{1,0:T(8,128)S(1)}, f32[128,128]{1,0:T(8,128)S(1)}, u32[]{:S(2)}, u32[]{:S(2)}) collective-permute-start(f32[128,128]{1,0:T(8,128)S(1)} %get-tuple-element.89), channel_id=1, source_target_pairs={{0,6},{2,4},{4,2},{6,0},{8,14},{10,12},{12,10},{14,8},{16,22},{18,... | collective-permute-start | bytes 196616 | tf_op jit(solution)/shard_map/ppermute | solution.py:183
  24.6 5.7 %collective-permute-start.6 = (f32[128,128]{1,0:T(8,128)S(1)}, f32[128,128]{1,0:T(8,128)S(1)}, u32[]{:S(2)}, u32[]{:S(2)}) collective-permute-start(f32[128,128]{1,0:T(8,128)S(1)} %get-tuple-element.90), channel_id=1, source_target_pairs={{0,4},{2,6},{4,0},{6,2},{8,12},{10,14},{12,8},{14,10},{16,20},{18,... | collective-permute-start | bytes 196616 | tf_op jit(solution)/shard_map/ppermute | solution.py:183
  25.1 5.2 %collective-permute-start.7 = (f32[128,128]{1,0:T(8,128)S(1)}, f32[128,128]{1,0:T(8,128)S(1)}, u32[]{:S(2)}, u32[]{:S(2)}) collective-permute-start(f32[128,128]{1,0:T(8,128)S(1)} %get-tuple-element.91), channel_id=1, source_target_pairs={{0,2},{2,0},{4,6},{6,4},{8,10},{10,8},{12,14},{14,12},{16,18},{18,... | collective-permute-start | bytes 196616 | tf_op jit(solution)/shard_map/ppermute | solution.py:183
  26.7 6.8 %collective-permute-start.13 = (f32[128,128]{1,0:T(8,128)S(1)}, f32[128,128]{1,0:T(8,128)S(1)}, u32[]{:S(2)}, u32[]{:S(2)}) collective-permute-start(f32[128,128]{1,0:T(8,128)S(1)} %get-tuple-element.102), channel_id=1, source_target_pairs={{0,6},{2,4},{4,2},{6,0},{8,14},{10,12},{12,10},{14,8},{16,22},{18,... | collective-permute-start | bytes 196616 | tf_op jit(solution)/shard_map/ppermute | solution.py:183
  28.3 6.4 %collective-permute-start.14 = (f32[128,128]{1,0:T(8,128)S(1)}, f32[128,128]{1,0:T(8,128)S(1)}, u32[]{:S(2)}, u32[]{:S(2)}) collective-permute-start(f32[128,128]{1,0:T(8,128)S(1)} %get-tuple-element.103), channel_id=1, source_target_pairs={{0,4},{2,6},{4,0},{6,2},{8,12},{10,14},{12,8},{14,10},{16,20},{18,... | collective-permute-start | bytes 196616 | tf_op jit(solution)/shard_map/ppermute | solution.py:183
  28.7 5.9 %collective-permute-start.15 = (f32[128,128]{1,0:T(8,128)S(1)}, f32[128,128]{1,0:T(8,128)S(1)}, u32[]{:S(2)}, u32[]{:S(2)}) collective-permute-start(f32[128,128]{1,0:T(8,128)S(1)} %get-tuple-element.104), channel_id=1, source_target_pairs={{0,2},{2,0},{4,6},{6,4},{8,10},{10,8},{12,14},{14,12},{16,18},{18,... | collective-permute-start | bytes 196616 | tf_op jit(solution)/shard_map/ppermute | solution.py:183
  31.1 6.7 %collective-permute-start.16 = (f32[128,128]{1,0:T(8,128)S(1)}, f32[128,128]{1,0:T(8,128)S(1)}, u32[]{:S(2)}, u32[]{:S(2)}) collective-permute-start(f32[128,128]{1,0:T(8,128)S(1)} %get-tuple-element.111), channel_id=1, source_target_pairs={{0,6},{2,4},{4,2},{6,0},{8,14},{10,12},{12,10},{14,8},{16,22},{18,... | collective-permute-start | bytes 196616 | tf_op jit(solution)/shard_map/ppermute | solution.py:183
  32.6 6.3 %collective-permute-start.17 = (f32[128,128]{1,0:T(8,128)S(1)}, f32[128,128]{1,0:T(8,128)S(1)}, u32[]{:S(2)}, u32[]{:S(2)}) collective-permute-start(f32[128,128]{1,0:T(8,128)S(1)} %get-tuple-element.112), channel_id=1, source_target_pairs={{0,4},{2,6},{4,0},{6,2},{8,12},{10,14},{12,8},{14,10},{16,20},{18,... | collective-permute-start | bytes 196616 | tf_op jit(solution)/shard_map/ppermute | solution.py:183
  33.5 5.4 %collective-permute-start.18 = (f32[128,128]{1,0:T(8,128)S(1)}, f32[128,128]{1,0:T(8,128)S(1)}, u32[]{:S(2)}, u32[]{:S(2)}) collective-permute-start(f32[128,128]{1,0:T(8,128)S(1)} %get-tuple-element.113), channel_id=1, source_target_pairs={{0,2},{2,0},{4,6},{6,4},{8,10},{10,8},{12,14},{14,12},{16,18},{18,... | collective-permute-start | bytes 196616 | tf_op jit(solution)/shard_map/ppermute | solution.py:183
  35.4 7.0 %collective-permute-start.25 = (f32[136,128]{1,0:T(8,128)S(1)}, f32[136,128]{1,0:T(8,128)S(1)}, u32[]{:S(2)}, u32[]{:S(2)}) collective-permute-start(f32[136,128]{1,0:T(8,128)S(1)} %get-tuple-element.126), channel_id=1, source_target_pairs={{0,6},{2,4},{4,2},{6,0},{8,14},{10,12},{12,10},{14,8},{16,22},{18,... | collective-permute-start | bytes 208904 | tf_op jit(solution)/shard_map/ppermute | solution.py:183
  36.9 6.0 %collective-permute-start.26 = (f32[136,128]{1,0:T(8,128)S(1)}, f32[136,128]{1,0:T(8,128)S(1)}, u32[]{:S(2)}, u32[]{:S(2)}) collective-permute-start(f32[136,128]{1,0:T(8,128)S(1)} %get-tuple-element.127), channel_id=1, source_target_pairs={{0,4},{2,6},{4,0},{6,2},{8,12},{10,14},{12,8},{14,10},{16,20},{18,... | collective-permute-start | bytes 208904 | tf_op jit(solution)/shard_map/ppermute | solution.py:183
  37.8 5.1 %collective-permute-start.27 = (f32[136,128]{1,0:T(8,128)S(1)}, f32[136,128]{1,0:T(8,128)S(1)}, u32[]{:S(2)}, u32[]{:S(2)}) collective-permute-start(f32[136,128]{1,0:T(8,128)S(1)} %get-tuple-element.128), channel_id=1, source_target_pairs={{0,2},{2,0},{4,6},{6,4},{8,10},{10,8},{12,14},{14,12},{16,18},{18,... | collective-permute-start | bytes 208904 | tf_op jit(solution)/shard_map/ppermute | solution.py:183
  39.0 7.9 %collective-permute-start.19 = (f32[128,128]{1,0:T(8,128)S(1)}, f32[128,128]{1,0:T(8,128)S(1)}, u32[]{:S(2)}, u32[]{:S(2)}) collective-permute-start(f32[128,128]{1,0:T(8,128)S(1)} %add_add_fusion.3), channel_id=1, source_target_pairs={{0,8},{2,10},{4,12},{6,14},{8,0},{10,2},{12,4},{14,6},{16,24},{18,... | collective-permute-start | bytes 196616 | tf_op jit(solution)/shard_map/ppermute | solution.py:183
  40.1 6.8 %collective-permute-start.20 = (f32[128,128]{1,0:T(8,128)S(1)}, f32[128,128]{1,0:T(8,128)S(1)}, u32[]{:S(2)}, u32[]{:S(2)}) collective-permute-start(f32[128,128]{1,0:T(8,128)S(1)} %add_add_fusion.3), channel_id=1, source_target_pairs={{0,24},{2,26},{4,28},{6,30},{8,16},{10,18},{12,20},{14,22},{16,8},... | collective-permute-start | bytes 196616 | tf_op jit(solution)/shard_map/ppermute | solution.py:183
  42.4 5.9 %collective-permute-start.21 = (f32[128,128]{1,0:T(8,128)S(1)}, f32[128,128]{1,0:T(8,128)S(1)}, u32[]{:S(2)}, u32[]{:S(2)}) collective-permute-start(f32[128,128]{1,0:T(8,128)S(1)} %add_add_fusion.3), channel_id=1, source_target_pairs={{0,16},{2,18},{4,20},{6,22},{8,24},{10,26},{12,28},{14,30},{16,0},... | collective-permute-start | bytes 196616 | tf_op jit(solution)/shard_map/ppermute | solution.py:183
  42.9 8.0 %collective-permute-start.28 = (f32[136,128]{1,0:T(8,128)S(1)}, f32[136,128]{1,0:T(8,128)S(1)}, u32[]{:S(2)}, u32[]{:S(2)}) collective-permute-start(f32[136,128]{1,0:T(8,128)S(1)} %add_add_fusion.1), channel_id=1, source_target_pairs={{0,8},{2,10},{4,12},{6,14},{8,0},{10,2},{12,4},{14,6},{16,24},{18,... | collective-permute-start | bytes 208904 | tf_op jit(solution)/shard_map/ppermute | solution.py:183
  44.6 7.3 %collective-permute-start.29 = (f32[136,128]{1,0:T(8,128)S(1)}, f32[136,128]{1,0:T(8,128)S(1)}, u32[]{:S(2)}, u32[]{:S(2)}) collective-permute-start(f32[136,128]{1,0:T(8,128)S(1)} %add_add_fusion.1), channel_id=1, source_target_pairs={{0,24},{2,26},{4,28},{6,30},{8,16},{10,18},{12,20},{14,22},{16,8},... | collective-permute-start | bytes 208904 | tf_op jit(solution)/shard_map/ppermute | solution.py:183
  46.9 5.5 %collective-permute-start.30 = (f32[136,128]{1,0:T(8,128)S(1)}, f32[136,128]{1,0:T(8,128)S(1)}, u32[]{:S(2)}, u32[]{:S(2)}) collective-permute-start(f32[136,128]{1,0:T(8,128)S(1)} %add_add_fusion.1), channel_id=1, source_target_pairs={{0,16},{2,18},{4,20},{6,22},{8,24},{10,26},{12,28},{14,30},{16,0},... | collective-permute-start | bytes 208904 | tf_op jit(solution)/shard_map/ppermute | solution.py:183
  48.4 6.9 %collective-permute-start.22 = (f32[128,128]{1,0:T(8,128)S(1)}, f32[128,128]{1,0:T(8,128)S(1)}, u32[]{:S(2)}, u32[]{:S(2)}) collective-permute-start(f32[128,128]{1,0:T(8,128)S(1)} %get-tuple-element.122), channel_id=1, source_target_pairs={{0,6},{2,4},{4,2},{6,0},{8,14},{10,12},{12,10},{14,8},{16,22},{18,... | collective-permute-start | bytes 196616 | tf_op jit(solution)/shard_map/ppermute | solution.py:183
  49.9 9.3 %collective-permute-start.23 = (f32[128,128]{1,0:T(8,128)S(1)}, f32[128,128]{1,0:T(8,128)S(1)}, u32[]{:S(2)}, u32[]{:S(2)}) collective-permute-start(f32[128,128]{1,0:T(8,128)S(1)} %get-tuple-element.123), channel_id=1, source_target_pairs={{0,4},{2,6},{4,0},{6,2},{8,12},{10,14},{12,8},{14,10},{16,20},{18,... | collective-permute-start | bytes 196616 | tf_op jit(solution)/shard_map/ppermute | solution.py:183
  51.0 8.3 %collective-permute-start.24 = (f32[128,128]{1,0:T(8,128)S(1)}, f32[128,128]{1,0:T(8,128)S(1)}, u32[]{:S(2)}, u32[]{:S(2)}) collective-permute-start(f32[128,128]{1,0:T(8,128)S(1)} %get-tuple-element.124), channel_id=1, source_target_pairs={{0,2},{2,0},{4,6},{6,4},{8,10},{10,8},{12,14},{14,12},{16,18},{18,... | collective-permute-start | bytes 196616 | tf_op jit(solution)/shard_map/ppermute | solution.py:183
  52.6 6.7 %collective-permute-start.31 = (f32[136,128]{1,0:T(8,128)S(1)}, f32[136,128]{1,0:T(8,128)S(1)}, u32[]{:S(2)}, u32[]{:S(2)}) collective-permute-start(f32[136,128]{1,0:T(8,128)S(1)} %get-tuple-element.137), channel_id=1, source_target_pairs={{0,6},{2,4},{4,2},{6,0},{8,14},{10,12},{12,10},{14,8},{16,22},{18,... | collective-permute-start | bytes 208904 | tf_op jit(solution)/shard_map/ppermute | solution.py:183
  54.3 4.9 %collective-permute-start.32 = (f32[136,128]{1,0:T(8,128)S(1)}, f32[136,128]{1,0:T(8,128)S(1)}, u32[]{:S(2)}, u32[]{:S(2)}) collective-permute-start(f32[136,128]{1,0:T(8,128)S(1)} %get-tuple-element.138), channel_id=1, source_target_pairs={{0,4},{2,6},{4,0},{6,2},{8,12},{10,14},{12,8},{14,10},{16,20},{18,... | collective-permute-start | bytes 208904 | tf_op jit(solution)/shard_map/ppermute | solution.py:183
  55.3 4.3 %collective-permute-start.33 = (f32[136,128]{1,0:T(8,128)S(1)}, f32[136,128]{1,0:T(8,128)S(1)}, u32[]{:S(2)}, u32[]{:S(2)}) collective-permute-start(f32[136,128]{1,0:T(8,128)S(1)} %get-tuple-element.139), channel_id=1, source_target_pairs={{0,2},{2,0},{4,6},{6,4},{8,10},{10,8},{12,14},{14,12},{16,18},{18,... | collective-permute-start | bytes 208904 | tf_op jit(solution)/shard_map/ppermute | solution.py:183
  (8 other events, 60.8 us)

commit v21 on v19

--- a/solution.py
+++ b/solution.py
@@ -159,10 +159,11 @@
     )
 
 
-def exchange_steps(direct):
+def exchange_steps(near_first):
     count, base, steps = lax.axis_size("seq"), GROUP, []
     while base < count:
-        masks = [base, 3 * base, 2 * base] if direct and 4 * base <= count else [base]
+        masks = [base, 3 * base, 2 * base] if near_first else [3 * base, 2 * base, base]
+        masks = masks if 4 * base <= count else [base]
         steps.append(masks)
         base *= len(masks) + 1
     return steps
@@ -186,7 +187,6 @@
     total, arrived, steps, result = plane_sum(held), [], exchange_steps(reverse), None
     for masks in steps:
         if beside and masks == steps[-1]:
-            total, operands = lax.optimization_barrier((total, operands))
             result = beside(*operands)
         got = [swap(total, mask) for mask in masks]
         if result is not None:
@@ -237,7 +237,8 @@
         lambda place_ref, *refs: inner_body(*refs), [wide] * 3, wide, full_float, 16 * unit, "inner"
     )
     first, second = [lax.optimization_barrier(plane_swap(deltas[chain])) for chain in chains]
-    state, inner = carried_in(first, False, place, inner_call, (place, query, key, value))
+    second, operands = lax.optimization_barrier((second, (place, query, key, value)))
+    state, inner = carried_in(first, False, place, inner_call, operands)
     states = [state, carried_in(second, False, place)[0]]
     attns, later = [], []
     for chain in range(CHAINS):

time: 61.9 us -> 61.2 us (0.989)
  waiting for transfers between devices: 4.88 us -> 4.22 us
    ppermute x34 -> x36, waiting for transfers between devices: 4.88 us -> 4.22 us  [swap(): lax.ppermute(array, 'seq', [(s, s ^ mask) for s in range(lax.axis_size('s...]
    ppermute x34 -> x36, starting transfers between devices: 46.2 us -> 46.1 us  [swap(): lax.ppermute(array, 'seq', [(s, s ^ mask) for s in range(lax.axis_size('s...]
  transfers between devices with their start and end apart: 35 -> 37, of which waited for: 9 -> 4; matrix products, arithmetic and copies ran while one was open for 0% -> 0% of each run, Pallas kernels for 12% -> 12%
where the time goes in v21:
time: 61.2 us; the launch traced here: 61 us
  starting transfers between devices  46.1 us (75%)
  Pallas kernels  9.06 us (15%)
  waiting for transfers between devices  4.22 us (7%)
  between operations  0.82 us (1%)
  other arithmetic  0.75 us (1%)
    ppermute x36, starting transfers between devices, swap(): lax.ppermute(array, 'seq', [(s, s ^ mask) for s in range(lax.axis_size('s...  46.1 us
    ppermute x36, waiting for transfers between devices, swap(): lax.ppermute(array, 'seq', [(s, s ^ mask) for s in range(lax.axis_size('s...  4.22 us
    pallas_call x1, Pallas kernels, local(): call(partial_body, [wide] * 3 + [half] * CHAINS + [short] * HEADS, [wide]...  3.09 us
    pallas_call x1, Pallas kernels, local(): call(delta_body, [pl.BlockSpec(memory_space=pltpu.HBM)] * 2, [short] * HE...  1.61 us
    pallas_call x1, Pallas kernels, local(): call(final_body, [wide] * 4 + [tall] * HEADS, [chunk] * 2, [full_low] * 2...  1.61 us
    pallas_call x2, Pallas kernels, local(): call(functools.partial(norm_body, chain), [wide, wide, wide, whole(1, HEA...  1.48 us
  transfers between devices with their start and end apart: 37, of which 4 were waited for; matrix products, arithmetic and copies ran while one was open for 0% of the time, Pallas kernels for 12%

profile of v21, /device:TPU:0, one launch (start us, length us, event | category | flops | bytes accessed | tf_op | source)
XLA Modules:
  0.0 61.0 jit_solution(3185304957678336795)
XLA Ops:
  0.7 1.6 %delta.1 = (f32[128,128]{1,0:T(8,128)S(1)}, f32[128,128]{1,0:T(8,128)S(1)}, f32[128,128]{1,0:T(8,128)S(1)}, f32[128,128]{1,0:T(8,128)S(1)}, f32[128,128]{1,0:T(8...) custom-call(s32[1]{0:T(128)} %bitcast.place_ref, bf16[256,1024]{1,0:T(8,128)(2,1)} %bitcast.19, ...), custom_call_target="tpu_custom_call" | custom-call | flops 402653184 | bytes 2097152 | tf_op jit(solution)/shard_map/delta/pallas_call | solution.py:226
  2.3 4.0 %collective-permute-start = (f32[128,128]{1,0:T(8,128)S(1)}, f32[128,128]{1,0:T(8,128)S(1)}, u32[]{:S(2)}, u32[]{:S(2)}) collective-permute-start(f32[128,128]{1,0:T(8,128)S(1)} %get-tuple-element.81), channel_id=1, source_target_pairs={{0,6},{2,4},{4,2},{6,0},{8,14},{10,12},{12,10},{14,8},{16,22},{18,... | collective-permute-start | bytes 196616 | tf_op jit(solution)/shard_map/ppermute | solution.py:175
  6.9 2.8 %collective-permute-start.6 = (f32[128,128]{1,0:T(8,128)S(1)}, f32[128,128]{1,0:T(8,128)S(1)}, u32[]{:S(2)}, u32[]{:S(2)}) collective-permute-start(f32[128,128]{1,0:T(8,128)S(1)} %get-tuple-element.89), channel_id=1, source_target_pairs={{0,6},{2,4},{4,2},{6,0},{8,14},{10,12},{12,10},{14,8},{16,22},{18,... | collective-permute-start | bytes 196616 | tf_op jit(solution)/shard_map/ppermute | solution.py:175
  11.3 3.7 %collective-permute-start.3 = (f32[128,128]{1,0:T(8,128)S(1)}, f32[128,128]{1,0:T(8,128)S(1)}, u32[]{:S(2)}, u32[]{:S(2)}) collective-permute-start(f32[128,128]{1,0:T(8,128)S(1)} %add_add_fusion.7), channel_id=1, source_target_pairs={{0,24},{2,26},{4,28},{6,30},{8,16},{10,18},{12,20},{14,22},{16,8},... | collective-permute-start | bytes 196616 | tf_op jit(solution)/shard_map/ppermute | solution.py:175
  15.0 0.8 %collective-permute-start.5 = (f32[128,128]{1,0:T(8,128)S(1)}, f32[128,128]{1,0:T(8,128)S(1)}, u32[]{:S(2)}, u32[]{:S(2)}) collective-permute-start(f32[128,128]{1,0:T(8,128)S(1)} %add_add_fusion.7), channel_id=1, source_target_pairs={{0,8},{2,10},{4,12},{6,14},{8,0},{10,2},{12,4},{14,6},{16,24},{18,... | collective-permute-start | bytes 196616 | tf_op jit(solution)/shard_map/ppermute | solution.py:175
  15.8 3.7 %collective-permute-start.12 = (f32[128,128]{1,0:T(8,128)S(1)}, f32[128,128]{1,0:T(8,128)S(1)}, u32[]{:S(2)}, u32[]{:S(2)}) collective-permute-start(f32[128,128]{1,0:T(8,128)S(1)} %add_add_fusion.5), channel_id=1, source_target_pairs={{0,24},{2,26},{4,28},{6,30},{8,16},{10,18},{12,20},{14,22},{16,8},... | collective-permute-start | bytes 196616 | tf_op jit(solution)/shard_map/ppermute | solution.py:175
  19.5 0.9 %inner.1.inner_ref = f32[256,1024]{1,0:T(8,128)S(1)} custom-call(s32[1]{0:T(128)} %bitcast.place_ref, bf16[256,1024]{1,0:T(8,128)(2,1)S(1)} %bitcast.13, bf16[256,1024]{1,0:T(8,128)(2,1)S(1)} %bitcast.20, bf16[256,1024]{1,0:T(8,128)(2,1)S(1)} %bitcast.24), custom_call_target="tpu_custom_call" | custom-call | flops 1073741824 | bytes 2097152 | tf_op jit(solution)/shard_map/inner/pallas_call | solution.py:190
  20.5 0.8 %collective-permute-start.14 = (f32[128,128]{1,0:T(8,128)S(1)}, f32[128,128]{1,0:T(8,128)S(1)}, u32[]{:S(2)}, u32[]{:S(2)}) collective-permute-start(f32[128,128]{1,0:T(8,128)S(1)} %add_add_fusion.5), channel_id=1, source_target_pairs={{0,8},{2,10},{4,12},{6,14},{8,0},{10,2},{12,4},{14,6},{16,24},{18,... | collective-permute-start | bytes 196616 | tf_op jit(solution)/shard_map/ppermute | solution.py:175
  21.3 1.6 %collective-permute-done.4.refs_2_ = f32[128,128]{1,0:T(8,128)S(1)} collective-permute-done((f32[128,128]{1,0:T(8,128)S(1)}, f32[128,128]{1,0:T(8,128)S(1)}, u32[]{:S(2)}, u32[]{:S(2)}) %collective-permute-start.4) | collective-permute-done | bytes 65568 | tf_op jit(solution)/shard_map/ppermute | solution.py:175
  23.0 1.9 %collective-permute-start.9 = (f32[128,128]{1,0:T(8,128)S(1)}, f32[128,128]{1,0:T(8,128)S(1)}, u32[]{:S(2)}, u32[]{:S(2)}) collective-permute-start(f32[128,128]{1,0:T(8,128)S(1)} %get-tuple-element.105), channel_id=1, source_target_pairs={{0,6},{2,4},{4,2},{6,0},{8,14},{10,12},{12,10},{14,8},{16,22},{18,... | collective-permute-start | bytes 196616 | tf_op jit(solution)/shard_map/ppermute | solution.py:175
  24.9 1.1 %collective-permute-start.10 = (f32[128,128]{1,0:T(8,128)S(1)}, f32[128,128]{1,0:T(8,128)S(1)}, u32[]{:S(2)}, u32[]{:S(2)}) collective-permute-start(f32[128,128]{1,0:T(8,128)S(1)} %get-tuple-element.106), channel_id=1, source_target_pairs={{0,4},{2,6},{4,0},{6,2},{8,12},{10,14},{12,8},{14,10},{16,20},{18,... | collective-permute-start | bytes 196616 | tf_op jit(solution)/shard_map/ppermute | solution.py:175
  26.7 1.9 %collective-permute-start.15 = (f32[128,128]{1,0:T(8,128)S(1)}, f32[128,128]{1,0:T(8,128)S(1)}, u32[]{:S(2)}, u32[]{:S(2)}) collective-permute-start(f32[128,128]{1,0:T(8,128)S(1)} %get-tuple-element.117), channel_id=1, source_target_pairs={{0,6},{2,4},{4,2},{6,0},{8,14},{10,12},{12,10},{14,8},{16,22},{18,... | collective-permute-start | bytes 196616 | tf_op jit(solution)/shard_map/ppermute | solution.py:175
  28.5 1.1 %collective-permute-start.16 = (f32[128,128]{1,0:T(8,128)S(1)}, f32[128,128]{1,0:T(8,128)S(1)}, u32[]{:S(2)}, u32[]{:S(2)}) collective-permute-start(f32[128,128]{1,0:T(8,128)S(1)} %get-tuple-element.118), channel_id=1, source_target_pairs={{0,4},{2,6},{4,0},{6,2},{8,12},{10,14},{12,8},{14,10},{16,20},{18,... | collective-permute-start | bytes 196616 | tf_op jit(solution)/shard_map/ppermute | solution.py:175
  29.7 0.7 %collective-permute-start.17 = (f32[128,128]{1,0:T(8,128)S(1)}, f32[128,128]{1,0:T(8,128)S(1)}, u32[]{:S(2)}, u32[]{:S(2)}) collective-permute-start(f32[128,128]{1,0:T(8,128)S(1)} %get-tuple-element.119), channel_id=1, source_target_pairs={{0,2},{2,0},{4,6},{6,4},{8,10},{10,8},{12,14},{14,12},{16,18},{18,... | collective-permute-start | bytes 196616 | tf_op jit(solution)/shard_map/ppermute | solution.py:175
  30.5 0.7 %norm.2 = (bf16[256,512]{1,0:T(8,128)(2,1)S(1)}, f32[136,128]{1,0:T(8,128)S(1)}, f32[136,128]{1,0:T(8,128)S(1)}, f32[136,128]{1,0:T(8,128)S(1)}, f32[136,128]{1,0:T(8,128)S(1)}) custom-call(s32[1]{0:T(128)} %bitcast.place_ref, bf16[256,1024]{1,0:T(8,128)(2,1)S(1)} %bitcast.14, bf16[256,1024]{1,0:T(8,128)(2,1)S(1)} %bitcast.11, ...), custom_call_target="tpu_custom_call" | custom-call | flops 536870912 | bytes 2097152 | tf_op jit(solution)/shard_map/norm/pallas_call | solution.py:245
  31.2 1.8 %collective-permute-start.18 = (f32[136,128]{1,0:T(8,128)S(1)}, f32[136,128]{1,0:T(8,128)S(1)}, u32[]{:S(2)}, u32[]{:S(2)}) collective-permute-start(f32[136,128]{1,0:T(8,128)S(1)} %get-tuple-element.125), channel_id=1, source_target_pairs={{0,6},{2,4},{4,2},{6,0},{8,14},{10,12},{12,10},{14,8},{16,22},{18,... | collective-permute-start | bytes 208904 | tf_op jit(solution)/shard_map/ppermute | solution.py:175
  33.0 1.1 %collective-permute-start.19 = (f32[136,128]{1,0:T(8,128)S(1)}, f32[136,128]{1,0:T(8,128)S(1)}, u32[]{:S(2)}, u32[]{:S(2)}) collective-permute-start(f32[136,128]{1,0:T(8,128)S(1)} %get-tuple-element.126), channel_id=1, source_target_pairs={{0,4},{2,6},{4,0},{6,2},{8,12},{10,14},{12,8},{14,10},{16,20},{18,... | collective-permute-start | bytes 208904 | tf_op jit(solution)/shard_map/ppermute | solution.py:175
  34.1 0.7 %collective-permute-start.20 = (f32[136,128]{1,0:T(8,128)S(1)}, f32[136,128]{1,0:T(8,128)S(1)}, u32[]{:S(2)}, u32[]{:S(2)}) collective-permute-start(f32[136,128]{1,0:T(8,128)S(1)} %get-tuple-element.127), channel_id=1, source_target_pairs={{0,2},{2,0},{4,6},{6,4},{8,10},{10,8},{12,14},{14,12},{16,18},{18,... | collective-permute-start | bytes 208904 | tf_op jit(solution)/shard_map/ppermute | solution.py:175
  34.8 0.7 %norm.3 = (bf16[256,512]{1,0:T(8,128)(2,1)S(1)}, f32[136,128]{1,0:T(8,128)S(1)}, f32[136,128]{1,0:T(8,128)S(1)}, f32[136,128]{1,0:T(8,128)S(1)}, f32[136,128]{1,0:T(8,128)S(1)}) custom-call(s32[1]{0:T(128)} %bitcast.place_ref, bf16[256,1024]{1,0:T(8,128)(2,1)S(1)} %bitcast.15, bf16[256,1024]{1,0:T(8,128)(2,1)S(1)} %bitcast.12, ...), custom_call_target="tpu_custom_call" | custom-call | flops 536870912 | bytes 2097152 | tf_op jit(solution)/shard_map/norm/pallas_call | solution.py:245
  35.5 1.8 %collective-permute-start.27 = (f32[136,128]{1,0:T(8,128)S(1)}, f32[136,128]{1,0:T(8,128)S(1)}, u32[]{:S(2)}, u32[]{:S(2)}) collective-permute-start(f32[136,128]{1,0:T(8,128)S(1)} %get-tuple-element.140), channel_id=1, source_target_pairs={{0,6},{2,4},{4,2},{6,0},{8,14},{10,12},{12,10},{14,8},{16,22},{18,... | collective-permute-start | bytes 208904 | tf_op jit(solution)/shard_map/ppermute | solution.py:175
  37.3 1.1 %collective-permute-start.28 = (f32[136,128]{1,0:T(8,128)S(1)}, f32[136,128]{1,0:T(8,128)S(1)}, u32[]{:S(2)}, u32[]{:S(2)}) collective-permute-start(f32[136,128]{1,0:T(8,128)S(1)} %get-tuple-element.141), channel_id=1, source_target_pairs={{0,4},{2,6},{4,0},{6,2},{8,12},{10,14},{12,8},{14,10},{16,20},{18,... | collective-permute-start | bytes 208904 | tf_op jit(solution)/shard_map/ppermute | solution.py:175
  39.2 2.4 %collective-permute-start.22 = (f32[136,128]{1,0:T(8,128)S(1)}, f32[136,128]{1,0:T(8,128)S(1)}, u32[]{:S(2)}, u32[]{:S(2)}) collective-permute-start(f32[136,128]{1,0:T(8,128)S(1)} %add_add_fusion.3), channel_id=1, source_target_pairs={{0,24},{2,26},{4,28},{6,30},{8,16},{10,18},{12,20},{14,22},{16,8},... | collective-permute-start | bytes 208904 | tf_op jit(solution)/shard_map/ppermute | solution.py:175
  41.6 1.1 %collective-permute-start.23 = (f32[136,128]{1,0:T(8,128)S(1)}, f32[136,128]{1,0:T(8,128)S(1)}, u32[]{:S(2)}, u32[]{:S(2)}) collective-permute-start(f32[136,128]{1,0:T(8,128)S(1)} %add_add_fusion.3), channel_id=1, source_target_pairs={{0,16},{2,18},{4,20},{6,22},{8,24},{10,26},{12,28},{14,30},{16,0},... | collective-permute-start | bytes 208904 | tf_op jit(solution)/shard_map/ppermute | solution.py:175
  42.7 1.0 %collective-permute-start.30 = (f32[136,128]{1,0:T(8,128)S(1)}, f32[136,128]{1,0:T(8,128)S(1)}, u32[]{:S(2)}, u32[]{:S(2)}) collective-permute-start(f32[136,128]{1,0:T(8,128)S(1)} %add_add_fusion.1), channel_id=1, source_target_pairs={{0,8},{2,10},{4,12},{6,14},{8,0},{10,2},{12,4},{14,6},{16,24},{18,... | collective-permute-start | bytes 208904 | tf_op jit(solution)/shard_map/ppermute | solution.py:175
  43.7 2.3 %collective-permute-start.31 = (f32[136,128]{1,0:T(8,128)S(1)}, f32[136,128]{1,0:T(8,128)S(1)}, u32[]{:S(2)}, u32[]{:S(2)}) collective-permute-start(f32[136,128]{1,0:T(8,128)S(1)} %add_add_fusion.1), channel_id=1, source_target_pairs={{0,24},{2,26},{4,28},{6,30},{8,16},{10,18},{12,20},{14,22},{16,8},... | collective-permute-start | bytes 208904 | tf_op jit(solution)/shard_map/ppermute | solution.py:175
  46.3 1.5 %collective-permute-done.23.refs_3_ = f32[136,128]{1,0:T(8,128)S(1)} collective-permute-done((f32[136,128]{1,0:T(8,128)S(1)}, f32[136,128]{1,0:T(8,128)S(1)}, u32[]{:S(2)}, u32[]{:S(2)}) %collective-permute-start.23) | collective-permute-done | bytes 69664 | tf_op jit(solution)/shard_map/ppermute | solution.py:175
  47.9 1.8 %collective-permute-start.24 = (f32[136,128]{1,0:T(8,128)S(1)}, f32[136,128]{1,0:T(8,128)S(1)}, u32[]{:S(2)}, u32[]{:S(2)}) collective-permute-start(f32[136,128]{1,0:T(8,128)S(1)} %get-tuple-element.136), channel_id=1, source_target_pairs={{0,6},{2,4},{4,2},{6,0},{8,14},{10,12},{12,10},{14,8},{16,22},{18,... | collective-permute-start | bytes 208904 | tf_op jit(solution)/shard_map/ppermute | solution.py:175
  49.7 1.1 %collective-permute-start.25 = (f32[136,128]{1,0:T(8,128)S(1)}, f32[136,128]{1,0:T(8,128)S(1)}, u32[]{:S(2)}, u32[]{:S(2)}) collective-permute-start(f32[136,128]{1,0:T(8,128)S(1)} %get-tuple-element.137), channel_id=1, source_target_pairs={{0,4},{2,6},{4,0},{6,2},{8,12},{10,14},{12,8},{14,10},{16,20},{18,... | collective-permute-start | bytes 208904 | tf_op jit(solution)/shard_map/ppermute | solution.py:175
  51.6 1.8 %collective-permute-start.33 = (f32[136,128]{1,0:T(8,128)S(1)}, f32[136,128]{1,0:T(8,128)S(1)}, u32[]{:S(2)}, u32[]{:S(2)}) collective-permute-start(f32[136,128]{1,0:T(8,128)S(1)} %get-tuple-element.151), channel_id=1, source_target_pairs={{0,6},{2,4},{4,2},{6,0},{8,14},{10,12},{12,10},{14,8},{16,22},{18,... | collective-permute-start | bytes 208904 | tf_op jit(solution)/shard_map/ppermute | solution.py:175
  53.4 1.1 %collective-permute-start.34 = (f32[136,128]{1,0:T(8,128)S(1)}, f32[136,128]{1,0:T(8,128)S(1)}, u32[]{:S(2)}, u32[]{:S(2)}) collective-permute-start(f32[136,128]{1,0:T(8,128)S(1)} %get-tuple-element.152), channel_id=1, source_target_pairs={{0,4},{2,6},{4,0},{6,2},{8,12},{10,14},{12,8},{14,10},{16,20},{18,... | collective-permute-start | bytes 208904 | tf_op jit(solution)/shard_map/ppermute | solution.py:175
  55.1 3.1 %partial.1 = (bf16[256,1024]{1,0:T(8,128)(2,1)}, f32[256,1024]{1,0:T(8,128)S(1)}, f32[256,1024]{1,0:T(8,128)S(1)}) custom-call(s32[1]{0:T(128)} %bitcast.place_ref, bf16[256,1024]{1,0:T(8,128)(2,1)S(1)} %bitcast.16, bf16[256,1024]{1,0:T(8,128)(2,1)S(1)} %bitcast.21, bf16[256,1024]{1,0:T(8,128)(2,1)S(1)} %bitcast.25, ...), custom_call_target="tpu_custom_call" | custom-call | flops 3221225472 | bytes 2097152 | tf_op jit(solution)/shard_map/partial/pallas_call | solution.py:256
  58.8 1.6 %final.1 = (bf16[256,1024]{1,0:T(8,128)(2,1)}, bf16[256,1024]{1,0:T(8,128)(2,1)}) custom-call(s32[1]{0:T(128)} %bitcast.place_ref, bf16[256,1024]{1,0:T(8,128)(2,1)S(1)} %bitcast.22, bf16[256,1024]{1,0:T(8,128)(2,1)S(1)} %bitcast.26, f32[256,1024]{1,0:T(8,128)S(1)} %get-tuple-element.122.key_part_ref, f32[256,1024]{1,0:T(8,128)S(1)} %get-tuple-element.123.value_part_ref, ...), custom_call_target="tpu_custom_call" | custom-call | flops 1073741824 | bytes 2097152 | tf_op jit(solution)/shard_map/final/pallas_call | solution.py:272
  (72 shorter events, 6.9 us)
Async XLA Ops:
  2.3 8.0 %collective-permute-start = (f32[128,128]{1,0:T(8,128)S(1)}, f32[128,128]{1,0:T(8,128)S(1)}, u32[]{:S(2)}, u32[]{:S(2)}) collective-permute-start(f32[128,128]{1,0:T(8,128)S(1)} %get-tuple-element.81), channel_id=1, source_target_pairs={{0,6},{2,4},{4,2},{6,0},{8,14},{10,12},{12,10},{14,8},{16,22},{18,... | collective-permute-start | bytes 196616 | tf_op jit(solution)/shard_map/ppermute | solution.py:175
  6.2 5.1 %collective-permute-start.1 = (f32[128,128]{1,0:T(8,128)S(1)}, f32[128,128]{1,0:T(8,128)S(1)}, u32[]{:S(2)}, u32[]{:S(2)}) collective-permute-start(f32[128,128]{1,0:T(8,128)S(1)} %get-tuple-element.82), channel_id=1, source_target_pairs={{0,4},{2,6},{4,0},{6,2},{8,12},{10,14},{12,8},{14,10},{16,20},{18,... | collective-permute-start | bytes 196616 | tf_op jit(solution)/shard_map/ppermute | solution.py:175
  6.9 8.1 %collective-permute-start.6 = (f32[128,128]{1,0:T(8,128)S(1)}, f32[128,128]{1,0:T(8,128)S(1)}, u32[]{:S(2)}, u32[]{:S(2)}) collective-permute-start(f32[128,128]{1,0:T(8,128)S(1)} %get-tuple-element.89), channel_id=1, source_target_pairs={{0,6},{2,4},{4,2},{6,0},{8,14},{10,12},{12,10},{14,8},{16,22},{18,... | collective-permute-start | bytes 196616 | tf_op jit(solution)/shard_map/ppermute | solution.py:175
  9.7 6.1 %collective-permute-start.7 = (f32[128,128]{1,0:T(8,128)S(1)}, f32[128,128]{1,0:T(8,128)S(1)}, u32[]{:S(2)}, u32[]{:S(2)}) collective-permute-start(f32[128,128]{1,0:T(8,128)S(1)} %get-tuple-element.90), channel_id=1, source_target_pairs={{0,4},{2,6},{4,0},{6,2},{8,12},{10,14},{12,8},{14,10},{16,20},{18,... | collective-permute-start | bytes 196616 | tf_op jit(solution)/shard_map/ppermute | solution.py:175
  10.2 5.6 %collective-permute-start.8 = (f32[128,128]{1,0:T(8,128)S(1)}, f32[128,128]{1,0:T(8,128)S(1)}, u32[]{:S(2)}, u32[]{:S(2)}) collective-permute-start(f32[128,128]{1,0:T(8,128)S(1)} %get-tuple-element.91), channel_id=1, source_target_pairs={{0,2},{2,0},{4,6},{6,4},{8,10},{10,8},{12,14},{14,12},{16,18},{18,... | collective-permute-start | bytes 196616 | tf_op jit(solution)/shard_map/ppermute | solution.py:175
  11.3 9.1 %collective-permute-start.3 = (f32[128,128]{1,0:T(8,128)S(1)}, f32[128,128]{1,0:T(8,128)S(1)}, u32[]{:S(2)}, u32[]{:S(2)}) collective-permute-start(f32[128,128]{1,0:T(8,128)S(1)} %add_add_fusion.7), channel_id=1, source_target_pairs={{0,24},{2,26},{4,28},{6,30},{8,16},{10,18},{12,20},{14,22},{16,8},... | collective-permute-start | bytes 196616 | tf_op jit(solution)/shard_map/ppermute | solution.py:175
  15.0 7.9 %collective-permute-start.4 = (f32[128,128]{1,0:T(8,128)S(1)}, f32[128,128]{1,0:T(8,128)S(1)}, u32[]{:S(2)}, u32[]{:S(2)}) collective-permute-start(f32[128,128]{1,0:T(8,128)S(1)} %add_add_fusion.7), channel_id=1, source_target_pairs={{0,16},{2,18},{4,20},{6,22},{8,24},{10,26},{12,28},{14,30},{16,0},... | collective-permute-start | bytes 196616 | tf_op jit(solution)/shard_map/ppermute | solution.py:175
  15.0 7.9 %collective-permute-start.5 = (f32[128,128]{1,0:T(8,128)S(1)}, f32[128,128]{1,0:T(8,128)S(1)}, u32[]{:S(2)}, u32[]{:S(2)}) collective-permute-start(f32[128,128]{1,0:T(8,128)S(1)} %add_add_fusion.7), channel_id=1, source_target_pairs={{0,8},{2,10},{4,12},{6,14},{8,0},{10,2},{12,4},{14,6},{16,24},{18,... | collective-permute-start | bytes 196616 | tf_op jit(solution)/shard_map/ppermute | solution.py:175
  15.8 10.2 %collective-permute-start.12 = (f32[128,128]{1,0:T(8,128)S(1)}, f32[128,128]{1,0:T(8,128)S(1)}, u32[]{:S(2)}, u32[]{:S(2)}) collective-permute-start(f32[128,128]{1,0:T(8,128)S(1)} %add_add_fusion.5), channel_id=1, source_target_pairs={{0,24},{2,26},{4,28},{6,30},{8,16},{10,18},{12,20},{14,22},{16,8},... | collective-permute-start | bytes 196616 | tf_op jit(solution)/shard_map/ppermute | solution.py:175
  19.5 7.1 %collective-permute-start.13 = (f32[128,128]{1,0:T(8,128)S(1)}, f32[128,128]{1,0:T(8,128)S(1)}, u32[]{:S(2)}, u32[]{:S(2)}) collective-permute-start(f32[128,128]{1,0:T(8,128)S(1)} %add_add_fusion.5), channel_id=1, source_target_pairs={{0,16},{2,18},{4,20},{6,22},{8,24},{10,26},{12,28},{14,30},{16,0},... | collective-permute-start | bytes 196616 | tf_op jit(solution)/shard_map/ppermute | solution.py:175
  20.5 6.1 %collective-permute-start.14 = (f32[128,128]{1,0:T(8,128)S(1)}, f32[128,128]{1,0:T(8,128)S(1)}, u32[]{:S(2)}, u32[]{:S(2)}) collective-permute-start(f32[128,128]{1,0:T(8,128)S(1)} %add_add_fusion.5), channel_id=1, source_target_pairs={{0,8},{2,10},{4,12},{6,14},{8,0},{10,2},{12,4},{14,6},{16,24},{18,... | collective-permute-start | bytes 196616 | tf_op jit(solution)/shard_map/ppermute | solution.py:175
  23.0 6.6 %collective-permute-start.9 = (f32[128,128]{1,0:T(8,128)S(1)}, f32[128,128]{1,0:T(8,128)S(1)}, u32[]{:S(2)}, u32[]{:S(2)}) collective-permute-start(f32[128,128]{1,0:T(8,128)S(1)} %get-tuple-element.105), channel_id=1, source_target_pairs={{0,6},{2,4},{4,2},{6,0},{8,14},{10,12},{12,10},{14,8},{16,22},{18,... | collective-permute-start | bytes 196616 | tf_op jit(solution)/shard_map/ppermute | solution.py:175
  24.9 5.5 %collective-permute-start.10 = (f32[128,128]{1,0:T(8,128)S(1)}, f32[128,128]{1,0:T(8,128)S(1)}, u32[]{:S(2)}, u32[]{:S(2)}) collective-permute-start(f32[128,128]{1,0:T(8,128)S(1)} %get-tuple-element.106), channel_id=1, source_target_pairs={{0,4},{2,6},{4,0},{6,2},{8,12},{10,14},{12,8},{14,10},{16,20},{18,... | collective-permute-start | bytes 196616 | tf_op jit(solution)/shard_map/ppermute | solution.py:175
  26.7 7.4 %collective-permute-start.15 = (f32[128,128]{1,0:T(8,128)S(1)}, f32[128,128]{1,0:T(8,128)S(1)}, u32[]{:S(2)}, u32[]{:S(2)}) collective-permute-start(f32[128,128]{1,0:T(8,128)S(1)} %get-tuple-element.117), channel_id=1, source_target_pairs={{0,6},{2,4},{4,2},{6,0},{8,14},{10,12},{12,10},{14,8},{16,22},{18,... | collective-permute-start | bytes 196616 | tf_op jit(solution)/shard_map/ppermute | solution.py:175
  28.5 6.2 %collective-permute-start.16 = (f32[128,128]{1,0:T(8,128)S(1)}, f32[128,128]{1,0:T(8,128)S(1)}, u32[]{:S(2)}, u32[]{:S(2)}) collective-permute-start(f32[128,128]{1,0:T(8,128)S(1)} %get-tuple-element.118), channel_id=1, source_target_pairs={{0,4},{2,6},{4,0},{6,2},{8,12},{10,14},{12,8},{14,10},{16,20},{18,... | collective-permute-start | bytes 196616 | tf_op jit(solution)/shard_map/ppermute | solution.py:175
  29.7 5.1 %collective-permute-start.17 = (f32[128,128]{1,0:T(8,128)S(1)}, f32[128,128]{1,0:T(8,128)S(1)}, u32[]{:S(2)}, u32[]{:S(2)}) collective-permute-start(f32[128,128]{1,0:T(8,128)S(1)} %get-tuple-element.119), channel_id=1, source_target_pairs={{0,2},{2,0},{4,6},{6,4},{8,10},{10,8},{12,14},{14,12},{16,18},{18,... | collective-permute-start | bytes 196616 | tf_op jit(solution)/shard_map/ppermute | solution.py:175
  31.2 7.2 %collective-permute-start.18 = (f32[136,128]{1,0:T(8,128)S(1)}, f32[136,128]{1,0:T(8,128)S(1)}, u32[]{:S(2)}, u32[]{:S(2)}) collective-permute-start(f32[136,128]{1,0:T(8,128)S(1)} %get-tuple-element.125), channel_id=1, source_target_pairs={{0,6},{2,4},{4,2},{6,0},{8,14},{10,12},{12,10},{14,8},{16,22},{18,... | collective-permute-start | bytes 208904 | tf_op jit(solution)/shard_map/ppermute | solution.py:175
  33.0 6.1 %collective-permute-start.19 = (f32[136,128]{1,0:T(8,128)S(1)}, f32[136,128]{1,0:T(8,128)S(1)}, u32[]{:S(2)}, u32[]{:S(2)}) collective-permute-start(f32[136,128]{1,0:T(8,128)S(1)} %get-tuple-element.126), channel_id=1, source_target_pairs={{0,4},{2,6},{4,0},{6,2},{8,12},{10,14},{12,8},{14,10},{16,20},{18,... | collective-permute-start | bytes 208904 | tf_op jit(solution)/shard_map/ppermute | solution.py:175
  34.1 5.0 %collective-permute-start.20 = (f32[136,128]{1,0:T(8,128)S(1)}, f32[136,128]{1,0:T(8,128)S(1)}, u32[]{:S(2)}, u32[]{:S(2)}) collective-permute-start(f32[136,128]{1,0:T(8,128)S(1)} %get-tuple-element.127), channel_id=1, source_target_pairs={{0,2},{2,0},{4,6},{6,4},{8,10},{10,8},{12,14},{14,12},{16,18},{18,... | collective-permute-start | bytes 208904 | tf_op jit(solution)/shard_map/ppermute | solution.py:175
  35.5 6.1 %collective-permute-start.27 = (f32[136,128]{1,0:T(8,128)S(1)}, f32[136,128]{1,0:T(8,128)S(1)}, u32[]{:S(2)}, u32[]{:S(2)}) collective-permute-start(f32[136,128]{1,0:T(8,128)S(1)} %get-tuple-element.140), channel_id=1, source_target_pairs={{0,6},{2,4},{4,2},{6,0},{8,14},{10,12},{12,10},{14,8},{16,22},{18,... | collective-permute-start | bytes 208904 | tf_op jit(solution)/shard_map/ppermute | solution.py:175
  37.3 5.4 %collective-permute-start.28 = (f32[136,128]{1,0:T(8,128)S(1)}, f32[136,128]{1,0:T(8,128)S(1)}, u32[]{:S(2)}, u32[]{:S(2)}) collective-permute-start(f32[136,128]{1,0:T(8,128)S(1)} %get-tuple-element.141), channel_id=1, source_target_pairs={{0,4},{2,6},{4,0},{6,2},{8,12},{10,14},{12,8},{14,10},{16,20},{18,... | collective-permute-start | bytes 208904 | tf_op jit(solution)/shard_map/ppermute | solution.py:175
  39.1 7.0 %collective-permute-start.21 = (f32[136,128]{1,0:T(8,128)S(1)}, f32[136,128]{1,0:T(8,128)S(1)}, u32[]{:S(2)}, u32[]{:S(2)}) collective-permute-start(f32[136,128]{1,0:T(8,128)S(1)} %add_add_fusion.3), channel_id=1, source_target_pairs={{0,8},{2,10},{4,12},{6,14},{8,0},{10,2},{12,4},{14,6},{16,24},{18,... | collective-permute-start | bytes 208904 | tf_op jit(solution)/shard_map/ppermute | solution.py:175
  39.2 7.1 %collective-permute-start.22 = (f32[136,128]{1,0:T(8,128)S(1)}, f32[136,128]{1,0:T(8,128)S(1)}, u32[]{:S(2)}, u32[]{:S(2)}) collective-permute-start(f32[136,128]{1,0:T(8,128)S(1)} %add_add_fusion.3), channel_id=1, source_target_pairs={{0,24},{2,26},{4,28},{6,30},{8,16},{10,18},{12,20},{14,22},{16,8},... | collective-permute-start | bytes 208904 | tf_op jit(solution)/shard_map/ppermute | solution.py:175
  41.6 6.2 %collective-permute-start.23 = (f32[136,128]{1,0:T(8,128)S(1)}, f32[136,128]{1,0:T(8,128)S(1)}, u32[]{:S(2)}, u32[]{:S(2)}) collective-permute-start(f32[136,128]{1,0:T(8,128)S(1)} %add_add_fusion.3), channel_id=1, source_target_pairs={{0,16},{2,18},{4,20},{6,22},{8,24},{10,26},{12,28},{14,30},{16,0},... | collective-permute-start | bytes 208904 | tf_op jit(solution)/shard_map/ppermute | solution.py:175
  42.7 8.1 %collective-permute-start.30 = (f32[136,128]{1,0:T(8,128)S(1)}, f32[136,128]{1,0:T(8,128)S(1)}, u32[]{:S(2)}, u32[]{:S(2)}) collective-permute-start(f32[136,128]{1,0:T(8,128)S(1)} %add_add_fusion.1), channel_id=1, source_target_pairs={{0,8},{2,10},{4,12},{6,14},{8,0},{10,2},{12,4},{14,6},{16,24},{18,... | collective-permute-start | bytes 208904 | tf_op jit(solution)/shard_map/ppermute | solution.py:175
  43.7 7.7 %collective-permute-start.31 = (f32[136,128]{1,0:T(8,128)S(1)}, f32[136,128]{1,0:T(8,128)S(1)}, u32[]{:S(2)}, u32[]{:S(2)}) collective-permute-start(f32[136,128]{1,0:T(8,128)S(1)} %add_add_fusion.1), channel_id=1, source_target_pairs={{0,24},{2,26},{4,28},{6,30},{8,16},{10,18},{12,20},{14,22},{16,8},... | collective-permute-start | bytes 208904 | tf_op jit(solution)/shard_map/ppermute | solution.py:175
  46.1 5.4 %collective-permute-start.32 = (f32[136,128]{1,0:T(8,128)S(1)}, f32[136,128]{1,0:T(8,128)S(1)}, u32[]{:S(2)}, u32[]{:S(2)}) collective-permute-start(f32[136,128]{1,0:T(8,128)S(1)} %add_add_fusion.1), channel_id=1, source_target_pairs={{0,16},{2,18},{4,20},{6,22},{8,24},{10,26},{12,28},{14,30},{16,0},... | collective-permute-start | bytes 208904 | tf_op jit(solution)/shard_map/ppermute | solution.py:175
  47.9 6.6 %collective-permute-start.24 = (f32[136,128]{1,0:T(8,128)S(1)}, f32[136,128]{1,0:T(8,128)S(1)}, u32[]{:S(2)}, u32[]{:S(2)}) collective-permute-start(f32[136,128]{1,0:T(8,128)S(1)} %get-tuple-element.136), channel_id=1, source_target_pairs={{0,6},{2,4},{4,2},{6,0},{8,14},{10,12},{12,10},{14,8},{16,22},{18,... | collective-permute-start | bytes 208904 | tf_op jit(solution)/shard_map/ppermute | solution.py:175
  49.7 8.5 %collective-permute-start.25 = (f32[136,128]{1,0:T(8,128)S(1)}, f32[136,128]{1,0:T(8,128)S(1)}, u32[]{:S(2)}, u32[]{:S(2)}) collective-permute-start(f32[136,128]{1,0:T(8,128)S(1)} %get-tuple-element.137), channel_id=1, source_target_pairs={{0,4},{2,6},{4,0},{6,2},{8,12},{10,14},{12,8},{14,10},{16,20},{18,... | collective-permute-start | bytes 208904 | tf_op jit(solution)/shard_map/ppermute | solution.py:175
  50.8 7.4 %collective-permute-start.26 = (f32[136,128]{1,0:T(8,128)S(1)}, f32[136,128]{1,0:T(8,128)S(1)}, u32[]{:S(2)}, u32[]{:S(2)}) collective-permute-start(f32[136,128]{1,0:T(8,128)S(1)} %get-tuple-element.138), channel_id=1, source_target_pairs={{0,2},{2,0},{4,6},{6,4},{8,10},{10,8},{12,14},{14,12},{16,18},{18,... | collective-permute-start | bytes 208904 | tf_op jit(solution)/shard_map/ppermute | solution.py:175
  51.6 6.7 %collective-permute-start.33 = (f32[136,128]{1,0:T(8,128)S(1)}, f32[136,128]{1,0:T(8,128)S(1)}, u32[]{:S(2)}, u32[]{:S(2)}) collective-permute-start(f32[136,128]{1,0:T(8,128)S(1)} %get-tuple-element.151), channel_id=1, source_target_pairs={{0,6},{2,4},{4,2},{6,0},{8,14},{10,12},{12,10},{14,8},{16,22},{18,... | collective-permute-start | bytes 208904 | tf_op jit(solution)/shard_map/ppermute | solution.py:175
  53.4 4.9 %collective-permute-start.34 = (f32[136,128]{1,0:T(8,128)S(1)}, f32[136,128]{1,0:T(8,128)S(1)}, u32[]{:S(2)}, u32[]{:S(2)}) collective-permute-start(f32[136,128]{1,0:T(8,128)S(1)} %get-tuple-element.152), channel_id=1, source_target_pairs={{0,4},{2,6},{4,0},{6,2},{8,12},{10,14},{12,8},{14,10},{16,20},{18,... | collective-permute-start | bytes 208904 | tf_op jit(solution)/shard_map/ppermute | solution.py:175
  (10 other events, 83.6 us)

commit v22 on v21

--- a/solution.py
+++ b/solution.py
@@ -60,15 +60,17 @@
             delta_ref[...] = delta if part == 0 else delta_ref[...] + delta
 
 
-def inner_body(query_ref, key_ref, value_ref, inner_ref):
+def inner_body(query_ref, key_ref, value_ref, inner_ref, turned_ref):
     keep = causal()
     for head in range(HEADS):
         at = columns(head)
-        scores = jnp.where(keep, dot(query_ref[:, at], key_ref[:, at], NT), 0.0).astype(jnp.bfloat16)
+        query = query_ref[:, at]
+        scores = jnp.where(keep, dot(query, key_ref[:, at], NT), 0.0).astype(jnp.bfloat16)
         inner_ref[:, at] = dot(scores, value_ref[:, at], NN)
-
-
-def norm_body(chain, place_ref, query_ref, grad_ref, inner_ref, gain_ref, *refs):
+        turned_ref[at, :] = query.T
+
+
+def norm_body(chain, place_ref, query_ref, turned_ref, grad_ref, inner_ref, gain_ref, *refs):
     state_refs, (attn_ref, *delta_refs) = refs[:GROUP], refs[GROUP:]
     for mask, state_ref, delta_ref in zip(ORDER, state_refs, delta_refs):
         at = own_columns(place_ref, mask, chain)
@@ -82,7 +84,7 @@
         shared = jnp.mean(product * gain, axis=-1, keepdims=True)
         grad_attn = ((gain * cotangent - normed * shared) * per_root).astype(jnp.bfloat16)
         attn_ref[:, own_columns(place_ref, mask)] = grad_attn
-        delta_ref[:DH] = dot(query, grad_attn, TN)
+        delta_ref[:DH] = dot(turned_ref[at, :], grad_attn, NN)
         delta_ref[DH:] = jnp.broadcast_to(jnp.sum(product, axis=0, keepdims=True), (GAIN_ROWS, DH))
 
 
@@ -218,6 +220,7 @@
     taller = jax.ShapeDtypeStruct((DH + GAIN_ROWS, DH), jnp.float32)
     full_float = jax.ShapeDtypeStruct(flat, jnp.float32)
     full_low = jax.ShapeDtypeStruct(flat, jnp.bfloat16)
+    turned_low = jax.ShapeDtypeStruct(flat[::-1], jnp.bfloat16)
     half_low = jax.ShapeDtypeStruct((BLOCK, WIDE), jnp.bfloat16)
     short, tall, wide, half = whole(*square.shape), whole(*taller.shape), whole(*flat), whole(BLOCK, WIDE)
     unit = 2 * BLOCK * DH * DH * HEADS
@@ -234,22 +237,27 @@
     )(place, *[pltpu.with_memory_space_constraint(a, pltpu.HBM) for a in (key, value)])
     chains = [slice(chain * GROUP, (chain + 1) * GROUP) for chain in range(CHAINS)]
     inner_call = call(
-        lambda place_ref, *refs: inner_body(*refs), [wide] * 3, wide, full_float, 16 * unit, "inner"
+        lambda place_ref, *refs: inner_body(*refs),
+        [wide] * 3,
+        [wide, whole(*turned_low.shape)],
+        [full_float, turned_low],
+        16 * unit,
+        "inner",
     )
     first, second = [lax.optimization_barrier(plane_swap(deltas[chain])) for chain in chains]
     second, operands = lax.optimization_barrier((second, (place, query, key, value)))
-    state, inner = carried_in(first, False, place, inner_call, operands)
+    state, (inner, turned) = carried_in(first, False, place, inner_call, operands)
     states = [state, carried_in(second, False, place)[0]]
     attns, later = [], []
     for chain in range(CHAINS):
         attn, *deltas = call(
             functools.partial(norm_body, chain),
-            [wide, wide, wide, whole(1, HEADS * DH)] + [short] * GROUP,
+            [wide, whole(*turned_low.shape), wide, wide, whole(1, HEADS * DH)] + [short] * GROUP,
             [half] + [tall] * GROUP,
             [half_low] + [taller] * GROUP,
             8 * unit,
             "norm",
-        )(place, query, grad, inner, gain, *states[chain])
+        )(place, query, turned, grad, inner, gain, *states[chain])
         attns.append(attn)
         held = lax.optimization_barrier(plane_swap(deltas))
         later += carried_in(held, True, place)[0]

time: 61.2 us -> 61.1 us (level)
  no operation moved by 1% of the time
where the time goes in v22:
time: 61.1 us; the launch traced here: 60.9 us
  starting transfers between devices  46.2 us (76%)
  Pallas kernels  8.98 us (15%)
  waiting for transfers between devices  4.2 us (7%)
  between operations  0.83 us (1%)
  other arithmetic  0.75 us (1%)
    ppermute x36, starting transfers between devices, swap(): lax.ppermute(array, 'seq', [(s, s ^ mask) for s in range(lax.axis_size('s...  46.2 us
    ppermute x36, waiting for transfers between devices, swap(): lax.ppermute(array, 'seq', [(s, s ^ mask) for s in range(lax.axis_size('s...  4.2 us
    pallas_call x1, Pallas kernels, local(): call(partial_body, [wide] * 3 + [half] * CHAINS + [short] * HEADS, [wide]...  3.08 us
    pallas_call x1, Pallas kernels, local(): call(delta_body, [pl.BlockSpec(memory_space=pltpu.HBM)] * 2, [short] * HE...  1.61 us
    pallas_call x1, Pallas kernels, local(): call(final_body, [wide] * 4 + [tall] * HEADS, [chunk] * 2, [full_low] * 2...  1.61 us
    pallas_call x2, Pallas kernels, local(): call(functools.partial(norm_body, chain), [wide, whole(*turned_low.shape)...  1.39 us
  transfers between devices with their start and end apart: 37, of which 4 were waited for; matrix products, arithmetic and copies ran while one was open for 0% of the time, Pallas kernels for 12%

profile of v22, /device:TPU:0, one launch (start us, length us, event | category | flops | bytes accessed | tf_op | source)
XLA Modules:
  0.0 60.9 jit_solution(8982514604556637340)
XLA Ops:
  0.7 1.6 %delta.1 = (f32[128,128]{1,0:T(8,128)S(1)}, f32[128,128]{1,0:T(8,128)S(1)}, f32[128,128]{1,0:T(8,128)S(1)}, f32[128,128]{1,0:T(8,128)S(1)}, f32[128,128]{1,0:T(8...) custom-call(s32[1]{0:T(128)} %bitcast.place_ref, bf16[256,1024]{1,0:T(8,128)(2,1)} %bitcast.19, ...), custom_call_target="tpu_custom_call" | custom-call | flops 402653184 | bytes 2097152 | tf_op jit(solution)/shard_map/delta/pallas_call | solution.py:229
  2.3 4.0 %collective-permute-start = (f32[128,128]{1,0:T(8,128)S(1)}, f32[128,128]{1,0:T(8,128)S(1)}, u32[]{:S(2)}, u32[]{:S(2)}) collective-permute-start(f32[128,128]{1,0:T(8,128)S(1)} %get-tuple-element.84), channel_id=1, source_target_pairs={{0,6},{2,4},{4,2},{6,0},{8,14},{10,12},{12,10},{14,8},{16,22},{18,... | collective-permute-start | bytes 196616 | tf_op jit(solution)/shard_map/ppermute | solution.py:177
  6.9 2.8 %collective-permute-start.6 = (f32[128,128]{1,0:T(8,128)S(1)}, f32[128,128]{1,0:T(8,128)S(1)}, u32[]{:S(2)}, u32[]{:S(2)}) collective-permute-start(f32[128,128]{1,0:T(8,128)S(1)} %get-tuple-element.92), channel_id=1, source_target_pairs={{0,6},{2,4},{4,2},{6,0},{8,14},{10,12},{12,10},{14,8},{16,22},{18,... | collective-permute-start | bytes 196616 | tf_op jit(solution)/shard_map/ppermute | solution.py:177
  11.3 3.7 %collective-permute-start.3 = (f32[128,128]{1,0:T(8,128)S(1)}, f32[128,128]{1,0:T(8,128)S(1)}, u32[]{:S(2)}, u32[]{:S(2)}) collective-permute-start(f32[128,128]{1,0:T(8,128)S(1)} %add_add_fusion.7), channel_id=1, source_target_pairs={{0,24},{2,26},{4,28},{6,30},{8,16},{10,18},{12,20},{14,22},{16,8},... | collective-permute-start | bytes 196616 | tf_op jit(solution)/shard_map/ppermute | solution.py:177
  15.0 0.8 %collective-permute-start.5 = (f32[128,128]{1,0:T(8,128)S(1)}, f32[128,128]{1,0:T(8,128)S(1)}, u32[]{:S(2)}, u32[]{:S(2)}) collective-permute-start(f32[128,128]{1,0:T(8,128)S(1)} %add_add_fusion.7), channel_id=1, source_target_pairs={{0,8},{2,10},{4,12},{6,14},{8,0},{10,2},{12,4},{14,6},{16,24},{18,... | collective-permute-start | bytes 196616 | tf_op jit(solution)/shard_map/ppermute | solution.py:177
  15.8 3.7 %collective-permute-start.12 = (f32[128,128]{1,0:T(8,128)S(1)}, f32[128,128]{1,0:T(8,128)S(1)}, u32[]{:S(2)}, u32[]{:S(2)}) collective-permute-start(f32[128,128]{1,0:T(8,128)S(1)} %add_add_fusion.5), channel_id=1, source_target_pairs={{0,24},{2,26},{4,28},{6,30},{8,16},{10,18},{12,20},{14,22},{16,8},... | collective-permute-start | bytes 196616 | tf_op jit(solution)/shard_map/ppermute | solution.py:177
  19.5 0.9 %inner.1 = (f32[256,1024]{1,0:T(8,128)S(1)}, bf16[1024,256]{1,0:T(8,128)(2,1)S(1)}) custom-call(s32[1]{0:T(128)} %bitcast.place_ref, bf16[256,1024]{1,0:T(8,128)(2,1)S(1)} %bitcast.13, bf16[256,1024]{1,0:T(8,128)(2,1)S(1)} %bitcast.20, bf16[256,1024]{1,0:T(8,128)(2,1)S(1)} %bitcast.24), custom_call_target="tpu_custom_call" | custom-call | flops 1073741824 | bytes 2097152 | tf_op jit(solution)/shard_map/inner/pallas_call | solution.py:192
  20.5 0.8 %collective-permute-start.14 = (f32[128,128]{1,0:T(8,128)S(1)}, f32[128,128]{1,0:T(8,128)S(1)}, u32[]{:S(2)}, u32[]{:S(2)}) collective-permute-start(f32[128,128]{1,0:T(8,128)S(1)} %add_add_fusion.5), channel_id=1, source_target_pairs={{0,8},{2,10},{4,12},{6,14},{8,0},{10,2},{12,4},{14,6},{16,24},{18,... | collective-permute-start | bytes 196616 | tf_op jit(solution)/shard_map/ppermute | solution.py:177
  21.3 1.6 %collective-permute-done.4.refs_2_ = f32[128,128]{1,0:T(8,128)S(1)} collective-permute-done((f32[128,128]{1,0:T(8,128)S(1)}, f32[128,128]{1,0:T(8,128)S(1)}, u32[]{:S(2)}, u32[]{:S(2)}) %collective-permute-start.4) | collective-permute-done | bytes 65568 | tf_op jit(solution)/shard_map/ppermute | solution.py:177
  23.0 1.9 %collective-permute-start.9 = (f32[128,128]{1,0:T(8,128)S(1)}, f32[128,128]{1,0:T(8,128)S(1)}, u32[]{:S(2)}, u32[]{:S(2)}) collective-permute-start(f32[128,128]{1,0:T(8,128)S(1)} %get-tuple-element.111), channel_id=1, source_target_pairs={{0,6},{2,4},{4,2},{6,0},{8,14},{10,12},{12,10},{14,8},{16,22},{18,... | collective-permute-start | bytes 196616 | tf_op jit(solution)/shard_map/ppermute | solution.py:177
  24.9 1.1 %collective-permute-start.10 = (f32[128,128]{1,0:T(8,128)S(1)}, f32[128,128]{1,0:T(8,128)S(1)}, u32[]{:S(2)}, u32[]{:S(2)}) collective-permute-start(f32[128,128]{1,0:T(8,128)S(1)} %get-tuple-element.112), channel_id=1, source_target_pairs={{0,4},{2,6},{4,0},{6,2},{8,12},{10,14},{12,8},{14,10},{16,20},{18,... | collective-permute-start | bytes 196616 | tf_op jit(solution)/shard_map/ppermute | solution.py:177
  26.7 1.9 %collective-permute-start.15 = (f32[128,128]{1,0:T(8,128)S(1)}, f32[128,128]{1,0:T(8,128)S(1)}, u32[]{:S(2)}, u32[]{:S(2)}) collective-permute-start(f32[128,128]{1,0:T(8,128)S(1)} %get-tuple-element.123), channel_id=1, source_target_pairs={{0,6},{2,4},{4,2},{6,0},{8,14},{10,12},{12,10},{14,8},{16,22},{18,... | collective-permute-start | bytes 196616 | tf_op jit(solution)/shard_map/ppermute | solution.py:177
  28.5 1.1 %collective-permute-start.16 = (f32[128,128]{1,0:T(8,128)S(1)}, f32[128,128]{1,0:T(8,128)S(1)}, u32[]{:S(2)}, u32[]{:S(2)}) collective-permute-start(f32[128,128]{1,0:T(8,128)S(1)} %get-tuple-element.124), channel_id=1, source_target_pairs={{0,4},{2,6},{4,0},{6,2},{8,12},{10,14},{12,8},{14,10},{16,20},{18,... | collective-permute-start | bytes 196616 | tf_op jit(solution)/shard_map/ppermute | solution.py:177
  29.7 0.8 %collective-permute-start.17 = (f32[128,128]{1,0:T(8,128)S(1)}, f32[128,128]{1,0:T(8,128)S(1)}, u32[]{:S(2)}, u32[]{:S(2)}) collective-permute-start(f32[128,128]{1,0:T(8,128)S(1)} %get-tuple-element.125), channel_id=1, source_target_pairs={{0,2},{2,0},{4,6},{6,4},{8,10},{10,8},{12,14},{14,12},{16,18},{18,... | collective-permute-start | bytes 196616 | tf_op jit(solution)/shard_map/ppermute | solution.py:177
  31.2 1.8 %collective-permute-start.18 = (f32[136,128]{1,0:T(8,128)S(1)}, f32[136,128]{1,0:T(8,128)S(1)}, u32[]{:S(2)}, u32[]{:S(2)}) collective-permute-start(f32[136,128]{1,0:T(8,128)S(1)} %get-tuple-element.131), channel_id=1, source_target_pairs={{0,6},{2,4},{4,2},{6,0},{8,14},{10,12},{12,10},{14,8},{16,22},{18,... | collective-permute-start | bytes 208904 | tf_op jit(solution)/shard_map/ppermute | solution.py:177
  32.9 1.1 %collective-permute-start.19 = (f32[136,128]{1,0:T(8,128)S(1)}, f32[136,128]{1,0:T(8,128)S(1)}, u32[]{:S(2)}, u32[]{:S(2)}) collective-permute-start(f32[136,128]{1,0:T(8,128)S(1)} %get-tuple-element.132), channel_id=1, source_target_pairs={{0,4},{2,6},{4,0},{6,2},{8,12},{10,14},{12,8},{14,10},{16,20},{18,... | collective-permute-start | bytes 208904 | tf_op jit(solution)/shard_map/ppermute | solution.py:177
  34.7 0.7 %norm.3 = (bf16[256,512]{1,0:T(8,128)(2,1)S(1)}, f32[136,128]{1,0:T(8,128)S(1)}, f32[136,128]{1,0:T(8,128)S(1)}, f32[136,128]{1,0:T(8,128)S(1)}, f32[136,128]{1,0:T(8,128)S(1)}) custom-call(s32[1]{0:T(128)} %bitcast.place_ref, bf16[256,1024]{1,0:T(8,128)(2,1)S(1)} %bitcast.15, bf16[1024,256]{1,0:T(8,128)(2,1)S(1)} %get-tuple-element.105.turned_ref, ...), custom_call_target="tpu_custom_call" | custom-call | flops 536870912 | bytes 2097152 | tf_op jit(solution)/shard_map/norm/pallas_call | solution.py:253
  35.4 1.8 %collective-permute-start.27 = (f32[136,128]{1,0:T(8,128)S(1)}, f32[136,128]{1,0:T(8,128)S(1)}, u32[]{:S(2)}, u32[]{:S(2)}) collective-permute-start(f32[136,128]{1,0:T(8,128)S(1)} %get-tuple-element.146), channel_id=1, source_target_pairs={{0,6},{2,4},{4,2},{6,0},{8,14},{10,12},{12,10},{14,8},{16,22},{18,... | collective-permute-start | bytes 208904 | tf_op jit(solution)/shard_map/ppermute | solution.py:177
  37.2 1.1 %collective-permute-start.28 = (f32[136,128]{1,0:T(8,128)S(1)}, f32[136,128]{1,0:T(8,128)S(1)}, u32[]{:S(2)}, u32[]{:S(2)}) collective-permute-start(f32[136,128]{1,0:T(8,128)S(1)} %get-tuple-element.147), channel_id=1, source_target_pairs={{0,4},{2,6},{4,0},{6,2},{8,12},{10,14},{12,8},{14,10},{16,20},{18,... | collective-permute-start | bytes 208904 | tf_op jit(solution)/shard_map/ppermute | solution.py:177
  39.1 2.4 %collective-permute-start.22 = (f32[136,128]{1,0:T(8,128)S(1)}, f32[136,128]{1,0:T(8,128)S(1)}, u32[]{:S(2)}, u32[]{:S(2)}) collective-permute-start(f32[136,128]{1,0:T(8,128)S(1)} %add_add_fusion.3), channel_id=1, source_target_pairs={{0,24},{2,26},{4,28},{6,30},{8,16},{10,18},{12,20},{14,22},{16,8},... | collective-permute-start | bytes 208904 | tf_op jit(solution)/shard_map/ppermute | solution.py:177
  41.5 1.1 %collective-permute-start.23 = (f32[136,128]{1,0:T(8,128)S(1)}, f32[136,128]{1,0:T(8,128)S(1)}, u32[]{:S(2)}, u32[]{:S(2)}) collective-permute-start(f32[136,128]{1,0:T(8,128)S(1)} %add_add_fusion.3), channel_id=1, source_target_pairs={{0,16},{2,18},{4,20},{6,22},{8,24},{10,26},{12,28},{14,30},{16,0},... | collective-permute-start | bytes 208904 | tf_op jit(solution)/shard_map/ppermute | solution.py:177
  42.6 1.0 %collective-permute-start.30 = (f32[136,128]{1,0:T(8,128)S(1)}, f32[136,128]{1,0:T(8,128)S(1)}, u32[]{:S(2)}, u32[]{:S(2)}) collective-permute-start(f32[136,128]{1,0:T(8,128)S(1)} %add_add_fusion.1), channel_id=1, source_target_pairs={{0,8},{2,10},{4,12},{6,14},{8,0},{10,2},{12,4},{14,6},{16,24},{18,... | collective-permute-start | bytes 208904 | tf_op jit(solution)/shard_map/ppermute | solution.py:177
  43.6 2.3 %collective-permute-start.31 = (f32[136,128]{1,0:T(8,128)S(1)}, f32[136,128]{1,0:T(8,128)S(1)}, u32[]{:S(2)}, u32[]{:S(2)}) collective-permute-start(f32[136,128]{1,0:T(8,128)S(1)} %add_add_fusion.1), channel_id=1, source_target_pairs={{0,24},{2,26},{4,28},{6,30},{8,16},{10,18},{12,20},{14,22},{16,8},... | collective-permute-start | bytes 208904 | tf_op jit(solution)/shard_map/ppermute | solution.py:177
  46.2 1.6 %collective-permute-done.23.refs_3_ = f32[136,128]{1,0:T(8,128)S(1)} collective-permute-done((f32[136,128]{1,0:T(8,128)S(1)}, f32[136,128]{1,0:T(8,128)S(1)}, u32[]{:S(2)}, u32[]{:S(2)}) %collective-permute-start.23) | collective-permute-done | bytes 69664 | tf_op jit(solution)/shard_map/ppermute | solution.py:177
  47.9 1.7 %collective-permute-start.24 = (f32[136,128]{1,0:T(8,128)S(1)}, f32[136,128]{1,0:T(8,128)S(1)}, u32[]{:S(2)}, u32[]{:S(2)}) collective-permute-start(f32[136,128]{1,0:T(8,128)S(1)} %get-tuple-element.142), channel_id=1, source_target_pairs={{0,6},{2,4},{4,2},{6,0},{8,14},{10,12},{12,10},{14,8},{16,22},{18,... | collective-permute-start | bytes 208904 | tf_op jit(solution)/shard_map/ppermute | solution.py:177
  49.6 1.1 %collective-permute-start.25 = (f32[136,128]{1,0:T(8,128)S(1)}, f32[136,128]{1,0:T(8,128)S(1)}, u32[]{:S(2)}, u32[]{:S(2)}) collective-permute-start(f32[136,128]{1,0:T(8,128)S(1)} %get-tuple-element.143), channel_id=1, source_target_pairs={{0,4},{2,6},{4,0},{6,2},{8,12},{10,14},{12,8},{14,10},{16,20},{18,... | collective-permute-start | bytes 208904 | tf_op jit(solution)/shard_map/ppermute | solution.py:177
  50.7 0.7 %collective-permute-start.26 = (f32[136,128]{1,0:T(8,128)S(1)}, f32[136,128]{1,0:T(8,128)S(1)}, u32[]{:S(2)}, u32[]{:S(2)}) collective-permute-start(f32[136,128]{1,0:T(8,128)S(1)} %get-tuple-element.144), channel_id=1, source_target_pairs={{0,2},{2,0},{4,6},{6,4},{8,10},{10,8},{12,14},{14,12},{16,18},{18,... | collective-permute-start | bytes 208904 | tf_op jit(solution)/shard_map/ppermute | solution.py:177
  51.6 1.7 %collective-permute-start.33 = (f32[136,128]{1,0:T(8,128)S(1)}, f32[136,128]{1,0:T(8,128)S(1)}, u32[]{:S(2)}, u32[]{:S(2)}) collective-permute-start(f32[136,128]{1,0:T(8,128)S(1)} %get-tuple-element.157), channel_id=1, source_target_pairs={{0,6},{2,4},{4,2},{6,0},{8,14},{10,12},{12,10},{14,8},{16,22},{18,... | collective-permute-start | bytes 208904 | tf_op jit(solution)/shard_map/ppermute | solution.py:177
  53.3 1.1 %collective-permute-start.34 = (f32[136,128]{1,0:T(8,128)S(1)}, f32[136,128]{1,0:T(8,128)S(1)}, u32[]{:S(2)}, u32[]{:S(2)}) collective-permute-start(f32[136,128]{1,0:T(8,128)S(1)} %get-tuple-element.158), channel_id=1, source_target_pairs={{0,4},{2,6},{4,0},{6,2},{8,12},{10,14},{12,8},{14,10},{16,20},{18,... | collective-permute-start | bytes 208904 | tf_op jit(solution)/shard_map/ppermute | solution.py:177
  54.4 0.7 %collective-permute-start.35 = (f32[136,128]{1,0:T(8,128)S(1)}, f32[136,128]{1,0:T(8,128)S(1)}, u32[]{:S(2)}, u32[]{:S(2)}) collective-permute-start(f32[136,128]{1,0:T(8,128)S(1)} %get-tuple-element.159), channel_id=1, source_target_pairs={{0,2},{2,0},{4,6},{6,4},{8,10},{10,8},{12,14},{14,12},{16,18},{18,... | collective-permute-start | bytes 208904 | tf_op jit(solution)/shard_map/ppermute | solution.py:177
  55.1 3.1 %partial.1 = (bf16[256,1024]{1,0:T(8,128)(2,1)}, f32[256,1024]{1,0:T(8,128)S(1)}, f32[256,1024]{1,0:T(8,128)S(1)}) custom-call(s32[1]{0:T(128)} %bitcast.place_ref, bf16[256,1024]{1,0:T(8,128)(2,1)S(1)} %bitcast.16, bf16[256,1024]{1,0:T(8,128)(2,1)S(1)} %bitcast.21, bf16[256,1024]{1,0:T(8,128)(2,1)S(1)} %bitcast.25, ...), custom_call_target="tpu_custom_call" | custom-call | flops 3221225472 | bytes 2097152 | tf_op jit(solution)/shard_map/partial/pallas_call | solution.py:264
  58.7 1.6 %final.1 = (bf16[256,1024]{1,0:T(8,128)(2,1)}, bf16[256,1024]{1,0:T(8,128)(2,1)}) custom-call(s32[1]{0:T(128)} %bitcast.place_ref, bf16[256,1024]{1,0:T(8,128)(2,1)S(1)} %bitcast.22, bf16[256,1024]{1,0:T(8,128)(2,1)S(1)} %bitcast.26, f32[256,1024]{1,0:T(8,128)S(1)} %get-tuple-element.128.key_part_ref, f32[256,1024]{1,0:T(8,128)S(1)} %get-tuple-element.129.value_part_ref, ...), custom_call_target="tpu_custom_call" | custom-call | flops 1073741824 | bytes 2097152 | tf_op jit(solution)/shard_map/final/pallas_call | solution.py:280
  (72 shorter events, 6.9 us)
Async XLA Ops:
  2.3 8.0 %collective-permute-start = (f32[128,128]{1,0:T(8,128)S(1)}, f32[128,128]{1,0:T(8,128)S(1)}, u32[]{:S(2)}, u32[]{:S(2)}) collective-permute-start(f32[128,128]{1,0:T(8,128)S(1)} %get-tuple-element.84), channel_id=1, source_target_pairs={{0,6},{2,4},{4,2},{6,0},{8,14},{10,12},{12,10},{14,8},{16,22},{18,... | collective-permute-start | bytes 196616 | tf_op jit(solution)/shard_map/ppermute | solution.py:177
  6.2 5.1 %collective-permute-start.1 = (f32[128,128]{1,0:T(8,128)S(1)}, f32[128,128]{1,0:T(8,128)S(1)}, u32[]{:S(2)}, u32[]{:S(2)}) collective-permute-start(f32[128,128]{1,0:T(8,128)S(1)} %get-tuple-element.85), channel_id=1, source_target_pairs={{0,4},{2,6},{4,0},{6,2},{8,12},{10,14},{12,8},{14,10},{16,20},{18,... | collective-permute-start | bytes 196616 | tf_op jit(solution)/shard_map/ppermute | solution.py:177
  6.9 8.1 %collective-permute-start.6 = (f32[128,128]{1,0:T(8,128)S(1)}, f32[128,128]{1,0:T(8,128)S(1)}, u32[]{:S(2)}, u32[]{:S(2)}) collective-permute-start(f32[128,128]{1,0:T(8,128)S(1)} %get-tuple-element.92), channel_id=1, source_target_pairs={{0,6},{2,4},{4,2},{6,0},{8,14},{10,12},{12,10},{14,8},{16,22},{18,... | collective-permute-start | bytes 196616 | tf_op jit(solution)/shard_map/ppermute | solution.py:177
  9.7 6.1 %collective-permute-start.7 = (f32[128,128]{1,0:T(8,128)S(1)}, f32[128,128]{1,0:T(8,128)S(1)}, u32[]{:S(2)}, u32[]{:S(2)}) collective-permute-start(f32[128,128]{1,0:T(8,128)S(1)} %get-tuple-element.93), channel_id=1, source_target_pairs={{0,4},{2,6},{4,0},{6,2},{8,12},{10,14},{12,8},{14,10},{16,20},{18,... | collective-permute-start | bytes 196616 | tf_op jit(solution)/shard_map/ppermute | solution.py:177
  10.2 5.6 %collective-permute-start.8 = (f32[128,128]{1,0:T(8,128)S(1)}, f32[128,128]{1,0:T(8,128)S(1)}, u32[]{:S(2)}, u32[]{:S(2)}) collective-permute-start(f32[128,128]{1,0:T(8,128)S(1)} %get-tuple-element.94), channel_id=1, source_target_pairs={{0,2},{2,0},{4,6},{6,4},{8,10},{10,8},{12,14},{14,12},{16,18},{18,... | collective-permute-start | bytes 196616 | tf_op jit(solution)/shard_map/ppermute | solution.py:177
  11.3 9.1 %collective-permute-start.3 = (f32[128,128]{1,0:T(8,128)S(1)}, f32[128,128]{1,0:T(8,128)S(1)}, u32[]{:S(2)}, u32[]{:S(2)}) collective-permute-start(f32[128,128]{1,0:T(8,128)S(1)} %add_add_fusion.7), channel_id=1, source_target_pairs={{0,24},{2,26},{4,28},{6,30},{8,16},{10,18},{12,20},{14,22},{16,8},... | collective-permute-start | bytes 196616 | tf_op jit(solution)/shard_map/ppermute | solution.py:177
  15.0 7.9 %collective-permute-start.4 = (f32[128,128]{1,0:T(8,128)S(1)}, f32[128,128]{1,0:T(8,128)S(1)}, u32[]{:S(2)}, u32[]{:S(2)}) collective-permute-start(f32[128,128]{1,0:T(8,128)S(1)} %add_add_fusion.7), channel_id=1, source_target_pairs={{0,16},{2,18},{4,20},{6,22},{8,24},{10,26},{12,28},{14,30},{16,0},... | collective-permute-start | bytes 196616 | tf_op jit(solution)/shard_map/ppermute | solution.py:177
  15.0 7.9 %collective-permute-start.5 = (f32[128,128]{1,0:T(8,128)S(1)}, f32[128,128]{1,0:T(8,128)S(1)}, u32[]{:S(2)}, u32[]{:S(2)}) collective-permute-start(f32[128,128]{1,0:T(8,128)S(1)} %add_add_fusion.7), channel_id=1, source_target_pairs={{0,8},{2,10},{4,12},{6,14},{8,0},{10,2},{12,4},{14,6},{16,24},{18,... | collective-permute-start | bytes 196616 | tf_op jit(solution)/shard_map/ppermute | solution.py:177
  15.8 10.2 %collective-permute-start.12 = (f32[128,128]{1,0:T(8,128)S(1)}, f32[128,128]{1,0:T(8,128)S(1)}, u32[]{:S(2)}, u32[]{:S(2)}) collective-permute-start(f32[128,128]{1,0:T(8,128)S(1)} %add_add_fusion.5), channel_id=1, source_target_pairs={{0,24},{2,26},{4,28},{6,30},{8,16},{10,18},{12,20},{14,22},{16,8},... | collective-permute-start | bytes 196616 | tf_op jit(solution)/shard_map/ppermute | solution.py:177
  19.5 7.1 %collective-permute-start.13 = (f32[128,128]{1,0:T(8,128)S(1)}, f32[128,128]{1,0:T(8,128)S(1)}, u32[]{:S(2)}, u32[]{:S(2)}) collective-permute-start(f32[128,128]{1,0:T(8,128)S(1)} %add_add_fusion.5), channel_id=1, source_target_pairs={{0,16},{2,18},{4,20},{6,22},{8,24},{10,26},{12,28},{14,30},{16,0},... | collective-permute-start | bytes 196616 | tf_op jit(solution)/shard_map/ppermute | solution.py:177
  20.5 6.1 %collective-permute-start.14 = (f32[128,128]{1,0:T(8,128)S(1)}, f32[128,128]{1,0:T(8,128)S(1)}, u32[]{:S(2)}, u32[]{:S(2)}) collective-permute-start(f32[128,128]{1,0:T(8,128)S(1)} %add_add_fusion.5), channel_id=1, source_target_pairs={{0,8},{2,10},{4,12},{6,14},{8,0},{10,2},{12,4},{14,6},{16,24},{18,... | collective-permute-start | bytes 196616 | tf_op jit(solution)/shard_map/ppermute | solution.py:177
  23.0 6.6 %collective-permute-start.9 = (f32[128,128]{1,0:T(8,128)S(1)}, f32[128,128]{1,0:T(8,128)S(1)}, u32[]{:S(2)}, u32[]{:S(2)}) collective-permute-start(f32[128,128]{1,0:T(8,128)S(1)} %get-tuple-element.111), channel_id=1, source_target_pairs={{0,6},{2,4},{4,2},{6,0},{8,14},{10,12},{12,10},{14,8},{16,22},{18,... | collective-permute-start | bytes 196616 | tf_op jit(solution)/shard_map/ppermute | solution.py:177
  24.9 5.6 %collective-permute-start.10 = (f32[128,128]{1,0:T(8,128)S(1)}, f32[128,128]{1,0:T(8,128)S(1)}, u32[]{:S(2)}, u32[]{:S(2)}) collective-permute-start(f32[128,128]{1,0:T(8,128)S(1)} %get-tuple-element.112), channel_id=1, source_target_pairs={{0,4},{2,6},{4,0},{6,2},{8,12},{10,14},{12,8},{14,10},{16,20},{18,... | collective-permute-start | bytes 196616 | tf_op jit(solution)/shard_map/ppermute | solution.py:177
  26.7 7.4 %collective-permute-start.15 = (f32[128,128]{1,0:T(8,128)S(1)}, f32[128,128]{1,0:T(8,128)S(1)}, u32[]{:S(2)}, u32[]{:S(2)}) collective-permute-start(f32[128,128]{1,0:T(8,128)S(1)} %get-tuple-element.123), channel_id=1, source_target_pairs={{0,6},{2,4},{4,2},{6,0},{8,14},{10,12},{12,10},{14,8},{16,22},{18,... | collective-permute-start | bytes 196616 | tf_op jit(solution)/shard_map/ppermute | solution.py:177
  28.5 6.2 %collective-permute-start.16 = (f32[128,128]{1,0:T(8,128)S(1)}, f32[128,128]{1,0:T(8,128)S(1)}, u32[]{:S(2)}, u32[]{:S(2)}) collective-permute-start(f32[128,128]{1,0:T(8,128)S(1)} %get-tuple-element.124), channel_id=1, source_target_pairs={{0,4},{2,6},{4,0},{6,2},{8,12},{10,14},{12,8},{14,10},{16,20},{18,... | collective-permute-start | bytes 196616 | tf_op jit(solution)/shard_map/ppermute | solution.py:177
  29.7 5.1 %collective-permute-start.17 = (f32[128,128]{1,0:T(8,128)S(1)}, f32[128,128]{1,0:T(8,128)S(1)}, u32[]{:S(2)}, u32[]{:S(2)}) collective-permute-start(f32[128,128]{1,0:T(8,128)S(1)} %get-tuple-element.125), channel_id=1, source_target_pairs={{0,2},{2,0},{4,6},{6,4},{8,10},{10,8},{12,14},{14,12},{16,18},{18,... | collective-permute-start | bytes 196616 | tf_op jit(solution)/shard_map/ppermute | solution.py:177
  31.2 7.2 %collective-permute-start.18 = (f32[136,128]{1,0:T(8,128)S(1)}, f32[136,128]{1,0:T(8,128)S(1)}, u32[]{:S(2)}, u32[]{:S(2)}) collective-permute-start(f32[136,128]{1,0:T(8,128)S(1)} %get-tuple-element.131), channel_id=1, source_target_pairs={{0,6},{2,4},{4,2},{6,0},{8,14},{10,12},{12,10},{14,8},{16,22},{18,... | collective-permute-start | bytes 208904 | tf_op jit(solution)/shard_map/ppermute | solution.py:177
  32.9 6.1 %collective-permute-start.19 = (f32[136,128]{1,0:T(8,128)S(1)}, f32[136,128]{1,0:T(8,128)S(1)}, u32[]{:S(2)}, u32[]{:S(2)}) collective-permute-start(f32[136,128]{1,0:T(8,128)S(1)} %get-tuple-element.132), channel_id=1, source_target_pairs={{0,4},{2,6},{4,0},{6,2},{8,12},{10,14},{12,8},{14,10},{16,20},{18,... | collective-permute-start | bytes 208904 | tf_op jit(solution)/shard_map/ppermute | solution.py:177
  34.0 5.0 %collective-permute-start.20 = (f32[136,128]{1,0:T(8,128)S(1)}, f32[136,128]{1,0:T(8,128)S(1)}, u32[]{:S(2)}, u32[]{:S(2)}) collective-permute-start(f32[136,128]{1,0:T(8,128)S(1)} %get-tuple-element.133), channel_id=1, source_target_pairs={{0,2},{2,0},{4,6},{6,4},{8,10},{10,8},{12,14},{14,12},{16,18},{18,... | collective-permute-start | bytes 208904 | tf_op jit(solution)/shard_map/ppermute | solution.py:177
  35.4 6.1 %collective-permute-start.27 = (f32[136,128]{1,0:T(8,128)S(1)}, f32[136,128]{1,0:T(8,128)S(1)}, u32[]{:S(2)}, u32[]{:S(2)}) collective-permute-start(f32[136,128]{1,0:T(8,128)S(1)} %get-tuple-element.146), channel_id=1, source_target_pairs={{0,6},{2,4},{4,2},{6,0},{8,14},{10,12},{12,10},{14,8},{16,22},{18,... | collective-permute-start | bytes 208904 | tf_op jit(solution)/shard_map/ppermute | solution.py:177
  37.2 5.4 %collective-permute-start.28 = (f32[136,128]{1,0:T(8,128)S(1)}, f32[136,128]{1,0:T(8,128)S(1)}, u32[]{:S(2)}, u32[]{:S(2)}) collective-permute-start(f32[136,128]{1,0:T(8,128)S(1)} %get-tuple-element.147), channel_id=1, source_target_pairs={{0,4},{2,6},{4,0},{6,2},{8,12},{10,14},{12,8},{14,10},{16,20},{18,... | collective-permute-start | bytes 208904 | tf_op jit(solution)/shard_map/ppermute | solution.py:177
  39.0 7.0 %collective-permute-start.21 = (f32[136,128]{1,0:T(8,128)S(1)}, f32[136,128]{1,0:T(8,128)S(1)}, u32[]{:S(2)}, u32[]{:S(2)}) collective-permute-start(f32[136,128]{1,0:T(8,128)S(1)} %add_add_fusion.3), channel_id=1, source_target_pairs={{0,8},{2,10},{4,12},{6,14},{8,0},{10,2},{12,4},{14,6},{16,24},{18,... | collective-permute-start | bytes 208904 | tf_op jit(solution)/shard_map/ppermute | solution.py:177
  39.1 7.1 %collective-permute-start.22 = (f32[136,128]{1,0:T(8,128)S(1)}, f32[136,128]{1,0:T(8,128)S(1)}, u32[]{:S(2)}, u32[]{:S(2)}) collective-permute-start(f32[136,128]{1,0:T(8,128)S(1)} %add_add_fusion.3), channel_id=1, source_target_pairs={{0,24},{2,26},{4,28},{6,30},{8,16},{10,18},{12,20},{14,22},{16,8},... | collective-permute-start | bytes 208904 | tf_op jit(solution)/shard_map/ppermute | solution.py:177
  41.5 6.3 %collective-permute-start.23 = (f32[136,128]{1,0:T(8,128)S(1)}, f32[136,128]{1,0:T(8,128)S(1)}, u32[]{:S(2)}, u32[]{:S(2)}) collective-permute-start(f32[136,128]{1,0:T(8,128)S(1)} %add_add_fusion.3), channel_id=1, source_target_pairs={{0,16},{2,18},{4,20},{6,22},{8,24},{10,26},{12,28},{14,30},{16,0},... | collective-permute-start | bytes 208904 | tf_op jit(solution)/shard_map/ppermute | solution.py:177
  42.6 8.1 %collective-permute-start.30 = (f32[136,128]{1,0:T(8,128)S(1)}, f32[136,128]{1,0:T(8,128)S(1)}, u32[]{:S(2)}, u32[]{:S(2)}) collective-permute-start(f32[136,128]{1,0:T(8,128)S(1)} %add_add_fusion.1), channel_id=1, source_target_pairs={{0,8},{2,10},{4,12},{6,14},{8,0},{10,2},{12,4},{14,6},{16,24},{18,... | collective-permute-start | bytes 208904 | tf_op jit(solution)/shard_map/ppermute | solution.py:177
  43.6 7.8 %collective-permute-start.31 = (f32[136,128]{1,0:T(8,128)S(1)}, f32[136,128]{1,0:T(8,128)S(1)}, u32[]{:S(2)}, u32[]{:S(2)}) collective-permute-start(f32[136,128]{1,0:T(8,128)S(1)} %add_add_fusion.1), channel_id=1, source_target_pairs={{0,24},{2,26},{4,28},{6,30},{8,16},{10,18},{12,20},{14,22},{16,8},... | collective-permute-start | bytes 208904 | tf_op jit(solution)/shard_map/ppermute | solution.py:177
  46.0 5.4 %collective-permute-start.32 = (f32[136,128]{1,0:T(8,128)S(1)}, f32[136,128]{1,0:T(8,128)S(1)}, u32[]{:S(2)}, u32[]{:S(2)}) collective-permute-start(f32[136,128]{1,0:T(8,128)S(1)} %add_add_fusion.1), channel_id=1, source_target_pairs={{0,16},{2,18},{4,20},{6,22},{8,24},{10,26},{12,28},{14,30},{16,0},... | collective-permute-start | bytes 208904 | tf_op jit(solution)/shard_map/ppermute | solution.py:177
  47.9 6.5 %collective-permute-start.24 = (f32[136,128]{1,0:T(8,128)S(1)}, f32[136,128]{1,0:T(8,128)S(1)}, u32[]{:S(2)}, u32[]{:S(2)}) collective-permute-start(f32[136,128]{1,0:T(8,128)S(1)} %get-tuple-element.142), channel_id=1, source_target_pairs={{0,6},{2,4},{4,2},{6,0},{8,14},{10,12},{12,10},{14,8},{16,22},{18,... | collective-permute-start | bytes 208904 | tf_op jit(solution)/shard_map/ppermute | solution.py:177
  49.6 8.6 %collective-permute-start.25 = (f32[136,128]{1,0:T(8,128)S(1)}, f32[136,128]{1,0:T(8,128)S(1)}, u32[]{:S(2)}, u32[]{:S(2)}) collective-permute-start(f32[136,128]{1,0:T(8,128)S(1)} %get-tuple-element.143), channel_id=1, source_target_pairs={{0,4},{2,6},{4,0},{6,2},{8,12},{10,14},{12,8},{14,10},{16,20},{18,... | collective-permute-start | bytes 208904 | tf_op jit(solution)/shard_map/ppermute | solution.py:177
  50.7 7.5 %collective-permute-start.26 = (f32[136,128]{1,0:T(8,128)S(1)}, f32[136,128]{1,0:T(8,128)S(1)}, u32[]{:S(2)}, u32[]{:S(2)}) collective-permute-start(f32[136,128]{1,0:T(8,128)S(1)} %get-tuple-element.144), channel_id=1, source_target_pairs={{0,2},{2,0},{4,6},{6,4},{8,10},{10,8},{12,14},{14,12},{16,18},{18,... | collective-permute-start | bytes 208904 | tf_op jit(solution)/shard_map/ppermute | solution.py:177
  51.6 6.7 %collective-permute-start.33 = (f32[136,128]{1,0:T(8,128)S(1)}, f32[136,128]{1,0:T(8,128)S(1)}, u32[]{:S(2)}, u32[]{:S(2)}) collective-permute-start(f32[136,128]{1,0:T(8,128)S(1)} %get-tuple-element.157), channel_id=1, source_target_pairs={{0,6},{2,4},{4,2},{6,0},{8,14},{10,12},{12,10},{14,8},{16,22},{18,... | collective-permute-start | bytes 208904 | tf_op jit(solution)/shard_map/ppermute | solution.py:177
  53.3 4.9 %collective-permute-start.34 = (f32[136,128]{1,0:T(8,128)S(1)}, f32[136,128]{1,0:T(8,128)S(1)}, u32[]{:S(2)}, u32[]{:S(2)}) collective-permute-start(f32[136,128]{1,0:T(8,128)S(1)} %get-tuple-element.158), channel_id=1, source_target_pairs={{0,4},{2,6},{4,0},{6,2},{8,12},{10,14},{12,8},{14,10},{16,20},{18,... | collective-permute-start | bytes 208904 | tf_op jit(solution)/shard_map/ppermute | solution.py:177
  (10 other events, 83.6 us)

commit v23 on v22

--- a/solution.py
+++ b/solution.py
@@ -60,14 +60,16 @@
             delta_ref[...] = delta if part == 0 else delta_ref[...] + delta
 
 
-def inner_body(query_ref, key_ref, value_ref, inner_ref, turned_ref):
-    keep = causal()
+def inner_body(query_ref, key_ref, value_ref, inner_ref, turned_ref, scores_ref):
+    keep, kept = causal(), causal(True)
     for head in range(HEADS):
         at = columns(head)
         query = query_ref[:, at]
         scores = jnp.where(keep, dot(query, key_ref[:, at], NT), 0.0).astype(jnp.bfloat16)
         inner_ref[:, at] = dot(scores, value_ref[:, at], NN)
-        turned_ref[at, :] = query.T
+        turned = query.T
+        turned_ref[at, :] = turned
+        scores_ref[head] = jnp.where(kept, dot(key_ref[:, at], turned, NN), 0.0).astype(jnp.bfloat16)
 
 
 def norm_body(chain, place_ref, query_ref, turned_ref, grad_ref, inner_ref, gain_ref, *refs):
@@ -88,31 +90,34 @@
         delta_ref[DH:] = jnp.broadcast_to(jnp.sum(product, axis=0, keepdims=True), (GAIN_ROWS, DH))
 
 
-def partial_body(place_ref, query_ref, key_ref, value_ref, *refs):
+def partial_body(place_ref, query_ref, key_ref, value_ref, scores_ref, *refs):
     attn_refs, state_refs = refs[:CHAINS], refs[CHAINS : CHAINS + HEADS]
-    grad_query_ref, key_part_ref, value_part_ref = refs[-3:]
+    later_refs, (grad_query_ref, *out_refs) = refs[CHAINS + HEADS : -5], refs[-5:]
     keep, kept = causal(), causal(True)
     for at_head, state_ref in enumerate(state_refs):
         chain, mask = at_head // GROUP, ORDER[at_head % GROUP]
         at, here = own_columns(place_ref, mask, chain), own_columns(place_ref, mask)
         query, key, value, grad_attn = query_ref[:, at], key_ref[:, at], value_ref[:, at], attn_refs[chain][:, here]
-        turned = jnp.where(kept, dot(key, query, NT), 0.0).astype(jnp.bfloat16)
+        turned = scores_ref[chain * GROUP + (place_ref[0] & (GROUP - 1) ^ mask)]
         grad_scores = jnp.where(keep, dot(grad_attn, value, NT), 0.0).astype(jnp.bfloat16)
         turned_grad = jnp.where(kept, dot(value, grad_attn, NT), 0.0).astype(jnp.bfloat16)
         carried = dot(grad_attn, state_ref[...].astype(jnp.bfloat16), NT)
         grad_query_ref[:, at] = (dot(grad_scores, key, NN) + carried).astype(jnp.bfloat16)
-        key_part_ref[:, at] = dot(turned_grad, query, NN)
-        value_part_ref[:, at] = dot(turned, grad_attn, NN)
+        parts = [dot(turned_grad, query, NN), dot(turned, grad_attn, NN)]
+        if chain == 0:
+            state = later_refs[at_head][:DH].astype(jnp.bfloat16)
+            parts = [parts[0] + dot(value, state, NT), parts[1] + dot(key, state, NN)]
+        for part, out_ref in zip(parts, out_refs[2 * chain :]):
+            out_ref[:, here] = part.astype(out_ref.dtype)
 
 
 def final_body(place_ref, key_ref, value_ref, key_part_ref, value_part_ref, *refs):
-    state_refs, (grad_key_ref, grad_value_ref) = refs[:HEADS], refs[HEADS:]
-    rows = pl.ds(pl.multiple_of(pl.program_id(0) * PART_ROWS, PART_ROWS), PART_ROWS)
-    for at_head, state_ref in enumerate(state_refs):
-        at = own_columns(place_ref, ORDER[at_head % GROUP], at_head // GROUP)
+    state_refs, (grad_key_ref, grad_value_ref) = refs[:GROUP], refs[-2:]
+    for mask, state_ref in zip(ORDER, state_refs):
+        at, here = own_columns(place_ref, mask, 1), own_columns(place_ref, mask)
         state = state_ref[:DH].astype(jnp.bfloat16)
-        grad_key_ref[:, at] = (key_part_ref[rows, at] + dot(value_ref[rows, at], state, NT)).astype(jnp.bfloat16)
-        grad_value_ref[:, at] = (value_part_ref[rows, at] + dot(key_ref[rows, at], state, NN)).astype(jnp.bfloat16)
+        grad_key_ref[:, here] = (key_part_ref[:, here] + dot(value_ref[:, at], state, NT)).astype(jnp.bfloat16)
+        grad_value_ref[:, here] = (value_part_ref[:, here] + dot(key_ref[:, at], state, NN)).astype(jnp.bfloat16)
 
 
 def gain_body(place_ref, *refs):
@@ -147,7 +152,7 @@
 PLACE = pl.BlockSpec(memory_space=pltpu.SMEM)
 
 
-def call(body, in_specs, out_specs, outs, flops, name, steps=1, scratch=()):
+def call(body, in_specs, out_specs, outs, flops, name, steps=1, scratch=(), aliases=None):
     return pl.pallas_call(
         body,
         grid=(steps,),
@@ -155,6 +160,7 @@
         out_specs=out_specs,
         out_shape=outs,
         scratch_shapes=scratch,
+        input_output_aliases=aliases or {},
         compiler_params=pltpu.CompilerParams(vmem_limit_bytes=16 * 1024 * 1024),
         cost_estimate=pl.CostEstimate(flops=flops, bytes_accessed=2 << 20, transcendentals=0),
         name=name,
@@ -220,7 +226,9 @@
     taller = jax.ShapeDtypeStruct((DH + GAIN_ROWS, DH), jnp.float32)
     full_float = jax.ShapeDtypeStruct(flat, jnp.float32)
     full_low = jax.ShapeDtypeStruct(flat, jnp.bfloat16)
+    scores_low = jax.ShapeDtypeStruct((HEADS, BLOCK, BLOCK), jnp.bfloat16)
     turned_low = jax.ShapeDtypeStruct(flat[::-1], jnp.bfloat16)
+    half_float = jax.ShapeDtypeStruct((BLOCK, WIDE), jnp.float32)
     half_low = jax.ShapeDtypeStruct((BLOCK, WIDE), jnp.bfloat16)
     short, tall, wide, half = whole(*square.shape), whole(*taller.shape), whole(*flat), whole(BLOCK, WIDE)
     unit = 2 * BLOCK * DH * DH * HEADS
@@ -239,14 +247,14 @@
     inner_call = call(
         lambda place_ref, *refs: inner_body(*refs),
         [wide] * 3,
-        [wide, whole(*turned_low.shape)],
-        [full_float, turned_low],
+        [wide, whole(*turned_low.shape), whole(*scores_low.shape)],
+        [full_float, turned_low, scores_low],
         16 * unit,
         "inner",
     )
     first, second = [lax.optimization_barrier(plane_swap(deltas[chain])) for chain in chains]
     second, operands = lax.optimization_barrier((second, (place, query, key, value)))
-    state, (inner, turned) = carried_in(first, False, place, inner_call, operands)
+    state, (inner, turned, scores) = carried_in(first, False, place, inner_call, operands)
     states = [state, carried_in(second, False, place)[0]]
     attns, later = [], []
     for chain in range(CHAINS):
@@ -261,25 +269,32 @@
         attns.append(attn)
         held = lax.optimization_barrier(plane_swap(deltas))
         later += carried_in(held, True, place)[0]
-    grad_query, key_part, value_part = call(
+    chunks = [pl.BlockSpec((BLOCK, WIDE), lambda step, chain=chain: (0, chain)) for chain in range(CHAINS)]
+    grad_query, grad_key, grad_value, key_part, value_part = call(
         partial_body,
-        [wide] * 3 + [half] * CHAINS + [short] * HEADS,
-        [wide] * 3,
-        [full_low, full_float, full_float],
+        [wide] * 3 + [whole(*scores_low.shape)] + [half] * CHAINS + [short] * HEADS + [tall] * GROUP,
+        [wide] + [chunks[0]] * 2 + [half] * 2,
+        [full_low] * 3 + [half_float] * 2,
         48 * unit,
         "partial",
-    )(place, query, key, value, *attns, *[state for chain in states for state in chain])
+    )(place, query, key, value, scores, *attns, *[state for chain in states for state in chain], *later[:GROUP])
     gain_terms = call(
         gain_body, [tall] * HEADS, whole(HEADS, DH), jax.ShapeDtypeStruct((HEADS, DH), jnp.float32), unit, "gain"
     )(place, *later)
+    gain_terms, value_part = lax.optimization_barrier((gain_terms, value_part))
     docs, mask = lax.axis_size("dp"), 1
     while mask < docs:
         gain_terms = gain_terms + lax.ppermute(gain_terms, "dp", [(d, d ^ mask) for d in range(docs)])
         mask *= 2
-    chunk = pl.BlockSpec((PART_ROWS, HEADS * DH), lambda step: (step, 0))
     grad_key, grad_value = call(
-        final_body, [wide] * 4 + [tall] * HEADS, [chunk] * 2, [full_low] * 2, 16 * unit, "final", steps=PARTS
-    )(place, key, value, key_part, value_part, *later)
+        final_body,
+        [wide] * 2 + [half] * 2 + [tall] * GROUP + [pl.BlockSpec(memory_space=pl.ANY)] * 2,
+        [chunks[1]] * 2,
+        [full_low] * 2,
+        8 * unit,
+        "final",
+        aliases={5 + GROUP: 0, 6 + GROUP: 1},
+    )(place, key, value, key_part, value_part, *later[GROUP:], grad_key, grad_value)
     grad_gain = gain_terms / math.sqrt(lax.axis_size("seq") * docs * BLOCK)
     return (
         grad_query.reshape(full),

time: 61.1 us -> 60.7 us (level)
    pallas_call x1, Pallas kernels: 0.93 us -> 1.63 us  [carried_in(): result = beside(*operands)]
    pallas_call x2, Pallas kernels: 4.69 us -> 4.02 us  [the longest x1 2.92 us: local(): call(partial_body, [wide] * 3 + [whole(*scores_low.shape)] + [half] * CHA...]
  transfers between devices with their start and end apart: 37 -> 37, of which waited for: 4 -> 6; matrix products, arithmetic and copies ran while one was open for 0% -> 0% of each run, Pallas kernels for 12% -> 12%
where the time goes in v23:
time: 60.7 us; the launch traced here: 60.6 us
  starting transfers between devices  46.2 us (76%)
  Pallas kernels  8.99 us (15%)
  waiting for transfers between devices  3.77 us (6%)
  between operations  0.83 us (1%)
  other arithmetic  0.76 us (1%)
    ppermute x36, starting transfers between devices, swap(): lax.ppermute(array, 'seq', [(s, s ^ mask) for s in range(lax.axis_size('s...  46.2 us
    ppermute x36, waiting for transfers between devices, swap(): lax.ppermute(array, 'seq', [(s, s ^ mask) for s in range(lax.axis_size('s...  3.72 us
    pallas_call x1, Pallas kernels, local(): call(partial_body, [wide] * 3 + [whole(*scores_low.shape)] + [half] * CHA...  2.92 us
    pallas_call x1, Pallas kernels, carried_in(): result = beside(*operands)  1.63 us
    pallas_call x1, Pallas kernels, local(): call(delta_body, [pl.BlockSpec(memory_space=pltpu.HBM)] * 2, [short] * HE...  1.61 us
    pallas_call x2, Pallas kernels, local(): call(functools.partial(norm_body, chain), [wide, whole(*turned_low.shape)...  1.4 us
  transfers between devices with their start and end apart: 37, of which 6 were waited for; matrix products, arithmetic and copies ran while one was open for 0% of the time, Pallas kernels for 12%

profile of v23, /device:TPU:0, one launch (start us, length us, event | category | flops | bytes accessed | tf_op | source)
XLA Modules:
  0.0 60.6 jit_solution(4902147620929795426)
XLA Ops:
  0.7 1.6 %delta.1 = (f32[128,128]{1,0:T(8,128)S(1)}, f32[128,128]{1,0:T(8,128)S(1)}, f32[128,128]{1,0:T(8,128)S(1)}, f32[128,128]{1,0:T(8,128)S(1)}, f32[128,128]{1,0:T(8...) custom-call(s32[1]{0:T(128)} %bitcast.place_ref, bf16[256,1024]{1,0:T(8,128)(2,1)} %bitcast.17, ...), custom_call_target="tpu_custom_call" | custom-call | flops 402653184 | bytes 2097152 | tf_op jit(solution)/shard_map/delta/pallas_call | solution.py:237
  2.3 4.0 %collective-permute-start = (f32[128,128]{1,0:T(8,128)S(1)}, f32[128,128]{1,0:T(8,128)S(1)}, u32[]{:S(2)}, u32[]{:S(2)}) collective-permute-start(f32[128,128]{1,0:T(8,128)S(1)} %get-tuple-element.90), channel_id=1, source_target_pairs={{0,6},{2,4},{4,2},{6,0},{8,14},{10,12},{12,10},{14,8},{16,22},{18,... | collective-permute-start | bytes 196616 | tf_op jit(solution)/shard_map/ppermute | solution.py:183
  6.9 2.8 %collective-permute-start.6 = (f32[128,128]{1,0:T(8,128)S(1)}, f32[128,128]{1,0:T(8,128)S(1)}, u32[]{:S(2)}, u32[]{:S(2)}) collective-permute-start(f32[128,128]{1,0:T(8,128)S(1)} %get-tuple-element.98), channel_id=1, source_target_pairs={{0,6},{2,4},{4,2},{6,0},{8,14},{10,12},{12,10},{14,8},{16,22},{18,... | collective-permute-start | bytes 196616 | tf_op jit(solution)/shard_map/ppermute | solution.py:183
  11.3 3.7 %collective-permute-start.3 = (f32[128,128]{1,0:T(8,128)S(1)}, f32[128,128]{1,0:T(8,128)S(1)}, u32[]{:S(2)}, u32[]{:S(2)}) collective-permute-start(f32[128,128]{1,0:T(8,128)S(1)} %add_add_fusion.7), channel_id=1, source_target_pairs={{0,24},{2,26},{4,28},{6,30},{8,16},{10,18},{12,20},{14,22},{16,8},... | collective-permute-start | bytes 196616 | tf_op jit(solution)/shard_map/ppermute | solution.py:183
  15.0 0.8 %collective-permute-start.5 = (f32[128,128]{1,0:T(8,128)S(1)}, f32[128,128]{1,0:T(8,128)S(1)}, u32[]{:S(2)}, u32[]{:S(2)}) collective-permute-start(f32[128,128]{1,0:T(8,128)S(1)} %add_add_fusion.7), channel_id=1, source_target_pairs={{0,8},{2,10},{4,12},{6,14},{8,0},{10,2},{12,4},{14,6},{16,24},{18,... | collective-permute-start | bytes 196616 | tf_op jit(solution)/shard_map/ppermute | solution.py:183
  15.8 3.7 %collective-permute-start.12 = (f32[128,128]{1,0:T(8,128)S(1)}, f32[128,128]{1,0:T(8,128)S(1)}, u32[]{:S(2)}, u32[]{:S(2)}) collective-permute-start(f32[128,128]{1,0:T(8,128)S(1)} %add_add_fusion.5), channel_id=1, source_target_pairs={{0,24},{2,26},{4,28},{6,30},{8,16},{10,18},{12,20},{14,22},{16,8},... | collective-permute-start | bytes 196616 | tf_op jit(solution)/shard_map/ppermute | solution.py:183
  19.5 1.6 %inner.1 = (f32[256,1024]{1,0:T(8,128)S(1)}, bf16[1024,256]{1,0:T(8,128)(2,1)S(1)}, bf16[8,256,256]{2,1,0:T(8,128)(2,1)S(1)}) custom-call(s32[1]{0:T(128)} %bitcast.place_ref, bf16[256,1024]{1,0:T(8,128)(2,1)S(1)} %bitcast.13, bf16[256,1024]{1,0:T(8,128)(2,1)S(1)} %bitcast.18, bf16[256,1024]{1,0:T(8,128)(2,1)S(1)} %bitcast.22), custom_call_target="tpu_custom_call" | custom-call | flops 1073741824 | bytes 2097152 | tf_op jit(solution)/shard_map/inner/pallas_call | solution.py:198
  21.2 0.8 %collective-permute-start.14 = (f32[128,128]{1,0:T(8,128)S(1)}, f32[128,128]{1,0:T(8,128)S(1)}, u32[]{:S(2)}, u32[]{:S(2)}) collective-permute-start(f32[128,128]{1,0:T(8,128)S(1)} %add_add_fusion.5), channel_id=1, source_target_pairs={{0,8},{2,10},{4,12},{6,14},{8,0},{10,2},{12,4},{14,6},{16,24},{18,... | collective-permute-start | bytes 196616 | tf_op jit(solution)/shard_map/ppermute | solution.py:183
  22.0 1.4 %collective-permute-done.4.refs_2_ = f32[128,128]{1,0:T(8,128)S(1)} collective-permute-done((f32[128,128]{1,0:T(8,128)S(1)}, f32[128,128]{1,0:T(8,128)S(1)}, u32[]{:S(2)}, u32[]{:S(2)}) %collective-permute-start.4) | collective-permute-done | bytes 65568 | tf_op jit(solution)/shard_map/ppermute | solution.py:183
  23.5 1.8 %collective-permute-start.9 = (f32[128,128]{1,0:T(8,128)S(1)}, f32[128,128]{1,0:T(8,128)S(1)}, u32[]{:S(2)}, u32[]{:S(2)}) collective-permute-start(f32[128,128]{1,0:T(8,128)S(1)} %get-tuple-element.119), channel_id=1, source_target_pairs={{0,6},{2,4},{4,2},{6,0},{8,14},{10,12},{12,10},{14,8},{16,22},{18,... | collective-permute-start | bytes 196616 | tf_op jit(solution)/shard_map/ppermute | solution.py:183
  25.3 1.0 %collective-permute-start.10 = (f32[128,128]{1,0:T(8,128)S(1)}, f32[128,128]{1,0:T(8,128)S(1)}, u32[]{:S(2)}, u32[]{:S(2)}) collective-permute-start(f32[128,128]{1,0:T(8,128)S(1)} %get-tuple-element.120), channel_id=1, source_target_pairs={{0,4},{2,6},{4,0},{6,2},{8,12},{10,14},{12,8},{14,10},{16,20},{18,... | collective-permute-start | bytes 196616 | tf_op jit(solution)/shard_map/ppermute | solution.py:183
  26.2 0.8 %collective-permute-start.11 = (f32[128,128]{1,0:T(8,128)S(1)}, f32[128,128]{1,0:T(8,128)S(1)}, u32[]{:S(2)}, u32[]{:S(2)}) collective-permute-start(f32[128,128]{1,0:T(8,128)S(1)} %get-tuple-element.121), channel_id=1, source_target_pairs={{0,2},{2,0},{4,6},{6,4},{8,10},{10,8},{12,14},{14,12},{16,18},{18,... | collective-permute-start | bytes 196616 | tf_op jit(solution)/shard_map/ppermute | solution.py:183
  27.2 1.8 %collective-permute-start.15 = (f32[128,128]{1,0:T(8,128)S(1)}, f32[128,128]{1,0:T(8,128)S(1)}, u32[]{:S(2)}, u32[]{:S(2)}) collective-permute-start(f32[128,128]{1,0:T(8,128)S(1)} %get-tuple-element.131), channel_id=1, source_target_pairs={{0,6},{2,4},{4,2},{6,0},{8,14},{10,12},{12,10},{14,8},{16,22},{18,... | collective-permute-start | bytes 196616 | tf_op jit(solution)/shard_map/ppermute | solution.py:183
  28.9 1.0 %collective-permute-start.16 = (f32[128,128]{1,0:T(8,128)S(1)}, f32[128,128]{1,0:T(8,128)S(1)}, u32[]{:S(2)}, u32[]{:S(2)}) collective-permute-start(f32[128,128]{1,0:T(8,128)S(1)} %get-tuple-element.132), channel_id=1, source_target_pairs={{0,4},{2,6},{4,0},{6,2},{8,12},{10,14},{12,8},{14,10},{16,20},{18,... | collective-permute-start | bytes 196616 | tf_op jit(solution)/shard_map/ppermute | solution.py:183
  29.9 0.8 %collective-permute-start.17 = (f32[128,128]{1,0:T(8,128)S(1)}, f32[128,128]{1,0:T(8,128)S(1)}, u32[]{:S(2)}, u32[]{:S(2)}) collective-permute-start(f32[128,128]{1,0:T(8,128)S(1)} %get-tuple-element.133), channel_id=1, source_target_pairs={{0,2},{2,0},{4,6},{6,4},{8,10},{10,8},{12,14},{14,12},{16,18},{18,... | collective-permute-start | bytes 196616 | tf_op jit(solution)/shard_map/ppermute | solution.py:183
  30.7 0.7 %norm.2 = (bf16[256,512]{1,0:T(8,128)(2,1)S(1)}, f32[136,128]{1,0:T(8,128)S(1)}, f32[136,128]{1,0:T(8,128)S(1)}, f32[136,128]{1,0:T(8,128)S(1)}, f32[136,128]{1,0:T(8,128)S(1)}) custom-call(s32[1]{0:T(128)} %bitcast.place_ref, bf16[256,1024]{1,0:T(8,128)(2,1)S(1)} %bitcast.14, bf16[1024,256]{1,0:T(8,128)(2,1)S(1)} %get-tuple-element.113.turned_ref, ...), custom_call_target="tpu_custom_call" | custom-call | flops 536870912 | bytes 2097152 | tf_op jit(solution)/shard_map/norm/pallas_call | solution.py:261
  31.4 1.8 %collective-permute-start.18 = (f32[136,128]{1,0:T(8,128)S(1)}, f32[136,128]{1,0:T(8,128)S(1)}, u32[]{:S(2)}, u32[]{:S(2)}) collective-permute-start(f32[136,128]{1,0:T(8,128)S(1)} %get-tuple-element.136), channel_id=1, source_target_pairs={{0,6},{2,4},{4,2},{6,0},{8,14},{10,12},{12,10},{14,8},{16,22},{18,... | collective-permute-start | bytes 208904 | tf_op jit(solution)/shard_map/ppermute | solution.py:183
  33.2 0.9 %collective-permute-start.19 = (f32[136,128]{1,0:T(8,128)S(1)}, f32[136,128]{1,0:T(8,128)S(1)}, u32[]{:S(2)}, u32[]{:S(2)}) collective-permute-start(f32[136,128]{1,0:T(8,128)S(1)} %get-tuple-element.137), channel_id=1, source_target_pairs={{0,4},{2,6},{4,0},{6,2},{8,12},{10,14},{12,8},{14,10},{16,20},{18,... | collective-permute-start | bytes 208904 | tf_op jit(solution)/shard_map/ppermute | solution.py:183
  34.2 0.8 %collective-permute-start.20 = (f32[136,128]{1,0:T(8,128)S(1)}, f32[136,128]{1,0:T(8,128)S(1)}, u32[]{:S(2)}, u32[]{:S(2)}) collective-permute-start(f32[136,128]{1,0:T(8,128)S(1)} %get-tuple-element.138), channel_id=1, source_target_pairs={{0,2},{2,0},{4,6},{6,4},{8,10},{10,8},{12,14},{14,12},{16,18},{18,... | collective-permute-start | bytes 208904 | tf_op jit(solution)/shard_map/ppermute | solution.py:183
  35.7 1.8 %collective-permute-start.27 = (f32[136,128]{1,0:T(8,128)S(1)}, f32[136,128]{1,0:T(8,128)S(1)}, u32[]{:S(2)}, u32[]{:S(2)}) collective-permute-start(f32[136,128]{1,0:T(8,128)S(1)} %get-tuple-element.153), channel_id=1, source_target_pairs={{0,6},{2,4},{4,2},{6,0},{8,14},{10,12},{12,10},{14,8},{16,22},{18,... | collective-permute-start | bytes 208904 | tf_op jit(solution)/shard_map/ppermute | solution.py:183
  37.5 0.9 %collective-permute-start.28 = (f32[136,128]{1,0:T(8,128)S(1)}, f32[136,128]{1,0:T(8,128)S(1)}, u32[]{:S(2)}, u32[]{:S(2)}) collective-permute-start(f32[136,128]{1,0:T(8,128)S(1)} %get-tuple-element.154), channel_id=1, source_target_pairs={{0,4},{2,6},{4,0},{6,2},{8,12},{10,14},{12,8},{14,10},{16,20},{18,... | collective-permute-start | bytes 208904 | tf_op jit(solution)/shard_map/ppermute | solution.py:183
  38.5 0.8 %collective-permute-start.29 = (f32[136,128]{1,0:T(8,128)S(1)}, f32[136,128]{1,0:T(8,128)S(1)}, u32[]{:S(2)}, u32[]{:S(2)}) collective-permute-start(f32[136,128]{1,0:T(8,128)S(1)} %get-tuple-element.155), channel_id=1, source_target_pairs={{0,2},{2,0},{4,6},{6,4},{8,10},{10,8},{12,14},{14,12},{16,18},{18,... | collective-permute-start | bytes 208904 | tf_op jit(solution)/shard_map/ppermute | solution.py:183
  39.4 2.8 %collective-permute-start.22 = (f32[136,128]{1,0:T(8,128)S(1)}, f32[136,128]{1,0:T(8,128)S(1)}, u32[]{:S(2)}, u32[]{:S(2)}) collective-permute-start(f32[136,128]{1,0:T(8,128)S(1)} %add_add_fusion.3), channel_id=1, source_target_pairs={{0,24},{2,26},{4,28},{6,30},{8,16},{10,18},{12,20},{14,22},{16,8},... | collective-permute-start | bytes 208904 | tf_op jit(solution)/shard_map/ppermute | solution.py:183
  42.9 1.0 %collective-permute-start.30 = (f32[136,128]{1,0:T(8,128)S(1)}, f32[136,128]{1,0:T(8,128)S(1)}, u32[]{:S(2)}, u32[]{:S(2)}) collective-permute-start(f32[136,128]{1,0:T(8,128)S(1)} %add_add_fusion.1), channel_id=1, source_target_pairs={{0,8},{2,10},{4,12},{6,14},{8,0},{10,2},{12,4},{14,6},{16,24},{18,... | collective-permute-start | bytes 208904 | tf_op jit(solution)/shard_map/ppermute | solution.py:183
  43.9 2.7 %collective-permute-start.31 = (f32[136,128]{1,0:T(8,128)S(1)}, f32[136,128]{1,0:T(8,128)S(1)}, u32[]{:S(2)}, u32[]{:S(2)}) collective-permute-start(f32[136,128]{1,0:T(8,128)S(1)} %add_add_fusion.1), channel_id=1, source_target_pairs={{0,24},{2,26},{4,28},{6,30},{8,16},{10,18},{12,20},{14,22},{16,8},... | collective-permute-start | bytes 208904 | tf_op jit(solution)/shard_map/ppermute | solution.py:183
  46.7 1.4 %collective-permute-done.23.refs_3_ = f32[136,128]{1,0:T(8,128)S(1)} collective-permute-done((f32[136,128]{1,0:T(8,128)S(1)}, f32[136,128]{1,0:T(8,128)S(1)}, u32[]{:S(2)}, u32[]{:S(2)}) %collective-permute-start.23) | collective-permute-done | bytes 69664 | tf_op jit(solution)/shard_map/ppermute | solution.py:183
  48.3 2.0 %collective-permute-start.24 = (f32[136,128]{1,0:T(8,128)S(1)}, f32[136,128]{1,0:T(8,128)S(1)}, u32[]{:S(2)}, u32[]{:S(2)}) collective-permute-start(f32[136,128]{1,0:T(8,128)S(1)} %get-tuple-element.147), channel_id=1, source_target_pairs={{0,6},{2,4},{4,2},{6,0},{8,14},{10,12},{12,10},{14,8},{16,22},{18,... | collective-permute-start | bytes 208904 | tf_op jit(solution)/shard_map/ppermute | solution.py:183
  50.8 1.0 %collective-permute-start.26 = (f32[136,128]{1,0:T(8,128)S(1)}, f32[136,128]{1,0:T(8,128)S(1)}, u32[]{:S(2)}, u32[]{:S(2)}) collective-permute-start(f32[136,128]{1,0:T(8,128)S(1)} %get-tuple-element.149), channel_id=1, source_target_pairs={{0,2},{2,0},{4,6},{6,4},{8,10},{10,8},{12,14},{14,12},{16,18},{18,... | collective-permute-start | bytes 208904 | tf_op jit(solution)/shard_map/ppermute | solution.py:183
  52.0 2.0 %collective-permute-start.33 = (f32[136,128]{1,0:T(8,128)S(1)}, f32[136,128]{1,0:T(8,128)S(1)}, u32[]{:S(2)}, u32[]{:S(2)}) collective-permute-start(f32[136,128]{1,0:T(8,128)S(1)} %get-tuple-element.164), channel_id=1, source_target_pairs={{0,6},{2,4},{4,2},{6,0},{8,14},{10,12},{12,10},{14,8},{16,22},{18,... | collective-permute-start | bytes 208904 | tf_op jit(solution)/shard_map/ppermute | solution.py:183
  54.5 1.0 %collective-permute-start.35 = (f32[136,128]{1,0:T(8,128)S(1)}, f32[136,128]{1,0:T(8,128)S(1)}, u32[]{:S(2)}, u32[]{:S(2)}) collective-permute-start(f32[136,128]{1,0:T(8,128)S(1)} %get-tuple-element.166), channel_id=1, source_target_pairs={{0,2},{2,0},{4,6},{6,4},{8,10},{10,8},{12,14},{14,12},{16,18},{18,... | collective-permute-start | bytes 208904 | tf_op jit(solution)/shard_map/ppermute | solution.py:183
  55.6 2.9 %partial.1 = (bf16[256,1024]{1,0:T(8,128)(2,1)}, bf16[256,1024]{1,0:T(8,128)(2,1)}, bf16[256,1024]{1,0:T(8,128)(2,1)}, f32[256,512]{1,0:T(8,128)S(1)}, f32[256,512]{1,0:T(8,128)S(1)}) custom-call(s32[1]{0:T(128)} %bitcast.place_ref, bf16[256,1024]{1,0:T(8,128)(2,1)S(1)} %bitcast.16, bf16[256,1024]{1,0:T(8,128)(2,1)S(1)} %bitcast.19, ...), custom_call_target="tpu_custom_call" | custom-call | flops 3221225472 | bytes 2097152 | tf_op jit(solution)/shard_map/partial/pallas_call | solution.py:273
  58.8 1.1 %final.1 = (bf16[256,1024]{1,0:T(8,128)(2,1)}, bf16[256,1024]{1,0:T(8,128)(2,1)}) custom-call(s32[1]{0:T(128)} %bitcast.place_ref, bf16[256,1024]{1,0:T(8,128)(2,1)S(1)} %bitcast.20, bf16[256,1024]{1,0:T(8,128)(2,1)S(1)} %bitcast.24, f32[256,512]{1,0:T(8,128)S(1)} %get-tuple-element.151.key_part_ref, ...), custom_call_target="tpu_custom_call", output_to_operand_aliasing={{0}: (9, {}), {1}: (10, {})} | custom-call | flops 536870912 | bytes 2097152 | tf_op jit(solution)/shard_map/final/pallas_call | solution.py:289
  (72 shorter events, 6.4 us)
Async XLA Ops:
  2.3 8.0 %collective-permute-start = (f32[128,128]{1,0:T(8,128)S(1)}, f32[128,128]{1,0:T(8,128)S(1)}, u32[]{:S(2)}, u32[]{:S(2)}) collective-permute-start(f32[128,128]{1,0:T(8,128)S(1)} %get-tuple-element.90), channel_id=1, source_target_pairs={{0,6},{2,4},{4,2},{6,0},{8,14},{10,12},{12,10},{14,8},{16,22},{18,... | collective-permute-start | bytes 196616 | tf_op jit(solution)/shard_map/ppermute | solution.py:183
  6.2 5.1 %collective-permute-start.1 = (f32[128,128]{1,0:T(8,128)S(1)}, f32[128,128]{1,0:T(8,128)S(1)}, u32[]{:S(2)}, u32[]{:S(2)}) collective-permute-start(f32[128,128]{1,0:T(8,128)S(1)} %get-tuple-element.91), channel_id=1, source_target_pairs={{0,4},{2,6},{4,0},{6,2},{8,12},{10,14},{12,8},{14,10},{16,20},{18,... | collective-permute-start | bytes 196616 | tf_op jit(solution)/shard_map/ppermute | solution.py:183
  6.8 4.6 %collective-permute-start.2 = (f32[128,128]{1,0:T(8,128)S(1)}, f32[128,128]{1,0:T(8,128)S(1)}, u32[]{:S(2)}, u32[]{:S(2)}) collective-permute-start(f32[128,128]{1,0:T(8,128)S(1)} %get-tuple-element.92), channel_id=1, source_target_pairs={{0,2},{2,0},{4,6},{6,4},{8,10},{10,8},{12,14},{14,12},{16,18},{18,... | collective-permute-start | bytes 196616 | tf_op jit(solution)/shard_map/ppermute | solution.py:183
  6.9 8.1 %collective-permute-start.6 = (f32[128,128]{1,0:T(8,128)S(1)}, f32[128,128]{1,0:T(8,128)S(1)}, u32[]{:S(2)}, u32[]{:S(2)}) collective-permute-start(f32[128,128]{1,0:T(8,128)S(1)} %get-tuple-element.98), channel_id=1, source_target_pairs={{0,6},{2,4},{4,2},{6,0},{8,14},{10,12},{12,10},{14,8},{16,22},{18,... | collective-permute-start | bytes 196616 | tf_op jit(solution)/shard_map/ppermute | solution.py:183
  9.7 6.1 %collective-permute-start.7 = (f32[128,128]{1,0:T(8,128)S(1)}, f32[128,128]{1,0:T(8,128)S(1)}, u32[]{:S(2)}, u32[]{:S(2)}) collective-permute-start(f32[128,128]{1,0:T(8,128)S(1)} %get-tuple-element.99), channel_id=1, source_target_pairs={{0,4},{2,6},{4,0},{6,2},{8,12},{10,14},{12,8},{14,10},{16,20},{18,... | collective-permute-start | bytes 196616 | tf_op jit(solution)/shard_map/ppermute | solution.py:183
  10.2 5.6 %collective-permute-start.8 = (f32[128,128]{1,0:T(8,128)S(1)}, f32[128,128]{1,0:T(8,128)S(1)}, u32[]{:S(2)}, u32[]{:S(2)}) collective-permute-start(f32[128,128]{1,0:T(8,128)S(1)} %get-tuple-element.100), channel_id=1, source_target_pairs={{0,2},{2,0},{4,6},{6,4},{8,10},{10,8},{12,14},{14,12},{16,18},{18,... | collective-permute-start | bytes 196616 | tf_op jit(solution)/shard_map/ppermute | solution.py:183
  11.3 9.8 %collective-permute-start.3 = (f32[128,128]{1,0:T(8,128)S(1)}, f32[128,128]{1,0:T(8,128)S(1)}, u32[]{:S(2)}, u32[]{:S(2)}) collective-permute-start(f32[128,128]{1,0:T(8,128)S(1)} %add_add_fusion.7), channel_id=1, source_target_pairs={{0,24},{2,26},{4,28},{6,30},{8,16},{10,18},{12,20},{14,22},{16,8},... | collective-permute-start | bytes 196616 | tf_op jit(solution)/shard_map/ppermute | solution.py:183
  15.0 8.3 %collective-permute-start.4 = (f32[128,128]{1,0:T(8,128)S(1)}, f32[128,128]{1,0:T(8,128)S(1)}, u32[]{:S(2)}, u32[]{:S(2)}) collective-permute-start(f32[128,128]{1,0:T(8,128)S(1)} %add_add_fusion.7), channel_id=1, source_target_pairs={{0,16},{2,18},{4,20},{6,22},{8,24},{10,26},{12,28},{14,30},{16,0},... | collective-permute-start | bytes 196616 | tf_op jit(solution)/shard_map/ppermute | solution.py:183
  15.0 8.3 %collective-permute-start.5 = (f32[128,128]{1,0:T(8,128)S(1)}, f32[128,128]{1,0:T(8,128)S(1)}, u32[]{:S(2)}, u32[]{:S(2)}) collective-permute-start(f32[128,128]{1,0:T(8,128)S(1)} %add_add_fusion.7), channel_id=1, source_target_pairs={{0,8},{2,10},{4,12},{6,14},{8,0},{10,2},{12,4},{14,6},{16,24},{18,... | collective-permute-start | bytes 196616 | tf_op jit(solution)/shard_map/ppermute | solution.py:183
  15.8 10.4 %collective-permute-start.12 = (f32[128,128]{1,0:T(8,128)S(1)}, f32[128,128]{1,0:T(8,128)S(1)}, u32[]{:S(2)}, u32[]{:S(2)}) collective-permute-start(f32[128,128]{1,0:T(8,128)S(1)} %add_add_fusion.5), channel_id=1, source_target_pairs={{0,24},{2,26},{4,28},{6,30},{8,16},{10,18},{12,20},{14,22},{16,8},... | collective-permute-start | bytes 196616 | tf_op jit(solution)/shard_map/ppermute | solution.py:183
  19.5 7.5 %collective-permute-start.13 = (f32[128,128]{1,0:T(8,128)S(1)}, f32[128,128]{1,0:T(8,128)S(1)}, u32[]{:S(2)}, u32[]{:S(2)}) collective-permute-start(f32[128,128]{1,0:T(8,128)S(1)} %add_add_fusion.5), channel_id=1, source_target_pairs={{0,16},{2,18},{4,20},{6,22},{8,24},{10,26},{12,28},{14,30},{16,0},... | collective-permute-start | bytes 196616 | tf_op jit(solution)/shard_map/ppermute | solution.py:183
  21.2 5.9 %collective-permute-start.14 = (f32[128,128]{1,0:T(8,128)S(1)}, f32[128,128]{1,0:T(8,128)S(1)}, u32[]{:S(2)}, u32[]{:S(2)}) collective-permute-start(f32[128,128]{1,0:T(8,128)S(1)} %add_add_fusion.5), channel_id=1, source_target_pairs={{0,8},{2,10},{4,12},{6,14},{8,0},{10,2},{12,4},{14,6},{16,24},{18,... | collective-permute-start | bytes 196616 | tf_op jit(solution)/shard_map/ppermute | solution.py:183
  23.5 6.4 %collective-permute-start.9 = (f32[128,128]{1,0:T(8,128)S(1)}, f32[128,128]{1,0:T(8,128)S(1)}, u32[]{:S(2)}, u32[]{:S(2)}) collective-permute-start(f32[128,128]{1,0:T(8,128)S(1)} %get-tuple-element.119), channel_id=1, source_target_pairs={{0,6},{2,4},{4,2},{6,0},{8,14},{10,12},{12,10},{14,8},{16,22},{18,... | collective-permute-start | bytes 196616 | tf_op jit(solution)/shard_map/ppermute | solution.py:183
  25.3 5.5 %collective-permute-start.10 = (f32[128,128]{1,0:T(8,128)S(1)}, f32[128,128]{1,0:T(8,128)S(1)}, u32[]{:S(2)}, u32[]{:S(2)}) collective-permute-start(f32[128,128]{1,0:T(8,128)S(1)} %get-tuple-element.120), channel_id=1, source_target_pairs={{0,4},{2,6},{4,0},{6,2},{8,12},{10,14},{12,8},{14,10},{16,20},{18,... | collective-permute-start | bytes 196616 | tf_op jit(solution)/shard_map/ppermute | solution.py:183
  27.2 7.0 %collective-permute-start.15 = (f32[128,128]{1,0:T(8,128)S(1)}, f32[128,128]{1,0:T(8,128)S(1)}, u32[]{:S(2)}, u32[]{:S(2)}) collective-permute-start(f32[128,128]{1,0:T(8,128)S(1)} %get-tuple-element.131), channel_id=1, source_target_pairs={{0,6},{2,4},{4,2},{6,0},{8,14},{10,12},{12,10},{14,8},{16,22},{18,... | collective-permute-start | bytes 196616 | tf_op jit(solution)/shard_map/ppermute | solution.py:183
  28.9 6.1 %collective-permute-start.16 = (f32[128,128]{1,0:T(8,128)S(1)}, f32[128,128]{1,0:T(8,128)S(1)}, u32[]{:S(2)}, u32[]{:S(2)}) collective-permute-start(f32[128,128]{1,0:T(8,128)S(1)} %get-tuple-element.132), channel_id=1, source_target_pairs={{0,4},{2,6},{4,0},{6,2},{8,12},{10,14},{12,8},{14,10},{16,20},{18,... | collective-permute-start | bytes 196616 | tf_op jit(solution)/shard_map/ppermute | solution.py:183
  29.9 5.1 %collective-permute-start.17 = (f32[128,128]{1,0:T(8,128)S(1)}, f32[128,128]{1,0:T(8,128)S(1)}, u32[]{:S(2)}, u32[]{:S(2)}) collective-permute-start(f32[128,128]{1,0:T(8,128)S(1)} %get-tuple-element.133), channel_id=1, source_target_pairs={{0,2},{2,0},{4,6},{6,4},{8,10},{10,8},{12,14},{14,12},{16,18},{18,... | collective-permute-start | bytes 196616 | tf_op jit(solution)/shard_map/ppermute | solution.py:183
  31.4 7.0 %collective-permute-start.18 = (f32[136,128]{1,0:T(8,128)S(1)}, f32[136,128]{1,0:T(8,128)S(1)}, u32[]{:S(2)}, u32[]{:S(2)}) collective-permute-start(f32[136,128]{1,0:T(8,128)S(1)} %get-tuple-element.136), channel_id=1, source_target_pairs={{0,6},{2,4},{4,2},{6,0},{8,14},{10,12},{12,10},{14,8},{16,22},{18,... | collective-permute-start | bytes 208904 | tf_op jit(solution)/shard_map/ppermute | solution.py:183
  33.2 6.0 %collective-permute-start.19 = (f32[136,128]{1,0:T(8,128)S(1)}, f32[136,128]{1,0:T(8,128)S(1)}, u32[]{:S(2)}, u32[]{:S(2)}) collective-permute-start(f32[136,128]{1,0:T(8,128)S(1)} %get-tuple-element.137), channel_id=1, source_target_pairs={{0,4},{2,6},{4,0},{6,2},{8,12},{10,14},{12,8},{14,10},{16,20},{18,... | collective-permute-start | bytes 208904 | tf_op jit(solution)/shard_map/ppermute | solution.py:183
  34.2 5.1 %collective-permute-start.20 = (f32[136,128]{1,0:T(8,128)S(1)}, f32[136,128]{1,0:T(8,128)S(1)}, u32[]{:S(2)}, u32[]{:S(2)}) collective-permute-start(f32[136,128]{1,0:T(8,128)S(1)} %get-tuple-element.138), channel_id=1, source_target_pairs={{0,2},{2,0},{4,6},{6,4},{8,10},{10,8},{12,14},{14,12},{16,18},{18,... | collective-permute-start | bytes 208904 | tf_op jit(solution)/shard_map/ppermute | solution.py:183
  35.7 6.5 %collective-permute-start.27 = (f32[136,128]{1,0:T(8,128)S(1)}, f32[136,128]{1,0:T(8,128)S(1)}, u32[]{:S(2)}, u32[]{:S(2)}) collective-permute-start(f32[136,128]{1,0:T(8,128)S(1)} %get-tuple-element.153), channel_id=1, source_target_pairs={{0,6},{2,4},{4,2},{6,0},{8,14},{10,12},{12,10},{14,8},{16,22},{18,... | collective-permute-start | bytes 208904 | tf_op jit(solution)/shard_map/ppermute | solution.py:183
  37.5 5.3 %collective-permute-start.28 = (f32[136,128]{1,0:T(8,128)S(1)}, f32[136,128]{1,0:T(8,128)S(1)}, u32[]{:S(2)}, u32[]{:S(2)}) collective-permute-start(f32[136,128]{1,0:T(8,128)S(1)} %get-tuple-element.154), channel_id=1, source_target_pairs={{0,4},{2,6},{4,0},{6,2},{8,12},{10,14},{12,8},{14,10},{16,20},{18,... | collective-permute-start | bytes 208904 | tf_op jit(solution)/shard_map/ppermute | solution.py:183
  39.3 7.4 %collective-permute-start.21 = (f32[136,128]{1,0:T(8,128)S(1)}, f32[136,128]{1,0:T(8,128)S(1)}, u32[]{:S(2)}, u32[]{:S(2)}) collective-permute-start(f32[136,128]{1,0:T(8,128)S(1)} %add_add_fusion.3), channel_id=1, source_target_pairs={{0,8},{2,10},{4,12},{6,14},{8,0},{10,2},{12,4},{14,6},{16,24},{18,... | collective-permute-start | bytes 208904 | tf_op jit(solution)/shard_map/ppermute | solution.py:183
  39.4 7.3 %collective-permute-start.22 = (f32[136,128]{1,0:T(8,128)S(1)}, f32[136,128]{1,0:T(8,128)S(1)}, u32[]{:S(2)}, u32[]{:S(2)}) collective-permute-start(f32[136,128]{1,0:T(8,128)S(1)} %add_add_fusion.3), channel_id=1, source_target_pairs={{0,24},{2,26},{4,28},{6,30},{8,16},{10,18},{12,20},{14,22},{16,8},... | collective-permute-start | bytes 208904 | tf_op jit(solution)/shard_map/ppermute | solution.py:183
  42.2 5.9 %collective-permute-start.23 = (f32[136,128]{1,0:T(8,128)S(1)}, f32[136,128]{1,0:T(8,128)S(1)}, u32[]{:S(2)}, u32[]{:S(2)}) collective-permute-start(f32[136,128]{1,0:T(8,128)S(1)} %add_add_fusion.3), channel_id=1, source_target_pairs={{0,16},{2,18},{4,20},{6,22},{8,24},{10,26},{12,28},{14,30},{16,0},... | collective-permute-start | bytes 208904 | tf_op jit(solution)/shard_map/ppermute | solution.py:183
  42.9 8.0 %collective-permute-start.30 = (f32[136,128]{1,0:T(8,128)S(1)}, f32[136,128]{1,0:T(8,128)S(1)}, u32[]{:S(2)}, u32[]{:S(2)}) collective-permute-start(f32[136,128]{1,0:T(8,128)S(1)} %add_add_fusion.1), channel_id=1, source_target_pairs={{0,8},{2,10},{4,12},{6,14},{8,0},{10,2},{12,4},{14,6},{16,24},{18,... | collective-permute-start | bytes 208904 | tf_op jit(solution)/shard_map/ppermute | solution.py:183
  43.9 7.9 %collective-permute-start.31 = (f32[136,128]{1,0:T(8,128)S(1)}, f32[136,128]{1,0:T(8,128)S(1)}, u32[]{:S(2)}, u32[]{:S(2)}) collective-permute-start(f32[136,128]{1,0:T(8,128)S(1)} %add_add_fusion.1), channel_id=1, source_target_pairs={{0,24},{2,26},{4,28},{6,30},{8,16},{10,18},{12,20},{14,22},{16,8},... | collective-permute-start | bytes 208904 | tf_op jit(solution)/shard_map/ppermute | solution.py:183
  46.7 5.2 %collective-permute-start.32 = (f32[136,128]{1,0:T(8,128)S(1)}, f32[136,128]{1,0:T(8,128)S(1)}, u32[]{:S(2)}, u32[]{:S(2)}) collective-permute-start(f32[136,128]{1,0:T(8,128)S(1)} %add_add_fusion.1), channel_id=1, source_target_pairs={{0,16},{2,18},{4,20},{6,22},{8,24},{10,26},{12,28},{14,30},{16,0},... | collective-permute-start | bytes 208904 | tf_op jit(solution)/shard_map/ppermute | solution.py:183
  48.3 6.3 %collective-permute-start.24 = (f32[136,128]{1,0:T(8,128)S(1)}, f32[136,128]{1,0:T(8,128)S(1)}, u32[]{:S(2)}, u32[]{:S(2)}) collective-permute-start(f32[136,128]{1,0:T(8,128)S(1)} %get-tuple-element.147), channel_id=1, source_target_pairs={{0,6},{2,4},{4,2},{6,0},{8,14},{10,12},{12,10},{14,8},{16,22},{18,... | collective-permute-start | bytes 208904 | tf_op jit(solution)/shard_map/ppermute | solution.py:183
  50.2 5.3 %collective-permute-start.25 = (f32[136,128]{1,0:T(8,128)S(1)}, f32[136,128]{1,0:T(8,128)S(1)}, u32[]{:S(2)}, u32[]{:S(2)}) collective-permute-start(f32[136,128]{1,0:T(8,128)S(1)} %get-tuple-element.148), channel_id=1, source_target_pairs={{0,4},{2,6},{4,0},{6,2},{8,12},{10,14},{12,8},{14,10},{16,20},{18,... | collective-permute-start | bytes 208904 | tf_op jit(solution)/shard_map/ppermute | solution.py:183
  50.8 4.7 %collective-permute-start.26 = (f32[136,128]{1,0:T(8,128)S(1)}, f32[136,128]{1,0:T(8,128)S(1)}, u32[]{:S(2)}, u32[]{:S(2)}) collective-permute-start(f32[136,128]{1,0:T(8,128)S(1)} %get-tuple-element.149), channel_id=1, source_target_pairs={{0,2},{2,0},{4,6},{6,4},{8,10},{10,8},{12,14},{14,12},{16,18},{18,... | collective-permute-start | bytes 208904 | tf_op jit(solution)/shard_map/ppermute | solution.py:183
  52.0 6.5 %collective-permute-start.33 = (f32[136,128]{1,0:T(8,128)S(1)}, f32[136,128]{1,0:T(8,128)S(1)}, u32[]{:S(2)}, u32[]{:S(2)}) collective-permute-start(f32[136,128]{1,0:T(8,128)S(1)} %get-tuple-element.164), channel_id=1, source_target_pairs={{0,6},{2,4},{4,2},{6,0},{8,14},{10,12},{12,10},{14,8},{16,22},{18,... | collective-permute-start | bytes 208904 | tf_op jit(solution)/shard_map/ppermute | solution.py:183
  (10 other events, 82.9 us)

commit v24 on v23

--- a/solution.py
+++ b/solution.py
@@ -60,16 +60,14 @@
             delta_ref[...] = delta if part == 0 else delta_ref[...] + delta
 
 
-def inner_body(query_ref, key_ref, value_ref, inner_ref, turned_ref, scores_ref):
-    keep, kept = causal(), causal(True)
+def inner_body(query_ref, key_ref, value_ref, inner_ref, turned_ref):
+    keep = causal()
     for head in range(HEADS):
         at = columns(head)
         query = query_ref[:, at]
         scores = jnp.where(keep, dot(query, key_ref[:, at], NT), 0.0).astype(jnp.bfloat16)
         inner_ref[:, at] = dot(scores, value_ref[:, at], NN)
-        turned = query.T
-        turned_ref[at, :] = turned
-        scores_ref[head] = jnp.where(kept, dot(key_ref[:, at], turned, NN), 0.0).astype(jnp.bfloat16)
+        turned_ref[at, :] = query.T
 
 
 def norm_body(chain, place_ref, query_ref, turned_ref, grad_ref, inner_ref, gain_ref, *refs):
@@ -90,7 +88,7 @@
         delta_ref[DH:] = jnp.broadcast_to(jnp.sum(product, axis=0, keepdims=True), (GAIN_ROWS, DH))
 
 
-def partial_body(place_ref, query_ref, key_ref, value_ref, scores_ref, *refs):
+def partial_body(place_ref, query_ref, key_ref, value_ref, turned_ref, *refs):
     attn_refs, state_refs = refs[:CHAINS], refs[CHAINS : CHAINS + HEADS]
     later_refs, (grad_query_ref, *out_refs) = refs[CHAINS + HEADS : -5], refs[-5:]
     keep, kept = causal(), causal(True)
@@ -98,7 +96,7 @@
         chain, mask = at_head // GROUP, ORDER[at_head % GROUP]
         at, here = own_columns(place_ref, mask, chain), own_columns(place_ref, mask)
         query, key, value, grad_attn = query_ref[:, at], key_ref[:, at], value_ref[:, at], attn_refs[chain][:, here]
-        turned = scores_ref[chain * GROUP + (place_ref[0] & (GROUP - 1) ^ mask)]
+        turned = jnp.where(kept, dot(key, turned_ref[at, :], NN), 0.0).astype(jnp.bfloat16)
         grad_scores = jnp.where(keep, dot(grad_attn, value, NT), 0.0).astype(jnp.bfloat16)
         turned_grad = jnp.where(kept, dot(value, grad_attn, NT), 0.0).astype(jnp.bfloat16)
         carried = dot(grad_attn, state_ref[...].astype(jnp.bfloat16), NT)
@@ -226,7 +224,6 @@
     taller = jax.ShapeDtypeStruct((DH + GAIN_ROWS, DH), jnp.float32)
     full_float = jax.ShapeDtypeStruct(flat, jnp.float32)
     full_low = jax.ShapeDtypeStruct(flat, jnp.bfloat16)
-    scores_low = jax.ShapeDtypeStruct((HEADS, BLOCK, BLOCK), jnp.bfloat16)
     turned_low = jax.ShapeDtypeStruct(flat[::-1], jnp.bfloat16)
     half_float = jax.ShapeDtypeStruct((BLOCK, WIDE), jnp.float32)
     half_low = jax.ShapeDtypeStruct((BLOCK, WIDE), jnp.bfloat16)
@@ -247,14 +244,14 @@
     inner_call = call(
         lambda place_ref, *refs: inner_body(*refs),
         [wide] * 3,
-        [wide, whole(*turned_low.shape), whole(*scores_low.shape)],
-        [full_float, turned_low, scores_low],
+        [wide, whole(*turned_low.shape)],
+        [full_float, turned_low],
         16 * unit,
         "inner",
     )
     first, second = [lax.optimization_barrier(plane_swap(deltas[chain])) for chain in chains]
     second, operands = lax.optimization_barrier((second, (place, query, key, value)))
-    state, (inner, turned, scores) = carried_in(first, False, place, inner_call, operands)
+    state, (inner, turned) = carried_in(first, False, place, inner_call, operands)
     states = [state, carried_in(second, False, place)[0]]
     attns, later = [], []
     for chain in range(CHAINS):
@@ -272,12 +269,12 @@
     chunks = [pl.BlockSpec((BLOCK, WIDE), lambda step, chain=chain: (0, chain)) for chain in range(CHAINS)]
     grad_query, grad_key, grad_value, key_part, value_part = call(
         partial_body,
-        [wide] * 3 + [whole(*scores_low.shape)] + [half] * CHAINS + [short] * HEADS + [tall] * GROUP,
+        [wide] * 3 + [whole(*turned_low.shape)] + [half] * CHAINS + [short] * HEADS + [tall] * GROUP,
         [wide] + [chunks[0]] * 2 + [half] * 2,
         [full_low] * 3 + [half_float] * 2,
         48 * unit,
         "partial",
-    )(place, query, key, value, scores, *attns, *[state for chain in states for state in chain], *later[:GROUP])
+    )(place, query, key, value, turned, *attns, *[state for chain in states for state in chain], *later[:GROUP])
     gain_terms = call(
         gain_body, [tall] * HEADS, whole(HEADS, DH), jax.ShapeDtypeStruct((HEADS, DH), jnp.float32), unit, "gain"
     )(place, *later)

time: 60.7 us -> 60.6 us (level)
    pallas_call x1, Pallas kernels: 1.63 us -> 0.93 us  [carried_in(): result = beside(*operands)]
  transfers between devices with their start and end apart: 37 -> 37, of which waited for: 6 -> 5; matrix products, arithmetic and copies ran while one was open for 0% -> 0% of each run, Pallas kernels for 12% -> 11%
where the time goes in v24:
time: 60.6 us; the launch traced here: 60.5 us
  starting transfers between devices  46.2 us (76%)
  Pallas kernels  8.55 us (14%)
  waiting for transfers between devices  4.2 us (7%)
  between operations  0.82 us (1%)
  other arithmetic  0.75 us (1%)
    ppermute x36, starting transfers between devices, swap(): lax.ppermute(array, 'seq', [(s, s ^ mask) for s in range(lax.axis_size('s...  46.1 us
    ppermute x36, waiting for transfers between devices, swap(): lax.ppermute(array, 'seq', [(s, s ^ mask) for s in range(lax.axis_size('s...  4.14 us
    pallas_call x1, Pallas kernels, local(): call(partial_body, [wide] * 3 + [whole(*turned_low.shape)] + [half] * CHA...  3.16 us
    pallas_call x1, Pallas kernels, local(): call(delta_body, [pl.BlockSpec(memory_space=pltpu.HBM)] * 2, [short] * HE...  1.61 us
    pallas_call x2, Pallas kernels, local(): call(functools.partial(norm_body, chain), [wide, whole(*turned_low.shape)...  1.4 us
  transfers between devices with their start and end apart: 37, of which 5 were waited for; matrix products, arithmetic and copies ran while one was open for 0% of the time, Pallas kernels for 11%

profile of v24, /device:TPU:0, one launch (start us, length us, event | category | flops | bytes accessed | tf_op | source)
XLA Modules:
  0.0 60.5 jit_solution(9863733150115285798)
XLA Ops:
  0.7 1.6 %delta.1 = (f32[128,128]{1,0:T(8,128)S(1)}, f32[128,128]{1,0:T(8,128)S(1)}, f32[128,128]{1,0:T(8,128)S(1)}, f32[128,128]{1,0:T(8,128)S(1)}, f32[128,128]{1,0:T(8...) custom-call(s32[1]{0:T(128)} %bitcast.place_ref, bf16[256,1024]{1,0:T(8,128)(2,1)} %bitcast.17, ...), custom_call_target="tpu_custom_call" | custom-call | flops 402653184 | bytes 2097152 | tf_op jit(solution)/shard_map/delta/pallas_call | solution.py:234
  2.3 4.0 %collective-permute-start = (f32[128,128]{1,0:T(8,128)S(1)}, f32[128,128]{1,0:T(8,128)S(1)}, u32[]{:S(2)}, u32[]{:S(2)}) collective-permute-start(f32[128,128]{1,0:T(8,128)S(1)} %get-tuple-element.88), channel_id=1, source_target_pairs={{0,6},{2,4},{4,2},{6,0},{8,14},{10,12},{12,10},{14,8},{16,22},{18,... | collective-permute-start | bytes 196616 | tf_op jit(solution)/shard_map/ppermute | solution.py:181
  6.9 2.8 %collective-permute-start.6 = (f32[128,128]{1,0:T(8,128)S(1)}, f32[128,128]{1,0:T(8,128)S(1)}, u32[]{:S(2)}, u32[]{:S(2)}) collective-permute-start(f32[128,128]{1,0:T(8,128)S(1)} %get-tuple-element.96), channel_id=1, source_target_pairs={{0,6},{2,4},{4,2},{6,0},{8,14},{10,12},{12,10},{14,8},{16,22},{18,... | collective-permute-start | bytes 196616 | tf_op jit(solution)/shard_map/ppermute | solution.py:181
  11.3 3.7 %collective-permute-start.3 = (f32[128,128]{1,0:T(8,128)S(1)}, f32[128,128]{1,0:T(8,128)S(1)}, u32[]{:S(2)}, u32[]{:S(2)}) collective-permute-start(f32[128,128]{1,0:T(8,128)S(1)} %add_add_fusion.7), channel_id=1, source_target_pairs={{0,24},{2,26},{4,28},{6,30},{8,16},{10,18},{12,20},{14,22},{16,8},... | collective-permute-start | bytes 196616 | tf_op jit(solution)/shard_map/ppermute | solution.py:181
  15.0 0.8 %collective-permute-start.5 = (f32[128,128]{1,0:T(8,128)S(1)}, f32[128,128]{1,0:T(8,128)S(1)}, u32[]{:S(2)}, u32[]{:S(2)}) collective-permute-start(f32[128,128]{1,0:T(8,128)S(1)} %add_add_fusion.7), channel_id=1, source_target_pairs={{0,8},{2,10},{4,12},{6,14},{8,0},{10,2},{12,4},{14,6},{16,24},{18,... | collective-permute-start | bytes 196616 | tf_op jit(solution)/shard_map/ppermute | solution.py:181
  15.8 3.7 %collective-permute-start.12 = (f32[128,128]{1,0:T(8,128)S(1)}, f32[128,128]{1,0:T(8,128)S(1)}, u32[]{:S(2)}, u32[]{:S(2)}) collective-permute-start(f32[128,128]{1,0:T(8,128)S(1)} %add_add_fusion.5), channel_id=1, source_target_pairs={{0,24},{2,26},{4,28},{6,30},{8,16},{10,18},{12,20},{14,22},{16,8},... | collective-permute-start | bytes 196616 | tf_op jit(solution)/shard_map/ppermute | solution.py:181
  19.5 0.9 %inner.1 = (f32[256,1024]{1,0:T(8,128)S(1)}, bf16[1024,256]{1,0:T(8,128)(2,1)S(1)}) custom-call(s32[1]{0:T(128)} %bitcast.place_ref, bf16[256,1024]{1,0:T(8,128)(2,1)S(1)} %bitcast.13, bf16[256,1024]{1,0:T(8,128)(2,1)S(1)} %bitcast.18, bf16[256,1024]{1,0:T(8,128)(2,1)S(1)} %bitcast.22), custom_call_target="tpu_custom_call" | custom-call | flops 1073741824 | bytes 2097152 | tf_op jit(solution)/shard_map/inner/pallas_call | solution.py:196
  20.5 0.8 %collective-permute-start.14 = (f32[128,128]{1,0:T(8,128)S(1)}, f32[128,128]{1,0:T(8,128)S(1)}, u32[]{:S(2)}, u32[]{:S(2)}) collective-permute-start(f32[128,128]{1,0:T(8,128)S(1)} %add_add_fusion.5), channel_id=1, source_target_pairs={{0,8},{2,10},{4,12},{6,14},{8,0},{10,2},{12,4},{14,6},{16,24},{18,... | collective-permute-start | bytes 196616 | tf_op jit(solution)/shard_map/ppermute | solution.py:181
  21.3 1.6 %collective-permute-done.4.refs_2_ = f32[128,128]{1,0:T(8,128)S(1)} collective-permute-done((f32[128,128]{1,0:T(8,128)S(1)}, f32[128,128]{1,0:T(8,128)S(1)}, u32[]{:S(2)}, u32[]{:S(2)}) %collective-permute-start.4) | collective-permute-done | bytes 65568 | tf_op jit(solution)/shard_map/ppermute | solution.py:181
  23.0 1.9 %collective-permute-start.9 = (f32[128,128]{1,0:T(8,128)S(1)}, f32[128,128]{1,0:T(8,128)S(1)}, u32[]{:S(2)}, u32[]{:S(2)}) collective-permute-start(f32[128,128]{1,0:T(8,128)S(1)} %get-tuple-element.115), channel_id=1, source_target_pairs={{0,6},{2,4},{4,2},{6,0},{8,14},{10,12},{12,10},{14,8},{16,22},{18,... | collective-permute-start | bytes 196616 | tf_op jit(solution)/shard_map/ppermute | solution.py:181
  24.9 1.1 %collective-permute-start.10 = (f32[128,128]{1,0:T(8,128)S(1)}, f32[128,128]{1,0:T(8,128)S(1)}, u32[]{:S(2)}, u32[]{:S(2)}) collective-permute-start(f32[128,128]{1,0:T(8,128)S(1)} %get-tuple-element.116), channel_id=1, source_target_pairs={{0,4},{2,6},{4,0},{6,2},{8,12},{10,14},{12,8},{14,10},{16,20},{18,... | collective-permute-start | bytes 196616 | tf_op jit(solution)/shard_map/ppermute | solution.py:181
  26.7 1.9 %collective-permute-start.15 = (f32[128,128]{1,0:T(8,128)S(1)}, f32[128,128]{1,0:T(8,128)S(1)}, u32[]{:S(2)}, u32[]{:S(2)}) collective-permute-start(f32[128,128]{1,0:T(8,128)S(1)} %get-tuple-element.127), channel_id=1, source_target_pairs={{0,6},{2,4},{4,2},{6,0},{8,14},{10,12},{12,10},{14,8},{16,22},{18,... | collective-permute-start | bytes 196616 | tf_op jit(solution)/shard_map/ppermute | solution.py:181
  28.5 1.1 %collective-permute-start.16 = (f32[128,128]{1,0:T(8,128)S(1)}, f32[128,128]{1,0:T(8,128)S(1)}, u32[]{:S(2)}, u32[]{:S(2)}) collective-permute-start(f32[128,128]{1,0:T(8,128)S(1)} %get-tuple-element.128), channel_id=1, source_target_pairs={{0,4},{2,6},{4,0},{6,2},{8,12},{10,14},{12,8},{14,10},{16,20},{18,... | collective-permute-start | bytes 196616 | tf_op jit(solution)/shard_map/ppermute | solution.py:181
  29.7 0.8 %collective-permute-start.17 = (f32[128,128]{1,0:T(8,128)S(1)}, f32[128,128]{1,0:T(8,128)S(1)}, u32[]{:S(2)}, u32[]{:S(2)}) collective-permute-start(f32[128,128]{1,0:T(8,128)S(1)} %get-tuple-element.129), channel_id=1, source_target_pairs={{0,2},{2,0},{4,6},{6,4},{8,10},{10,8},{12,14},{14,12},{16,18},{18,... | collective-permute-start | bytes 196616 | tf_op jit(solution)/shard_map/ppermute | solution.py:181
  30.5 0.7 %norm.2 = (bf16[256,512]{1,0:T(8,128)(2,1)S(1)}, f32[136,128]{1,0:T(8,128)S(1)}, f32[136,128]{1,0:T(8,128)S(1)}, f32[136,128]{1,0:T(8,128)S(1)}, f32[136,128]{1,0:T(8,128)S(1)}) custom-call(s32[1]{0:T(128)} %bitcast.place_ref, bf16[256,1024]{1,0:T(8,128)(2,1)S(1)} %bitcast.14, bf16[1024,256]{1,0:T(8,128)(2,1)S(1)} %get-tuple-element.109.turned_ref, ...), custom_call_target="tpu_custom_call" | custom-call | flops 536870912 | bytes 2097152 | tf_op jit(solution)/shard_map/norm/pallas_call | solution.py:258
  31.2 1.8 %collective-permute-start.18 = (f32[136,128]{1,0:T(8,128)S(1)}, f32[136,128]{1,0:T(8,128)S(1)}, u32[]{:S(2)}, u32[]{:S(2)}) collective-permute-start(f32[136,128]{1,0:T(8,128)S(1)} %get-tuple-element.132), channel_id=1, source_target_pairs={{0,6},{2,4},{4,2},{6,0},{8,14},{10,12},{12,10},{14,8},{16,22},{18,... | collective-permute-start | bytes 208904 | tf_op jit(solution)/shard_map/ppermute | solution.py:181
  32.9 1.1 %collective-permute-start.19 = (f32[136,128]{1,0:T(8,128)S(1)}, f32[136,128]{1,0:T(8,128)S(1)}, u32[]{:S(2)}, u32[]{:S(2)}) collective-permute-start(f32[136,128]{1,0:T(8,128)S(1)} %get-tuple-element.133), channel_id=1, source_target_pairs={{0,4},{2,6},{4,0},{6,2},{8,12},{10,14},{12,8},{14,10},{16,20},{18,... | collective-permute-start | bytes 208904 | tf_op jit(solution)/shard_map/ppermute | solution.py:181
  35.4 1.7 %collective-permute-start.27 = (f32[136,128]{1,0:T(8,128)S(1)}, f32[136,128]{1,0:T(8,128)S(1)}, u32[]{:S(2)}, u32[]{:S(2)}) collective-permute-start(f32[136,128]{1,0:T(8,128)S(1)} %get-tuple-element.149), channel_id=1, source_target_pairs={{0,6},{2,4},{4,2},{6,0},{8,14},{10,12},{12,10},{14,8},{16,22},{18,... | collective-permute-start | bytes 208904 | tf_op jit(solution)/shard_map/ppermute | solution.py:181
  37.2 1.1 %collective-permute-start.28 = (f32[136,128]{1,0:T(8,128)S(1)}, f32[136,128]{1,0:T(8,128)S(1)}, u32[]{:S(2)}, u32[]{:S(2)}) collective-permute-start(f32[136,128]{1,0:T(8,128)S(1)} %get-tuple-element.150), channel_id=1, source_target_pairs={{0,4},{2,6},{4,0},{6,2},{8,12},{10,14},{12,8},{14,10},{16,20},{18,... | collective-permute-start | bytes 208904 | tf_op jit(solution)/shard_map/ppermute | solution.py:181
  39.1 2.4 %collective-permute-start.22 = (f32[136,128]{1,0:T(8,128)S(1)}, f32[136,128]{1,0:T(8,128)S(1)}, u32[]{:S(2)}, u32[]{:S(2)}) collective-permute-start(f32[136,128]{1,0:T(8,128)S(1)} %add_add_fusion.3), channel_id=1, source_target_pairs={{0,24},{2,26},{4,28},{6,30},{8,16},{10,18},{12,20},{14,22},{16,8},... | collective-permute-start | bytes 208904 | tf_op jit(solution)/shard_map/ppermute | solution.py:181
  41.5 1.1 %collective-permute-start.23 = (f32[136,128]{1,0:T(8,128)S(1)}, f32[136,128]{1,0:T(8,128)S(1)}, u32[]{:S(2)}, u32[]{:S(2)}) collective-permute-start(f32[136,128]{1,0:T(8,128)S(1)} %add_add_fusion.3), channel_id=1, source_target_pairs={{0,16},{2,18},{4,20},{6,22},{8,24},{10,26},{12,28},{14,30},{16,0},... | collective-permute-start | bytes 208904 | tf_op jit(solution)/shard_map/ppermute | solution.py:181
  42.7 1.0 %collective-permute-start.30 = (f32[136,128]{1,0:T(8,128)S(1)}, f32[136,128]{1,0:T(8,128)S(1)}, u32[]{:S(2)}, u32[]{:S(2)}) collective-permute-start(f32[136,128]{1,0:T(8,128)S(1)} %add_add_fusion.1), channel_id=1, source_target_pairs={{0,8},{2,10},{4,12},{6,14},{8,0},{10,2},{12,4},{14,6},{16,24},{18,... | collective-permute-start | bytes 208904 | tf_op jit(solution)/shard_map/ppermute | solution.py:181
  43.7 2.3 %collective-permute-start.31 = (f32[136,128]{1,0:T(8,128)S(1)}, f32[136,128]{1,0:T(8,128)S(1)}, u32[]{:S(2)}, u32[]{:S(2)}) collective-permute-start(f32[136,128]{1,0:T(8,128)S(1)} %add_add_fusion.1), channel_id=1, source_target_pairs={{0,24},{2,26},{4,28},{6,30},{8,16},{10,18},{12,20},{14,22},{16,8},... | collective-permute-start | bytes 208904 | tf_op jit(solution)/shard_map/ppermute | solution.py:181
  46.2 1.5 %collective-permute-done.23.refs_3_ = f32[136,128]{1,0:T(8,128)S(1)} collective-permute-done((f32[136,128]{1,0:T(8,128)S(1)}, f32[136,128]{1,0:T(8,128)S(1)}, u32[]{:S(2)}, u32[]{:S(2)}) %collective-permute-start.23) | collective-permute-done | bytes 69664 | tf_op jit(solution)/shard_map/ppermute | solution.py:181
  47.9 1.7 %collective-permute-start.24 = (f32[136,128]{1,0:T(8,128)S(1)}, f32[136,128]{1,0:T(8,128)S(1)}, u32[]{:S(2)}, u32[]{:S(2)}) collective-permute-start(f32[136,128]{1,0:T(8,128)S(1)} %get-tuple-element.143), channel_id=1, source_target_pairs={{0,6},{2,4},{4,2},{6,0},{8,14},{10,12},{12,10},{14,8},{16,22},{18,... | collective-permute-start | bytes 208904 | tf_op jit(solution)/shard_map/ppermute | solution.py:181
  49.6 1.1 %collective-permute-start.25 = (f32[136,128]{1,0:T(8,128)S(1)}, f32[136,128]{1,0:T(8,128)S(1)}, u32[]{:S(2)}, u32[]{:S(2)}) collective-permute-start(f32[136,128]{1,0:T(8,128)S(1)} %get-tuple-element.144), channel_id=1, source_target_pairs={{0,4},{2,6},{4,0},{6,2},{8,12},{10,14},{12,8},{14,10},{16,20},{18,... | collective-permute-start | bytes 208904 | tf_op jit(solution)/shard_map/ppermute | solution.py:181
  50.7 0.7 %collective-permute-start.26 = (f32[136,128]{1,0:T(8,128)S(1)}, f32[136,128]{1,0:T(8,128)S(1)}, u32[]{:S(2)}, u32[]{:S(2)}) collective-permute-start(f32[136,128]{1,0:T(8,128)S(1)} %get-tuple-element.145), channel_id=1, source_target_pairs={{0,2},{2,0},{4,6},{6,4},{8,10},{10,8},{12,14},{14,12},{16,18},{18,... | collective-permute-start | bytes 208904 | tf_op jit(solution)/shard_map/ppermute | solution.py:181
  51.6 1.7 %collective-permute-start.33 = (f32[136,128]{1,0:T(8,128)S(1)}, f32[136,128]{1,0:T(8,128)S(1)}, u32[]{:S(2)}, u32[]{:S(2)}) collective-permute-start(f32[136,128]{1,0:T(8,128)S(1)} %get-tuple-element.160), channel_id=1, source_target_pairs={{0,6},{2,4},{4,2},{6,0},{8,14},{10,12},{12,10},{14,8},{16,22},{18,... | collective-permute-start | bytes 208904 | tf_op jit(solution)/shard_map/ppermute | solution.py:181
  53.3 1.1 %collective-permute-start.34 = (f32[136,128]{1,0:T(8,128)S(1)}, f32[136,128]{1,0:T(8,128)S(1)}, u32[]{:S(2)}, u32[]{:S(2)}) collective-permute-start(f32[136,128]{1,0:T(8,128)S(1)} %get-tuple-element.161), channel_id=1, source_target_pairs={{0,4},{2,6},{4,0},{6,2},{8,12},{10,14},{12,8},{14,10},{16,20},{18,... | collective-permute-start | bytes 208904 | tf_op jit(solution)/shard_map/ppermute | solution.py:181
  54.4 0.7 %collective-permute-start.35 = (f32[136,128]{1,0:T(8,128)S(1)}, f32[136,128]{1,0:T(8,128)S(1)}, u32[]{:S(2)}, u32[]{:S(2)}) collective-permute-start(f32[136,128]{1,0:T(8,128)S(1)} %get-tuple-element.162), channel_id=1, source_target_pairs={{0,2},{2,0},{4,6},{6,4},{8,10},{10,8},{12,14},{14,12},{16,18},{18,... | collective-permute-start | bytes 208904 | tf_op jit(solution)/shard_map/ppermute | solution.py:181
  55.1 3.2 %partial.1 = (bf16[256,1024]{1,0:T(8,128)(2,1)}, bf16[256,1024]{1,0:T(8,128)(2,1)}, bf16[256,1024]{1,0:T(8,128)(2,1)}, f32[256,512]{1,0:T(8,128)S(1)}, f32[256,512]{1,0:T(8,128)S(1)}) custom-call(s32[1]{0:T(128)} %bitcast.place_ref, bf16[256,1024]{1,0:T(8,128)(2,1)S(1)} %bitcast.16, bf16[256,1024]{1,0:T(8,128)(2,1)S(1)} %bitcast.19, ...), custom_call_target="tpu_custom_call" | custom-call | flops 3221225472 | bytes 2097152 | tf_op jit(solution)/shard_map/partial/pallas_call | solution.py:270
  58.7 1.1 %final.1 = (bf16[256,1024]{1,0:T(8,128)(2,1)}, bf16[256,1024]{1,0:T(8,128)(2,1)}) custom-call(s32[1]{0:T(128)} %bitcast.place_ref, bf16[256,1024]{1,0:T(8,128)(2,1)S(1)} %bitcast.20, bf16[256,1024]{1,0:T(8,128)(2,1)S(1)} %bitcast.24, f32[256,512]{1,0:T(8,128)S(1)} %get-tuple-element.147.key_part_ref, ...), custom_call_target="tpu_custom_call", output_to_operand_aliasing={{0}: (9, {}), {1}: (10, {})} | custom-call | flops 536870912 | bytes 2097152 | tf_op jit(solution)/shard_map/final/pallas_call | solution.py:286
  (72 shorter events, 6.9 us)
Async XLA Ops:
  2.3 8.0 %collective-permute-start = (f32[128,128]{1,0:T(8,128)S(1)}, f32[128,128]{1,0:T(8,128)S(1)}, u32[]{:S(2)}, u32[]{:S(2)}) collective-permute-start(f32[128,128]{1,0:T(8,128)S(1)} %get-tuple-element.88), channel_id=1, source_target_pairs={{0,6},{2,4},{4,2},{6,0},{8,14},{10,12},{12,10},{14,8},{16,22},{18,... | collective-permute-start | bytes 196616 | tf_op jit(solution)/shard_map/ppermute | solution.py:181
  6.2 5.1 %collective-permute-start.1 = (f32[128,128]{1,0:T(8,128)S(1)}, f32[128,128]{1,0:T(8,128)S(1)}, u32[]{:S(2)}, u32[]{:S(2)}) collective-permute-start(f32[128,128]{1,0:T(8,128)S(1)} %get-tuple-element.89), channel_id=1, source_target_pairs={{0,4},{2,6},{4,0},{6,2},{8,12},{10,14},{12,8},{14,10},{16,20},{18,... | collective-permute-start | bytes 196616 | tf_op jit(solution)/shard_map/ppermute | solution.py:181
  6.8 4.6 %collective-permute-start.2 = (f32[128,128]{1,0:T(8,128)S(1)}, f32[128,128]{1,0:T(8,128)S(1)}, u32[]{:S(2)}, u32[]{:S(2)}) collective-permute-start(f32[128,128]{1,0:T(8,128)S(1)} %get-tuple-element.90), channel_id=1, source_target_pairs={{0,2},{2,0},{4,6},{6,4},{8,10},{10,8},{12,14},{14,12},{16,18},{18,... | collective-permute-start | bytes 196616 | tf_op jit(solution)/shard_map/ppermute | solution.py:181
  6.9 8.1 %collective-permute-start.6 = (f32[128,128]{1,0:T(8,128)S(1)}, f32[128,128]{1,0:T(8,128)S(1)}, u32[]{:S(2)}, u32[]{:S(2)}) collective-permute-start(f32[128,128]{1,0:T(8,128)S(1)} %get-tuple-element.96), channel_id=1, source_target_pairs={{0,6},{2,4},{4,2},{6,0},{8,14},{10,12},{12,10},{14,8},{16,22},{18,... | collective-permute-start | bytes 196616 | tf_op jit(solution)/shard_map/ppermute | solution.py:181
  9.7 6.1 %collective-permute-start.7 = (f32[128,128]{1,0:T(8,128)S(1)}, f32[128,128]{1,0:T(8,128)S(1)}, u32[]{:S(2)}, u32[]{:S(2)}) collective-permute-start(f32[128,128]{1,0:T(8,128)S(1)} %get-tuple-element.97), channel_id=1, source_target_pairs={{0,4},{2,6},{4,0},{6,2},{8,12},{10,14},{12,8},{14,10},{16,20},{18,... | collective-permute-start | bytes 196616 | tf_op jit(solution)/shard_map/ppermute | solution.py:181
  10.2 5.6 %collective-permute-start.8 = (f32[128,128]{1,0:T(8,128)S(1)}, f32[128,128]{1,0:T(8,128)S(1)}, u32[]{:S(2)}, u32[]{:S(2)}) collective-permute-start(f32[128,128]{1,0:T(8,128)S(1)} %get-tuple-element.98), channel_id=1, source_target_pairs={{0,2},{2,0},{4,6},{6,4},{8,10},{10,8},{12,14},{14,12},{16,18},{18,... | collective-permute-start | bytes 196616 | tf_op jit(solution)/shard_map/ppermute | solution.py:181
  11.3 9.1 %collective-permute-start.3 = (f32[128,128]{1,0:T(8,128)S(1)}, f32[128,128]{1,0:T(8,128)S(1)}, u32[]{:S(2)}, u32[]{:S(2)}) collective-permute-start(f32[128,128]{1,0:T(8,128)S(1)} %add_add_fusion.7), channel_id=1, source_target_pairs={{0,24},{2,26},{4,28},{6,30},{8,16},{10,18},{12,20},{14,22},{16,8},... | collective-permute-start | bytes 196616 | tf_op jit(solution)/shard_map/ppermute | solution.py:181
  15.0 7.9 %collective-permute-start.4 = (f32[128,128]{1,0:T(8,128)S(1)}, f32[128,128]{1,0:T(8,128)S(1)}, u32[]{:S(2)}, u32[]{:S(2)}) collective-permute-start(f32[128,128]{1,0:T(8,128)S(1)} %add_add_fusion.7), channel_id=1, source_target_pairs={{0,16},{2,18},{4,20},{6,22},{8,24},{10,26},{12,28},{14,30},{16,0},... | collective-permute-start | bytes 196616 | tf_op jit(solution)/shard_map/ppermute | solution.py:181
  15.0 7.9 %collective-permute-start.5 = (f32[128,128]{1,0:T(8,128)S(1)}, f32[128,128]{1,0:T(8,128)S(1)}, u32[]{:S(2)}, u32[]{:S(2)}) collective-permute-start(f32[128,128]{1,0:T(8,128)S(1)} %add_add_fusion.7), channel_id=1, source_target_pairs={{0,8},{2,10},{4,12},{6,14},{8,0},{10,2},{12,4},{14,6},{16,24},{18,... | collective-permute-start | bytes 196616 | tf_op jit(solution)/shard_map/ppermute | solution.py:181
  15.8 10.2 %collective-permute-start.12 = (f32[128,128]{1,0:T(8,128)S(1)}, f32[128,128]{1,0:T(8,128)S(1)}, u32[]{:S(2)}, u32[]{:S(2)}) collective-permute-start(f32[128,128]{1,0:T(8,128)S(1)} %add_add_fusion.5), channel_id=1, source_target_pairs={{0,24},{2,26},{4,28},{6,30},{8,16},{10,18},{12,20},{14,22},{16,8},... | collective-permute-start | bytes 196616 | tf_op jit(solution)/shard_map/ppermute | solution.py:181
  19.5 7.1 %collective-permute-start.13 = (f32[128,128]{1,0:T(8,128)S(1)}, f32[128,128]{1,0:T(8,128)S(1)}, u32[]{:S(2)}, u32[]{:S(2)}) collective-permute-start(f32[128,128]{1,0:T(8,128)S(1)} %add_add_fusion.5), channel_id=1, source_target_pairs={{0,16},{2,18},{4,20},{6,22},{8,24},{10,26},{12,28},{14,30},{16,0},... | collective-permute-start | bytes 196616 | tf_op jit(solution)/shard_map/ppermute | solution.py:181
  20.5 6.1 %collective-permute-start.14 = (f32[128,128]{1,0:T(8,128)S(1)}, f32[128,128]{1,0:T(8,128)S(1)}, u32[]{:S(2)}, u32[]{:S(2)}) collective-permute-start(f32[128,128]{1,0:T(8,128)S(1)} %add_add_fusion.5), channel_id=1, source_target_pairs={{0,8},{2,10},{4,12},{6,14},{8,0},{10,2},{12,4},{14,6},{16,24},{18,... | collective-permute-start | bytes 196616 | tf_op jit(solution)/shard_map/ppermute | solution.py:181
  23.0 6.6 %collective-permute-start.9 = (f32[128,128]{1,0:T(8,128)S(1)}, f32[128,128]{1,0:T(8,128)S(1)}, u32[]{:S(2)}, u32[]{:S(2)}) collective-permute-start(f32[128,128]{1,0:T(8,128)S(1)} %get-tuple-element.115), channel_id=1, source_target_pairs={{0,6},{2,4},{4,2},{6,0},{8,14},{10,12},{12,10},{14,8},{16,22},{18,... | collective-permute-start | bytes 196616 | tf_op jit(solution)/shard_map/ppermute | solution.py:181
  24.9 5.5 %collective-permute-start.10 = (f32[128,128]{1,0:T(8,128)S(1)}, f32[128,128]{1,0:T(8,128)S(1)}, u32[]{:S(2)}, u32[]{:S(2)}) collective-permute-start(f32[128,128]{1,0:T(8,128)S(1)} %get-tuple-element.116), channel_id=1, source_target_pairs={{0,4},{2,6},{4,0},{6,2},{8,12},{10,14},{12,8},{14,10},{16,20},{18,... | collective-permute-start | bytes 196616 | tf_op jit(solution)/shard_map/ppermute | solution.py:181
  26.7 7.4 %collective-permute-start.15 = (f32[128,128]{1,0:T(8,128)S(1)}, f32[128,128]{1,0:T(8,128)S(1)}, u32[]{:S(2)}, u32[]{:S(2)}) collective-permute-start(f32[128,128]{1,0:T(8,128)S(1)} %get-tuple-element.127), channel_id=1, source_target_pairs={{0,6},{2,4},{4,2},{6,0},{8,14},{10,12},{12,10},{14,8},{16,22},{18,... | collective-permute-start | bytes 196616 | tf_op jit(solution)/shard_map/ppermute | solution.py:181
  28.5 6.2 %collective-permute-start.16 = (f32[128,128]{1,0:T(8,128)S(1)}, f32[128,128]{1,0:T(8,128)S(1)}, u32[]{:S(2)}, u32[]{:S(2)}) collective-permute-start(f32[128,128]{1,0:T(8,128)S(1)} %get-tuple-element.128), channel_id=1, source_target_pairs={{0,4},{2,6},{4,0},{6,2},{8,12},{10,14},{12,8},{14,10},{16,20},{18,... | collective-permute-start | bytes 196616 | tf_op jit(solution)/shard_map/ppermute | solution.py:181
  29.7 5.1 %collective-permute-start.17 = (f32[128,128]{1,0:T(8,128)S(1)}, f32[128,128]{1,0:T(8,128)S(1)}, u32[]{:S(2)}, u32[]{:S(2)}) collective-permute-start(f32[128,128]{1,0:T(8,128)S(1)} %get-tuple-element.129), channel_id=1, source_target_pairs={{0,2},{2,0},{4,6},{6,4},{8,10},{10,8},{12,14},{14,12},{16,18},{18,... | collective-permute-start | bytes 196616 | tf_op jit(solution)/shard_map/ppermute | solution.py:181
  31.2 7.2 %collective-permute-start.18 = (f32[136,128]{1,0:T(8,128)S(1)}, f32[136,128]{1,0:T(8,128)S(1)}, u32[]{:S(2)}, u32[]{:S(2)}) collective-permute-start(f32[136,128]{1,0:T(8,128)S(1)} %get-tuple-element.132), channel_id=1, source_target_pairs={{0,6},{2,4},{4,2},{6,0},{8,14},{10,12},{12,10},{14,8},{16,22},{18,... | collective-permute-start | bytes 208904 | tf_op jit(solution)/shard_map/ppermute | solution.py:181
  32.9 6.1 %collective-permute-start.19 = (f32[136,128]{1,0:T(8,128)S(1)}, f32[136,128]{1,0:T(8,128)S(1)}, u32[]{:S(2)}, u32[]{:S(2)}) collective-permute-start(f32[136,128]{1,0:T(8,128)S(1)} %get-tuple-element.133), channel_id=1, source_target_pairs={{0,4},{2,6},{4,0},{6,2},{8,12},{10,14},{12,8},{14,10},{16,20},{18,... | collective-permute-start | bytes 208904 | tf_op jit(solution)/shard_map/ppermute | solution.py:181
  34.0 5.0 %collective-permute-start.20 = (f32[136,128]{1,0:T(8,128)S(1)}, f32[136,128]{1,0:T(8,128)S(1)}, u32[]{:S(2)}, u32[]{:S(2)}) collective-permute-start(f32[136,128]{1,0:T(8,128)S(1)} %get-tuple-element.134), channel_id=1, source_target_pairs={{0,2},{2,0},{4,6},{6,4},{8,10},{10,8},{12,14},{14,12},{16,18},{18,... | collective-permute-start | bytes 208904 | tf_op jit(solution)/shard_map/ppermute | solution.py:181
  35.4 6.1 %collective-permute-start.27 = (f32[136,128]{1,0:T(8,128)S(1)}, f32[136,128]{1,0:T(8,128)S(1)}, u32[]{:S(2)}, u32[]{:S(2)}) collective-permute-start(f32[136,128]{1,0:T(8,128)S(1)} %get-tuple-element.149), channel_id=1, source_target_pairs={{0,6},{2,4},{4,2},{6,0},{8,14},{10,12},{12,10},{14,8},{16,22},{18,... | collective-permute-start | bytes 208904 | tf_op jit(solution)/shard_map/ppermute | solution.py:181
  37.2 5.4 %collective-permute-start.28 = (f32[136,128]{1,0:T(8,128)S(1)}, f32[136,128]{1,0:T(8,128)S(1)}, u32[]{:S(2)}, u32[]{:S(2)}) collective-permute-start(f32[136,128]{1,0:T(8,128)S(1)} %get-tuple-element.150), channel_id=1, source_target_pairs={{0,4},{2,6},{4,0},{6,2},{8,12},{10,14},{12,8},{14,10},{16,20},{18,... | collective-permute-start | bytes 208904 | tf_op jit(solution)/shard_map/ppermute | solution.py:181
  39.0 7.0 %collective-permute-start.21 = (f32[136,128]{1,0:T(8,128)S(1)}, f32[136,128]{1,0:T(8,128)S(1)}, u32[]{:S(2)}, u32[]{:S(2)}) collective-permute-start(f32[136,128]{1,0:T(8,128)S(1)} %add_add_fusion.3), channel_id=1, source_target_pairs={{0,8},{2,10},{4,12},{6,14},{8,0},{10,2},{12,4},{14,6},{16,24},{18,... | collective-permute-start | bytes 208904 | tf_op jit(solution)/shard_map/ppermute | solution.py:181
  39.1 7.1 %collective-permute-start.22 = (f32[136,128]{1,0:T(8,128)S(1)}, f32[136,128]{1,0:T(8,128)S(1)}, u32[]{:S(2)}, u32[]{:S(2)}) collective-permute-start(f32[136,128]{1,0:T(8,128)S(1)} %add_add_fusion.3), channel_id=1, source_target_pairs={{0,24},{2,26},{4,28},{6,30},{8,16},{10,18},{12,20},{14,22},{16,8},... | collective-permute-start | bytes 208904 | tf_op jit(solution)/shard_map/ppermute | solution.py:181
  41.5 6.2 %collective-permute-start.23 = (f32[136,128]{1,0:T(8,128)S(1)}, f32[136,128]{1,0:T(8,128)S(1)}, u32[]{:S(2)}, u32[]{:S(2)}) collective-permute-start(f32[136,128]{1,0:T(8,128)S(1)} %add_add_fusion.3), channel_id=1, source_target_pairs={{0,16},{2,18},{4,20},{6,22},{8,24},{10,26},{12,28},{14,30},{16,0},... | collective-permute-start | bytes 208904 | tf_op jit(solution)/shard_map/ppermute | solution.py:181
  42.7 8.1 %collective-permute-start.30 = (f32[136,128]{1,0:T(8,128)S(1)}, f32[136,128]{1,0:T(8,128)S(1)}, u32[]{:S(2)}, u32[]{:S(2)}) collective-permute-start(f32[136,128]{1,0:T(8,128)S(1)} %add_add_fusion.1), channel_id=1, source_target_pairs={{0,8},{2,10},{4,12},{6,14},{8,0},{10,2},{12,4},{14,6},{16,24},{18,... | collective-permute-start | bytes 208904 | tf_op jit(solution)/shard_map/ppermute | solution.py:181
  43.7 7.8 %collective-permute-start.31 = (f32[136,128]{1,0:T(8,128)S(1)}, f32[136,128]{1,0:T(8,128)S(1)}, u32[]{:S(2)}, u32[]{:S(2)}) collective-permute-start(f32[136,128]{1,0:T(8,128)S(1)} %add_add_fusion.1), channel_id=1, source_target_pairs={{0,24},{2,26},{4,28},{6,30},{8,16},{10,18},{12,20},{14,22},{16,8},... | collective-permute-start | bytes 208904 | tf_op jit(solution)/shard_map/ppermute | solution.py:181
  46.0 5.4 %collective-permute-start.32 = (f32[136,128]{1,0:T(8,128)S(1)}, f32[136,128]{1,0:T(8,128)S(1)}, u32[]{:S(2)}, u32[]{:S(2)}) collective-permute-start(f32[136,128]{1,0:T(8,128)S(1)} %add_add_fusion.1), channel_id=1, source_target_pairs={{0,16},{2,18},{4,20},{6,22},{8,24},{10,26},{12,28},{14,30},{16,0},... | collective-permute-start | bytes 208904 | tf_op jit(solution)/shard_map/ppermute | solution.py:181
  47.9 6.5 %collective-permute-start.24 = (f32[136,128]{1,0:T(8,128)S(1)}, f32[136,128]{1,0:T(8,128)S(1)}, u32[]{:S(2)}, u32[]{:S(2)}) collective-permute-start(f32[136,128]{1,0:T(8,128)S(1)} %get-tuple-element.143), channel_id=1, source_target_pairs={{0,6},{2,4},{4,2},{6,0},{8,14},{10,12},{12,10},{14,8},{16,22},{18,... | collective-permute-start | bytes 208904 | tf_op jit(solution)/shard_map/ppermute | solution.py:181
  49.6 5.5 %collective-permute-start.25 = (f32[136,128]{1,0:T(8,128)S(1)}, f32[136,128]{1,0:T(8,128)S(1)}, u32[]{:S(2)}, u32[]{:S(2)}) collective-permute-start(f32[136,128]{1,0:T(8,128)S(1)} %get-tuple-element.144), channel_id=1, source_target_pairs={{0,4},{2,6},{4,0},{6,2},{8,12},{10,14},{12,8},{14,10},{16,20},{18,... | collective-permute-start | bytes 208904 | tf_op jit(solution)/shard_map/ppermute | solution.py:181
  51.6 6.7 %collective-permute-start.33 = (f32[136,128]{1,0:T(8,128)S(1)}, f32[136,128]{1,0:T(8,128)S(1)}, u32[]{:S(2)}, u32[]{:S(2)}) collective-permute-start(f32[136,128]{1,0:T(8,128)S(1)} %get-tuple-element.160), channel_id=1, source_target_pairs={{0,6},{2,4},{4,2},{6,0},{8,14},{10,12},{12,10},{14,8},{16,22},{18,... | collective-permute-start | bytes 208904 | tf_op jit(solution)/shard_map/ppermute | solution.py:181
  53.3 5.0 %collective-permute-start.34 = (f32[136,128]{1,0:T(8,128)S(1)}, f32[136,128]{1,0:T(8,128)S(1)}, u32[]{:S(2)}, u32[]{:S(2)}) collective-permute-start(f32[136,128]{1,0:T(8,128)S(1)} %get-tuple-element.161), channel_id=1, source_target_pairs={{0,4},{2,6},{4,0},{6,2},{8,12},{10,14},{12,8},{14,10},{16,20},{18,... | collective-permute-start | bytes 208904 | tf_op jit(solution)/shard_map/ppermute | solution.py:181
  (10 other events, 83.0 us)

commit v25 on v24

--- a/solution.py
+++ b/solution.py
@@ -168,7 +168,7 @@
 def exchange_steps(near_first):
     count, base, steps = lax.axis_size("seq"), GROUP, []
     while base < count:
-        masks = [base, 3 * base, 2 * base] if near_first else [3 * base, 2 * base, base]
+        masks = [base, 3 * base, 2 * base] if near_first else [2 * base, 3 * base, base]
         masks = masks if 4 * base <= count else [base]
         steps.append(masks)
         base *= len(masks) + 1

time: 60.6 us -> 61.7 us (1.018)
  starting transfers between devices: 46.2 us -> 47.5 us
    ppermute x36, starting transfers between devices: 46.1 us -> 47.5 us  [swap(): lax.ppermute(array, 'seq', [(s, s ^ mask) for s in range(lax.axis_size('s...]
  transfers between devices with their start and end apart: 37 -> 37, of which waited for: 5 -> 7; matrix products, arithmetic and copies ran while one was open for 0% -> 0% of each run, Pallas kernels for 11% -> 11%
where the time goes in v25:
time: 61.7 us; the launch traced here: 61.6 us
  starting transfers between devices  47.5 us (77%)
  Pallas kernels  8.55 us (14%)
  waiting for transfers between devices  3.98 us (6%)
  between operations  0.83 us (1%)
  other arithmetic  0.75 us (1%)
    ppermute x36, starting transfers between devices, swap(): lax.ppermute(array, 'seq', [(s, s ^ mask) for s in range(lax.axis_size('s...  47.5 us
    ppermute x36, waiting for transfers between devices, swap(): lax.ppermute(array, 'seq', [(s, s ^ mask) for s in range(lax.axis_size('s...  3.92 us
    pallas_call x1, Pallas kernels, local(): call(partial_body, [wide] * 3 + [whole(*turned_low.shape)] + [half] * CHA...  3.15 us
    pallas_call x1, Pallas kernels, local(): call(delta_body, [pl.BlockSpec(memory_space=pltpu.HBM)] * 2, [short] * HE...  1.61 us
    pallas_call x2, Pallas kernels, local(): call(functools.partial(norm_body, chain), [wide, whole(*turned_low.shape)...  1.41 us
  transfers between devices with their start and end apart: 37, of which 7 were waited for; matrix products, arithmetic and copies ran while one was open for 0% of the time, Pallas kernels for 11%

profile of v25, /device:TPU:0, one launch (start us, length us, event | category | flops | bytes accessed | tf_op | source)
XLA Modules:
  0.0 61.6 jit_solution(10308015863720884881)
XLA Ops:
  0.7 1.6 %delta.1 = (f32[128,128]{1,0:T(8,128)S(1)}, f32[128,128]{1,0:T(8,128)S(1)}, f32[128,128]{1,0:T(8,128)S(1)}, f32[128,128]{1,0:T(8,128)S(1)}, f32[128,128]{1,0:T(8...) custom-call(s32[1]{0:T(128)} %bitcast.place_ref, bf16[256,1024]{1,0:T(8,128)(2,1)} %bitcast.17, ...), custom_call_target="tpu_custom_call" | custom-call | flops 402653184 | bytes 2097152 | tf_op jit(solution)/shard_map/delta/pallas_call | solution.py:234
  2.3 4.0 %collective-permute-start = (f32[128,128]{1,0:T(8,128)S(1)}, f32[128,128]{1,0:T(8,128)S(1)}, u32[]{:S(2)}, u32[]{:S(2)}) collective-permute-start(f32[128,128]{1,0:T(8,128)S(1)} %get-tuple-element.88), channel_id=1, source_target_pairs={{0,6},{2,4},{4,2},{6,0},{8,14},{10,12},{12,10},{14,8},{16,22},{18,... | collective-permute-start | bytes 196616 | tf_op jit(solution)/shard_map/ppermute | solution.py:181
  6.9 2.8 %collective-permute-start.6 = (f32[128,128]{1,0:T(8,128)S(1)}, f32[128,128]{1,0:T(8,128)S(1)}, u32[]{:S(2)}, u32[]{:S(2)}) collective-permute-start(f32[128,128]{1,0:T(8,128)S(1)} %get-tuple-element.96), channel_id=1, source_target_pairs={{0,6},{2,4},{4,2},{6,0},{8,14},{10,12},{12,10},{14,8},{16,22},{18,... | collective-permute-start | bytes 196616 | tf_op jit(solution)/shard_map/ppermute | solution.py:181
  11.3 2.7 %collective-permute-start.3 = (f32[128,128]{1,0:T(8,128)S(1)}, f32[128,128]{1,0:T(8,128)S(1)}, u32[]{:S(2)}, u32[]{:S(2)}) collective-permute-start(f32[128,128]{1,0:T(8,128)S(1)} %add_add_fusion.7), channel_id=1, source_target_pairs={{0,16},{2,18},{4,20},{6,22},{8,24},{10,26},{12,28},{14,30},{16,0},... | collective-permute-start | bytes 196616 | tf_op jit(solution)/shard_map/ppermute | solution.py:181
  14.0 1.3 %collective-permute-start.4 = (f32[128,128]{1,0:T(8,128)S(1)}, f32[128,128]{1,0:T(8,128)S(1)}, u32[]{:S(2)}, u32[]{:S(2)}) collective-permute-start(f32[128,128]{1,0:T(8,128)S(1)} %add_add_fusion.7), channel_id=1, source_target_pairs={{0,24},{2,26},{4,28},{6,30},{8,16},{10,18},{12,20},{14,22},{16,8},... | collective-permute-start | bytes 196616 | tf_op jit(solution)/shard_map/ppermute | solution.py:181
  15.6 2.9 %collective-permute-start.12 = (f32[128,128]{1,0:T(8,128)S(1)}, f32[128,128]{1,0:T(8,128)S(1)}, u32[]{:S(2)}, u32[]{:S(2)}) collective-permute-start(f32[128,128]{1,0:T(8,128)S(1)} %add_add_fusion.5), channel_id=1, source_target_pairs={{0,16},{2,18},{4,20},{6,22},{8,24},{10,26},{12,28},{14,30},{16,0},... | collective-permute-start | bytes 196616 | tf_op jit(solution)/shard_map/ppermute | solution.py:181
  18.5 1.3 %collective-permute-start.13 = (f32[128,128]{1,0:T(8,128)S(1)}, f32[128,128]{1,0:T(8,128)S(1)}, u32[]{:S(2)}, u32[]{:S(2)}) collective-permute-start(f32[128,128]{1,0:T(8,128)S(1)} %add_add_fusion.5), channel_id=1, source_target_pairs={{0,24},{2,26},{4,28},{6,30},{8,16},{10,18},{12,20},{14,22},{16,8},... | collective-permute-start | bytes 196616 | tf_op jit(solution)/shard_map/ppermute | solution.py:181
  19.8 0.9 %inner.1 = (f32[256,1024]{1,0:T(8,128)S(1)}, bf16[1024,256]{1,0:T(8,128)(2,1)S(1)}) custom-call(s32[1]{0:T(128)} %bitcast.place_ref, bf16[256,1024]{1,0:T(8,128)(2,1)S(1)} %bitcast.13, bf16[256,1024]{1,0:T(8,128)(2,1)S(1)} %bitcast.18, bf16[256,1024]{1,0:T(8,128)(2,1)S(1)} %bitcast.22), custom_call_target="tpu_custom_call" | custom-call | flops 1073741824 | bytes 2097152 | tf_op jit(solution)/shard_map/inner/pallas_call | solution.py:196
  20.9 1.1 %collective-permute-done.5.refs_3_ = f32[128,128]{1,0:T(8,128)S(1)} collective-permute-done((f32[128,128]{1,0:T(8,128)S(1)}, f32[128,128]{1,0:T(8,128)S(1)}, u32[]{:S(2)}, u32[]{:S(2)}) %collective-permute-start.5) | collective-permute-done | bytes 65568 | tf_op jit(solution)/shard_map/ppermute | solution.py:181
  22.1 2.1 %collective-permute-start.9 = (f32[128,128]{1,0:T(8,128)S(1)}, f32[128,128]{1,0:T(8,128)S(1)}, u32[]{:S(2)}, u32[]{:S(2)}) collective-permute-start(f32[128,128]{1,0:T(8,128)S(1)} %get-tuple-element.115), channel_id=1, source_target_pairs={{0,6},{2,4},{4,2},{6,0},{8,14},{10,12},{12,10},{14,8},{16,22},{18,... | collective-permute-start | bytes 196616 | tf_op jit(solution)/shard_map/ppermute | solution.py:181
  24.7 1.2 %collective-permute-start.11 = (f32[128,128]{1,0:T(8,128)S(1)}, f32[128,128]{1,0:T(8,128)S(1)}, u32[]{:S(2)}, u32[]{:S(2)}) collective-permute-start(f32[128,128]{1,0:T(8,128)S(1)} %get-tuple-element.117), channel_id=1, source_target_pairs={{0,2},{2,0},{4,6},{6,4},{8,10},{10,8},{12,14},{14,12},{16,18},{18,... | collective-permute-start | bytes 196616 | tf_op jit(solution)/shard_map/ppermute | solution.py:181
  26.0 1.8 %collective-permute-start.15 = (f32[128,128]{1,0:T(8,128)S(1)}, f32[128,128]{1,0:T(8,128)S(1)}, u32[]{:S(2)}, u32[]{:S(2)}) collective-permute-start(f32[128,128]{1,0:T(8,128)S(1)} %get-tuple-element.127), channel_id=1, source_target_pairs={{0,6},{2,4},{4,2},{6,0},{8,14},{10,12},{12,10},{14,8},{16,22},{18,... | collective-permute-start | bytes 196616 | tf_op jit(solution)/shard_map/ppermute | solution.py:181
  28.4 1.1 %collective-permute-start.17 = (f32[128,128]{1,0:T(8,128)S(1)}, f32[128,128]{1,0:T(8,128)S(1)}, u32[]{:S(2)}, u32[]{:S(2)}) collective-permute-start(f32[128,128]{1,0:T(8,128)S(1)} %get-tuple-element.129), channel_id=1, source_target_pairs={{0,2},{2,0},{4,6},{6,4},{8,10},{10,8},{12,14},{14,12},{16,18},{18,... | collective-permute-start | bytes 196616 | tf_op jit(solution)/shard_map/ppermute | solution.py:181
  29.6 0.7 %norm.2 = (bf16[256,512]{1,0:T(8,128)(2,1)S(1)}, f32[136,128]{1,0:T(8,128)S(1)}, f32[136,128]{1,0:T(8,128)S(1)}, f32[136,128]{1,0:T(8,128)S(1)}, f32[136,128]{1,0:T(8,128)S(1)}) custom-call(s32[1]{0:T(128)} %bitcast.place_ref, bf16[256,1024]{1,0:T(8,128)(2,1)S(1)} %bitcast.14, bf16[1024,256]{1,0:T(8,128)(2,1)S(1)} %get-tuple-element.109.turned_ref, ...), custom_call_target="tpu_custom_call" | custom-call | flops 536870912 | bytes 2097152 | tf_op jit(solution)/shard_map/norm/pallas_call | solution.py:258
  30.3 1.8 %collective-permute-start.18 = (f32[136,128]{1,0:T(8,128)S(1)}, f32[136,128]{1,0:T(8,128)S(1)}, u32[]{:S(2)}, u32[]{:S(2)}) collective-permute-start(f32[136,128]{1,0:T(8,128)S(1)} %get-tuple-element.132), channel_id=1, source_target_pairs={{0,6},{2,4},{4,2},{6,0},{8,14},{10,12},{12,10},{14,8},{16,22},{18,... | collective-permute-start | bytes 208904 | tf_op jit(solution)/shard_map/ppermute | solution.py:181
  32.7 1.1 %collective-permute-start.20 = (f32[136,128]{1,0:T(8,128)S(1)}, f32[136,128]{1,0:T(8,128)S(1)}, u32[]{:S(2)}, u32[]{:S(2)}) collective-permute-start(f32[136,128]{1,0:T(8,128)S(1)} %get-tuple-element.134), channel_id=1, source_target_pairs={{0,2},{2,0},{4,6},{6,4},{8,10},{10,8},{12,14},{14,12},{16,18},{18,... | collective-permute-start | bytes 208904 | tf_op jit(solution)/shard_map/ppermute | solution.py:181
  33.9 0.7 %norm.3 = (bf16[256,512]{1,0:T(8,128)(2,1)S(1)}, f32[136,128]{1,0:T(8,128)S(1)}, f32[136,128]{1,0:T(8,128)S(1)}, f32[136,128]{1,0:T(8,128)S(1)}, f32[136,128]{1,0:T(8,128)S(1)}) custom-call(s32[1]{0:T(128)} %bitcast.place_ref, bf16[256,1024]{1,0:T(8,128)(2,1)S(1)} %bitcast.15, bf16[1024,256]{1,0:T(8,128)(2,1)S(1)} %get-tuple-element.109.turned_ref, ...), custom_call_target="tpu_custom_call" | custom-call | flops 536870912 | bytes 2097152 | tf_op jit(solution)/shard_map/norm/pallas_call | solution.py:258
  34.6 1.8 %collective-permute-start.27 = (f32[136,128]{1,0:T(8,128)S(1)}, f32[136,128]{1,0:T(8,128)S(1)}, u32[]{:S(2)}, u32[]{:S(2)}) collective-permute-start(f32[136,128]{1,0:T(8,128)S(1)} %get-tuple-element.149), channel_id=1, source_target_pairs={{0,6},{2,4},{4,2},{6,0},{8,14},{10,12},{12,10},{14,8},{16,22},{18,... | collective-permute-start | bytes 208904 | tf_op jit(solution)/shard_map/ppermute | solution.py:181
  37.0 1.1 %collective-permute-start.29 = (f32[136,128]{1,0:T(8,128)S(1)}, f32[136,128]{1,0:T(8,128)S(1)}, u32[]{:S(2)}, u32[]{:S(2)}) collective-permute-start(f32[136,128]{1,0:T(8,128)S(1)} %get-tuple-element.151), channel_id=1, source_target_pairs={{0,2},{2,0},{4,6},{6,4},{8,10},{10,8},{12,14},{14,12},{16,18},{18,... | collective-permute-start | bytes 208904 | tf_op jit(solution)/shard_map/ppermute | solution.py:181
  38.2 1.6 %collective-permute-start.21 = (f32[136,128]{1,0:T(8,128)S(1)}, f32[136,128]{1,0:T(8,128)S(1)}, u32[]{:S(2)}, u32[]{:S(2)}) collective-permute-start(f32[136,128]{1,0:T(8,128)S(1)} %add_add_fusion.3), channel_id=1, source_target_pairs={{0,8},{2,10},{4,12},{6,14},{8,0},{10,2},{12,4},{14,6},{16,24},{18,... | collective-permute-start | bytes 208904 | tf_op jit(solution)/shard_map/ppermute | solution.py:181
  39.8 3.3 %collective-permute-start.22 = (f32[136,128]{1,0:T(8,128)S(1)}, f32[136,128]{1,0:T(8,128)S(1)}, u32[]{:S(2)}, u32[]{:S(2)}) collective-permute-start(f32[136,128]{1,0:T(8,128)S(1)} %add_add_fusion.3), channel_id=1, source_target_pairs={{0,24},{2,26},{4,28},{6,30},{8,16},{10,18},{12,20},{14,22},{16,8},... | collective-permute-start | bytes 208904 | tf_op jit(solution)/shard_map/ppermute | solution.py:181
  43.3 1.0 %collective-permute-start.30 = (f32[136,128]{1,0:T(8,128)S(1)}, f32[136,128]{1,0:T(8,128)S(1)}, u32[]{:S(2)}, u32[]{:S(2)}) collective-permute-start(f32[136,128]{1,0:T(8,128)S(1)} %add_add_fusion.1), channel_id=1, source_target_pairs={{0,8},{2,10},{4,12},{6,14},{8,0},{10,2},{12,4},{14,6},{16,24},{18,... | collective-permute-start | bytes 208904 | tf_op jit(solution)/shard_map/ppermute | solution.py:181
  44.3 3.3 %collective-permute-start.31 = (f32[136,128]{1,0:T(8,128)S(1)}, f32[136,128]{1,0:T(8,128)S(1)}, u32[]{:S(2)}, u32[]{:S(2)}) collective-permute-start(f32[136,128]{1,0:T(8,128)S(1)} %add_add_fusion.1), channel_id=1, source_target_pairs={{0,24},{2,26},{4,28},{6,30},{8,16},{10,18},{12,20},{14,22},{16,8},... | collective-permute-start | bytes 208904 | tf_op jit(solution)/shard_map/ppermute | solution.py:181
  47.6 0.8 %collective-permute-done.23.refs_3_ = f32[136,128]{1,0:T(8,128)S(1)} collective-permute-done((f32[136,128]{1,0:T(8,128)S(1)}, f32[136,128]{1,0:T(8,128)S(1)}, u32[]{:S(2)}, u32[]{:S(2)}) %collective-permute-start.23) | collective-permute-done | bytes 69664 | tf_op jit(solution)/shard_map/ppermute | solution.py:181
  48.4 1.9 %collective-permute-start.24 = (f32[136,128]{1,0:T(8,128)S(1)}, f32[136,128]{1,0:T(8,128)S(1)}, u32[]{:S(2)}, u32[]{:S(2)}) collective-permute-start(f32[136,128]{1,0:T(8,128)S(1)} %get-tuple-element.143), channel_id=1, source_target_pairs={{0,6},{2,4},{4,2},{6,0},{8,14},{10,12},{12,10},{14,8},{16,22},{18,... | collective-permute-start | bytes 208904 | tf_op jit(solution)/shard_map/ppermute | solution.py:181
  50.4 0.7 %collective-permute-start.25 = (f32[136,128]{1,0:T(8,128)S(1)}, f32[136,128]{1,0:T(8,128)S(1)}, u32[]{:S(2)}, u32[]{:S(2)}) collective-permute-start(f32[136,128]{1,0:T(8,128)S(1)} %get-tuple-element.144), channel_id=1, source_target_pairs={{0,4},{2,6},{4,0},{6,2},{8,12},{10,14},{12,8},{14,10},{16,20},{18,... | collective-permute-start | bytes 208904 | tf_op jit(solution)/shard_map/ppermute | solution.py:181
  51.1 0.9 %collective-permute-start.26 = (f32[136,128]{1,0:T(8,128)S(1)}, f32[136,128]{1,0:T(8,128)S(1)}, u32[]{:S(2)}, u32[]{:S(2)}) collective-permute-start(f32[136,128]{1,0:T(8,128)S(1)} %get-tuple-element.145), channel_id=1, source_target_pairs={{0,2},{2,0},{4,6},{6,4},{8,10},{10,8},{12,14},{14,12},{16,18},{18,... | collective-permute-start | bytes 208904 | tf_op jit(solution)/shard_map/ppermute | solution.py:181
  52.0 0.8 %collective-permute-done.32.refs_3_ = f32[136,128]{1,0:T(8,128)S(1)} collective-permute-done((f32[136,128]{1,0:T(8,128)S(1)}, f32[136,128]{1,0:T(8,128)S(1)}, u32[]{:S(2)}, u32[]{:S(2)}) %collective-permute-start.32) | collective-permute-done | bytes 69664 | tf_op jit(solution)/shard_map/ppermute | solution.py:181
  52.9 1.9 %collective-permute-start.33 = (f32[136,128]{1,0:T(8,128)S(1)}, f32[136,128]{1,0:T(8,128)S(1)}, u32[]{:S(2)}, u32[]{:S(2)}) collective-permute-start(f32[136,128]{1,0:T(8,128)S(1)} %get-tuple-element.160), channel_id=1, source_target_pairs={{0,6},{2,4},{4,2},{6,0},{8,14},{10,12},{12,10},{14,8},{16,22},{18,... | collective-permute-start | bytes 208904 | tf_op jit(solution)/shard_map/ppermute | solution.py:181
  55.5 0.9 %collective-permute-start.35 = (f32[136,128]{1,0:T(8,128)S(1)}, f32[136,128]{1,0:T(8,128)S(1)}, u32[]{:S(2)}, u32[]{:S(2)}) collective-permute-start(f32[136,128]{1,0:T(8,128)S(1)} %get-tuple-element.162), channel_id=1, source_target_pairs={{0,2},{2,0},{4,6},{6,4},{8,10},{10,8},{12,14},{14,12},{16,18},{18,... | collective-permute-start | bytes 208904 | tf_op jit(solution)/shard_map/ppermute | solution.py:181
  56.4 3.2 %partial.1 = (bf16[256,1024]{1,0:T(8,128)(2,1)}, bf16[256,1024]{1,0:T(8,128)(2,1)}, bf16[256,1024]{1,0:T(8,128)(2,1)}, f32[256,512]{1,0:T(8,128)S(1)}, f32[256,512]{1,0:T(8,128)S(1)}) custom-call(s32[1]{0:T(128)} %bitcast.place_ref, bf16[256,1024]{1,0:T(8,128)(2,1)S(1)} %bitcast.16, bf16[256,1024]{1,0:T(8,128)(2,1)S(1)} %bitcast.19, ...), custom_call_target="tpu_custom_call" | custom-call | flops 3221225472 | bytes 2097152 | tf_op jit(solution)/shard_map/partial/pallas_call | solution.py:270
  59.8 1.1 %final.1 = (bf16[256,1024]{1,0:T(8,128)(2,1)}, bf16[256,1024]{1,0:T(8,128)(2,1)}) custom-call(s32[1]{0:T(128)} %bitcast.place_ref, bf16[256,1024]{1,0:T(8,128)(2,1)S(1)} %bitcast.20, bf16[256,1024]{1,0:T(8,128)(2,1)S(1)} %bitcast.24, f32[256,512]{1,0:T(8,128)S(1)} %get-tuple-element.147.key_part_ref, ...), custom_call_target="tpu_custom_call", output_to_operand_aliasing={{0}: (9, {}), {1}: (10, {})} | custom-call | flops 536870912 | bytes 2097152 | tf_op jit(solution)/shard_map/final/pallas_call | solution.py:286
  (72 shorter events, 7.1 us)
Async XLA Ops:
  2.3 8.0 %collective-permute-start = (f32[128,128]{1,0:T(8,128)S(1)}, f32[128,128]{1,0:T(8,128)S(1)}, u32[]{:S(2)}, u32[]{:S(2)}) collective-permute-start(f32[128,128]{1,0:T(8,128)S(1)} %get-tuple-element.88), channel_id=1, source_target_pairs={{0,6},{2,4},{4,2},{6,0},{8,14},{10,12},{12,10},{14,8},{16,22},{18,... | collective-permute-start | bytes 196616 | tf_op jit(solution)/shard_map/ppermute | solution.py:181
  6.2 5.1 %collective-permute-start.1 = (f32[128,128]{1,0:T(8,128)S(1)}, f32[128,128]{1,0:T(8,128)S(1)}, u32[]{:S(2)}, u32[]{:S(2)}) collective-permute-start(f32[128,128]{1,0:T(8,128)S(1)} %get-tuple-element.89), channel_id=1, source_target_pairs={{0,4},{2,6},{4,0},{6,2},{8,12},{10,14},{12,8},{14,10},{16,20},{18,... | collective-permute-start | bytes 196616 | tf_op jit(solution)/shard_map/ppermute | solution.py:181
  6.9 8.5 %collective-permute-start.6 = (f32[128,128]{1,0:T(8,128)S(1)}, f32[128,128]{1,0:T(8,128)S(1)}, u32[]{:S(2)}, u32[]{:S(2)}) collective-permute-start(f32[128,128]{1,0:T(8,128)S(1)} %get-tuple-element.96), channel_id=1, source_target_pairs={{0,6},{2,4},{4,2},{6,0},{8,14},{10,12},{12,10},{14,8},{16,22},{18,... | collective-permute-start | bytes 196616 | tf_op jit(solution)/shard_map/ppermute | solution.py:181
  9.7 5.9 %collective-permute-start.7 = (f32[128,128]{1,0:T(8,128)S(1)}, f32[128,128]{1,0:T(8,128)S(1)}, u32[]{:S(2)}, u32[]{:S(2)}) collective-permute-start(f32[128,128]{1,0:T(8,128)S(1)} %get-tuple-element.97), channel_id=1, source_target_pairs={{0,4},{2,6},{4,0},{6,2},{8,12},{10,14},{12,8},{14,10},{16,20},{18,... | collective-permute-start | bytes 196616 | tf_op jit(solution)/shard_map/ppermute | solution.py:181
  10.2 5.3 %collective-permute-start.8 = (f32[128,128]{1,0:T(8,128)S(1)}, f32[128,128]{1,0:T(8,128)S(1)}, u32[]{:S(2)}, u32[]{:S(2)}) collective-permute-start(f32[128,128]{1,0:T(8,128)S(1)} %get-tuple-element.98), channel_id=1, source_target_pairs={{0,2},{2,0},{4,6},{6,4},{8,10},{10,8},{12,14},{14,12},{16,18},{18,... | collective-permute-start | bytes 196616 | tf_op jit(solution)/shard_map/ppermute | solution.py:181
  11.3 9.4 %collective-permute-start.3 = (f32[128,128]{1,0:T(8,128)S(1)}, f32[128,128]{1,0:T(8,128)S(1)}, u32[]{:S(2)}, u32[]{:S(2)}) collective-permute-start(f32[128,128]{1,0:T(8,128)S(1)} %add_add_fusion.7), channel_id=1, source_target_pairs={{0,16},{2,18},{4,20},{6,22},{8,24},{10,26},{12,28},{14,30},{16,0},... | collective-permute-start | bytes 196616 | tf_op jit(solution)/shard_map/ppermute | solution.py:181
  14.0 6.9 %collective-permute-start.4 = (f32[128,128]{1,0:T(8,128)S(1)}, f32[128,128]{1,0:T(8,128)S(1)}, u32[]{:S(2)}, u32[]{:S(2)}) collective-permute-start(f32[128,128]{1,0:T(8,128)S(1)} %add_add_fusion.7), channel_id=1, source_target_pairs={{0,24},{2,26},{4,28},{6,30},{8,16},{10,18},{12,20},{14,22},{16,8},... | collective-permute-start | bytes 196616 | tf_op jit(solution)/shard_map/ppermute | solution.py:181
  15.3 6.7 %collective-permute-start.5 = (f32[128,128]{1,0:T(8,128)S(1)}, f32[128,128]{1,0:T(8,128)S(1)}, u32[]{:S(2)}, u32[]{:S(2)}) collective-permute-start(f32[128,128]{1,0:T(8,128)S(1)} %add_add_fusion.7), channel_id=1, source_target_pairs={{0,8},{2,10},{4,12},{6,14},{8,0},{10,2},{12,4},{14,6},{16,24},{18,... | collective-permute-start | bytes 196616 | tf_op jit(solution)/shard_map/ppermute | solution.py:181
  15.6 9.1 %collective-permute-start.12 = (f32[128,128]{1,0:T(8,128)S(1)}, f32[128,128]{1,0:T(8,128)S(1)}, u32[]{:S(2)}, u32[]{:S(2)}) collective-permute-start(f32[128,128]{1,0:T(8,128)S(1)} %add_add_fusion.5), channel_id=1, source_target_pairs={{0,16},{2,18},{4,20},{6,22},{8,24},{10,26},{12,28},{14,30},{16,0},... | collective-permute-start | bytes 196616 | tf_op jit(solution)/shard_map/ppermute | solution.py:181
  18.5 7.4 %collective-permute-start.13 = (f32[128,128]{1,0:T(8,128)S(1)}, f32[128,128]{1,0:T(8,128)S(1)}, u32[]{:S(2)}, u32[]{:S(2)}) collective-permute-start(f32[128,128]{1,0:T(8,128)S(1)} %add_add_fusion.5), channel_id=1, source_target_pairs={{0,24},{2,26},{4,28},{6,30},{8,16},{10,18},{12,20},{14,22},{16,8},... | collective-permute-start | bytes 196616 | tf_op jit(solution)/shard_map/ppermute | solution.py:181
  20.8 5.1 %collective-permute-start.14 = (f32[128,128]{1,0:T(8,128)S(1)}, f32[128,128]{1,0:T(8,128)S(1)}, u32[]{:S(2)}, u32[]{:S(2)}) collective-permute-start(f32[128,128]{1,0:T(8,128)S(1)} %add_add_fusion.5), channel_id=1, source_target_pairs={{0,8},{2,10},{4,12},{6,14},{8,0},{10,2},{12,4},{14,6},{16,24},{18,... | collective-permute-start | bytes 196616 | tf_op jit(solution)/shard_map/ppermute | solution.py:181
  22.1 6.3 %collective-permute-start.9 = (f32[128,128]{1,0:T(8,128)S(1)}, f32[128,128]{1,0:T(8,128)S(1)}, u32[]{:S(2)}, u32[]{:S(2)}) collective-permute-start(f32[128,128]{1,0:T(8,128)S(1)} %get-tuple-element.115), channel_id=1, source_target_pairs={{0,6},{2,4},{4,2},{6,0},{8,14},{10,12},{12,10},{14,8},{16,22},{18,... | collective-permute-start | bytes 196616 | tf_op jit(solution)/shard_map/ppermute | solution.py:181
  24.2 5.4 %collective-permute-start.10 = (f32[128,128]{1,0:T(8,128)S(1)}, f32[128,128]{1,0:T(8,128)S(1)}, u32[]{:S(2)}, u32[]{:S(2)}) collective-permute-start(f32[128,128]{1,0:T(8,128)S(1)} %get-tuple-element.116), channel_id=1, source_target_pairs={{0,4},{2,6},{4,0},{6,2},{8,12},{10,14},{12,8},{14,10},{16,20},{18,... | collective-permute-start | bytes 196616 | tf_op jit(solution)/shard_map/ppermute | solution.py:181
  26.0 6.7 %collective-permute-start.15 = (f32[128,128]{1,0:T(8,128)S(1)}, f32[128,128]{1,0:T(8,128)S(1)}, u32[]{:S(2)}, u32[]{:S(2)}) collective-permute-start(f32[128,128]{1,0:T(8,128)S(1)} %get-tuple-element.127), channel_id=1, source_target_pairs={{0,6},{2,4},{4,2},{6,0},{8,14},{10,12},{12,10},{14,8},{16,22},{18,... | collective-permute-start | bytes 196616 | tf_op jit(solution)/shard_map/ppermute | solution.py:181
  27.9 6.0 %collective-permute-start.16 = (f32[128,128]{1,0:T(8,128)S(1)}, f32[128,128]{1,0:T(8,128)S(1)}, u32[]{:S(2)}, u32[]{:S(2)}) collective-permute-start(f32[128,128]{1,0:T(8,128)S(1)} %get-tuple-element.128), channel_id=1, source_target_pairs={{0,4},{2,6},{4,0},{6,2},{8,12},{10,14},{12,8},{14,10},{16,20},{18,... | collective-permute-start | bytes 196616 | tf_op jit(solution)/shard_map/ppermute | solution.py:181
  28.4 5.4 %collective-permute-start.17 = (f32[128,128]{1,0:T(8,128)S(1)}, f32[128,128]{1,0:T(8,128)S(1)}, u32[]{:S(2)}, u32[]{:S(2)}) collective-permute-start(f32[128,128]{1,0:T(8,128)S(1)} %get-tuple-element.129), channel_id=1, source_target_pairs={{0,2},{2,0},{4,6},{6,4},{8,10},{10,8},{12,14},{14,12},{16,18},{18,... | collective-permute-start | bytes 196616 | tf_op jit(solution)/shard_map/ppermute | solution.py:181
  30.3 6.7 %collective-permute-start.18 = (f32[136,128]{1,0:T(8,128)S(1)}, f32[136,128]{1,0:T(8,128)S(1)}, u32[]{:S(2)}, u32[]{:S(2)}) collective-permute-start(f32[136,128]{1,0:T(8,128)S(1)} %get-tuple-element.132), channel_id=1, source_target_pairs={{0,6},{2,4},{4,2},{6,0},{8,14},{10,12},{12,10},{14,8},{16,22},{18,... | collective-permute-start | bytes 208904 | tf_op jit(solution)/shard_map/ppermute | solution.py:181
  32.2 6.0 %collective-permute-start.19 = (f32[136,128]{1,0:T(8,128)S(1)}, f32[136,128]{1,0:T(8,128)S(1)}, u32[]{:S(2)}, u32[]{:S(2)}) collective-permute-start(f32[136,128]{1,0:T(8,128)S(1)} %get-tuple-element.133), channel_id=1, source_target_pairs={{0,4},{2,6},{4,0},{6,2},{8,12},{10,14},{12,8},{14,10},{16,20},{18,... | collective-permute-start | bytes 208904 | tf_op jit(solution)/shard_map/ppermute | solution.py:181
  32.7 5.4 %collective-permute-start.20 = (f32[136,128]{1,0:T(8,128)S(1)}, f32[136,128]{1,0:T(8,128)S(1)}, u32[]{:S(2)}, u32[]{:S(2)}) collective-permute-start(f32[136,128]{1,0:T(8,128)S(1)} %get-tuple-element.134), channel_id=1, source_target_pairs={{0,2},{2,0},{4,6},{6,4},{8,10},{10,8},{12,14},{14,12},{16,18},{18,... | collective-permute-start | bytes 208904 | tf_op jit(solution)/shard_map/ppermute | solution.py:181
  34.6 8.5 %collective-permute-start.27 = (f32[136,128]{1,0:T(8,128)S(1)}, f32[136,128]{1,0:T(8,128)S(1)}, u32[]{:S(2)}, u32[]{:S(2)}) collective-permute-start(f32[136,128]{1,0:T(8,128)S(1)} %get-tuple-element.149), channel_id=1, source_target_pairs={{0,6},{2,4},{4,2},{6,0},{8,14},{10,12},{12,10},{14,8},{16,22},{18,... | collective-permute-start | bytes 208904 | tf_op jit(solution)/shard_map/ppermute | solution.py:181
  36.4 6.8 %collective-permute-start.28 = (f32[136,128]{1,0:T(8,128)S(1)}, f32[136,128]{1,0:T(8,128)S(1)}, u32[]{:S(2)}, u32[]{:S(2)}) collective-permute-start(f32[136,128]{1,0:T(8,128)S(1)} %get-tuple-element.150), channel_id=1, source_target_pairs={{0,4},{2,6},{4,0},{6,2},{8,12},{10,14},{12,8},{14,10},{16,20},{18,... | collective-permute-start | bytes 208904 | tf_op jit(solution)/shard_map/ppermute | solution.py:181
  37.0 6.2 %collective-permute-start.29 = (f32[136,128]{1,0:T(8,128)S(1)}, f32[136,128]{1,0:T(8,128)S(1)}, u32[]{:S(2)}, u32[]{:S(2)}) collective-permute-start(f32[136,128]{1,0:T(8,128)S(1)} %get-tuple-element.151), channel_id=1, source_target_pairs={{0,2},{2,0},{4,6},{6,4},{8,10},{10,8},{12,14},{14,12},{16,18},{18,... | collective-permute-start | bytes 208904 | tf_op jit(solution)/shard_map/ppermute | solution.py:181
  38.2 9.4 %collective-permute-start.21 = (f32[136,128]{1,0:T(8,128)S(1)}, f32[136,128]{1,0:T(8,128)S(1)}, u32[]{:S(2)}, u32[]{:S(2)}) collective-permute-start(f32[136,128]{1,0:T(8,128)S(1)} %add_add_fusion.3), channel_id=1, source_target_pairs={{0,8},{2,10},{4,12},{6,14},{8,0},{10,2},{12,4},{14,6},{16,24},{18,... | collective-permute-start | bytes 208904 | tf_op jit(solution)/shard_map/ppermute | solution.py:181
  39.8 7.8 %collective-permute-start.22 = (f32[136,128]{1,0:T(8,128)S(1)}, f32[136,128]{1,0:T(8,128)S(1)}, u32[]{:S(2)}, u32[]{:S(2)}) collective-permute-start(f32[136,128]{1,0:T(8,128)S(1)} %add_add_fusion.3), channel_id=1, source_target_pairs={{0,24},{2,26},{4,28},{6,30},{8,16},{10,18},{12,20},{14,22},{16,8},... | collective-permute-start | bytes 208904 | tf_op jit(solution)/shard_map/ppermute | solution.py:181
  43.1 5.3 %collective-permute-start.23 = (f32[136,128]{1,0:T(8,128)S(1)}, f32[136,128]{1,0:T(8,128)S(1)}, u32[]{:S(2)}, u32[]{:S(2)}) collective-permute-start(f32[136,128]{1,0:T(8,128)S(1)} %add_add_fusion.3), channel_id=1, source_target_pairs={{0,16},{2,18},{4,20},{6,22},{8,24},{10,26},{12,28},{14,30},{16,0},... | collective-permute-start | bytes 208904 | tf_op jit(solution)/shard_map/ppermute | solution.py:181
  43.3 7.8 %collective-permute-start.30 = (f32[136,128]{1,0:T(8,128)S(1)}, f32[136,128]{1,0:T(8,128)S(1)}, u32[]{:S(2)}, u32[]{:S(2)}) collective-permute-start(f32[136,128]{1,0:T(8,128)S(1)} %add_add_fusion.1), channel_id=1, source_target_pairs={{0,8},{2,10},{4,12},{6,14},{8,0},{10,2},{12,4},{14,6},{16,24},{18,... | collective-permute-start | bytes 208904 | tf_op jit(solution)/shard_map/ppermute | solution.py:181
  44.3 7.8 %collective-permute-start.31 = (f32[136,128]{1,0:T(8,128)S(1)}, f32[136,128]{1,0:T(8,128)S(1)}, u32[]{:S(2)}, u32[]{:S(2)}) collective-permute-start(f32[136,128]{1,0:T(8,128)S(1)} %add_add_fusion.1), channel_id=1, source_target_pairs={{0,24},{2,26},{4,28},{6,30},{8,16},{10,18},{12,20},{14,22},{16,8},... | collective-permute-start | bytes 208904 | tf_op jit(solution)/shard_map/ppermute | solution.py:181
  47.6 5.2 %collective-permute-start.32 = (f32[136,128]{1,0:T(8,128)S(1)}, f32[136,128]{1,0:T(8,128)S(1)}, u32[]{:S(2)}, u32[]{:S(2)}) collective-permute-start(f32[136,128]{1,0:T(8,128)S(1)} %add_add_fusion.1), channel_id=1, source_target_pairs={{0,16},{2,18},{4,20},{6,22},{8,24},{10,26},{12,28},{14,30},{16,0},... | collective-permute-start | bytes 208904 | tf_op jit(solution)/shard_map/ppermute | solution.py:181
  48.4 7.0 %collective-permute-start.24 = (f32[136,128]{1,0:T(8,128)S(1)}, f32[136,128]{1,0:T(8,128)S(1)}, u32[]{:S(2)}, u32[]{:S(2)}) collective-permute-start(f32[136,128]{1,0:T(8,128)S(1)} %get-tuple-element.143), channel_id=1, source_target_pairs={{0,6},{2,4},{4,2},{6,0},{8,14},{10,12},{12,10},{14,8},{16,22},{18,... | collective-permute-start | bytes 208904 | tf_op jit(solution)/shard_map/ppermute | solution.py:181
  50.4 6.1 %collective-permute-start.25 = (f32[136,128]{1,0:T(8,128)S(1)}, f32[136,128]{1,0:T(8,128)S(1)}, u32[]{:S(2)}, u32[]{:S(2)}) collective-permute-start(f32[136,128]{1,0:T(8,128)S(1)} %get-tuple-element.144), channel_id=1, source_target_pairs={{0,4},{2,6},{4,0},{6,2},{8,12},{10,14},{12,8},{14,10},{16,20},{18,... | collective-permute-start | bytes 208904 | tf_op jit(solution)/shard_map/ppermute | solution.py:181
  51.1 5.4 %collective-permute-start.26 = (f32[136,128]{1,0:T(8,128)S(1)}, f32[136,128]{1,0:T(8,128)S(1)}, u32[]{:S(2)}, u32[]{:S(2)}) collective-permute-start(f32[136,128]{1,0:T(8,128)S(1)} %get-tuple-element.145), channel_id=1, source_target_pairs={{0,2},{2,0},{4,6},{6,4},{8,10},{10,8},{12,14},{14,12},{16,18},{18,... | collective-permute-start | bytes 208904 | tf_op jit(solution)/shard_map/ppermute | solution.py:181
  52.9 6.7 %collective-permute-start.33 = (f32[136,128]{1,0:T(8,128)S(1)}, f32[136,128]{1,0:T(8,128)S(1)}, u32[]{:S(2)}, u32[]{:S(2)}) collective-permute-start(f32[136,128]{1,0:T(8,128)S(1)} %get-tuple-element.160), channel_id=1, source_target_pairs={{0,6},{2,4},{4,2},{6,0},{8,14},{10,12},{12,10},{14,8},{16,22},{18,... | collective-permute-start | bytes 208904 | tf_op jit(solution)/shard_map/ppermute | solution.py:181
  (10 other events, 84.8 us)

commit v26 on v25

--- a/solution.py
+++ b/solution.py
@@ -168,7 +168,7 @@
 def exchange_steps(near_first):
     count, base, steps = lax.axis_size("seq"), GROUP, []
     while base < count:
-        masks = [base, 3 * base, 2 * base] if near_first else [2 * base, 3 * base, base]
+        masks = [3 * base, base, 2 * base] if near_first else [3 * base, 2 * base, base]
         masks = masks if 4 * base <= count else [base]
         steps.append(masks)
         base *= len(masks) + 1

time: 61.7 us -> 60.9 us (0.987)
  waiting for transfers between devices: 3.98 us -> 2.69 us
    ppermute x36, waiting for transfers between devices: 3.92 us -> 2.63 us  [swap(): lax.ppermute(array, 'seq', [(s, s ^ mask) for s in range(lax.axis_size('s...]
  transfers between devices with their start and end apart: 37 -> 37, of which waited for: 7 -> 5; matrix products, arithmetic and copies ran while one was open for 0% -> 0% of each run, Pallas kernels for 11% -> 11%
where the time goes in v26:
time: 60.9 us; the launch traced here: 60.7 us
  starting transfers between devices  47.9 us (79%)
  Pallas kernels  8.55 us (14%)
  waiting for transfers between devices  2.69 us (4%)
  between operations  0.81 us (1%)
  other arithmetic  0.75 us (1%)
    ppermute x36, starting transfers between devices, swap(): lax.ppermute(array, 'seq', [(s, s ^ mask) for s in range(lax.axis_size('s...  47.9 us
    pallas_call x1, Pallas kernels, local(): call(partial_body, [wide] * 3 + [whole(*turned_low.shape)] + [half] * CHA...  3.16 us
    ppermute x36, waiting for transfers between devices, swap(): lax.ppermute(array, 'seq', [(s, s ^ mask) for s in range(lax.axis_size('s...  2.63 us
    pallas_call x1, Pallas kernels, local(): call(delta_body, [pl.BlockSpec(memory_space=pltpu.HBM)] * 2, [short] * HE...  1.61 us
    pallas_call x2, Pallas kernels, local(): call(functools.partial(norm_body, chain), [wide, whole(*turned_low.shape)...  1.4 us
  transfers between devices with their start and end apart: 37, of which 5 were waited for; matrix products, arithmetic and copies ran while one was open for 0% of the time, Pallas kernels for 11%

profile of v26, /device:TPU:0, one launch (start us, length us, event | category | flops | bytes accessed | tf_op | source)
XLA Modules:
  0.0 60.7 jit_solution(99130130480697618)
XLA Ops:
  0.7 1.6 %delta.1 = (f32[128,128]{1,0:T(8,128)S(1)}, f32[128,128]{1,0:T(8,128)S(1)}, f32[128,128]{1,0:T(8,128)S(1)}, f32[128,128]{1,0:T(8,128)S(1)}, f32[128,128]{1,0:T(8...) custom-call(s32[1]{0:T(128)} %bitcast.place_ref, bf16[256,1024]{1,0:T(8,128)(2,1)} %bitcast.17, ...), custom_call_target="tpu_custom_call" | custom-call | flops 402653184 | bytes 2097152 | tf_op jit(solution)/shard_map/delta/pallas_call | solution.py:234
  2.3 4.0 %collective-permute-start = (f32[128,128]{1,0:T(8,128)S(1)}, f32[128,128]{1,0:T(8,128)S(1)}, u32[]{:S(2)}, u32[]{:S(2)}) collective-permute-start(f32[128,128]{1,0:T(8,128)S(1)} %get-tuple-element.88), channel_id=1, source_target_pairs={{0,6},{2,4},{4,2},{6,0},{8,14},{10,12},{12,10},{14,8},{16,22},{18,... | collective-permute-start | bytes 196616 | tf_op jit(solution)/shard_map/ppermute | solution.py:181
  6.9 2.8 %collective-permute-start.6 = (f32[128,128]{1,0:T(8,128)S(1)}, f32[128,128]{1,0:T(8,128)S(1)}, u32[]{:S(2)}, u32[]{:S(2)}) collective-permute-start(f32[128,128]{1,0:T(8,128)S(1)} %get-tuple-element.96), channel_id=1, source_target_pairs={{0,6},{2,4},{4,2},{6,0},{8,14},{10,12},{12,10},{14,8},{16,22},{18,... | collective-permute-start | bytes 196616 | tf_op jit(solution)/shard_map/ppermute | solution.py:181
  11.3 3.7 %collective-permute-start.3 = (f32[128,128]{1,0:T(8,128)S(1)}, f32[128,128]{1,0:T(8,128)S(1)}, u32[]{:S(2)}, u32[]{:S(2)}) collective-permute-start(f32[128,128]{1,0:T(8,128)S(1)} %add_add_fusion.7), channel_id=1, source_target_pairs={{0,24},{2,26},{4,28},{6,30},{8,16},{10,18},{12,20},{14,22},{16,8},... | collective-permute-start | bytes 196616 | tf_op jit(solution)/shard_map/ppermute | solution.py:181
  15.0 0.8 %collective-permute-start.5 = (f32[128,128]{1,0:T(8,128)S(1)}, f32[128,128]{1,0:T(8,128)S(1)}, u32[]{:S(2)}, u32[]{:S(2)}) collective-permute-start(f32[128,128]{1,0:T(8,128)S(1)} %add_add_fusion.7), channel_id=1, source_target_pairs={{0,8},{2,10},{4,12},{6,14},{8,0},{10,2},{12,4},{14,6},{16,24},{18,... | collective-permute-start | bytes 196616 | tf_op jit(solution)/shard_map/ppermute | solution.py:181
  15.8 3.7 %collective-permute-start.12 = (f32[128,128]{1,0:T(8,128)S(1)}, f32[128,128]{1,0:T(8,128)S(1)}, u32[]{:S(2)}, u32[]{:S(2)}) collective-permute-start(f32[128,128]{1,0:T(8,128)S(1)} %add_add_fusion.5), channel_id=1, source_target_pairs={{0,24},{2,26},{4,28},{6,30},{8,16},{10,18},{12,20},{14,22},{16,8},... | collective-permute-start | bytes 196616 | tf_op jit(solution)/shard_map/ppermute | solution.py:181
  19.5 0.9 %inner.1 = (f32[256,1024]{1,0:T(8,128)S(1)}, bf16[1024,256]{1,0:T(8,128)(2,1)S(1)}) custom-call(s32[1]{0:T(128)} %bitcast.place_ref, bf16[256,1024]{1,0:T(8,128)(2,1)S(1)} %bitcast.13, bf16[256,1024]{1,0:T(8,128)(2,1)S(1)} %bitcast.18, bf16[256,1024]{1,0:T(8,128)(2,1)S(1)} %bitcast.22), custom_call_target="tpu_custom_call" | custom-call | flops 1073741824 | bytes 2097152 | tf_op jit(solution)/shard_map/inner/pallas_call | solution.py:196
  20.5 0.8 %collective-permute-start.14 = (f32[128,128]{1,0:T(8,128)S(1)}, f32[128,128]{1,0:T(8,128)S(1)}, u32[]{:S(2)}, u32[]{:S(2)}) collective-permute-start(f32[128,128]{1,0:T(8,128)S(1)} %add_add_fusion.5), channel_id=1, source_target_pairs={{0,8},{2,10},{4,12},{6,14},{8,0},{10,2},{12,4},{14,6},{16,24},{18,... | collective-permute-start | bytes 196616 | tf_op jit(solution)/shard_map/ppermute | solution.py:181
  21.3 1.6 %collective-permute-done.4.refs_2_ = f32[128,128]{1,0:T(8,128)S(1)} collective-permute-done((f32[128,128]{1,0:T(8,128)S(1)}, f32[128,128]{1,0:T(8,128)S(1)}, u32[]{:S(2)}, u32[]{:S(2)}) %collective-permute-start.4) | collective-permute-done | bytes 65568 | tf_op jit(solution)/shard_map/ppermute | solution.py:181
  23.0 1.9 %collective-permute-start.9 = (f32[128,128]{1,0:T(8,128)S(1)}, f32[128,128]{1,0:T(8,128)S(1)}, u32[]{:S(2)}, u32[]{:S(2)}) collective-permute-start(f32[128,128]{1,0:T(8,128)S(1)} %get-tuple-element.115), channel_id=1, source_target_pairs={{0,6},{2,4},{4,2},{6,0},{8,14},{10,12},{12,10},{14,8},{16,22},{18,... | collective-permute-start | bytes 196616 | tf_op jit(solution)/shard_map/ppermute | solution.py:181
  24.9 1.1 %collective-permute-start.10 = (f32[128,128]{1,0:T(8,128)S(1)}, f32[128,128]{1,0:T(8,128)S(1)}, u32[]{:S(2)}, u32[]{:S(2)}) collective-permute-start(f32[128,128]{1,0:T(8,128)S(1)} %get-tuple-element.116), channel_id=1, source_target_pairs={{0,4},{2,6},{4,0},{6,2},{8,12},{10,14},{12,8},{14,10},{16,20},{18,... | collective-permute-start | bytes 196616 | tf_op jit(solution)/shard_map/ppermute | solution.py:181
  26.7 1.9 %collective-permute-start.15 = (f32[128,128]{1,0:T(8,128)S(1)}, f32[128,128]{1,0:T(8,128)S(1)}, u32[]{:S(2)}, u32[]{:S(2)}) collective-permute-start(f32[128,128]{1,0:T(8,128)S(1)} %get-tuple-element.127), channel_id=1, source_target_pairs={{0,6},{2,4},{4,2},{6,0},{8,14},{10,12},{12,10},{14,8},{16,22},{18,... | collective-permute-start | bytes 196616 | tf_op jit(solution)/shard_map/ppermute | solution.py:181
  28.5 1.1 %collective-permute-start.16 = (f32[128,128]{1,0:T(8,128)S(1)}, f32[128,128]{1,0:T(8,128)S(1)}, u32[]{:S(2)}, u32[]{:S(2)}) collective-permute-start(f32[128,128]{1,0:T(8,128)S(1)} %get-tuple-element.128), channel_id=1, source_target_pairs={{0,4},{2,6},{4,0},{6,2},{8,12},{10,14},{12,8},{14,10},{16,20},{18,... | collective-permute-start | bytes 196616 | tf_op jit(solution)/shard_map/ppermute | solution.py:181
  29.7 0.8 %collective-permute-start.17 = (f32[128,128]{1,0:T(8,128)S(1)}, f32[128,128]{1,0:T(8,128)S(1)}, u32[]{:S(2)}, u32[]{:S(2)}) collective-permute-start(f32[128,128]{1,0:T(8,128)S(1)} %get-tuple-element.129), channel_id=1, source_target_pairs={{0,2},{2,0},{4,6},{6,4},{8,10},{10,8},{12,14},{14,12},{16,18},{18,... | collective-permute-start | bytes 196616 | tf_op jit(solution)/shard_map/ppermute | solution.py:181
  30.5 0.7 %norm.2 = (bf16[256,512]{1,0:T(8,128)(2,1)S(1)}, f32[136,128]{1,0:T(8,128)S(1)}, f32[136,128]{1,0:T(8,128)S(1)}, f32[136,128]{1,0:T(8,128)S(1)}, f32[136,128]{1,0:T(8,128)S(1)}) custom-call(s32[1]{0:T(128)} %bitcast.place_ref, bf16[256,1024]{1,0:T(8,128)(2,1)S(1)} %bitcast.14, bf16[1024,256]{1,0:T(8,128)(2,1)S(1)} %get-tuple-element.109.turned_ref, ...), custom_call_target="tpu_custom_call" | custom-call | flops 536870912 | bytes 2097152 | tf_op jit(solution)/shard_map/norm/pallas_call | solution.py:258
  31.2 1.8 %collective-permute-start.18 = (f32[136,128]{1,0:T(8,128)S(1)}, f32[136,128]{1,0:T(8,128)S(1)}, u32[]{:S(2)}, u32[]{:S(2)}) collective-permute-start(f32[136,128]{1,0:T(8,128)S(1)} %get-tuple-element.132), channel_id=1, source_target_pairs={{0,6},{2,4},{4,2},{6,0},{8,14},{10,12},{12,10},{14,8},{16,22},{18,... | collective-permute-start | bytes 208904 | tf_op jit(solution)/shard_map/ppermute | solution.py:181
  32.9 1.1 %collective-permute-start.19 = (f32[136,128]{1,0:T(8,128)S(1)}, f32[136,128]{1,0:T(8,128)S(1)}, u32[]{:S(2)}, u32[]{:S(2)}) collective-permute-start(f32[136,128]{1,0:T(8,128)S(1)} %get-tuple-element.133), channel_id=1, source_target_pairs={{0,4},{2,6},{4,0},{6,2},{8,12},{10,14},{12,8},{14,10},{16,20},{18,... | collective-permute-start | bytes 208904 | tf_op jit(solution)/shard_map/ppermute | solution.py:181
  34.7 0.7 %norm.3 = (bf16[256,512]{1,0:T(8,128)(2,1)S(1)}, f32[136,128]{1,0:T(8,128)S(1)}, f32[136,128]{1,0:T(8,128)S(1)}, f32[136,128]{1,0:T(8,128)S(1)}, f32[136,128]{1,0:T(8,128)S(1)}) custom-call(s32[1]{0:T(128)} %bitcast.place_ref, bf16[256,1024]{1,0:T(8,128)(2,1)S(1)} %bitcast.15, bf16[1024,256]{1,0:T(8,128)(2,1)S(1)} %get-tuple-element.109.turned_ref, ...), custom_call_target="tpu_custom_call" | custom-call | flops 536870912 | bytes 2097152 | tf_op jit(solution)/shard_map/norm/pallas_call | solution.py:258
  35.4 1.7 %collective-permute-start.27 = (f32[136,128]{1,0:T(8,128)S(1)}, f32[136,128]{1,0:T(8,128)S(1)}, u32[]{:S(2)}, u32[]{:S(2)}) collective-permute-start(f32[136,128]{1,0:T(8,128)S(1)} %get-tuple-element.149), channel_id=1, source_target_pairs={{0,6},{2,4},{4,2},{6,0},{8,14},{10,12},{12,10},{14,8},{16,22},{18,... | collective-permute-start | bytes 208904 | tf_op jit(solution)/shard_map/ppermute | solution.py:181
  37.2 1.1 %collective-permute-start.28 = (f32[136,128]{1,0:T(8,128)S(1)}, f32[136,128]{1,0:T(8,128)S(1)}, u32[]{:S(2)}, u32[]{:S(2)}) collective-permute-start(f32[136,128]{1,0:T(8,128)S(1)} %get-tuple-element.150), channel_id=1, source_target_pairs={{0,4},{2,6},{4,0},{6,2},{8,12},{10,14},{12,8},{14,10},{16,20},{18,... | collective-permute-start | bytes 208904 | tf_op jit(solution)/shard_map/ppermute | solution.py:181
  39.0 2.0 %collective-permute-start.21 = (f32[136,128]{1,0:T(8,128)S(1)}, f32[136,128]{1,0:T(8,128)S(1)}, u32[]{:S(2)}, u32[]{:S(2)}) collective-permute-start(f32[136,128]{1,0:T(8,128)S(1)} %add_add_fusion.3), channel_id=1, source_target_pairs={{0,24},{2,26},{4,28},{6,30},{8,16},{10,18},{12,20},{14,22},{16,8},... | collective-permute-start | bytes 208904 | tf_op jit(solution)/shard_map/ppermute | solution.py:181
  41.0 2.5 %collective-permute-start.23 = (f32[136,128]{1,0:T(8,128)S(1)}, f32[136,128]{1,0:T(8,128)S(1)}, u32[]{:S(2)}, u32[]{:S(2)}) collective-permute-start(f32[136,128]{1,0:T(8,128)S(1)} %add_add_fusion.3), channel_id=1, source_target_pairs={{0,16},{2,18},{4,20},{6,22},{8,24},{10,26},{12,28},{14,30},{16,0},... | collective-permute-start | bytes 208904 | tf_op jit(solution)/shard_map/ppermute | solution.py:181
  43.5 2.0 %collective-permute-start.30 = (f32[136,128]{1,0:T(8,128)S(1)}, f32[136,128]{1,0:T(8,128)S(1)}, u32[]{:S(2)}, u32[]{:S(2)}) collective-permute-start(f32[136,128]{1,0:T(8,128)S(1)} %add_add_fusion.1), channel_id=1, source_target_pairs={{0,24},{2,26},{4,28},{6,30},{8,16},{10,18},{12,20},{14,22},{16,8},... | collective-permute-start | bytes 208904 | tf_op jit(solution)/shard_map/ppermute | solution.py:181
  45.5 2.4 %collective-permute-start.32 = (f32[136,128]{1,0:T(8,128)S(1)}, f32[136,128]{1,0:T(8,128)S(1)}, u32[]{:S(2)}, u32[]{:S(2)}) collective-permute-start(f32[136,128]{1,0:T(8,128)S(1)} %add_add_fusion.1), channel_id=1, source_target_pairs={{0,16},{2,18},{4,20},{6,22},{8,24},{10,26},{12,28},{14,30},{16,0},... | collective-permute-start | bytes 208904 | tf_op jit(solution)/shard_map/ppermute | solution.py:181
  48.1 1.7 %collective-permute-start.24 = (f32[136,128]{1,0:T(8,128)S(1)}, f32[136,128]{1,0:T(8,128)S(1)}, u32[]{:S(2)}, u32[]{:S(2)}) collective-permute-start(f32[136,128]{1,0:T(8,128)S(1)} %get-tuple-element.143), channel_id=1, source_target_pairs={{0,6},{2,4},{4,2},{6,0},{8,14},{10,12},{12,10},{14,8},{16,22},{18,... | collective-permute-start | bytes 208904 | tf_op jit(solution)/shard_map/ppermute | solution.py:181
  49.8 1.1 %collective-permute-start.25 = (f32[136,128]{1,0:T(8,128)S(1)}, f32[136,128]{1,0:T(8,128)S(1)}, u32[]{:S(2)}, u32[]{:S(2)}) collective-permute-start(f32[136,128]{1,0:T(8,128)S(1)} %get-tuple-element.144), channel_id=1, source_target_pairs={{0,4},{2,6},{4,0},{6,2},{8,12},{10,14},{12,8},{14,10},{16,20},{18,... | collective-permute-start | bytes 208904 | tf_op jit(solution)/shard_map/ppermute | solution.py:181
  51.0 0.7 %collective-permute-start.26 = (f32[136,128]{1,0:T(8,128)S(1)}, f32[136,128]{1,0:T(8,128)S(1)}, u32[]{:S(2)}, u32[]{:S(2)}) collective-permute-start(f32[136,128]{1,0:T(8,128)S(1)} %get-tuple-element.145), channel_id=1, source_target_pairs={{0,2},{2,0},{4,6},{6,4},{8,10},{10,8},{12,14},{14,12},{16,18},{18,... | collective-permute-start | bytes 208904 | tf_op jit(solution)/shard_map/ppermute | solution.py:181
  51.8 1.7 %collective-permute-start.33 = (f32[136,128]{1,0:T(8,128)S(1)}, f32[136,128]{1,0:T(8,128)S(1)}, u32[]{:S(2)}, u32[]{:S(2)}) collective-permute-start(f32[136,128]{1,0:T(8,128)S(1)} %get-tuple-element.160), channel_id=1, source_target_pairs={{0,6},{2,4},{4,2},{6,0},{8,14},{10,12},{12,10},{14,8},{16,22},{18,... | collective-permute-start | bytes 208904 | tf_op jit(solution)/shard_map/ppermute | solution.py:181
  53.5 1.1 %collective-permute-start.34 = (f32[136,128]{1,0:T(8,128)S(1)}, f32[136,128]{1,0:T(8,128)S(1)}, u32[]{:S(2)}, u32[]{:S(2)}) collective-permute-start(f32[136,128]{1,0:T(8,128)S(1)} %get-tuple-element.161), channel_id=1, source_target_pairs={{0,4},{2,6},{4,0},{6,2},{8,12},{10,14},{12,8},{14,10},{16,20},{18,... | collective-permute-start | bytes 208904 | tf_op jit(solution)/shard_map/ppermute | solution.py:181
  54.7 0.7 %collective-permute-start.35 = (f32[136,128]{1,0:T(8,128)S(1)}, f32[136,128]{1,0:T(8,128)S(1)}, u32[]{:S(2)}, u32[]{:S(2)}) collective-permute-start(f32[136,128]{1,0:T(8,128)S(1)} %get-tuple-element.162), channel_id=1, source_target_pairs={{0,2},{2,0},{4,6},{6,4},{8,10},{10,8},{12,14},{14,12},{16,18},{18,... | collective-permute-start | bytes 208904 | tf_op jit(solution)/shard_map/ppermute | solution.py:181
  55.3 3.2 %partial.1 = (bf16[256,1024]{1,0:T(8,128)(2,1)}, bf16[256,1024]{1,0:T(8,128)(2,1)}, bf16[256,1024]{1,0:T(8,128)(2,1)}, f32[256,512]{1,0:T(8,128)S(1)}, f32[256,512]{1,0:T(8,128)S(1)}) custom-call(s32[1]{0:T(128)} %bitcast.place_ref, bf16[256,1024]{1,0:T(8,128)(2,1)S(1)} %bitcast.16, bf16[256,1024]{1,0:T(8,128)(2,1)S(1)} %bitcast.19, ...), custom_call_target="tpu_custom_call" | custom-call | flops 3221225472 | bytes 2097152 | tf_op jit(solution)/shard_map/partial/pallas_call | solution.py:270
  59.0 1.1 %final.1 = (bf16[256,1024]{1,0:T(8,128)(2,1)}, bf16[256,1024]{1,0:T(8,128)(2,1)}) custom-call(s32[1]{0:T(128)} %bitcast.place_ref, bf16[256,1024]{1,0:T(8,128)(2,1)S(1)} %bitcast.20, bf16[256,1024]{1,0:T(8,128)(2,1)S(1)} %bitcast.24, f32[256,512]{1,0:T(8,128)S(1)} %get-tuple-element.147.key_part_ref, ...), custom_call_target="tpu_custom_call", output_to_operand_aliasing={{0}: (9, {}), {1}: (10, {})} | custom-call | flops 536870912 | bytes 2097152 | tf_op jit(solution)/shard_map/final/pallas_call | solution.py:286
  (72 shorter events, 6.0 us)
Async XLA Ops:
  2.3 8.0 %collective-permute-start = (f32[128,128]{1,0:T(8,128)S(1)}, f32[128,128]{1,0:T(8,128)S(1)}, u32[]{:S(2)}, u32[]{:S(2)}) collective-permute-start(f32[128,128]{1,0:T(8,128)S(1)} %get-tuple-element.88), channel_id=1, source_target_pairs={{0,6},{2,4},{4,2},{6,0},{8,14},{10,12},{12,10},{14,8},{16,22},{18,... | collective-permute-start | bytes 196616 | tf_op jit(solution)/shard_map/ppermute | solution.py:181
  6.2 5.1 %collective-permute-start.1 = (f32[128,128]{1,0:T(8,128)S(1)}, f32[128,128]{1,0:T(8,128)S(1)}, u32[]{:S(2)}, u32[]{:S(2)}) collective-permute-start(f32[128,128]{1,0:T(8,128)S(1)} %get-tuple-element.89), channel_id=1, source_target_pairs={{0,4},{2,6},{4,0},{6,2},{8,12},{10,14},{12,8},{14,10},{16,20},{18,... | collective-permute-start | bytes 196616 | tf_op jit(solution)/shard_map/ppermute | solution.py:181
  6.9 8.1 %collective-permute-start.6 = (f32[128,128]{1,0:T(8,128)S(1)}, f32[128,128]{1,0:T(8,128)S(1)}, u32[]{:S(2)}, u32[]{:S(2)}) collective-permute-start(f32[128,128]{1,0:T(8,128)S(1)} %get-tuple-element.96), channel_id=1, source_target_pairs={{0,6},{2,4},{4,2},{6,0},{8,14},{10,12},{12,10},{14,8},{16,22},{18,... | collective-permute-start | bytes 196616 | tf_op jit(solution)/shard_map/ppermute | solution.py:181
  9.7 6.1 %collective-permute-start.7 = (f32[128,128]{1,0:T(8,128)S(1)}, f32[128,128]{1,0:T(8,128)S(1)}, u32[]{:S(2)}, u32[]{:S(2)}) collective-permute-start(f32[128,128]{1,0:T(8,128)S(1)} %get-tuple-element.97), channel_id=1, source_target_pairs={{0,4},{2,6},{4,0},{6,2},{8,12},{10,14},{12,8},{14,10},{16,20},{18,... | collective-permute-start | bytes 196616 | tf_op jit(solution)/shard_map/ppermute | solution.py:181
  10.2 5.6 %collective-permute-start.8 = (f32[128,128]{1,0:T(8,128)S(1)}, f32[128,128]{1,0:T(8,128)S(1)}, u32[]{:S(2)}, u32[]{:S(2)}) collective-permute-start(f32[128,128]{1,0:T(8,128)S(1)} %get-tuple-element.98), channel_id=1, source_target_pairs={{0,2},{2,0},{4,6},{6,4},{8,10},{10,8},{12,14},{14,12},{16,18},{18,... | collective-permute-start | bytes 196616 | tf_op jit(solution)/shard_map/ppermute | solution.py:181
  11.3 9.1 %collective-permute-start.3 = (f32[128,128]{1,0:T(8,128)S(1)}, f32[128,128]{1,0:T(8,128)S(1)}, u32[]{:S(2)}, u32[]{:S(2)}) collective-permute-start(f32[128,128]{1,0:T(8,128)S(1)} %add_add_fusion.7), channel_id=1, source_target_pairs={{0,24},{2,26},{4,28},{6,30},{8,16},{10,18},{12,20},{14,22},{16,8},... | collective-permute-start | bytes 196616 | tf_op jit(solution)/shard_map/ppermute | solution.py:181
  15.0 7.9 %collective-permute-start.4 = (f32[128,128]{1,0:T(8,128)S(1)}, f32[128,128]{1,0:T(8,128)S(1)}, u32[]{:S(2)}, u32[]{:S(2)}) collective-permute-start(f32[128,128]{1,0:T(8,128)S(1)} %add_add_fusion.7), channel_id=1, source_target_pairs={{0,16},{2,18},{4,20},{6,22},{8,24},{10,26},{12,28},{14,30},{16,0},... | collective-permute-start | bytes 196616 | tf_op jit(solution)/shard_map/ppermute | solution.py:181
  15.0 7.9 %collective-permute-start.5 = (f32[128,128]{1,0:T(8,128)S(1)}, f32[128,128]{1,0:T(8,128)S(1)}, u32[]{:S(2)}, u32[]{:S(2)}) collective-permute-start(f32[128,128]{1,0:T(8,128)S(1)} %add_add_fusion.7), channel_id=1, source_target_pairs={{0,8},{2,10},{4,12},{6,14},{8,0},{10,2},{12,4},{14,6},{16,24},{18,... | collective-permute-start | bytes 196616 | tf_op jit(solution)/shard_map/ppermute | solution.py:181
  15.8 10.2 %collective-permute-start.12 = (f32[128,128]{1,0:T(8,128)S(1)}, f32[128,128]{1,0:T(8,128)S(1)}, u32[]{:S(2)}, u32[]{:S(2)}) collective-permute-start(f32[128,128]{1,0:T(8,128)S(1)} %add_add_fusion.5), channel_id=1, source_target_pairs={{0,24},{2,26},{4,28},{6,30},{8,16},{10,18},{12,20},{14,22},{16,8},... | collective-permute-start | bytes 196616 | tf_op jit(solution)/shard_map/ppermute | solution.py:181
  19.5 7.1 %collective-permute-start.13 = (f32[128,128]{1,0:T(8,128)S(1)}, f32[128,128]{1,0:T(8,128)S(1)}, u32[]{:S(2)}, u32[]{:S(2)}) collective-permute-start(f32[128,128]{1,0:T(8,128)S(1)} %add_add_fusion.5), channel_id=1, source_target_pairs={{0,16},{2,18},{4,20},{6,22},{8,24},{10,26},{12,28},{14,30},{16,0},... | collective-permute-start | bytes 196616 | tf_op jit(solution)/shard_map/ppermute | solution.py:181
  20.5 6.1 %collective-permute-start.14 = (f32[128,128]{1,0:T(8,128)S(1)}, f32[128,128]{1,0:T(8,128)S(1)}, u32[]{:S(2)}, u32[]{:S(2)}) collective-permute-start(f32[128,128]{1,0:T(8,128)S(1)} %add_add_fusion.5), channel_id=1, source_target_pairs={{0,8},{2,10},{4,12},{6,14},{8,0},{10,2},{12,4},{14,6},{16,24},{18,... | collective-permute-start | bytes 196616 | tf_op jit(solution)/shard_map/ppermute | solution.py:181
  23.0 6.6 %collective-permute-start.9 = (f32[128,128]{1,0:T(8,128)S(1)}, f32[128,128]{1,0:T(8,128)S(1)}, u32[]{:S(2)}, u32[]{:S(2)}) collective-permute-start(f32[128,128]{1,0:T(8,128)S(1)} %get-tuple-element.115), channel_id=1, source_target_pairs={{0,6},{2,4},{4,2},{6,0},{8,14},{10,12},{12,10},{14,8},{16,22},{18,... | collective-permute-start | bytes 196616 | tf_op jit(solution)/shard_map/ppermute | solution.py:181
  24.9 5.5 %collective-permute-start.10 = (f32[128,128]{1,0:T(8,128)S(1)}, f32[128,128]{1,0:T(8,128)S(1)}, u32[]{:S(2)}, u32[]{:S(2)}) collective-permute-start(f32[128,128]{1,0:T(8,128)S(1)} %get-tuple-element.116), channel_id=1, source_target_pairs={{0,4},{2,6},{4,0},{6,2},{8,12},{10,14},{12,8},{14,10},{16,20},{18,... | collective-permute-start | bytes 196616 | tf_op jit(solution)/shard_map/ppermute | solution.py:181
  26.7 7.4 %collective-permute-start.15 = (f32[128,128]{1,0:T(8,128)S(1)}, f32[128,128]{1,0:T(8,128)S(1)}, u32[]{:S(2)}, u32[]{:S(2)}) collective-permute-start(f32[128,128]{1,0:T(8,128)S(1)} %get-tuple-element.127), channel_id=1, source_target_pairs={{0,6},{2,4},{4,2},{6,0},{8,14},{10,12},{12,10},{14,8},{16,22},{18,... | collective-permute-start | bytes 196616 | tf_op jit(solution)/shard_map/ppermute | solution.py:181
  28.5 6.2 %collective-permute-start.16 = (f32[128,128]{1,0:T(8,128)S(1)}, f32[128,128]{1,0:T(8,128)S(1)}, u32[]{:S(2)}, u32[]{:S(2)}) collective-permute-start(f32[128,128]{1,0:T(8,128)S(1)} %get-tuple-element.128), channel_id=1, source_target_pairs={{0,4},{2,6},{4,0},{6,2},{8,12},{10,14},{12,8},{14,10},{16,20},{18,... | collective-permute-start | bytes 196616 | tf_op jit(solution)/shard_map/ppermute | solution.py:181
  29.7 5.1 %collective-permute-start.17 = (f32[128,128]{1,0:T(8,128)S(1)}, f32[128,128]{1,0:T(8,128)S(1)}, u32[]{:S(2)}, u32[]{:S(2)}) collective-permute-start(f32[128,128]{1,0:T(8,128)S(1)} %get-tuple-element.129), channel_id=1, source_target_pairs={{0,2},{2,0},{4,6},{6,4},{8,10},{10,8},{12,14},{14,12},{16,18},{18,... | collective-permute-start | bytes 196616 | tf_op jit(solution)/shard_map/ppermute | solution.py:181
  31.2 7.2 %collective-permute-start.18 = (f32[136,128]{1,0:T(8,128)S(1)}, f32[136,128]{1,0:T(8,128)S(1)}, u32[]{:S(2)}, u32[]{:S(2)}) collective-permute-start(f32[136,128]{1,0:T(8,128)S(1)} %get-tuple-element.132), channel_id=1, source_target_pairs={{0,6},{2,4},{4,2},{6,0},{8,14},{10,12},{12,10},{14,8},{16,22},{18,... | collective-permute-start | bytes 208904 | tf_op jit(solution)/shard_map/ppermute | solution.py:181
  32.9 6.1 %collective-permute-start.19 = (f32[136,128]{1,0:T(8,128)S(1)}, f32[136,128]{1,0:T(8,128)S(1)}, u32[]{:S(2)}, u32[]{:S(2)}) collective-permute-start(f32[136,128]{1,0:T(8,128)S(1)} %get-tuple-element.133), channel_id=1, source_target_pairs={{0,4},{2,6},{4,0},{6,2},{8,12},{10,14},{12,8},{14,10},{16,20},{18,... | collective-permute-start | bytes 208904 | tf_op jit(solution)/shard_map/ppermute | solution.py:181
  34.0 5.0 %collective-permute-start.20 = (f32[136,128]{1,0:T(8,128)S(1)}, f32[136,128]{1,0:T(8,128)S(1)}, u32[]{:S(2)}, u32[]{:S(2)}) collective-permute-start(f32[136,128]{1,0:T(8,128)S(1)} %get-tuple-element.134), channel_id=1, source_target_pairs={{0,2},{2,0},{4,6},{6,4},{8,10},{10,8},{12,14},{14,12},{16,18},{18,... | collective-permute-start | bytes 208904 | tf_op jit(solution)/shard_map/ppermute | solution.py:181
  35.4 5.6 %collective-permute-start.27 = (f32[136,128]{1,0:T(8,128)S(1)}, f32[136,128]{1,0:T(8,128)S(1)}, u32[]{:S(2)}, u32[]{:S(2)}) collective-permute-start(f32[136,128]{1,0:T(8,128)S(1)} %get-tuple-element.149), channel_id=1, source_target_pairs={{0,6},{2,4},{4,2},{6,0},{8,14},{10,12},{12,10},{14,8},{16,22},{18,... | collective-permute-start | bytes 208904 | tf_op jit(solution)/shard_map/ppermute | solution.py:181
  37.2 6.3 %collective-permute-start.28 = (f32[136,128]{1,0:T(8,128)S(1)}, f32[136,128]{1,0:T(8,128)S(1)}, u32[]{:S(2)}, u32[]{:S(2)}) collective-permute-start(f32[136,128]{1,0:T(8,128)S(1)} %get-tuple-element.150), channel_id=1, source_target_pairs={{0,4},{2,6},{4,0},{6,2},{8,12},{10,14},{12,8},{14,10},{16,20},{18,... | collective-permute-start | bytes 208904 | tf_op jit(solution)/shard_map/ppermute | solution.py:181
  38.3 5.2 %collective-permute-start.29 = (f32[136,128]{1,0:T(8,128)S(1)}, f32[136,128]{1,0:T(8,128)S(1)}, u32[]{:S(2)}, u32[]{:S(2)}) collective-permute-start(f32[136,128]{1,0:T(8,128)S(1)} %get-tuple-element.151), channel_id=1, source_target_pairs={{0,2},{2,0},{4,6},{6,4},{8,10},{10,8},{12,14},{14,12},{16,18},{18,... | collective-permute-start | bytes 208904 | tf_op jit(solution)/shard_map/ppermute | solution.py:181
  39.0 6.5 %collective-permute-start.21 = (f32[136,128]{1,0:T(8,128)S(1)}, f32[136,128]{1,0:T(8,128)S(1)}, u32[]{:S(2)}, u32[]{:S(2)}) collective-permute-start(f32[136,128]{1,0:T(8,128)S(1)} %add_add_fusion.3), channel_id=1, source_target_pairs={{0,24},{2,26},{4,28},{6,30},{8,16},{10,18},{12,20},{14,22},{16,8},... | collective-permute-start | bytes 208904 | tf_op jit(solution)/shard_map/ppermute | solution.py:181
  41.0 7.0 %collective-permute-start.22 = (f32[136,128]{1,0:T(8,128)S(1)}, f32[136,128]{1,0:T(8,128)S(1)}, u32[]{:S(2)}, u32[]{:S(2)}) collective-permute-start(f32[136,128]{1,0:T(8,128)S(1)} %add_add_fusion.3), channel_id=1, source_target_pairs={{0,8},{2,10},{4,12},{6,14},{8,0},{10,2},{12,4},{14,6},{16,24},{18,... | collective-permute-start | bytes 208904 | tf_op jit(solution)/shard_map/ppermute | solution.py:181
  41.0 7.0 %collective-permute-start.23 = (f32[136,128]{1,0:T(8,128)S(1)}, f32[136,128]{1,0:T(8,128)S(1)}, u32[]{:S(2)}, u32[]{:S(2)}) collective-permute-start(f32[136,128]{1,0:T(8,128)S(1)} %add_add_fusion.3), channel_id=1, source_target_pairs={{0,16},{2,18},{4,20},{6,22},{8,24},{10,26},{12,28},{14,30},{16,0},... | collective-permute-start | bytes 208904 | tf_op jit(solution)/shard_map/ppermute | solution.py:181
  43.5 7.5 %collective-permute-start.30 = (f32[136,128]{1,0:T(8,128)S(1)}, f32[136,128]{1,0:T(8,128)S(1)}, u32[]{:S(2)}, u32[]{:S(2)}) collective-permute-start(f32[136,128]{1,0:T(8,128)S(1)} %add_add_fusion.1), channel_id=1, source_target_pairs={{0,24},{2,26},{4,28},{6,30},{8,16},{10,18},{12,20},{14,22},{16,8},... | collective-permute-start | bytes 208904 | tf_op jit(solution)/shard_map/ppermute | solution.py:181
  45.5 6.2 %collective-permute-start.31 = (f32[136,128]{1,0:T(8,128)S(1)}, f32[136,128]{1,0:T(8,128)S(1)}, u32[]{:S(2)}, u32[]{:S(2)}) collective-permute-start(f32[136,128]{1,0:T(8,128)S(1)} %add_add_fusion.1), channel_id=1, source_target_pairs={{0,8},{2,10},{4,12},{6,14},{8,0},{10,2},{12,4},{14,6},{16,24},{18,... | collective-permute-start | bytes 208904 | tf_op jit(solution)/shard_map/ppermute | solution.py:181
  45.5 6.1 %collective-permute-start.32 = (f32[136,128]{1,0:T(8,128)S(1)}, f32[136,128]{1,0:T(8,128)S(1)}, u32[]{:S(2)}, u32[]{:S(2)}) collective-permute-start(f32[136,128]{1,0:T(8,128)S(1)} %add_add_fusion.1), channel_id=1, source_target_pairs={{0,16},{2,18},{4,20},{6,22},{8,24},{10,26},{12,28},{14,30},{16,0},... | collective-permute-start | bytes 208904 | tf_op jit(solution)/shard_map/ppermute | solution.py:181
  48.1 6.6 %collective-permute-start.24 = (f32[136,128]{1,0:T(8,128)S(1)}, f32[136,128]{1,0:T(8,128)S(1)}, u32[]{:S(2)}, u32[]{:S(2)}) collective-permute-start(f32[136,128]{1,0:T(8,128)S(1)} %get-tuple-element.143), channel_id=1, source_target_pairs={{0,6},{2,4},{4,2},{6,0},{8,14},{10,12},{12,10},{14,8},{16,22},{18,... | collective-permute-start | bytes 208904 | tf_op jit(solution)/shard_map/ppermute | solution.py:181
  49.8 5.5 %collective-permute-start.25 = (f32[136,128]{1,0:T(8,128)S(1)}, f32[136,128]{1,0:T(8,128)S(1)}, u32[]{:S(2)}, u32[]{:S(2)}) collective-permute-start(f32[136,128]{1,0:T(8,128)S(1)} %get-tuple-element.144), channel_id=1, source_target_pairs={{0,4},{2,6},{4,0},{6,2},{8,12},{10,14},{12,8},{14,10},{16,20},{18,... | collective-permute-start | bytes 208904 | tf_op jit(solution)/shard_map/ppermute | solution.py:181
  51.8 6.7 %collective-permute-start.33 = (f32[136,128]{1,0:T(8,128)S(1)}, f32[136,128]{1,0:T(8,128)S(1)}, u32[]{:S(2)}, u32[]{:S(2)}) collective-permute-start(f32[136,128]{1,0:T(8,128)S(1)} %get-tuple-element.160), channel_id=1, source_target_pairs={{0,6},{2,4},{4,2},{6,0},{8,14},{10,12},{12,10},{14,8},{16,22},{18,... | collective-permute-start | bytes 208904 | tf_op jit(solution)/shard_map/ppermute | solution.py:181
  53.5 5.0 %collective-permute-start.34 = (f32[136,128]{1,0:T(8,128)S(1)}, f32[136,128]{1,0:T(8,128)S(1)}, u32[]{:S(2)}, u32[]{:S(2)}) collective-permute-start(f32[136,128]{1,0:T(8,128)S(1)} %get-tuple-element.161), channel_id=1, source_target_pairs={{0,4},{2,6},{4,0},{6,2},{8,12},{10,14},{12,8},{14,10},{16,20},{18,... | collective-permute-start | bytes 208904 | tf_op jit(solution)/shard_map/ppermute | solution.py:181
  (10 other events, 83.2 us)
